TPU v7x, 32 devices: a whole 2x2x4 slice. The times are simulated.
32 devices in a mesh: dp: 8 (over z, y), vocab: 4 (over x, core).
Axes of the slice: x: 2, y: 2, z: 4, core: 2. Of those that a mesh axis runs over, the one named last changes fastest.
Arguments:
- hidden: bfloat16 [1024, 4096], P('dp', 'vocab')
- weight: bfloat16 [4096, 16384], P(None, ('dp', 'vocab'))
- loss_mask: int32 [1024], P('dp'), may hold values from 0 to 1, as said below
- target_ids: int32 [1024], P('dp'), may hold values from 0 to 16383
- turn_ids: int32 [1024], P('dp'), may hold values from 0 to 31, never falling along the last dimension, each value on 1 to 128 neighbouring positions
- advantages: float32 [32], replicated, may hold values from -4 to 4
Outputs:
- loss_value: float32 [], replicated
- hidden_grad: bfloat16 [1024, 4096], P('dp', 'vocab')
- weight_grad: bfloat16 [4096, 16384], P(None, ('dp', 'vocab'))
Inputs may be any that keep to these rules, and one draw needn't show every extreme that they name: `loss_mask`: of the 128 tokens of one index of dp at most 32 bear loss, and some index has exactly 32.
All inputs are finite; a program needn't handle non-finite values.
Results may differ from a plain program's by a relative error of at most 0.0051.
Values may be sent and summed in bfloat16 or wider, within the bound.
No kernel may reach another device: no remote copies, remote signals or barrier semaphores. Data moves between devices by JAX's collectives and lax.ppermute only.
A program may use at most 128 MiB of HBM per device.

v0:
```python
import jax
import jax.numpy as jnp
from jax import lax
from jax.sharding import PartitionSpec as P

CAP = 32


grad_scale = 16384.0


def body(hidden, weight, loss_mask, target_ids, turn_ids, advantages):
    capacity = CAP
    num_turns = advantages.shape[0]
    vocab_width = weight.shape[1]
    row_slot = jnp.cumsum(loss_mask, dtype=jnp.int32) - 1
    slot_grid = jnp.arange(capacity, dtype=jnp.int32)[:, None]
    chosen = (row_slot[None, :] == slot_grid) & (loss_mask[None, :] == 1)
    local_rows = jnp.dot(
        chosen.astype(jnp.bfloat16), hidden, preferred_element_type=jnp.float32
    ).astype(jnp.bfloat16)
    id_table = jnp.stack([target_ids, turn_ids, loss_mask], axis=1)
    packed_ids = jnp.dot(chosen.astype(jnp.int32), id_table)
    full_rows = lax.all_gather(local_rows, "vocab", axis=1, tiled=True)
    rows_hidden, rows_ids = (
        lax.all_gather(full_rows, "dp", axis=0, tiled=True),
        lax.all_gather(packed_ids, "dp", axis=0, tiled=True),
    )
    logits = jnp.dot(rows_hidden, weight, preferred_element_type=jnp.float32)
    shard_index = lax.axis_index("dp") * lax.axis_size("vocab") + lax.axis_index("vocab")
    local_target = rows_ids[:, 0] - shard_index * vocab_width
    columns = jnp.arange(vocab_width, dtype=jnp.int32)[None, :]
    is_target = columns == local_target[:, None]
    target_part = jnp.sum(jnp.where(is_target, logits, 0.0), axis=1)
    local_peak = jnp.max(logits, axis=1)
    local_total = jnp.sum(jnp.exp(logits - local_peak[:, None]), axis=1)
    row_peak = lax.pmax(local_peak, ("dp", "vocab"))
    row_total, target_logit = lax.psum(
        (local_total * jnp.exp(local_peak - row_peak), target_part), ("dp", "vocab")
    )
    log_total = row_peak + jnp.log(row_total)
    is_valid = rows_ids[:, 2].astype(jnp.float32)
    turn_match = rows_ids[:, 1][:, None] == jnp.arange(num_turns, dtype=jnp.int32)[None, :]
    row_advantage = jnp.sum(jnp.where(turn_match, advantages[None, :], 0.0), axis=1)
    row_weight = is_valid * row_advantage / jnp.sum(is_valid)
    loss_value = -jnp.sum(row_weight * (target_logit - log_total))
    probability = jnp.exp(logits - log_total[:, None])
    logit_grad = (
        grad_scale * row_weight[:, None] * (probability - is_target.astype(jnp.float32))
    ).astype(jnp.bfloat16)
    weight_grad = lax.dot_general(
        rows_hidden, logit_grad, (((0,), (0,)), ((), ())), preferred_element_type=jnp.float32
    ).astype(jnp.bfloat16)
    whole_grad = lax.dot_general(
        logit_grad, weight, (((1,), (1,)), ((), ())), preferred_element_type=jnp.float32
    )
    column_part = lax.psum_scatter(whole_grad, "vocab", scatter_dimension=1, tiled=True)
    own_grad = lax.psum_scatter(column_part, "dp", scatter_dimension=0, tiled=True)
    hidden_grad = lax.dot_general(
        chosen.astype(jnp.float32),
        own_grad,
        (((0,), (0,)), ((), ())),
        precision=lax.Precision.HIGHEST,
        preferred_element_type=jnp.float32,
    )
    return (loss_value, hidden_grad.astype(jnp.bfloat16), weight_grad)


def solution(mesh):
    return jax.shard_map(
        body,
        mesh=mesh,
        in_specs=(P("dp", "vocab"), P(None, ("dp", "vocab")), P("dp"), P("dp"), P("dp"), P()),
        out_specs=(P(), P("dp", "vocab"), P(None, ("dp", "vocab"))),
        check_vma=False,
    )
```

profile of v0, /device:TPU:0, one launch (start us, length us, event | category | flops | bytes accessed | tf_op | source)
XLA Modules:
  0.0 279.1 jit_solution(7641329929644787846)
XLA Ops:
  7.2 0.0 copy-start
  7.2 0.0 all-gather.3.cloned.1.call-start
  7.2 0.7 broadcast_compare_fusion
  7.9 0.8 copy.14
  8.7 0.2 reduce-window.8
  8.9 0.1 add_reduce_fusion
  9.0 0.0 copy-done
  9.0 0.2 convolution_convert_fusion.2
  9.1 7.7 %all_gather.10 = bf16[32,4096]{1,0:T(8,128)(2,1)} all-gather(bf16[32,1024]{1,0:T(8,128)(2,1)S(1)} %convolution_convert_fusion.2), channel_id=1, replica_groups=mesh['dp'=8,'vocab'=4] {'vocab'}, dimensions={1}, use_global_device_ids=true | all-gather | bytes 327680 | tf_op jit(solution)/shard_map/all_gather | solution.py:24
  16.8 0.0 all-gather.3.cloned.1.call-update
  16.8 0.0 reduce-scatter.3.cloned.1.call-start
  16.9 0.8 convolution_bitcast_fusion
  17.7 26.6 %all-gather = s32[8,32,3]{1,2,0:T(4,128)S(1)} all-gather(s32[1,32,3]{1,2,0:T(4,128)S(1)} %convolution_bitcast_fusion), channel_id=1, replica_groups=mesh['dp'=8,'vocab'=4] {'dp'}, dimensions={0}, use_global_device_ids=true | all-gather | bytes 3456 | tf_op jit(solution)/shard_map/all_gather | solution.py:27
  44.3 0.1 reshape.43
  44.4 0.6 fusion.17
  45.0 0.7 select_reduce_fusion.1
  45.7 0.7 divide_multiply_fusion.1
  46.4 21.2 %all-gather.3.cloned.1.call-done = bf16[256,4096]{1,0:T(8,128)(2,1)} async-done(((bf16[32,4096]{1,0:T(8,128)(2,1)}), bf16[256,4096]{1,0:T(8,128)(2,1)}) %all-gather.3.cloned.1.call-update) | async-done | bytes 2097168 | tf_op jit(solution)/shard_map/all_gather | solution.py:26
  67.6 4.1 %fusion.20 = (f32[256]{0:T(256)S(1)}, f32[256,512]{1,0:T(8,128)S(1)}) fusion(bf16[256,4096]{1,0:T(8,128)(2,1)} %all-gather.3.cloned.1.call-done, bf16[4096,512]{1,0:T(8,128)(2,1)} %param.7), kind=kOutput, calls=%fused_computation.36 | convolution fusion | flops 1073872640 | bytes 6816768 | tf_op jit(solution)/shard_map/dot_general | solution.py:29
  71.8 39.3 %pmax.7 = f32[256]{0:T(256)S(1)} all-reduce(f32[256]{0:T(256)S(1)} %get-tuple-element.12), channel_id=1, replica_groups=mesh['dp'=8,'vocab'=4] {'dp','vocab'}, use_global_device_ids=true, to_apply=%region_6.7 | all-reduce | flops 256 | bytes 2048 | tf_op jit(solution)/shard_map/pmax | solution.py:37
  111.1 0.3 exponential_reduce_fusion
  111.4 39.9 %all-reduce = (f32[256]{0:T(256)S(1)}, f32[256]{0:T(256)S(1)}) all-reduce(f32[256]{0:T(256)S(1)} %get-tuple-element.4, f32[256]{0:T(256)S(1)} %exponential_multiply_fusion), channel_id=1, replica_groups=mesh['dp'=8,'vocab'=4] {'dp','vocab'}, use_global_device_ids=true, to_apply=%region_4.5 | all-reduce | flops 512 | bytes 4096 | tf_op jit(solution)/shard_map/psum | solution.py:38
  151.3 1.3 fusion.15
  152.5 5.6 %fusion.18 = f32[256,4096]{1,0:T(8,128)} fusion(bf16[4096,512]{1,0:T(8,128)(2,1)} %param.7, f32[256,512]{1,0:T(8,128)S(1)} %get-tuple-element.13, f32[256]{0:T(256)S(1)} %get-tuple-element.8, f32[256]{0:T(256)S(1)} %bitcast.21, s32[256]{0:T(256)S(1)} %bitcast.19), kind=kOutput, calls=%fused_computation.34 | convolution fusion | flops 1074528256 | bytes 8915968 | tf_op jit(solution)/shard_map/dot_general | solution.py:54
  158.1 0.0 reduce-scatter.3.cloned.1.call-update
  158.1 0.0 reduce-scatter.5.cloned.1.call-start
  158.2 44.0 %reduce-scatter.3.cloned.1.call-done = f32[256,1024]{1,0:T(8,128)} async-done(((f32[256,4096]{1,0:T(8,128)}), f32[256,1024]{1,0:T(8,128)}) %reduce-scatter.3.cloned.1.call-update) | async-done | bytes 1048592 | tf_op jit(solution)/shard_map/reduce_scatter | solution.py:57
  202.1 0.0 reduce-scatter.5.cloned.1.call-update
  202.8 0.0 copy-done.1
  202.8 3.5 %convolution_convert_fusion = bf16[4096,512]{1,0:T(8,128)(2,1)} fusion(bf16[256,4096]{1,0:T(8,128)(2,1)S(1)} %copy-done.1, f32[256,512]{1,0:T(8,128)S(1)} %get-tuple-element.13, f32[256]{0:T(256)S(1)} %get-tuple-element.8, f32[256]{0:T(256)S(1)} %bitcast.22, s32[256]{0:T(256)S(1)} %bitcast.20), kind=kOutput, calls=%fused_computation | convolution fusion | flops 1076625408 | bytes 6818816 | tf_op jit(solution)/shard_map/dot_general | solution.py:51
  206.3 63.1 %reduce-scatter.5.cloned.1.call-done = f32[32,1024]{1,0:T(8,128)} async-done(((f32[256,1024]{1,0:T(8,128)}), f32[32,1024]{1,0:T(8,128)}) %reduce-scatter.5.cloned.1.call-update) | async-done | bytes 131088 | tf_op jit(solution)/shard_map/reduce_scatter | solution.py:58
  269.4 2.0 convolution_convert_fusion.1
  (4 shorter events, 0.0 us)
Async XLA Ops:
  7.2 1.8 copy-start
  7.2 60.5 %all-gather.3.cloned.1.call-start = ((), (), s32[]{:S(2)}) async-start(), calls=%async_computation.2 | async-start | bytes 2359296 | tf_op jit(solution)/shard_map/all_gather | solution.py:26
  16.8 185.3 %reduce-scatter.3.cloned.1.call-start = ((), (), s32[]{:S(2)}) async-start(), calls=%async_computation.3 | async-start | bytes 5242880 | tf_op jit(solution)/shard_map/reduce_scatter | solution.py:57
  158.1 44.7 %copy-start.1 = (bf16[256,4096]{1,0:T(8,128)(2,1)S(1)}, bf16[256,4096]{1,0:T(8,128)(2,1)}, u32[]{:S(2)}) copy-start(bf16[256,4096]{1,0:T(8,128)(2,1)} %all-gather.3.cloned.1.call-done) | copy-start | bytes 6291460
  158.1 111.3 %reduce-scatter.5.cloned.1.call-start = ((), (), s32[]{:S(2)}) async-start(), calls=%async_computation.4 | async-start | bytes 1179648 | tf_op jit(solution)/shard_map/reduce_scatter | solution.py:58
Sparse Core Ops, SparseCore 0:
  16.9 50.6 all-gather.2
  158.2 43.8 reduce-scatter.2
  205.9 63.4 reduce-scatter.4
where the time goes:
time: 280 us; the launch traced here: 279 us
  waiting for transfers between devices  128 us (46%)
  blocking collectives  113 us (40%)
  matrix products  16.2 us (6%)
  between operations  15.6 us (6%)
  other arithmetic  4.52 us (2%)
    reduce_scatter x1, waiting for transfers between devices, body(): lax.psum_scatter(column_part, 'dp', scatter_dimension=0, tiled=True)  63.1 us
    reduce_scatter x1, waiting for transfers between devices, body(): lax.psum_scatter(whole_grad, 'vocab', scatter_dimension=1, tiled=True)  44 us
    psum x1, blocking collectives, body(): lax.psum((local_total * jnp.exp(local_peak - row_peak), target_part), ('d...  39.9 us
    pmax x1, blocking collectives, body(): row_peak = lax.pmax(local_peak, ('dp', 'vocab'))  39.3 us
    all_gather x1, blocking collectives, body(): lax.all_gather(packed_ids, 'dp', axis=0, tiled=True)  26.6 us
    all_gather x1, waiting for transfers between devices, body(): lax.all_gather(full_rows, 'dp', axis=0, tiled=True)  21.2 us
    all_gather x1, blocking collectives, body(): full_rows = lax.all_gather(local_rows, 'vocab', axis=1, tiled=True)  7.67 us
  transfers between devices with their start and end apart: 3, of which 3 were waited for; matrix products, arithmetic and copies ran while one was open for 2% of the time, Pallas kernels for 0%

commit v1 on v0

v1 whole, which is shorter than its diff:
```python
import functools

import jax
import jax.numpy as jnp
from jax import lax
from jax.experimental import pallas as pl
from jax.experimental.pallas import tpu as pltpu
from jax.sharding import PartitionSpec as P

CAP = 32
grad_scale = 16384.0
VMEM_BYTES = 56 * 1024 * 1024
AXES = ("dp", "vocab")


def params():
    return pltpu.CompilerParams(vmem_limit_bytes=VMEM_BYTES)


def vmem(count):
    return [pl.BlockSpec(memory_space=pltpu.VMEM)] * count


def choose(mask):
    tokens = mask.shape[1]
    wide = jnp.broadcast_to(mask.astype(jnp.float32), (8, tokens))
    before = lax.broadcasted_iota(jnp.int32, (tokens, tokens), 0)
    after = lax.broadcasted_iota(jnp.int32, (tokens, tokens), 1)
    upto = (before <= after).astype(jnp.float32)
    slot = jnp.dot(
        wide.astype(jnp.bfloat16), upto.astype(jnp.bfloat16), preferred_element_type=jnp.float32
    )[0:1]
    grid = lax.broadcasted_iota(jnp.int32, (CAP, tokens), 0) + 1
    return (slot.astype(jnp.int32) == grid) & (mask == 1)


def pack_kernel(hidden, mask, target, turn, rows, ids):
    chosen = choose(mask[...])
    rows[...] = jnp.dot(
        chosen.astype(jnp.float32).astype(jnp.bfloat16),
        hidden[...],
        preferred_element_type=jnp.float32,
    ).astype(jnp.bfloat16)
    lane = lax.broadcasted_iota(jnp.int32, ids.shape, 1)
    table = jnp.zeros(ids.shape, jnp.float32)
    for place, field in enumerate((mask, turn, target)):
        picked = jnp.where(chosen, field[...].astype(jnp.float32), 0.0)
        table = jnp.where(lane == place, jnp.sum(picked, axis=1, keepdims=True), table)
    ids[...] = table


def info_kernel(own, other, advantages, info):
    table = jnp.concatenate([own[...], other[...]], axis=0)
    valid, turn, target = table[:, 0:1], table[:, 1:2], table[:, 2:3]
    turns = advantages.shape[1]
    spot = lax.broadcasted_iota(jnp.int32, (table.shape[0], turns), 1)
    gain = jnp.sum(
        jnp.where(spot == turn.astype(jnp.int32), advantages[...], 0.0), axis=1, keepdims=True
    )
    weight = valid * gain / jnp.sum(valid)
    lane = lax.broadcasted_iota(jnp.int32, info.shape, 1)
    info[...] = jnp.where(lane == 0, weight, jnp.where(lane == 1, target, 0.0))


def reorder(stats, position, groups):
    lanes = stats.shape[1]
    lane = lax.broadcasted_iota(jnp.int32, stats.shape, 1)
    bit = 1
    while bit < groups:
        size = CAP * bit
        swapped = jnp.where(
            (lane & size) != 0,
            pltpu.roll(stats, size, 1),
            pltpu.roll(stats, lanes - size, 1),
        )
        stats = jnp.where((position & bit) != 0, swapped, stats)
        bit *= 2
    return stats


def load_rows(pieces, rows, sems):
    copies = {}
    for number, (block, start, ref) in enumerate(pieces):
        height, width = ref.shape
        copy = pltpu.make_async_copy(
            ref,
            rows.at[pl.ds(start, height), pl.ds(block * width, width)],
            sems.at[number],
        )
        copy.start()
        copies.setdefault(block, []).append(copy)
    return copies


def load_weight(weight, held, sems, vocab_rank, blocks):
    copies = []
    width = weight.shape[0] // blocks
    for block in range(blocks):
        start = pl.multiple_of((vocab_rank ^ block) * width, width)
        copy = pltpu.make_async_copy(
            weight.at[pl.ds(start, width)],
            held.at[pl.ds(block * width, width)],
            sems.at[block],
        )
        copy.start()
        copies.append(copy)
    return copies


def logits_kernel(places, blocks, groups, where, info, weight, *refs):
    count = len(places)
    pieces = [(b, s, r) for (b, s), r in zip(places, refs[:count])]
    logits, stats, rows, held, row_sems, weight_sems = refs[count:]
    rank, position, shard = where[0], where[1], where[2]
    weight_copies = load_weight(weight, held, weight_sems, rank, blocks)
    row_copies = load_rows(pieces, rows, row_sems)
    width = weight.shape[0] // blocks
    total = None
    for block in range(blocks):
        weight_copies[block].wait()
        for copy in row_copies[block]:
            copy.wait()
        part = jnp.dot(
            rows[:, block * width:(block + 1) * width],
            held[block * width:(block + 1) * width],
            preferred_element_type=jnp.float32,
        )
        total = part if total is None else total + part
    logits[...] = total
    height, columns = total.shape
    target = info[:, 1:2].astype(jnp.int32) - shard * columns
    column = lax.broadcasted_iota(jnp.int32, total.shape, 1)
    hit = jnp.sum(jnp.where(column == target, total, 0.0), axis=1, keepdims=True)
    peak = jnp.max(total, axis=1, keepdims=True)
    mass = jnp.sum(jnp.exp(total - peak), axis=1, keepdims=True)
    lane = lax.broadcasted_iota(jnp.int32, (height, 128), 1)
    table = jnp.where(lane == 0, peak, jnp.where(lane == 1, mass, jnp.where(lane == 2, hit, 0.0)))
    stats[...] = reorder(jnp.transpose(table)[0:8], position, groups)


def merge(tables):
    peak = functools.reduce(jnp.maximum, [table[0:1] for table in tables])
    mass = sum(table[1:2] * jnp.exp(table[0:1] - peak) for table in tables)
    hit = sum(table[2:3] for table in tables)
    return peak, mass, hit


def merge_kernel(*refs):
    out = refs[-1]
    peak, mass, hit = merge([ref[...] for ref in refs[:-1]])
    row = lax.broadcasted_iota(jnp.int32, out.shape, 0)
    out[...] = jnp.where(row == 0, peak, jnp.where(row == 1, mass, jnp.where(row == 2, hit, 0.0)))


def grad_kernel(count, blocks, groups, where, info, logits, weight, *refs):
    tables = [ref[...] for ref in refs[:count]]
    outs = refs[count:count + 2 * blocks]
    logit_grad, loss, held, weight_sems = refs[count + 2 * blocks:]
    rank, position, shard = where[0], where[1], where[2]
    copies = load_weight(weight, held, weight_sems, rank, blocks)
    peak, mass, hit = merge(tables)
    lanes = peak.shape[1]
    row = lax.broadcasted_iota(jnp.int32, (8, lanes), 0)
    both = jnp.where(row == 0, peak + jnp.log(mass), jnp.where(row == 1, hit, 0.0))
    both = reorder(both, position, groups)
    both = jnp.transpose(jnp.concatenate([both] * 16, axis=0))
    log_total, target_logit = both[:, 0:1], both[:, 1:2]
    row_weight = info[:, 0:1]
    loss[0, 0] = -jnp.sum(row_weight * (target_logit - log_total))
    columns = logits.shape[1]
    target = info[:, 1:2].astype(jnp.int32) - shard * columns
    column = lax.broadcasted_iota(jnp.int32, logits.shape, 1)
    probability = jnp.exp(logits[...] - log_total)
    grad = (
        grad_scale * row_weight * (probability - (column == target).astype(jnp.float32))
    ).astype(jnp.bfloat16)
    logit_grad[...] = grad
    width = weight.shape[0] // blocks
    half = logits.shape[0] // 2
    order = [b for b in range(blocks) if b % 2] + [b for b in range(blocks) if not b % 2]
    for copy in copies:
        copy.wait()
    for block in order:
        part = lax.dot_general(
            grad,
            held[block * width:(block + 1) * width],
            (((1,), (1,)), ((), ())),
            preferred_element_type=jnp.float32,
        )
        for side in range(2):
            out = outs[2 * block + side]
            out[...] = part[side * half:(side + 1) * half].astype(out.dtype)


def weight_kernel(places, blocks, where, logit_grad, *refs):
    count = len(places)
    pieces = [(b, s, r) for (b, s), r in zip(places, refs[:count])]
    out, rows, done, row_sems, out_sems = refs[count:]
    rank = where[0]
    row_copies = load_rows(pieces, rows, row_sems)
    width = rows.shape[1] // blocks
    out_copies = []
    for block in range(blocks):
        for copy in row_copies[block]:
            copy.wait()
        done[block * width:(block + 1) * width] = lax.dot_general(
            rows[:, block * width:(block + 1) * width],
            logit_grad[...],
            (((0,), (0,)), ((), ())),
            preferred_element_type=jnp.float32,
        ).astype(jnp.bfloat16)
        start = pl.multiple_of((rank ^ block) * width, width)
        copy = pltpu.make_async_copy(
            done.at[pl.ds(block * width, width)], out.at[pl.ds(start, width)], out_sems.at[block]
        )
        copy.start()
        out_copies.append(copy)
    for copy in out_copies:
        copy.wait()


def unpack_kernel(*refs):
    mask, out = refs[0], refs[-1]
    total = sum(ref[...].astype(jnp.float32) for ref in refs[1:-1])
    chosen = choose(mask[...])
    out[...] = lax.dot_general(
        chosen.astype(jnp.float32).astype(jnp.bfloat16),
        total.astype(jnp.bfloat16),
        (((0,), (0,)), ((), ())),
        preferred_element_type=jnp.float32,
    ).astype(jnp.bfloat16)


def body(dps, ranks, hidden, weight, loss_mask, target_ids, turn_ids, advantages):
    tokens, width = hidden.shape
    columns = weight.shape[1]
    zs, xs = dps // 2, ranks // 2
    height = zs * CAP
    half = height // 2
    total_rows = dps * CAP
    bf16, f32 = jnp.bfloat16, jnp.float32
    shape = jax.ShapeDtypeStruct

    def send(value, z, y, x, core):
        far, near = 2 * z + y, 2 * x + core
        pairs = [
            (d * ranks + v, (d ^ far) * ranks + (v ^ near))
            for d in range(dps)
            for v in range(ranks)
        ]
        return lax.ppermute(value, AXES, pairs)

    group, rank = lax.axis_index("dp"), lax.axis_index("vocab")
    position = (group & 1) * zs + (group >> 1)
    where = jnp.stack([rank, position, group * ranks + rank]).astype(jnp.int32)
    mask = loss_mask.reshape(1, tokens)

    packed, ids = pl.pallas_call(
        pack_kernel,
        out_shape=(shape((CAP, width), bf16), shape((CAP, 128), f32)),
        in_specs=vmem(4),
        out_specs=tuple(vmem(2)),
        compiler_params=params(),
    )(hidden, mask, target_ids.reshape(1, tokens), turn_ids.reshape(1, tokens))

    own = jnp.concatenate([packed] + [send(packed, z, 0, 0, 0) for z in range(1, zs)], axis=0)
    own_ids = jnp.concatenate([ids] + [send(ids, z, 0, 0, 0) for z in range(1, zs)], axis=0)
    across = send(own, 0, 1, 0, 0)
    other_ids = send(own_ids, 0, 1, 0, 0)
    pieces = [(0, 0, own), (0, height, across)]
    for x in range(1, xs):
        beside = send(own, 0, 0, x, 0)
        upper = send(beside[:half], 0, 1, 0, 0)
        lower = send(across[half:], 0, 0, x, 0)
        pieces += [(2 * x, 0, beside), (2 * x, height, upper), (2 * x, height + half, lower)]
    pieces += [(b + 1, start, send(piece, 0, 0, 0, 1)) for b, start, piece in pieces]
    places = [(b, start) for b, start, _ in pieces]
    arrays = [piece for _, _, piece in pieces]

    info = pl.pallas_call(
        info_kernel,
        out_shape=shape((total_rows, 128), f32),
        in_specs=vmem(3),
        out_specs=vmem(1)[0],
        compiler_params=params(),
    )(own_ids, other_ids, advantages.reshape(1, -1))

    smem = pl.BlockSpec(memory_space=pltpu.SMEM)
    hbm = pl.BlockSpec(memory_space=pl.ANY)
    depth = weight.shape[0]
    logits, stats = pl.pallas_call(
        functools.partial(logits_kernel, places, ranks, dps),
        out_shape=(shape((total_rows, columns), f32), shape((8, total_rows), f32)),
        in_specs=[smem] + vmem(1) + [hbm] * (1 + len(arrays)),
        out_specs=tuple(vmem(2)),
        scratch_shapes=[
            pltpu.VMEM((total_rows, depth), bf16),
            pltpu.VMEM((depth, columns), bf16),
            pltpu.SemaphoreType.DMA((len(arrays),)),
            pltpu.SemaphoreType.DMA((ranks,)),
        ],
        compiler_params=params(),
    )(where, info, weight, *arrays)

    near = [stats] + [
        send(stats, 0, y, x, core)
        for y in range(2)
        for x in range(xs)
        for core in range(2)
        if y + x + core
    ]
    stats = pl.pallas_call(
        merge_kernel,
        out_shape=shape((8, total_rows), f32),
        in_specs=vmem(len(near)),
        out_specs=vmem(1)[0],
        compiler_params=params(),
    )(*near)
    tables = [stats] + [send(stats, z, 0, 0, 0) for z in range(1, zs)]

    outs = []
    for b in range(ranks):
        outs += [shape((height, width), bf16 if b % 2 else f32)] * 2
    *parts, logit_grad, loss = pl.pallas_call(
        functools.partial(grad_kernel, len(tables), ranks, dps),
        out_shape=tuple(outs) + (shape((total_rows, columns), bf16), shape((1, 1), f32)),
        in_specs=[smem] + vmem(2) + [hbm] + vmem(len(tables)),
        out_specs=tuple(vmem(len(outs) + 1)) + (smem,),
        scratch_shapes=[
            pltpu.VMEM((depth, columns), bf16),
            pltpu.SemaphoreType.DMA((ranks,)),
        ],
        compiler_params=params(),
    )(where, info, logits, weight, *tables)

    def back(x, side):
        return parts[4 * x + side] + send(parts[4 * x + 2 + side], 0, 0, 0, 1).astype(f32)

    corner = [back(x, 1) for x in range(1, xs)]
    across, beside, own = back(0, 1), [back(x, 0) for x in range(1, xs)], back(0, 0)
    across_low, across_high = across[half:], across[:half]
    own = own + jnp.concatenate(
        [jnp.zeros((half, width), f32), send(across_low.astype(bf16), 0, 1, 0, 0).astype(f32)]
    )
    for x in range(1, xs):
        diagonal = corner[x - 1].astype(bf16)
        across_high = across_high + send(diagonal[:half], 0, 0, x, 0).astype(f32)
        low = beside[x - 1][half:] + send(diagonal[half:], 0, 1, 0, 0).astype(f32)
        high = beside[x - 1][:half]
        own = own + jnp.concatenate(
            [send(high.astype(bf16), 0, 0, x, 0), send(low.astype(bf16), 0, 0, x, 0)]
        ).astype(f32)
    own = own + jnp.concatenate(
        [send(across_high.astype(bf16), 0, 1, 0, 0).astype(f32), jnp.zeros((half, width), f32)]
    )
    sums = [own[:CAP]] + [
        send(own[z * CAP:(z + 1) * CAP].astype(bf16), z, 0, 0, 0) for z in range(1, zs)
    ]

    weight_grad = pl.pallas_call(
        functools.partial(weight_kernel, places, ranks),
        out_shape=shape((depth, columns), bf16),
        in_specs=[smem] + vmem(1) + [hbm] * len(arrays),
        out_specs=hbm,
        scratch_shapes=[
            pltpu.VMEM((total_rows, depth), bf16),
            pltpu.VMEM((depth, columns), bf16),
            pltpu.SemaphoreType.DMA((len(arrays),)),
            pltpu.SemaphoreType.DMA((ranks,)),
        ],
        compiler_params=params(),
        cost_estimate=pl.CostEstimate(
            flops=2 * total_rows * depth * columns,
            bytes_accessed=2 * depth * (columns + total_rows),
            transcendentals=0,
        ),
    )(where, logit_grad, *arrays)

    hidden_grad = pl.pallas_call(
        unpack_kernel,
        out_shape=shape((tokens, width), bf16),
        in_specs=vmem(1 + len(sums)),
        out_specs=vmem(1)[0],
        compiler_params=params(),
    )(mask, *sums)
    return loss[0, 0], hidden_grad, weight_grad


def solution(mesh):
    return jax.shard_map(
        functools.partial(body, mesh.shape["dp"], mesh.shape["vocab"]),
        mesh=mesh,
        in_specs=(P("dp", "vocab"), P(None, AXES), P("dp"), P("dp"), P("dp"), P()),
        out_specs=(P(), P("dp", "vocab"), P(None, AXES)),
        check_vma=False,
    )
```

time: 280 us -> 105 us (0.38)
  blocking collectives: 113 us -> 0 us
  waiting for transfers between devices: 128 us -> 28.7 us
  starting transfers between devices: 0.12 us -> 40 us
  Pallas kernels: 0 us -> 23.7 us
  matrix products: 16.2 us -> 0 us
  between operations: 15.6 us -> 1.04 us
  local copies, waits for them, and re-layouts: 0.86 us -> 6.92 us
    reduce_scatter x2 -> x0, waiting for transfers between devices: 107 us -> none  [the longest x1 63.1 us: body(): lax.psum_scatter(column_part, 'dp', scatter_dimension=0, tiled=True)]
    ppermute x0 -> x39, starting transfers between devices: none -> 40 us  [send(): return lax.ppermute(value, AXES, pairs)]
    psum x1 -> x0, blocking collectives: 39.9 us -> none  [body(): lax.psum((local_total * jnp.exp(local_peak - row_peak), target_part), ('d...]
    pmax x1 -> x0, blocking collectives: 39.3 us -> none  [body(): row_peak = lax.pmax(local_peak, ('dp', 'vocab'))]
    all_gather x2 -> x0, blocking collectives: 34.3 us -> none  [the longest x1 26.6 us: body(): lax.all_gather(packed_ids, 'dp', axis=0, tiled=True)]
    ppermute x0 -> x39, waiting for transfers between devices: none -> 28.7 us  [send(): return lax.ppermute(value, AXES, pairs)]
    pallas_call x0 -> x7, Pallas kernels: none -> 23.7 us  [the longest x1 6.09 us: body(): pl.pallas_call(functools.partial(grad_kernel, len(tables), ranks, dps), o...]
    all_gather x1 -> x0, waiting for transfers between devices: 21.2 us -> none  [body(): lax.all_gather(full_rows, 'dp', axis=0, tiled=True)]
  transfers between devices with their start and end apart: 3 -> 39, of which waited for: 3 -> 15; matrix products, arithmetic and copies ran while one was open for 2% -> 6% of each run, Pallas kernels for 0% -> 7%
where the time goes in v1:
time: 105 us
  starting transfers between devices  40 us (38%)
  waiting for transfers between devices  28.7 us (27%)
  Pallas kernels  23.7 us (23%)
  local copies, waits for them, and re-layouts  6.92 us (7%)
  other arithmetic  4.14 us (4%)
    ppermute x39, starting transfers between devices, send(): return lax.ppermute(value, AXES, pairs)  40 us
    ppermute x39, waiting for transfers between devices, send(): return lax.ppermute(value, AXES, pairs)  28.7 us
    unnamed x58, local copies, waits for them, and re-layouts  6.16 us
    pallas_call x1, Pallas kernels, body(): pl.pallas_call(functools.partial(grad_kernel, len(tables), ranks, dps), o...  6.09 us
    pallas_call x1, Pallas kernels, body(): pl.pallas_call(functools.partial(logits_kernel, places, ranks, dps), out_...  5.38 us
    pallas_call x1, Pallas kernels, body(): pl.pallas_call(functools.partial(weight_kernel, places, ranks), out_shape...  4.97 us
    add x2, other arithmetic, back(): parts[4 * x + side] + send(parts[4 * x + 2 + side], 0, 0, 0, 1).astype(f32)  2.22 us
  transfers between devices with their start and end apart: 39, of which 15 were waited for; matrix products, arithmetic and copies ran while one was open for 6% of the time, Pallas kernels for 7%

profile of v1, /device:TPU:0, one launch (start us, length us, event | category | flops | bytes accessed | tf_op | source)
XLA Modules:
  0.0 104.5 jit_solution(10481937952675134713)
XLA Ops:
  0.6 1.9 %shard_map.85 = (bf16[32,1024]{1,0:T(8,128)(2,1)}, f32[32,128]{1,0:T(8,128)}) custom-call(bf16[128,1024]{1,0:T(8,128)(2,1)} %hidden.1, s32[1,128]{1,0:T(1,128)} %bitcast.8, s32[1,128]{1,0:T(1,128)} %bitcast.10, s32[1,128]{1,0:T(1,128)} %bitcast.11), custom_call_target="tpu_custom_call" | custom-call | tf_op jit(solution)/shard_map/pallas_call | solution.py:258
  2.5 5.0 %collective-permute-start.2 = (f32[32,128]{1,0:T(8,128)}, f32[32,128]{1,0:T(8,128)S(1)}, u32[]{:S(2)}, u32[]{:S(2)}) collective-permute-start(f32[32,128]{1,0:T(8,128)} %get-tuple-element.17), channel_id=1, source_target_pairs={{0,24},{1,25},{2,26},{3,27},{4,28},{5,29},{6,30},{7,31},{8,16},{9,... | collective-permute-start | bytes 49160 | tf_op jit(solution)/shard_map/ppermute | solution.py:251
  8.2 3.8 %collective-permute-start.6 = (bf16[32,1024]{1,0:T(8,128)(2,1)}, bf16[32,1024]{1,0:T(8,128)(2,1)S(1)}, u32[]{:S(2)}, u32[]{:S(2)}) collective-permute-start(bf16[32,1024]{1,0:T(8,128)(2,1)} %get-tuple-element.18), channel_id=1, source_target_pairs={{0,24},{1,25},{2,26},{3,27},{4,28},{5,29},{6,30},{7,31},{8,16},{9,... | collective-permute-start | bytes 196616 | tf_op jit(solution)/shard_map/ppermute | solution.py:251
  14.1 3.9 %collective-permute-done.4 = bf16[32,1024]{1,0:T(8,128)(2,1)S(1)} collective-permute-done((bf16[32,1024]{1,0:T(8,128)(2,1)}, bf16[32,1024]{1,0:T(8,128)(2,1)S(1)}, u32[]{:S(2)}, u32[]{:S(2)}) %collective-permute-start.4) | collective-permute-done | bytes 65568 | tf_op jit(solution)/shard_map/ppermute | solution.py:251
  18.1 1.6 %collective-permute-start.8 = (bf16[128,1024]{1,0:T(8,128)(2,1)S(1)}, bf16[128,1024]{1,0:T(8,128)(2,1)S(1)}, u32[]{:S(2)}, u32[]{:S(2)}) collective-permute-start(bf16[128,1024]{1,0:T(8,128)(2,1)S(1)} %constant_dynamic-update-slice_fusion.4.refs_0_), channel_id=1, source_target_pairs={{0,2},{1,3},{2,0},{3,1},{4,6},{5,7},{6,4},{7,5},{8,10},{9,11},{10,... | collective-permute-start | bytes 786440 | tf_op jit(solution)/shard_map/ppermute | solution.py:251
  19.7 1.5 %collective-permute-start.7 = (bf16[128,1024]{1,0:T(8,128)(2,1)S(1)}, bf16[128,1024]{1,0:T(8,128)(2,1)S(1)}, u32[]{:S(2)}, u32[]{:S(2)}) collective-permute-start(bf16[128,1024]{1,0:T(8,128)(2,1)S(1)} %constant_dynamic-update-slice_fusion.4.refs_0_), channel_id=1, source_target_pairs={{0,4},{1,5},{2,6},{3,7},{4,0},{5,1},{6,2},{7,3},{8,12},{9,13},{10,... | collective-permute-start | bytes 786440 | tf_op jit(solution)/shard_map/ppermute | solution.py:251
  21.8 2.9 %collective-permute-done.8.refs_2_ = bf16[128,1024]{1,0:T(8,128)(2,1)S(1)} collective-permute-done((bf16[128,1024]{1,0:T(8,128)(2,1)S(1)}, bf16[128,1024]{1,0:T(8,128)(2,1)S(1)}, u32[]{:S(2)}, u32[]{:S(2)}) %collective-permute-start.8) | collective-permute-done | bytes 262176 | tf_op jit(solution)/shard_map/ppermute | solution.py:251
  24.7 1.6 %collective-permute-start.9 = (bf16[64,1024]{1,0:T(8,128)(2,1)S(1)}, bf16[64,1024]{1,0:T(8,128)(2,1)S(1)}, u32[]{:S(2)}, u32[]{:S(2)}) collective-permute-start(bf16[64,1024]{1,0:T(8,128)(2,1)S(1)} %slice.53), channel_id=1, source_target_pairs={{0,4},{1,5},{2,6},{3,7},{4,0},{5,1},{6,2},{7,3},{8,12},{9,13},{10,... | collective-permute-start | bytes 393224 | tf_op jit(solution)/shard_map/ppermute | solution.py:251
  26.3 1.7 %collective-permute-done.7.refs_1_ = bf16[128,1024]{1,0:T(8,128)(2,1)S(1)} collective-permute-done((bf16[128,1024]{1,0:T(8,128)(2,1)S(1)}, bf16[128,1024]{1,0:T(8,128)(2,1)S(1)}, u32[]{:S(2)}, u32[]{:S(2)}) %collective-permute-start.7) | collective-permute-done | bytes 262176 | tf_op jit(solution)/shard_map/ppermute | solution.py:251
  30.2 3.9 %collective-permute-done.10.refs_4_ = bf16[64,1024]{1,0:T(8,128)(2,1)S(1)} collective-permute-done((bf16[64,1024]{1,0:T(8,128)(2,1)S(1)}, bf16[64,1024]{1,0:T(8,128)(2,1)S(1)}, u32[]{:S(2)}, u32[]{:S(2)}) %collective-permute-start.10) | collective-permute-done | bytes 131104 | tf_op jit(solution)/shard_map/ppermute | solution.py:251
  34.7 1.9 %shard_map.86.info = f32[256,128]{1,0:T(8,128)} custom-call(f32[128,128]{1,0:T(8,128)} %copy-done.11, f32[128,128]{1,0:T(8,128)} %copy-done.12, f32[1,32]{1,0:T(1,128)} %bitcast.12), custom_call_target="tpu_custom_call" | custom-call | tf_op jit(solution)/shard_map/pallas_call | solution.py:280
  38.1 5.4 %shard_map.87 = (f32[256,512]{1,0:T(8,128)}, f32[8,256]{1,0:T(8,128)}) custom-call(s32[3]{0:T(128)} %pad_add_fusion.where, f32[256,128]{1,0:T(8,128)} %shard_map.86.info, bf16[4096,512]{1,0:T(8,128)(2,1)} %weight.3, bf16[128,1024]{1,0:T(8,128)(2,1)} %copy-done.2, bf16[128,1024]{1,0:T(8,128)(2,1)} %copy-done.1, bf16[128,1024]{1,0:T(8,128)(2,1)} %copy-done, ...), custom_call_target="tpu_custom_call" | custom-call | tf_op jit(solution)/shard_map/pallas_call | solution.py:291
  43.5 1.4 %collective-permute-start.22 = (f32[8,256]{1,0:T(8,128)}, f32[8,256]{1,0:T(8,128)S(1)}, u32[]{:S(2)}, u32[]{:S(2)}) collective-permute-start(f32[8,256]{1,0:T(8,128)} %get-tuple-element.20.refs_0_), channel_id=1, source_target_pairs={{0,7},{1,6},{2,5},{3,4},{4,3},{5,2},{6,1},{7,0},{8,15},{9,14},{10,... | collective-permute-start | bytes 24584 | tf_op jit(solution)/shard_map/ppermute | solution.py:251
  44.9 1.7 %collective-permute-start.21 = (f32[8,256]{1,0:T(8,128)}, f32[8,256]{1,0:T(8,128)S(1)}, u32[]{:S(2)}, u32[]{:S(2)}) collective-permute-start(f32[8,256]{1,0:T(8,128)} %get-tuple-element.20.refs_0_), channel_id=1, source_target_pairs={{0,6},{1,7},{2,4},{3,5},{4,2},{5,3},{6,0},{7,1},{8,14},{9,15},{10,... | collective-permute-start | bytes 24584 | tf_op jit(solution)/shard_map/ppermute | solution.py:251
  48.4 1.7 %collective-permute-start.17 = (f32[8,256]{1,0:T(8,128)}, f32[8,256]{1,0:T(8,128)S(1)}, u32[]{:S(2)}, u32[]{:S(2)}) collective-permute-start(f32[8,256]{1,0:T(8,128)} %get-tuple-element.20.refs_0_), channel_id=1, source_target_pairs={{0,2},{1,3},{2,0},{3,1},{4,6},{5,7},{6,4},{7,5},{8,10},{9,11},{10,... | collective-permute-start | bytes 24584 | tf_op jit(solution)/shard_map/ppermute | solution.py:251
  53.4 1.4 %shard_map.88.refs_0_ = f32[8,256]{1,0:T(8,128)} custom-call(f32[8,256]{1,0:T(8,128)} %get-tuple-element.20.refs_0_, f32[8,256]{1,0:T(8,128)} %copy-done.25, f32[8,256]{1,0:T(8,128)} %copy-done.24, f32[8,256]{1,0:T(8,128)} %copy-done.23, f32[8,256]{1,0:T(8,128)} %copy-done.22, f32[8,256]{1,0:T(8,128)} %copy-done.21, f32[8,256]{1,0:T(8,128)} %copy-done.20, ...), custom_call_target="tpu_custom_call" | custom-call | tf_op jit(solution)/shard_map/pallas_call | solution.py:312
  54.9 2.8 %collective-permute-start.25 = (f32[8,256]{1,0:T(8,128)}, f32[8,256]{1,0:T(8,128)S(1)}, u32[]{:S(2)}, u32[]{:S(2)}) collective-permute-start(f32[8,256]{1,0:T(8,128)} %shard_map.88.refs_0_), channel_id=1, source_target_pairs={{0,24},{1,25},{2,26},{3,27},{4,28},{5,29},{6,30},{7,31},{8,16},{9,... | collective-permute-start | bytes 24584 | tf_op jit(solution)/shard_map/ppermute | solution.py:251
  57.7 1.6 %collective-permute-start.23 = (f32[8,256]{1,0:T(8,128)}, f32[8,256]{1,0:T(8,128)S(1)}, u32[]{:S(2)}, u32[]{:S(2)}) collective-permute-start(f32[8,256]{1,0:T(8,128)} %shard_map.88.refs_0_), channel_id=1, source_target_pairs={{0,8},{1,9},{2,10},{3,11},{4,12},{5,13},{6,14},{7,15},{8,0},{9,1},... | collective-permute-start | bytes 24584 | tf_op jit(solution)/shard_map/ppermute | solution.py:251
  59.2 1.3 %collective-permute-done.25.refs_3_ = f32[8,256]{1,0:T(8,128)S(1)} collective-permute-done((f32[8,256]{1,0:T(8,128)}, f32[8,256]{1,0:T(8,128)S(1)}, u32[]{:S(2)}, u32[]{:S(2)}) %collective-permute-start.25) | collective-permute-done | bytes 8224 | tf_op jit(solution)/shard_map/ppermute | solution.py:251
  60.5 1.9 %collective-permute-done.24.refs_2_ = f32[8,256]{1,0:T(8,128)S(1)} collective-permute-done((f32[8,256]{1,0:T(8,128)}, f32[8,256]{1,0:T(8,128)S(1)}, u32[]{:S(2)}, u32[]{:S(2)}) %collective-permute-start.24) | collective-permute-done | bytes 8224 | tf_op jit(solution)/shard_map/ppermute | solution.py:251
  63.0 6.1 %shard_map.89 = (f32[128,1024]{1,0:T(8,128)}, f32[128,1024]{1,0:T(8,128)}, bf16[128,1024]{1,0:T(8,128)(2,1)}, bf16[128,1024]{1,0:T(8,128)(2,1)}, f32[128,1024]{1...) custom-call(s32[3]{0:T(128)} %pad_add_fusion.where, ...), custom_call_target="tpu_custom_call" | custom-call | tf_op jit(solution)/shard_map/pallas_call | solution.py:324
  72.1 1.5 %collective-permute-start.28 = (bf16[64,1024]{1,0:T(8,128)(2,1)S(1)}, bf16[64,1024]{1,0:T(8,128)(2,1)S(1)}, u32[]{:S(2)}, u32[]{:S(2)}) collective-permute-start(bf16[64,1024]{1,0:T(8,128)(2,1)S(1)} %slice.74), channel_id=1, source_target_pairs={{0,4},{1,5},{2,6},{3,7},{4,0},{5,1},{6,2},{7,3},{8,12},{9,13},{10,... | collective-permute-start | bytes 393224 | tf_op jit(solution)/shard_map/ppermute | solution.py:251
  76.5 1.9 %collective-permute-start.30 = (bf16[64,1024]{1,0:T(8,128)(2,1)S(1)}, bf16[64,1024]{1,0:T(8,128)(2,1)S(1)}, u32[]{:S(2)}, u32[]{:S(2)}) collective-permute-start(bf16[64,1024]{1,0:T(8,128)(2,1)S(1)} %slice.73), channel_id=1, source_target_pairs={{0,2},{1,3},{2,0},{3,1},{4,6},{5,7},{6,4},{7,5},{8,10},{9,11},{10,... | collective-permute-start | bytes 393224 | tf_op jit(solution)/shard_map/ppermute | solution.py:251
  78.6 1.9 %collective-permute-done.32 = bf16[64,1024]{1,0:T(8,128)(2,1)S(1)} collective-permute-done((bf16[64,1024]{1,0:T(8,128)(2,1)S(1)}, bf16[64,1024]{1,0:T(8,128)(2,1)S(1)}, u32[]{:S(2)}, u32[]{:S(2)}) %collective-permute-start.32) | collective-permute-done | bytes 131104 | tf_op jit(solution)/shard_map/ppermute | solution.py:251
  80.5 1.9 %collective-permute-start.33 = (bf16[64,1024]{1,0:T(8,128)(2,1)S(1)}, bf16[64,1024]{1,0:T(8,128)(2,1)S(1)}, u32[]{:S(2)}, u32[]{:S(2)}) collective-permute-start(bf16[64,1024]{1,0:T(8,128)(2,1)S(1)} %fusion.1), channel_id=1, source_target_pairs={{0,2},{1,3},{2,0},{3,1},{4,6},{5,7},{6,4},{7,5},{8,10},{9,11},{10,... | collective-permute-start | bytes 393224 | tf_op jit(solution)/shard_map/ppermute | solution.py:251
  82.4 3.4 %collective-permute-done.34 = bf16[64,1024]{1,0:T(8,128)(2,1)S(1)} collective-permute-done((bf16[64,1024]{1,0:T(8,128)(2,1)S(1)}, bf16[64,1024]{1,0:T(8,128)(2,1)S(1)}, u32[]{:S(2)}, u32[]{:S(2)}) %collective-permute-start.34) | collective-permute-done | bytes 131104 | tf_op jit(solution)/shard_map/ppermute | solution.py:251
  85.9 1.5 %collective-permute-start.35 = (bf16[64,1024]{1,0:T(8,128)(2,1)S(1)}, bf16[64,1024]{1,0:T(8,128)(2,1)S(1)}, u32[]{:S(2)}, u32[]{:S(2)}) collective-permute-start(bf16[64,1024]{1,0:T(8,128)(2,1)S(1)} %fusion), channel_id=1, source_target_pairs={{0,4},{1,5},{2,6},{3,7},{4,0},{5,1},{6,2},{7,3},{8,12},{9,13},{10,... | collective-permute-start | bytes 393224 | tf_op jit(solution)/shard_map/ppermute | solution.py:251
  87.4 3.5 %collective-permute-done.35 = bf16[64,1024]{1,0:T(8,128)(2,1)S(1)} collective-permute-done((bf16[64,1024]{1,0:T(8,128)(2,1)S(1)}, bf16[64,1024]{1,0:T(8,128)(2,1)S(1)}, u32[]{:S(2)}, u32[]{:S(2)}) %collective-permute-start.35) | collective-permute-done | bytes 131104 | tf_op jit(solution)/shard_map/ppermute | solution.py:251
  91.1 1.6 %collective-permute-start.38 = (bf16[32,1024]{1,0:T(8,128)(2,1)S(1)}, bf16[32,1024]{1,0:T(8,128)(2,1)S(1)}, u32[]{:S(2)}, u32[]{:S(2)}) collective-permute-start(bf16[32,1024]{1,0:T(8,128)(2,1)S(1)} %get-tuple-element.33), channel_id=1, source_target_pairs={{0,24},{1,25},{2,26},{3,27},{4,28},{5,29},{6,30},{7,31},{8,16},{9,... | collective-permute-start | bytes 196616 | tf_op jit(solution)/shard_map/ppermute | solution.py:251
  93.2 2.3 %collective-permute-start.36 = (bf16[32,1024]{1,0:T(8,128)(2,1)S(1)}, bf16[32,1024]{1,0:T(8,128)(2,1)S(1)}, u32[]{:S(2)}, u32[]{:S(2)}) collective-permute-start(bf16[32,1024]{1,0:T(8,128)(2,1)S(1)} %get-tuple-element.35), channel_id=1, source_target_pairs={{0,8},{1,9},{2,10},{3,11},{4,12},{5,13},{6,14},{7,15},{8,0},{9,1},... | collective-permute-start | bytes 196616 | tf_op jit(solution)/shard_map/ppermute | solution.py:251
  95.5 5.0 %shard_map.91 = bf16[4096,512]{1,0:T(8,128)(2,1)} custom-call(s32[3]{0:T(128)} %pad_add_fusion.where, bf16[256,512]{1,0:T(8,128)(2,1)} %get-tuple-element.30.logit_grad, bf16[128,1024]{1,0:T(8,128)(2,1)} %copy-done.2, bf16[128,1024]{1,0:T(8,128)(2,1)} %copy-done.1, bf16[128,1024]{1,0:T(8,128)(2,1)} %copy-done, bf16[64,1024]{1,0:T(8,128)(2,1)} %copy-done.7, ...), custom_call_target="tpu_custom_call" | custom-call | flops 1073741824 | bytes 6291456 | tf_op jit(solution)/shard_map/pallas_call | solution.py:360
  102.5 2.1 %shard_map.90 = bf16[128,1024]{1,0:T(8,128)(2,1)} custom-call(s32[1,128]{1,0:T(1,128)} %bitcast.9, f32[32,1024]{1,0:T(8,128)} %slice.61.refs_1_, bf16[32,1024]{1,0:T(8,128)(2,1)} %copy-done.15, bf16[32,1024]{1,0:T(8,128)(2,1)} %copy-done.14, bf16[32,1024]{1,0:T(8,128)(2,1)} %copy-done.13), custom_call_target="tpu_custom_call" | custom-call | tf_op jit(solution)/shard_map/pallas_call | solution.py:379
  (127 shorter events, 21.9 us)
Async XLA Ops:
  2.5 18.7 %collective-permute-start.2 = (f32[32,128]{1,0:T(8,128)}, f32[32,128]{1,0:T(8,128)S(1)}, u32[]{:S(2)}, u32[]{:S(2)}) collective-permute-start(f32[32,128]{1,0:T(8,128)} %get-tuple-element.17), channel_id=1, source_target_pairs={{0,24},{1,25},{2,26},{3,27},{4,28},{5,29},{6,30},{7,31},{8,16},{9,... | collective-permute-start | bytes 49160 | tf_op jit(solution)/shard_map/ppermute | solution.py:251
  7.6 13.6 %collective-permute-start.1 = (f32[32,128]{1,0:T(8,128)}, f32[32,128]{1,0:T(8,128)S(1)}, u32[]{:S(2)}, u32[]{:S(2)}) collective-permute-start(f32[32,128]{1,0:T(8,128)} %get-tuple-element.17), channel_id=1, source_target_pairs={{0,16},{1,17},{2,18},{3,19},{4,20},{5,21},{6,22},{7,23},{8,24},{9,... | collective-permute-start | bytes 49160 | tf_op jit(solution)/shard_map/ppermute | solution.py:251
  7.6 6.0 %collective-permute-start = (f32[32,128]{1,0:T(8,128)}, f32[32,128]{1,0:T(8,128)S(1)}, u32[]{:S(2)}, u32[]{:S(2)}) collective-permute-start(f32[32,128]{1,0:T(8,128)} %get-tuple-element.17), channel_id=1, source_target_pairs={{0,8},{1,9},{2,10},{3,11},{4,12},{5,13},{6,14},{7,15},{8,0},{9,1},... | collective-permute-start | bytes 49160 | tf_op jit(solution)/shard_map/ppermute | solution.py:251
  8.2 10.0 %collective-permute-start.6 = (bf16[32,1024]{1,0:T(8,128)(2,1)}, bf16[32,1024]{1,0:T(8,128)(2,1)S(1)}, u32[]{:S(2)}, u32[]{:S(2)}) collective-permute-start(bf16[32,1024]{1,0:T(8,128)(2,1)} %get-tuple-element.18), channel_id=1, source_target_pairs={{0,24},{1,25},{2,26},{3,27},{4,28},{5,29},{6,30},{7,31},{8,16},{9,... | collective-permute-start | bytes 196616 | tf_op jit(solution)/shard_map/ppermute | solution.py:251
  12.0 6.1 %collective-permute-start.5 = (bf16[32,1024]{1,0:T(8,128)(2,1)}, bf16[32,1024]{1,0:T(8,128)(2,1)S(1)}, u32[]{:S(2)}, u32[]{:S(2)}) collective-permute-start(bf16[32,1024]{1,0:T(8,128)(2,1)} %get-tuple-element.18), channel_id=1, source_target_pairs={{0,16},{1,17},{2,18},{3,19},{4,20},{5,21},{6,22},{7,23},{8,24},{9,... | collective-permute-start | bytes 196616 | tf_op jit(solution)/shard_map/ppermute | solution.py:251
  13.6 4.5 %collective-permute-start.4 = (bf16[32,1024]{1,0:T(8,128)(2,1)}, bf16[32,1024]{1,0:T(8,128)(2,1)S(1)}, u32[]{:S(2)}, u32[]{:S(2)}) collective-permute-start(bf16[32,1024]{1,0:T(8,128)(2,1)} %get-tuple-element.18), channel_id=1, source_target_pairs={{0,8},{1,9},{2,10},{3,11},{4,12},{5,13},{6,14},{7,15},{8,0},{9,1},... | collective-permute-start | bytes 196616 | tf_op jit(solution)/shard_map/ppermute | solution.py:251
  18.1 6.6 %collective-permute-start.8 = (bf16[128,1024]{1,0:T(8,128)(2,1)S(1)}, bf16[128,1024]{1,0:T(8,128)(2,1)S(1)}, u32[]{:S(2)}, u32[]{:S(2)}) collective-permute-start(bf16[128,1024]{1,0:T(8,128)(2,1)S(1)} %constant_dynamic-update-slice_fusion.4.refs_0_), channel_id=1, source_target_pairs={{0,2},{1,3},{2,0},{3,1},{4,6},{5,7},{6,4},{7,5},{8,10},{9,11},{10,... | collective-permute-start | bytes 786440 | tf_op jit(solution)/shard_map/ppermute | solution.py:251
  19.7 8.3 %collective-permute-start.7 = (bf16[128,1024]{1,0:T(8,128)(2,1)S(1)}, bf16[128,1024]{1,0:T(8,128)(2,1)S(1)}, u32[]{:S(2)}, u32[]{:S(2)}) collective-permute-start(bf16[128,1024]{1,0:T(8,128)(2,1)S(1)} %constant_dynamic-update-slice_fusion.4.refs_0_), channel_id=1, source_target_pairs={{0,4},{1,5},{2,6},{3,7},{4,0},{5,1},{6,2},{7,3},{8,12},{9,13},{10,... | collective-permute-start | bytes 786440 | tf_op jit(solution)/shard_map/ppermute | solution.py:251
  21.3 7.5 %collective-permute-start.3 = (f32[128,128]{1,0:T(8,128)S(1)}, f32[128,128]{1,0:T(8,128)S(1)}, u32[]{:S(2)}, u32[]{:S(2)}) collective-permute-start(f32[128,128]{1,0:T(8,128)S(1)} %constant_dynamic-update-slice_fusion.own), channel_id=1, source_target_pairs={{0,4},{1,5},{2,6},{3,7},{4,0},{5,1},{6,2},{7,3},{8,12},{9,13},{10,... | collective-permute-start | bytes 196616 | tf_op jit(solution)/shard_map/ppermute | solution.py:251
  21.8 14.7 %collective-permute-start.11 = (bf16[128,1024]{1,0:T(8,128)(2,1)S(1)}, bf16[128,1024]{1,0:T(8,128)(2,1)S(1)}, u32[]{:S(2)}, u32[]{:S(2)}) collective-permute-start(bf16[128,1024]{1,0:T(8,128)(2,1)S(1)} %constant_dynamic-update-slice_fusion.4.refs_0_), channel_id=1, source_target_pairs={{0,1},{1,0},{2,3},{3,2},{4,5},{5,4},{6,7},{7,6},{8,9},{9,8},{10,11... | collective-permute-start | bytes 786440 | tf_op jit(solution)/shard_map/ppermute | solution.py:251
  24.7 5.4 %collective-permute-start.9 = (bf16[64,1024]{1,0:T(8,128)(2,1)S(1)}, bf16[64,1024]{1,0:T(8,128)(2,1)S(1)}, u32[]{:S(2)}, u32[]{:S(2)}) collective-permute-start(bf16[64,1024]{1,0:T(8,128)(2,1)S(1)} %slice.53), channel_id=1, source_target_pairs={{0,4},{1,5},{2,6},{3,7},{4,0},{5,1},{6,2},{7,3},{8,12},{9,13},{10,... | collective-permute-start | bytes 393224 | tf_op jit(solution)/shard_map/ppermute | solution.py:251
  26.3 10.2 %collective-permute-start.13 = (bf16[128,1024]{1,0:T(8,128)(2,1)S(1)}, bf16[128,1024]{1,0:T(8,128)(2,1)S(1)}, u32[]{:S(2)}, u32[]{:S(2)}) collective-permute-start(bf16[128,1024]{1,0:T(8,128)(2,1)S(1)} %collective-permute-done.8.refs_2_), channel_id=1, source_target_pairs={{0,1},{1,0},{2,3},{3,2},{4,5},{5,4},{6,7},{7,6},{8,9},{9,8},{10,11... | collective-permute-start | bytes 786440 | tf_op jit(solution)/shard_map/ppermute | solution.py:251
  28.1 8.5 %collective-permute-start.12 = (bf16[128,1024]{1,0:T(8,128)(2,1)S(1)}, bf16[128,1024]{1,0:T(8,128)(2,1)S(1)}, u32[]{:S(2)}, u32[]{:S(2)}) collective-permute-start(bf16[128,1024]{1,0:T(8,128)(2,1)S(1)} %collective-permute-done.7.refs_1_), channel_id=1, source_target_pairs={{0,1},{1,0},{2,3},{3,2},{4,5},{5,4},{6,7},{7,6},{8,9},{9,8},{10,11... | collective-permute-start | bytes 786440 | tf_op jit(solution)/shard_map/ppermute | solution.py:251
  28.7 5.3 %collective-permute-start.10 = (bf16[64,1024]{1,0:T(8,128)(2,1)S(1)}, bf16[64,1024]{1,0:T(8,128)(2,1)S(1)}, u32[]{:S(2)}, u32[]{:S(2)}) collective-permute-start(bf16[64,1024]{1,0:T(8,128)(2,1)S(1)} %slice.54), channel_id=1, source_target_pairs={{0,2},{1,3},{2,0},{3,1},{4,6},{5,7},{6,4},{7,5},{8,10},{9,11},{10,... | collective-permute-start | bytes 393224 | tf_op jit(solution)/shard_map/ppermute | solution.py:251
  30.2 6.4 %collective-permute-start.14 = (bf16[64,1024]{1,0:T(8,128)(2,1)S(1)}, bf16[64,1024]{1,0:T(8,128)(2,1)S(1)}, u32[]{:S(2)}, u32[]{:S(2)}) collective-permute-start(bf16[64,1024]{1,0:T(8,128)(2,1)S(1)} %collective-permute-done.9.refs_3_), channel_id=1, source_target_pairs={{0,1},{1,0},{2,3},{3,2},{4,5},{5,4},{6,7},{7,6},{8,9},{9,8},{10,11... | collective-permute-start | bytes 393224 | tf_op jit(solution)/shard_map/ppermute | solution.py:251
  43.5 4.9 %collective-permute-start.22 = (f32[8,256]{1,0:T(8,128)}, f32[8,256]{1,0:T(8,128)S(1)}, u32[]{:S(2)}, u32[]{:S(2)}) collective-permute-start(f32[8,256]{1,0:T(8,128)} %get-tuple-element.20.refs_0_), channel_id=1, source_target_pairs={{0,7},{1,6},{2,5},{3,4},{4,3},{5,2},{6,1},{7,0},{8,15},{9,14},{10,... | collective-permute-start | bytes 24584 | tf_op jit(solution)/shard_map/ppermute | solution.py:251
  44.9 5.2 %collective-permute-start.21 = (f32[8,256]{1,0:T(8,128)}, f32[8,256]{1,0:T(8,128)S(1)}, u32[]{:S(2)}, u32[]{:S(2)}) collective-permute-start(f32[8,256]{1,0:T(8,128)} %get-tuple-element.20.refs_0_), channel_id=1, source_target_pairs={{0,6},{1,7},{2,4},{3,5},{4,2},{5,3},{6,0},{7,1},{8,14},{9,15},{10,... | collective-permute-start | bytes 24584 | tf_op jit(solution)/shard_map/ppermute | solution.py:251
  54.9 5.7 %collective-permute-start.25 = (f32[8,256]{1,0:T(8,128)}, f32[8,256]{1,0:T(8,128)S(1)}, u32[]{:S(2)}, u32[]{:S(2)}) collective-permute-start(f32[8,256]{1,0:T(8,128)} %shard_map.88.refs_0_), channel_id=1, source_target_pairs={{0,24},{1,25},{2,26},{3,27},{4,28},{5,29},{6,30},{7,31},{8,16},{9,... | collective-permute-start | bytes 24584 | tf_op jit(solution)/shard_map/ppermute | solution.py:251
  57.7 4.8 %collective-permute-start.24 = (f32[8,256]{1,0:T(8,128)}, f32[8,256]{1,0:T(8,128)S(1)}, u32[]{:S(2)}, u32[]{:S(2)}) collective-permute-start(f32[8,256]{1,0:T(8,128)} %shard_map.88.refs_0_), channel_id=1, source_target_pairs={{0,16},{1,17},{2,18},{3,19},{4,20},{5,21},{6,22},{7,23},{8,24},{9,... | collective-permute-start | bytes 24584 | tf_op jit(solution)/shard_map/ppermute | solution.py:251
  57.7 4.8 %collective-permute-start.23 = (f32[8,256]{1,0:T(8,128)}, f32[8,256]{1,0:T(8,128)S(1)}, u32[]{:S(2)}, u32[]{:S(2)}) collective-permute-start(f32[8,256]{1,0:T(8,128)} %shard_map.88.refs_0_), channel_id=1, source_target_pairs={{0,8},{1,9},{2,10},{3,11},{4,12},{5,13},{6,14},{7,15},{8,0},{9,1},... | collective-permute-start | bytes 24584 | tf_op jit(solution)/shard_map/ppermute | solution.py:251
  69.2 4.4 %collective-permute-start.31 = (bf16[128,1024]{1,0:T(8,128)(2,1)}, bf16[128,1024]{1,0:T(8,128)(2,1)S(1)}, u32[]{:S(2)}, u32[]{:S(2)}) collective-permute-start(bf16[128,1024]{1,0:T(8,128)(2,1)} %get-tuple-element.29), channel_id=1, source_target_pairs={{0,1},{1,0},{2,3},{3,2},{4,5},{5,4},{6,7},{7,6},{8,9},{9,8},{10,11... | collective-permute-start | bytes 786440 | tf_op jit(solution)/shard_map/ppermute | solution.py:251
  69.7 17.6 %collective-permute-start.26 = (bf16[128,1024]{1,0:T(8,128)(2,1)}, bf16[128,1024]{1,0:T(8,128)(2,1)S(1)}, u32[]{:S(2)}, u32[]{:S(2)}) collective-permute-start(bf16[128,1024]{1,0:T(8,128)(2,1)} %get-tuple-element.23), channel_id=1, source_target_pairs={{0,1},{1,0},{2,3},{3,2},{4,5},{5,4},{6,7},{7,6},{8,9},{9,8},{10,11... | collective-permute-start | bytes 786440 | tf_op jit(solution)/shard_map/ppermute | solution.py:251
  69.8 5.6 %collective-permute-start.29 = (bf16[128,1024]{1,0:T(8,128)(2,1)}, bf16[128,1024]{1,0:T(8,128)(2,1)S(1)}, u32[]{:S(2)}, u32[]{:S(2)}) collective-permute-start(bf16[128,1024]{1,0:T(8,128)(2,1)} %get-tuple-element.27), channel_id=1, source_target_pairs={{0,1},{1,0},{2,3},{3,2},{4,5},{5,4},{6,7},{7,6},{8,9},{9,8},{10,11... | collective-permute-start | bytes 786440 | tf_op jit(solution)/shard_map/ppermute | solution.py:251
  72.1 15.3 %collective-permute-start.28 = (bf16[64,1024]{1,0:T(8,128)(2,1)S(1)}, bf16[64,1024]{1,0:T(8,128)(2,1)S(1)}, u32[]{:S(2)}, u32[]{:S(2)}) collective-permute-start(bf16[64,1024]{1,0:T(8,128)(2,1)S(1)} %slice.74), channel_id=1, source_target_pairs={{0,4},{1,5},{2,6},{3,7},{4,0},{5,1},{6,2},{7,3},{8,12},{9,13},{10,... | collective-permute-start | bytes 393224 | tf_op jit(solution)/shard_map/ppermute | solution.py:251
  74.7 5.8 %collective-permute-start.32 = (bf16[64,1024]{1,0:T(8,128)(2,1)S(1)}, bf16[64,1024]{1,0:T(8,128)(2,1)S(1)}, u32[]{:S(2)}, u32[]{:S(2)}) collective-permute-start(bf16[64,1024]{1,0:T(8,128)(2,1)S(1)} %get-tuple-element.36), channel_id=1, source_target_pairs={{0,4},{1,5},{2,6},{3,7},{4,0},{5,1},{6,2},{7,3},{8,12},{9,13},{10,... | collective-permute-start | bytes 393224 | tf_op jit(solution)/shard_map/ppermute | solution.py:251
  76.5 10.8 %collective-permute-start.30 = (bf16[64,1024]{1,0:T(8,128)(2,1)S(1)}, bf16[64,1024]{1,0:T(8,128)(2,1)S(1)}, u32[]{:S(2)}, u32[]{:S(2)}) collective-permute-start(bf16[64,1024]{1,0:T(8,128)(2,1)S(1)} %slice.73), channel_id=1, source_target_pairs={{0,2},{1,3},{2,0},{3,1},{4,6},{5,7},{6,4},{7,5},{8,10},{9,11},{10,... | collective-permute-start | bytes 393224 | tf_op jit(solution)/shard_map/ppermute | solution.py:251
  78.4 7.4 %collective-permute-start.34 = (bf16[64,1024]{1,0:T(8,128)(2,1)S(1)}, bf16[64,1024]{1,0:T(8,128)(2,1)S(1)}, u32[]{:S(2)}, u32[]{:S(2)}) collective-permute-start(bf16[64,1024]{1,0:T(8,128)(2,1)S(1)} %get-tuple-element.37), channel_id=1, source_target_pairs={{0,2},{1,3},{2,0},{3,1},{4,6},{5,7},{6,4},{7,5},{8,10},{9,11},{10,... | collective-permute-start | bytes 393224 | tf_op jit(solution)/shard_map/ppermute | solution.py:251
  80.5 6.8 %collective-permute-start.33 = (bf16[64,1024]{1,0:T(8,128)(2,1)S(1)}, bf16[64,1024]{1,0:T(8,128)(2,1)S(1)}, u32[]{:S(2)}, u32[]{:S(2)}) collective-permute-start(bf16[64,1024]{1,0:T(8,128)(2,1)S(1)} %fusion.1), channel_id=1, source_target_pairs={{0,2},{1,3},{2,0},{3,1},{4,6},{5,7},{6,4},{7,5},{8,10},{9,11},{10,... | collective-permute-start | bytes 393224 | tf_op jit(solution)/shard_map/ppermute | solution.py:251
  85.9 5.0 %collective-permute-start.35 = (bf16[64,1024]{1,0:T(8,128)(2,1)S(1)}, bf16[64,1024]{1,0:T(8,128)(2,1)S(1)}, u32[]{:S(2)}, u32[]{:S(2)}) collective-permute-start(bf16[64,1024]{1,0:T(8,128)(2,1)S(1)} %fusion), channel_id=1, source_target_pairs={{0,4},{1,5},{2,6},{3,7},{4,0},{5,1},{6,2},{7,3},{8,12},{9,13},{10,... | collective-permute-start | bytes 393224 | tf_op jit(solution)/shard_map/ppermute | solution.py:251
  91.1 10.1 %collective-permute-start.38 = (bf16[32,1024]{1,0:T(8,128)(2,1)S(1)}, bf16[32,1024]{1,0:T(8,128)(2,1)S(1)}, u32[]{:S(2)}, u32[]{:S(2)}) collective-permute-start(bf16[32,1024]{1,0:T(8,128)(2,1)S(1)} %get-tuple-element.33), channel_id=1, source_target_pairs={{0,24},{1,25},{2,26},{3,27},{4,28},{5,29},{6,30},{7,31},{8,16},{9,... | collective-permute-start | bytes 196616 | tf_op jit(solution)/shard_map/ppermute | solution.py:251
  92.7 8.5 %collective-permute-start.37 = (bf16[32,1024]{1,0:T(8,128)(2,1)S(1)}, bf16[32,1024]{1,0:T(8,128)(2,1)S(1)}, u32[]{:S(2)}, u32[]{:S(2)}) collective-permute-start(bf16[32,1024]{1,0:T(8,128)(2,1)S(1)} %get-tuple-element.34), channel_id=1, source_target_pairs={{0,16},{1,17},{2,18},{3,19},{4,20},{5,21},{6,22},{7,23},{8,24},{9,... | collective-permute-start | bytes 196616 | tf_op jit(solution)/shard_map/ppermute | solution.py:251
  93.2 8.0 %collective-permute-start.36 = (bf16[32,1024]{1,0:T(8,128)(2,1)S(1)}, bf16[32,1024]{1,0:T(8,128)(2,1)S(1)}, u32[]{:S(2)}, u32[]{:S(2)}) collective-permute-start(bf16[32,1024]{1,0:T(8,128)(2,1)S(1)} %get-tuple-element.35), channel_id=1, source_target_pairs={{0,8},{1,9},{2,10},{3,11},{4,12},{5,13},{6,14},{7,15},{8,0},{9,1},... | collective-permute-start | bytes 196616 | tf_op jit(solution)/shard_map/ppermute | solution.py:251
  (33 other events, 130.1 us)

commit v2 on v0

v2 whole, which is shorter than its diff:
```python
import functools
import math

import jax
import jax.numpy as jnp
from jax import lax
from jax.experimental import pallas as pl
from jax.experimental.pallas import tpu as pltpu
from jax.sharding import PartitionSpec as P

CAP = 32
IDS = 128
grad_scale = 16384.0
AXES = ("dp", "vocab")
SMEM = pl.BlockSpec(memory_space=pltpu.SMEM)
VMEM = pl.BlockSpec(memory_space=pltpu.VMEM)
HBM = pl.BlockSpec(memory_space=pl.ANY)


def size_of(value):
    return math.prod(value.shape) * jnp.dtype(value.dtype).itemsize


def call(kernel, operands, in_specs, out_shape, out_specs, scratch=(), spare=4, flops=0):
    outs = jax.tree.leaves(out_shape)
    sized = [v for v, s in zip(operands, in_specs) if s is VMEM]
    sized += [v for v, s in zip(outs, jax.tree.leaves(out_specs)) if s is VMEM]
    held = [s for s in scratch if s.memory_space == pltpu.VMEM]
    total = sum(size_of(v) for v in sized) + sum(size_of(s) for s in held)
    return pl.pallas_call(
        kernel,
        out_shape=out_shape,
        in_specs=in_specs,
        out_specs=out_specs,
        scratch_shapes=scratch,
        compiler_params=pltpu.CompilerParams(vmem_limit_bytes=total + spare * 1024 * 1024),
        cost_estimate=pl.CostEstimate(
            flops=flops,
            bytes_accessed=sum(size_of(v) for v in list(operands) + outs),
            transcendentals=0,
        ),
    )(*operands)


def choose(mask):
    tokens = mask.shape[1]
    wide = jnp.broadcast_to(mask.astype(jnp.float32), (8, tokens))
    before = lax.broadcasted_iota(jnp.int32, (tokens, tokens), 0)
    after = lax.broadcasted_iota(jnp.int32, (tokens, tokens), 1)
    upto = (before <= after).astype(jnp.float32)
    slot = jnp.dot(
        wide.astype(jnp.bfloat16), upto.astype(jnp.bfloat16), preferred_element_type=jnp.float32
    )[0:1]
    grid = lax.broadcasted_iota(jnp.int32, (CAP, tokens), 0) + 1
    return (slot.astype(jnp.int32) == grid) & (mask == 1)


def pack_kernel(hidden, mask, target, turn, rows, chosen_out):
    width = hidden.shape[1]
    chosen = choose(mask[...])
    one_hot = chosen.astype(jnp.float32).astype(jnp.bfloat16)
    chosen_out[...] = one_hot
    packed = jnp.dot(one_hot, hidden[...], preferred_element_type=jnp.float32)
    packed = packed.astype(jnp.bfloat16)
    turns, targets = turn[...], target[...]
    fields = (
        mask[...],
        turns & 255,
        turns >> 8,
        targets & 255,
        (targets >> 8) & 255,
        targets >> 16,
    )
    lane = lax.broadcasted_iota(jnp.int32, (CAP, IDS), 1)
    table = jnp.zeros((CAP, IDS), jnp.float32)
    for place, field in enumerate(fields):
        picked = jnp.where(chosen, field.astype(jnp.float32), 0.0)
        table = jnp.where(lane == place, jnp.sum(picked, axis=1, keepdims=True), table)
    table = table.astype(jnp.bfloat16)
    for copy in range(rows.shape[0]):
        rows[copy, :, :width] = packed
        rows[copy, :, width:] = table


def info_kernel(where, own, other, advantages, info, held):
    half = own.shape[0]
    side = where[1]
    held[pl.ds(pl.multiple_of(side * half, half), half)] = own[...].astype(jnp.float32)
    held[pl.ds(pl.multiple_of((1 - side) * half, half), half)] = other[...].astype(jnp.float32)
    table = held[...]
    valid = table[:, 0:1]
    turn = table[:, 1:2] + 256.0 * table[:, 2:3]
    target = table[:, 3:4] + 256.0 * table[:, 4:5] + 65536.0 * table[:, 5:6]
    turns = advantages.shape[1]
    spot = lax.broadcasted_iota(jnp.int32, (table.shape[0], turns), 1)
    gain = jnp.sum(
        jnp.where(spot == turn.astype(jnp.int32), advantages[...], 0.0), axis=1, keepdims=True
    )
    weight = valid * gain / jnp.sum(valid)
    lane = lax.broadcasted_iota(jnp.int32, info.shape, 1)
    info[...] = jnp.where(lane == 0, weight, jnp.where(lane == 1, target, 0.0))


def logits_kernel(blocks, where, info, weight, *refs):
    pieces, (logits, stats) = refs[:2 * blocks], refs[2 * blocks:]
    rank, side, shard = where[0], where[1], where[2]
    width = weight.shape[0] // blocks
    total = None
    for block in range(blocks):
        start = pl.multiple_of((rank ^ block) * width, width)
        part = jnp.dot(
            jnp.concatenate([pieces[2 * block][...], pieces[2 * block + 1][...]], axis=0),
            weight[pl.ds(start, width), :],
            preferred_element_type=jnp.float32,
        )
        total = part if total is None else total + part
    half = total.shape[0] // 2
    logits[pl.ds(pl.multiple_of(side * half, half), half)] = total[:half]
    logits[pl.ds(pl.multiple_of((1 - side) * half, half), half)] = total[half:]
    total = logits[...]
    height, columns = total.shape
    target = info[:, 1:2].astype(jnp.int32) - shard * columns
    column = lax.broadcasted_iota(jnp.int32, total.shape, 1)
    hit = jnp.sum(jnp.where(column == target, total, 0.0), axis=1, keepdims=True)
    hit = jnp.sum(hit * info[:, 0:1])
    peak = jnp.max(total, axis=1, keepdims=True)
    mass = jnp.sum(jnp.exp(total - peak), axis=1, keepdims=True)
    lane = lax.broadcasted_iota(jnp.int32, (height, 128), 1)
    table = jnp.transpose(jnp.where(lane == 0, peak, mass))
    whole = (stats.shape[0], 1, height)
    stats[:, :, :height] = jnp.broadcast_to(table[0:1][None], whole)
    stats[:, :, height:2 * height] = jnp.broadcast_to(table[1:2][None], whole)
    stats[:, :, 2 * height:] = jnp.full((stats.shape[0], 1, 128), hit, jnp.float32)


def grad_kernel(blocks, where, info, logits, weight, stats, *refs):
    outs = refs[:2 * blocks]
    logit_grad, loss = refs[2 * blocks:]
    rank, side, shard = where[0], where[1], where[2]
    height, columns = logits.shape
    peaks, masses = stats[:, :, :height], stats[:, :, height:2 * height]
    peak = jnp.max(peaks, axis=0)
    mass = jnp.sum(masses * jnp.exp(peaks - peak[None]), axis=0)
    log_total = jnp.broadcast_to(peak + jnp.log(mass), (128, height))
    log_total = jnp.transpose(log_total)[:, 0:1]
    row_weight = info[:, 0:1]
    hit = jnp.sum(stats[:, :, 2 * height:], axis=0)[0, 0]
    loss[0, 0] = jnp.sum(row_weight * log_total) - hit
    target = info[:, 1:2].astype(jnp.int32) - shard * columns
    column = lax.broadcasted_iota(jnp.int32, logits.shape, 1)
    probability = jnp.exp(logits[...] - log_total)
    grad = (
        grad_scale * row_weight * (probability - (column == target).astype(jnp.float32))
    ).astype(jnp.bfloat16)
    half = height // 2
    logit_grad[pl.ds(pl.multiple_of(side * half, half), half)] = grad[:half]
    logit_grad[pl.ds(pl.multiple_of((1 - side) * half, half), half)] = grad[half:]
    grad = logit_grad[...]
    width = weight.shape[0] // blocks
    order = [b for b in range(blocks) if b % 2] + [b for b in range(blocks) if not b % 2]
    for block in order:
        start = pl.multiple_of((rank ^ block) * width, width)
        part = lax.dot_general(
            grad,
            weight[pl.ds(start, width), :],
            (((1,), (1,)), ((), ())),
            preferred_element_type=jnp.float32,
        )
        for y in range(2):
            out = outs[2 * block + y]
            out[...] = part[y * half:(y + 1) * half].astype(out.dtype)


def weight_kernel(blocks, where, logit_grad, *refs):
    pieces, (out, done, sems) = refs[:2 * blocks], refs[2 * blocks:]
    rank = where[0]
    width = pieces[0].shape[1]
    copies = []
    for block in range(blocks):
        done[block * width:(block + 1) * width] = lax.dot_general(
            jnp.concatenate([pieces[2 * block][...], pieces[2 * block + 1][...]], axis=0),
            logit_grad[...],
            (((0,), (0,)), ((), ())),
            preferred_element_type=jnp.float32,
        ).astype(jnp.bfloat16)
        start = pl.multiple_of((rank ^ block) * width, width)
        copy = pltpu.make_async_copy(
            done.at[pl.ds(block * width, width)], out.at[pl.ds(start, width)], sems.at[block]
        )
        copy.start()
        copies.append(copy)
    for copy in copies:
        copy.wait()


def unpack_kernel(chosen, parts, out):
    total = jnp.sum(parts[...].astype(jnp.float32), axis=0)
    out[...] = lax.dot_general(
        chosen[...],
        total.astype(jnp.bfloat16),
        (((0,), (0,)), ((), ())),
        preferred_element_type=jnp.float32,
    ).astype(jnp.bfloat16)


def body(dps, ranks, hidden, weight, loss_mask, target_ids, turn_ids, advantages):
    tokens, width = hidden.shape
    depth, columns = weight.shape
    zs, xs = dps // 2, ranks // 2
    half, total_rows = zs * CAP, dps * CAP
    bf16, f32 = jnp.bfloat16, jnp.float32
    shape = jax.ShapeDtypeStruct
    lines = [[2 * z + y for z in range(zs)] for y in range(2)]

    def send(value, y, x, core):
        near = 2 * x + core
        pairs = [
            (d * ranks + v, (d ^ y) * ranks + (v ^ near))
            for d in range(dps)
            for v in range(ranks)
        ]
        return lax.ppermute(value, AXES, pairs)

    def spread(value):
        return lax.all_to_all(value, "dp", 0, 0, axis_index_groups=lines)

    group, rank = lax.axis_index("dp"), lax.axis_index("vocab")
    where = jnp.stack([rank, group & 1, group * ranks + rank]).astype(jnp.int32)

    packed, chosen = call(
        pack_kernel,
        (
            hidden,
            loss_mask.reshape(1, tokens),
            target_ids.reshape(1, tokens),
            turn_ids.reshape(1, tokens),
        ),
        [VMEM] * 4,
        (shape((zs, CAP, width + IDS), bf16), shape((CAP, tokens), bf16)),
        (VMEM, VMEM),
    )

    line = spread(packed).reshape(half, width + IDS)
    own, own_ids = line[:, :width], line[:, width:]
    pieces = {(0, 0): own}
    for x in reversed(range(xs)):
        for y in (1, 0):
            if x or y:
                pieces[2 * x, y] = send(own, y, x, 0)
    other_ids = send(own_ids, 1, 0, 0)
    for b, y in list(pieces):
        pieces[b + 1, y] = send(pieces[b, y], 0, 0, 1)
    rows = [pieces[b, y] for b in range(ranks) for y in range(2)]

    info = call(
        info_kernel,
        (where, own_ids, other_ids, advantages.reshape(1, -1)),
        [SMEM] + [VMEM] * 3,
        shape((total_rows, 128), f32),
        VMEM,
        [pltpu.VMEM((total_rows, IDS), f32)],
    )
    flops = 2 * total_rows * depth * columns
    logits, stats = call(
        functools.partial(logits_kernel, ranks),
        (where, info, weight, *rows),
        [SMEM] + [VMEM] * (2 + len(rows)),
        (shape((total_rows, columns), f32), shape((dps * ranks, 1, 2 * total_rows + 128), f32)),
        (VMEM, VMEM),
        flops=flops,
    )

    stats = lax.all_to_all(stats, AXES, 0, 0)

    outs = [
        shape((half, width), bf16 if b % 2 else f32) for b in range(ranks) for y in range(2)
    ]
    *parts, logit_grad, loss = call(
        functools.partial(grad_kernel, ranks),
        (where, info, logits, weight, stats),
        [SMEM] + [VMEM] * 4,
        tuple(outs) + (shape((total_rows, columns), bf16), shape((1, 1), f32)),
        (VMEM,) * (len(outs) + 1) + (SMEM,),
        flops=flops,
    )

    sums = {}
    for x in reversed(range(xs)):
        for y in (1, 0):
            beside = send(parts[4 * x + 2 + y], 0, 0, 1)
            sums[x, y] = parts[4 * x + y] + beside.astype(f32)
    total = sums[0, 0]
    for x, y in sums:
        if x or y:
            total = total + send(sums[x, y].astype(bf16), y, x, 0).astype(f32)
    line = spread(total.astype(bf16).reshape(zs, CAP, width))

    weight_grad = call(
        functools.partial(weight_kernel, ranks),
        (where, logit_grad, *rows),
        [SMEM] + [VMEM] * (1 + len(rows)),
        shape((depth, columns), bf16),
        HBM,
        [pltpu.VMEM((depth, columns), bf16), pltpu.SemaphoreType.DMA((ranks,))],
        flops=flops,
    )
    hidden_grad = call(
        unpack_kernel, (chosen, line), [VMEM, VMEM], shape((tokens, width), bf16), VMEM
    )
    return loss[0, 0], hidden_grad, weight_grad


def solution(mesh):
    return jax.shard_map(
        functools.partial(body, mesh.shape["dp"], mesh.shape["vocab"]),
        mesh=mesh,
        in_specs=(P("dp", "vocab"), P(None, AXES), P("dp"), P("dp"), P("dp"), P()),
        out_specs=(P(), P("dp", "vocab"), P(None, AXES)),
        check_vma=False,
    )
```

time: 280 us -> 88.3 us (0.32)
  waiting for transfers between devices: 128 us -> 29.9 us
  blocking collectives: 113 us -> 27.5 us
  matrix products: 16.2 us -> 0 us
  between operations: 15.6 us -> 0.78 us
  starting transfers between devices: 0.12 us -> 13.2 us
  Pallas kernels: 0 us -> 9.62 us
  local copies, waits for them, and re-layouts: 0.86 us -> 5.77 us
  other arithmetic: 4.52 us -> 1.14 us
    reduce_scatter x2 -> x0, waiting for transfers between devices: 107 us -> none  [the longest x1 63.1 us: body(): lax.psum_scatter(column_part, 'dp', scatter_dimension=0, tiled=True)]
    psum x1 -> x0, blocking collectives: 39.9 us -> none  [body(): lax.psum((local_total * jnp.exp(local_peak - row_peak), target_part), ('d...]
    pmax x1 -> x0, blocking collectives: 39.3 us -> none  [body(): row_peak = lax.pmax(local_peak, ('dp', 'vocab'))]
    all_gather x2 -> x0, blocking collectives: 34.3 us -> none  [the longest x1 26.6 us: body(): lax.all_gather(packed_ids, 'dp', axis=0, tiled=True)]
    all_to_all x0 -> x2, blocking collectives: none -> 27.5 us  [the longest x1 15.7 us: spread(): return lax.all_to_all(value, 'dp', 0, 0, axis_index_groups=lines)]
    ppermute x0 -> x15, waiting for transfers between devices: none -> 23.7 us  [send(): return lax.ppermute(value, AXES, pairs)]
    all_gather x1 -> x0, waiting for transfers between devices: 21.2 us -> none  [body(): lax.all_gather(full_rows, 'dp', axis=0, tiled=True)]
    dot_general x6 -> x0, matrix products: 16.2 us -> none  [the longest x1 5.56 us: body(): lax.dot_general(logit_grad, weight, (((1,), (1,)), ((), ())), preferred_e...]
  transfers between devices with their start and end apart: 3 -> 16, of which waited for: 3 -> 8; matrix products, arithmetic and copies ran while one was open for 2% -> 0% of each run, Pallas kernels for 0% -> 5%
where the time goes in v2:
time: 88.3 us; the launch traced here: 87.9 us
  waiting for transfers between devices  29.9 us (34%)
  blocking collectives  27.5 us (31%)
  starting transfers between devices  13.2 us (15%)
  Pallas kernels  9.62 us (11%)
  local copies, waits for them, and re-layouts  5.77 us (7%)
  other arithmetic  1.14 us (1%)
    ppermute x15, waiting for transfers between devices, send(): return lax.ppermute(value, AXES, pairs)  23.7 us
    all_to_all x1, blocking collectives, spread(): return lax.all_to_all(value, 'dp', 0, 0, axis_index_groups=lines)  15.7 us
    all_to_all x1, blocking collectives, body(): stats = lax.all_to_all(stats, AXES, 0, 0)  11.8 us
    ppermute x15, starting transfers between devices, send(): return lax.ppermute(value, AXES, pairs)  9.75 us
    pallas_call x6, Pallas kernels, call(): pl.pallas_call(kernel, out_shape=out_shape, in_specs=in_specs, out_specs=...  9.62 us
    all_to_all x1, waiting for transfers between devices, spread(): return lax.all_to_all(value, 'dp', 0, 0, axis_index_groups=lines)  6.24 us
    unnamed x14, local copies, waits for them, and re-layouts  5.75 us
    all_to_all x1, starting transfers between devices, spread(): return lax.all_to_all(value, 'dp', 0, 0, axis_index_groups=lines)  3.41 us
  transfers between devices with their start and end apart: 16, of which 8 were waited for; matrix products, arithmetic and copies ran while one was open for 0% of the time, Pallas kernels for 5%

profile of v2, /device:TPU:0, one launch (start us, length us, event | category | flops | bytes accessed | tf_op | source)
XLA Modules:
  0.0 87.9 jit_solution(9074794259527414957)
XLA Ops:
  0.6 0.9 %copy-done.2 = bf16[128,1024]{1,0:T(8,128)(2,1)S(1)} copy-done((bf16[128,1024]{1,0:T(8,128)(2,1)S(1)}, bf16[128,1024]{1,0:T(8,128)(2,1)}, u32[]{:S(2)}) %copy-start.2) | copy-done | bytes 262168
  1.6 0.7 copy-done.3
  2.2 0.7 copy-done.4
  2.9 0.7 copy-done.5
  3.8 15.7 %all_to_all.15 = bf16[4,32,1152]{2,1,0:T(8,128)(2,1)S(1)} all-to-all(bf16[4,32,1152]{2,1,0:T(8,128)(2,1)S(1)} %get-tuple-element.17), channel_id=1, replica_groups={{0,8,16,24},{4,12,20,28},{1,9,17,25},{5,13,21,29},{2,10,18,26},{6,14,22..., dimensions={0} | all-to-all | bytes 589824 | tf_op jit(solution)/shard_map/all_to_all | solution.py:225
  19.6 2.5 %collective-permute-start.5 = (bf16[128,1024]{1,0:T(8,128)(2,1)S(1)}, bf16[128,1024]{1,0:T(8,128)(2,1)S(1)}, u32[]{:S(2)}, u32[]{:S(2)}) collective-permute-start(bf16[128,1024]{1,0:T(8,128)(2,1)S(1)} %slice.9.refs_0_), channel_id=1, source_target_pairs={{0,6},{1,7},{2,4},{3,5},{4,2},{5,3},{6,0},{7,1},{8,14},{9,15},{10,... | collective-permute-start | bytes 786440 | tf_op jit(solution)/shard_map/ppermute | solution.py:222
  22.1 0.5 collective-permute-start.4
  22.6 0.5 collective-permute-start.1
  23.1 6.3 %collective-permute-done.5.refs_5_ = bf16[128,1024]{1,0:T(8,128)(2,1)S(1)} collective-permute-done((bf16[128,1024]{1,0:T(8,128)(2,1)S(1)}, bf16[128,1024]{1,0:T(8,128)(2,1)S(1)}, u32[]{:S(2)}, u32[]{:S(2)}) %collective-permute-start.5) | collective-permute-done | bytes 262176 | tf_op jit(solution)/shard_map/ppermute | solution.py:222
  29.4 2.9 %collective-permute-done.4.refs_4_ = bf16[128,1024]{1,0:T(8,128)(2,1)S(1)} collective-permute-done((bf16[128,1024]{1,0:T(8,128)(2,1)S(1)}, bf16[128,1024]{1,0:T(8,128)(2,1)S(1)}, u32[]{:S(2)}, u32[]{:S(2)}) %collective-permute-start.4) | collective-permute-done | bytes 262176 | tf_op jit(solution)/shard_map/ppermute | solution.py:222
  32.3 0.5 collective-permute-start.3
  32.8 0.9 %collective-permute-start = (bf16[128,128]{1,0:T(8,128)(2,1)S(1)}, bf16[128,128]{1,0:T(8,128)(2,1)S(1)}, u32[]{:S(2)}, u32[]{:S(2)}) collective-permute-start(bf16[128,128]{1,0:T(8,128)(2,1)S(1)} %slice.8.own), channel_id=1, source_target_pairs={{0,4},{1,5},{2,6},{3,7},{4,0},{5,1},{6,2},{7,3},{8,12},{9,13},{10,... | collective-permute-start | bytes 98312 | tf_op jit(solution)/shard_map/ppermute | solution.py:222
  33.8 2.9 %collective-permute-done.other = bf16[128,128]{1,0:T(8,128)(2,1)S(1)} collective-permute-done((bf16[128,128]{1,0:T(8,128)(2,1)S(1)}, bf16[128,128]{1,0:T(8,128)(2,1)S(1)}, u32[]{:S(2)}, u32[]{:S(2)}) %collective-permute-start) | collective-permute-done | bytes 32800 | tf_op jit(solution)/shard_map/ppermute | solution.py:222
  36.7 0.7 copy-done.6
  37.3 0.9 %shard_map.86.info = f32[256,128]{1,0:T(8,128)S(1)} custom-call(s32[3]{0:T(128)S(1)} %pad_add_fusion.where, bf16[128,128]{1,0:T(8,128)(2,1)S(1)} %slice.8.own, bf16[128,128]{1,0:T(8,128)(2,1)S(1)} %collective-permute-done.other, f32[1,32]{1,0:T(1,128)S(1)} %bitcast.13), custom_call_target="tpu_custom_call" | custom-call | bytes 196748 | tf_op jit(solution)/shard_map/pallas_call | solution.py:30
  38.3 2.2 %copy-done = bf16[4096,512]{1,0:T(8,128)(2,1)S(1)} copy-done((bf16[4096,512]{1,0:T(8,128)(2,1)S(1)}, bf16[4096,512]{1,0:T(8,128)(2,1)}, u32[]{:S(2)}) %copy-start) | copy-done | bytes 4194328
  40.5 2.2 %shard_map.87 = (f32[256,512]{1,0:T(8,128)S(1)}, f32[32,1,640]{2,1,0:T(1,128)S(1)}) custom-call(s32[3]{0:T(128)S(1)} %pad_add_fusion.where, f32[256,128]{1,0:T(8,128)S(1)} %shard_map.86.info, bf16[4096,512]{1,0:T(8,128)(2,1)S(1)} %copy-done, bf16[128,1024]{1,0:T(8,128)(2,1)S(1)} %slice.9.refs_0_, bf16[128,1024]{1,0:T(8,128)(2,1)S(1)} %collective-permute-done.1.refs_1_, ...), custom_call_target="tpu_custom_call" | custom-call | flops 1073741824 | bytes 7028748 | tf_op jit(solution)/shard_map/pallas_call | solution.py:30
  42.7 11.8 %all_to_all.16.stats = f32[32,1,640]{2,1,0:T(1,128)S(1)} all-to-all(f32[32,1,640]{2,1,0:T(1,128)S(1)} %get-tuple-element.19), channel_id=1, replica_groups=mesh['dp'=8,'vocab'=4] {'dp','vocab'}, dimensions={0} | all-to-all | bytes 163840 | tf_op jit(solution)/shard_map/all_to_all | solution.py:273
  54.5 2.2 %shard_map.88 = (f32[128,1024]{1,0:T(8,128)S(1)}, f32[128,1024]{1,0:T(8,128)S(1)}, bf16[128,1024]{1,0:T(8,128)(2,1)S(1)}, bf16[128,1024]{1,0:T(8,128)(2,1)S(1)},...) custom-call(s32[3]{0:T(128)S(1)} %pad_add_fusion.where, ...), custom_call_target="tpu_custom_call" | custom-call | flops 1073741824 | bytes 8339472 | tf_op jit(solution)/shard_map/pallas_call | solution.py:30
  57.0 0.4 collective-permute-start.11
  57.9 0.5 collective-permute-done.9
  58.4 0.8 collective-permute-start.10
  59.3 1.4 %collective-permute-start.12 = (bf16[128,1024]{1,0:T(8,128)(2,1)S(1)}, bf16[128,1024]{1,0:T(8,128)(2,1)S(1)}, u32[]{:S(2)}, u32[]{:S(2)}) collective-permute-start(bf16[128,1024]{1,0:T(8,128)(2,1)S(1)} %add_convert_fusion.2), channel_id=1, source_target_pairs={{0,2},{1,3},{2,0},{3,1},{4,6},{5,7},{6,4},{7,5},{8,10},{9,11},{10,... | collective-permute-start | bytes 786440 | tf_op jit(solution)/shard_map/ppermute | solution.py:222
  60.8 1.5 %collective-permute-start.14 = (bf16[128,1024]{1,0:T(8,128)(2,1)S(1)}, bf16[128,1024]{1,0:T(8,128)(2,1)S(1)}, u32[]{:S(2)}, u32[]{:S(2)}) collective-permute-start(bf16[128,1024]{1,0:T(8,128)(2,1)S(1)} %add_convert_fusion.1), channel_id=1, source_target_pairs={{0,4},{1,5},{2,6},{3,7},{4,0},{5,1},{6,2},{7,3},{8,12},{9,13},{10,... | collective-permute-start | bytes 786440 | tf_op jit(solution)/shard_map/ppermute | solution.py:222
  62.2 6.3 %collective-permute-done.10 = bf16[128,1024]{1,0:T(8,128)(2,1)S(1)} collective-permute-done((bf16[128,1024]{1,0:T(8,128)(2,1)S(1)}, bf16[128,1024]{1,0:T(8,128)(2,1)S(1)}, u32[]{:S(2)}, u32[]{:S(2)}) %collective-permute-start.10) | collective-permute-done | bytes 262176 | tf_op jit(solution)/shard_map/ppermute | solution.py:222
  68.6 4.0 %collective-permute-done.12 = bf16[128,1024]{1,0:T(8,128)(2,1)S(1)} collective-permute-done((bf16[128,1024]{1,0:T(8,128)(2,1)S(1)}, bf16[128,1024]{1,0:T(8,128)(2,1)S(1)}, u32[]{:S(2)}, u32[]{:S(2)}) %collective-permute-start.12) | collective-permute-done | bytes 262176 | tf_op jit(solution)/shard_map/ppermute | solution.py:222
  72.6 0.8 collective-permute-done.14
  73.4 0.9 %add_convert_fusion = bf16[128,1024]{1,0:T(8,128)(2,1)} fusion(bf16[128,1024]{1,0:T(8,128)(2,1)S(1)} %collective-permute-done.14, bf16[128,1024]{1,0:T(8,128)(2,1)S(1)} %collective-permute-done.12, bf16[128,1024]{1,0:T(8,128)(2,1)S(1)} %collective-permute-done.10, f32[128,1024]{1,0:T(8,128)S(1)} %get-tuple-element.22, ...), kind=kLoop, calls=%fused_computation | loop fusion | flops 1179648 | bytes 1835008 | tf_op jit(solution)/shard_map/convert_element_type | solution.py:296
  74.3 3.4 %all-to-all-start.2 = ((bf16[4,32,1024]{2,1,0:T(8,128)(2,1)}), bf16[4,32,1024]{2,1,0:T(8,128)(2,1)S(1)}, u32[]{:S(2)}, u32[]{:S(2)}) async-start(bf16[4,32,1024]{2,1,0:T(8,128)(2,1)} %bitcast.9), calls=%async_computation.2 | async-start | bytes 524288 | tf_op jit(solution)/shard_map/all_to_all | solution.py:225
  77.7 3.1 %shard_map.90 = bf16[4096,512]{1,0:T(8,128)(2,1)} custom-call(s32[3]{0:T(128)S(1)} %pad_add_fusion.where, bf16[256,512]{1,0:T(8,128)(2,1)S(1)} %get-tuple-element.30.logit_grad, bf16[128,1024]{1,0:T(8,128)(2,1)S(1)} %slice.9.refs_0_, bf16[128,1024]{1,0:T(8,128)(2,1)S(1)} %collective-permute-done.1.refs_1_, ...), custom_call_target="tpu_custom_call" | custom-call | flops 1073741824 | bytes 6553612 | tf_op jit(solution)/shard_map/pallas_call | solution.py:30
  80.7 6.2 %all-to-all-done.2.parts = bf16[4,32,1024]{2,1,0:T(8,128)(2,1)S(1)} async-done(((bf16[4,32,1024]{2,1,0:T(8,128)(2,1)}), bf16[4,32,1024]{2,1,0:T(8,128)(2,1)S(1)}, u32[]{:S(2)}, u32[]{:S(2)}) %all-to-all-start.2) | async-done | bytes 262176 | tf_op jit(solution)/shard_map/all_to_all | solution.py:225
  87.0 0.9 %shard_map.89 = bf16[128,1024]{1,0:T(8,128)(2,1)} custom-call(bf16[32,128]{1,0:T(8,128)(2,1)S(1)} %get-tuple-element.21.chosen, bf16[4,32,1024]{2,1,0:T(8,128)(2,1)S(1)} %all-to-all-done.2.parts), custom_call_target="tpu_custom_call" | custom-call | bytes 532480 | tf_op jit(solution)/shard_map/pallas_call | solution.py:30
  (29 shorter events, 1.3 us)
Async XLA Ops:
  0.6 1.0 %copy-start.2 = (bf16[128,1024]{1,0:T(8,128)(2,1)S(1)}, bf16[128,1024]{1,0:T(8,128)(2,1)}, u32[]{:S(2)}) copy-start(bf16[128,1024]{1,0:T(8,128)(2,1)} %hidden.1) | copy-start | bytes 786436
  1.6 0.7 copy-start.3
  2.2 0.7 copy-start.4
  2.9 0.7 copy-start.5
  19.6 9.8 %collective-permute-start.5 = (bf16[128,1024]{1,0:T(8,128)(2,1)S(1)}, bf16[128,1024]{1,0:T(8,128)(2,1)S(1)}, u32[]{:S(2)}, u32[]{:S(2)}) collective-permute-start(bf16[128,1024]{1,0:T(8,128)(2,1)S(1)} %slice.9.refs_0_), channel_id=1, source_target_pairs={{0,6},{1,7},{2,4},{3,5},{4,2},{5,3},{6,0},{7,1},{8,14},{9,15},{10,... | collective-permute-start | bytes 786440 | tf_op jit(solution)/shard_map/ppermute | solution.py:222
  22.1 10.2 %collective-permute-start.4 = (bf16[128,1024]{1,0:T(8,128)(2,1)S(1)}, bf16[128,1024]{1,0:T(8,128)(2,1)S(1)}, u32[]{:S(2)}, u32[]{:S(2)}) collective-permute-start(bf16[128,1024]{1,0:T(8,128)(2,1)S(1)} %slice.9.refs_0_), channel_id=1, source_target_pairs={{0,2},{1,3},{2,0},{3,1},{4,6},{5,7},{6,4},{7,5},{8,10},{9,11},{10,... | collective-permute-start | bytes 786440 | tf_op jit(solution)/shard_map/ppermute | solution.py:222
  22.6 9.6 %collective-permute-start.1 = (bf16[128,1024]{1,0:T(8,128)(2,1)S(1)}, bf16[128,1024]{1,0:T(8,128)(2,1)S(1)}, u32[]{:S(2)}, u32[]{:S(2)}) collective-permute-start(bf16[128,1024]{1,0:T(8,128)(2,1)S(1)} %slice.9.refs_0_), channel_id=1, source_target_pairs={{0,4},{1,5},{2,6},{3,7},{4,0},{5,1},{6,2},{7,3},{8,12},{9,13},{10,... | collective-permute-start | bytes 786440 | tf_op jit(solution)/shard_map/ppermute | solution.py:222
  23.1 15.2 %collective-permute-start.2 = (bf16[128,1024]{1,0:T(8,128)(2,1)S(1)}, bf16[128,1024]{1,0:T(8,128)(2,1)S(1)}, u32[]{:S(2)}, u32[]{:S(2)}) collective-permute-start(bf16[128,1024]{1,0:T(8,128)(2,1)S(1)} %slice.9.refs_0_), channel_id=1, source_target_pairs={{0,1},{1,0},{2,3},{3,2},{4,5},{5,4},{6,7},{7,6},{8,9},{9,8},{10,11... | collective-permute-start | bytes 786440 | tf_op jit(solution)/shard_map/ppermute | solution.py:222
  29.4 8.9 %collective-permute-start.7 = (bf16[128,1024]{1,0:T(8,128)(2,1)S(1)}, bf16[128,1024]{1,0:T(8,128)(2,1)S(1)}, u32[]{:S(2)}, u32[]{:S(2)}) collective-permute-start(bf16[128,1024]{1,0:T(8,128)(2,1)S(1)} %collective-permute-done.5.refs_5_), channel_id=1, source_target_pairs={{0,1},{1,0},{2,3},{3,2},{4,5},{5,4},{6,7},{7,6},{8,9},{9,8},{10,11... | collective-permute-start | bytes 786440 | tf_op jit(solution)/shard_map/ppermute | solution.py:222
  32.2 6.1 %collective-permute-start.6 = (bf16[128,1024]{1,0:T(8,128)(2,1)S(1)}, bf16[128,1024]{1,0:T(8,128)(2,1)S(1)}, u32[]{:S(2)}, u32[]{:S(2)}) collective-permute-start(bf16[128,1024]{1,0:T(8,128)(2,1)S(1)} %collective-permute-done.4.refs_4_), channel_id=1, source_target_pairs={{0,1},{1,0},{2,3},{3,2},{4,5},{5,4},{6,7},{7,6},{8,9},{9,8},{10,11... | collective-permute-start | bytes 786440 | tf_op jit(solution)/shard_map/ppermute | solution.py:222
  32.3 6.1 %collective-permute-start.3 = (bf16[128,1024]{1,0:T(8,128)(2,1)S(1)}, bf16[128,1024]{1,0:T(8,128)(2,1)S(1)}, u32[]{:S(2)}, u32[]{:S(2)}) collective-permute-start(bf16[128,1024]{1,0:T(8,128)(2,1)S(1)} %collective-permute-done.1.refs_1_), channel_id=1, source_target_pairs={{0,1},{1,0},{2,3},{3,2},{4,5},{5,4},{6,7},{7,6},{8,9},{9,8},{10,11... | collective-permute-start | bytes 786440 | tf_op jit(solution)/shard_map/ppermute | solution.py:222
  32.8 3.9 %collective-permute-start = (bf16[128,128]{1,0:T(8,128)(2,1)S(1)}, bf16[128,128]{1,0:T(8,128)(2,1)S(1)}, u32[]{:S(2)}, u32[]{:S(2)}) collective-permute-start(bf16[128,128]{1,0:T(8,128)(2,1)S(1)} %slice.8.own), channel_id=1, source_target_pairs={{0,4},{1,5},{2,6},{3,7},{4,0},{5,1},{6,2},{7,3},{8,12},{9,13},{10,... | collective-permute-start | bytes 98312 | tf_op jit(solution)/shard_map/ppermute | solution.py:222
  36.7 0.7 copy-start.6
  38.3 2.2 %copy-start = (bf16[4096,512]{1,0:T(8,128)(2,1)S(1)}, bf16[4096,512]{1,0:T(8,128)(2,1)}, u32[]{:S(2)}) copy-start(bf16[4096,512]{1,0:T(8,128)(2,1)} %weight.3) | copy-start | bytes 12582916
  40.5 14.0 %copy-start.1 = (bf16[4096,512]{1,0:T(8,128)(2,1)S(1)}, bf16[4096,512]{1,0:T(8,128)(2,1)}, u32[]{:S(2)}) copy-start(bf16[4096,512]{1,0:T(8,128)(2,1)} %weight.3) | copy-start | bytes 12582916
  56.8 1.6 %collective-permute-start.9 = (bf16[128,1024]{1,0:T(8,128)(2,1)S(1)}, bf16[128,1024]{1,0:T(8,128)(2,1)S(1)}, u32[]{:S(2)}, u32[]{:S(2)}) collective-permute-start(bf16[128,1024]{1,0:T(8,128)(2,1)S(1)} %get-tuple-element.25), channel_id=1, source_target_pairs={{0,1},{1,0},{2,3},{3,2},{4,5},{5,4},{6,7},{7,6},{8,9},{9,8},{10,11... | collective-permute-start | bytes 786440 | tf_op jit(solution)/shard_map/ppermute | solution.py:222
  57.0 2.3 %collective-permute-start.11 = (bf16[128,1024]{1,0:T(8,128)(2,1)S(1)}, bf16[128,1024]{1,0:T(8,128)(2,1)S(1)}, u32[]{:S(2)}, u32[]{:S(2)}) collective-permute-start(bf16[128,1024]{1,0:T(8,128)(2,1)S(1)} %get-tuple-element.27), channel_id=1, source_target_pairs={{0,1},{1,0},{2,3},{3,2},{4,5},{5,4},{6,7},{7,6},{8,9},{9,8},{10,11... | collective-permute-start | bytes 786440 | tf_op jit(solution)/shard_map/ppermute | solution.py:222
  57.3 4.9 %collective-permute-start.8 = (bf16[128,1024]{1,0:T(8,128)(2,1)S(1)}, bf16[128,1024]{1,0:T(8,128)(2,1)S(1)}, u32[]{:S(2)}, u32[]{:S(2)}) collective-permute-start(bf16[128,1024]{1,0:T(8,128)(2,1)S(1)} %get-tuple-element.23), channel_id=1, source_target_pairs={{0,1},{1,0},{2,3},{3,2},{4,5},{5,4},{6,7},{7,6},{8,9},{9,8},{10,11... | collective-permute-start | bytes 786440 | tf_op jit(solution)/shard_map/ppermute | solution.py:222
  57.5 3.2 %collective-permute-start.13 = (bf16[128,1024]{1,0:T(8,128)(2,1)S(1)}, bf16[128,1024]{1,0:T(8,128)(2,1)S(1)}, u32[]{:S(2)}, u32[]{:S(2)}) collective-permute-start(bf16[128,1024]{1,0:T(8,128)(2,1)S(1)} %get-tuple-element.29), channel_id=1, source_target_pairs={{0,1},{1,0},{2,3},{3,2},{4,5},{5,4},{6,7},{7,6},{8,9},{9,8},{10,11... | collective-permute-start | bytes 786440 | tf_op jit(solution)/shard_map/ppermute | solution.py:222
  58.4 10.2 %collective-permute-start.10 = (bf16[128,1024]{1,0:T(8,128)(2,1)S(1)}, bf16[128,1024]{1,0:T(8,128)(2,1)S(1)}, u32[]{:S(2)}, u32[]{:S(2)}) collective-permute-start(bf16[128,1024]{1,0:T(8,128)(2,1)S(1)} %add_convert_fusion.3), channel_id=1, source_target_pairs={{0,6},{1,7},{2,4},{3,5},{4,2},{5,3},{6,0},{7,1},{8,14},{9,15},{10,... | collective-permute-start | bytes 786440 | tf_op jit(solution)/shard_map/ppermute | solution.py:222
  59.3 13.2 %collective-permute-start.12 = (bf16[128,1024]{1,0:T(8,128)(2,1)S(1)}, bf16[128,1024]{1,0:T(8,128)(2,1)S(1)}, u32[]{:S(2)}, u32[]{:S(2)}) collective-permute-start(bf16[128,1024]{1,0:T(8,128)(2,1)S(1)} %add_convert_fusion.2), channel_id=1, source_target_pairs={{0,2},{1,3},{2,0},{3,1},{4,6},{5,7},{6,4},{7,5},{8,10},{9,11},{10,... | collective-permute-start | bytes 786440 | tf_op jit(solution)/shard_map/ppermute | solution.py:222
  60.8 12.6 %collective-permute-start.14 = (bf16[128,1024]{1,0:T(8,128)(2,1)S(1)}, bf16[128,1024]{1,0:T(8,128)(2,1)S(1)}, u32[]{:S(2)}, u32[]{:S(2)}) collective-permute-start(bf16[128,1024]{1,0:T(8,128)(2,1)S(1)} %add_convert_fusion.1), channel_id=1, source_target_pairs={{0,4},{1,5},{2,6},{3,7},{4,0},{5,1},{6,2},{7,3},{8,12},{9,13},{10,... | collective-permute-start | bytes 786440 | tf_op jit(solution)/shard_map/ppermute | solution.py:222
  74.3 12.7 %all-to-all-start.2 = ((bf16[4,32,1024]{2,1,0:T(8,128)(2,1)}), bf16[4,32,1024]{2,1,0:T(8,128)(2,1)S(1)}, u32[]{:S(2)}, u32[]{:S(2)}) async-start(bf16[4,32,1024]{2,1,0:T(8,128)(2,1)} %bitcast.9), calls=%async_computation.2 | async-start | bytes 524288 | tf_op jit(solution)/shard_map/all_to_all | solution.py:225

commit v3 on v2

v3 whole, which is shorter than its diff:
```python
import functools
import math

import jax
import jax.numpy as jnp
from jax import lax
from jax.experimental import pallas as pl
from jax.experimental.pallas import tpu as pltpu
from jax.sharding import PartitionSpec as P

CAP = 32
MOST_VMEM = 56 * 1024 * 1024
IDS = 128
grad_scale = 16384.0
AXES = ("dp", "vocab")
SMEM = pl.BlockSpec(memory_space=pltpu.SMEM)
VMEM = pl.BlockSpec(memory_space=pltpu.VMEM)
HBM = pl.BlockSpec(memory_space=pltpu.HBM)
ANY = pl.BlockSpec(memory_space=pl.ANY)


def size_of(value):
    return math.prod(value.shape) * jnp.dtype(value.dtype).itemsize


def call(kernel, operands, in_specs, out_shape, out_specs, scratch=(), spare=4, flops=0):
    outs = jax.tree.leaves(out_shape)
    sized = [v for v, s in zip(operands, in_specs) if s is VMEM]
    sized += [v for v, s in zip(outs, jax.tree.leaves(out_specs)) if s is VMEM]
    held = [s for s in scratch if getattr(s, "memory_space", None) == pltpu.VMEM]
    total = sum(size_of(v) for v in sized) + sum(size_of(s) for s in held)
    return pl.pallas_call(
        kernel,
        out_shape=out_shape,
        in_specs=in_specs,
        out_specs=out_specs,
        scratch_shapes=scratch,
        compiler_params=pltpu.CompilerParams(vmem_limit_bytes=min(total + spare * 1024 * 1024, MOST_VMEM)),
        cost_estimate=pl.CostEstimate(
            flops=flops,
            bytes_accessed=sum(size_of(v) for v in list(operands) + outs),
            transcendentals=0,
        ),
    )(*operands)


def in_hbm(value):
    return pltpu.with_memory_space_constraint(value, pltpu.HBM)


def choose(mask):
    tokens = mask.shape[1]
    wide = jnp.broadcast_to(mask.astype(jnp.float32), (8, tokens))
    before = lax.broadcasted_iota(jnp.int32, (tokens, tokens), 0)
    after = lax.broadcasted_iota(jnp.int32, (tokens, tokens), 1)
    upto = (before <= after).astype(jnp.float32)
    slot = jnp.dot(
        wide.astype(jnp.bfloat16), upto.astype(jnp.bfloat16), preferred_element_type=jnp.float32
    )[0:1]
    grid = lax.broadcasted_iota(jnp.int32, (CAP, tokens), 0) + 1
    return (slot.astype(jnp.int32) == grid) & (mask == 1)


def pack_kernel(hidden_hbm, mask_hbm, target_hbm, turn_hbm, rows, chosen_out, *scratch):
    hidden, mask, target, turn, sems = scratch
    copies = []
    for place, (source, held) in enumerate(
        ((mask_hbm, mask), (target_hbm, target), (turn_hbm, turn), (hidden_hbm, hidden))
    ):
        copy = pltpu.make_async_copy(source, held, sems.at[place])
        copy.start()
        copies.append(copy)
    for copy in copies[:3]:
        copy.wait()
    width = hidden.shape[1]
    chosen = choose(mask[...])
    one_hot = chosen.astype(jnp.float32).astype(jnp.bfloat16)
    chosen_out[...] = one_hot
    turns, targets = turn[...], target[...]
    fields = (
        mask[...],
        turns & 255,
        turns >> 8,
        targets & 255,
        (targets >> 8) & 255,
        targets >> 16,
    )
    lane = lax.broadcasted_iota(jnp.int32, (CAP, IDS), 1)
    table = jnp.zeros((CAP, IDS), jnp.float32)
    for place, field in enumerate(fields):
        picked = jnp.where(chosen, field.astype(jnp.float32), 0.0)
        table = jnp.where(lane == place, jnp.sum(picked, axis=1, keepdims=True), table)
    rows[:, width:] = table.astype(jnp.bfloat16)
    copies[3].wait()
    packed = jnp.dot(one_hot, hidden[...], preferred_element_type=jnp.float32)
    rows[:, :width] = packed.astype(jnp.bfloat16)


def stage_kernel(after, weight, held, sem):
    copy = pltpu.make_async_copy(weight, held, sem)
    copy.start()
    copy.wait()


def info_kernel(own, other, advantages, info):
    start = own.shape[1] - IDS
    table = jnp.concatenate([own[:, start:], other[:, start:]], axis=0).astype(jnp.float32)
    valid = table[:, 0:1]
    turn = table[:, 1:2] + 256.0 * table[:, 2:3]
    target = table[:, 3:4] + 256.0 * table[:, 4:5] + 65536.0 * table[:, 5:6]
    turns = advantages.shape[1]
    spot = lax.broadcasted_iota(jnp.int32, (table.shape[0], turns), 1)
    gain = jnp.sum(
        jnp.where(spot == turn.astype(jnp.int32), advantages[...], 0.0), axis=1, keepdims=True
    )
    weight = valid * gain / jnp.sum(valid)
    lane = lax.broadcasted_iota(jnp.int32, info.shape, 1)
    info[...] = jnp.where(lane == 0, weight, jnp.where(lane == 1, target, 0.0))


def reorder(stats, position, groups):
    lanes = stats.shape[1]
    lane = lax.broadcasted_iota(jnp.int32, stats.shape, 1)
    bit = 1
    while bit < groups:
        size = CAP * bit
        swapped = jnp.where(
            (lane & size) != 0,
            pltpu.roll(stats, size, 1),
            pltpu.roll(stats, lanes - size, 1),
        )
        stats = jnp.where((position & bit) != 0, swapped, stats)
        bit *= 2
    return stats


def both_sides(pieces, block, width):
    pair = [pieces[2 * block + y][:, :width] for y in range(2)]
    return jnp.concatenate(pair, axis=0)


def logits_kernel(blocks, groups, where, info, weight, *refs):
    pieces, (logits, stats) = refs[:2 * blocks], refs[2 * blocks:]
    rank, position, shard = where[0], where[1], where[2]
    width = weight.shape[0] // blocks
    total = None
    for block in range(blocks):
        start = pl.multiple_of((rank ^ block) * width, width)
        part = jnp.dot(
            both_sides(pieces, block, width),
            weight[pl.ds(start, width), :],
            preferred_element_type=jnp.float32,
        )
        total = part if total is None else total + part
    logits[...] = total
    height, columns = total.shape
    target = info[:, 1:2].astype(jnp.int32) - shard * columns
    column = lax.broadcasted_iota(jnp.int32, total.shape, 1)
    hit = jnp.sum(jnp.where(column == target, total, 0.0), axis=1, keepdims=True)
    hit = jnp.sum(hit * info[:, 0:1])
    peak = jnp.max(total, axis=1, keepdims=True)
    mass = jnp.sum(jnp.exp(total - peak), axis=1, keepdims=True)
    lane = lax.broadcasted_iota(jnp.int32, (height, 128), 1)
    table = jnp.where(lane == 0, peak, jnp.where(lane == 1, mass, hit))
    stats[...] = reorder(jnp.transpose(table)[0:8], position, groups)


def merge(tables):
    peak = functools.reduce(jnp.maximum, [table[0:1] for table in tables])
    mass = sum(table[1:2] * jnp.exp(table[0:1] - peak) for table in tables)
    hit = sum(table[2:3] for table in tables)
    return peak, mass, hit


def merge_kernel(*refs):
    out = refs[-1]
    peak, mass, hit = merge([ref[...] for ref in refs[:-1]])
    row = lax.broadcasted_iota(jnp.int32, out.shape, 0)
    out[...] = jnp.where(row == 0, peak, jnp.where(row == 1, mass, hit))


def grad_kernel(count, blocks, groups, where, info, logits, weight, *refs):
    tables = [ref[...] for ref in refs[:count]]
    outs = refs[count:count + 2 * blocks]
    logit_grad, loss = refs[count + 2 * blocks:]
    rank, position, shard = where[0], where[1], where[2]
    height, columns = logits.shape
    peak, mass, hit = merge(tables)
    log_total = jnp.broadcast_to(peak + jnp.log(mass), (8, height))
    log_total = reorder(log_total, position, groups)
    log_total = jnp.transpose(jnp.concatenate([log_total] * 16, axis=0))[:, 0:1]
    row_weight = info[:, 0:1]
    loss[0, 0] = jnp.sum(row_weight * log_total) - hit[0, 0]
    target = info[:, 1:2].astype(jnp.int32) - shard * columns
    column = lax.broadcasted_iota(jnp.int32, logits.shape, 1)
    probability = jnp.exp(logits[...] - log_total)
    grad = (
        grad_scale * row_weight * (probability - (column == target).astype(jnp.float32))
    ).astype(jnp.bfloat16)
    logit_grad[...] = grad
    half = height // 2
    width = weight.shape[0] // blocks
    order = [b for b in range(blocks) if b % 2] + [b for b in range(blocks) if not b % 2]
    for block in order:
        start = pl.multiple_of((rank ^ block) * width, width)
        part = lax.dot_general(
            grad,
            weight[pl.ds(start, width), :],
            (((1,), (1,)), ((), ())),
            preferred_element_type=jnp.float32,
        )
        for y in range(2):
            out = outs[2 * block + y]
            out[...] = part[y * half:(y + 1) * half].astype(out.dtype)


def weight_kernel(blocks, where, after, logit_grad, *refs):
    pieces, (out, token, done, sems) = refs[:2 * blocks], refs[2 * blocks:]
    rank = where[0]
    width = done.shape[0] // blocks
    copies = []
    for block in range(blocks):
        done[block * width:(block + 1) * width] = lax.dot_general(
            both_sides(pieces, block, width),
            logit_grad[...],
            (((0,), (0,)), ((), ())),
            preferred_element_type=jnp.float32,
        ).astype(jnp.bfloat16)
        start = pl.multiple_of((rank ^ block) * width, width)
        copy = pltpu.make_async_copy(
            done.at[pl.ds(block * width, width)], out.at[pl.ds(start, width)], sems.at[block]
        )
        copy.start()
        copies.append(copy)
    for copy in copies:
        copy.wait()
    token[0, 0] = rank


def corner_kernel(count, token, kept, *refs):
    total = kept[...]
    for ref in refs[:count]:
        total = total + ref[...].astype(jnp.float32)
    for z, out in enumerate(refs[count:]):
        out[...] = total[z * CAP:(z + 1) * CAP].astype(out.dtype)


def unpack_kernel(chosen, *refs):
    out = refs[-1]
    total = sum(ref[...].astype(jnp.float32) for ref in refs[:-1])
    out[...] = lax.dot_general(
        chosen[...],
        total.astype(jnp.bfloat16),
        (((0,), (0,)), ((), ())),
        preferred_element_type=jnp.float32,
    ).astype(jnp.bfloat16)


def body(dps, ranks, hidden, weight, loss_mask, target_ids, turn_ids, advantages):
    tokens, width = hidden.shape
    depth, columns = weight.shape
    zs, xs = dps // 2, ranks // 2
    half, total_rows = zs * CAP, dps * CAP
    bf16, f32, i32 = jnp.bfloat16, jnp.float32, jnp.int32
    shape = jax.ShapeDtypeStruct
    square = [(y, x) for x in reversed(range(xs)) for y in (1, 0) if x or y]
    flops = 2 * total_rows * depth * columns

    def send(value, z=0, y=0, x=0, core=0):
        far, near = 2 * z + y, 2 * x + core
        pairs = [
            (d * ranks + v, (d ^ far) * ranks + (v ^ near))
            for d in range(dps)
            for v in range(ranks)
        ]
        return lax.ppermute(value, AXES, pairs)

    group, rank = lax.axis_index("dp"), lax.axis_index("vocab")
    position = (group & 1) * zs + (group >> 1)
    where = jnp.stack([rank, position, group * ranks + rank]).astype(i32)

    packed, chosen = call(
        pack_kernel,
        (
            in_hbm(hidden),
            in_hbm(loss_mask.reshape(1, tokens)),
            in_hbm(target_ids.reshape(1, tokens)),
            in_hbm(turn_ids.reshape(1, tokens)),
        ),
        [HBM] * 4,
        (shape((CAP, width + IDS), bf16), shape((CAP, tokens), bf16)),
        (VMEM, VMEM),
        [pltpu.VMEM((tokens, width), bf16)]
        + [pltpu.VMEM((1, tokens), i32)] * 3
        + [pltpu.SemaphoreType.DMA((4,))],
    )

    line = jnp.concatenate([packed] + [send(packed, z=z) for z in range(1, zs)], axis=0)
    own = line[:, :width]
    pieces = {(0, 0): line, (0, 1): send(line, y=1)}
    for y, x in square:
        if x:
            pieces[2 * x, y] = send(own, y=y, x=x)
    for b, y in list(pieces):
        pieces[b + 1, y] = send(pieces[b, y], core=1)
    rows = [pieces[b, y] for b in range(ranks) for y in range(2)]

    held = call(
        stage_kernel,
        (line, in_hbm(weight)),
        [ANY, HBM],
        shape((depth, columns), bf16),
        VMEM,
        [pltpu.SemaphoreType.DMA],
    )
    info = call(
        info_kernel,
        (pieces[0, 0], pieces[0, 1], advantages.reshape(1, -1)),
        [VMEM] * 3,
        shape((total_rows, 128), f32),
        VMEM,
    )
    logits, stats = call(
        functools.partial(logits_kernel, ranks, dps),
        (where, info, held, *rows),
        [SMEM] + [VMEM] * (2 + len(rows)),
        (shape((total_rows, columns), f32), shape((8, total_rows), f32)),
        (VMEM, VMEM),
        flops=flops,
    )

    for hops in ([{"core": 1}], [{"y": y, "x": x} for y, x in square]):
        tables = [stats] + [send(stats, **hop) for hop in hops]
        stats = call(
            merge_kernel, tables, [VMEM] * len(tables), shape((8, total_rows), f32), VMEM
        )
    tables = [stats] + [send(stats, z=z) for z in range(1, zs)]

    outs = [
        shape((half, width), bf16 if b % 2 else f32) for b in range(ranks) for y in range(2)
    ]
    *parts, logit_grad, loss = call(
        functools.partial(grad_kernel, len(tables), ranks, dps),
        (where, info, logits, held, *tables),
        [SMEM] + [VMEM] * (3 + len(tables)),
        tuple(outs) + (shape((total_rows, columns), bf16), shape((1, 1), f32)),
        (VMEM,) * (len(outs) + 1) + (SMEM,),
        flops=flops,
    )

    arrived, last = [], None
    for y, x in square:
        beside = send(parts[4 * x + 2 + y], core=1)
        last = (parts[4 * x + y] + beside.astype(f32)).astype(bf16)
        arrived.append(send(last, y=y, x=x))
    beside = send(parts[2], core=1)

    weight_grad, token = call(
        functools.partial(weight_kernel, ranks),
        (where, last, logit_grad, *rows),
        [SMEM, ANY] + [VMEM] * (1 + len(rows)),
        (shape((depth, columns), bf16), shape((1, 1), i32)),
        (HBM, SMEM),
        [pltpu.VMEM((depth, columns), bf16), pltpu.SemaphoreType.DMA((ranks,))],
        flops=flops,
    )
    ends = call(
        functools.partial(corner_kernel, 1 + len(arrived)),
        (token, parts[0], beside, *arrived),
        [SMEM] + [VMEM] * (2 + len(arrived)),
        tuple(shape((CAP, width), bf16 if z else f32) for z in range(zs)),
        (VMEM,) * zs,
    )
    ends = [ends[0]] + [send(ends[z], z=z) for z in range(1, zs)]
    hidden_grad = call(
        unpack_kernel,
        (chosen, *ends),
        [VMEM] * (1 + len(ends)),
        shape((tokens, width), bf16),
        VMEM,
    )
    return loss[0, 0], hidden_grad, weight_grad


def solution(mesh):
    return jax.shard_map(
        functools.partial(body, mesh.shape["dp"], mesh.shape["vocab"]),
        mesh=mesh,
        in_specs=(P("dp", "vocab"), P(None, AXES), P("dp"), P("dp"), P("dp"), P()),
        out_specs=(P(), P("dp", "vocab"), P(None, AXES)),
        check_vma=False,
    )
```

time: 88.3 us -> 78.5 us (0.89)
  blocking collectives: 27.5 us -> 0 us
  starting transfers between devices: 13.2 us -> 27.6 us
  waiting for transfers between devices: 29.9 us -> 36 us
  local copies, waits for them, and re-layouts: 5.77 us -> 0.07 us
  Pallas kernels: 9.62 us -> 13.6 us
  other arithmetic: 1.14 us -> 0.23 us
    all_to_all x2 -> x0, blocking collectives: 27.5 us -> none  [the longest x1 15.7 us: spread(): return lax.all_to_all(value, 'dp', 0, 0, axis_index_groups=lines)]
    ppermute x15 -> x27, starting transfers between devices: 9.75 us -> 27.6 us  [send(): return lax.ppermute(value, AXES, pairs)]
    ppermute x15 -> x27, waiting for transfers between devices: 23.7 us -> 36 us  [send(): return lax.ppermute(value, AXES, pairs)]
    all_to_all x1 -> x0, waiting for transfers between devices: 6.24 us -> none  [spread(): return lax.all_to_all(value, 'dp', 0, 0, axis_index_groups=lines)]
    unnamed x14 -> x5, local copies, waits for them, and re-layouts: 5.75 us -> 0.04 us
    pallas_call x6 -> x10, Pallas kernels: 9.62 us -> 13.6 us  [call(): pl.pallas_call(kernel, out_shape=out_shape, in_specs=in_specs, out_specs=...]
    all_to_all x1 -> x0, starting transfers between devices: 3.41 us -> none  [spread(): return lax.all_to_all(value, 'dp', 0, 0, axis_index_groups=lines)]
    convert_element_type x4 -> x3, other arithmetic: 1.06 us -> 0.16 us  [body(): last = (parts[4 * x + y] + beside.astype(f32)).astype(bf16)]
  transfers between devices with their start and end apart: 16 -> 27, of which waited for: 8 -> 15; matrix products, arithmetic and copies ran while one was open for 0% -> 0% of each run, Pallas kernels for 5% -> 8%
where the time goes in v3:
time: 78.5 us; the launch traced here: 78.3 us
  waiting for transfers between devices  36 us (46%)
  starting transfers between devices  27.6 us (35%)
  Pallas kernels  13.6 us (17%)
  between operations  0.81 us (1%)
    ppermute x27, waiting for transfers between devices, send(): return lax.ppermute(value, AXES, pairs)  36 us
    ppermute x27, starting transfers between devices, send(): return lax.ppermute(value, AXES, pairs)  27.6 us
    pallas_call x10, Pallas kernels, call(): pl.pallas_call(kernel, out_shape=out_shape, in_specs=in_specs, out_specs=...  13.6 us
  transfers between devices with their start and end apart: 27, of which 15 were waited for; matrix products, arithmetic and copies ran while one was open for 0% of the time, Pallas kernels for 8%

profile of v3, /device:TPU:0, one launch (start us, length us, event | category | flops | bytes accessed | tf_op | source)
XLA Modules:
  0.0 78.3 jit_solution(4027331507187922386)
XLA Ops:
  0.6 1.2 %shard_map.85 = (bf16[32,1152]{1,0:T(8,128)(2,1)S(1)}, bf16[32,128]{1,0:T(8,128)(2,1)S(1)}) custom-call(bf16[128,1024]{1,0:T(8,128)(2,1)} %hidden_hbm.1, s32[1,128]{1,0:T(1,128)} %bitcast.9, s32[1,128]{1,0:T(1,128)} %bitcast.10, s32[1,128]{1,0:T(1,128)} %bitcast.11), custom_call_target="tpu_custom_call" | custom-call | bytes 345600 | tf_op jit(solution)/shard_map/pallas_call | solution.py:32
  1.9 5.1 %collective-permute-start.2 = (bf16[32,1152]{1,0:T(8,128)(2,1)S(1)}, bf16[32,1152]{1,0:T(8,128)(2,1)S(1)}, u32[]{:S(2)}, u32[]{:S(2)}) collective-permute-start(bf16[32,1152]{1,0:T(8,128)(2,1)S(1)} %get-tuple-element.23), channel_id=1, source_target_pairs={{0,24},{1,25},{2,26},{3,27},{4,28},{5,29},{6,30},{7,31},{8,16},{9,... | collective-permute-start | bytes 221192 | tf_op jit(solution)/shard_map/ppermute | solution.py:276
  7.0 0.6 collective-permute-start
  7.6 4.1 %collective-permute-done = bf16[32,1152]{1,0:T(8,128)(2,1)S(1)} collective-permute-done((bf16[32,1152]{1,0:T(8,128)(2,1)S(1)}, bf16[32,1152]{1,0:T(8,128)(2,1)S(1)}, u32[]{:S(2)}, u32[]{:S(2)}) %collective-permute-start) | collective-permute-done | bytes 73760 | tf_op jit(solution)/shard_map/ppermute | solution.py:276
  11.7 1.5 %collective-permute-done.1 = bf16[32,1152]{1,0:T(8,128)(2,1)S(1)} collective-permute-done((bf16[32,1152]{1,0:T(8,128)(2,1)S(1)}, bf16[32,1152]{1,0:T(8,128)(2,1)S(1)}, u32[]{:S(2)}, u32[]{:S(2)}) %collective-permute-start.1) | collective-permute-done | bytes 73760 | tf_op jit(solution)/shard_map/ppermute | solution.py:276
  13.2 1.6 %collective-permute-start.3 = (bf16[128,1152]{1,0:T(8,128)(2,1)S(1)}, bf16[128,1152]{1,0:T(8,128)(2,1)S(1)}, u32[]{:S(2)}, u32[]{:S(2)}) collective-permute-start(bf16[128,1152]{1,0:T(8,128)(2,1)S(1)} %constant_dynamic-update-slice_fusion.own.after.refs_0_), channel_id=1, source_target_pairs={{0,4},{1,5},{2,6},{3,7},{4,0},{5,1},{6,2},{7,3},{8,12},{9,13},{10,... | collective-permute-start | bytes 884744 | tf_op jit(solution)/shard_map/ppermute | solution.py:276
  14.8 1.5 %collective-permute-start.7 = (bf16[128,1024]{1,0:T(8,128)(2,1)S(1)}, bf16[128,1024]{1,0:T(8,128)(2,1)S(1)}, u32[]{:S(2)}, u32[]{:S(2)}) collective-permute-start(bf16[128,1024]{1,0:T(8,128)(2,1)S(1)} %slice.4), channel_id=1, source_target_pairs={{0,6},{1,7},{2,4},{3,5},{4,2},{5,3},{6,0},{7,1},{8,14},{9,15},{10,... | collective-permute-start | bytes 786440 | tf_op jit(solution)/shard_map/ppermute | solution.py:276
  16.9 10.4 %collective-permute-done.3.other.refs_1_ = bf16[128,1152]{1,0:T(8,128)(2,1)S(1)} collective-permute-done((bf16[128,1152]{1,0:T(8,128)(2,1)S(1)}, bf16[128,1152]{1,0:T(8,128)(2,1)S(1)}, u32[]{:S(2)}, u32[]{:S(2)}) %collective-permute-start.3) | collective-permute-done | bytes 294944 | tf_op jit(solution)/shard_map/ppermute | solution.py:276
  28.0 2.2 %shard_map.87.weight = bf16[4096,512]{1,0:T(8,128)(2,1)S(1)} custom-call(bf16[128,1152]{1,0:T(8,128)(2,1)S(1)} %constant_dynamic-update-slice_fusion.own.after.refs_0_, bf16[4096,512]{1,0:T(8,128)(2,1)} %weight.1), custom_call_target="tpu_custom_call" | custom-call | bytes 8683520 | tf_op jit(solution)/shard_map/pallas_call | solution.py:32
  30.7 2.2 %shard_map.88 = (f32[256,512]{1,0:T(8,128)S(1)}, f32[8,256]{1,0:T(8,128)S(1)}) custom-call(s32[3]{0:T(128)S(1)} %pad_add_fusion.where, f32[256,128]{1,0:T(8,128)S(1)} %shard_map.86.info, bf16[4096,512]{1,0:T(8,128)(2,1)S(1)} %shard_map.87.weight, bf16[128,1152]{1,0:T(8,128)(2,1)S(1)} %constant_dynamic-update-slice_fusion.own.after.refs_0_, ...), custom_call_target="tpu_custom_call" | custom-call | flops 1073741824 | bytes 7086092 | tf_op jit(solution)/shard_map/pallas_call | solution.py:32
  33.4 0.8 %collective-permute-done.10.refs_1_ = f32[8,256]{1,0:T(8,128)S(1)} collective-permute-done((f32[8,256]{1,0:T(8,128)S(1)}, f32[8,256]{1,0:T(8,128)S(1)}, u32[]{:S(2)}, u32[]{:S(2)}) %collective-permute-start.10) | collective-permute-done | bytes 8224 | tf_op jit(solution)/shard_map/ppermute | solution.py:276
  34.3 1.8 %collective-permute-start.13 = (f32[8,256]{1,0:T(8,128)S(1)}, f32[8,256]{1,0:T(8,128)S(1)}, u32[]{:S(2)}, u32[]{:S(2)}) collective-permute-start(f32[8,256]{1,0:T(8,128)S(1)} %shard_map.89.refs_0_), channel_id=1, source_target_pairs={{0,4},{1,5},{2,6},{3,7},{4,0},{5,1},{6,2},{7,3},{8,12},{9,13},{10,... | collective-permute-start | bytes 24584 | tf_op jit(solution)/shard_map/ppermute | solution.py:276
  36.0 1.5 %collective-permute-start.12 = (f32[8,256]{1,0:T(8,128)S(1)}, f32[8,256]{1,0:T(8,128)S(1)}, u32[]{:S(2)}, u32[]{:S(2)}) collective-permute-start(f32[8,256]{1,0:T(8,128)S(1)} %shard_map.89.refs_0_), channel_id=1, source_target_pairs={{0,2},{1,3},{2,0},{3,1},{4,6},{5,7},{6,4},{7,5},{8,10},{9,11},{10,... | collective-permute-start | bytes 24584 | tf_op jit(solution)/shard_map/ppermute | solution.py:276
  38.0 1.7 %collective-permute-done.12.refs_2_ = f32[8,256]{1,0:T(8,128)S(1)} collective-permute-done((f32[8,256]{1,0:T(8,128)S(1)}, f32[8,256]{1,0:T(8,128)S(1)}, u32[]{:S(2)}, u32[]{:S(2)}) %collective-permute-start.12) | collective-permute-done | bytes 8224 | tf_op jit(solution)/shard_map/ppermute | solution.py:276
  39.7 2.4 %collective-permute-done.11.refs_1_ = f32[8,256]{1,0:T(8,128)S(1)} collective-permute-done((f32[8,256]{1,0:T(8,128)S(1)}, f32[8,256]{1,0:T(8,128)S(1)}, u32[]{:S(2)}, u32[]{:S(2)}) %collective-permute-start.11) | collective-permute-done | bytes 8224 | tf_op jit(solution)/shard_map/ppermute | solution.py:276
  42.1 1.7 %collective-permute-start.16 = (f32[8,256]{1,0:T(8,128)S(1)}, f32[8,256]{1,0:T(8,128)S(1)}, u32[]{:S(2)}, u32[]{:S(2)}) collective-permute-start(f32[8,256]{1,0:T(8,128)S(1)} %shard_map.90.refs_0_), channel_id=1, source_target_pairs={{0,24},{1,25},{2,26},{3,27},{4,28},{5,29},{6,30},{7,31},{8,16},{9,... | collective-permute-start | bytes 24584 | tf_op jit(solution)/shard_map/ppermute | solution.py:276
  43.8 2.8 %collective-permute-start.14 = (f32[8,256]{1,0:T(8,128)S(1)}, f32[8,256]{1,0:T(8,128)S(1)}, u32[]{:S(2)}, u32[]{:S(2)}) collective-permute-start(f32[8,256]{1,0:T(8,128)S(1)} %shard_map.90.refs_0_), channel_id=1, source_target_pairs={{0,8},{1,9},{2,10},{3,11},{4,12},{5,13},{6,14},{7,15},{8,0},{9,1},... | collective-permute-start | bytes 24584 | tf_op jit(solution)/shard_map/ppermute | solution.py:276
  46.6 1.1 %collective-permute-done.16.refs_3_ = f32[8,256]{1,0:T(8,128)S(1)} collective-permute-done((f32[8,256]{1,0:T(8,128)S(1)}, f32[8,256]{1,0:T(8,128)S(1)}, u32[]{:S(2)}, u32[]{:S(2)}) %collective-permute-start.16) | collective-permute-done | bytes 8224 | tf_op jit(solution)/shard_map/ppermute | solution.py:276
  47.6 0.7 collective-permute-done.15.refs_2_
  48.3 2.2 %shard_map.91 = (f32[128,1024]{1,0:T(8,128)S(1)}, f32[128,1024]{1,0:T(8,128)S(1)}, bf16[128,1024]{1,0:T(8,128)(2,1)S(1)}, bf16[128,1024]{1,0:T(8,128)(2,1)S(1)},...) custom-call(s32[3]{0:T(128)S(1)} %pad_add_fusion.where, ...), custom_call_target="tpu_custom_call" | custom-call | flops 1073741824 | bytes 8290320 | tf_op jit(solution)/shard_map/pallas_call | solution.py:32
  52.8 1.6 %collective-permute-start.20 = (bf16[128,1024]{1,0:T(8,128)(2,1)S(1)}, bf16[128,1024]{1,0:T(8,128)(2,1)S(1)}, u32[]{:S(2)}, u32[]{:S(2)}) collective-permute-start(bf16[128,1024]{1,0:T(8,128)(2,1)S(1)} %add_convert_fusion.1), channel_id=1, source_target_pairs={{0,6},{1,7},{2,4},{3,5},{4,2},{5,3},{6,0},{7,1},{8,14},{9,15},{10,... | collective-permute-start | bytes 786440 | tf_op jit(solution)/shard_map/ppermute | solution.py:276
  54.4 1.6 %collective-permute-start.22 = (bf16[128,1024]{1,0:T(8,128)(2,1)S(1)}, bf16[128,1024]{1,0:T(8,128)(2,1)S(1)}, u32[]{:S(2)}, u32[]{:S(2)}) collective-permute-start(bf16[128,1024]{1,0:T(8,128)(2,1)S(1)} %add_convert_fusion), channel_id=1, source_target_pairs={{0,2},{1,3},{2,0},{3,1},{4,6},{5,7},{6,4},{7,5},{8,10},{9,11},{10,... | collective-permute-start | bytes 786440 | tf_op jit(solution)/shard_map/ppermute | solution.py:276
  56.0 3.6 %shard_map.92 = (bf16[4096,512]{1,0:T(8,128)(2,1)}, s32[1,1]{1,0:T(1,128)}) custom-call(s32[3]{0:T(128)S(1)} %pad_add_fusion.where, bf16[128,1024]{1,0:T(8,128)(2,1)S(1)} %add_convert_fusion.2.after, bf16[256,512]{1,0:T(8,128)(2,1)S(1)} %get-tuple-element.30.logit_grad, bf16[128,1152]{1,0:T(8,128)(2,1)S(1)} %constant_dynamic-update-slice_fusion.own.after.refs_0_, ...), custom_call_target="tpu_custom_call" | custom-call | flops 1073741824 | bytes 6946832 | tf_op jit(solution)/shard_map/pallas_call | solution.py:32
  59.6 6.6 %collective-permute-done.23.refs_3_ = bf16[128,1024]{1,0:T(8,128)(2,1)S(1)} collective-permute-done((bf16[128,1024]{1,0:T(8,128)(2,1)S(1)}, bf16[128,1024]{1,0:T(8,128)(2,1)S(1)}, u32[]{:S(2)}, u32[]{:S(2)}) %collective-permute-start.23) | collective-permute-done | bytes 262176 | tf_op jit(solution)/shard_map/ppermute | solution.py:276
  66.2 1.4 %collective-permute-done.22.refs_2_ = bf16[128,1024]{1,0:T(8,128)(2,1)S(1)} collective-permute-done((bf16[128,1024]{1,0:T(8,128)(2,1)S(1)}, bf16[128,1024]{1,0:T(8,128)(2,1)S(1)}, u32[]{:S(2)}, u32[]{:S(2)}) %collective-permute-start.22) | collective-permute-done | bytes 262176 | tf_op jit(solution)/shard_map/ppermute | solution.py:276
  67.6 0.8 %shard_map.93 = (f32[32,1024]{1,0:T(8,128)S(1)}, bf16[32,1024]{1,0:T(8,128)(2,1)S(1)}, bf16[32,1024]{1,0:T(8,128)(2,1)S(1)}, bf16[32,1024]{1,0:T(8,128)(2,1)S(1)}) custom-call(s32[1,1]{1,0:T(1,128)} %get-tuple-element.31.token, f32[128,1024]{1,0:T(8,128)S(1)} %get-tuple-element.32.kept, bf16[128,1024]{1,0:T(8,128)(2,1)S(1)} %collective-permute-done.18.refs_0_, ...), custom_call_target="tpu_custom_call" | custom-call | bytes 1900548 | tf_op jit(solution)/shard_map/pallas_call | solution.py:32
  68.4 1.9 %collective-permute-start.24 = (bf16[32,1024]{1,0:T(8,128)(2,1)S(1)}, bf16[32,1024]{1,0:T(8,128)(2,1)S(1)}, u32[]{:S(2)}, u32[]{:S(2)}) collective-permute-start(bf16[32,1024]{1,0:T(8,128)(2,1)S(1)} %get-tuple-element.39), channel_id=1, source_target_pairs={{0,8},{1,9},{2,10},{3,11},{4,12},{5,13},{6,14},{7,15},{8,0},{9,1},... | collective-permute-start | bytes 196616 | tf_op jit(solution)/shard_map/ppermute | solution.py:276
  70.3 0.9 %collective-permute-start.25 = (bf16[32,1024]{1,0:T(8,128)(2,1)S(1)}, bf16[32,1024]{1,0:T(8,128)(2,1)S(1)}, u32[]{:S(2)}, u32[]{:S(2)}) collective-permute-start(bf16[32,1024]{1,0:T(8,128)(2,1)S(1)} %get-tuple-element.40), channel_id=1, source_target_pairs={{0,16},{1,17},{2,18},{3,19},{4,20},{5,21},{6,22},{7,23},{8,24},{9,... | collective-permute-start | bytes 196616 | tf_op jit(solution)/shard_map/ppermute | solution.py:276
  71.2 1.6 %collective-permute-start.26 = (bf16[32,1024]{1,0:T(8,128)(2,1)S(1)}, bf16[32,1024]{1,0:T(8,128)(2,1)S(1)}, u32[]{:S(2)}, u32[]{:S(2)}) collective-permute-start(bf16[32,1024]{1,0:T(8,128)(2,1)S(1)} %get-tuple-element.41), channel_id=1, source_target_pairs={{0,24},{1,25},{2,26},{3,27},{4,28},{5,29},{6,30},{7,31},{8,16},{9,... | collective-permute-start | bytes 196616 | tf_op jit(solution)/shard_map/ppermute | solution.py:276
  72.8 3.7 %collective-permute-done.25.refs_2_ = bf16[32,1024]{1,0:T(8,128)(2,1)S(1)} collective-permute-done((bf16[32,1024]{1,0:T(8,128)(2,1)S(1)}, bf16[32,1024]{1,0:T(8,128)(2,1)S(1)}, u32[]{:S(2)}, u32[]{:S(2)}) %collective-permute-start.25) | collective-permute-done | bytes 65568 | tf_op jit(solution)/shard_map/ppermute | solution.py:276
  76.5 0.8 %collective-permute-done.26.refs_3_ = bf16[32,1024]{1,0:T(8,128)(2,1)S(1)} collective-permute-done((bf16[32,1024]{1,0:T(8,128)(2,1)S(1)}, bf16[32,1024]{1,0:T(8,128)(2,1)S(1)}, u32[]{:S(2)}, u32[]{:S(2)}) %collective-permute-start.26) | collective-permute-done | bytes 65568 | tf_op jit(solution)/shard_map/ppermute | solution.py:276
  77.4 0.9 %shard_map.94 = bf16[128,1024]{1,0:T(8,128)(2,1)} custom-call(bf16[32,128]{1,0:T(8,128)(2,1)S(1)} %get-tuple-element.27.chosen, f32[32,1024]{1,0:T(8,128)S(1)} %get-tuple-element.38.refs_0_, bf16[32,1024]{1,0:T(8,128)(2,1)S(1)} %collective-permute-done.24.refs_1_, bf16[32,1024]{1,0:T(8,128)(2,1)S(1)} %collective-permute-done.25.refs_2_, ...), custom_call_target="tpu_custom_call" | custom-call | bytes 598016 | tf_op jit(solution)/shard_map/pallas_call | solution.py:32
  (43 shorter events, 5.1 us)
Async XLA Ops:
  1.9 11.3 %collective-permute-start.2 = (bf16[32,1152]{1,0:T(8,128)(2,1)S(1)}, bf16[32,1152]{1,0:T(8,128)(2,1)S(1)}, u32[]{:S(2)}, u32[]{:S(2)}) collective-permute-start(bf16[32,1152]{1,0:T(8,128)(2,1)S(1)} %get-tuple-element.23), channel_id=1, source_target_pairs={{0,24},{1,25},{2,26},{3,27},{4,28},{5,29},{6,30},{7,31},{8,16},{9,... | collective-permute-start | bytes 221192 | tf_op jit(solution)/shard_map/ppermute | solution.py:276
  7.0 6.2 %collective-permute-start.1 = (bf16[32,1152]{1,0:T(8,128)(2,1)S(1)}, bf16[32,1152]{1,0:T(8,128)(2,1)S(1)}, u32[]{:S(2)}, u32[]{:S(2)}) collective-permute-start(bf16[32,1152]{1,0:T(8,128)(2,1)S(1)} %get-tuple-element.23), channel_id=1, source_target_pairs={{0,16},{1,17},{2,18},{3,19},{4,20},{5,21},{6,22},{7,23},{8,24},{9,... | collective-permute-start | bytes 221192 | tf_op jit(solution)/shard_map/ppermute | solution.py:276
  7.0 4.7 %collective-permute-start = (bf16[32,1152]{1,0:T(8,128)(2,1)S(1)}, bf16[32,1152]{1,0:T(8,128)(2,1)S(1)}, u32[]{:S(2)}, u32[]{:S(2)}) collective-permute-start(bf16[32,1152]{1,0:T(8,128)(2,1)S(1)} %get-tuple-element.23), channel_id=1, source_target_pairs={{0,8},{1,9},{2,10},{3,11},{4,12},{5,13},{6,14},{7,15},{8,0},{9,1},... | collective-permute-start | bytes 221192 | tf_op jit(solution)/shard_map/ppermute | solution.py:276
  13.2 14.0 %collective-permute-start.3 = (bf16[128,1152]{1,0:T(8,128)(2,1)S(1)}, bf16[128,1152]{1,0:T(8,128)(2,1)S(1)}, u32[]{:S(2)}, u32[]{:S(2)}) collective-permute-start(bf16[128,1152]{1,0:T(8,128)(2,1)S(1)} %constant_dynamic-update-slice_fusion.own.after.refs_0_), channel_id=1, source_target_pairs={{0,4},{1,5},{2,6},{3,7},{4,0},{5,1},{6,2},{7,3},{8,12},{9,13},{10,... | collective-permute-start | bytes 884744 | tf_op jit(solution)/shard_map/ppermute | solution.py:276
  14.8 12.4 %collective-permute-start.7 = (bf16[128,1024]{1,0:T(8,128)(2,1)S(1)}, bf16[128,1024]{1,0:T(8,128)(2,1)S(1)}, u32[]{:S(2)}, u32[]{:S(2)}) collective-permute-start(bf16[128,1024]{1,0:T(8,128)(2,1)S(1)} %slice.4), channel_id=1, source_target_pairs={{0,6},{1,7},{2,4},{3,5},{4,2},{5,3},{6,0},{7,1},{8,14},{9,15},{10,... | collective-permute-start | bytes 786440 | tf_op jit(solution)/shard_map/ppermute | solution.py:276
  16.3 11.6 %collective-permute-start.6 = (bf16[128,1024]{1,0:T(8,128)(2,1)S(1)}, bf16[128,1024]{1,0:T(8,128)(2,1)S(1)}, u32[]{:S(2)}, u32[]{:S(2)}) collective-permute-start(bf16[128,1024]{1,0:T(8,128)(2,1)S(1)} %slice.4), channel_id=1, source_target_pairs={{0,2},{1,3},{2,0},{3,1},{4,6},{5,7},{6,4},{7,5},{8,10},{9,11},{10,... | collective-permute-start | bytes 786440 | tf_op jit(solution)/shard_map/ppermute | solution.py:276
  16.9 13.7 %collective-permute-start.4 = (bf16[128,1152]{1,0:T(8,128)(2,1)S(1)}, bf16[128,1152]{1,0:T(8,128)(2,1)S(1)}, u32[]{:S(2)}, u32[]{:S(2)}) collective-permute-start(bf16[128,1152]{1,0:T(8,128)(2,1)S(1)} %constant_dynamic-update-slice_fusion.own.after.refs_0_), channel_id=1, source_target_pairs={{0,1},{1,0},{2,3},{3,2},{4,5},{5,4},{6,7},{7,6},{8,9},{9,8},{10,11... | collective-permute-start | bytes 884744 | tf_op jit(solution)/shard_map/ppermute | solution.py:276
  27.3 3.4 %collective-permute-start.5 = (bf16[128,1152]{1,0:T(8,128)(2,1)S(1)}, bf16[128,1152]{1,0:T(8,128)(2,1)S(1)}, u32[]{:S(2)}, u32[]{:S(2)}) collective-permute-start(bf16[128,1152]{1,0:T(8,128)(2,1)S(1)} %collective-permute-done.3.other.refs_1_), channel_id=1, source_target_pairs={{0,1},{1,0},{2,3},{3,2},{4,5},{5,4},{6,7},{7,6},{8,9},{9,8},{10,11... | collective-permute-start | bytes 884744 | tf_op jit(solution)/shard_map/ppermute | solution.py:276
  27.3 3.4 %collective-permute-start.9 = (bf16[128,1024]{1,0:T(8,128)(2,1)S(1)}, bf16[128,1024]{1,0:T(8,128)(2,1)S(1)}, u32[]{:S(2)}, u32[]{:S(2)}) collective-permute-start(bf16[128,1024]{1,0:T(8,128)(2,1)S(1)} %collective-permute-done.7.refs_5_), channel_id=1, source_target_pairs={{0,1},{1,0},{2,3},{3,2},{4,5},{5,4},{6,7},{7,6},{8,9},{9,8},{10,11... | collective-permute-start | bytes 786440 | tf_op jit(solution)/shard_map/ppermute | solution.py:276
  27.9 2.7 %collective-permute-start.8 = (bf16[128,1024]{1,0:T(8,128)(2,1)S(1)}, bf16[128,1024]{1,0:T(8,128)(2,1)S(1)}, u32[]{:S(2)}, u32[]{:S(2)}) collective-permute-start(bf16[128,1024]{1,0:T(8,128)(2,1)S(1)} %collective-permute-done.6.refs_4_), channel_id=1, source_target_pairs={{0,1},{1,0},{2,3},{3,2},{4,5},{5,4},{6,7},{7,6},{8,9},{9,8},{10,11... | collective-permute-start | bytes 786440 | tf_op jit(solution)/shard_map/ppermute | solution.py:276
  28.0 2.2 %copy-start = (f32[32]{0:T(128)S(1)}, f32[32]{0:T(128)}, u32[]{:S(2)}) copy-start(f32[32]{0:T(128)} %param.11) | copy-start | bytes 388
  32.9 1.3 %collective-permute-start.10 = (f32[8,256]{1,0:T(8,128)S(1)}, f32[8,256]{1,0:T(8,128)S(1)}, u32[]{:S(2)}, u32[]{:S(2)}) collective-permute-start(f32[8,256]{1,0:T(8,128)S(1)} %get-tuple-element.25.refs_0_), channel_id=1, source_target_pairs={{0,1},{1,0},{2,3},{3,2},{4,5},{5,4},{6,7},{7,6},{8,9},{9,8},{10,11... | collective-permute-start | bytes 24584 | tf_op jit(solution)/shard_map/ppermute | solution.py:276
  34.3 3.7 %collective-permute-start.13 = (f32[8,256]{1,0:T(8,128)S(1)}, f32[8,256]{1,0:T(8,128)S(1)}, u32[]{:S(2)}, u32[]{:S(2)}) collective-permute-start(f32[8,256]{1,0:T(8,128)S(1)} %shard_map.89.refs_0_), channel_id=1, source_target_pairs={{0,4},{1,5},{2,6},{3,7},{4,0},{5,1},{6,2},{7,3},{8,12},{9,13},{10,... | collective-permute-start | bytes 24584 | tf_op jit(solution)/shard_map/ppermute | solution.py:276
  36.0 3.7 %collective-permute-start.12 = (f32[8,256]{1,0:T(8,128)S(1)}, f32[8,256]{1,0:T(8,128)S(1)}, u32[]{:S(2)}, u32[]{:S(2)}) collective-permute-start(f32[8,256]{1,0:T(8,128)S(1)} %shard_map.89.refs_0_), channel_id=1, source_target_pairs={{0,2},{1,3},{2,0},{3,1},{4,6},{5,7},{6,4},{7,5},{8,10},{9,11},{10,... | collective-permute-start | bytes 24584 | tf_op jit(solution)/shard_map/ppermute | solution.py:276
  37.5 4.5 %collective-permute-start.11 = (f32[8,256]{1,0:T(8,128)S(1)}, f32[8,256]{1,0:T(8,128)S(1)}, u32[]{:S(2)}, u32[]{:S(2)}) collective-permute-start(f32[8,256]{1,0:T(8,128)S(1)} %shard_map.89.refs_0_), channel_id=1, source_target_pairs={{0,6},{1,7},{2,4},{3,5},{4,2},{5,3},{6,0},{7,1},{8,14},{9,15},{10,... | collective-permute-start | bytes 24584 | tf_op jit(solution)/shard_map/ppermute | solution.py:276
  42.1 5.5 %collective-permute-start.16 = (f32[8,256]{1,0:T(8,128)S(1)}, f32[8,256]{1,0:T(8,128)S(1)}, u32[]{:S(2)}, u32[]{:S(2)}) collective-permute-start(f32[8,256]{1,0:T(8,128)S(1)} %shard_map.90.refs_0_), channel_id=1, source_target_pairs={{0,24},{1,25},{2,26},{3,27},{4,28},{5,29},{6,30},{7,31},{8,16},{9,... | collective-permute-start | bytes 24584 | tf_op jit(solution)/shard_map/ppermute | solution.py:276
  43.8 4.5 %collective-permute-start.15 = (f32[8,256]{1,0:T(8,128)S(1)}, f32[8,256]{1,0:T(8,128)S(1)}, u32[]{:S(2)}, u32[]{:S(2)}) collective-permute-start(f32[8,256]{1,0:T(8,128)S(1)} %shard_map.90.refs_0_), channel_id=1, source_target_pairs={{0,16},{1,17},{2,18},{3,19},{4,20},{5,21},{6,22},{7,23},{8,24},{9,... | collective-permute-start | bytes 24584 | tf_op jit(solution)/shard_map/ppermute | solution.py:276
  43.8 4.5 %collective-permute-start.14 = (f32[8,256]{1,0:T(8,128)S(1)}, f32[8,256]{1,0:T(8,128)S(1)}, u32[]{:S(2)}, u32[]{:S(2)}) collective-permute-start(f32[8,256]{1,0:T(8,128)S(1)} %shard_map.90.refs_0_), channel_id=1, source_target_pairs={{0,8},{1,9},{2,10},{3,11},{4,12},{5,13},{6,14},{7,15},{8,0},{9,1},... | collective-permute-start | bytes 24584 | tf_op jit(solution)/shard_map/ppermute | solution.py:276
  50.5 1.6 %collective-permute-start.17 = (bf16[128,1024]{1,0:T(8,128)(2,1)S(1)}, bf16[128,1024]{1,0:T(8,128)(2,1)S(1)}, u32[]{:S(2)}, u32[]{:S(2)}) collective-permute-start(bf16[128,1024]{1,0:T(8,128)(2,1)S(1)} %get-tuple-element.29), channel_id=1, source_target_pairs={{0,1},{1,0},{2,3},{3,2},{4,5},{5,4},{6,7},{7,6},{8,9},{9,8},{10,11... | collective-permute-start | bytes 786440 | tf_op jit(solution)/shard_map/ppermute | solution.py:276
  50.6 2.2 %collective-permute-start.19 = (bf16[128,1024]{1,0:T(8,128)(2,1)S(1)}, bf16[128,1024]{1,0:T(8,128)(2,1)S(1)}, u32[]{:S(2)}, u32[]{:S(2)}) collective-permute-start(bf16[128,1024]{1,0:T(8,128)(2,1)S(1)} %get-tuple-element.35), channel_id=1, source_target_pairs={{0,1},{1,0},{2,3},{3,2},{4,5},{5,4},{6,7},{7,6},{8,9},{9,8},{10,11... | collective-permute-start | bytes 786440 | tf_op jit(solution)/shard_map/ppermute | solution.py:276
  51.1 8.5 %collective-permute-start.18 = (bf16[128,1024]{1,0:T(8,128)(2,1)S(1)}, bf16[128,1024]{1,0:T(8,128)(2,1)S(1)}, u32[]{:S(2)}, u32[]{:S(2)}) collective-permute-start(bf16[128,1024]{1,0:T(8,128)(2,1)S(1)} %get-tuple-element.33), channel_id=1, source_target_pairs={{0,1},{1,0},{2,3},{3,2},{4,5},{5,4},{6,7},{7,6},{8,9},{9,8},{10,11... | collective-permute-start | bytes 786440 | tf_op jit(solution)/shard_map/ppermute | solution.py:276
  51.2 3.2 %collective-permute-start.21 = (bf16[128,1024]{1,0:T(8,128)(2,1)S(1)}, bf16[128,1024]{1,0:T(8,128)(2,1)S(1)}, u32[]{:S(2)}, u32[]{:S(2)}) collective-permute-start(bf16[128,1024]{1,0:T(8,128)(2,1)S(1)} %get-tuple-element.37), channel_id=1, source_target_pairs={{0,1},{1,0},{2,3},{3,2},{4,5},{5,4},{6,7},{7,6},{8,9},{9,8},{10,11... | collective-permute-start | bytes 786440 | tf_op jit(solution)/shard_map/ppermute | solution.py:276
  52.2 14.0 %collective-permute-start.23 = (bf16[128,1024]{1,0:T(8,128)(2,1)S(1)}, bf16[128,1024]{1,0:T(8,128)(2,1)S(1)}, u32[]{:S(2)}, u32[]{:S(2)}) collective-permute-start(bf16[128,1024]{1,0:T(8,128)(2,1)S(1)} %add_convert_fusion.2.after), channel_id=1, source_target_pairs={{0,4},{1,5},{2,6},{3,7},{4,0},{5,1},{6,2},{7,3},{8,12},{9,13},{10,... | collective-permute-start | bytes 786440 | tf_op jit(solution)/shard_map/ppermute | solution.py:276
  52.8 13.4 %collective-permute-start.20 = (bf16[128,1024]{1,0:T(8,128)(2,1)S(1)}, bf16[128,1024]{1,0:T(8,128)(2,1)S(1)}, u32[]{:S(2)}, u32[]{:S(2)}) collective-permute-start(bf16[128,1024]{1,0:T(8,128)(2,1)S(1)} %add_convert_fusion.1), channel_id=1, source_target_pairs={{0,6},{1,7},{2,4},{3,5},{4,2},{5,3},{6,0},{7,1},{8,14},{9,15},{10,... | collective-permute-start | bytes 786440 | tf_op jit(solution)/shard_map/ppermute | solution.py:276
  54.4 13.1 %collective-permute-start.22 = (bf16[128,1024]{1,0:T(8,128)(2,1)S(1)}, bf16[128,1024]{1,0:T(8,128)(2,1)S(1)}, u32[]{:S(2)}, u32[]{:S(2)}) collective-permute-start(bf16[128,1024]{1,0:T(8,128)(2,1)S(1)} %add_convert_fusion), channel_id=1, source_target_pairs={{0,2},{1,3},{2,0},{3,1},{4,6},{5,7},{6,4},{7,5},{8,10},{9,11},{10,... | collective-permute-start | bytes 786440 | tf_op jit(solution)/shard_map/ppermute | solution.py:276
  68.4 4.5 %collective-permute-start.24 = (bf16[32,1024]{1,0:T(8,128)(2,1)S(1)}, bf16[32,1024]{1,0:T(8,128)(2,1)S(1)}, u32[]{:S(2)}, u32[]{:S(2)}) collective-permute-start(bf16[32,1024]{1,0:T(8,128)(2,1)S(1)} %get-tuple-element.39), channel_id=1, source_target_pairs={{0,8},{1,9},{2,10},{3,11},{4,12},{5,13},{6,14},{7,15},{8,0},{9,1},... | collective-permute-start | bytes 196616 | tf_op jit(solution)/shard_map/ppermute | solution.py:276
  70.3 6.2 %collective-permute-start.25 = (bf16[32,1024]{1,0:T(8,128)(2,1)S(1)}, bf16[32,1024]{1,0:T(8,128)(2,1)S(1)}, u32[]{:S(2)}, u32[]{:S(2)}) collective-permute-start(bf16[32,1024]{1,0:T(8,128)(2,1)S(1)} %get-tuple-element.40), channel_id=1, source_target_pairs={{0,16},{1,17},{2,18},{3,19},{4,20},{5,21},{6,22},{7,23},{8,24},{9,... | collective-permute-start | bytes 196616 | tf_op jit(solution)/shard_map/ppermute | solution.py:276
  71.2 6.2 %collective-permute-start.26 = (bf16[32,1024]{1,0:T(8,128)(2,1)S(1)}, bf16[32,1024]{1,0:T(8,128)(2,1)S(1)}, u32[]{:S(2)}, u32[]{:S(2)}) collective-permute-start(bf16[32,1024]{1,0:T(8,128)(2,1)S(1)} %get-tuple-element.41), channel_id=1, source_target_pairs={{0,24},{1,25},{2,26},{3,27},{4,28},{5,29},{6,30},{7,31},{8,16},{9,... | collective-permute-start | bytes 196616 | tf_op jit(solution)/shard_map/ppermute | solution.py:276

commit v4 on v3

--- a/solution.py
+++ b/solution.py
@@ -96,15 +96,37 @@
     rows[:, :width] = packed.astype(jnp.bfloat16)
 
 
-def stage_kernel(after, weight, held, sem):
-    copy = pltpu.make_async_copy(weight, held, sem)
-    copy.start()
-    copy.wait()
-
-
-def info_kernel(own, other, advantages, info):
-    start = own.shape[1] - IDS
-    table = jnp.concatenate([own[:, start:], other[:, start:]], axis=0).astype(jnp.float32)
+def join_kernel(token, *refs):
+    blocks, (line, own, again) = refs[:-3], refs[-3:]
+    width, start = own.shape[1], 0
+    skip = line.shape[0] - own.shape[0]
+    for block in blocks:
+        end = start + block.shape[0]
+        line[start:end] = block[...]
+        if start >= skip:
+            own[start - skip:end - skip] = block[:, :width]
+        start = end
+    again[...] = line[:CAP]
+
+
+def stage_kernel(after, weight, held, token, sems):
+    count = sems.shape[0]
+    height = weight.shape[0] // count
+    copies = []
+    for place in range(count):
+        part = pl.ds(place * height, height)
+        copy = pltpu.make_async_copy(weight.at[part], held.at[part], sems.at[place])
+        copy.start()
+        copies.append(copy)
+    for copy in copies:
+        copy.wait()
+    token[0, 0] = 0
+
+
+def info_kernel(*refs):
+    advantages, info = refs[-2:]
+    start = refs[0].shape[1] - IDS
+    table = jnp.concatenate([ref[:, start:] for ref in refs[:-2]], axis=0).astype(jnp.float32)
     valid = table[:, 0:1]
     turn = table[:, 1:2] + 256.0 * table[:, 2:3]
     target = table[:, 3:4] + 256.0 * table[:, 4:5] + 65536.0 * table[:, 5:6]
@@ -134,20 +156,23 @@
     return stats
 
 
-def both_sides(pieces, block, width):
-    pair = [pieces[2 * block + y][:, :width] for y in range(2)]
-    return jnp.concatenate(pair, axis=0)
-
-
-def logits_kernel(blocks, groups, where, info, weight, *refs):
-    pieces, (logits, stats) = refs[:2 * blocks], refs[2 * blocks:]
+def all_rows(pieces, counts, block, width):
+    start = sum(counts[:block])
+    return jnp.concatenate(
+        [ref[:, :width] for ref in pieces[start:start + counts[block]]], axis=0
+    )
+
+
+def logits_kernel(counts, groups, where, info, weight, *refs):
+    blocks = len(counts)
+    pieces, (logits, stats) = refs[:-2], refs[-2:]
     rank, position, shard = where[0], where[1], where[2]
     width = weight.shape[0] // blocks
     total = None
     for block in range(blocks):
         start = pl.multiple_of((rank ^ block) * width, width)
         part = jnp.dot(
-            both_sides(pieces, block, width),
+            all_rows(pieces, counts, block, width),
             weight[pl.ds(start, width), :],
             preferred_element_type=jnp.float32,
         )
@@ -181,8 +206,7 @@
 
 def grad_kernel(count, blocks, groups, where, info, logits, weight, *refs):
     tables = [ref[...] for ref in refs[:count]]
-    outs = refs[count:count + 2 * blocks]
-    logit_grad, loss = refs[count + 2 * blocks:]
+    away, kept, logit_grad, loss = refs[count:count + 2], refs[count + 2:count + 4], *refs[count + 4:]
     rank, position, shard = where[0], where[1], where[2]
     height, columns = logits.shape
     peak, mass, hit = merge(tables)
@@ -198,7 +222,7 @@
         grad_scale * row_weight * (probability - (column == target).astype(jnp.float32))
     ).astype(jnp.bfloat16)
     logit_grad[...] = grad
-    half = height // 2
+    part_rows = height // 4
     width = weight.shape[0] // blocks
     order = [b for b in range(blocks) if b % 2] + [b for b in range(blocks) if not b % 2]
     for block in order:
@@ -209,19 +233,23 @@
             (((1,), (1,)), ((), ())),
             preferred_element_type=jnp.float32,
         )
-        for y in range(2):
-            out = outs[2 * block + y]
-            out[...] = part[y * half:(y + 1) * half].astype(out.dtype)
-
-
-def weight_kernel(blocks, where, after, logit_grad, *refs):
-    pieces, (out, token, done, sems) = refs[:2 * blocks], refs[2 * blocks:]
+        outs = away if block % 2 else kept
+        for quarter in range(4):
+            side, chunk = quarter // 2, quarter % 2
+            out = outs[chunk]
+            piece = part[quarter * part_rows:(quarter + 1) * part_rows]
+            out[block // 2 * 2 + side] = piece.astype(out.dtype)
+
+
+def weight_kernel(counts, where, after, logit_grad, *refs):
+    blocks = len(counts)
+    pieces, (out, token, done, sems) = refs[:-4], refs[-4:]
     rank = where[0]
     width = done.shape[0] // blocks
     copies = []
     for block in range(blocks):
         done[block * width:(block + 1) * width] = lax.dot_general(
-            both_sides(pieces, block, width),
+            all_rows(pieces, counts, block, width),
             logit_grad[...],
             (((0,), (0,)), ((), ())),
             preferred_element_type=jnp.float32,
@@ -237,12 +265,18 @@
     token[0, 0] = rank
 
 
+def pair_kernel(kept, beside, *outs):
+    for place, out in enumerate(reversed(outs)):
+        total = kept[place] + beside[place].astype(jnp.float32)
+        out[...] = total.astype(out.dtype)
+
+
 def corner_kernel(count, token, kept, *refs):
     total = kept[...]
     for ref in refs[:count]:
         total = total + ref[...].astype(jnp.float32)
-    for z, out in enumerate(refs[count:]):
-        out[...] = total[z * CAP:(z + 1) * CAP].astype(out.dtype)
+    for place, out in enumerate(refs[count:]):
+        out[...] = total[place * CAP:(place + 1) * CAP].astype(out.dtype)
 
 
 def unpack_kernel(chosen, *refs):
@@ -260,7 +294,7 @@
     tokens, width = hidden.shape
     depth, columns = weight.shape
     zs, xs = dps // 2, ranks // 2
-    half, total_rows = zs * CAP, dps * CAP
+    total_rows = dps * CAP
     bf16, f32, i32 = jnp.bfloat16, jnp.float32, jnp.int32
     shape = jax.ShapeDtypeStruct
     square = [(y, x) for x in reversed(range(xs)) for y in (1, 0) if x or y]
@@ -295,33 +329,50 @@
         + [pltpu.SemaphoreType.DMA((4,))],
     )
 
-    line = jnp.concatenate([packed] + [send(packed, z=z) for z in range(1, zs)], axis=0)
-    own = line[:, :width]
-    pieces = {(0, 0): line, (0, 1): send(line, y=1)}
-    for y, x in square:
-        if x:
-            pieces[2 * x, y] = send(own, y=y, x=x)
-    for b, y in list(pieces):
-        pieces[b + 1, y] = send(pieces[b, y], core=1)
-    rows = [pieces[b, y] for b in range(ranks) for y in range(2)]
-
-    held = call(
+    held, token = call(
         stage_kernel,
-        (line, in_hbm(weight)),
+        (packed, in_hbm(weight)),
         [ANY, HBM],
-        shape((depth, columns), bf16),
-        VMEM,
-        [pltpu.SemaphoreType.DMA],
-    )
+        (shape((depth, columns), bf16), shape((1, 1), i32)),
+        (VMEM, SMEM),
+        [pltpu.SemaphoreType.DMA((4,))],
+    )
+    pieces, before, again = {}, [], packed
+    for chunk in range(2):
+        near = range(chunk * zs // 2, (chunk + 1) * zs // 2)
+        blocks = [send(again, z=z) if z else packed for z in near]
+        line, own, again = call(
+            join_kernel,
+            (token, *before, *blocks),
+            [SMEM] + [VMEM] * len(before + blocks),
+            (
+                shape(((chunk + 1) * zs // 2 * CAP, width + IDS), bf16),
+                shape((zs // 2 * CAP, width), bf16),
+                shape((CAP, width + IDS), bf16),
+            ),
+            (VMEM,) * 3,
+        )
+        before = [line]
+        pieces[0, 1, chunk] = send(line[chunk * zs // 2 * CAP:], y=1)
+        for y, x in square:
+            if x:
+                pieces[2 * x, y, chunk] = send(own, y=y, x=x)
+    pieces[0, 0, 0] = line
+    for b, y, chunk in list(pieces):
+        pieces[b + 1, y, chunk] = send(pieces[b, y, chunk], core=1)
+    parted = [[pieces[k] for k in sorted(pieces) if k[0] == b] for b in range(ranks)]
+    counts = [len(part) for part in parted]
+    rows = [piece for part in parted for piece in part]
+
     info = call(
         info_kernel,
-        (pieces[0, 0], pieces[0, 1], advantages.reshape(1, -1)),
-        [VMEM] * 3,
+        (*parted[0], advantages.reshape(1, -1)),
+        [VMEM] * (counts[0] + 1),
         shape((total_rows, 128), f32),
         VMEM,
     )
     logits, stats = call(
-        functools.partial(logits_kernel, ranks, dps),
+        functools.partial(logits_kernel, counts, dps),
         (where, info, held, *rows),
         [SMEM] + [VMEM] * (2 + len(rows)),
         (shape((total_rows, columns), f32), shape((8, total_rows), f32)),
@@ -336,9 +387,9 @@
         )
     tables = [stats] + [send(stats, z=z) for z in range(1, zs)]
 
-    outs = [
-        shape((half, width), bf16 if b % 2 else f32) for b in range(ranks) for y in range(2)
-    ]
+    rows_part = total_rows // 4
+    whole = (ranks, rows_part, width)
+    outs = [shape(whole, bf16)] * 2 + [shape(whole, f32)] * 2
     *parts, logit_grad, loss = call(
         functools.partial(grad_kernel, len(tables), ranks, dps),
         (where, info, logits, held, *tables),
@@ -348,30 +399,46 @@
         flops=flops,
     )
 
-    arrived, last = [], None
-    for y, x in square:
-        beside = send(parts[4 * x + 2 + y], core=1)
-        last = (parts[4 * x + y] + beside.astype(f32)).astype(bf16)
-        arrived.append(send(last, y=y, x=x))
-    beside = send(parts[2], core=1)
-
-    weight_grad, token = call(
-        functools.partial(weight_kernel, ranks),
-        (where, last, logit_grad, *rows),
-        [SMEM, ANY] + [VMEM] * (1 + len(rows)),
-        (shape((depth, columns), bf16), shape((1, 1), i32)),
-        (HBM, SMEM),
-        [pltpu.VMEM((depth, columns), bf16), pltpu.SemaphoreType.DMA((ranks,))],
-        flops=flops,
-    )
-    ends = call(
-        functools.partial(corner_kernel, 1 + len(arrived)),
-        (token, parts[0], beside, *arrived),
-        [SMEM] + [VMEM] * (2 + len(arrived)),
-        tuple(shape((CAP, width), bf16 if z else f32) for z in range(zs)),
-        (VMEM,) * zs,
-    )
-    ends = [ends[0]] + [send(ends[z], z=z) for z in range(1, zs)]
+    ends, token = [None] * zs, jnp.zeros((1, 1), i32)
+    besides = [None, None]
+    for chunk in (1, 0):
+        besides[chunk] = send(parts[chunk], core=1)
+    sums = [None, None]
+    for chunk in (1, 0):
+        small = shape((rows_part, width), bf16)
+        *going, corner = call(
+            pair_kernel,
+            (parts[2 + chunk], besides[chunk]),
+            [VMEM, VMEM],
+            (small,) * (ranks - 1) + (shape((rows_part, width), f32),),
+            (VMEM,) * ranks,
+        )
+        arrived = []
+        for place, value in enumerate(going):
+            x, y = divmod(ranks - 1 - place, 2)
+            arrived.append(send(value, y=y, x=x))
+        sums[chunk] = (corner, *arrived)
+    for chunk in (1, 0):
+        near = chunk * zs // 2
+        parts_z = call(
+            functools.partial(corner_kernel, ranks - 1),
+            (token, *sums[chunk]),
+            [SMEM] + [VMEM] * ranks,
+            tuple(shape((CAP, width), bf16 if near + z else f32) for z in range(zs // 2)),
+            (VMEM,) * (zs // 2),
+        )
+        for z, value in enumerate(parts_z):
+            ends[near + z] = send(value, z=near + z) if near + z else value
+        if chunk:
+            weight_grad, token = call(
+                functools.partial(weight_kernel, counts),
+                (where, parts_z[0], logit_grad, *rows),
+                [SMEM, ANY] + [VMEM] * (1 + len(rows)),
+                (shape((depth, columns), bf16), shape((1, 1), i32)),
+                (HBM, SMEM),
+                [pltpu.VMEM((depth, columns), bf16), pltpu.SemaphoreType.DMA((ranks,))],
+                flops=flops,
+            )
     hidden_grad = call(
         unpack_kernel,
         (chosen, *ends),

time: 78.5 us -> 80.6 us (1.027)
  waiting for transfers between devices: 36 us -> 24.3 us
  starting transfers between devices: 27.6 us -> 34.8 us
  local copies, waits for them, and re-layouts: 0.07 us -> 4.22 us
  Pallas kernels: 13.6 us -> 16.3 us
    ppermute x27 -> x34, waiting for transfers between devices: 36 us -> 24.3 us  [send(): return lax.ppermute(value, AXES, pairs)]
    ppermute x27 -> x34, starting transfers between devices: 27.6 us -> 34.8 us  [send(): return lax.ppermute(value, AXES, pairs)]
    unnamed x5 -> x8, local copies, waits for them, and re-layouts: 0.04 us -> 4.2 us
    pallas_call x10 -> x15, Pallas kernels: 13.6 us -> 16.3 us  [call(): pl.pallas_call(kernel, out_shape=out_shape, in_specs=in_specs, out_specs=...]
  transfers between devices with their start and end apart: 27 -> 34, of which waited for: 15 -> 18; matrix products, arithmetic and copies ran while one was open for 0% -> 0% of each run, Pallas kernels for 8% -> 11%
where the time goes in v4:
time: 80.6 us; the launch traced here: 80.4 us
  starting transfers between devices  34.8 us (43%)
  waiting for transfers between devices  24.3 us (30%)
  Pallas kernels  16.3 us (20%)
  local copies, waits for them, and re-layouts  4.22 us (5%)
    ppermute x34, starting transfers between devices, send(): return lax.ppermute(value, AXES, pairs)  34.8 us
    ppermute x34, waiting for transfers between devices, send(): return lax.ppermute(value, AXES, pairs)  24.3 us
    pallas_call x15, Pallas kernels, call(): pl.pallas_call(kernel, out_shape=out_shape, in_specs=in_specs, out_specs=...  16.3 us
    unnamed x8, local copies, waits for them, and re-layouts  4.2 us
  transfers between devices with their start and end apart: 34, of which 18 were waited for; matrix products, arithmetic and copies ran while one was open for 0% of the time, Pallas kernels for 11%

profile of v4, /device:TPU:0, one launch (start us, length us, event | category | flops | bytes accessed | tf_op | source)
XLA Modules:
  0.0 80.4 jit_solution(12732633967751156286)
XLA Ops:
  0.6 1.2 %shard_map.85 = (bf16[32,1152]{1,0:T(8,128)(2,1)S(1)}, bf16[32,128]{1,0:T(8,128)(2,1)S(1)}) custom-call(bf16[128,1024]{1,0:T(8,128)(2,1)} %hidden_hbm.1, s32[1,128]{1,0:T(1,128)} %bitcast.9, s32[1,128]{1,0:T(1,128)} %bitcast.10, s32[1,128]{1,0:T(1,128)} %bitcast.11), custom_call_target="tpu_custom_call" | custom-call | bytes 345600 | tf_op jit(solution)/shard_map/pallas_call | solution.py:32
  1.9 3.1 %collective-permute-start = (bf16[32,1152]{1,0:T(8,128)(2,1)S(1)}, bf16[32,1152]{1,0:T(8,128)(2,1)S(1)}, u32[]{:S(2)}, u32[]{:S(2)}) collective-permute-start(bf16[32,1152]{1,0:T(8,128)(2,1)S(1)} %get-tuple-element.34.after.refs_0_), channel_id=1, source_target_pairs={{0,8},{1,9},{2,10},{3,11},{4,12},{5,13},{6,14},{7,15},{8,0},{9,1},... | collective-permute-start | bytes 221192 | tf_op jit(solution)/shard_map/ppermute | solution.py:310
  5.0 2.7 %shard_map.86 = (bf16[4096,512]{1,0:T(8,128)(2,1)S(1)}, s32[1,1]{1,0:T(1,128)}) custom-call(bf16[32,1152]{1,0:T(8,128)(2,1)S(1)} %get-tuple-element.34.after.refs_0_, bf16[4096,512]{1,0:T(8,128)(2,1)} %weight.1), custom_call_target="tpu_custom_call" | custom-call | bytes 8462340 | tf_op jit(solution)/shard_map/pallas_call | solution.py:32
  7.7 2.0 %copy-done = bf16[4096,512]{1,0:T(8,128)(2,1)} copy-done((bf16[4096,512]{1,0:T(8,128)(2,1)}, bf16[4096,512]{1,0:T(8,128)(2,1)S(1)}, u32[]{:S(2)}) %copy-start) | copy-done | bytes 4194328
  10.4 2.5 %collective-permute-start.2 = (bf16[32,1152]{1,0:T(8,128)(2,1)S(1)}, bf16[32,1152]{1,0:T(8,128)(2,1)S(1)}, u32[]{:S(2)}, u32[]{:S(2)}) collective-permute-start(bf16[32,1152]{1,0:T(8,128)(2,1)S(1)} %get-tuple-element.37), channel_id=1, source_target_pairs={{0,24},{1,25},{2,26},{3,27},{4,28},{5,29},{6,30},{7,31},{8,16},{9,... | collective-permute-start | bytes 221192 | tf_op jit(solution)/shard_map/ppermute | solution.py:310
  13.1 2.4 %collective-permute-start.10 = (bf16[64,1024]{1,0:T(8,128)(2,1)S(1)}, bf16[64,1024]{1,0:T(8,128)(2,1)S(1)}, u32[]{:S(2)}, u32[]{:S(2)}) collective-permute-start(bf16[64,1024]{1,0:T(8,128)(2,1)S(1)} %get-tuple-element.40), channel_id=1, source_target_pairs={{0,6},{1,7},{2,4},{3,5},{4,2},{5,3},{6,0},{7,1},{8,14},{9,15},{10,... | collective-permute-start | bytes 393224 | tf_op jit(solution)/shard_map/ppermute | solution.py:310
  17.5 2.4 %collective-permute-done.1.refs_1_ = bf16[32,1152]{1,0:T(8,128)(2,1)S(1)} collective-permute-done((bf16[32,1152]{1,0:T(8,128)(2,1)S(1)}, bf16[32,1152]{1,0:T(8,128)(2,1)S(1)}, u32[]{:S(2)}, u32[]{:S(2)}) %collective-permute-start.1) | collective-permute-done | bytes 73760 | tf_op jit(solution)/shard_map/ppermute | solution.py:310
  19.9 1.3 %shard_map.88 = (bf16[128,1152]{1,0:T(8,128)(2,1)S(1)}, bf16[64,1024]{1,0:T(8,128)(2,1)S(1)}, bf16[32,1152]{1,0:T(8,128)(2,1)}) custom-call(s32[1,1]{1,0:T(1,128)} %get-tuple-element.35.token, bf16[64,1152]{1,0:T(8,128)(2,1)S(1)} %get-tuple-element.36.refs_0_, bf16[32,1152]{1,0:T(8,128)(2,1)S(1)} %collective-permute-done.1.refs_1_, ...), custom_call_target="tpu_custom_call" | custom-call | bytes 794628 | tf_op jit(solution)/shard_map/pallas_call | solution.py:32
  21.2 2.4 %collective-permute-start.11 = (bf16[64,1024]{1,0:T(8,128)(2,1)S(1)}, bf16[64,1024]{1,0:T(8,128)(2,1)S(1)}, u32[]{:S(2)}, u32[]{:S(2)}) collective-permute-start(bf16[64,1024]{1,0:T(8,128)(2,1)S(1)} %get-tuple-element.41), channel_id=1, source_target_pairs={{0,6},{1,7},{2,4},{3,5},{4,2},{5,3},{6,0},{7,1},{8,14},{9,15},{10,... | collective-permute-start | bytes 393224 | tf_op jit(solution)/shard_map/ppermute | solution.py:310
  25.1 2.5 %collective-permute-done.11.refs_9_ = bf16[64,1024]{1,0:T(8,128)(2,1)S(1)} collective-permute-done((bf16[64,1024]{1,0:T(8,128)(2,1)S(1)}, bf16[64,1024]{1,0:T(8,128)(2,1)S(1)}, u32[]{:S(2)}, u32[]{:S(2)}) %collective-permute-start.11) | collective-permute-done | bytes 131104 | tf_op jit(solution)/shard_map/ppermute | solution.py:310
  27.6 2.7 %collective-permute-done.9.refs_7_ = bf16[64,1024]{1,0:T(8,128)(2,1)S(1)} collective-permute-done((bf16[64,1024]{1,0:T(8,128)(2,1)S(1)}, bf16[64,1024]{1,0:T(8,128)(2,1)S(1)}, u32[]{:S(2)}, u32[]{:S(2)}) %collective-permute-start.9) | collective-permute-done | bytes 131104 | tf_op jit(solution)/shard_map/ppermute | solution.py:310
  32.4 2.2 %copy-done.1 = bf16[4096,512]{1,0:T(8,128)(2,1)S(1)} copy-done((bf16[4096,512]{1,0:T(8,128)(2,1)S(1)}, bf16[4096,512]{1,0:T(8,128)(2,1)}, u32[]{:S(2)}) %copy-start.1) | copy-done | bytes 4194328
  34.6 2.2 %shard_map.90 = (f32[256,512]{1,0:T(8,128)S(1)}, f32[8,256]{1,0:T(8,128)S(1)}) custom-call(s32[3]{0:T(128)S(1)} %pad_add_fusion.where, f32[256,128]{1,0:T(8,128)S(1)} %shard_map.89.info, bf16[4096,512]{1,0:T(8,128)(2,1)S(1)} %copy-done.1, bf16[128,1152]{1,0:T(8,128)(2,1)S(1)} %get-tuple-element.38.refs_0_, ...), custom_call_target="tpu_custom_call" | custom-call | flops 1073741824 | bytes 7086092 | tf_op jit(solution)/shard_map/pallas_call | solution.py:32
  38.0 1.6 %collective-permute-start.19 = (f32[8,256]{1,0:T(8,128)S(1)}, f32[8,256]{1,0:T(8,128)S(1)}, u32[]{:S(2)}, u32[]{:S(2)}) collective-permute-start(f32[8,256]{1,0:T(8,128)S(1)} %shard_map.91.refs_0_), channel_id=1, source_target_pairs={{0,4},{1,5},{2,6},{3,7},{4,0},{5,1},{6,2},{7,3},{8,12},{9,13},{10,... | collective-permute-start | bytes 24584 | tf_op jit(solution)/shard_map/ppermute | solution.py:310
  41.7 1.5 %collective-permute-done.18.refs_2_ = f32[8,256]{1,0:T(8,128)S(1)} collective-permute-done((f32[8,256]{1,0:T(8,128)S(1)}, f32[8,256]{1,0:T(8,128)S(1)}, u32[]{:S(2)}, u32[]{:S(2)}) %collective-permute-start.18) | collective-permute-done | bytes 8224 | tf_op jit(solution)/shard_map/ppermute | solution.py:310
  43.3 1.8 %collective-permute-done.17.refs_1_ = f32[8,256]{1,0:T(8,128)S(1)} collective-permute-done((f32[8,256]{1,0:T(8,128)S(1)}, f32[8,256]{1,0:T(8,128)S(1)}, u32[]{:S(2)}, u32[]{:S(2)}) %collective-permute-start.17) | collective-permute-done | bytes 8224 | tf_op jit(solution)/shard_map/ppermute | solution.py:310
  45.1 2.0 %collective-permute-start.22 = (f32[8,256]{1,0:T(8,128)S(1)}, f32[8,256]{1,0:T(8,128)S(1)}, u32[]{:S(2)}, u32[]{:S(2)}) collective-permute-start(f32[8,256]{1,0:T(8,128)S(1)} %shard_map.92.refs_0_), channel_id=1, source_target_pairs={{0,24},{1,25},{2,26},{3,27},{4,28},{5,29},{6,30},{7,31},{8,16},{9,... | collective-permute-start | bytes 24584 | tf_op jit(solution)/shard_map/ppermute | solution.py:310
  47.1 2.4 %collective-permute-start.20 = (f32[8,256]{1,0:T(8,128)S(1)}, f32[8,256]{1,0:T(8,128)S(1)}, u32[]{:S(2)}, u32[]{:S(2)}) collective-permute-start(f32[8,256]{1,0:T(8,128)S(1)} %shard_map.92.refs_0_), channel_id=1, source_target_pairs={{0,8},{1,9},{2,10},{3,11},{4,12},{5,13},{6,14},{7,15},{8,0},{9,1},... | collective-permute-start | bytes 24584 | tf_op jit(solution)/shard_map/ppermute | solution.py:310
  51.7 2.2 %shard_map.93 = (bf16[4,64,1024]{2,1,0:T(8,128)(2,1)S(1)}, bf16[4,64,1024]{2,1,0:T(8,128)(2,1)S(1)}, f32[4,64,1024]{2,1,0:T(8,128)S(1)}, f32[4,64,1024]{2,1,0:T(...) custom-call(s32[3]{0:T(128)S(1)} %pad_add_fusion.where, f32[256,128]{1,0:T(8,128)S(1)} %shard_map.89.info, ...), custom_call_target="tpu_custom_call" | custom-call | flops 1073741824 | bytes 8290320 | tf_op jit(solution)/shard_map/pallas_call | solution.py:32
  54.4 1.4 %collective-permute-done.23.beside = bf16[4,64,1024]{2,1,0:T(8,128)(2,1)S(1)} collective-permute-done((bf16[4,64,1024]{2,1,0:T(8,128)(2,1)S(1)}, bf16[4,64,1024]{2,1,0:T(8,128)(2,1)S(1)}, u32[]{:S(2)}, u32[]{:S(2)}) %collective-permute-start.23) | collective-permute-done | bytes 524320 | tf_op jit(solution)/shard_map/ppermute | solution.py:310
  55.9 1.5 %collective-permute-start.24 = (bf16[64,1024]{1,0:T(8,128)(2,1)S(1)}, bf16[64,1024]{1,0:T(8,128)(2,1)S(1)}, u32[]{:S(2)}, u32[]{:S(2)}) collective-permute-start(bf16[64,1024]{1,0:T(8,128)(2,1)S(1)} %get-tuple-element.49), channel_id=1, source_target_pairs={{0,6},{1,7},{2,4},{3,5},{4,2},{5,3},{6,0},{7,1},{8,14},{9,15},{10,... | collective-permute-start | bytes 393224 | tf_op jit(solution)/shard_map/ppermute | solution.py:310
  57.4 1.3 %collective-permute-start.25 = (bf16[64,1024]{1,0:T(8,128)(2,1)S(1)}, bf16[64,1024]{1,0:T(8,128)(2,1)S(1)}, u32[]{:S(2)}, u32[]{:S(2)}) collective-permute-start(bf16[64,1024]{1,0:T(8,128)(2,1)S(1)} %get-tuple-element.50), channel_id=1, source_target_pairs={{0,2},{1,3},{2,0},{3,1},{4,6},{5,7},{6,4},{7,5},{8,10},{9,11},{10,... | collective-permute-start | bytes 393224 | tf_op jit(solution)/shard_map/ppermute | solution.py:310
  59.6 1.5 %collective-permute-start.28 = (bf16[64,1024]{1,0:T(8,128)(2,1)S(1)}, bf16[64,1024]{1,0:T(8,128)(2,1)S(1)}, u32[]{:S(2)}, u32[]{:S(2)}) collective-permute-start(bf16[64,1024]{1,0:T(8,128)(2,1)S(1)} %get-tuple-element.58), channel_id=1, source_target_pairs={{0,6},{1,7},{2,4},{3,5},{4,2},{5,3},{6,0},{7,1},{8,14},{9,15},{10,... | collective-permute-start | bytes 393224 | tf_op jit(solution)/shard_map/ppermute | solution.py:310
  61.1 1.3 %collective-permute-start.29 = (bf16[64,1024]{1,0:T(8,128)(2,1)S(1)}, bf16[64,1024]{1,0:T(8,128)(2,1)S(1)}, u32[]{:S(2)}, u32[]{:S(2)}) collective-permute-start(bf16[64,1024]{1,0:T(8,128)(2,1)S(1)} %get-tuple-element.59), channel_id=1, source_target_pairs={{0,2},{1,3},{2,0},{3,1},{4,6},{5,7},{6,4},{7,5},{8,10},{9,11},{10,... | collective-permute-start | bytes 393224 | tf_op jit(solution)/shard_map/ppermute | solution.py:310
  63.2 1.2 %collective-permute-start.30 = (bf16[64,1024]{1,0:T(8,128)(2,1)S(1)}, bf16[64,1024]{1,0:T(8,128)(2,1)S(1)}, u32[]{:S(2)}, u32[]{:S(2)}) collective-permute-start(bf16[64,1024]{1,0:T(8,128)(2,1)S(1)} %get-tuple-element.60), channel_id=1, source_target_pairs={{0,4},{1,5},{2,6},{3,7},{4,0},{5,1},{6,2},{7,3},{8,12},{9,13},{10,... | collective-permute-start | bytes 393224 | tf_op jit(solution)/shard_map/ppermute | solution.py:310
  64.5 1.3 %collective-permute-done.25.refs_1_ = bf16[64,1024]{1,0:T(8,128)(2,1)S(1)} collective-permute-done((bf16[64,1024]{1,0:T(8,128)(2,1)S(1)}, bf16[64,1024]{1,0:T(8,128)(2,1)S(1)}, u32[]{:S(2)}, u32[]{:S(2)}) %collective-permute-start.25) | collective-permute-done | bytes 131104 | tf_op jit(solution)/shard_map/ppermute | solution.py:310
  65.8 2.0 %collective-permute-done.26.refs_2_ = bf16[64,1024]{1,0:T(8,128)(2,1)S(1)} collective-permute-done((bf16[64,1024]{1,0:T(8,128)(2,1)S(1)}, bf16[64,1024]{1,0:T(8,128)(2,1)S(1)}, u32[]{:S(2)}, u32[]{:S(2)}) %collective-permute-start.26) | collective-permute-done | bytes 131104 | tf_op jit(solution)/shard_map/ppermute | solution.py:310
  67.9 1.8 %collective-permute-start.33 = (bf16[32,1024]{1,0:T(8,128)(2,1)S(1)}, bf16[32,1024]{1,0:T(8,128)(2,1)S(1)}, u32[]{:S(2)}, u32[]{:S(2)}) collective-permute-start(bf16[32,1024]{1,0:T(8,128)(2,1)S(1)} %get-tuple-element.63), channel_id=1, source_target_pairs={{0,24},{1,25},{2,26},{3,27},{4,28},{5,29},{6,30},{7,31},{8,16},{9,... | collective-permute-start | bytes 196616 | tf_op jit(solution)/shard_map/ppermute | solution.py:310
  69.7 1.1 %collective-permute-start.32 = (bf16[32,1024]{1,0:T(8,128)(2,1)S(1)}, bf16[32,1024]{1,0:T(8,128)(2,1)S(1)}, u32[]{:S(2)}, u32[]{:S(2)}) collective-permute-start(bf16[32,1024]{1,0:T(8,128)(2,1)S(1)} %get-tuple-element.52.after), channel_id=1, source_target_pairs={{0,16},{1,17},{2,18},{3,19},{4,20},{5,21},{6,22},{7,23},{8,24},{9,... | collective-permute-start | bytes 196616 | tf_op jit(solution)/shard_map/ppermute | solution.py:310
  70.8 3.6 %shard_map.96 = (bf16[4096,512]{1,0:T(8,128)(2,1)}, s32[1,1]{1,0:T(1,128)}) custom-call(s32[3]{0:T(128)S(1)} %pad_add_fusion.where, bf16[32,1024]{1,0:T(8,128)(2,1)S(1)} %get-tuple-element.52.after, bf16[256,512]{1,0:T(8,128)(2,1)S(1)} %get-tuple-element.53.logit_grad, bf16[128,1152]{1,0:T(8,128)(2,1)S(1)} %get-tuple-element.38.refs_0_, ...), custom_call_target="tpu_custom_call" | custom-call | flops 1073741824 | bytes 6750224 | tf_op jit(solution)/shard_map/pallas_call | solution.py:32
  75.1 1.6 %collective-permute-start.31 = (bf16[32,1024]{1,0:T(8,128)(2,1)S(1)}, bf16[32,1024]{1,0:T(8,128)(2,1)S(1)}, u32[]{:S(2)}, u32[]{:S(2)}) collective-permute-start(bf16[32,1024]{1,0:T(8,128)(2,1)S(1)} %get-tuple-element.62), channel_id=1, source_target_pairs={{0,8},{1,9},{2,10},{3,11},{4,12},{5,13},{6,14},{7,15},{8,0},{9,1},... | collective-permute-start | bytes 196616 | tf_op jit(solution)/shard_map/ppermute | solution.py:310
  76.7 2.7 %collective-permute-done.31.refs_1_ = bf16[32,1024]{1,0:T(8,128)(2,1)S(1)} collective-permute-done((bf16[32,1024]{1,0:T(8,128)(2,1)S(1)}, bf16[32,1024]{1,0:T(8,128)(2,1)S(1)}, u32[]{:S(2)}, u32[]{:S(2)}) %collective-permute-start.31) | collective-permute-done | bytes 65568 | tf_op jit(solution)/shard_map/ppermute | solution.py:310
  (61 shorter events, 15.9 us)
Async XLA Ops:
  1.9 7.8 %collective-permute-start = (bf16[32,1152]{1,0:T(8,128)(2,1)S(1)}, bf16[32,1152]{1,0:T(8,128)(2,1)S(1)}, u32[]{:S(2)}, u32[]{:S(2)}) collective-permute-start(bf16[32,1152]{1,0:T(8,128)(2,1)S(1)} %get-tuple-element.34.after.refs_0_), channel_id=1, source_target_pairs={{0,8},{1,9},{2,10},{3,11},{4,12},{5,13},{6,14},{7,15},{8,0},{9,1},... | collective-permute-start | bytes 221192 | tf_op jit(solution)/shard_map/ppermute | solution.py:310
  10.4 7.1 %collective-permute-start.2 = (bf16[32,1152]{1,0:T(8,128)(2,1)S(1)}, bf16[32,1152]{1,0:T(8,128)(2,1)S(1)}, u32[]{:S(2)}, u32[]{:S(2)}) collective-permute-start(bf16[32,1152]{1,0:T(8,128)(2,1)S(1)} %get-tuple-element.37), channel_id=1, source_target_pairs={{0,24},{1,25},{2,26},{3,27},{4,28},{5,29},{6,30},{7,31},{8,16},{9,... | collective-permute-start | bytes 221192 | tf_op jit(solution)/shard_map/ppermute | solution.py:310
  12.9 7.0 %collective-permute-start.1 = (bf16[32,1152]{1,0:T(8,128)(2,1)S(1)}, bf16[32,1152]{1,0:T(8,128)(2,1)S(1)}, u32[]{:S(2)}, u32[]{:S(2)}) collective-permute-start(bf16[32,1152]{1,0:T(8,128)(2,1)S(1)} %get-tuple-element.37), channel_id=1, source_target_pairs={{0,16},{1,17},{2,18},{3,19},{4,20},{5,21},{6,22},{7,23},{8,24},{9,... | collective-permute-start | bytes 221192 | tf_op jit(solution)/shard_map/ppermute | solution.py:310
  13.1 11.2 %collective-permute-start.10 = (bf16[64,1024]{1,0:T(8,128)(2,1)S(1)}, bf16[64,1024]{1,0:T(8,128)(2,1)S(1)}, u32[]{:S(2)}, u32[]{:S(2)}) collective-permute-start(bf16[64,1024]{1,0:T(8,128)(2,1)S(1)} %get-tuple-element.40), channel_id=1, source_target_pairs={{0,6},{1,7},{2,4},{3,5},{4,2},{5,3},{6,0},{7,1},{8,14},{9,15},{10,... | collective-permute-start | bytes 393224 | tf_op jit(solution)/shard_map/ppermute | solution.py:310
  15.6 8.7 %collective-permute-start.8 = (bf16[64,1024]{1,0:T(8,128)(2,1)S(1)}, bf16[64,1024]{1,0:T(8,128)(2,1)S(1)}, u32[]{:S(2)}, u32[]{:S(2)}) collective-permute-start(bf16[64,1024]{1,0:T(8,128)(2,1)S(1)} %get-tuple-element.40), channel_id=1, source_target_pairs={{0,2},{1,3},{2,0},{3,1},{4,6},{5,7},{6,4},{7,5},{8,10},{9,11},{10,... | collective-permute-start | bytes 393224 | tf_op jit(solution)/shard_map/ppermute | solution.py:310
  16.1 8.8 %collective-permute-start.3 = (bf16[64,1152]{1,0:T(8,128)(2,1)S(1)}, bf16[64,1152]{1,0:T(8,128)(2,1)S(1)}, u32[]{:S(2)}, u32[]{:S(2)}) collective-permute-start(bf16[64,1152]{1,0:T(8,128)(2,1)S(1)} %get-tuple-element.36.refs_0_), channel_id=1, source_target_pairs={{0,4},{1,5},{2,6},{3,7},{4,0},{5,1},{6,2},{7,3},{8,12},{9,13},{10,... | collective-permute-start | bytes 442376 | tf_op jit(solution)/shard_map/ppermute | solution.py:310
  21.2 6.4 %collective-permute-start.11 = (bf16[64,1024]{1,0:T(8,128)(2,1)S(1)}, bf16[64,1024]{1,0:T(8,128)(2,1)S(1)}, u32[]{:S(2)}, u32[]{:S(2)}) collective-permute-start(bf16[64,1024]{1,0:T(8,128)(2,1)S(1)} %get-tuple-element.41), channel_id=1, source_target_pairs={{0,6},{1,7},{2,4},{3,5},{4,2},{5,3},{6,0},{7,1},{8,14},{9,15},{10,... | collective-permute-start | bytes 393224 | tf_op jit(solution)/shard_map/ppermute | solution.py:310
  23.7 6.8 %collective-permute-start.4 = (bf16[64,1152]{1,0:T(8,128)(2,1)S(1)}, bf16[64,1152]{1,0:T(8,128)(2,1)S(1)}, u32[]{:S(2)}, u32[]{:S(2)}) collective-permute-start(bf16[64,1152]{1,0:T(8,128)(2,1)S(1)} %slice.3), channel_id=1, source_target_pairs={{0,4},{1,5},{2,6},{3,7},{4,0},{5,1},{6,2},{7,3},{8,12},{9,13},{10,... | collective-permute-start | bytes 442376 | tf_op jit(solution)/shard_map/ppermute | solution.py:310
  24.3 8.1 %collective-permute-start.5 = (bf16[128,1152]{1,0:T(8,128)(2,1)S(1)}, bf16[128,1152]{1,0:T(8,128)(2,1)S(1)}, u32[]{:S(2)}, u32[]{:S(2)}) collective-permute-start(bf16[128,1152]{1,0:T(8,128)(2,1)S(1)} %get-tuple-element.38.refs_0_), channel_id=1, source_target_pairs={{0,1},{1,0},{2,3},{3,2},{4,5},{5,4},{6,7},{7,6},{8,9},{9,8},{10,11... | collective-permute-start | bytes 884744 | tf_op jit(solution)/shard_map/ppermute | solution.py:310
  24.3 6.0 %collective-permute-start.9 = (bf16[64,1024]{1,0:T(8,128)(2,1)S(1)}, bf16[64,1024]{1,0:T(8,128)(2,1)S(1)}, u32[]{:S(2)}, u32[]{:S(2)}) collective-permute-start(bf16[64,1024]{1,0:T(8,128)(2,1)S(1)} %get-tuple-element.41), channel_id=1, source_target_pairs={{0,2},{1,3},{2,0},{3,1},{4,6},{5,7},{6,4},{7,5},{8,10},{9,11},{10,... | collective-permute-start | bytes 393224 | tf_op jit(solution)/shard_map/ppermute | solution.py:310
  24.9 5.9 %collective-permute-start.14 = (bf16[64,1024]{1,0:T(8,128)(2,1)S(1)}, bf16[64,1024]{1,0:T(8,128)(2,1)S(1)}, u32[]{:S(2)}, u32[]{:S(2)}) collective-permute-start(bf16[64,1024]{1,0:T(8,128)(2,1)S(1)} %collective-permute-done.10.refs_8_), channel_id=1, source_target_pairs={{0,1},{1,0},{2,3},{3,2},{4,5},{5,4},{6,7},{7,6},{8,9},{9,8},{10,11... | collective-permute-start | bytes 393224 | tf_op jit(solution)/shard_map/ppermute | solution.py:310
  27.6 3.5 %collective-permute-start.12 = (bf16[64,1024]{1,0:T(8,128)(2,1)S(1)}, bf16[64,1024]{1,0:T(8,128)(2,1)S(1)}, u32[]{:S(2)}, u32[]{:S(2)}) collective-permute-start(bf16[64,1024]{1,0:T(8,128)(2,1)S(1)} %collective-permute-done.8.refs_6_), channel_id=1, source_target_pairs={{0,1},{1,0},{2,3},{3,2},{4,5},{5,4},{6,7},{7,6},{8,9},{9,8},{10,11... | collective-permute-start | bytes 393224 | tf_op jit(solution)/shard_map/ppermute | solution.py:310
  30.3 1.5 %collective-permute-start.6 = (bf16[64,1152]{1,0:T(8,128)(2,1)S(1)}, bf16[64,1152]{1,0:T(8,128)(2,1)S(1)}, u32[]{:S(2)}, u32[]{:S(2)}) collective-permute-start(bf16[64,1152]{1,0:T(8,128)(2,1)S(1)} %collective-permute-done.3.refs_1_), channel_id=1, source_target_pairs={{0,1},{1,0},{2,3},{3,2},{4,5},{5,4},{6,7},{7,6},{8,9},{9,8},{10,11... | collective-permute-start | bytes 442376 | tf_op jit(solution)/shard_map/ppermute | solution.py:310
  30.5 1.9 %collective-permute-start.7 = (bf16[64,1152]{1,0:T(8,128)(2,1)S(1)}, bf16[64,1152]{1,0:T(8,128)(2,1)S(1)}, u32[]{:S(2)}, u32[]{:S(2)}) collective-permute-start(bf16[64,1152]{1,0:T(8,128)(2,1)S(1)} %collective-permute-done.4.refs_2_), channel_id=1, source_target_pairs={{0,1},{1,0},{2,3},{3,2},{4,5},{5,4},{6,7},{7,6},{8,9},{9,8},{10,11... | collective-permute-start | bytes 442376 | tf_op jit(solution)/shard_map/ppermute | solution.py:310
  31.1 1.3 %collective-permute-start.13 = (bf16[64,1024]{1,0:T(8,128)(2,1)S(1)}, bf16[64,1024]{1,0:T(8,128)(2,1)S(1)}, u32[]{:S(2)}, u32[]{:S(2)}) collective-permute-start(bf16[64,1024]{1,0:T(8,128)(2,1)S(1)} %collective-permute-done.9.refs_7_), channel_id=1, source_target_pairs={{0,1},{1,0},{2,3},{3,2},{4,5},{5,4},{6,7},{7,6},{8,9},{9,8},{10,11... | collective-permute-start | bytes 393224 | tf_op jit(solution)/shard_map/ppermute | solution.py:310
  38.0 3.7 %collective-permute-start.19 = (f32[8,256]{1,0:T(8,128)S(1)}, f32[8,256]{1,0:T(8,128)S(1)}, u32[]{:S(2)}, u32[]{:S(2)}) collective-permute-start(f32[8,256]{1,0:T(8,128)S(1)} %shard_map.91.refs_0_), channel_id=1, source_target_pairs={{0,4},{1,5},{2,6},{3,7},{4,0},{5,1},{6,2},{7,3},{8,12},{9,13},{10,... | collective-permute-start | bytes 24584 | tf_op jit(solution)/shard_map/ppermute | solution.py:310
  39.6 3.7 %collective-permute-start.18 = (f32[8,256]{1,0:T(8,128)S(1)}, f32[8,256]{1,0:T(8,128)S(1)}, u32[]{:S(2)}, u32[]{:S(2)}) collective-permute-start(f32[8,256]{1,0:T(8,128)S(1)} %shard_map.91.refs_0_), channel_id=1, source_target_pairs={{0,2},{1,3},{2,0},{3,1},{4,6},{5,7},{6,4},{7,5},{8,10},{9,11},{10,... | collective-permute-start | bytes 24584 | tf_op jit(solution)/shard_map/ppermute | solution.py:310
  40.5 4.5 %collective-permute-start.17 = (f32[8,256]{1,0:T(8,128)S(1)}, f32[8,256]{1,0:T(8,128)S(1)}, u32[]{:S(2)}, u32[]{:S(2)}) collective-permute-start(f32[8,256]{1,0:T(8,128)S(1)} %shard_map.91.refs_0_), channel_id=1, source_target_pairs={{0,6},{1,7},{2,4},{3,5},{4,2},{5,3},{6,0},{7,1},{8,14},{9,15},{10,... | collective-permute-start | bytes 24584 | tf_op jit(solution)/shard_map/ppermute | solution.py:310
  45.1 5.5 %collective-permute-start.22 = (f32[8,256]{1,0:T(8,128)S(1)}, f32[8,256]{1,0:T(8,128)S(1)}, u32[]{:S(2)}, u32[]{:S(2)}) collective-permute-start(f32[8,256]{1,0:T(8,128)S(1)} %shard_map.92.refs_0_), channel_id=1, source_target_pairs={{0,24},{1,25},{2,26},{3,27},{4,28},{5,29},{6,30},{7,31},{8,16},{9,... | collective-permute-start | bytes 24584 | tf_op jit(solution)/shard_map/ppermute | solution.py:310
  47.1 4.5 %collective-permute-start.21 = (f32[8,256]{1,0:T(8,128)S(1)}, f32[8,256]{1,0:T(8,128)S(1)}, u32[]{:S(2)}, u32[]{:S(2)}) collective-permute-start(f32[8,256]{1,0:T(8,128)S(1)} %shard_map.92.refs_0_), channel_id=1, source_target_pairs={{0,16},{1,17},{2,18},{3,19},{4,20},{5,21},{6,22},{7,23},{8,24},{9,... | collective-permute-start | bytes 24584 | tf_op jit(solution)/shard_map/ppermute | solution.py:310
  47.1 4.5 %collective-permute-start.20 = (f32[8,256]{1,0:T(8,128)S(1)}, f32[8,256]{1,0:T(8,128)S(1)}, u32[]{:S(2)}, u32[]{:S(2)}) collective-permute-start(f32[8,256]{1,0:T(8,128)S(1)} %shard_map.92.refs_0_), channel_id=1, source_target_pairs={{0,8},{1,9},{2,10},{3,11},{4,12},{5,13},{6,14},{7,15},{8,0},{9,1},... | collective-permute-start | bytes 24584 | tf_op jit(solution)/shard_map/ppermute | solution.py:310
  53.8 2.0 %collective-permute-start.23 = (bf16[4,64,1024]{2,1,0:T(8,128)(2,1)S(1)}, bf16[4,64,1024]{2,1,0:T(8,128)(2,1)S(1)}, u32[]{:S(2)}, u32[]{:S(2)}) collective-permute-start(bf16[4,64,1024]{2,1,0:T(8,128)(2,1)S(1)} %get-tuple-element.47), channel_id=1, source_target_pairs={{0,1},{1,0},{2,3},{3,2},{4,5},{5,4},{6,7},{7,6},{8,9},{9,8},{10,11... | collective-permute-start | bytes 1572872 | tf_op jit(solution)/shard_map/ppermute | solution.py:310
  53.9 5.6 %collective-permute-start.27 = (bf16[4,64,1024]{2,1,0:T(8,128)(2,1)S(1)}, bf16[4,64,1024]{2,1,0:T(8,128)(2,1)S(1)}, u32[]{:S(2)}, u32[]{:S(2)}) collective-permute-start(bf16[4,64,1024]{2,1,0:T(8,128)(2,1)S(1)} %get-tuple-element.56), channel_id=1, source_target_pairs={{0,1},{1,0},{2,3},{3,2},{4,5},{5,4},{6,7},{7,6},{8,9},{9,8},{10,11... | collective-permute-start | bytes 1572872 | tf_op jit(solution)/shard_map/ppermute | solution.py:310
  55.9 7.3 %collective-permute-start.24 = (bf16[64,1024]{1,0:T(8,128)(2,1)S(1)}, bf16[64,1024]{1,0:T(8,128)(2,1)S(1)}, u32[]{:S(2)}, u32[]{:S(2)}) collective-permute-start(bf16[64,1024]{1,0:T(8,128)(2,1)S(1)} %get-tuple-element.49), channel_id=1, source_target_pairs={{0,6},{1,7},{2,4},{3,5},{4,2},{5,3},{6,0},{7,1},{8,14},{9,15},{10,... | collective-permute-start | bytes 393224 | tf_op jit(solution)/shard_map/ppermute | solution.py:310
  57.4 8.4 %collective-permute-start.25 = (bf16[64,1024]{1,0:T(8,128)(2,1)S(1)}, bf16[64,1024]{1,0:T(8,128)(2,1)S(1)}, u32[]{:S(2)}, u32[]{:S(2)}) collective-permute-start(bf16[64,1024]{1,0:T(8,128)(2,1)S(1)} %get-tuple-element.50), channel_id=1, source_target_pairs={{0,2},{1,3},{2,0},{3,1},{4,6},{5,7},{6,4},{7,5},{8,10},{9,11},{10,... | collective-permute-start | bytes 393224 | tf_op jit(solution)/shard_map/ppermute | solution.py:310
  58.7 9.1 %collective-permute-start.26 = (bf16[64,1024]{1,0:T(8,128)(2,1)S(1)}, bf16[64,1024]{1,0:T(8,128)(2,1)S(1)}, u32[]{:S(2)}, u32[]{:S(2)}) collective-permute-start(bf16[64,1024]{1,0:T(8,128)(2,1)S(1)} %get-tuple-element.51), channel_id=1, source_target_pairs={{0,4},{1,5},{2,6},{3,7},{4,0},{5,1},{6,2},{7,3},{8,12},{9,13},{10,... | collective-permute-start | bytes 393224 | tf_op jit(solution)/shard_map/ppermute | solution.py:310
  59.6 14.8 %collective-permute-start.28 = (bf16[64,1024]{1,0:T(8,128)(2,1)S(1)}, bf16[64,1024]{1,0:T(8,128)(2,1)S(1)}, u32[]{:S(2)}, u32[]{:S(2)}) collective-permute-start(bf16[64,1024]{1,0:T(8,128)(2,1)S(1)} %get-tuple-element.58), channel_id=1, source_target_pairs={{0,6},{1,7},{2,4},{3,5},{4,2},{5,3},{6,0},{7,1},{8,14},{9,15},{10,... | collective-permute-start | bytes 393224 | tf_op jit(solution)/shard_map/ppermute | solution.py:310
  61.1 13.3 %collective-permute-start.29 = (bf16[64,1024]{1,0:T(8,128)(2,1)S(1)}, bf16[64,1024]{1,0:T(8,128)(2,1)S(1)}, u32[]{:S(2)}, u32[]{:S(2)}) collective-permute-start(bf16[64,1024]{1,0:T(8,128)(2,1)S(1)} %get-tuple-element.59), channel_id=1, source_target_pairs={{0,2},{1,3},{2,0},{3,1},{4,6},{5,7},{6,4},{7,5},{8,10},{9,11},{10,... | collective-permute-start | bytes 393224 | tf_op jit(solution)/shard_map/ppermute | solution.py:310
  63.2 11.2 %collective-permute-start.30 = (bf16[64,1024]{1,0:T(8,128)(2,1)S(1)}, bf16[64,1024]{1,0:T(8,128)(2,1)S(1)}, u32[]{:S(2)}, u32[]{:S(2)}) collective-permute-start(bf16[64,1024]{1,0:T(8,128)(2,1)S(1)} %get-tuple-element.60), channel_id=1, source_target_pairs={{0,4},{1,5},{2,6},{3,7},{4,0},{5,1},{6,2},{7,3},{8,12},{9,13},{10,... | collective-permute-start | bytes 393224 | tf_op jit(solution)/shard_map/ppermute | solution.py:310
  67.9 8.8 %collective-permute-start.33 = (bf16[32,1024]{1,0:T(8,128)(2,1)S(1)}, bf16[32,1024]{1,0:T(8,128)(2,1)S(1)}, u32[]{:S(2)}, u32[]{:S(2)}) collective-permute-start(bf16[32,1024]{1,0:T(8,128)(2,1)S(1)} %get-tuple-element.63), channel_id=1, source_target_pairs={{0,24},{1,25},{2,26},{3,27},{4,28},{5,29},{6,30},{7,31},{8,16},{9,... | collective-permute-start | bytes 196616 | tf_op jit(solution)/shard_map/ppermute | solution.py:310
  69.7 7.1 %collective-permute-start.32 = (bf16[32,1024]{1,0:T(8,128)(2,1)S(1)}, bf16[32,1024]{1,0:T(8,128)(2,1)S(1)}, u32[]{:S(2)}, u32[]{:S(2)}) collective-permute-start(bf16[32,1024]{1,0:T(8,128)(2,1)S(1)} %get-tuple-element.52.after), channel_id=1, source_target_pairs={{0,16},{1,17},{2,18},{3,19},{4,20},{5,21},{6,22},{7,23},{8,24},{9,... | collective-permute-start | bytes 196616 | tf_op jit(solution)/shard_map/ppermute | solution.py:310
  75.1 4.3 %collective-permute-start.31 = (bf16[32,1024]{1,0:T(8,128)(2,1)S(1)}, bf16[32,1024]{1,0:T(8,128)(2,1)S(1)}, u32[]{:S(2)}, u32[]{:S(2)}) collective-permute-start(bf16[32,1024]{1,0:T(8,128)(2,1)S(1)} %get-tuple-element.62), channel_id=1, source_target_pairs={{0,8},{1,9},{2,10},{3,11},{4,12},{5,13},{6,14},{7,15},{8,0},{9,1},... | collective-permute-start | bytes 196616 | tf_op jit(solution)/shard_map/ppermute | solution.py:310
  (6 other events, 54.6 us)

commit v5 on v4

--- a/solution.py
+++ b/solution.py
@@ -61,7 +61,7 @@
     return (slot.astype(jnp.int32) == grid) & (mask == 1)
 
 
-def pack_kernel(hidden_hbm, mask_hbm, target_hbm, turn_hbm, rows, chosen_out, *scratch):
+def pack_kernel(where, hidden_hbm, mask_hbm, target_hbm, turn_hbm, rows, plain, chosen_out, *scratch):
     hidden, mask, target, turn, sems = scratch
     copies = []
     for place, (source, held) in enumerate(
@@ -93,23 +93,29 @@
     rows[:, width:] = table.astype(jnp.bfloat16)
     copies[3].wait()
     packed = jnp.dot(one_hot, hidden[...], preferred_element_type=jnp.float32)
-    rows[:, :width] = packed.astype(jnp.bfloat16)
-
-
-def join_kernel(token, *refs):
-    blocks, (line, own, again) = refs[:-3], refs[-3:]
-    width, start = own.shape[1], 0
-    skip = line.shape[0] - own.shape[0]
+    packed = packed.astype(jnp.bfloat16)
+    rows[:, :width] = packed
+    plain[...] = packed
+
+
+def join_kernel(skipped, *refs):
+    blocks, line, plain = refs[skipped:-2], refs[-2], refs[-1]
+    start = 0
     for block in blocks:
         end = start + block.shape[0]
         line[start:end] = block[...]
-        if start >= skip:
-            own[start - skip:end - skip] = block[:, :width]
+        plain[start:end] = block[:, :plain.shape[1]]
         start = end
-    again[...] = line[:CAP]
-
-
-def stage_kernel(after, weight, held, token, sems):
+
+
+def stack_kernel(*refs):
+    out, start = refs[-1], 0
+    for block in refs[:-1]:
+        out[start:start + block.shape[0]] = block[...]
+        start += block.shape[0]
+
+
+def stage_kernel(line, weight, held, same, sems):
     count = sems.shape[0]
     height = weight.shape[0] // count
     copies = []
@@ -118,9 +124,9 @@
         copy = pltpu.make_async_copy(weight.at[part], held.at[part], sems.at[place])
         copy.start()
         copies.append(copy)
+    same[...] = line[...]
     for copy in copies:
         copy.wait()
-    token[0, 0] = 0
 
 
 def info_kernel(*refs):
@@ -156,15 +162,11 @@
     return stats
 
 
-def all_rows(pieces, counts, block, width):
-    start = sum(counts[:block])
-    return jnp.concatenate(
-        [ref[:, :width] for ref in pieces[start:start + counts[block]]], axis=0
-    )
-
-
-def logits_kernel(counts, groups, where, info, weight, *refs):
-    blocks = len(counts)
+def all_rows(pieces, block, width):
+    return jnp.concatenate([ref[:, :width] for ref in pieces[2 * block:2 * block + 2]], axis=0)
+
+
+def logits_kernel(blocks, groups, where, info, weight, *refs):
     pieces, (logits, stats) = refs[:-2], refs[-2:]
     rank, position, shard = where[0], where[1], where[2]
     width = weight.shape[0] // blocks
@@ -172,7 +174,7 @@
     for block in range(blocks):
         start = pl.multiple_of((rank ^ block) * width, width)
         part = jnp.dot(
-            all_rows(pieces, counts, block, width),
+            all_rows(pieces, block, width),
             weight[pl.ds(start, width), :],
             preferred_element_type=jnp.float32,
         )
@@ -204,12 +206,28 @@
     out[...] = jnp.where(row == 0, peak, jnp.where(row == 1, mass, hit))
 
 
-def grad_kernel(count, blocks, groups, where, info, logits, weight, *refs):
-    tables = [ref[...] for ref in refs[:count]]
-    away, kept, logit_grad, loss = refs[count:count + 2], refs[count + 2:count + 4], *refs[count + 4:]
+def block_grads(blocks, rank, first, grad, weight, outs):
+    height = grad.shape[0] // 4
+    width = weight.shape[0] // blocks
+    for block in range(first, blocks, 2):
+        start = pl.multiple_of((rank ^ block) * width, width)
+        part = lax.dot_general(
+            grad,
+            weight[pl.ds(start, width), :],
+            (((1,), (1,)), ((), ())),
+            preferred_element_type=jnp.float32,
+        )
+        for quarter in range(4):
+            side, out = quarter // 2, outs[quarter % 2]
+            piece = part[quarter * height:(quarter + 1) * height]
+            out[block // 2 * 2 + side] = piece.astype(out.dtype)
+
+
+def grad_kernel(blocks, groups, where, info, logits, weight, mine, theirs, *refs):
+    away, (logit_grad, loss) = refs[:2], refs[2:]
     rank, position, shard = where[0], where[1], where[2]
     height, columns = logits.shape
-    peak, mass, hit = merge(tables)
+    peak, mass, hit = merge([mine[...], theirs[...]])
     log_total = jnp.broadcast_to(peak + jnp.log(mass), (8, height))
     log_total = reorder(log_total, position, groups)
     log_total = jnp.transpose(jnp.concatenate([log_total] * 16, axis=0))[:, 0:1]
@@ -222,34 +240,21 @@
         grad_scale * row_weight * (probability - (column == target).astype(jnp.float32))
     ).astype(jnp.bfloat16)
     logit_grad[...] = grad
-    part_rows = height // 4
-    width = weight.shape[0] // blocks
-    order = [b for b in range(blocks) if b % 2] + [b for b in range(blocks) if not b % 2]
-    for block in order:
-        start = pl.multiple_of((rank ^ block) * width, width)
-        part = lax.dot_general(
-            grad,
-            weight[pl.ds(start, width), :],
-            (((1,), (1,)), ((), ())),
-            preferred_element_type=jnp.float32,
-        )
-        outs = away if block % 2 else kept
-        for quarter in range(4):
-            side, chunk = quarter // 2, quarter % 2
-            out = outs[chunk]
-            piece = part[quarter * part_rows:(quarter + 1) * part_rows]
-            out[block // 2 * 2 + side] = piece.astype(out.dtype)
-
-
-def weight_kernel(counts, where, after, logit_grad, *refs):
-    blocks = len(counts)
+    block_grads(blocks, rank, 1, grad, weight, away)
+
+
+def kept_kernel(blocks, where, logit_grad, weight, *kept):
+    block_grads(blocks, where[0], 0, logit_grad[...], weight, kept)
+
+
+def weight_kernel(blocks, where, after, logit_grad, *refs):
     pieces, (out, token, done, sems) = refs[:-4], refs[-4:]
     rank = where[0]
     width = done.shape[0] // blocks
     copies = []
     for block in range(blocks):
         done[block * width:(block + 1) * width] = lax.dot_general(
-            all_rows(pieces, counts, block, width),
+            all_rows(pieces, block, width),
             logit_grad[...],
             (((0,), (0,)), ((), ())),
             preferred_element_type=jnp.float32,
@@ -313,66 +318,68 @@
     position = (group & 1) * zs + (group >> 1)
     where = jnp.stack([rank, position, group * ranks + rank]).astype(i32)
 
-    packed, chosen = call(
+    packed, plain, chosen = call(
         pack_kernel,
         (
+            where,
             in_hbm(hidden),
             in_hbm(loss_mask.reshape(1, tokens)),
             in_hbm(target_ids.reshape(1, tokens)),
             in_hbm(turn_ids.reshape(1, tokens)),
         ),
-        [HBM] * 4,
-        (shape((CAP, width + IDS), bf16), shape((CAP, tokens), bf16)),
-        (VMEM, VMEM),
+        [SMEM] + [HBM] * 4,
+        (
+            shape((CAP, width + IDS), bf16),
+            shape((CAP, width), bf16),
+            shape((CAP, tokens), bf16),
+        ),
+        (VMEM,) * 3,
         [pltpu.VMEM((tokens, width), bf16)]
         + [pltpu.VMEM((1, tokens), i32)] * 3
         + [pltpu.SemaphoreType.DMA((4,))],
     )
 
-    held, token = call(
+    far = [send(packed, z=z) for z in range(1, zs)]
+    small = {(y, x): send(plain if x else packed, y=y, x=x) for y, x in square}
+    far_rows = (zs - 1) * CAP
+    line, line_plain = call(
+        functools.partial(join_kernel, len(small)),
+        (*small.values(), *far),
+        [ANY] * len(small) + [VMEM] * len(far),
+        (shape((far_rows, width + IDS), bf16), shape((far_rows, width), bf16)),
+        (VMEM, VMEM),
+    )
+    large = {(y, x): send(line_plain if x else line, y=y, x=x) for y, x in square}
+    held, same = call(
         stage_kernel,
-        (packed, in_hbm(weight)),
-        [ANY, HBM],
-        (shape((depth, columns), bf16), shape((1, 1), i32)),
-        (VMEM, SMEM),
+        (line, in_hbm(weight)),
+        [VMEM, HBM],
+        (shape((depth, columns), bf16), shape(line.shape, bf16)),
+        (VMEM, VMEM),
         [pltpu.SemaphoreType.DMA((4,))],
     )
-    pieces, before, again = {}, [], packed
-    for chunk in range(2):
-        near = range(chunk * zs // 2, (chunk + 1) * zs // 2)
-        blocks = [send(again, z=z) if z else packed for z in near]
-        line, own, again = call(
-            join_kernel,
-            (token, *before, *blocks),
-            [SMEM] + [VMEM] * len(before + blocks),
-            (
-                shape(((chunk + 1) * zs // 2 * CAP, width + IDS), bf16),
-                shape((zs // 2 * CAP, width), bf16),
-                shape((CAP, width + IDS), bf16),
-            ),
-            (VMEM,) * 3,
-        )
-        before = [line]
-        pieces[0, 1, chunk] = send(line[chunk * zs // 2 * CAP:], y=1)
-        for y, x in square:
-            if x:
-                pieces[2 * x, y, chunk] = send(own, y=y, x=x)
-    pieces[0, 0, 0] = line
-    for b, y, chunk in list(pieces):
-        pieces[b + 1, y, chunk] = send(pieces[b, y, chunk], core=1)
-    parted = [[pieces[k] for k in sorted(pieces) if k[0] == b] for b in range(ranks)]
-    counts = [len(part) for part in parted]
-    rows = [piece for part in parted for piece in part]
+    small[0, 0], large[0, 0] = packed, same
+    pieces = {}
+    for y, x in [(0, 0)] + square:
+        piece = call(
+            stack_kernel,
+            (small[y, x], large[y, x]),
+            [VMEM, VMEM],
+            shape((zs * CAP, small[y, x].shape[1]), bf16),
+            VMEM,
+        )
+        pieces[2 * x, y], pieces[2 * x + 1, y] = piece, send(piece, core=1)
+    rows = [pieces[b, y] for b in range(ranks) for y in range(2)]
 
     info = call(
         info_kernel,
-        (*parted[0], advantages.reshape(1, -1)),
-        [VMEM] * (counts[0] + 1),
+        (*rows[:2], advantages.reshape(1, -1)),
+        [VMEM] * 3,
         shape((total_rows, 128), f32),
         VMEM,
     )
     logits, stats = call(
-        functools.partial(logits_kernel, counts, dps),
+        functools.partial(logits_kernel, ranks, dps),
         (where, info, held, *rows),
         [SMEM] + [VMEM] * (2 + len(rows)),
         (shape((total_rows, columns), f32), shape((8, total_rows), f32)),
@@ -380,37 +387,47 @@
         flops=flops,
     )
 
-    for hops in ([{"core": 1}], [{"y": y, "x": x} for y, x in square]):
-        tables = [stats] + [send(stats, **hop) for hop in hops]
-        stats = call(
-            merge_kernel, tables, [VMEM] * len(tables), shape((8, total_rows), f32), VMEM
-        )
-    tables = [stats] + [send(stats, z=z) for z in range(1, zs)]
+    hops = [{"core": 1}]
+    hops += [{"x": 1 << bit} for bit in range((xs - 1).bit_length())] + [{"y": 1}]
+    hops += [{"z": 1 << bit} for bit in range((zs - 1).bit_length())]
+    for place, hop in enumerate(hops):
+        theirs = send(stats, **hop)
+        if place + 1 < len(hops):
+            stats = call(
+                merge_kernel, (stats, theirs), [VMEM] * 2, shape((8, total_rows), f32), VMEM
+            )
 
     rows_part = total_rows // 4
     whole = (ranks, rows_part, width)
-    outs = [shape(whole, bf16)] * 2 + [shape(whole, f32)] * 2
-    *parts, logit_grad, loss = call(
-        functools.partial(grad_kernel, len(tables), ranks, dps),
-        (where, info, logits, held, *tables),
-        [SMEM] + [VMEM] * (3 + len(tables)),
-        tuple(outs) + (shape((total_rows, columns), bf16), shape((1, 1), f32)),
-        (VMEM,) * (len(outs) + 1) + (SMEM,),
-        flops=flops,
+    *away, logit_grad, loss = call(
+        functools.partial(grad_kernel, ranks, dps),
+        (where, info, logits, held, stats, theirs),
+        [SMEM] + [VMEM] * 5,
+        (shape(whole, bf16),) * 2 + (shape((total_rows, columns), bf16), shape((1, 1), f32)),
+        (VMEM,) * 3 + (SMEM,),
+        flops=flops // 2,
+    )
+    kept = call(
+        functools.partial(kept_kernel, ranks),
+        (where, logit_grad, held),
+        [SMEM] + [VMEM] * 2,
+        (shape(whole, f32),) * 2,
+        (VMEM,) * 2,
+        flops=flops // 2,
     )
 
     ends, token = [None] * zs, jnp.zeros((1, 1), i32)
     besides = [None, None]
     for chunk in (1, 0):
-        besides[chunk] = send(parts[chunk], core=1)
+        besides[chunk] = send(away[chunk], core=1)
     sums = [None, None]
     for chunk in (1, 0):
-        small = shape((rows_part, width), bf16)
+        part = shape((rows_part, width), bf16)
         *going, corner = call(
             pair_kernel,
-            (parts[2 + chunk], besides[chunk]),
+            (kept[chunk], besides[chunk]),
             [VMEM, VMEM],
-            (small,) * (ranks - 1) + (shape((rows_part, width), f32),),
+            (part,) * (ranks - 1) + (shape((rows_part, width), f32),),
             (VMEM,) * ranks,
         )
         arrived = []
@@ -418,27 +435,26 @@
             x, y = divmod(ranks - 1 - place, 2)
             arrived.append(send(value, y=y, x=x))
         sums[chunk] = (corner, *arrived)
+    weight_grad, last_token = call(
+        functools.partial(weight_kernel, ranks),
+        (where, sums[0][0], logit_grad, *rows),
+        [SMEM, ANY] + [VMEM] * (1 + len(rows)),
+        (shape((depth, columns), bf16), shape((1, 1), i32)),
+        (HBM, SMEM),
+        [pltpu.VMEM((depth, columns), bf16), pltpu.SemaphoreType.DMA((ranks,))],
+        flops=flops,
+    )
     for chunk in (1, 0):
         near = chunk * zs // 2
         parts_z = call(
             functools.partial(corner_kernel, ranks - 1),
-            (token, *sums[chunk]),
+            (token if chunk else last_token, *sums[chunk]),
             [SMEM] + [VMEM] * ranks,
             tuple(shape((CAP, width), bf16 if near + z else f32) for z in range(zs // 2)),
             (VMEM,) * (zs // 2),
         )
         for z, value in enumerate(parts_z):
             ends[near + z] = send(value, z=near + z) if near + z else value
-        if chunk:
-            weight_grad, token = call(
-                functools.partial(weight_kernel, counts),
-                (where, parts_z[0], logit_grad, *rows),
-                [SMEM, ANY] + [VMEM] * (1 + len(rows)),
-                (shape((depth, columns), bf16), shape((1, 1), i32)),
-                (HBM, SMEM),
-                [pltpu.VMEM((depth, columns), bf16), pltpu.SemaphoreType.DMA((ranks,))],
-                flops=flops,
-            )
     hidden_grad = call(
         unpack_kernel,
         (chosen, *ends),

time: 80.6 us -> 73.9 us (0.917)
  local copies, waits for them, and re-layouts: 4.22 us -> 0.01 us
  starting transfers between devices: 34.8 us -> 32.8 us
  Pallas kernels: 16.3 us -> 15.1 us
    unnamed x8 -> x2, local copies, waits for them, and re-layouts: 4.2 us -> 0.01 us
    ppermute x34 -> x29, starting transfers between devices: 34.8 us -> 32.8 us  [send(): return lax.ppermute(value, AXES, pairs)]
    pallas_call x15 -> x21, Pallas kernels: 16.3 us -> 15.1 us  [call(): pl.pallas_call(kernel, out_shape=out_shape, in_specs=in_specs, out_specs=...]
    ppermute x34 -> x29, waiting for transfers between devices: 24.3 us -> 24.9 us  [send(): return lax.ppermute(value, AXES, pairs)]
  transfers between devices with their start and end apart: 34 -> 29, of which waited for: 18 -> 15; matrix products, arithmetic and copies ran while one was open for 0% -> 0% of each run, Pallas kernels for 11% -> 12%
where the time goes in v5:
time: 73.9 us; the launch traced here: 73.7 us
  starting transfers between devices  32.8 us (44%)
  waiting for transfers between devices  24.9 us (34%)
  Pallas kernels  15.1 us (20%)
  between operations  0.86 us (1%)
    ppermute x29, starting transfers between devices, send(): return lax.ppermute(value, AXES, pairs)  32.8 us
    ppermute x29, waiting for transfers between devices, send(): return lax.ppermute(value, AXES, pairs)  24.9 us
    pallas_call x21, Pallas kernels, call(): pl.pallas_call(kernel, out_shape=out_shape, in_specs=in_specs, out_specs=...  15.1 us
  transfers between devices with their start and end apart: 29, of which 15 were waited for; matrix products, arithmetic and copies ran while one was open for 0% of the time, Pallas kernels for 12%

profile of v5, /device:TPU:0, one launch (start us, length us, event | category | flops | bytes accessed | tf_op | source)
XLA Modules:
  0.0 73.7 jit_solution(13764708922477151117)
XLA Ops:
  0.7 1.8 %shard_map.85 = (bf16[32,1152]{1,0:T(8,128)(2,1)S(1)}, bf16[32,1024]{1,0:T(8,128)(2,1)S(1)}, bf16[32,128]{1,0:T(8,128)(2,1)S(1)}) custom-call(s32[3]{0:T(128)S(1)} %pad_add_fusion.where, bf16[128,1024]{1,0:T(8,128)(2,1)} %hidden_hbm.1, s32[1,128]{1,0:T(1,128)} %bitcast.9, s32[1,128]{1,0:T(1,128)} %bitcast.10, s32[1,128]{1,0:T(1,128)} %bitcast.11), custom_call_target="tpu_custom_call" | custom-call | bytes 411148 | tf_op jit(solution)/shard_map/pallas_call | solution.py:32
  2.5 3.0 %collective-permute-start.1 = (bf16[32,1024]{1,0:T(8,128)(2,1)S(1)}, bf16[32,1024]{1,0:T(8,128)(2,1)S(1)}, u32[]{:S(2)}, u32[]{:S(2)}) collective-permute-start(bf16[32,1024]{1,0:T(8,128)(2,1)S(1)} %get-tuple-element.33), channel_id=1, source_target_pairs={{0,2},{1,3},{2,0},{3,1},{4,6},{5,7},{6,4},{7,5},{8,10},{9,11},{10,... | collective-permute-start | bytes 196616 | tf_op jit(solution)/shard_map/ppermute | solution.py:315
  5.5 3.6 %collective-permute-start.5 = (bf16[32,1152]{1,0:T(8,128)(2,1)S(1)}, bf16[32,1152]{1,0:T(8,128)(2,1)S(1)}, u32[]{:S(2)}, u32[]{:S(2)}) collective-permute-start(bf16[32,1152]{1,0:T(8,128)(2,1)S(1)} %get-tuple-element.32.refs_0_), channel_id=1, source_target_pairs={{0,24},{1,25},{2,26},{3,27},{4,28},{5,29},{6,30},{7,31},{8,16},{9,... | collective-permute-start | bytes 221192 | tf_op jit(solution)/shard_map/ppermute | solution.py:315
  9.9 1.5 %collective-permute-start.2 = (bf16[32,1152]{1,0:T(8,128)(2,1)S(1)}, bf16[32,1152]{1,0:T(8,128)(2,1)S(1)}, u32[]{:S(2)}, u32[]{:S(2)}) collective-permute-start(bf16[32,1152]{1,0:T(8,128)(2,1)S(1)} %get-tuple-element.32.refs_0_), channel_id=1, source_target_pairs={{0,4},{1,5},{2,6},{3,7},{4,0},{5,1},{6,2},{7,3},{8,12},{9,13},{10,... | collective-permute-start | bytes 221192 | tf_op jit(solution)/shard_map/ppermute | solution.py:315
  11.7 4.9 %collective-permute-done.refs_0_ = bf16[32,1024]{1,0:T(8,128)(2,1)S(1)} collective-permute-done((bf16[32,1024]{1,0:T(8,128)(2,1)S(1)}, bf16[32,1024]{1,0:T(8,128)(2,1)S(1)}, u32[]{:S(2)}, u32[]{:S(2)}) %collective-permute-start) | collective-permute-done | bytes 65568 | tf_op jit(solution)/shard_map/ppermute | solution.py:315
  17.5 2.7 %collective-permute-start.10 = (bf16[96,1024]{1,0:T(8,128)(2,1)S(1)}, bf16[96,1024]{1,0:T(8,128)(2,1)S(1)}, u32[]{:S(2)}, u32[]{:S(2)}) collective-permute-start(bf16[96,1024]{1,0:T(8,128)(2,1)S(1)} %get-tuple-element.37), channel_id=1, source_target_pairs={{0,6},{1,7},{2,4},{3,5},{4,2},{5,3},{6,0},{7,1},{8,14},{9,15},{10,... | collective-permute-start | bytes 589832 | tf_op jit(solution)/shard_map/ppermute | solution.py:315
  20.2 2.2 %shard_map.87 = (bf16[4096,512]{1,0:T(8,128)(2,1)S(1)}, bf16[96,1152]{1,0:T(8,128)(2,1)S(1)}) custom-call(bf16[96,1152]{1,0:T(8,128)(2,1)S(1)} %get-tuple-element.34.line, bf16[4096,512]{1,0:T(8,128)(2,1)} %weight.1), custom_call_target="tpu_custom_call" | custom-call | bytes 8830976 | tf_op jit(solution)/shard_map/pallas_call | solution.py:32
  22.5 2.2 %collective-permute-done.6.refs_1_ = bf16[96,1152]{1,0:T(8,128)(2,1)S(1)} collective-permute-done((bf16[96,1152]{1,0:T(8,128)(2,1)S(1)}, bf16[96,1152]{1,0:T(8,128)(2,1)S(1)}, u32[]{:S(2)}, u32[]{:S(2)}) %collective-permute-start.6) | collective-permute-done | bytes 221216 | tf_op jit(solution)/shard_map/ppermute | solution.py:315
  25.4 1.8 %collective-permute-done.10.refs_1_ = bf16[96,1024]{1,0:T(8,128)(2,1)S(1)} collective-permute-done((bf16[96,1024]{1,0:T(8,128)(2,1)S(1)}, bf16[96,1024]{1,0:T(8,128)(2,1)S(1)}, u32[]{:S(2)}, u32[]{:S(2)}) %collective-permute-start.10) | collective-permute-done | bytes 196640 | tf_op jit(solution)/shard_map/ppermute | solution.py:315
  27.8 1.1 %collective-permute-done.12.refs_7_ = bf16[128,1024]{1,0:T(8,128)(2,1)S(1)} collective-permute-done((bf16[128,1024]{1,0:T(8,128)(2,1)S(1)}, bf16[128,1024]{1,0:T(8,128)(2,1)S(1)}, u32[]{:S(2)}, u32[]{:S(2)}) %collective-permute-start.12) | collective-permute-done | bytes 262176 | tf_op jit(solution)/shard_map/ppermute | solution.py:315
  28.9 2.2 %shard_map.93 = (f32[256,512]{1,0:T(8,128)S(1)}, f32[8,256]{1,0:T(8,128)S(1)}) custom-call(s32[3]{0:T(128)S(1)} %pad_add_fusion.where, f32[256,128]{1,0:T(8,128)S(1)} %shard_map.90.info, bf16[4096,512]{1,0:T(8,128)(2,1)S(1)} %get-tuple-element.36.weight, bf16[128,1152]{1,0:T(8,128)(2,1)S(1)} %shard_map.88.refs_0_, bf16[128,1152]{1,0:T(8,128)(2,1)S(1)} %shard_map.89.refs_1_, ...), custom_call_target="tpu_custom_call" | custom-call | flops 1073741824 | bytes 7086092 | tf_op jit(solution)/shard_map/pallas_call | solution.py:32
  31.3 1.0 %collective-permute-done.13.refs_1_ = f32[8,256]{1,0:T(8,128)S(1)} collective-permute-done((f32[8,256]{1,0:T(8,128)S(1)}, f32[8,256]{1,0:T(8,128)S(1)}, u32[]{:S(2)}, u32[]{:S(2)}) %collective-permute-start.13) | collective-permute-done | bytes 8224 | tf_op jit(solution)/shard_map/ppermute | solution.py:315
  33.0 3.1 %collective-permute-done.14.refs_1_ = f32[8,256]{1,0:T(8,128)S(1)} collective-permute-done((f32[8,256]{1,0:T(8,128)S(1)}, f32[8,256]{1,0:T(8,128)S(1)}, u32[]{:S(2)}, u32[]{:S(2)}) %collective-permute-start.14) | collective-permute-done | bytes 8224 | tf_op jit(solution)/shard_map/ppermute | solution.py:315
  36.1 1.6 %collective-permute-start.15 = (f32[8,256]{1,0:T(8,128)S(1)}, f32[8,256]{1,0:T(8,128)S(1)}, u32[]{:S(2)}, u32[]{:S(2)}) collective-permute-start(f32[8,256]{1,0:T(8,128)S(1)} %shard_map.95.refs_0_), channel_id=1, source_target_pairs={{0,4},{1,5},{2,6},{3,7},{4,0},{5,1},{6,2},{7,3},{8,12},{9,13},{10,... | collective-permute-start | bytes 24584 | tf_op jit(solution)/shard_map/ppermute | solution.py:315
  37.6 2.1 %collective-permute-done.15.refs_1_ = f32[8,256]{1,0:T(8,128)S(1)} collective-permute-done((f32[8,256]{1,0:T(8,128)S(1)}, f32[8,256]{1,0:T(8,128)S(1)}, u32[]{:S(2)}, u32[]{:S(2)}) %collective-permute-start.15) | collective-permute-done | bytes 8224 | tf_op jit(solution)/shard_map/ppermute | solution.py:315
  39.8 1.7 %collective-permute-start.16 = (f32[8,256]{1,0:T(8,128)S(1)}, f32[8,256]{1,0:T(8,128)S(1)}, u32[]{:S(2)}, u32[]{:S(2)}) collective-permute-start(f32[8,256]{1,0:T(8,128)S(1)} %shard_map.96.refs_0_), channel_id=1, source_target_pairs={{0,8},{1,9},{2,10},{3,11},{4,12},{5,13},{6,14},{7,15},{8,0},{9,1},... | collective-permute-start | bytes 24584 | tf_op jit(solution)/shard_map/ppermute | solution.py:315
  41.5 2.0 %collective-permute-done.16.refs_1_ = f32[8,256]{1,0:T(8,128)S(1)} collective-permute-done((f32[8,256]{1,0:T(8,128)S(1)}, f32[8,256]{1,0:T(8,128)S(1)}, u32[]{:S(2)}, u32[]{:S(2)}) %collective-permute-start.16) | collective-permute-done | bytes 8224 | tf_op jit(solution)/shard_map/ppermute | solution.py:315
  43.5 2.6 %collective-permute-start.17 = (f32[8,256]{1,0:T(8,128)S(1)}, f32[8,256]{1,0:T(8,128)S(1)}, u32[]{:S(2)}, u32[]{:S(2)}) collective-permute-start(f32[8,256]{1,0:T(8,128)S(1)} %shard_map.97.mine), channel_id=1, source_target_pairs={{0,16},{1,17},{2,18},{3,19},{4,20},{5,21},{6,22},{7,23},{8,24},{9,... | collective-permute-start | bytes 24584 | tf_op jit(solution)/shard_map/ppermute | solution.py:315
  46.1 2.0 %collective-permute-done.17.theirs = f32[8,256]{1,0:T(8,128)S(1)} collective-permute-done((f32[8,256]{1,0:T(8,128)S(1)}, f32[8,256]{1,0:T(8,128)S(1)}, u32[]{:S(2)}, u32[]{:S(2)}) %collective-permute-start.17) | collective-permute-done | bytes 8224 | tf_op jit(solution)/shard_map/ppermute | solution.py:315
  48.1 1.6 %shard_map.98 = (bf16[4,64,1024]{2,1,0:T(8,128)(2,1)S(1)}, bf16[4,64,1024]{2,1,0:T(8,128)(2,1)S(1)}, bf16[256,512]{1,0:T(8,128)(2,1)S(1)}, f32[1,1]{1,0:T(1,128)}) custom-call(s32[3]{0:T(128)S(1)} %pad_add_fusion.where, f32[256,128]{1,0:T(8,128)S(1)} %shard_map.90.info, f32[256,512]{1,0:T(8,128)S(1)} %get-tuple-element.38.logits, ...), custom_call_target="tpu_custom_call" | custom-call | flops 536870912 | bytes 6176784 | tf_op jit(solution)/shard_map/pallas_call | solution.py:32
  50.4 1.3 %shard_map.99 = (f32[4,64,1024]{2,1,0:T(8,128)S(1)}, f32[4,64,1024]{2,1,0:T(8,128)S(1)}) custom-call(s32[3]{0:T(128)S(1)} %pad_add_fusion.where, bf16[256,512]{1,0:T(8,128)(2,1)S(1)} %get-tuple-element.42.logit_grad, bf16[4096,512]{1,0:T(8,128)(2,1)S(1)} %get-tuple-element.36.weight), custom_call_target="tpu_custom_call" | custom-call | flops 536870912 | bytes 6553612 | tf_op jit(solution)/shard_map/pallas_call | solution.py:32
  51.8 1.6 %collective-permute-start.24 = (bf16[64,1024]{1,0:T(8,128)(2,1)S(1)}, bf16[64,1024]{1,0:T(8,128)(2,1)S(1)}, u32[]{:S(2)}, u32[]{:S(2)}) collective-permute-start(bf16[64,1024]{1,0:T(8,128)(2,1)S(1)} %get-tuple-element.55), channel_id=1, source_target_pairs={{0,6},{1,7},{2,4},{3,5},{4,2},{5,3},{6,0},{7,1},{8,14},{9,15},{10,... | collective-permute-start | bytes 393224 | tf_op jit(solution)/shard_map/ppermute | solution.py:315
  53.4 1.5 %collective-permute-start.25 = (bf16[64,1024]{1,0:T(8,128)(2,1)S(1)}, bf16[64,1024]{1,0:T(8,128)(2,1)S(1)}, u32[]{:S(2)}, u32[]{:S(2)}) collective-permute-start(bf16[64,1024]{1,0:T(8,128)(2,1)S(1)} %get-tuple-element.56), channel_id=1, source_target_pairs={{0,2},{1,3},{2,0},{3,1},{4,6},{5,7},{6,4},{7,5},{8,10},{9,11},{10,... | collective-permute-start | bytes 393224 | tf_op jit(solution)/shard_map/ppermute | solution.py:315
  55.5 1.6 %collective-permute-start.19 = (bf16[64,1024]{1,0:T(8,128)(2,1)S(1)}, bf16[64,1024]{1,0:T(8,128)(2,1)S(1)}, u32[]{:S(2)}, u32[]{:S(2)}) collective-permute-start(bf16[64,1024]{1,0:T(8,128)(2,1)S(1)} %get-tuple-element.47), channel_id=1, source_target_pairs={{0,6},{1,7},{2,4},{3,5},{4,2},{5,3},{6,0},{7,1},{8,14},{9,15},{10,... | collective-permute-start | bytes 393224 | tf_op jit(solution)/shard_map/ppermute | solution.py:315
  57.1 1.5 %collective-permute-start.20 = (bf16[64,1024]{1,0:T(8,128)(2,1)S(1)}, bf16[64,1024]{1,0:T(8,128)(2,1)S(1)}, u32[]{:S(2)}, u32[]{:S(2)}) collective-permute-start(bf16[64,1024]{1,0:T(8,128)(2,1)S(1)} %get-tuple-element.48), channel_id=1, source_target_pairs={{0,2},{1,3},{2,0},{3,1},{4,6},{5,7},{6,4},{7,5},{8,10},{9,11},{10,... | collective-permute-start | bytes 393224 | tf_op jit(solution)/shard_map/ppermute | solution.py:315
  59.1 1.6 %collective-permute-start.21 = (bf16[64,1024]{1,0:T(8,128)(2,1)S(1)}, bf16[64,1024]{1,0:T(8,128)(2,1)S(1)}, u32[]{:S(2)}, u32[]{:S(2)}) collective-permute-start(bf16[64,1024]{1,0:T(8,128)(2,1)S(1)} %get-tuple-element.49), channel_id=1, source_target_pairs={{0,4},{1,5},{2,6},{3,7},{4,0},{5,1},{6,2},{7,3},{8,12},{9,13},{10,... | collective-permute-start | bytes 393224 | tf_op jit(solution)/shard_map/ppermute | solution.py:315
  60.7 3.6 %shard_map.101 = (bf16[4096,512]{1,0:T(8,128)(2,1)}, s32[1,1]{1,0:T(1,128)}) custom-call(s32[3]{0:T(128)S(1)} %pad_add_fusion.where, f32[64,1024]{1,0:T(8,128)S(1)} %get-tuple-element.45.after.kept, bf16[256,512]{1,0:T(8,128)(2,1)S(1)} %get-tuple-element.42.logit_grad, bf16[128,1152]{1,0:T(8,128)(2,1)S(1)} %shard_map.88.refs_0_, ...), custom_call_target="tpu_custom_call" | custom-call | flops 1073741824 | bytes 6946832 | tf_op jit(solution)/shard_map/pallas_call | solution.py:32
  64.4 1.4 %collective-permute-start.27 = (bf16[32,1024]{1,0:T(8,128)(2,1)S(1)}, bf16[32,1024]{1,0:T(8,128)(2,1)S(1)}, u32[]{:S(2)}, u32[]{:S(2)}) collective-permute-start(bf16[32,1024]{1,0:T(8,128)(2,1)S(1)} %get-tuple-element.58), channel_id=1, source_target_pairs={{0,16},{1,17},{2,18},{3,19},{4,20},{5,21},{6,22},{7,23},{8,24},{9,... | collective-permute-start | bytes 196616 | tf_op jit(solution)/shard_map/ppermute | solution.py:315
  65.8 1.5 %collective-permute-start.28 = (bf16[32,1024]{1,0:T(8,128)(2,1)S(1)}, bf16[32,1024]{1,0:T(8,128)(2,1)S(1)}, u32[]{:S(2)}, u32[]{:S(2)}) collective-permute-start(bf16[32,1024]{1,0:T(8,128)(2,1)S(1)} %get-tuple-element.59), channel_id=1, source_target_pairs={{0,24},{1,25},{2,26},{3,27},{4,28},{5,29},{6,30},{7,31},{8,16},{9,... | collective-permute-start | bytes 196616 | tf_op jit(solution)/shard_map/ppermute | solution.py:315
  68.1 1.1 %collective-permute-start.22 = (bf16[32,1024]{1,0:T(8,128)(2,1)S(1)}, bf16[32,1024]{1,0:T(8,128)(2,1)S(1)}, u32[]{:S(2)}, u32[]{:S(2)}) collective-permute-start(bf16[32,1024]{1,0:T(8,128)(2,1)S(1)} %get-tuple-element.51), channel_id=1, source_target_pairs={{0,8},{1,9},{2,10},{3,11},{4,12},{5,13},{6,14},{7,15},{8,0},{9,1},... | collective-permute-start | bytes 196616 | tf_op jit(solution)/shard_map/ppermute | solution.py:315
  69.1 1.9 %collective-permute-done.27.refs_2_ = bf16[32,1024]{1,0:T(8,128)(2,1)S(1)} collective-permute-done((bf16[32,1024]{1,0:T(8,128)(2,1)S(1)}, bf16[32,1024]{1,0:T(8,128)(2,1)S(1)}, u32[]{:S(2)}, u32[]{:S(2)}) %collective-permute-start.27) | collective-permute-done | bytes 65568 | tf_op jit(solution)/shard_map/ppermute | solution.py:315
  71.1 1.0 %collective-permute-done.28.refs_3_ = bf16[32,1024]{1,0:T(8,128)(2,1)S(1)} collective-permute-done((bf16[32,1024]{1,0:T(8,128)(2,1)S(1)}, bf16[32,1024]{1,0:T(8,128)(2,1)S(1)}, u32[]{:S(2)}, u32[]{:S(2)}) %collective-permute-start.28) | collective-permute-done | bytes 65568 | tf_op jit(solution)/shard_map/ppermute | solution.py:315
  (50 shorter events, 8.5 us)
Async XLA Ops:
  0.6 26.8 %copy-start = (f32[32]{0:T(128)S(1)}, f32[32]{0:T(128)}, u32[]{:S(2)}) copy-start(f32[32]{0:T(128)} %param.11) | copy-start | bytes 388
  2.5 8.9 %collective-permute-start.1 = (bf16[32,1024]{1,0:T(8,128)(2,1)S(1)}, bf16[32,1024]{1,0:T(8,128)(2,1)S(1)}, u32[]{:S(2)}, u32[]{:S(2)}) collective-permute-start(bf16[32,1024]{1,0:T(8,128)(2,1)S(1)} %get-tuple-element.33), channel_id=1, source_target_pairs={{0,2},{1,3},{2,0},{3,1},{4,6},{5,7},{6,4},{7,5},{8,10},{9,11},{10,... | collective-permute-start | bytes 196616 | tf_op jit(solution)/shard_map/ppermute | solution.py:315
  5.5 11.1 %collective-permute-start.5 = (bf16[32,1152]{1,0:T(8,128)(2,1)S(1)}, bf16[32,1152]{1,0:T(8,128)(2,1)S(1)}, u32[]{:S(2)}, u32[]{:S(2)}) collective-permute-start(bf16[32,1152]{1,0:T(8,128)(2,1)S(1)} %get-tuple-element.32.refs_0_), channel_id=1, source_target_pairs={{0,24},{1,25},{2,26},{3,27},{4,28},{5,29},{6,30},{7,31},{8,16},{9,... | collective-permute-start | bytes 221192 | tf_op jit(solution)/shard_map/ppermute | solution.py:315
  9.1 7.5 %collective-permute-start.4 = (bf16[32,1152]{1,0:T(8,128)(2,1)S(1)}, bf16[32,1152]{1,0:T(8,128)(2,1)S(1)}, u32[]{:S(2)}, u32[]{:S(2)}) collective-permute-start(bf16[32,1152]{1,0:T(8,128)(2,1)S(1)} %get-tuple-element.32.refs_0_), channel_id=1, source_target_pairs={{0,16},{1,17},{2,18},{3,19},{4,20},{5,21},{6,22},{7,23},{8,24},{9,... | collective-permute-start | bytes 221192 | tf_op jit(solution)/shard_map/ppermute | solution.py:315
  9.1 7.5 %collective-permute-start.3 = (bf16[32,1152]{1,0:T(8,128)(2,1)S(1)}, bf16[32,1152]{1,0:T(8,128)(2,1)S(1)}, u32[]{:S(2)}, u32[]{:S(2)}) collective-permute-start(bf16[32,1152]{1,0:T(8,128)(2,1)S(1)} %get-tuple-element.32.refs_0_), channel_id=1, source_target_pairs={{0,8},{1,9},{2,10},{3,11},{4,12},{5,13},{6,14},{7,15},{8,0},{9,1},... | collective-permute-start | bytes 221192 | tf_op jit(solution)/shard_map/ppermute | solution.py:315
  9.9 6.7 %collective-permute-start.2 = (bf16[32,1152]{1,0:T(8,128)(2,1)S(1)}, bf16[32,1152]{1,0:T(8,128)(2,1)S(1)}, u32[]{:S(2)}, u32[]{:S(2)}) collective-permute-start(bf16[32,1152]{1,0:T(8,128)(2,1)S(1)} %get-tuple-element.32.refs_0_), channel_id=1, source_target_pairs={{0,4},{1,5},{2,6},{3,7},{4,0},{5,1},{6,2},{7,3},{8,12},{9,13},{10,... | collective-permute-start | bytes 221192 | tf_op jit(solution)/shard_map/ppermute | solution.py:315
  11.4 5.2 %collective-permute-start = (bf16[32,1024]{1,0:T(8,128)(2,1)S(1)}, bf16[32,1024]{1,0:T(8,128)(2,1)S(1)}, u32[]{:S(2)}, u32[]{:S(2)}) collective-permute-start(bf16[32,1024]{1,0:T(8,128)(2,1)S(1)} %get-tuple-element.33), channel_id=1, source_target_pairs={{0,6},{1,7},{2,4},{3,5},{4,2},{5,3},{6,0},{7,1},{8,14},{9,15},{10,... | collective-permute-start | bytes 196616 | tf_op jit(solution)/shard_map/ppermute | solution.py:315
  16.6 8.1 %collective-permute-start.6 = (bf16[96,1152]{1,0:T(8,128)(2,1)S(1)}, bf16[96,1152]{1,0:T(8,128)(2,1)S(1)}, u32[]{:S(2)}, u32[]{:S(2)}) collective-permute-start(bf16[96,1152]{1,0:T(8,128)(2,1)S(1)} %get-tuple-element.34.line), channel_id=1, source_target_pairs={{0,4},{1,5},{2,6},{3,7},{4,0},{5,1},{6,2},{7,3},{8,12},{9,13},{10,... | collective-permute-start | bytes 663560 | tf_op jit(solution)/shard_map/ppermute | solution.py:315
  17.2 7.8 %collective-permute-start.9 = (bf16[96,1024]{1,0:T(8,128)(2,1)S(1)}, bf16[96,1024]{1,0:T(8,128)(2,1)S(1)}, u32[]{:S(2)}, u32[]{:S(2)}) collective-permute-start(bf16[96,1024]{1,0:T(8,128)(2,1)S(1)} %get-tuple-element.37), channel_id=1, source_target_pairs={{0,2},{1,3},{2,0},{3,1},{4,6},{5,7},{6,4},{7,5},{8,10},{9,11},{10,... | collective-permute-start | bytes 589832 | tf_op jit(solution)/shard_map/ppermute | solution.py:315
  17.5 9.8 %collective-permute-start.10 = (bf16[96,1024]{1,0:T(8,128)(2,1)S(1)}, bf16[96,1024]{1,0:T(8,128)(2,1)S(1)}, u32[]{:S(2)}, u32[]{:S(2)}) collective-permute-start(bf16[96,1024]{1,0:T(8,128)(2,1)S(1)} %get-tuple-element.37), channel_id=1, source_target_pairs={{0,6},{1,7},{2,4},{3,5},{4,2},{5,3},{6,0},{7,1},{8,14},{9,15},{10,... | collective-permute-start | bytes 589832 | tf_op jit(solution)/shard_map/ppermute | solution.py:315
  22.4 5.4 %collective-permute-start.7 = (bf16[128,1152]{1,0:T(8,128)(2,1)S(1)}, bf16[128,1152]{1,0:T(8,128)(2,1)S(1)}, u32[]{:S(2)}, u32[]{:S(2)}) collective-permute-start(bf16[128,1152]{1,0:T(8,128)(2,1)S(1)} %shard_map.88.refs_0_), channel_id=1, source_target_pairs={{0,1},{1,0},{2,3},{3,2},{4,5},{5,4},{6,7},{7,6},{8,9},{9,8},{10,11... | collective-permute-start | bytes 884744 | tf_op jit(solution)/shard_map/ppermute | solution.py:315
  24.8 4.1 %collective-permute-start.8 = (bf16[128,1152]{1,0:T(8,128)(2,1)S(1)}, bf16[128,1152]{1,0:T(8,128)(2,1)S(1)}, u32[]{:S(2)}, u32[]{:S(2)}) collective-permute-start(bf16[128,1152]{1,0:T(8,128)(2,1)S(1)} %shard_map.89.refs_1_), channel_id=1, source_target_pairs={{0,1},{1,0},{2,3},{3,2},{4,5},{5,4},{6,7},{7,6},{8,9},{9,8},{10,11... | collective-permute-start | bytes 884744 | tf_op jit(solution)/shard_map/ppermute | solution.py:315
  25.1 2.7 %collective-permute-start.11 = (bf16[128,1024]{1,0:T(8,128)(2,1)S(1)}, bf16[128,1024]{1,0:T(8,128)(2,1)S(1)}, u32[]{:S(2)}, u32[]{:S(2)}) collective-permute-start(bf16[128,1024]{1,0:T(8,128)(2,1)S(1)} %shard_map.91.refs_4_), channel_id=1, source_target_pairs={{0,1},{1,0},{2,3},{3,2},{4,5},{5,4},{6,7},{7,6},{8,9},{9,8},{10,11... | collective-permute-start | bytes 786440 | tf_op jit(solution)/shard_map/ppermute | solution.py:315
  27.3 1.6 %collective-permute-start.12 = (bf16[128,1024]{1,0:T(8,128)(2,1)S(1)}, bf16[128,1024]{1,0:T(8,128)(2,1)S(1)}, u32[]{:S(2)}, u32[]{:S(2)}) collective-permute-start(bf16[128,1024]{1,0:T(8,128)(2,1)S(1)} %shard_map.92.refs_5_), channel_id=1, source_target_pairs={{0,1},{1,0},{2,3},{3,2},{4,5},{5,4},{6,7},{7,6},{8,9},{9,8},{10,11... | collective-permute-start | bytes 786440 | tf_op jit(solution)/shard_map/ppermute | solution.py:315
  31.1 1.2 %collective-permute-start.13 = (f32[8,256]{1,0:T(8,128)S(1)}, f32[8,256]{1,0:T(8,128)S(1)}, u32[]{:S(2)}, u32[]{:S(2)}) collective-permute-start(f32[8,256]{1,0:T(8,128)S(1)} %get-tuple-element.39.refs_0_), channel_id=1, source_target_pairs={{0,1},{1,0},{2,3},{3,2},{4,5},{5,4},{6,7},{7,6},{8,9},{9,8},{10,11... | collective-permute-start | bytes 24584 | tf_op jit(solution)/shard_map/ppermute | solution.py:315
  32.3 3.7 %collective-permute-start.14 = (f32[8,256]{1,0:T(8,128)S(1)}, f32[8,256]{1,0:T(8,128)S(1)}, u32[]{:S(2)}, u32[]{:S(2)}) collective-permute-start(f32[8,256]{1,0:T(8,128)S(1)} %shard_map.94.refs_0_), channel_id=1, source_target_pairs={{0,2},{1,3},{2,0},{3,1},{4,6},{5,7},{6,4},{7,5},{8,10},{9,11},{10,... | collective-permute-start | bytes 24584 | tf_op jit(solution)/shard_map/ppermute | solution.py:315
  36.1 3.7 %collective-permute-start.15 = (f32[8,256]{1,0:T(8,128)S(1)}, f32[8,256]{1,0:T(8,128)S(1)}, u32[]{:S(2)}, u32[]{:S(2)}) collective-permute-start(f32[8,256]{1,0:T(8,128)S(1)} %shard_map.95.refs_0_), channel_id=1, source_target_pairs={{0,4},{1,5},{2,6},{3,7},{4,0},{5,1},{6,2},{7,3},{8,12},{9,13},{10,... | collective-permute-start | bytes 24584 | tf_op jit(solution)/shard_map/ppermute | solution.py:315
  39.8 3.7 %collective-permute-start.16 = (f32[8,256]{1,0:T(8,128)S(1)}, f32[8,256]{1,0:T(8,128)S(1)}, u32[]{:S(2)}, u32[]{:S(2)}) collective-permute-start(f32[8,256]{1,0:T(8,128)S(1)} %shard_map.96.refs_0_), channel_id=1, source_target_pairs={{0,8},{1,9},{2,10},{3,11},{4,12},{5,13},{6,14},{7,15},{8,0},{9,1},... | collective-permute-start | bytes 24584 | tf_op jit(solution)/shard_map/ppermute | solution.py:315
  43.5 4.6 %collective-permute-start.17 = (f32[8,256]{1,0:T(8,128)S(1)}, f32[8,256]{1,0:T(8,128)S(1)}, u32[]{:S(2)}, u32[]{:S(2)}) collective-permute-start(f32[8,256]{1,0:T(8,128)S(1)} %shard_map.97.mine), channel_id=1, source_target_pairs={{0,16},{1,17},{2,18},{3,19},{4,20},{5,21},{6,22},{7,23},{8,24},{9,... | collective-permute-start | bytes 24584 | tf_op jit(solution)/shard_map/ppermute | solution.py:315
  49.8 2.0 %collective-permute-start.23 = (bf16[4,64,1024]{2,1,0:T(8,128)(2,1)S(1)}, bf16[4,64,1024]{2,1,0:T(8,128)(2,1)S(1)}, u32[]{:S(2)}, u32[]{:S(2)}) collective-permute-start(bf16[4,64,1024]{2,1,0:T(8,128)(2,1)S(1)} %get-tuple-element.53), channel_id=1, source_target_pairs={{0,1},{1,0},{2,3},{3,2},{4,5},{5,4},{6,7},{7,6},{8,9},{9,8},{10,11... | collective-permute-start | bytes 1572872 | tf_op jit(solution)/shard_map/ppermute | solution.py:315
  49.9 5.5 %collective-permute-start.18 = (bf16[4,64,1024]{2,1,0:T(8,128)(2,1)S(1)}, bf16[4,64,1024]{2,1,0:T(8,128)(2,1)S(1)}, u32[]{:S(2)}, u32[]{:S(2)}) collective-permute-start(bf16[4,64,1024]{2,1,0:T(8,128)(2,1)S(1)} %get-tuple-element.44), channel_id=1, source_target_pairs={{0,1},{1,0},{2,3},{3,2},{4,5},{5,4},{6,7},{7,6},{8,9},{9,8},{10,11... | collective-permute-start | bytes 1572872 | tf_op jit(solution)/shard_map/ppermute | solution.py:315
  51.8 7.3 %collective-permute-start.24 = (bf16[64,1024]{1,0:T(8,128)(2,1)S(1)}, bf16[64,1024]{1,0:T(8,128)(2,1)S(1)}, u32[]{:S(2)}, u32[]{:S(2)}) collective-permute-start(bf16[64,1024]{1,0:T(8,128)(2,1)S(1)} %get-tuple-element.55), channel_id=1, source_target_pairs={{0,6},{1,7},{2,4},{3,5},{4,2},{5,3},{6,0},{7,1},{8,14},{9,15},{10,... | collective-permute-start | bytes 393224 | tf_op jit(solution)/shard_map/ppermute | solution.py:315
  53.4 10.9 %collective-permute-start.25 = (bf16[64,1024]{1,0:T(8,128)(2,1)S(1)}, bf16[64,1024]{1,0:T(8,128)(2,1)S(1)}, u32[]{:S(2)}, u32[]{:S(2)}) collective-permute-start(bf16[64,1024]{1,0:T(8,128)(2,1)S(1)} %get-tuple-element.56), channel_id=1, source_target_pairs={{0,2},{1,3},{2,0},{3,1},{4,6},{5,7},{6,4},{7,5},{8,10},{9,11},{10,... | collective-permute-start | bytes 393224 | tf_op jit(solution)/shard_map/ppermute | solution.py:315
  54.9 9.4 %collective-permute-start.26 = (bf16[64,1024]{1,0:T(8,128)(2,1)S(1)}, bf16[64,1024]{1,0:T(8,128)(2,1)S(1)}, u32[]{:S(2)}, u32[]{:S(2)}) collective-permute-start(bf16[64,1024]{1,0:T(8,128)(2,1)S(1)} %get-tuple-element.57), channel_id=1, source_target_pairs={{0,4},{1,5},{2,6},{3,7},{4,0},{5,1},{6,2},{7,3},{8,12},{9,13},{10,... | collective-permute-start | bytes 393224 | tf_op jit(solution)/shard_map/ppermute | solution.py:315
  55.5 11.8 %collective-permute-start.19 = (bf16[64,1024]{1,0:T(8,128)(2,1)S(1)}, bf16[64,1024]{1,0:T(8,128)(2,1)S(1)}, u32[]{:S(2)}, u32[]{:S(2)}) collective-permute-start(bf16[64,1024]{1,0:T(8,128)(2,1)S(1)} %get-tuple-element.47), channel_id=1, source_target_pairs={{0,6},{1,7},{2,4},{3,5},{4,2},{5,3},{6,0},{7,1},{8,14},{9,15},{10,... | collective-permute-start | bytes 393224 | tf_op jit(solution)/shard_map/ppermute | solution.py:315
  57.1 10.3 %collective-permute-start.20 = (bf16[64,1024]{1,0:T(8,128)(2,1)S(1)}, bf16[64,1024]{1,0:T(8,128)(2,1)S(1)}, u32[]{:S(2)}, u32[]{:S(2)}) collective-permute-start(bf16[64,1024]{1,0:T(8,128)(2,1)S(1)} %get-tuple-element.48), channel_id=1, source_target_pairs={{0,2},{1,3},{2,0},{3,1},{4,6},{5,7},{6,4},{7,5},{8,10},{9,11},{10,... | collective-permute-start | bytes 393224 | tf_op jit(solution)/shard_map/ppermute | solution.py:315
  59.1 8.2 %collective-permute-start.21 = (bf16[64,1024]{1,0:T(8,128)(2,1)S(1)}, bf16[64,1024]{1,0:T(8,128)(2,1)S(1)}, u32[]{:S(2)}, u32[]{:S(2)}) collective-permute-start(bf16[64,1024]{1,0:T(8,128)(2,1)S(1)} %get-tuple-element.49), channel_id=1, source_target_pairs={{0,4},{1,5},{2,6},{3,7},{4,0},{5,1},{6,2},{7,3},{8,12},{9,13},{10,... | collective-permute-start | bytes 393224 | tf_op jit(solution)/shard_map/ppermute | solution.py:315
  64.4 6.7 %collective-permute-start.27 = (bf16[32,1024]{1,0:T(8,128)(2,1)S(1)}, bf16[32,1024]{1,0:T(8,128)(2,1)S(1)}, u32[]{:S(2)}, u32[]{:S(2)}) collective-permute-start(bf16[32,1024]{1,0:T(8,128)(2,1)S(1)} %get-tuple-element.58), channel_id=1, source_target_pairs={{0,16},{1,17},{2,18},{3,19},{4,20},{5,21},{6,22},{7,23},{8,24},{9,... | collective-permute-start | bytes 196616 | tf_op jit(solution)/shard_map/ppermute | solution.py:315
  65.8 6.2 %collective-permute-start.28 = (bf16[32,1024]{1,0:T(8,128)(2,1)S(1)}, bf16[32,1024]{1,0:T(8,128)(2,1)S(1)}, u32[]{:S(2)}, u32[]{:S(2)}) collective-permute-start(bf16[32,1024]{1,0:T(8,128)(2,1)S(1)} %get-tuple-element.59), channel_id=1, source_target_pairs={{0,24},{1,25},{2,26},{3,27},{4,28},{5,29},{6,30},{7,31},{8,16},{9,... | collective-permute-start | bytes 196616 | tf_op jit(solution)/shard_map/ppermute | solution.py:315
  68.1 4.7 %collective-permute-start.22 = (bf16[32,1024]{1,0:T(8,128)(2,1)S(1)}, bf16[32,1024]{1,0:T(8,128)(2,1)S(1)}, u32[]{:S(2)}, u32[]{:S(2)}) collective-permute-start(bf16[32,1024]{1,0:T(8,128)(2,1)S(1)} %get-tuple-element.51), channel_id=1, source_target_pairs={{0,8},{1,9},{2,10},{3,11},{4,12},{5,13},{6,14},{7,15},{8,0},{9,1},... | collective-permute-start | bytes 196616 | tf_op jit(solution)/shard_map/ppermute | solution.py:315

commit v6 on v5

--- a/solution.py
+++ b/solution.py
@@ -23,7 +23,7 @@
     return math.prod(value.shape) * jnp.dtype(value.dtype).itemsize
 
 
-def call(kernel, operands, in_specs, out_shape, out_specs, scratch=(), spare=4, flops=0):
+def call(kernel, operands, in_specs, out_shape, out_specs, scratch=(), spare=4, flops=0, aliases={}):
     outs = jax.tree.leaves(out_shape)
     sized = [v for v, s in zip(operands, in_specs) if s is VMEM]
     sized += [v for v, s in zip(outs, jax.tree.leaves(out_specs)) if s is VMEM]
@@ -35,6 +35,7 @@
         in_specs=in_specs,
         out_specs=out_specs,
         scratch_shapes=scratch,
+        input_output_aliases=aliases,
         compiler_params=pltpu.CompilerParams(vmem_limit_bytes=min(total + spare * 1024 * 1024, MOST_VMEM)),
         cost_estimate=pl.CostEstimate(
             flops=flops,
@@ -61,7 +62,7 @@
     return (slot.astype(jnp.int32) == grid) & (mask == 1)
 
 
-def pack_kernel(where, hidden_hbm, mask_hbm, target_hbm, turn_hbm, rows, plain, chosen_out, *scratch):
+def pack_kernel(where, hidden_hbm, mask_hbm, target_hbm, turn_hbm, rows, chosen_out, *scratch):
     hidden, mask, target, turn, sems = scratch
     copies = []
     for place, (source, held) in enumerate(
@@ -93,26 +94,17 @@
     rows[:, width:] = table.astype(jnp.bfloat16)
     copies[3].wait()
     packed = jnp.dot(one_hot, hidden[...], preferred_element_type=jnp.float32)
-    packed = packed.astype(jnp.bfloat16)
-    rows[:, :width] = packed
-    plain[...] = packed
-
-
-def join_kernel(skipped, *refs):
-    blocks, line, plain = refs[skipped:-2], refs[-2], refs[-1]
+    rows[:, :width] = packed.astype(jnp.bfloat16)
+
+
+def join_kernel(*refs):
+    blocks, line, plain = refs[:-2], refs[-2], refs[-1]
     start = 0
     for block in blocks:
         end = start + block.shape[0]
         line[start:end] = block[...]
         plain[start:end] = block[:, :plain.shape[1]]
         start = end
-
-
-def stack_kernel(*refs):
-    out, start = refs[-1], 0
-    for block in refs[:-1]:
-        out[start:start + block.shape[0]] = block[...]
-        start += block.shape[0]
 
 
 def stage_kernel(line, weight, held, same, sems):
@@ -223,11 +215,12 @@
             out[block // 2 * 2 + side] = piece.astype(out.dtype)
 
 
-def grad_kernel(blocks, groups, where, info, logits, weight, mine, theirs, *refs):
+def grad_kernel(blocks, groups, where, info, logits, weight, mine, handed, *refs):
     away, (logit_grad, loss) = refs[:2], refs[2:]
     rank, position, shard = where[0], where[1], where[2]
     height, columns = logits.shape
-    peak, mass, hit = merge([mine[...], theirs[...]])
+    table = jnp.where(rank % 2 == 1, mine[...], handed[...])
+    peak, mass, hit = table[0:1], table[1:2], table[2:3]
     log_total = jnp.broadcast_to(peak + jnp.log(mass), (8, height))
     log_total = reorder(log_total, position, groups)
     log_total = jnp.transpose(jnp.concatenate([log_total] * 16, axis=0))[:, 0:1]
@@ -247,21 +240,22 @@
     block_grads(blocks, where[0], 0, logit_grad[...], weight, kept)
 
 
-def weight_kernel(blocks, where, after, logit_grad, *refs):
-    pieces, (out, token, done, sems) = refs[:-4], refs[-4:]
+def weight_kernel(blocks, skipped, where, after, logit_grad, *refs):
+    out, token, done, sems = refs[-4:]
+    pieces = refs[skipped:-4]
     rank = where[0]
-    width = done.shape[0] // blocks
+    width = done.shape[0] // len(blocks)
     copies = []
-    for block in range(blocks):
-        done[block * width:(block + 1) * width] = lax.dot_general(
-            all_rows(pieces, block, width),
+    for place, block in enumerate(blocks):
+        done[place * width:(place + 1) * width] = lax.dot_general(
+            all_rows(pieces, place, width),
             logit_grad[...],
             (((0,), (0,)), ((), ())),
             preferred_element_type=jnp.float32,
         ).astype(jnp.bfloat16)
         start = pl.multiple_of((rank ^ block) * width, width)
         copy = pltpu.make_async_copy(
-            done.at[pl.ds(block * width, width)], out.at[pl.ds(start, width)], sems.at[block]
+            done.at[pl.ds(place * width, width)], out.at[pl.ds(start, width)], sems.at[place]
         )
         copy.start()
         copies.append(copy)
@@ -284,7 +278,7 @@
         out[...] = total[place * CAP:(place + 1) * CAP].astype(out.dtype)
 
 
-def unpack_kernel(chosen, *refs):
+def unpack_kernel(token, chosen, *refs):
     out = refs[-1]
     total = sum(ref[...].astype(jnp.float32) for ref in refs[:-1])
     out[...] = lax.dot_general(
@@ -305,12 +299,13 @@
     square = [(y, x) for x in reversed(range(xs)) for y in (1, 0) if x or y]
     flops = 2 * total_rows * depth * columns
 
-    def send(value, z=0, y=0, x=0, core=0):
+    def send(value, z=0, y=0, x=0, core=0, sources=(0, 1)):
         far, near = 2 * z + y, 2 * x + core
         pairs = [
             (d * ranks + v, (d ^ far) * ranks + (v ^ near))
             for d in range(dps)
             for v in range(ranks)
+            if v % 2 in sources
         ]
         return lax.ppermute(value, AXES, pairs)
 
@@ -318,7 +313,7 @@
     position = (group & 1) * zs + (group >> 1)
     where = jnp.stack([rank, position, group * ranks + rank]).astype(i32)
 
-    packed, plain, chosen = call(
+    packed, chosen = call(
         pack_kernel,
         (
             where,
@@ -330,26 +325,24 @@
         [SMEM] + [HBM] * 4,
         (
             shape((CAP, width + IDS), bf16),
-            shape((CAP, width), bf16),
             shape((CAP, tokens), bf16),
         ),
-        (VMEM,) * 3,
+        (VMEM,) * 2,
         [pltpu.VMEM((tokens, width), bf16)]
         + [pltpu.VMEM((1, tokens), i32)] * 3
         + [pltpu.SemaphoreType.DMA((4,))],
     )
 
-    far = [send(packed, z=z) for z in range(1, zs)]
-    small = {(y, x): send(plain if x else packed, y=y, x=x) for y, x in square}
-    far_rows = (zs - 1) * CAP
+    blocks = [packed] + [send(packed, z=z) for z in range(1, zs)]
+    line_rows = zs * CAP
     line, line_plain = call(
-        functools.partial(join_kernel, len(small)),
-        (*small.values(), *far),
-        [ANY] * len(small) + [VMEM] * len(far),
-        (shape((far_rows, width + IDS), bf16), shape((far_rows, width), bf16)),
+        join_kernel,
+        blocks,
+        [VMEM] * zs,
+        (shape((line_rows, width + IDS), bf16), shape((line_rows, width), bf16)),
         (VMEM, VMEM),
     )
-    large = {(y, x): send(line_plain if x else line, y=y, x=x) for y, x in square}
+    pieces = {(2 * x, y): send(line_plain if x else line, y=y, x=x) for y, x in square}
     held, same = call(
         stage_kernel,
         (line, in_hbm(weight)),
@@ -358,17 +351,9 @@
         (VMEM, VMEM),
         [pltpu.SemaphoreType.DMA((4,))],
     )
-    small[0, 0], large[0, 0] = packed, same
-    pieces = {}
-    for y, x in [(0, 0)] + square:
-        piece = call(
-            stack_kernel,
-            (small[y, x], large[y, x]),
-            [VMEM, VMEM],
-            shape((zs * CAP, small[y, x].shape[1]), bf16),
-            VMEM,
-        )
-        pieces[2 * x, y], pieces[2 * x + 1, y] = piece, send(piece, core=1)
+    pieces[0, 0] = same
+    for b, y in list(pieces):
+        pieces[b + 1, y] = send(pieces[b, y], core=1)
     rows = [pieces[b, y] for b in range(ranks) for y in range(2)]
 
     info = call(
@@ -387,21 +372,23 @@
         flops=flops,
     )
 
-    hops = [{"core": 1}]
-    hops += [{"x": 1 << bit} for bit in range((xs - 1).bit_length())] + [{"y": 1}]
-    hops += [{"z": 1 << bit} for bit in range((zs - 1).bit_length())]
-    for place, hop in enumerate(hops):
-        theirs = send(stats, **hop)
-        if place + 1 < len(hops):
-            stats = call(
-                merge_kernel, (stats, theirs), [VMEM] * 2, shape((8, total_rows), f32), VMEM
-            )
+    def combine(*tables):
+        return call(
+            merge_kernel, tables, [VMEM] * len(tables), shape((8, total_rows), f32), VMEM
+        )
+
+    stats = combine(stats, send(stats, core=1, sources=(0,)))
+    for bit in range((xs - 1).bit_length()):
+        stats = combine(stats, send(stats, x=1 << bit, sources=(1,)))
+    stats = combine(stats, send(stats, y=1, sources=(1,)))
+    stats = combine(stats, *[send(stats, z=z, sources=(1,)) for z in range(1, zs)])
+    handed = send(stats, core=1, sources=(1,))
 
     rows_part = total_rows // 4
     whole = (ranks, rows_part, width)
     *away, logit_grad, loss = call(
         functools.partial(grad_kernel, ranks, dps),
-        (where, info, logits, held, stats, theirs),
+        (where, info, logits, held, stats, handed),
         [SMEM] + [VMEM] * 5,
         (shape(whole, bf16),) * 2 + (shape((total_rows, columns), bf16), shape((1, 1), f32)),
         (VMEM,) * 3 + (SMEM,),
@@ -416,7 +403,7 @@
         flops=flops // 2,
     )
 
-    ends, token = [None] * zs, jnp.zeros((1, 1), i32)
+    ends = [None] * zs
     besides = [None, None]
     for chunk in (1, 0):
         besides[chunk] = send(away[chunk], core=1)
@@ -435,30 +422,42 @@
             x, y = divmod(ranks - 1 - place, 2)
             arrived.append(send(value, y=y, x=x))
         sums[chunk] = (corner, *arrived)
-    weight_grad, last_token = call(
-        functools.partial(weight_kernel, ranks),
-        (where, sums[0][0], logit_grad, *rows),
-        [SMEM, ANY] + [VMEM] * (1 + len(rows)),
-        (shape((depth, columns), bf16), shape((1, 1), i32)),
-        (HBM, SMEM),
-        [pltpu.VMEM((depth, columns), bf16), pltpu.SemaphoreType.DMA((ranks,))],
-        flops=flops,
-    )
+    weight_half = ranks // 2
+
+    def weight_part(first, after, partial):
+        blocks = range(first, first + weight_half)
+        chosen_rows = rows[2 * first:2 * (first + weight_half)]
+        return call(
+            functools.partial(weight_kernel, blocks, len(partial)),
+            (where, after, logit_grad, *partial, *chosen_rows),
+            [SMEM, ANY, VMEM] + [HBM] * len(partial) + [VMEM] * len(chosen_rows),
+            (shape((depth, columns), bf16), shape((1, 1), i32)),
+            (HBM, SMEM),
+            [
+                pltpu.VMEM((depth // 2, columns), bf16),
+                pltpu.SemaphoreType.DMA((weight_half,)),
+            ],
+            flops=flops // 2,
+            aliases={3: 0} if partial else {},
+        )
+
+    weight_grad, token = weight_part(0, sums[0][0], ())
     for chunk in (1, 0):
         near = chunk * zs // 2
         parts_z = call(
             functools.partial(corner_kernel, ranks - 1),
-            (token if chunk else last_token, *sums[chunk]),
+            (token, *sums[chunk]),
             [SMEM] + [VMEM] * ranks,
             tuple(shape((CAP, width), bf16 if near + z else f32) for z in range(zs // 2)),
             (VMEM,) * (zs // 2),
         )
         for z, value in enumerate(parts_z):
             ends[near + z] = send(value, z=near + z) if near + z else value
+    weight_grad, token = weight_part(weight_half, parts_z[0], (weight_grad,))
     hidden_grad = call(
         unpack_kernel,
-        (chosen, *ends),
-        [VMEM] * (1 + len(ends)),
+        (token, chosen, *ends),
+        [SMEM] + [VMEM] * (1 + len(ends)),
         shape((tokens, width), bf16),
         VMEM,
     )

time: 73.9 us -> 84.8 us (1.15)
  waiting for transfers between devices: 24.9 us -> 35.1 us
  Pallas kernels: 15.1 us -> 18.5 us
  starting transfers between devices: 32.8 us -> 29.9 us
    ppermute x29 -> x28, waiting for transfers between devices: 24.9 us -> 35.1 us  [send(): return lax.ppermute(value, AXES, pairs)]
    pallas_call x21 -> x18, Pallas kernels: 15.1 us -> 18.5 us  [call(): pl.pallas_call(kernel, out_shape=out_shape, in_specs=in_specs, out_specs=...]
    ppermute x29 -> x28, starting transfers between devices: 32.8 us -> 29.9 us  [send(): return lax.ppermute(value, AXES, pairs)]
  transfers between devices with their start and end apart: 29 -> 28, of which waited for: 15 -> 13; matrix products, arithmetic and copies ran while one was open for 0% -> 0% of each run, Pallas kernels for 12% -> 13%
where the time goes in v6:
time: 84.8 us; the launch traced here: 84.5 us
  waiting for transfers between devices  35.1 us (41%)
  starting transfers between devices  29.9 us (35%)
  Pallas kernels  18.5 us (22%)
  between operations  0.9 us (1%)
    ppermute x28, waiting for transfers between devices, send(): return lax.ppermute(value, AXES, pairs)  35.1 us
    ppermute x28, starting transfers between devices, send(): return lax.ppermute(value, AXES, pairs)  29.9 us
    pallas_call x18, Pallas kernels, call(): pl.pallas_call(kernel, out_shape=out_shape, in_specs=in_specs, out_specs=...  18.5 us
  transfers between devices with their start and end apart: 28, of which 13 were waited for; matrix products, arithmetic and copies ran while one was open for 0% of the time, Pallas kernels for 13%

profile of v6, /device:TPU:0, one launch (start us, length us, event | category | flops | bytes accessed | tf_op | source)
XLA Modules:
  0.0 84.5 jit_solution(14623238985979498922)
XLA Ops:
  0.7 1.8 %shard_map.85 = (bf16[32,1152]{1,0:T(8,128)(2,1)S(1)}, bf16[32,128]{1,0:T(8,128)(2,1)S(1)}) custom-call(s32[3]{0:T(128)S(1)} %pad_add_fusion.where, bf16[128,1024]{1,0:T(8,128)(2,1)} %hidden_hbm.1, s32[1,128]{1,0:T(1,128)} %bitcast.9, s32[1,128]{1,0:T(1,128)} %bitcast.10, s32[1,128]{1,0:T(1,128)} %bitcast.11), custom_call_target="tpu_custom_call" | custom-call | bytes 345612 | tf_op jit(solution)/shard_map/pallas_call | solution.py:32
  2.5 5.1 %collective-permute-start.2 = (bf16[32,1152]{1,0:T(8,128)(2,1)S(1)}, bf16[32,1152]{1,0:T(8,128)(2,1)S(1)}, u32[]{:S(2)}, u32[]{:S(2)}) collective-permute-start(bf16[32,1152]{1,0:T(8,128)(2,1)S(1)} %get-tuple-element.33.refs_0_), channel_id=1, source_target_pairs={{0,24},{1,25},{2,26},{3,27},{4,28},{5,29},{6,30},{7,31},{8,16},{9,... | collective-permute-start | bytes 221192 | tf_op jit(solution)/shard_map/ppermute | solution.py:310
  8.2 2.1 %collective-permute-done.2.refs_3_ = bf16[32,1152]{1,0:T(8,128)(2,1)S(1)} collective-permute-done((bf16[32,1152]{1,0:T(8,128)(2,1)S(1)}, bf16[32,1152]{1,0:T(8,128)(2,1)S(1)}, u32[]{:S(2)}, u32[]{:S(2)}) %collective-permute-start.2) | collective-permute-done | bytes 73760 | tf_op jit(solution)/shard_map/ppermute | solution.py:310
  10.4 3.5 %collective-permute-done.1.refs_2_ = bf16[32,1152]{1,0:T(8,128)(2,1)S(1)} collective-permute-done((bf16[32,1152]{1,0:T(8,128)(2,1)S(1)}, bf16[32,1152]{1,0:T(8,128)(2,1)S(1)}, u32[]{:S(2)}, u32[]{:S(2)}) %collective-permute-start.1) | collective-permute-done | bytes 73760 | tf_op jit(solution)/shard_map/ppermute | solution.py:310
  13.9 1.6 %collective-permute-start.3 = (bf16[128,1152]{1,0:T(8,128)(2,1)S(1)}, bf16[128,1152]{1,0:T(8,128)(2,1)S(1)}, u32[]{:S(2)}, u32[]{:S(2)}) collective-permute-start(bf16[128,1152]{1,0:T(8,128)(2,1)S(1)} %get-tuple-element.34.line), channel_id=1, source_target_pairs={{0,4},{1,5},{2,6},{3,7},{4,0},{5,1},{6,2},{7,3},{8,12},{9,13},{10,... | collective-permute-start | bytes 884744 | tf_op jit(solution)/shard_map/ppermute | solution.py:310
  15.5 1.4 %collective-permute-start.7 = (bf16[128,1024]{1,0:T(8,128)(2,1)S(1)}, bf16[128,1024]{1,0:T(8,128)(2,1)S(1)}, u32[]{:S(2)}, u32[]{:S(2)}) collective-permute-start(bf16[128,1024]{1,0:T(8,128)(2,1)S(1)} %get-tuple-element.37), channel_id=1, source_target_pairs={{0,6},{1,7},{2,4},{3,5},{4,2},{5,3},{6,0},{7,1},{8,14},{9,15},{10,... | collective-permute-start | bytes 786440 | tf_op jit(solution)/shard_map/ppermute | solution.py:310
  17.4 2.2 %shard_map.87 = (bf16[4096,512]{1,0:T(8,128)(2,1)S(1)}, bf16[128,1152]{1,0:T(8,128)(2,1)S(1)}) custom-call(bf16[128,1152]{1,0:T(8,128)(2,1)S(1)} %get-tuple-element.34.line, bf16[4096,512]{1,0:T(8,128)(2,1)} %weight.1), custom_call_target="tpu_custom_call" | custom-call | bytes 8978432 | tf_op jit(solution)/shard_map/pallas_call | solution.py:32
  19.7 8.2 %collective-permute-done.3.refs_1_ = bf16[128,1152]{1,0:T(8,128)(2,1)S(1)} collective-permute-done((bf16[128,1152]{1,0:T(8,128)(2,1)S(1)}, bf16[128,1152]{1,0:T(8,128)(2,1)S(1)}, u32[]{:S(2)}, u32[]{:S(2)}) %collective-permute-start.3) | collective-permute-done | bytes 294944 | tf_op jit(solution)/shard_map/ppermute | solution.py:310
  28.9 0.9 %collective-permute-done.9.refs_7_.refs_4_ = bf16[128,1024]{1,0:T(8,128)(2,1)S(1)} collective-permute-done((bf16[128,1024]{1,0:T(8,128)(2,1)S(1)}, bf16[128,1024]{1,0:T(8,128)(2,1)S(1)}, u32[]{:S(2)}, u32[]{:S(2)}) %collective-permute-start.9) | collective-permute-done | bytes 262176 | tf_op jit(solution)/shard_map/ppermute | solution.py:310
  30.2 2.2 %shard_map.89 = (f32[256,512]{1,0:T(8,128)S(1)}, f32[8,256]{1,0:T(8,128)S(1)}) custom-call(s32[3]{0:T(128)S(1)} %pad_add_fusion.where, f32[256,128]{1,0:T(8,128)S(1)} %shard_map.88.info, bf16[4096,512]{1,0:T(8,128)(2,1)S(1)} %get-tuple-element.36.weight, bf16[128,1152]{1,0:T(8,128)(2,1)S(1)} %get-tuple-element.35.refs_0_, ...), custom_call_target="tpu_custom_call" | custom-call | flops 1073741824 | bytes 7086092 | tf_op jit(solution)/shard_map/pallas_call | solution.py:32
  32.4 2.0 %collective-permute-start.10 = (f32[8,256]{1,0:T(8,128)S(1)}, f32[8,256]{1,0:T(8,128)S(1)}, u32[]{:S(2)}, u32[]{:S(2)}) collective-permute-start(f32[8,256]{1,0:T(8,128)S(1)} %get-tuple-element.39.refs_0_), channel_id=1, source_target_pairs={{0,1},{2,3},{4,5},{6,7},{8,9},{10,11},{12,13},{14,15},{16,17},{18,... | collective-permute-start | bytes 24584 | tf_op jit(solution)/shard_map/ppermute | solution.py:310
  34.5 0.8 collective-permute-done.10.refs_1_
  35.3 0.7 collective-permute-start.11
  36.0 0.7 collective-permute-start.12
  36.7 0.7 collective-permute-start.15
  37.4 0.7 collective-permute-start.14
  38.1 0.7 collective-permute-start.13
  38.8 1.3 %collective-permute-start.16 = (f32[8,256]{1,0:T(8,128)S(1)}, f32[8,256]{1,0:T(8,128)S(1)}, u32[]{:S(2)}, u32[]{:S(2)}) collective-permute-start(f32[8,256]{1,0:T(8,128)S(1)} %shard_map.93.mine), channel_id=1, source_target_pairs={{1,0},{3,2},{5,4},{7,6},{9,8},{11,10},{13,12},{15,14},{17,16},{19,... | collective-permute-start | bytes 24584 | tf_op jit(solution)/shard_map/ppermute | solution.py:310
  40.1 16.7 %collective-permute-done.16.handed = f32[8,256]{1,0:T(8,128)S(1)} collective-permute-done((f32[8,256]{1,0:T(8,128)S(1)}, f32[8,256]{1,0:T(8,128)S(1)}, u32[]{:S(2)}, u32[]{:S(2)}) %collective-permute-start.16) | collective-permute-done | bytes 8224 | tf_op jit(solution)/shard_map/ppermute | solution.py:310
  56.8 1.6 %shard_map.94 = (bf16[4,64,1024]{2,1,0:T(8,128)(2,1)S(1)}, bf16[4,64,1024]{2,1,0:T(8,128)(2,1)S(1)}, bf16[256,512]{1,0:T(8,128)(2,1)S(1)}, f32[1,1]{1,0:T(1,128)}) custom-call(s32[3]{0:T(128)S(1)} %pad_add_fusion.where, f32[256,128]{1,0:T(8,128)S(1)} %shard_map.88.info, f32[256,512]{1,0:T(8,128)S(1)} %get-tuple-element.38.logits, ...), custom_call_target="tpu_custom_call" | custom-call | flops 536870912 | bytes 6176784 | tf_op jit(solution)/shard_map/pallas_call | solution.py:32
  59.0 1.3 %shard_map.95 = (f32[4,64,1024]{2,1,0:T(8,128)S(1)}, f32[4,64,1024]{2,1,0:T(8,128)S(1)}) custom-call(s32[3]{0:T(128)S(1)} %pad_add_fusion.where, bf16[256,512]{1,0:T(8,128)(2,1)S(1)} %get-tuple-element.41.logit_grad, bf16[4096,512]{1,0:T(8,128)(2,1)S(1)} %get-tuple-element.36.weight), custom_call_target="tpu_custom_call" | custom-call | flops 536870912 | bytes 6553612 | tf_op jit(solution)/shard_map/pallas_call | solution.py:32
  60.5 2.7 %collective-permute-start.23 = (bf16[64,1024]{1,0:T(8,128)(2,1)S(1)}, bf16[64,1024]{1,0:T(8,128)(2,1)S(1)}, u32[]{:S(2)}, u32[]{:S(2)}) collective-permute-start(bf16[64,1024]{1,0:T(8,128)(2,1)S(1)} %get-tuple-element.57), channel_id=1, source_target_pairs={{0,6},{1,7},{2,4},{3,5},{4,2},{5,3},{6,0},{7,1},{8,14},{9,15},{10,... | collective-permute-start | bytes 393224 | tf_op jit(solution)/shard_map/ppermute | solution.py:310
  64.2 2.7 %collective-permute-start.18 = (bf16[64,1024]{1,0:T(8,128)(2,1)S(1)}, bf16[64,1024]{1,0:T(8,128)(2,1)S(1)}, u32[]{:S(2)}, u32[]{:S(2)}) collective-permute-start(bf16[64,1024]{1,0:T(8,128)(2,1)S(1)} %get-tuple-element.46), channel_id=1, source_target_pairs={{0,6},{1,7},{2,4},{3,5},{4,2},{5,3},{6,0},{7,1},{8,14},{9,15},{10,... | collective-permute-start | bytes 393224 | tf_op jit(solution)/shard_map/ppermute | solution.py:310
  67.8 1.8 %collective-permute-start.20 = (bf16[64,1024]{1,0:T(8,128)(2,1)S(1)}, bf16[64,1024]{1,0:T(8,128)(2,1)S(1)}, u32[]{:S(2)}, u32[]{:S(2)}) collective-permute-start(bf16[64,1024]{1,0:T(8,128)(2,1)S(1)} %get-tuple-element.48), channel_id=1, source_target_pairs={{0,4},{1,5},{2,6},{3,7},{4,0},{5,1},{6,2},{7,3},{8,12},{9,13},{10,... | collective-permute-start | bytes 393224 | tf_op jit(solution)/shard_map/ppermute | solution.py:310
  69.6 2.9 %shard_map.97 = (bf16[4096,512]{1,0:T(8,128)(2,1)}, s32[1,1]{1,0:T(1,128)}) custom-call(s32[3]{0:T(128)S(1)} %pad_add_fusion.where, f32[64,1024]{1,0:T(8,128)S(1)} %get-tuple-element.44.after.kept, bf16[256,512]{1,0:T(8,128)(2,1)S(1)} %get-tuple-element.41.logit_grad, bf16[128,1152]{1,0:T(8,128)(2,1)S(1)} %get-tuple-element.35.refs_0_, ...), custom_call_target="tpu_custom_call" | custom-call | flops 536870912 | bytes 5898256 | tf_op jit(solution)/shard_map/pallas_call | solution.py:32
  73.0 0.7 shard_map.101
  73.7 1.9 %collective-permute-start.26 = (bf16[32,1024]{1,0:T(8,128)(2,1)S(1)}, bf16[32,1024]{1,0:T(8,128)(2,1)S(1)}, u32[]{:S(2)}, u32[]{:S(2)}) collective-permute-start(bf16[32,1024]{1,0:T(8,128)(2,1)S(1)} %get-tuple-element.60), channel_id=1, source_target_pairs={{0,16},{1,17},{2,18},{3,19},{4,20},{5,21},{6,22},{7,23},{8,24},{9,... | collective-permute-start | bytes 196616 | tf_op jit(solution)/shard_map/ppermute | solution.py:310
  75.7 2.2 %collective-permute-start.27 = (bf16[32,1024]{1,0:T(8,128)(2,1)S(1)}, bf16[32,1024]{1,0:T(8,128)(2,1)S(1)}, u32[]{:S(2)}, u32[]{:S(2)}) collective-permute-start(bf16[32,1024]{1,0:T(8,128)(2,1)S(1)} %get-tuple-element.61), channel_id=1, source_target_pairs={{0,24},{1,25},{2,26},{3,27},{4,28},{5,29},{6,30},{7,31},{8,16},{9,... | collective-permute-start | bytes 196616 | tf_op jit(solution)/shard_map/ppermute | solution.py:310
  77.9 0.7 shard_map.98
  78.7 2.9 %shard_map.99 = (bf16[4096,512]{1,0:T(8,128)(2,1)}, s32[1,1]{1,0:T(1,128)}) custom-call(s32[3]{0:T(128)S(1)} %pad_add_fusion.where, f32[32,1024]{1,0:T(8,128)S(1)} %get-tuple-element.49.after.refs_0_, bf16[256,512]{1,0:T(8,128)(2,1)S(1)} %get-tuple-element.41.logit_grad, ...), custom_call_target="tpu_custom_call", output_to_operand_aliasing={{0}: (3, {})} | custom-call | flops 536870912 | bytes 9830416 | tf_op jit(solution)/shard_map/pallas_call | solution.py:32
  81.7 1.2 %collective-permute-done.21.refs_1_ = bf16[32,1024]{1,0:T(8,128)(2,1)S(1)} collective-permute-done((bf16[32,1024]{1,0:T(8,128)(2,1)S(1)}, bf16[32,1024]{1,0:T(8,128)(2,1)S(1)}, u32[]{:S(2)}, u32[]{:S(2)}) %collective-permute-start.21) | collective-permute-done | bytes 65568 | tf_op jit(solution)/shard_map/ppermute | solution.py:310
  82.9 1.6 %shard_map.102 = bf16[128,1024]{1,0:T(8,128)(2,1)} custom-call(s32[1,1]{1,0:T(1,128)} %get-tuple-element.51.token, bf16[32,128]{1,0:T(8,128)(2,1)S(1)} %get-tuple-element.52.chosen, f32[32,1024]{1,0:T(8,128)S(1)} %get-tuple-element.49.after.refs_0_, bf16[32,1024]{1,0:T(8,128)(2,1)S(1)} %collective-permute-done.21.refs_1_, ...), custom_call_target="tpu_custom_call" | custom-call | bytes 598020 | tf_op jit(solution)/shard_map/pallas_call | solution.py:32
  (45 shorter events, 6.3 us)
Async XLA Ops:
  0.6 27.9 %copy-start = (f32[32]{0:T(128)S(1)}, f32[32]{0:T(128)}, u32[]{:S(2)}) copy-start(f32[32]{0:T(128)} %param.11) | copy-start | bytes 388
  2.5 7.9 %collective-permute-start.2 = (bf16[32,1152]{1,0:T(8,128)(2,1)S(1)}, bf16[32,1152]{1,0:T(8,128)(2,1)S(1)}, u32[]{:S(2)}, u32[]{:S(2)}) collective-permute-start(bf16[32,1152]{1,0:T(8,128)(2,1)S(1)} %get-tuple-element.33.refs_0_), channel_id=1, source_target_pairs={{0,24},{1,25},{2,26},{3,27},{4,28},{5,29},{6,30},{7,31},{8,16},{9,... | collective-permute-start | bytes 221192 | tf_op jit(solution)/shard_map/ppermute | solution.py:310
  7.6 6.2 %collective-permute-start.1 = (bf16[32,1152]{1,0:T(8,128)(2,1)S(1)}, bf16[32,1152]{1,0:T(8,128)(2,1)S(1)}, u32[]{:S(2)}, u32[]{:S(2)}) collective-permute-start(bf16[32,1152]{1,0:T(8,128)(2,1)S(1)} %get-tuple-element.33.refs_0_), channel_id=1, source_target_pairs={{0,16},{1,17},{2,18},{3,19},{4,20},{5,21},{6,22},{7,23},{8,24},{9,... | collective-permute-start | bytes 221192 | tf_op jit(solution)/shard_map/ppermute | solution.py:310
  7.6 6.2 %collective-permute-start = (bf16[32,1152]{1,0:T(8,128)(2,1)S(1)}, bf16[32,1152]{1,0:T(8,128)(2,1)S(1)}, u32[]{:S(2)}, u32[]{:S(2)}) collective-permute-start(bf16[32,1152]{1,0:T(8,128)(2,1)S(1)} %get-tuple-element.33.refs_0_), channel_id=1, source_target_pairs={{0,8},{1,9},{2,10},{3,11},{4,12},{5,13},{6,14},{7,15},{8,0},{9,1},... | collective-permute-start | bytes 221192 | tf_op jit(solution)/shard_map/ppermute | solution.py:310
  13.9 14.0 %collective-permute-start.3 = (bf16[128,1152]{1,0:T(8,128)(2,1)S(1)}, bf16[128,1152]{1,0:T(8,128)(2,1)S(1)}, u32[]{:S(2)}, u32[]{:S(2)}) collective-permute-start(bf16[128,1152]{1,0:T(8,128)(2,1)S(1)} %get-tuple-element.34.line), channel_id=1, source_target_pairs={{0,4},{1,5},{2,6},{3,7},{4,0},{5,1},{6,2},{7,3},{8,12},{9,13},{10,... | collective-permute-start | bytes 884744 | tf_op jit(solution)/shard_map/ppermute | solution.py:310
  15.5 12.5 %collective-permute-start.7 = (bf16[128,1024]{1,0:T(8,128)(2,1)S(1)}, bf16[128,1024]{1,0:T(8,128)(2,1)S(1)}, u32[]{:S(2)}, u32[]{:S(2)}) collective-permute-start(bf16[128,1024]{1,0:T(8,128)(2,1)S(1)} %get-tuple-element.37), channel_id=1, source_target_pairs={{0,6},{1,7},{2,4},{3,5},{4,2},{5,3},{6,0},{7,1},{8,14},{9,15},{10,... | collective-permute-start | bytes 786440 | tf_op jit(solution)/shard_map/ppermute | solution.py:310
  16.9 11.6 %collective-permute-start.6 = (bf16[128,1024]{1,0:T(8,128)(2,1)S(1)}, bf16[128,1024]{1,0:T(8,128)(2,1)S(1)}, u32[]{:S(2)}, u32[]{:S(2)}) collective-permute-start(bf16[128,1024]{1,0:T(8,128)(2,1)S(1)} %get-tuple-element.37), channel_id=1, source_target_pairs={{0,2},{1,3},{2,0},{3,1},{4,6},{5,7},{6,4},{7,5},{8,10},{9,11},{10,... | collective-permute-start | bytes 786440 | tf_op jit(solution)/shard_map/ppermute | solution.py:310
  19.6 9.3 %collective-permute-start.4 = (bf16[128,1152]{1,0:T(8,128)(2,1)S(1)}, bf16[128,1152]{1,0:T(8,128)(2,1)S(1)}, u32[]{:S(2)}, u32[]{:S(2)}) collective-permute-start(bf16[128,1152]{1,0:T(8,128)(2,1)S(1)} %get-tuple-element.35.refs_0_), channel_id=1, source_target_pairs={{0,1},{1,0},{2,3},{3,2},{4,5},{5,4},{6,7},{7,6},{8,9},{9,8},{10,11... | collective-permute-start | bytes 884744 | tf_op jit(solution)/shard_map/ppermute | solution.py:310
  27.9 2.3 %collective-permute-start.5 = (bf16[128,1152]{1,0:T(8,128)(2,1)S(1)}, bf16[128,1152]{1,0:T(8,128)(2,1)S(1)}, u32[]{:S(2)}, u32[]{:S(2)}) collective-permute-start(bf16[128,1152]{1,0:T(8,128)(2,1)S(1)} %collective-permute-done.3.refs_1_), channel_id=1, source_target_pairs={{0,1},{1,0},{2,3},{3,2},{4,5},{5,4},{6,7},{7,6},{8,9},{9,8},{10,11... | collective-permute-start | bytes 884744 | tf_op jit(solution)/shard_map/ppermute | solution.py:310
  27.9 2.0 %collective-permute-start.9 = (bf16[128,1024]{1,0:T(8,128)(2,1)S(1)}, bf16[128,1024]{1,0:T(8,128)(2,1)S(1)}, u32[]{:S(2)}, u32[]{:S(2)}) collective-permute-start(bf16[128,1024]{1,0:T(8,128)(2,1)S(1)} %collective-permute-done.7.refs_5_.refs_2_), channel_id=1, source_target_pairs={{0,1},{1,0},{2,3},{3,2},{4,5},{5,4},{6,7},{7,6},{8,9},{9,8},{10,11... | collective-permute-start | bytes 786440 | tf_op jit(solution)/shard_map/ppermute | solution.py:310
  28.5 1.7 %collective-permute-start.8 = (bf16[128,1024]{1,0:T(8,128)(2,1)S(1)}, bf16[128,1024]{1,0:T(8,128)(2,1)S(1)}, u32[]{:S(2)}, u32[]{:S(2)}) collective-permute-start(bf16[128,1024]{1,0:T(8,128)(2,1)S(1)} %collective-permute-done.6.refs_4_.refs_1_), channel_id=1, source_target_pairs={{0,1},{1,0},{2,3},{3,2},{4,5},{5,4},{6,7},{7,6},{8,9},{9,8},{10,11... | collective-permute-start | bytes 786440 | tf_op jit(solution)/shard_map/ppermute | solution.py:310
  32.4 2.9 %collective-permute-start.10 = (f32[8,256]{1,0:T(8,128)S(1)}, f32[8,256]{1,0:T(8,128)S(1)}, u32[]{:S(2)}, u32[]{:S(2)}) collective-permute-start(f32[8,256]{1,0:T(8,128)S(1)} %get-tuple-element.39.refs_0_), channel_id=1, source_target_pairs={{0,1},{2,3},{4,5},{6,7},{8,9},{10,11},{12,13},{14,15},{16,17},{18,... | collective-permute-start | bytes 24584 | tf_op jit(solution)/shard_map/ppermute | solution.py:310
  35.3 0.7 collective-permute-start.11
  36.0 0.7 collective-permute-start.12
  36.7 2.0 %collective-permute-start.15 = (f32[8,256]{1,0:T(8,128)S(1)}, f32[8,256]{1,0:T(8,128)S(1)}, u32[]{:S(2)}, u32[]{:S(2)}) collective-permute-start(f32[8,256]{1,0:T(8,128)S(1)} %shard_map.92.refs_0_), channel_id=1, source_target_pairs={{1,25},{3,27},{5,29},{7,31},{9,17},{11,19},{13,21},{15,23},{17,9},... | collective-permute-start | bytes 24584 | tf_op jit(solution)/shard_map/ppermute | solution.py:310
  37.4 1.4 %collective-permute-start.14 = (f32[8,256]{1,0:T(8,128)S(1)}, f32[8,256]{1,0:T(8,128)S(1)}, u32[]{:S(2)}, u32[]{:S(2)}) collective-permute-start(f32[8,256]{1,0:T(8,128)S(1)} %shard_map.92.refs_0_), channel_id=1, source_target_pairs={{1,17},{3,19},{5,21},{7,23},{9,25},{11,27},{13,29},{15,31},{17,1},... | collective-permute-start | bytes 24584 | tf_op jit(solution)/shard_map/ppermute | solution.py:310
  38.1 0.7 collective-permute-start.13
  38.8 18.0 %collective-permute-start.16 = (f32[8,256]{1,0:T(8,128)S(1)}, f32[8,256]{1,0:T(8,128)S(1)}, u32[]{:S(2)}, u32[]{:S(2)}) collective-permute-start(f32[8,256]{1,0:T(8,128)S(1)} %shard_map.93.mine), channel_id=1, source_target_pairs={{1,0},{3,2},{5,4},{7,6},{9,8},{11,10},{13,12},{15,14},{17,16},{19,... | collective-permute-start | bytes 24584 | tf_op jit(solution)/shard_map/ppermute | solution.py:310
  58.4 2.0 %collective-permute-start.22 = (bf16[4,64,1024]{2,1,0:T(8,128)(2,1)S(1)}, bf16[4,64,1024]{2,1,0:T(8,128)(2,1)S(1)}, u32[]{:S(2)}, u32[]{:S(2)}) collective-permute-start(bf16[4,64,1024]{2,1,0:T(8,128)(2,1)S(1)} %get-tuple-element.55), channel_id=1, source_target_pairs={{0,1},{1,0},{2,3},{3,2},{4,5},{5,4},{6,7},{7,6},{8,9},{9,8},{10,11... | collective-permute-start | bytes 1572872 | tf_op jit(solution)/shard_map/ppermute | solution.py:310
  58.6 5.4 %collective-permute-start.17 = (bf16[4,64,1024]{2,1,0:T(8,128)(2,1)S(1)}, bf16[4,64,1024]{2,1,0:T(8,128)(2,1)S(1)}, u32[]{:S(2)}, u32[]{:S(2)}) collective-permute-start(bf16[4,64,1024]{2,1,0:T(8,128)(2,1)S(1)} %get-tuple-element.43), channel_id=1, source_target_pairs={{0,1},{1,0},{2,3},{3,2},{4,5},{5,4},{6,7},{7,6},{8,9},{9,8},{10,11... | collective-permute-start | bytes 1572872 | tf_op jit(solution)/shard_map/ppermute | solution.py:310
  60.5 7.3 %collective-permute-start.23 = (bf16[64,1024]{1,0:T(8,128)(2,1)S(1)}, bf16[64,1024]{1,0:T(8,128)(2,1)S(1)}, u32[]{:S(2)}, u32[]{:S(2)}) collective-permute-start(bf16[64,1024]{1,0:T(8,128)(2,1)S(1)} %get-tuple-element.57), channel_id=1, source_target_pairs={{0,6},{1,7},{2,4},{3,5},{4,2},{5,3},{6,0},{7,1},{8,14},{9,15},{10,... | collective-permute-start | bytes 393224 | tf_op jit(solution)/shard_map/ppermute | solution.py:310
  63.2 9.2 %collective-permute-start.24 = (bf16[64,1024]{1,0:T(8,128)(2,1)S(1)}, bf16[64,1024]{1,0:T(8,128)(2,1)S(1)}, u32[]{:S(2)}, u32[]{:S(2)}) collective-permute-start(bf16[64,1024]{1,0:T(8,128)(2,1)S(1)} %get-tuple-element.58), channel_id=1, source_target_pairs={{0,2},{1,3},{2,0},{3,1},{4,6},{5,7},{6,4},{7,5},{8,10},{9,11},{10,... | collective-permute-start | bytes 393224 | tf_op jit(solution)/shard_map/ppermute | solution.py:310
  63.8 9.2 %collective-permute-start.25 = (bf16[64,1024]{1,0:T(8,128)(2,1)S(1)}, bf16[64,1024]{1,0:T(8,128)(2,1)S(1)}, u32[]{:S(2)}, u32[]{:S(2)}) collective-permute-start(bf16[64,1024]{1,0:T(8,128)(2,1)S(1)} %get-tuple-element.59), channel_id=1, source_target_pairs={{0,4},{1,5},{2,6},{3,7},{4,0},{5,1},{6,2},{7,3},{8,12},{9,13},{10,... | collective-permute-start | bytes 393224 | tf_op jit(solution)/shard_map/ppermute | solution.py:310
  64.2 13.7 %collective-permute-start.18 = (bf16[64,1024]{1,0:T(8,128)(2,1)S(1)}, bf16[64,1024]{1,0:T(8,128)(2,1)S(1)}, u32[]{:S(2)}, u32[]{:S(2)}) collective-permute-start(bf16[64,1024]{1,0:T(8,128)(2,1)S(1)} %get-tuple-element.46), channel_id=1, source_target_pairs={{0,6},{1,7},{2,4},{3,5},{4,2},{5,3},{6,0},{7,1},{8,14},{9,15},{10,... | collective-permute-start | bytes 393224 | tf_op jit(solution)/shard_map/ppermute | solution.py:310
  66.9 11.0 %collective-permute-start.19 = (bf16[64,1024]{1,0:T(8,128)(2,1)S(1)}, bf16[64,1024]{1,0:T(8,128)(2,1)S(1)}, u32[]{:S(2)}, u32[]{:S(2)}) collective-permute-start(bf16[64,1024]{1,0:T(8,128)(2,1)S(1)} %get-tuple-element.47), channel_id=1, source_target_pairs={{0,2},{1,3},{2,0},{3,1},{4,6},{5,7},{6,4},{7,5},{8,10},{9,11},{10,... | collective-permute-start | bytes 393224 | tf_op jit(solution)/shard_map/ppermute | solution.py:310
  67.8 10.1 %collective-permute-start.20 = (bf16[64,1024]{1,0:T(8,128)(2,1)S(1)}, bf16[64,1024]{1,0:T(8,128)(2,1)S(1)}, u32[]{:S(2)}, u32[]{:S(2)}) collective-permute-start(bf16[64,1024]{1,0:T(8,128)(2,1)S(1)} %get-tuple-element.48), channel_id=1, source_target_pairs={{0,4},{1,5},{2,6},{3,7},{4,0},{5,1},{6,2},{7,3},{8,12},{9,13},{10,... | collective-permute-start | bytes 393224 | tf_op jit(solution)/shard_map/ppermute | solution.py:310
  73.7 7.8 %collective-permute-start.26 = (bf16[32,1024]{1,0:T(8,128)(2,1)S(1)}, bf16[32,1024]{1,0:T(8,128)(2,1)S(1)}, u32[]{:S(2)}, u32[]{:S(2)}) collective-permute-start(bf16[32,1024]{1,0:T(8,128)(2,1)S(1)} %get-tuple-element.60), channel_id=1, source_target_pairs={{0,16},{1,17},{2,18},{3,19},{4,20},{5,21},{6,22},{7,23},{8,24},{9,... | collective-permute-start | bytes 196616 | tf_op jit(solution)/shard_map/ppermute | solution.py:310
  75.7 6.1 %collective-permute-start.27 = (bf16[32,1024]{1,0:T(8,128)(2,1)S(1)}, bf16[32,1024]{1,0:T(8,128)(2,1)S(1)}, u32[]{:S(2)}, u32[]{:S(2)}) collective-permute-start(bf16[32,1024]{1,0:T(8,128)(2,1)S(1)} %get-tuple-element.61), channel_id=1, source_target_pairs={{0,24},{1,25},{2,26},{3,27},{4,28},{5,29},{6,30},{7,31},{8,16},{9,... | collective-permute-start | bytes 196616 | tf_op jit(solution)/shard_map/ppermute | solution.py:310
  78.6 4.3 %collective-permute-start.21 = (bf16[32,1024]{1,0:T(8,128)(2,1)S(1)}, bf16[32,1024]{1,0:T(8,128)(2,1)S(1)}, u32[]{:S(2)}, u32[]{:S(2)}) collective-permute-start(bf16[32,1024]{1,0:T(8,128)(2,1)S(1)} %get-tuple-element.53), channel_id=1, source_target_pairs={{0,8},{1,9},{2,10},{3,11},{4,12},{5,13},{6,14},{7,15},{8,0},{9,1},... | collective-permute-start | bytes 196616 | tf_op jit(solution)/shard_map/ppermute | solution.py:310

commit v7 on v6

--- a/solution.py
+++ b/solution.py
@@ -49,6 +49,13 @@
     return pltpu.with_memory_space_constraint(value, pltpu.HBM)
 
 
+def coordinates():
+    group, rank = lax.axis_index("dp"), lax.axis_index("vocab")
+    groups, ranks = lax.axis_size("dp"), lax.axis_size("vocab")
+    position = group % 2 * (groups // 2) + group // 2
+    return rank, position, group * ranks + rank
+
+
 def choose(mask):
     tokens = mask.shape[1]
     wide = jnp.broadcast_to(mask.astype(jnp.float32), (8, tokens))
@@ -62,7 +69,7 @@
     return (slot.astype(jnp.int32) == grid) & (mask == 1)
 
 
-def pack_kernel(where, hidden_hbm, mask_hbm, target_hbm, turn_hbm, rows, chosen_out, *scratch):
+def pack_kernel(hidden_hbm, mask_hbm, target_hbm, turn_hbm, rows, chosen_out, *scratch):
     hidden, mask, target, turn, sems = scratch
     copies = []
     for place, (source, held) in enumerate(
@@ -158,9 +165,9 @@
     return jnp.concatenate([ref[:, :width] for ref in pieces[2 * block:2 * block + 2]], axis=0)
 
 
-def logits_kernel(blocks, groups, where, info, weight, *refs):
+def logits_kernel(blocks, groups, info, weight, *refs):
     pieces, (logits, stats) = refs[:-2], refs[-2:]
-    rank, position, shard = where[0], where[1], where[2]
+    rank, position, shard = coordinates()
     width = weight.shape[0] // blocks
     total = None
     for block in range(blocks):
@@ -215,9 +222,9 @@
             out[block // 2 * 2 + side] = piece.astype(out.dtype)
 
 
-def grad_kernel(blocks, groups, where, info, logits, weight, mine, handed, *refs):
+def grad_kernel(blocks, groups, info, logits, weight, mine, handed, *refs):
     away, (logit_grad, loss) = refs[:2], refs[2:]
-    rank, position, shard = where[0], where[1], where[2]
+    rank, position, shard = coordinates()
     height, columns = logits.shape
     table = jnp.where(rank % 2 == 1, mine[...], handed[...])
     peak, mass, hit = table[0:1], table[1:2], table[2:3]
@@ -236,32 +243,31 @@
     block_grads(blocks, rank, 1, grad, weight, away)
 
 
-def kept_kernel(blocks, where, logit_grad, weight, *kept):
-    block_grads(blocks, where[0], 0, logit_grad[...], weight, kept)
-
-
-def weight_kernel(blocks, skipped, where, after, logit_grad, *refs):
-    out, token, done, sems = refs[-4:]
-    pieces = refs[skipped:-4]
-    rank = where[0]
-    width = done.shape[0] // len(blocks)
+def kept_kernel(blocks, logit_grad, weight, *kept):
+    block_grads(blocks, coordinates()[0], 0, logit_grad[...], weight, kept)
+
+
+def weight_kernel(blocks, after, logit_grad, *refs):
+    pieces, (out, finished, done, sems) = refs[:-4], refs[-4:]
+    rank = coordinates()[0]
+    finished[...] = jnp.zeros_like(finished)
+    width = done.shape[0] // blocks
     copies = []
-    for place, block in enumerate(blocks):
-        done[place * width:(place + 1) * width] = lax.dot_general(
-            all_rows(pieces, place, width),
+    for block in range(blocks):
+        done[block * width:(block + 1) * width] = lax.dot_general(
+            all_rows(pieces, block, width),
             logit_grad[...],
             (((0,), (0,)), ((), ())),
             preferred_element_type=jnp.float32,
         ).astype(jnp.bfloat16)
         start = pl.multiple_of((rank ^ block) * width, width)
         copy = pltpu.make_async_copy(
-            done.at[pl.ds(place * width, width)], out.at[pl.ds(start, width)], sems.at[place]
+            done.at[pl.ds(block * width, width)], out.at[pl.ds(start, width)], sems.at[block]
         )
         copy.start()
         copies.append(copy)
     for copy in copies:
         copy.wait()
-    token[0, 0] = rank
 
 
 def pair_kernel(kept, beside, *outs):
@@ -270,7 +276,7 @@
         out[...] = total.astype(out.dtype)
 
 
-def corner_kernel(count, token, kept, *refs):
+def corner_kernel(count, after, kept, *refs):
     total = kept[...]
     for ref in refs[:count]:
         total = total + ref[...].astype(jnp.float32)
@@ -278,7 +284,7 @@
         out[...] = total[place * CAP:(place + 1) * CAP].astype(out.dtype)
 
 
-def unpack_kernel(token, chosen, *refs):
+def unpack_kernel(chosen, *refs):
     out = refs[-1]
     total = sum(ref[...].astype(jnp.float32) for ref in refs[:-1])
     out[...] = lax.dot_general(
@@ -299,30 +305,24 @@
     square = [(y, x) for x in reversed(range(xs)) for y in (1, 0) if x or y]
     flops = 2 * total_rows * depth * columns
 
-    def send(value, z=0, y=0, x=0, core=0, sources=(0, 1)):
+    def send(value, z=0, y=0, x=0, core=0, cores=(0, 1)):
         far, near = 2 * z + y, 2 * x + core
         pairs = [
-            (d * ranks + v, (d ^ far) * ranks + (v ^ near))
+            (d * ranks + v, (d ^ far) * ranks + (v ^ near) if v % 2 in cores else d * ranks + v)
             for d in range(dps)
             for v in range(ranks)
-            if v % 2 in sources
         ]
         return lax.ppermute(value, AXES, pairs)
-
-    group, rank = lax.axis_index("dp"), lax.axis_index("vocab")
-    position = (group & 1) * zs + (group >> 1)
-    where = jnp.stack([rank, position, group * ranks + rank]).astype(i32)
 
     packed, chosen = call(
         pack_kernel,
         (
-            where,
             in_hbm(hidden),
             in_hbm(loss_mask.reshape(1, tokens)),
             in_hbm(target_ids.reshape(1, tokens)),
             in_hbm(turn_ids.reshape(1, tokens)),
         ),
-        [SMEM] + [HBM] * 4,
+        [HBM] * 4,
         (
             shape((CAP, width + IDS), bf16),
             shape((CAP, tokens), bf16),
@@ -365,8 +365,8 @@
     )
     logits, stats = call(
         functools.partial(logits_kernel, ranks, dps),
-        (where, info, held, *rows),
-        [SMEM] + [VMEM] * (2 + len(rows)),
+        (info, held, *rows),
+        [VMEM] * (2 + len(rows)),
         (shape((total_rows, columns), f32), shape((8, total_rows), f32)),
         (VMEM, VMEM),
         flops=flops,
@@ -377,27 +377,27 @@
             merge_kernel, tables, [VMEM] * len(tables), shape((8, total_rows), f32), VMEM
         )
 
-    stats = combine(stats, send(stats, core=1, sources=(0,)))
+    stats = combine(stats, send(stats, core=1))
     for bit in range((xs - 1).bit_length()):
-        stats = combine(stats, send(stats, x=1 << bit, sources=(1,)))
-    stats = combine(stats, send(stats, y=1, sources=(1,)))
-    stats = combine(stats, *[send(stats, z=z, sources=(1,)) for z in range(1, zs)])
-    handed = send(stats, core=1, sources=(1,))
+        stats = combine(stats, send(stats, x=1 << bit, cores=(1,)))
+    stats = combine(stats, send(stats, y=1, cores=(1,)))
+    stats = combine(stats, *[send(stats, z=z, cores=(1,)) for z in range(1, zs)])
+    handed = send(stats, core=1)
 
     rows_part = total_rows // 4
     whole = (ranks, rows_part, width)
     *away, logit_grad, loss = call(
         functools.partial(grad_kernel, ranks, dps),
-        (where, info, logits, held, stats, handed),
-        [SMEM] + [VMEM] * 5,
+        (info, logits, held, stats, handed),
+        [VMEM] * 5,
         (shape(whole, bf16),) * 2 + (shape((total_rows, columns), bf16), shape((1, 1), f32)),
         (VMEM,) * 3 + (SMEM,),
         flops=flops // 2,
     )
     kept = call(
         functools.partial(kept_kernel, ranks),
-        (where, logit_grad, held),
-        [SMEM] + [VMEM] * 2,
+        (logit_grad, held),
+        [VMEM] * 2,
         (shape(whole, f32),) * 2,
         (VMEM,) * 2,
         flops=flops // 2,
@@ -422,42 +422,30 @@
             x, y = divmod(ranks - 1 - place, 2)
             arrived.append(send(value, y=y, x=x))
         sums[chunk] = (corner, *arrived)
-    weight_half = ranks // 2
-
-    def weight_part(first, after, partial):
-        blocks = range(first, first + weight_half)
-        chosen_rows = rows[2 * first:2 * (first + weight_half)]
-        return call(
-            functools.partial(weight_kernel, blocks, len(partial)),
-            (where, after, logit_grad, *partial, *chosen_rows),
-            [SMEM, ANY, VMEM] + [HBM] * len(partial) + [VMEM] * len(chosen_rows),
-            (shape((depth, columns), bf16), shape((1, 1), i32)),
-            (HBM, SMEM),
-            [
-                pltpu.VMEM((depth // 2, columns), bf16),
-                pltpu.SemaphoreType.DMA((weight_half,)),
-            ],
-            flops=flops // 2,
-            aliases={3: 0} if partial else {},
-        )
-
-    weight_grad, token = weight_part(0, sums[0][0], ())
+    weight_grad, finished = call(
+        functools.partial(weight_kernel, ranks),
+        (sums[0][0], logit_grad, *rows),
+        [ANY] + [VMEM] * (1 + len(rows)),
+        (shape((depth, columns), bf16), shape((8, 128), f32)),
+        (HBM, VMEM),
+        [pltpu.VMEM((depth, columns), bf16), pltpu.SemaphoreType.DMA((ranks,))],
+        flops=flops,
+    )
     for chunk in (1, 0):
         near = chunk * zs // 2
         parts_z = call(
             functools.partial(corner_kernel, ranks - 1),
-            (token, *sums[chunk]),
-            [SMEM] + [VMEM] * ranks,
+            (logit_grad if chunk else finished, *sums[chunk]),
+            [ANY] + [VMEM] * ranks,
             tuple(shape((CAP, width), bf16 if near + z else f32) for z in range(zs // 2)),
             (VMEM,) * (zs // 2),
         )
         for z, value in enumerate(parts_z):
             ends[near + z] = send(value, z=near + z) if near + z else value
-    weight_grad, token = weight_part(weight_half, parts_z[0], (weight_grad,))
     hidden_grad = call(
         unpack_kernel,
-        (token, chosen, *ends),
-        [SMEM] + [VMEM] * (1 + len(ends)),
+        (chosen, *ends),
+        [VMEM] * (1 + len(ends)),
         shape((tokens, width), bf16),
         VMEM,
     )

time: 84.8 us -> 78.4 us (0.925)
  starting transfers between devices: 29.9 us -> 43.3 us
  waiting for transfers between devices: 35.1 us -> 22.8 us
  Pallas kernels: 18.5 us -> 11.3 us
    ppermute x28, starting transfers between devices: 29.9 us -> 43.3 us  [send(): return lax.ppermute(value, AXES, pairs)]
    ppermute x28, waiting for transfers between devices: 35.1 us -> 22.8 us  [send(): return lax.ppermute(value, AXES, pairs)]
    pallas_call x18 -> x17, Pallas kernels: 18.5 us -> 11.3 us  [call(): pl.pallas_call(kernel, out_shape=out_shape, in_specs=in_specs, out_specs=...]
  transfers between devices with their start and end apart: 28 -> 28, of which waited for: 13 -> 14; matrix products, arithmetic and copies ran while one was open for 0% -> 0% of each run, Pallas kernels for 13% -> 8%
where the time goes in v7:
time: 78.4 us; the launch traced here: 78.2 us
  starting transfers between devices  43.3 us (55%)
  waiting for transfers between devices  22.8 us (29%)
  Pallas kernels  11.3 us (14%)
  between operations  0.85 us (1%)
    ppermute x28, starting transfers between devices, send(): return lax.ppermute(value, AXES, pairs)  43.3 us
    ppermute x28, waiting for transfers between devices, send(): return lax.ppermute(value, AXES, pairs)  22.8 us
    pallas_call x17, Pallas kernels, call(): pl.pallas_call(kernel, out_shape=out_shape, in_specs=in_specs, out_specs=...  11.3 us
  transfers between devices with their start and end apart: 28, of which 14 were waited for; matrix products, arithmetic and copies ran while one was open for 0% of the time, Pallas kernels for 8%

profile of v7, /device:TPU:0, one launch (start us, length us, event | category | flops | bytes accessed | tf_op | source)
XLA Modules:
  0.0 78.2 jit_solution(16152223431280758946)
XLA Ops:
  0.6 1.2 %shard_map.85 = (bf16[32,1152]{1,0:T(8,128)(2,1)S(1)}, bf16[32,128]{1,0:T(8,128)(2,1)S(1)}) custom-call(bf16[128,1024]{1,0:T(8,128)(2,1)} %hidden_hbm.1, s32[1,128]{1,0:T(1,128)} %bitcast.6, s32[1,128]{1,0:T(1,128)} %bitcast.7, s32[1,128]{1,0:T(1,128)} %bitcast.8), custom_call_target="tpu_custom_call" | custom-call | bytes 345600 | tf_op jit(solution)/shard_map/pallas_call | solution.py:32
  1.9 5.1 %collective-permute-start.2 = (bf16[32,1152]{1,0:T(8,128)(2,1)S(1)}, bf16[32,1152]{1,0:T(8,128)(2,1)S(1)}, u32[]{:S(2)}, u32[]{:S(2)}) collective-permute-start(bf16[32,1152]{1,0:T(8,128)(2,1)S(1)} %get-tuple-element.31.refs_0_), channel_id=1, source_target_pairs={{0,24},{1,25},{2,26},{3,27},{4,28},{5,29},{6,30},{7,31},{8,16},{9,... | collective-permute-start | bytes 221192 | tf_op jit(solution)/shard_map/ppermute | solution.py:315
  7.0 0.6 collective-permute-start
  7.6 2.1 %collective-permute-done.2.refs_3_ = bf16[32,1152]{1,0:T(8,128)(2,1)S(1)} collective-permute-done((bf16[32,1152]{1,0:T(8,128)(2,1)S(1)}, bf16[32,1152]{1,0:T(8,128)(2,1)S(1)}, u32[]{:S(2)}, u32[]{:S(2)}) %collective-permute-start.2) | collective-permute-done | bytes 73760 | tf_op jit(solution)/shard_map/ppermute | solution.py:315
  9.7 3.5 %collective-permute-done.1.refs_2_ = bf16[32,1152]{1,0:T(8,128)(2,1)S(1)} collective-permute-done((bf16[32,1152]{1,0:T(8,128)(2,1)S(1)}, bf16[32,1152]{1,0:T(8,128)(2,1)S(1)}, u32[]{:S(2)}, u32[]{:S(2)}) %collective-permute-start.1) | collective-permute-done | bytes 73760 | tf_op jit(solution)/shard_map/ppermute | solution.py:315
  13.2 1.6 %collective-permute-start.3 = (bf16[128,1152]{1,0:T(8,128)(2,1)S(1)}, bf16[128,1152]{1,0:T(8,128)(2,1)S(1)}, u32[]{:S(2)}, u32[]{:S(2)}) collective-permute-start(bf16[128,1152]{1,0:T(8,128)(2,1)S(1)} %get-tuple-element.32.line), channel_id=1, source_target_pairs={{0,4},{1,5},{2,6},{3,7},{4,0},{5,1},{6,2},{7,3},{8,12},{9,13},{10,... | collective-permute-start | bytes 884744 | tf_op jit(solution)/shard_map/ppermute | solution.py:315
  14.8 1.4 %collective-permute-start.7 = (bf16[128,1024]{1,0:T(8,128)(2,1)S(1)}, bf16[128,1024]{1,0:T(8,128)(2,1)S(1)}, u32[]{:S(2)}, u32[]{:S(2)}) collective-permute-start(bf16[128,1024]{1,0:T(8,128)(2,1)S(1)} %get-tuple-element.35), channel_id=1, source_target_pairs={{0,6},{1,7},{2,4},{3,5},{4,2},{5,3},{6,0},{7,1},{8,14},{9,15},{10,... | collective-permute-start | bytes 786440 | tf_op jit(solution)/shard_map/ppermute | solution.py:315
  16.8 2.2 %shard_map.87 = (bf16[4096,512]{1,0:T(8,128)(2,1)S(1)}, bf16[128,1152]{1,0:T(8,128)(2,1)S(1)}) custom-call(bf16[128,1152]{1,0:T(8,128)(2,1)S(1)} %get-tuple-element.32.line, bf16[4096,512]{1,0:T(8,128)(2,1)} %weight.1), custom_call_target="tpu_custom_call" | custom-call | bytes 8978432 | tf_op jit(solution)/shard_map/pallas_call | solution.py:32
  19.1 8.2 %collective-permute-done.3.refs_1_ = bf16[128,1152]{1,0:T(8,128)(2,1)S(1)} collective-permute-done((bf16[128,1152]{1,0:T(8,128)(2,1)S(1)}, bf16[128,1152]{1,0:T(8,128)(2,1)S(1)}, u32[]{:S(2)}, u32[]{:S(2)}) %collective-permute-start.3) | collective-permute-done | bytes 294944 | tf_op jit(solution)/shard_map/ppermute | solution.py:315
  28.3 0.9 %collective-permute-done.9.refs_7_ = bf16[128,1024]{1,0:T(8,128)(2,1)S(1)} collective-permute-done((bf16[128,1024]{1,0:T(8,128)(2,1)S(1)}, bf16[128,1024]{1,0:T(8,128)(2,1)S(1)}, u32[]{:S(2)}, u32[]{:S(2)}) %collective-permute-start.9) | collective-permute-done | bytes 262176 | tf_op jit(solution)/shard_map/ppermute | solution.py:315
  29.6 1.7 %shard_map.89 = (f32[256,512]{1,0:T(8,128)S(1)}, f32[8,256]{1,0:T(8,128)S(1)}) custom-call(f32[256,128]{1,0:T(8,128)S(1)} %shard_map.88.info, bf16[4096,512]{1,0:T(8,128)(2,1)S(1)} %get-tuple-element.34.weight, bf16[128,1152]{1,0:T(8,128)(2,1)S(1)} %get-tuple-element.33.refs_0_, bf16[128,1152]{1,0:T(8,128)(2,1)S(1)} %collective-permute-done.3.refs_1_, ...), custom_call_target="tpu_custom_call" | custom-call | flops 1073741824 | bytes 7086080 | tf_op jit(solution)/shard_map/pallas_call | solution.py:32
  31.4 1.0 %collective-permute-done.10.refs_1_ = f32[8,256]{1,0:T(8,128)S(1)} collective-permute-done((f32[8,256]{1,0:T(8,128)S(1)}, f32[8,256]{1,0:T(8,128)S(1)}, u32[]{:S(2)}, u32[]{:S(2)}) %collective-permute-start.10) | collective-permute-done | bytes 8224 | tf_op jit(solution)/shard_map/ppermute | solution.py:315
  32.5 0.7 collective-permute-start.11
  33.2 0.7 collective-permute-start.12
  33.9 0.7 collective-permute-start.15
  34.6 0.7 collective-permute-start.14
  35.2 0.7 collective-permute-start.13
  36.0 15.9 %collective-permute-start.16 = (f32[8,256]{1,0:T(8,128)S(1)}, f32[8,256]{1,0:T(8,128)S(1)}, u32[]{:S(2)}, u32[]{:S(2)}) collective-permute-start(f32[8,256]{1,0:T(8,128)S(1)} %shard_map.93.mine), channel_id=1, source_target_pairs={{0,1},{1,0},{2,3},{3,2},{4,5},{5,4},{6,7},{7,6},{8,9},{9,8},{10,11... | collective-permute-start | bytes 24584 | tf_op jit(solution)/shard_map/ppermute | solution.py:315
  51.9 0.8 %collective-permute-done.16.handed = f32[8,256]{1,0:T(8,128)S(1)} collective-permute-done((f32[8,256]{1,0:T(8,128)S(1)}, f32[8,256]{1,0:T(8,128)S(1)}, u32[]{:S(2)}, u32[]{:S(2)}) %collective-permute-start.16) | collective-permute-done | bytes 8224 | tf_op jit(solution)/shard_map/ppermute | solution.py:315
  52.7 1.1 %shard_map.94 = (bf16[4,64,1024]{2,1,0:T(8,128)(2,1)S(1)}, bf16[4,64,1024]{2,1,0:T(8,128)(2,1)S(1)}, bf16[256,512]{1,0:T(8,128)(2,1)S(1)}, f32[1,1]{1,0:T(1,128)}) custom-call(f32[256,128]{1,0:T(8,128)S(1)} %shard_map.88.info, f32[256,512]{1,0:T(8,128)S(1)} %get-tuple-element.36.logits, bf16[4096,512]{1,0:T(8,128)(2,1)S(1)} %get-tuple-element.34.weight, ...), custom_call_target="tpu_custom_call" | custom-call | flops 536870912 | bytes 6176772 | tf_op jit(solution)/shard_map/pallas_call | solution.py:32
  54.4 0.8 shard_map.95
  55.9 2.7 %collective-permute-start.23 = (bf16[64,1024]{1,0:T(8,128)(2,1)S(1)}, bf16[64,1024]{1,0:T(8,128)(2,1)S(1)}, u32[]{:S(2)}, u32[]{:S(2)}) collective-permute-start(bf16[64,1024]{1,0:T(8,128)(2,1)S(1)} %get-tuple-element.53), channel_id=1, source_target_pairs={{0,6},{1,7},{2,4},{3,5},{4,2},{5,3},{6,0},{7,1},{8,14},{9,15},{10,... | collective-permute-start | bytes 393224 | tf_op jit(solution)/shard_map/ppermute | solution.py:315
  59.6 2.7 %collective-permute-start.18 = (bf16[64,1024]{1,0:T(8,128)(2,1)S(1)}, bf16[64,1024]{1,0:T(8,128)(2,1)S(1)}, u32[]{:S(2)}, u32[]{:S(2)}) collective-permute-start(bf16[64,1024]{1,0:T(8,128)(2,1)S(1)} %get-tuple-element.45), channel_id=1, source_target_pairs={{0,6},{1,7},{2,4},{3,5},{4,2},{5,3},{6,0},{7,1},{8,14},{9,15},{10,... | collective-permute-start | bytes 393224 | tf_op jit(solution)/shard_map/ppermute | solution.py:315
  63.2 1.8 %collective-permute-start.20 = (bf16[64,1024]{1,0:T(8,128)(2,1)S(1)}, bf16[64,1024]{1,0:T(8,128)(2,1)S(1)}, u32[]{:S(2)}, u32[]{:S(2)}) collective-permute-start(bf16[64,1024]{1,0:T(8,128)(2,1)S(1)} %get-tuple-element.47), channel_id=1, source_target_pairs={{0,4},{1,5},{2,6},{3,7},{4,0},{5,1},{6,2},{7,3},{8,12},{9,13},{10,... | collective-permute-start | bytes 393224 | tf_op jit(solution)/shard_map/ppermute | solution.py:315
  64.9 2.5 %shard_map.97 = (bf16[4096,512]{1,0:T(8,128)(2,1)}, f32[8,128]{1,0:T(8,128)S(1)}) custom-call(f32[64,1024]{1,0:T(8,128)S(1)} %get-tuple-element.43.after.kept, bf16[256,512]{1,0:T(8,128)(2,1)S(1)} %get-tuple-element.40.logit_grad.after, bf16[128,1152]{1,0:T(8,128)(2,1)S(1)} %get-tuple-element.33.refs_0_, ...), custom_call_target="tpu_custom_call" | custom-call | flops 1073741824 | bytes 6950912 | tf_op jit(solution)/shard_map/pallas_call | solution.py:32
  67.5 0.8 %collective-permute-done.25.refs_2_ = bf16[64,1024]{1,0:T(8,128)(2,1)S(1)} collective-permute-done((bf16[64,1024]{1,0:T(8,128)(2,1)S(1)}, bf16[64,1024]{1,0:T(8,128)(2,1)S(1)}, u32[]{:S(2)}, u32[]{:S(2)}) %collective-permute-start.25) | collective-permute-done | bytes 131104 | tf_op jit(solution)/shard_map/ppermute | solution.py:315
  68.3 1.9 %collective-permute-start.26 = (bf16[32,1024]{1,0:T(8,128)(2,1)S(1)}, bf16[32,1024]{1,0:T(8,128)(2,1)S(1)}, u32[]{:S(2)}, u32[]{:S(2)}) collective-permute-start(bf16[32,1024]{1,0:T(8,128)(2,1)S(1)} %get-tuple-element.56), channel_id=1, source_target_pairs={{0,16},{1,17},{2,18},{3,19},{4,20},{5,21},{6,22},{7,23},{8,24},{9,... | collective-permute-start | bytes 196616 | tf_op jit(solution)/shard_map/ppermute | solution.py:315
  70.3 2.2 %collective-permute-start.27 = (bf16[32,1024]{1,0:T(8,128)(2,1)S(1)}, bf16[32,1024]{1,0:T(8,128)(2,1)S(1)}, u32[]{:S(2)}, u32[]{:S(2)}) collective-permute-start(bf16[32,1024]{1,0:T(8,128)(2,1)S(1)} %get-tuple-element.57), channel_id=1, source_target_pairs={{0,24},{1,25},{2,26},{3,27},{4,28},{5,29},{6,30},{7,31},{8,16},{9,... | collective-permute-start | bytes 196616 | tf_op jit(solution)/shard_map/ppermute | solution.py:315
  72.6 0.7 collective-permute-start.21
  73.7 2.9 %collective-permute-done.27.refs_3_ = bf16[32,1024]{1,0:T(8,128)(2,1)S(1)} collective-permute-done((bf16[32,1024]{1,0:T(8,128)(2,1)S(1)}, bf16[32,1024]{1,0:T(8,128)(2,1)S(1)}, u32[]{:S(2)}, u32[]{:S(2)}) %collective-permute-start.27) | collective-permute-done | bytes 65568 | tf_op jit(solution)/shard_map/ppermute | solution.py:315
  76.6 0.7 collective-permute-done.21.refs_1_
  77.2 1.0 %shard_map.101 = bf16[128,1024]{1,0:T(8,128)(2,1)} custom-call(bf16[32,128]{1,0:T(8,128)(2,1)S(1)} %get-tuple-element.39.chosen, f32[32,1024]{1,0:T(8,128)S(1)} %get-tuple-element.48.refs_0_, bf16[32,1024]{1,0:T(8,128)(2,1)S(1)} %collective-permute-done.21.refs_1_, bf16[32,1024]{1,0:T(8,128)(2,1)S(1)} %collective-permute-done.26.refs_2_, ...), custom_call_target="tpu_custom_call" | custom-call | bytes 598016 | tf_op jit(solution)/shard_map/pallas_call | solution.py:32
  (43 shorter events, 6.0 us)
Async XLA Ops:
  0.6 27.3 %copy-start = (f32[32]{0:T(128)S(1)}, f32[32]{0:T(128)}, u32[]{:S(2)}) copy-start(f32[32]{0:T(128)} %param.11) | copy-start | bytes 388
  1.9 7.9 %collective-permute-start.2 = (bf16[32,1152]{1,0:T(8,128)(2,1)S(1)}, bf16[32,1152]{1,0:T(8,128)(2,1)S(1)}, u32[]{:S(2)}, u32[]{:S(2)}) collective-permute-start(bf16[32,1152]{1,0:T(8,128)(2,1)S(1)} %get-tuple-element.31.refs_0_), channel_id=1, source_target_pairs={{0,24},{1,25},{2,26},{3,27},{4,28},{5,29},{6,30},{7,31},{8,16},{9,... | collective-permute-start | bytes 221192 | tf_op jit(solution)/shard_map/ppermute | solution.py:315
  7.0 6.2 %collective-permute-start.1 = (bf16[32,1152]{1,0:T(8,128)(2,1)S(1)}, bf16[32,1152]{1,0:T(8,128)(2,1)S(1)}, u32[]{:S(2)}, u32[]{:S(2)}) collective-permute-start(bf16[32,1152]{1,0:T(8,128)(2,1)S(1)} %get-tuple-element.31.refs_0_), channel_id=1, source_target_pairs={{0,16},{1,17},{2,18},{3,19},{4,20},{5,21},{6,22},{7,23},{8,24},{9,... | collective-permute-start | bytes 221192 | tf_op jit(solution)/shard_map/ppermute | solution.py:315
  7.0 6.2 %collective-permute-start = (bf16[32,1152]{1,0:T(8,128)(2,1)S(1)}, bf16[32,1152]{1,0:T(8,128)(2,1)S(1)}, u32[]{:S(2)}, u32[]{:S(2)}) collective-permute-start(bf16[32,1152]{1,0:T(8,128)(2,1)S(1)} %get-tuple-element.31.refs_0_), channel_id=1, source_target_pairs={{0,8},{1,9},{2,10},{3,11},{4,12},{5,13},{6,14},{7,15},{8,0},{9,1},... | collective-permute-start | bytes 221192 | tf_op jit(solution)/shard_map/ppermute | solution.py:315
  13.2 14.0 %collective-permute-start.3 = (bf16[128,1152]{1,0:T(8,128)(2,1)S(1)}, bf16[128,1152]{1,0:T(8,128)(2,1)S(1)}, u32[]{:S(2)}, u32[]{:S(2)}) collective-permute-start(bf16[128,1152]{1,0:T(8,128)(2,1)S(1)} %get-tuple-element.32.line), channel_id=1, source_target_pairs={{0,4},{1,5},{2,6},{3,7},{4,0},{5,1},{6,2},{7,3},{8,12},{9,13},{10,... | collective-permute-start | bytes 884744 | tf_op jit(solution)/shard_map/ppermute | solution.py:315
  14.8 12.5 %collective-permute-start.7 = (bf16[128,1024]{1,0:T(8,128)(2,1)S(1)}, bf16[128,1024]{1,0:T(8,128)(2,1)S(1)}, u32[]{:S(2)}, u32[]{:S(2)}) collective-permute-start(bf16[128,1024]{1,0:T(8,128)(2,1)S(1)} %get-tuple-element.35), channel_id=1, source_target_pairs={{0,6},{1,7},{2,4},{3,5},{4,2},{5,3},{6,0},{7,1},{8,14},{9,15},{10,... | collective-permute-start | bytes 786440 | tf_op jit(solution)/shard_map/ppermute | solution.py:315
  16.3 11.6 %collective-permute-start.6 = (bf16[128,1024]{1,0:T(8,128)(2,1)S(1)}, bf16[128,1024]{1,0:T(8,128)(2,1)S(1)}, u32[]{:S(2)}, u32[]{:S(2)}) collective-permute-start(bf16[128,1024]{1,0:T(8,128)(2,1)S(1)} %get-tuple-element.35), channel_id=1, source_target_pairs={{0,2},{1,3},{2,0},{3,1},{4,6},{5,7},{6,4},{7,5},{8,10},{9,11},{10,... | collective-permute-start | bytes 786440 | tf_op jit(solution)/shard_map/ppermute | solution.py:315
  19.0 9.3 %collective-permute-start.4 = (bf16[128,1152]{1,0:T(8,128)(2,1)S(1)}, bf16[128,1152]{1,0:T(8,128)(2,1)S(1)}, u32[]{:S(2)}, u32[]{:S(2)}) collective-permute-start(bf16[128,1152]{1,0:T(8,128)(2,1)S(1)} %get-tuple-element.33.refs_0_), channel_id=1, source_target_pairs={{0,1},{1,0},{2,3},{3,2},{4,5},{5,4},{6,7},{7,6},{8,9},{9,8},{10,11... | collective-permute-start | bytes 884744 | tf_op jit(solution)/shard_map/ppermute | solution.py:315
  27.3 2.3 %collective-permute-start.5 = (bf16[128,1152]{1,0:T(8,128)(2,1)S(1)}, bf16[128,1152]{1,0:T(8,128)(2,1)S(1)}, u32[]{:S(2)}, u32[]{:S(2)}) collective-permute-start(bf16[128,1152]{1,0:T(8,128)(2,1)S(1)} %collective-permute-done.3.refs_1_), channel_id=1, source_target_pairs={{0,1},{1,0},{2,3},{3,2},{4,5},{5,4},{6,7},{7,6},{8,9},{9,8},{10,11... | collective-permute-start | bytes 884744 | tf_op jit(solution)/shard_map/ppermute | solution.py:315
  27.3 2.0 %collective-permute-start.9 = (bf16[128,1024]{1,0:T(8,128)(2,1)S(1)}, bf16[128,1024]{1,0:T(8,128)(2,1)S(1)}, u32[]{:S(2)}, u32[]{:S(2)}) collective-permute-start(bf16[128,1024]{1,0:T(8,128)(2,1)S(1)} %collective-permute-done.7.refs_5_), channel_id=1, source_target_pairs={{0,1},{1,0},{2,3},{3,2},{4,5},{5,4},{6,7},{7,6},{8,9},{9,8},{10,11... | collective-permute-start | bytes 786440 | tf_op jit(solution)/shard_map/ppermute | solution.py:315
  27.9 1.7 %collective-permute-start.8 = (bf16[128,1024]{1,0:T(8,128)(2,1)S(1)}, bf16[128,1024]{1,0:T(8,128)(2,1)S(1)}, u32[]{:S(2)}, u32[]{:S(2)}) collective-permute-start(bf16[128,1024]{1,0:T(8,128)(2,1)S(1)} %collective-permute-done.6.refs_4_), channel_id=1, source_target_pairs={{0,1},{1,0},{2,3},{3,2},{4,5},{5,4},{6,7},{7,6},{8,9},{9,8},{10,11... | collective-permute-start | bytes 786440 | tf_op jit(solution)/shard_map/ppermute | solution.py:315
  31.3 1.2 %collective-permute-start.10 = (f32[8,256]{1,0:T(8,128)S(1)}, f32[8,256]{1,0:T(8,128)S(1)}, u32[]{:S(2)}, u32[]{:S(2)}) collective-permute-start(f32[8,256]{1,0:T(8,128)S(1)} %get-tuple-element.37.refs_0_), channel_id=1, source_target_pairs={{0,1},{1,0},{2,3},{3,2},{4,5},{5,4},{6,7},{7,6},{8,9},{9,8},{10,11... | collective-permute-start | bytes 24584 | tf_op jit(solution)/shard_map/ppermute | solution.py:315
  32.5 0.7 collective-permute-start.11
  33.2 0.7 collective-permute-start.12
  33.9 2.0 %collective-permute-start.15 = (f32[8,256]{1,0:T(8,128)S(1)}, f32[8,256]{1,0:T(8,128)S(1)}, u32[]{:S(2)}, u32[]{:S(2)}) collective-permute-start(f32[8,256]{1,0:T(8,128)S(1)} %shard_map.92.refs_0_), channel_id=1, source_target_pairs={{0,0},{1,25},{2,2},{3,27},{4,4},{5,29},{6,6},{7,31},{8,8},{9,17},{... | collective-permute-start | bytes 24584 | tf_op jit(solution)/shard_map/ppermute | solution.py:315
  34.6 1.4 %collective-permute-start.14 = (f32[8,256]{1,0:T(8,128)S(1)}, f32[8,256]{1,0:T(8,128)S(1)}, u32[]{:S(2)}, u32[]{:S(2)}) collective-permute-start(f32[8,256]{1,0:T(8,128)S(1)} %shard_map.92.refs_0_), channel_id=1, source_target_pairs={{0,0},{1,17},{2,2},{3,19},{4,4},{5,21},{6,6},{7,23},{8,8},{9,25},{... | collective-permute-start | bytes 24584 | tf_op jit(solution)/shard_map/ppermute | solution.py:315
  35.2 0.7 collective-permute-start.13
  36.0 16.8 %collective-permute-start.16 = (f32[8,256]{1,0:T(8,128)S(1)}, f32[8,256]{1,0:T(8,128)S(1)}, u32[]{:S(2)}, u32[]{:S(2)}) collective-permute-start(f32[8,256]{1,0:T(8,128)S(1)} %shard_map.93.mine), channel_id=1, source_target_pairs={{0,1},{1,0},{2,3},{3,2},{4,5},{5,4},{6,7},{7,6},{8,9},{9,8},{10,11... | collective-permute-start | bytes 24584 | tf_op jit(solution)/shard_map/ppermute | solution.py:315
  53.8 2.0 %collective-permute-start.22 = (bf16[4,64,1024]{2,1,0:T(8,128)(2,1)S(1)}, bf16[4,64,1024]{2,1,0:T(8,128)(2,1)S(1)}, u32[]{:S(2)}, u32[]{:S(2)}) collective-permute-start(bf16[4,64,1024]{2,1,0:T(8,128)(2,1)S(1)} %get-tuple-element.51), channel_id=1, source_target_pairs={{0,1},{1,0},{2,3},{3,2},{4,5},{5,4},{6,7},{7,6},{8,9},{9,8},{10,11... | collective-permute-start | bytes 1572872 | tf_op jit(solution)/shard_map/ppermute | solution.py:315
  54.2 5.2 %collective-permute-start.17 = (bf16[4,64,1024]{2,1,0:T(8,128)(2,1)S(1)}, bf16[4,64,1024]{2,1,0:T(8,128)(2,1)S(1)}, u32[]{:S(2)}, u32[]{:S(2)}) collective-permute-start(bf16[4,64,1024]{2,1,0:T(8,128)(2,1)S(1)} %get-tuple-element.42), channel_id=1, source_target_pairs={{0,1},{1,0},{2,3},{3,2},{4,5},{5,4},{6,7},{7,6},{8,9},{9,8},{10,11... | collective-permute-start | bytes 1572872 | tf_op jit(solution)/shard_map/ppermute | solution.py:315
  55.9 7.3 %collective-permute-start.23 = (bf16[64,1024]{1,0:T(8,128)(2,1)S(1)}, bf16[64,1024]{1,0:T(8,128)(2,1)S(1)}, u32[]{:S(2)}, u32[]{:S(2)}) collective-permute-start(bf16[64,1024]{1,0:T(8,128)(2,1)S(1)} %get-tuple-element.53), channel_id=1, source_target_pairs={{0,6},{1,7},{2,4},{3,5},{4,2},{5,3},{6,0},{7,1},{8,14},{9,15},{10,... | collective-permute-start | bytes 393224 | tf_op jit(solution)/shard_map/ppermute | solution.py:315
  58.6 8.9 %collective-permute-start.24 = (bf16[64,1024]{1,0:T(8,128)(2,1)S(1)}, bf16[64,1024]{1,0:T(8,128)(2,1)S(1)}, u32[]{:S(2)}, u32[]{:S(2)}) collective-permute-start(bf16[64,1024]{1,0:T(8,128)(2,1)S(1)} %get-tuple-element.54), channel_id=1, source_target_pairs={{0,2},{1,3},{2,0},{3,1},{4,6},{5,7},{6,4},{7,5},{8,10},{9,11},{10,... | collective-permute-start | bytes 393224 | tf_op jit(solution)/shard_map/ppermute | solution.py:315
  59.1 9.1 %collective-permute-start.25 = (bf16[64,1024]{1,0:T(8,128)(2,1)S(1)}, bf16[64,1024]{1,0:T(8,128)(2,1)S(1)}, u32[]{:S(2)}, u32[]{:S(2)}) collective-permute-start(bf16[64,1024]{1,0:T(8,128)(2,1)S(1)} %get-tuple-element.55), channel_id=1, source_target_pairs={{0,4},{1,5},{2,6},{3,7},{4,0},{5,1},{6,2},{7,3},{8,12},{9,13},{10,... | collective-permute-start | bytes 393224 | tf_op jit(solution)/shard_map/ppermute | solution.py:315
  59.6 12.9 %collective-permute-start.18 = (bf16[64,1024]{1,0:T(8,128)(2,1)S(1)}, bf16[64,1024]{1,0:T(8,128)(2,1)S(1)}, u32[]{:S(2)}, u32[]{:S(2)}) collective-permute-start(bf16[64,1024]{1,0:T(8,128)(2,1)S(1)} %get-tuple-element.45), channel_id=1, source_target_pairs={{0,6},{1,7},{2,4},{3,5},{4,2},{5,3},{6,0},{7,1},{8,14},{9,15},{10,... | collective-permute-start | bytes 393224 | tf_op jit(solution)/shard_map/ppermute | solution.py:315
  62.3 10.2 %collective-permute-start.19 = (bf16[64,1024]{1,0:T(8,128)(2,1)S(1)}, bf16[64,1024]{1,0:T(8,128)(2,1)S(1)}, u32[]{:S(2)}, u32[]{:S(2)}) collective-permute-start(bf16[64,1024]{1,0:T(8,128)(2,1)S(1)} %get-tuple-element.46), channel_id=1, source_target_pairs={{0,2},{1,3},{2,0},{3,1},{4,6},{5,7},{6,4},{7,5},{8,10},{9,11},{10,... | collective-permute-start | bytes 393224 | tf_op jit(solution)/shard_map/ppermute | solution.py:315
  63.2 9.3 %collective-permute-start.20 = (bf16[64,1024]{1,0:T(8,128)(2,1)S(1)}, bf16[64,1024]{1,0:T(8,128)(2,1)S(1)}, u32[]{:S(2)}, u32[]{:S(2)}) collective-permute-start(bf16[64,1024]{1,0:T(8,128)(2,1)S(1)} %get-tuple-element.47), channel_id=1, source_target_pairs={{0,4},{1,5},{2,6},{3,7},{4,0},{5,1},{6,2},{7,3},{8,12},{9,13},{10,... | collective-permute-start | bytes 393224 | tf_op jit(solution)/shard_map/ppermute | solution.py:315
  68.3 5.3 %collective-permute-start.26 = (bf16[32,1024]{1,0:T(8,128)(2,1)S(1)}, bf16[32,1024]{1,0:T(8,128)(2,1)S(1)}, u32[]{:S(2)}, u32[]{:S(2)}) collective-permute-start(bf16[32,1024]{1,0:T(8,128)(2,1)S(1)} %get-tuple-element.56), channel_id=1, source_target_pairs={{0,16},{1,17},{2,18},{3,19},{4,20},{5,21},{6,22},{7,23},{8,24},{9,... | collective-permute-start | bytes 196616 | tf_op jit(solution)/shard_map/ppermute | solution.py:315
  70.3 6.3 %collective-permute-start.27 = (bf16[32,1024]{1,0:T(8,128)(2,1)S(1)}, bf16[32,1024]{1,0:T(8,128)(2,1)S(1)}, u32[]{:S(2)}, u32[]{:S(2)}) collective-permute-start(bf16[32,1024]{1,0:T(8,128)(2,1)S(1)} %get-tuple-element.57), channel_id=1, source_target_pairs={{0,24},{1,25},{2,26},{3,27},{4,28},{5,29},{6,30},{7,31},{8,16},{9,... | collective-permute-start | bytes 196616 | tf_op jit(solution)/shard_map/ppermute | solution.py:315
  72.6 4.7 %collective-permute-start.21 = (bf16[32,1024]{1,0:T(8,128)(2,1)S(1)}, bf16[32,1024]{1,0:T(8,128)(2,1)S(1)}, u32[]{:S(2)}, u32[]{:S(2)}) collective-permute-start(bf16[32,1024]{1,0:T(8,128)(2,1)S(1)} %get-tuple-element.49), channel_id=1, source_target_pairs={{0,8},{1,9},{2,10},{3,11},{4,12},{5,13},{6,14},{7,15},{8,0},{9,1},... | collective-permute-start | bytes 196616 | tf_op jit(solution)/shard_map/ppermute | solution.py:315

commit v8 on v7

--- a/solution.py
+++ b/solution.py
@@ -198,11 +198,10 @@
     return peak, mass, hit
 
 
-def merge_kernel(*refs):
-    out = refs[-1]
-    peak, mass, hit = merge([ref[...] for ref in refs[:-1]])
-    row = lax.broadcasted_iota(jnp.int32, out.shape, 0)
-    out[...] = jnp.where(row == 0, peak, jnp.where(row == 1, mass, hit))
+def merge_kernel(mine, theirs, out):
+    peak, mass, hit = merge([mine[...], theirs[...]])
+    line = jnp.concatenate([peak, mass, hit[:, :128]], axis=1)
+    out[...] = jnp.broadcast_to(line[None], out.shape)
 
 
 def block_grads(blocks, rank, first, grad, weight, outs):
@@ -222,12 +221,14 @@
             out[block // 2 * 2 + side] = piece.astype(out.dtype)
 
 
-def grad_kernel(blocks, groups, info, logits, weight, mine, handed, *refs):
+def grad_kernel(blocks, groups, info, logits, weight, stats, *refs):
     away, (logit_grad, loss) = refs[:2], refs[2:]
     rank, position, shard = coordinates()
     height, columns = logits.shape
-    table = jnp.where(rank % 2 == 1, mine[...], handed[...])
-    peak, mass, hit = table[0:1], table[1:2], table[2:3]
+    peaks, masses = stats[:, :, :height], stats[:, :, height:2 * height]
+    peak = jnp.max(peaks, axis=0)
+    mass = jnp.sum(masses * jnp.exp(peaks - peak[None]), axis=0)
+    hit = jnp.sum(stats[:, :, 2 * height:], axis=0)
     log_total = jnp.broadcast_to(peak + jnp.log(mass), (8, height))
     log_total = reorder(log_total, position, groups)
     log_total = jnp.transpose(jnp.concatenate([log_total] * 16, axis=0))[:, 0:1]
@@ -270,8 +271,8 @@
         copy.wait()
 
 
-def pair_kernel(kept, beside, *outs):
-    for place, out in enumerate(reversed(outs)):
+def pair_kernel(order, kept, beside, *outs):
+    for place, out in zip(order, outs):
         total = kept[place] + beside[place].astype(jnp.float32)
         out[...] = total.astype(out.dtype)
 
@@ -305,10 +306,10 @@
     square = [(y, x) for x in reversed(range(xs)) for y in (1, 0) if x or y]
     flops = 2 * total_rows * depth * columns
 
-    def send(value, z=0, y=0, x=0, core=0, cores=(0, 1)):
+    def send(value, z=0, y=0, x=0, core=0):
         far, near = 2 * z + y, 2 * x + core
         pairs = [
-            (d * ranks + v, (d ^ far) * ranks + (v ^ near) if v % 2 in cores else d * ranks + v)
+            (d * ranks + v, (d ^ far) * ranks + (v ^ near))
             for d in range(dps)
             for v in range(ranks)
         ]
@@ -372,24 +373,24 @@
         flops=flops,
     )
 
-    def combine(*tables):
-        return call(
-            merge_kernel, tables, [VMEM] * len(tables), shape((8, total_rows), f32), VMEM
-        )
-
-    stats = combine(stats, send(stats, core=1))
-    for bit in range((xs - 1).bit_length()):
-        stats = combine(stats, send(stats, x=1 << bit, cores=(1,)))
-    stats = combine(stats, send(stats, y=1, cores=(1,)))
-    stats = combine(stats, *[send(stats, z=z, cores=(1,)) for z in range(1, zs)])
-    handed = send(stats, core=1)
+    stats = call(
+        merge_kernel,
+        (stats, send(stats, core=1)),
+        [VMEM] * 2,
+        shape((dps * xs, 1, 2 * total_rows + 128), f32),
+        VMEM,
+    )
+    chips = [
+        [d * ranks + v for d in range(dps) for v in range(core, ranks, 2)] for core in range(2)
+    ]
+    stats = lax.all_to_all(stats, AXES, 0, 0, axis_index_groups=chips)
 
     rows_part = total_rows // 4
     whole = (ranks, rows_part, width)
     *away, logit_grad, loss = call(
         functools.partial(grad_kernel, ranks, dps),
-        (info, logits, held, stats, handed),
-        [VMEM] * 5,
+        (info, logits, held, stats),
+        [VMEM] * 4,
         (shape(whole, bf16),) * 2 + (shape((total_rows, columns), bf16), shape((1, 1), f32)),
         (VMEM,) * 3 + (SMEM,),
         flops=flops // 2,
@@ -405,22 +406,22 @@
 
     ends = [None] * zs
     besides = [None, None]
+    order = sorted(range(1, ranks), key=lambda place: (place % 2 + (place > 1), place))
     for chunk in (1, 0):
         besides[chunk] = send(away[chunk], core=1)
     sums = [None, None]
     for chunk in (1, 0):
         part = shape((rows_part, width), bf16)
         *going, corner = call(
-            pair_kernel,
+            functools.partial(pair_kernel, order + [0]),
             (kept[chunk], besides[chunk]),
             [VMEM, VMEM],
             (part,) * (ranks - 1) + (shape((rows_part, width), f32),),
             (VMEM,) * ranks,
         )
         arrived = []
-        for place, value in enumerate(going):
-            x, y = divmod(ranks - 1 - place, 2)
-            arrived.append(send(value, y=y, x=x))
+        for place, value in zip(order, going):
+            arrived.append(send(value, y=place % 2, x=place // 2))
         sums[chunk] = (corner, *arrived)
     weight_grad, finished = call(
         functools.partial(weight_kernel, ranks),

time: 78.4 us -> 68.7 us (0.88)
  starting transfers between devices: 43.3 us -> 20.8 us
  blocking collectives: 0 us -> 12.3 us
    ppermute x28 -> x22, starting transfers between devices: 43.3 us -> 20.8 us  [send(): return lax.ppermute(value, AXES, pairs)]
    all_to_all x0 -> x1, blocking collectives: none -> 12.3 us  [body(): stats = lax.all_to_all(stats, AXES, 0, 0, axis_index_groups=chips)]
    ppermute x28 -> x22, waiting for transfers between devices: 22.8 us -> 23.5 us  [send(): return lax.ppermute(value, AXES, pairs)]
    pallas_call x17 -> x14, Pallas kernels: 11.3 us -> 11.2 us  [call(): pl.pallas_call(kernel, out_shape=out_shape, in_specs=in_specs, out_specs=...]
  transfers between devices with their start and end apart: 28 -> 22, of which waited for: 14 -> 14; matrix products, arithmetic and copies ran while one was open for 0% -> 0% of each run, Pallas kernels for 8% -> 9%
where the time goes in v8:
time: 68.7 us; the launch traced here: 68.6 us
  waiting for transfers between devices  23.5 us (34%)
  starting transfers between devices  20.8 us (30%)
  blocking collectives  12.3 us (18%)
  Pallas kernels  11.2 us (16%)
  between operations  0.76 us (1%)
    ppermute x22, waiting for transfers between devices, send(): return lax.ppermute(value, AXES, pairs)  23.5 us
    ppermute x22, starting transfers between devices, send(): return lax.ppermute(value, AXES, pairs)  20.8 us
    all_to_all x1, blocking collectives, body(): stats = lax.all_to_all(stats, AXES, 0, 0, axis_index_groups=chips)  12.3 us
    pallas_call x14, Pallas kernels, call(): pl.pallas_call(kernel, out_shape=out_shape, in_specs=in_specs, out_specs=...  11.2 us
  transfers between devices with their start and end apart: 22, of which 14 were waited for; matrix products, arithmetic and copies ran while one was open for 0% of the time, Pallas kernels for 9%

profile of v8, /device:TPU:0, one launch (start us, length us, event | category | flops | bytes accessed | tf_op | source)
XLA Modules:
  0.0 68.6 jit_solution(10313016689480692707)
XLA Ops:
  0.6 1.2 %shard_map.85 = (bf16[32,1152]{1,0:T(8,128)(2,1)S(1)}, bf16[32,128]{1,0:T(8,128)(2,1)S(1)}) custom-call(bf16[128,1024]{1,0:T(8,128)(2,1)} %hidden_hbm.1, s32[1,128]{1,0:T(1,128)} %bitcast.6, s32[1,128]{1,0:T(1,128)} %bitcast.7, s32[1,128]{1,0:T(1,128)} %bitcast.8), custom_call_target="tpu_custom_call" | custom-call | bytes 345600 | tf_op jit(solution)/shard_map/pallas_call | solution.py:32
  1.9 5.1 %collective-permute-start.2 = (bf16[32,1152]{1,0:T(8,128)(2,1)S(1)}, bf16[32,1152]{1,0:T(8,128)(2,1)S(1)}, u32[]{:S(2)}, u32[]{:S(2)}) collective-permute-start(bf16[32,1152]{1,0:T(8,128)(2,1)S(1)} %get-tuple-element.31.refs_0_), channel_id=1, source_target_pairs={{0,24},{1,25},{2,26},{3,27},{4,28},{5,29},{6,30},{7,31},{8,16},{9,... | collective-permute-start | bytes 221192 | tf_op jit(solution)/shard_map/ppermute | solution.py:316
  7.0 0.6 collective-permute-start
  7.6 2.1 %collective-permute-done.2.refs_3_ = bf16[32,1152]{1,0:T(8,128)(2,1)S(1)} collective-permute-done((bf16[32,1152]{1,0:T(8,128)(2,1)S(1)}, bf16[32,1152]{1,0:T(8,128)(2,1)S(1)}, u32[]{:S(2)}, u32[]{:S(2)}) %collective-permute-start.2) | collective-permute-done | bytes 73760 | tf_op jit(solution)/shard_map/ppermute | solution.py:316
  9.7 3.5 %collective-permute-done.1.refs_2_ = bf16[32,1152]{1,0:T(8,128)(2,1)S(1)} collective-permute-done((bf16[32,1152]{1,0:T(8,128)(2,1)S(1)}, bf16[32,1152]{1,0:T(8,128)(2,1)S(1)}, u32[]{:S(2)}, u32[]{:S(2)}) %collective-permute-start.1) | collective-permute-done | bytes 73760 | tf_op jit(solution)/shard_map/ppermute | solution.py:316
  13.2 1.6 %collective-permute-start.3 = (bf16[128,1152]{1,0:T(8,128)(2,1)S(1)}, bf16[128,1152]{1,0:T(8,128)(2,1)S(1)}, u32[]{:S(2)}, u32[]{:S(2)}) collective-permute-start(bf16[128,1152]{1,0:T(8,128)(2,1)S(1)} %get-tuple-element.32.line), channel_id=1, source_target_pairs={{0,4},{1,5},{2,6},{3,7},{4,0},{5,1},{6,2},{7,3},{8,12},{9,13},{10,... | collective-permute-start | bytes 884744 | tf_op jit(solution)/shard_map/ppermute | solution.py:316
  14.8 1.4 %collective-permute-start.7 = (bf16[128,1024]{1,0:T(8,128)(2,1)S(1)}, bf16[128,1024]{1,0:T(8,128)(2,1)S(1)}, u32[]{:S(2)}, u32[]{:S(2)}) collective-permute-start(bf16[128,1024]{1,0:T(8,128)(2,1)S(1)} %get-tuple-element.35), channel_id=1, source_target_pairs={{0,6},{1,7},{2,4},{3,5},{4,2},{5,3},{6,0},{7,1},{8,14},{9,15},{10,... | collective-permute-start | bytes 786440 | tf_op jit(solution)/shard_map/ppermute | solution.py:316
  16.8 2.2 %shard_map.87 = (bf16[4096,512]{1,0:T(8,128)(2,1)S(1)}, bf16[128,1152]{1,0:T(8,128)(2,1)S(1)}) custom-call(bf16[128,1152]{1,0:T(8,128)(2,1)S(1)} %get-tuple-element.32.line, bf16[4096,512]{1,0:T(8,128)(2,1)} %weight.1), custom_call_target="tpu_custom_call" | custom-call | bytes 8978432 | tf_op jit(solution)/shard_map/pallas_call | solution.py:32
  19.1 8.2 %collective-permute-done.3.refs_1_ = bf16[128,1152]{1,0:T(8,128)(2,1)S(1)} collective-permute-done((bf16[128,1152]{1,0:T(8,128)(2,1)S(1)}, bf16[128,1152]{1,0:T(8,128)(2,1)S(1)}, u32[]{:S(2)}, u32[]{:S(2)}) %collective-permute-start.3) | collective-permute-done | bytes 294944 | tf_op jit(solution)/shard_map/ppermute | solution.py:316
  28.3 0.9 %collective-permute-done.9.refs_7_ = bf16[128,1024]{1,0:T(8,128)(2,1)S(1)} collective-permute-done((bf16[128,1024]{1,0:T(8,128)(2,1)S(1)}, bf16[128,1024]{1,0:T(8,128)(2,1)S(1)}, u32[]{:S(2)}, u32[]{:S(2)}) %collective-permute-start.9) | collective-permute-done | bytes 262176 | tf_op jit(solution)/shard_map/ppermute | solution.py:316
  29.6 1.7 %shard_map.89 = (f32[256,512]{1,0:T(8,128)S(1)}, f32[8,256]{1,0:T(8,128)S(1)}) custom-call(f32[256,128]{1,0:T(8,128)S(1)} %shard_map.88.info, bf16[4096,512]{1,0:T(8,128)(2,1)S(1)} %get-tuple-element.34.weight, bf16[128,1152]{1,0:T(8,128)(2,1)S(1)} %get-tuple-element.33.refs_0_, bf16[128,1152]{1,0:T(8,128)(2,1)S(1)} %collective-permute-done.3.refs_1_, ...), custom_call_target="tpu_custom_call" | custom-call | flops 1073741824 | bytes 7086080 | tf_op jit(solution)/shard_map/pallas_call | solution.py:32
  31.4 1.0 %collective-permute-done.10.theirs = f32[8,256]{1,0:T(8,128)S(1)} collective-permute-done((f32[8,256]{1,0:T(8,128)S(1)}, f32[8,256]{1,0:T(8,128)S(1)}, u32[]{:S(2)}, u32[]{:S(2)}) %collective-permute-start.10) | collective-permute-done | bytes 8224 | tf_op jit(solution)/shard_map/ppermute | solution.py:316
  32.5 12.3 %all_to_all.5.stats = f32[16,1,640]{2,1,0:T(1,128)S(1)} all-to-all(f32[16,1,640]{2,1,0:T(1,128)S(1)} %shard_map.90), channel_id=1, replica_groups={{0,2,4,6,8,10,12,14,16,18,20,22,24,26,28,30},{1,3,5,7,9,11,13,15,17,19,..., dimensions={0} | all-to-all | bytes 81920 | tf_op jit(solution)/shard_map/all_to_all | solution.py:386
  44.8 1.1 %shard_map.91 = (bf16[4,64,1024]{2,1,0:T(8,128)(2,1)S(1)}, bf16[4,64,1024]{2,1,0:T(8,128)(2,1)S(1)}, bf16[256,512]{1,0:T(8,128)(2,1)S(1)}, f32[1,1]{1,0:T(1,128)}) custom-call(f32[256,128]{1,0:T(8,128)S(1)} %shard_map.88.info, f32[256,512]{1,0:T(8,128)S(1)} %get-tuple-element.36.logits, bf16[4096,512]{1,0:T(8,128)(2,1)S(1)} %get-tuple-element.34.weight, ...), custom_call_target="tpu_custom_call" | custom-call | flops 536870912 | bytes 6201348 | tf_op jit(solution)/shard_map/pallas_call | solution.py:32
  46.5 0.8 %shard_map.92 = (f32[4,64,1024]{2,1,0:T(8,128)S(1)}, f32[4,64,1024]{2,1,0:T(8,128)S(1)}) custom-call(bf16[256,512]{1,0:T(8,128)(2,1)S(1)} %get-tuple-element.40.logit_grad.after, bf16[4096,512]{1,0:T(8,128)(2,1)S(1)} %get-tuple-element.34.weight), custom_call_target="tpu_custom_call" | custom-call | flops 536870912 | bytes 6553600 | tf_op jit(solution)/shard_map/pallas_call | solution.py:32
  47.3 0.6 collective-permute-done.16.beside
  48.0 0.7 collective-permute-start.17
  49.2 2.3 %collective-permute-start.19 = (bf16[64,1024]{1,0:T(8,128)(2,1)S(1)}, bf16[64,1024]{1,0:T(8,128)(2,1)S(1)}, u32[]{:S(2)}, u32[]{:S(2)}) collective-permute-start(bf16[64,1024]{1,0:T(8,128)(2,1)S(1)} %get-tuple-element.55), channel_id=1, source_target_pairs={{0,6},{1,7},{2,4},{3,5},{4,2},{5,3},{6,0},{7,1},{8,14},{9,15},{10,... | collective-permute-start | bytes 393224 | tf_op jit(solution)/shard_map/ppermute | solution.py:316
  51.7 0.7 collective-permute-start.12
  52.4 0.6 collective-permute-start.13
  52.9 0.7 collective-permute-done.17.refs_0_
  53.6 1.6 %collective-permute-start.14 = (bf16[64,1024]{1,0:T(8,128)(2,1)S(1)}, bf16[64,1024]{1,0:T(8,128)(2,1)S(1)}, u32[]{:S(2)}, u32[]{:S(2)}) collective-permute-start(bf16[64,1024]{1,0:T(8,128)(2,1)S(1)} %get-tuple-element.47), channel_id=1, source_target_pairs={{0,6},{1,7},{2,4},{3,5},{4,2},{5,3},{6,0},{7,1},{8,14},{9,15},{10,... | collective-permute-start | bytes 393224 | tf_op jit(solution)/shard_map/ppermute | solution.py:316
  55.2 2.5 %shard_map.94 = (bf16[4096,512]{1,0:T(8,128)(2,1)}, f32[8,128]{1,0:T(8,128)S(1)}) custom-call(f32[64,1024]{1,0:T(8,128)S(1)} %get-tuple-element.43.after.kept, bf16[256,512]{1,0:T(8,128)(2,1)S(1)} %get-tuple-element.40.logit_grad.after, bf16[128,1152]{1,0:T(8,128)(2,1)S(1)} %get-tuple-element.33.refs_0_, ...), custom_call_target="tpu_custom_call" | custom-call | flops 1073741824 | bytes 6950912 | tf_op jit(solution)/shard_map/pallas_call | solution.py:32
  57.8 0.9 %collective-permute-done.19.refs_2_ = bf16[64,1024]{1,0:T(8,128)(2,1)S(1)} collective-permute-done((bf16[64,1024]{1,0:T(8,128)(2,1)S(1)}, bf16[64,1024]{1,0:T(8,128)(2,1)S(1)}, u32[]{:S(2)}, u32[]{:S(2)}) %collective-permute-start.19) | collective-permute-done | bytes 131104 | tf_op jit(solution)/shard_map/ppermute | solution.py:316
  58.8 0.7 %collective-permute-start.20 = (bf16[32,1024]{1,0:T(8,128)(2,1)S(1)}, bf16[32,1024]{1,0:T(8,128)(2,1)S(1)}, u32[]{:S(2)}, u32[]{:S(2)}) collective-permute-start(bf16[32,1024]{1,0:T(8,128)(2,1)S(1)} %get-tuple-element.56), channel_id=1, source_target_pairs={{0,16},{1,17},{2,18},{3,19},{4,20},{5,21},{6,22},{7,23},{8,24},{9,... | collective-permute-start | bytes 196616 | tf_op jit(solution)/shard_map/ppermute | solution.py:316
  59.5 2.3 %collective-permute-start.21 = (bf16[32,1024]{1,0:T(8,128)(2,1)S(1)}, bf16[32,1024]{1,0:T(8,128)(2,1)S(1)}, u32[]{:S(2)}, u32[]{:S(2)}) collective-permute-start(bf16[32,1024]{1,0:T(8,128)(2,1)S(1)} %get-tuple-element.57), channel_id=1, source_target_pairs={{0,24},{1,25},{2,26},{3,27},{4,28},{5,29},{6,30},{7,31},{8,16},{9,... | collective-permute-start | bytes 196616 | tf_op jit(solution)/shard_map/ppermute | solution.py:316
  61.8 1.4 %collective-permute-done.14.refs_2_ = bf16[64,1024]{1,0:T(8,128)(2,1)S(1)} collective-permute-done((bf16[64,1024]{1,0:T(8,128)(2,1)S(1)}, bf16[64,1024]{1,0:T(8,128)(2,1)S(1)}, u32[]{:S(2)}, u32[]{:S(2)}) %collective-permute-start.14) | collective-permute-done | bytes 131104 | tf_op jit(solution)/shard_map/ppermute | solution.py:316
  63.3 0.7 collective-permute-start.15
  64.0 0.8 %collective-permute-done.20.refs_2_ = bf16[32,1024]{1,0:T(8,128)(2,1)S(1)} collective-permute-done((bf16[32,1024]{1,0:T(8,128)(2,1)S(1)}, bf16[32,1024]{1,0:T(8,128)(2,1)S(1)}, u32[]{:S(2)}, u32[]{:S(2)}) %collective-permute-start.20) | collective-permute-done | bytes 65568 | tf_op jit(solution)/shard_map/ppermute | solution.py:316
  64.7 1.4 %collective-permute-done.21.refs_3_ = bf16[32,1024]{1,0:T(8,128)(2,1)S(1)} collective-permute-done((bf16[32,1024]{1,0:T(8,128)(2,1)S(1)}, bf16[32,1024]{1,0:T(8,128)(2,1)S(1)}, u32[]{:S(2)}, u32[]{:S(2)}) %collective-permute-start.21) | collective-permute-done | bytes 65568 | tf_op jit(solution)/shard_map/ppermute | solution.py:316
  66.2 1.4 %collective-permute-done.15.refs_1_ = bf16[32,1024]{1,0:T(8,128)(2,1)S(1)} collective-permute-done((bf16[32,1024]{1,0:T(8,128)(2,1)S(1)}, bf16[32,1024]{1,0:T(8,128)(2,1)S(1)}, u32[]{:S(2)}, u32[]{:S(2)}) %collective-permute-start.15) | collective-permute-done | bytes 65568 | tf_op jit(solution)/shard_map/ppermute | solution.py:316
  67.6 1.0 %shard_map.98 = bf16[128,1024]{1,0:T(8,128)(2,1)} custom-call(bf16[32,128]{1,0:T(8,128)(2,1)S(1)} %get-tuple-element.39.chosen, f32[32,1024]{1,0:T(8,128)S(1)} %get-tuple-element.48.refs_0_, bf16[32,1024]{1,0:T(8,128)(2,1)S(1)} %collective-permute-done.15.refs_1_, bf16[32,1024]{1,0:T(8,128)(2,1)S(1)} %collective-permute-done.20.refs_2_, ...), custom_call_target="tpu_custom_call" | custom-call | bytes 598016 | tf_op jit(solution)/shard_map/pallas_call | solution.py:32
  (29 shorter events, 3.7 us)
Async XLA Ops:
  0.6 27.3 %copy-start = (f32[32]{0:T(128)S(1)}, f32[32]{0:T(128)}, u32[]{:S(2)}) copy-start(f32[32]{0:T(128)} %param.11) | copy-start | bytes 388
  1.9 7.9 %collective-permute-start.2 = (bf16[32,1152]{1,0:T(8,128)(2,1)S(1)}, bf16[32,1152]{1,0:T(8,128)(2,1)S(1)}, u32[]{:S(2)}, u32[]{:S(2)}) collective-permute-start(bf16[32,1152]{1,0:T(8,128)(2,1)S(1)} %get-tuple-element.31.refs_0_), channel_id=1, source_target_pairs={{0,24},{1,25},{2,26},{3,27},{4,28},{5,29},{6,30},{7,31},{8,16},{9,... | collective-permute-start | bytes 221192 | tf_op jit(solution)/shard_map/ppermute | solution.py:316
  7.0 6.2 %collective-permute-start.1 = (bf16[32,1152]{1,0:T(8,128)(2,1)S(1)}, bf16[32,1152]{1,0:T(8,128)(2,1)S(1)}, u32[]{:S(2)}, u32[]{:S(2)}) collective-permute-start(bf16[32,1152]{1,0:T(8,128)(2,1)S(1)} %get-tuple-element.31.refs_0_), channel_id=1, source_target_pairs={{0,16},{1,17},{2,18},{3,19},{4,20},{5,21},{6,22},{7,23},{8,24},{9,... | collective-permute-start | bytes 221192 | tf_op jit(solution)/shard_map/ppermute | solution.py:316
  7.0 6.2 %collective-permute-start = (bf16[32,1152]{1,0:T(8,128)(2,1)S(1)}, bf16[32,1152]{1,0:T(8,128)(2,1)S(1)}, u32[]{:S(2)}, u32[]{:S(2)}) collective-permute-start(bf16[32,1152]{1,0:T(8,128)(2,1)S(1)} %get-tuple-element.31.refs_0_), channel_id=1, source_target_pairs={{0,8},{1,9},{2,10},{3,11},{4,12},{5,13},{6,14},{7,15},{8,0},{9,1},... | collective-permute-start | bytes 221192 | tf_op jit(solution)/shard_map/ppermute | solution.py:316
  13.2 14.0 %collective-permute-start.3 = (bf16[128,1152]{1,0:T(8,128)(2,1)S(1)}, bf16[128,1152]{1,0:T(8,128)(2,1)S(1)}, u32[]{:S(2)}, u32[]{:S(2)}) collective-permute-start(bf16[128,1152]{1,0:T(8,128)(2,1)S(1)} %get-tuple-element.32.line), channel_id=1, source_target_pairs={{0,4},{1,5},{2,6},{3,7},{4,0},{5,1},{6,2},{7,3},{8,12},{9,13},{10,... | collective-permute-start | bytes 884744 | tf_op jit(solution)/shard_map/ppermute | solution.py:316
  14.8 12.5 %collective-permute-start.7 = (bf16[128,1024]{1,0:T(8,128)(2,1)S(1)}, bf16[128,1024]{1,0:T(8,128)(2,1)S(1)}, u32[]{:S(2)}, u32[]{:S(2)}) collective-permute-start(bf16[128,1024]{1,0:T(8,128)(2,1)S(1)} %get-tuple-element.35), channel_id=1, source_target_pairs={{0,6},{1,7},{2,4},{3,5},{4,2},{5,3},{6,0},{7,1},{8,14},{9,15},{10,... | collective-permute-start | bytes 786440 | tf_op jit(solution)/shard_map/ppermute | solution.py:316
  16.3 11.6 %collective-permute-start.6 = (bf16[128,1024]{1,0:T(8,128)(2,1)S(1)}, bf16[128,1024]{1,0:T(8,128)(2,1)S(1)}, u32[]{:S(2)}, u32[]{:S(2)}) collective-permute-start(bf16[128,1024]{1,0:T(8,128)(2,1)S(1)} %get-tuple-element.35), channel_id=1, source_target_pairs={{0,2},{1,3},{2,0},{3,1},{4,6},{5,7},{6,4},{7,5},{8,10},{9,11},{10,... | collective-permute-start | bytes 786440 | tf_op jit(solution)/shard_map/ppermute | solution.py:316
  19.0 9.3 %collective-permute-start.4 = (bf16[128,1152]{1,0:T(8,128)(2,1)S(1)}, bf16[128,1152]{1,0:T(8,128)(2,1)S(1)}, u32[]{:S(2)}, u32[]{:S(2)}) collective-permute-start(bf16[128,1152]{1,0:T(8,128)(2,1)S(1)} %get-tuple-element.33.refs_0_), channel_id=1, source_target_pairs={{0,1},{1,0},{2,3},{3,2},{4,5},{5,4},{6,7},{7,6},{8,9},{9,8},{10,11... | collective-permute-start | bytes 884744 | tf_op jit(solution)/shard_map/ppermute | solution.py:316
  27.3 2.3 %collective-permute-start.5 = (bf16[128,1152]{1,0:T(8,128)(2,1)S(1)}, bf16[128,1152]{1,0:T(8,128)(2,1)S(1)}, u32[]{:S(2)}, u32[]{:S(2)}) collective-permute-start(bf16[128,1152]{1,0:T(8,128)(2,1)S(1)} %collective-permute-done.3.refs_1_), channel_id=1, source_target_pairs={{0,1},{1,0},{2,3},{3,2},{4,5},{5,4},{6,7},{7,6},{8,9},{9,8},{10,11... | collective-permute-start | bytes 884744 | tf_op jit(solution)/shard_map/ppermute | solution.py:316
  27.3 2.0 %collective-permute-start.9 = (bf16[128,1024]{1,0:T(8,128)(2,1)S(1)}, bf16[128,1024]{1,0:T(8,128)(2,1)S(1)}, u32[]{:S(2)}, u32[]{:S(2)}) collective-permute-start(bf16[128,1024]{1,0:T(8,128)(2,1)S(1)} %collective-permute-done.7.refs_5_), channel_id=1, source_target_pairs={{0,1},{1,0},{2,3},{3,2},{4,5},{5,4},{6,7},{7,6},{8,9},{9,8},{10,11... | collective-permute-start | bytes 786440 | tf_op jit(solution)/shard_map/ppermute | solution.py:316
  27.9 1.7 %collective-permute-start.8 = (bf16[128,1024]{1,0:T(8,128)(2,1)S(1)}, bf16[128,1024]{1,0:T(8,128)(2,1)S(1)}, u32[]{:S(2)}, u32[]{:S(2)}) collective-permute-start(bf16[128,1024]{1,0:T(8,128)(2,1)S(1)} %collective-permute-done.6.refs_4_), channel_id=1, source_target_pairs={{0,1},{1,0},{2,3},{3,2},{4,5},{5,4},{6,7},{7,6},{8,9},{9,8},{10,11... | collective-permute-start | bytes 786440 | tf_op jit(solution)/shard_map/ppermute | solution.py:316
  31.3 1.2 %collective-permute-start.10 = (f32[8,256]{1,0:T(8,128)S(1)}, f32[8,256]{1,0:T(8,128)S(1)}, u32[]{:S(2)}, u32[]{:S(2)}) collective-permute-start(f32[8,256]{1,0:T(8,128)S(1)} %get-tuple-element.37.mine), channel_id=1, source_target_pairs={{0,1},{1,0},{2,3},{3,2},{4,5},{5,4},{6,7},{7,6},{8,9},{9,8},{10,11... | collective-permute-start | bytes 24584 | tf_op jit(solution)/shard_map/ppermute | solution.py:316
  45.9 2.0 %collective-permute-start.16 = (bf16[4,64,1024]{2,1,0:T(8,128)(2,1)S(1)}, bf16[4,64,1024]{2,1,0:T(8,128)(2,1)S(1)}, u32[]{:S(2)}, u32[]{:S(2)}) collective-permute-start(bf16[4,64,1024]{2,1,0:T(8,128)(2,1)S(1)} %get-tuple-element.51), channel_id=1, source_target_pairs={{0,1},{1,0},{2,3},{3,2},{4,5},{5,4},{6,7},{7,6},{8,9},{9,8},{10,11... | collective-permute-start | bytes 1572872 | tf_op jit(solution)/shard_map/ppermute | solution.py:316
  46.0 5.5 %collective-permute-start.11 = (bf16[4,64,1024]{2,1,0:T(8,128)(2,1)S(1)}, bf16[4,64,1024]{2,1,0:T(8,128)(2,1)S(1)}, u32[]{:S(2)}, u32[]{:S(2)}) collective-permute-start(bf16[4,64,1024]{2,1,0:T(8,128)(2,1)S(1)} %get-tuple-element.42), channel_id=1, source_target_pairs={{0,1},{1,0},{2,3},{3,2},{4,5},{5,4},{6,7},{7,6},{8,9},{9,8},{10,11... | collective-permute-start | bytes 1572872 | tf_op jit(solution)/shard_map/ppermute | solution.py:316
  48.0 5.6 %collective-permute-start.17 = (bf16[64,1024]{1,0:T(8,128)(2,1)S(1)}, bf16[64,1024]{1,0:T(8,128)(2,1)S(1)}, u32[]{:S(2)}, u32[]{:S(2)}) collective-permute-start(bf16[64,1024]{1,0:T(8,128)(2,1)S(1)} %get-tuple-element.53), channel_id=1, source_target_pairs={{0,4},{1,5},{2,6},{3,7},{4,0},{5,1},{6,2},{7,3},{8,12},{9,13},{10,... | collective-permute-start | bytes 393224 | tf_op jit(solution)/shard_map/ppermute | solution.py:316
  48.7 9.1 %collective-permute-start.18 = (bf16[64,1024]{1,0:T(8,128)(2,1)S(1)}, bf16[64,1024]{1,0:T(8,128)(2,1)S(1)}, u32[]{:S(2)}, u32[]{:S(2)}) collective-permute-start(bf16[64,1024]{1,0:T(8,128)(2,1)S(1)} %get-tuple-element.54), channel_id=1, source_target_pairs={{0,2},{1,3},{2,0},{3,1},{4,6},{5,7},{6,4},{7,5},{8,10},{9,11},{10,... | collective-permute-start | bytes 393224 | tf_op jit(solution)/shard_map/ppermute | solution.py:316
  49.2 9.5 %collective-permute-start.19 = (bf16[64,1024]{1,0:T(8,128)(2,1)S(1)}, bf16[64,1024]{1,0:T(8,128)(2,1)S(1)}, u32[]{:S(2)}, u32[]{:S(2)}) collective-permute-start(bf16[64,1024]{1,0:T(8,128)(2,1)S(1)} %get-tuple-element.55), channel_id=1, source_target_pairs={{0,6},{1,7},{2,4},{3,5},{4,2},{5,3},{6,0},{7,1},{8,14},{9,15},{10,... | collective-permute-start | bytes 393224 | tf_op jit(solution)/shard_map/ppermute | solution.py:316
  51.7 10.2 %collective-permute-start.12 = (bf16[64,1024]{1,0:T(8,128)(2,1)S(1)}, bf16[64,1024]{1,0:T(8,128)(2,1)S(1)}, u32[]{:S(2)}, u32[]{:S(2)}) collective-permute-start(bf16[64,1024]{1,0:T(8,128)(2,1)S(1)} %get-tuple-element.45), channel_id=1, source_target_pairs={{0,4},{1,5},{2,6},{3,7},{4,0},{5,1},{6,2},{7,3},{8,12},{9,13},{10,... | collective-permute-start | bytes 393224 | tf_op jit(solution)/shard_map/ppermute | solution.py:316
  52.4 9.5 %collective-permute-start.13 = (bf16[64,1024]{1,0:T(8,128)(2,1)S(1)}, bf16[64,1024]{1,0:T(8,128)(2,1)S(1)}, u32[]{:S(2)}, u32[]{:S(2)}) collective-permute-start(bf16[64,1024]{1,0:T(8,128)(2,1)S(1)} %get-tuple-element.46), channel_id=1, source_target_pairs={{0,2},{1,3},{2,0},{3,1},{4,6},{5,7},{6,4},{7,5},{8,10},{9,11},{10,... | collective-permute-start | bytes 393224 | tf_op jit(solution)/shard_map/ppermute | solution.py:316
  53.6 9.6 %collective-permute-start.14 = (bf16[64,1024]{1,0:T(8,128)(2,1)S(1)}, bf16[64,1024]{1,0:T(8,128)(2,1)S(1)}, u32[]{:S(2)}, u32[]{:S(2)}) collective-permute-start(bf16[64,1024]{1,0:T(8,128)(2,1)S(1)} %get-tuple-element.47), channel_id=1, source_target_pairs={{0,6},{1,7},{2,4},{3,5},{4,2},{5,3},{6,0},{7,1},{8,14},{9,15},{10,... | collective-permute-start | bytes 393224 | tf_op jit(solution)/shard_map/ppermute | solution.py:316
  58.8 5.9 %collective-permute-start.20 = (bf16[32,1024]{1,0:T(8,128)(2,1)S(1)}, bf16[32,1024]{1,0:T(8,128)(2,1)S(1)}, u32[]{:S(2)}, u32[]{:S(2)}) collective-permute-start(bf16[32,1024]{1,0:T(8,128)(2,1)S(1)} %get-tuple-element.56), channel_id=1, source_target_pairs={{0,16},{1,17},{2,18},{3,19},{4,20},{5,21},{6,22},{7,23},{8,24},{9,... | collective-permute-start | bytes 196616 | tf_op jit(solution)/shard_map/ppermute | solution.py:316
  59.5 6.6 %collective-permute-start.21 = (bf16[32,1024]{1,0:T(8,128)(2,1)S(1)}, bf16[32,1024]{1,0:T(8,128)(2,1)S(1)}, u32[]{:S(2)}, u32[]{:S(2)}) collective-permute-start(bf16[32,1024]{1,0:T(8,128)(2,1)S(1)} %get-tuple-element.57), channel_id=1, source_target_pairs={{0,24},{1,25},{2,26},{3,27},{4,28},{5,29},{6,30},{7,31},{8,16},{9,... | collective-permute-start | bytes 196616 | tf_op jit(solution)/shard_map/ppermute | solution.py:316
  63.3 4.3 %collective-permute-start.15 = (bf16[32,1024]{1,0:T(8,128)(2,1)S(1)}, bf16[32,1024]{1,0:T(8,128)(2,1)S(1)}, u32[]{:S(2)}, u32[]{:S(2)}) collective-permute-start(bf16[32,1024]{1,0:T(8,128)(2,1)S(1)} %get-tuple-element.49), channel_id=1, source_target_pairs={{0,8},{1,9},{2,10},{3,11},{4,12},{5,13},{6,14},{7,15},{8,0},{9,1},... | collective-permute-start | bytes 196616 | tf_op jit(solution)/shard_map/ppermute | solution.py:316

commit v9 on v8

--- a/solution.py
+++ b/solution.py
@@ -104,14 +104,11 @@
     rows[:, :width] = packed.astype(jnp.bfloat16)
 
 
-def join_kernel(*refs):
+def join_kernel(order, *refs):
     blocks, line, plain = refs[:-2], refs[-2], refs[-1]
-    start = 0
-    for block in blocks:
-        end = start + block.shape[0]
-        line[start:end] = block[...]
-        plain[start:end] = block[:, :plain.shape[1]]
-        start = end
+    for place, block in zip(order, blocks):
+        line[place * CAP:(place + 1) * CAP] = block[...]
+        plain[place * CAP:(place + 1) * CAP] = block[:, :plain.shape[1]]
 
 
 def stage_kernel(line, weight, held, same, sems):
@@ -165,19 +162,28 @@
     return jnp.concatenate([ref[:, :width] for ref in pieces[2 * block:2 * block + 2]], axis=0)
 
 
-def logits_kernel(blocks, groups, info, weight, *refs):
-    pieces, (logits, stats) = refs[:-2], refs[-2:]
-    rank, position, shard = coordinates()
+def some_logits(blocks, first, pieces, weight):
     width = weight.shape[0] // blocks
-    total = None
-    for block in range(blocks):
+    rank, total = coordinates()[0], None
+    for place, block in enumerate(range(first, blocks, 2)):
         start = pl.multiple_of((rank ^ block) * width, width)
         part = jnp.dot(
-            all_rows(pieces, block, width),
+            all_rows(pieces, place, width),
             weight[pl.ds(start, width), :],
             preferred_element_type=jnp.float32,
         )
         total = part if total is None else total + part
+    return total
+
+
+def first_kernel(blocks, weight, *refs):
+    refs[-1][...] = some_logits(blocks, 0, refs[:-1], weight)
+
+
+def logits_kernel(blocks, groups, info, partial, weight, *refs):
+    pieces, (logits, stats) = refs[:-2], refs[-2:]
+    _, position, shard = coordinates()
+    total = partial[...] + some_logits(blocks, 1, pieces, weight)
     logits[...] = total
     height, columns = total.shape
     target = info[:, 1:2].astype(jnp.int32) - shard * columns
@@ -188,20 +194,9 @@
     mass = jnp.sum(jnp.exp(total - peak), axis=1, keepdims=True)
     lane = lax.broadcasted_iota(jnp.int32, (height, 128), 1)
     table = jnp.where(lane == 0, peak, jnp.where(lane == 1, mass, hit))
-    stats[...] = reorder(jnp.transpose(table)[0:8], position, groups)
-
-
-def merge(tables):
-    peak = functools.reduce(jnp.maximum, [table[0:1] for table in tables])
-    mass = sum(table[1:2] * jnp.exp(table[0:1] - peak) for table in tables)
-    hit = sum(table[2:3] for table in tables)
-    return peak, mass, hit
-
-
-def merge_kernel(mine, theirs, out):
-    peak, mass, hit = merge([mine[...], theirs[...]])
-    line = jnp.concatenate([peak, mass, hit[:, :128]], axis=1)
-    out[...] = jnp.broadcast_to(line[None], out.shape)
+    table = reorder(jnp.transpose(table)[0:8], position, groups)
+    line = jnp.concatenate([table[0:1], table[1:2], table[2:3, :128]], axis=1)
+    stats[...] = jnp.broadcast_to(line[None], stats.shape)
 
 
 def block_grads(blocks, rank, first, grad, weight, outs):
@@ -334,10 +329,11 @@
         + [pltpu.SemaphoreType.DMA((4,))],
     )
 
-    blocks = [packed] + [send(packed, z=z) for z in range(1, zs)]
+    line_order = [0, 1] + list(range(zs - 1, 1, -1))
+    blocks = [send(packed, z=z) if z else packed for z in line_order]
     line_rows = zs * CAP
     line, line_plain = call(
-        join_kernel,
+        functools.partial(join_kernel, line_order),
         blocks,
         [VMEM] * zs,
         (shape((line_rows, width + IDS), bf16), shape((line_rows, width), bf16)),
@@ -364,26 +360,28 @@
         shape((total_rows, 128), f32),
         VMEM,
     )
+    near = [pieces[b, y] for b in range(0, ranks, 2) for y in range(2)]
+    partial = call(
+        functools.partial(first_kernel, ranks),
+        (held, *near),
+        [VMEM] * (1 + len(near)),
+        shape((total_rows, columns), f32),
+        VMEM,
+        flops=flops // 2,
+    )
+    beside = [pieces[b, y] for b in range(1, ranks, 2) for y in range(2)]
     logits, stats = call(
         functools.partial(logits_kernel, ranks, dps),
-        (info, held, *rows),
-        [VMEM] * (2 + len(rows)),
-        (shape((total_rows, columns), f32), shape((8, total_rows), f32)),
+        (info, partial, held, *beside),
+        [VMEM] * (3 + len(beside)),
+        (
+            shape((total_rows, columns), f32),
+            shape((dps * ranks, 1, 2 * total_rows + 128), f32),
+        ),
         (VMEM, VMEM),
-        flops=flops,
-    )
-
-    stats = call(
-        merge_kernel,
-        (stats, send(stats, core=1)),
-        [VMEM] * 2,
-        shape((dps * xs, 1, 2 * total_rows + 128), f32),
-        VMEM,
-    )
-    chips = [
-        [d * ranks + v for d in range(dps) for v in range(core, ranks, 2)] for core in range(2)
-    ]
-    stats = lax.all_to_all(stats, AXES, 0, 0, axis_index_groups=chips)
+        flops=flops // 2,
+    )
+    stats = lax.all_to_all(stats, AXES, 0, 0)
 
     rows_part = total_rows // 4
     whole = (ranks, rows_part, width)

time: 68.7 us -> 67.2 us (0.978)
  waiting for transfers between devices: 23.5 us -> 20.3 us
  blocking collectives: 12.3 us -> 13.9 us
    ppermute x22 -> x21, waiting for transfers between devices: 23.5 us -> 20.3 us  [send(): return lax.ppermute(value, AXES, pairs)]
    all_to_all x1, blocking collectives: 12.3 us -> 13.9 us  [body(): stats = lax.all_to_all(stats, AXES, 0, 0)]
    ppermute x22 -> x21, starting transfers between devices: 20.8 us -> 20.7 us  [send(): return lax.ppermute(value, AXES, pairs)]
  transfers between devices with their start and end apart: 22 -> 21, of which waited for: 14 -> 13; matrix products, arithmetic and copies ran while one was open for 0% -> 0% of each run, Pallas kernels for 9% -> 10%
where the time goes in v9:
time: 67.2 us; the launch traced here: 67.1 us
  starting transfers between devices  20.7 us (31%)
  waiting for transfers between devices  20.3 us (30%)
  blocking collectives  13.9 us (21%)
  Pallas kernels  11.4 us (17%)
  between operations  0.76 us (1%)
    ppermute x21, starting transfers between devices, send(): return lax.ppermute(value, AXES, pairs)  20.7 us
    ppermute x21, waiting for transfers between devices, send(): return lax.ppermute(value, AXES, pairs)  20.3 us
    all_to_all x1, blocking collectives, body(): stats = lax.all_to_all(stats, AXES, 0, 0)  13.9 us
    pallas_call x14, Pallas kernels, call(): pl.pallas_call(kernel, out_shape=out_shape, in_specs=in_specs, out_specs=...  11.4 us
  transfers between devices with their start and end apart: 21, of which 13 were waited for; matrix products, arithmetic and copies ran while one was open for 0% of the time, Pallas kernels for 10%

profile of v9, /device:TPU:0, one launch (start us, length us, event | category | flops | bytes accessed | tf_op | source)
XLA Modules:
  0.0 67.1 jit_solution(2981810182275909580)
XLA Ops:
  0.6 1.2 %shard_map.85 = (bf16[32,1152]{1,0:T(8,128)(2,1)S(1)}, bf16[32,128]{1,0:T(8,128)(2,1)S(1)}) custom-call(bf16[128,1024]{1,0:T(8,128)(2,1)} %hidden_hbm.1, s32[1,128]{1,0:T(1,128)} %bitcast.6, s32[1,128]{1,0:T(1,128)} %bitcast.7, s32[1,128]{1,0:T(1,128)} %bitcast.8), custom_call_target="tpu_custom_call" | custom-call | bytes 345600 | tf_op jit(solution)/shard_map/pallas_call | solution.py:32
  1.9 4.1 %collective-permute-start.2 = (bf16[32,1152]{1,0:T(8,128)(2,1)S(1)}, bf16[32,1152]{1,0:T(8,128)(2,1)S(1)}, u32[]{:S(2)}, u32[]{:S(2)}) collective-permute-start(bf16[32,1152]{1,0:T(8,128)(2,1)S(1)} %get-tuple-element.31.refs_0_), channel_id=1, source_target_pairs={{0,16},{1,17},{2,18},{3,19},{4,20},{5,21},{6,22},{7,23},{8,24},{9,... | collective-permute-start | bytes 221192 | tf_op jit(solution)/shard_map/ppermute | solution.py:311
  6.0 1.3 %collective-permute-start.1 = (bf16[32,1152]{1,0:T(8,128)(2,1)S(1)}, bf16[32,1152]{1,0:T(8,128)(2,1)S(1)}, u32[]{:S(2)}, u32[]{:S(2)}) collective-permute-start(bf16[32,1152]{1,0:T(8,128)(2,1)S(1)} %get-tuple-element.31.refs_0_), channel_id=1, source_target_pairs={{0,24},{1,25},{2,26},{3,27},{4,28},{5,29},{6,30},{7,31},{8,16},{9,... | collective-permute-start | bytes 221192 | tf_op jit(solution)/shard_map/ppermute | solution.py:311
  7.5 3.3 %collective-permute-done.2.refs_3_ = bf16[32,1152]{1,0:T(8,128)(2,1)S(1)} collective-permute-done((bf16[32,1152]{1,0:T(8,128)(2,1)S(1)}, bf16[32,1152]{1,0:T(8,128)(2,1)S(1)}, u32[]{:S(2)}, u32[]{:S(2)}) %collective-permute-start.2) | collective-permute-done | bytes 73760 | tf_op jit(solution)/shard_map/ppermute | solution.py:311
  10.8 1.6 %collective-permute-done.1.refs_2_ = bf16[32,1152]{1,0:T(8,128)(2,1)S(1)} collective-permute-done((bf16[32,1152]{1,0:T(8,128)(2,1)S(1)}, bf16[32,1152]{1,0:T(8,128)(2,1)S(1)}, u32[]{:S(2)}, u32[]{:S(2)}) %collective-permute-start.1) | collective-permute-done | bytes 73760 | tf_op jit(solution)/shard_map/ppermute | solution.py:311
  12.6 1.8 %collective-permute-start.3 = (bf16[128,1152]{1,0:T(8,128)(2,1)S(1)}, bf16[128,1152]{1,0:T(8,128)(2,1)S(1)}, u32[]{:S(2)}, u32[]{:S(2)}) collective-permute-start(bf16[128,1152]{1,0:T(8,128)(2,1)S(1)} %get-tuple-element.32.line), channel_id=1, source_target_pairs={{0,4},{1,5},{2,6},{3,7},{4,0},{5,1},{6,2},{7,3},{8,12},{9,13},{10,... | collective-permute-start | bytes 884744 | tf_op jit(solution)/shard_map/ppermute | solution.py:311
  14.4 1.4 %collective-permute-start.5 = (bf16[128,1024]{1,0:T(8,128)(2,1)S(1)}, bf16[128,1024]{1,0:T(8,128)(2,1)S(1)}, u32[]{:S(2)}, u32[]{:S(2)}) collective-permute-start(bf16[128,1024]{1,0:T(8,128)(2,1)S(1)} %get-tuple-element.35), channel_id=1, source_target_pairs={{0,6},{1,7},{2,4},{3,5},{4,2},{5,3},{6,0},{7,1},{8,14},{9,15},{10,... | collective-permute-start | bytes 786440 | tf_op jit(solution)/shard_map/ppermute | solution.py:311
  16.2 2.2 %shard_map.87 = (bf16[4096,512]{1,0:T(8,128)(2,1)S(1)}, bf16[128,1152]{1,0:T(8,128)(2,1)S(1)}) custom-call(bf16[128,1152]{1,0:T(8,128)(2,1)S(1)} %get-tuple-element.32.line, bf16[4096,512]{1,0:T(8,128)(2,1)} %weight.1), custom_call_target="tpu_custom_call" | custom-call | bytes 8978432 | tf_op jit(solution)/shard_map/pallas_call | solution.py:32
  18.5 7.4 %collective-permute-done.3.refs_1_ = bf16[128,1152]{1,0:T(8,128)(2,1)S(1)} collective-permute-done((bf16[128,1152]{1,0:T(8,128)(2,1)S(1)}, bf16[128,1152]{1,0:T(8,128)(2,1)S(1)}, u32[]{:S(2)}, u32[]{:S(2)}) %collective-permute-start.3) | collective-permute-done | bytes 294944 | tf_op jit(solution)/shard_map/ppermute | solution.py:311
  26.8 0.7 %shard_map.89.partial = f32[256,512]{1,0:T(8,128)S(1)} custom-call(bf16[4096,512]{1,0:T(8,128)(2,1)S(1)} %get-tuple-element.34.weight, bf16[128,1152]{1,0:T(8,128)(2,1)S(1)} %get-tuple-element.33.refs_0_, bf16[128,1152]{1,0:T(8,128)(2,1)S(1)} %collective-permute-done.3.refs_1_, bf16[128,1024]{1,0:T(8,128)(2,1)S(1)} %collective-permute-done.4.refs_2_.refs_4_, ...), custom_call_target="tpu_custom_call" | custom-call | flops 536870912 | bytes 5832704 | tf_op jit(solution)/shard_map/pallas_call | solution.py:32
  28.2 1.2 %shard_map.90 = (f32[256,512]{1,0:T(8,128)S(1)}, f32[32,1,640]{2,1,0:T(1,128)S(1)}) custom-call(f32[256,128]{1,0:T(8,128)S(1)} %shard_map.88.info, f32[256,512]{1,0:T(8,128)S(1)} %shard_map.89.partial, bf16[4096,512]{1,0:T(8,128)(2,1)S(1)} %get-tuple-element.34.weight, bf16[128,1152]{1,0:T(8,128)(2,1)S(1)} %collective-permute-done.6.refs_0_.refs_2_, ...), custom_call_target="tpu_custom_call" | custom-call | flops 536870912 | bytes 6569984 | tf_op jit(solution)/shard_map/pallas_call | solution.py:32
  29.4 13.9 %all_to_all.5.stats = f32[32,1,640]{2,1,0:T(1,128)S(1)} all-to-all(f32[32,1,640]{2,1,0:T(1,128)S(1)} %get-tuple-element.37), channel_id=1, replica_groups=mesh['dp'=8,'vocab'=4] {'dp','vocab'}, dimensions={0} | all-to-all | bytes 163840 | tf_op jit(solution)/shard_map/all_to_all | solution.py:384
  43.3 1.1 %shard_map.91 = (bf16[4,64,1024]{2,1,0:T(8,128)(2,1)S(1)}, bf16[4,64,1024]{2,1,0:T(8,128)(2,1)S(1)}, bf16[256,512]{1,0:T(8,128)(2,1)S(1)}, f32[1,1]{1,0:T(1,128)}) custom-call(f32[256,128]{1,0:T(8,128)S(1)} %shard_map.88.info, f32[256,512]{1,0:T(8,128)S(1)} %get-tuple-element.36.logits, bf16[4096,512]{1,0:T(8,128)(2,1)S(1)} %get-tuple-element.34.weight, ...), custom_call_target="tpu_custom_call" | custom-call | flops 536870912 | bytes 6242308 | tf_op jit(solution)/shard_map/pallas_call | solution.py:32
  45.0 0.7 %shard_map.92 = (f32[4,64,1024]{2,1,0:T(8,128)S(1)}, f32[4,64,1024]{2,1,0:T(8,128)S(1)}) custom-call(bf16[256,512]{1,0:T(8,128)(2,1)S(1)} %get-tuple-element.40.logit_grad.after, bf16[4096,512]{1,0:T(8,128)(2,1)S(1)} %get-tuple-element.34.weight), custom_call_target="tpu_custom_call" | custom-call | flops 536870912 | bytes 6553600 | tf_op jit(solution)/shard_map/pallas_call | solution.py:32
  45.8 0.7 collective-permute-done.15.beside
  46.5 0.7 %collective-permute-start.16 = (bf16[64,1024]{1,0:T(8,128)(2,1)S(1)}, bf16[64,1024]{1,0:T(8,128)(2,1)S(1)}, u32[]{:S(2)}, u32[]{:S(2)}) collective-permute-start(bf16[64,1024]{1,0:T(8,128)(2,1)S(1)} %get-tuple-element.53), channel_id=1, source_target_pairs={{0,4},{1,5},{2,6},{3,7},{4,0},{5,1},{6,2},{7,3},{8,12},{9,13},{10,... | collective-permute-start | bytes 393224 | tf_op jit(solution)/shard_map/ppermute | solution.py:311
  47.2 0.7 %collective-permute-start.17 = (bf16[64,1024]{1,0:T(8,128)(2,1)S(1)}, bf16[64,1024]{1,0:T(8,128)(2,1)S(1)}, u32[]{:S(2)}, u32[]{:S(2)}) collective-permute-start(bf16[64,1024]{1,0:T(8,128)(2,1)S(1)} %get-tuple-element.54), channel_id=1, source_target_pairs={{0,2},{1,3},{2,0},{3,1},{4,6},{5,7},{6,4},{7,5},{8,10},{9,11},{10,... | collective-permute-start | bytes 393224 | tf_op jit(solution)/shard_map/ppermute | solution.py:311
  47.9 2.2 %collective-permute-start.18 = (bf16[64,1024]{1,0:T(8,128)(2,1)S(1)}, bf16[64,1024]{1,0:T(8,128)(2,1)S(1)}, u32[]{:S(2)}, u32[]{:S(2)}) collective-permute-start(bf16[64,1024]{1,0:T(8,128)(2,1)S(1)} %get-tuple-element.55), channel_id=1, source_target_pairs={{0,6},{1,7},{2,4},{3,5},{4,2},{5,3},{6,0},{7,1},{8,14},{9,15},{10,... | collective-permute-start | bytes 393224 | tf_op jit(solution)/shard_map/ppermute | solution.py:311
  50.1 0.7 %collective-permute-start.11 = (bf16[64,1024]{1,0:T(8,128)(2,1)S(1)}, bf16[64,1024]{1,0:T(8,128)(2,1)S(1)}, u32[]{:S(2)}, u32[]{:S(2)}) collective-permute-start(bf16[64,1024]{1,0:T(8,128)(2,1)S(1)} %get-tuple-element.45), channel_id=1, source_target_pairs={{0,4},{1,5},{2,6},{3,7},{4,0},{5,1},{6,2},{7,3},{8,12},{9,13},{10,... | collective-permute-start | bytes 393224 | tf_op jit(solution)/shard_map/ppermute | solution.py:311
  50.8 0.7 %collective-permute-start.12 = (bf16[64,1024]{1,0:T(8,128)(2,1)S(1)}, bf16[64,1024]{1,0:T(8,128)(2,1)S(1)}, u32[]{:S(2)}, u32[]{:S(2)}) collective-permute-start(bf16[64,1024]{1,0:T(8,128)(2,1)S(1)} %get-tuple-element.46), channel_id=1, source_target_pairs={{0,2},{1,3},{2,0},{3,1},{4,6},{5,7},{6,4},{7,5},{8,10},{9,11},{10,... | collective-permute-start | bytes 393224 | tf_op jit(solution)/shard_map/ppermute | solution.py:311
  51.5 0.6 collective-permute-done.16.refs_0_
  52.1 1.6 %collective-permute-start.13 = (bf16[64,1024]{1,0:T(8,128)(2,1)S(1)}, bf16[64,1024]{1,0:T(8,128)(2,1)S(1)}, u32[]{:S(2)}, u32[]{:S(2)}) collective-permute-start(bf16[64,1024]{1,0:T(8,128)(2,1)S(1)} %get-tuple-element.47), channel_id=1, source_target_pairs={{0,6},{1,7},{2,4},{3,5},{4,2},{5,3},{6,0},{7,1},{8,14},{9,15},{10,... | collective-permute-start | bytes 393224 | tf_op jit(solution)/shard_map/ppermute | solution.py:311
  53.7 2.5 %shard_map.94 = (bf16[4096,512]{1,0:T(8,128)(2,1)}, f32[8,128]{1,0:T(8,128)S(1)}) custom-call(f32[64,1024]{1,0:T(8,128)S(1)} %get-tuple-element.43.after.kept, bf16[256,512]{1,0:T(8,128)(2,1)S(1)} %get-tuple-element.40.logit_grad.after, bf16[128,1152]{1,0:T(8,128)(2,1)S(1)} %get-tuple-element.33.refs_0_, ...), custom_call_target="tpu_custom_call" | custom-call | flops 1073741824 | bytes 6950912 | tf_op jit(solution)/shard_map/pallas_call | solution.py:32
  56.2 1.0 %collective-permute-done.18.refs_2_ = bf16[64,1024]{1,0:T(8,128)(2,1)S(1)} collective-permute-done((bf16[64,1024]{1,0:T(8,128)(2,1)S(1)}, bf16[64,1024]{1,0:T(8,128)(2,1)S(1)}, u32[]{:S(2)}, u32[]{:S(2)}) %collective-permute-start.18) | collective-permute-done | bytes 131104 | tf_op jit(solution)/shard_map/ppermute | solution.py:311
  57.3 0.8 %collective-permute-start.19 = (bf16[32,1024]{1,0:T(8,128)(2,1)S(1)}, bf16[32,1024]{1,0:T(8,128)(2,1)S(1)}, u32[]{:S(2)}, u32[]{:S(2)}) collective-permute-start(bf16[32,1024]{1,0:T(8,128)(2,1)S(1)} %get-tuple-element.56), channel_id=1, source_target_pairs={{0,16},{1,17},{2,18},{3,19},{4,20},{5,21},{6,22},{7,23},{8,24},{9,... | collective-permute-start | bytes 196616 | tf_op jit(solution)/shard_map/ppermute | solution.py:311
  58.1 2.3 %collective-permute-start.20 = (bf16[32,1024]{1,0:T(8,128)(2,1)S(1)}, bf16[32,1024]{1,0:T(8,128)(2,1)S(1)}, u32[]{:S(2)}, u32[]{:S(2)}) collective-permute-start(bf16[32,1024]{1,0:T(8,128)(2,1)S(1)} %get-tuple-element.57), channel_id=1, source_target_pairs={{0,24},{1,25},{2,26},{3,27},{4,28},{5,29},{6,30},{7,31},{8,16},{9,... | collective-permute-start | bytes 196616 | tf_op jit(solution)/shard_map/ppermute | solution.py:311
  60.3 1.4 %collective-permute-done.13.refs_2_ = bf16[64,1024]{1,0:T(8,128)(2,1)S(1)} collective-permute-done((bf16[64,1024]{1,0:T(8,128)(2,1)S(1)}, bf16[64,1024]{1,0:T(8,128)(2,1)S(1)}, u32[]{:S(2)}, u32[]{:S(2)}) %collective-permute-start.13) | collective-permute-done | bytes 131104 | tf_op jit(solution)/shard_map/ppermute | solution.py:311
  61.8 0.7 %collective-permute-start.14 = (bf16[32,1024]{1,0:T(8,128)(2,1)S(1)}, bf16[32,1024]{1,0:T(8,128)(2,1)S(1)}, u32[]{:S(2)}, u32[]{:S(2)}) collective-permute-start(bf16[32,1024]{1,0:T(8,128)(2,1)S(1)} %get-tuple-element.49), channel_id=1, source_target_pairs={{0,8},{1,9},{2,10},{3,11},{4,12},{5,13},{6,14},{7,15},{8,0},{9,1},... | collective-permute-start | bytes 196616 | tf_op jit(solution)/shard_map/ppermute | solution.py:311
  62.5 0.7 %collective-permute-done.19.refs_2_ = bf16[32,1024]{1,0:T(8,128)(2,1)S(1)} collective-permute-done((bf16[32,1024]{1,0:T(8,128)(2,1)S(1)}, bf16[32,1024]{1,0:T(8,128)(2,1)S(1)}, u32[]{:S(2)}, u32[]{:S(2)}) %collective-permute-start.19) | collective-permute-done | bytes 65568 | tf_op jit(solution)/shard_map/ppermute | solution.py:311
  63.2 1.4 %collective-permute-done.20.refs_3_ = bf16[32,1024]{1,0:T(8,128)(2,1)S(1)} collective-permute-done((bf16[32,1024]{1,0:T(8,128)(2,1)S(1)}, bf16[32,1024]{1,0:T(8,128)(2,1)S(1)}, u32[]{:S(2)}, u32[]{:S(2)}) %collective-permute-start.20) | collective-permute-done | bytes 65568 | tf_op jit(solution)/shard_map/ppermute | solution.py:311
  64.7 1.4 %collective-permute-done.14.refs_1_ = bf16[32,1024]{1,0:T(8,128)(2,1)S(1)} collective-permute-done((bf16[32,1024]{1,0:T(8,128)(2,1)S(1)}, bf16[32,1024]{1,0:T(8,128)(2,1)S(1)}, u32[]{:S(2)}, u32[]{:S(2)}) %collective-permute-start.14) | collective-permute-done | bytes 65568 | tf_op jit(solution)/shard_map/ppermute | solution.py:311
  66.1 1.0 %shard_map.98 = bf16[128,1024]{1,0:T(8,128)(2,1)} custom-call(bf16[32,128]{1,0:T(8,128)(2,1)S(1)} %get-tuple-element.39.chosen, f32[32,1024]{1,0:T(8,128)S(1)} %get-tuple-element.48.refs_0_, bf16[32,1024]{1,0:T(8,128)(2,1)S(1)} %collective-permute-done.14.refs_1_, bf16[32,1024]{1,0:T(8,128)(2,1)S(1)} %collective-permute-done.19.refs_2_, ...), custom_call_target="tpu_custom_call" | custom-call | bytes 598016 | tf_op jit(solution)/shard_map/pallas_call | solution.py:32
  (27 shorter events, 3.3 us)
Async XLA Ops:
  0.6 25.8 %copy-start = (f32[32]{0:T(128)S(1)}, f32[32]{0:T(128)}, u32[]{:S(2)}) copy-start(f32[32]{0:T(128)} %param.11) | copy-start | bytes 388
  1.9 9.0 %collective-permute-start.2 = (bf16[32,1152]{1,0:T(8,128)(2,1)S(1)}, bf16[32,1152]{1,0:T(8,128)(2,1)S(1)}, u32[]{:S(2)}, u32[]{:S(2)}) collective-permute-start(bf16[32,1152]{1,0:T(8,128)(2,1)S(1)} %get-tuple-element.31.refs_0_), channel_id=1, source_target_pairs={{0,16},{1,17},{2,18},{3,19},{4,20},{5,21},{6,22},{7,23},{8,24},{9,... | collective-permute-start | bytes 221192 | tf_op jit(solution)/shard_map/ppermute | solution.py:311
  6.0 6.5 %collective-permute-start.1 = (bf16[32,1152]{1,0:T(8,128)(2,1)S(1)}, bf16[32,1152]{1,0:T(8,128)(2,1)S(1)}, u32[]{:S(2)}, u32[]{:S(2)}) collective-permute-start(bf16[32,1152]{1,0:T(8,128)(2,1)S(1)} %get-tuple-element.31.refs_0_), channel_id=1, source_target_pairs={{0,24},{1,25},{2,26},{3,27},{4,28},{5,29},{6,30},{7,31},{8,16},{9,... | collective-permute-start | bytes 221192 | tf_op jit(solution)/shard_map/ppermute | solution.py:311
  7.3 5.3 %collective-permute-start = (bf16[32,1152]{1,0:T(8,128)(2,1)S(1)}, bf16[32,1152]{1,0:T(8,128)(2,1)S(1)}, u32[]{:S(2)}, u32[]{:S(2)}) collective-permute-start(bf16[32,1152]{1,0:T(8,128)(2,1)S(1)} %get-tuple-element.31.refs_0_), channel_id=1, source_target_pairs={{0,8},{1,9},{2,10},{3,11},{4,12},{5,13},{6,14},{7,15},{8,0},{9,1},... | collective-permute-start | bytes 221192 | tf_op jit(solution)/shard_map/ppermute | solution.py:311
  12.6 13.2 %collective-permute-start.3 = (bf16[128,1152]{1,0:T(8,128)(2,1)S(1)}, bf16[128,1152]{1,0:T(8,128)(2,1)S(1)}, u32[]{:S(2)}, u32[]{:S(2)}) collective-permute-start(bf16[128,1152]{1,0:T(8,128)(2,1)S(1)} %get-tuple-element.32.line), channel_id=1, source_target_pairs={{0,4},{1,5},{2,6},{3,7},{4,0},{5,1},{6,2},{7,3},{8,12},{9,13},{10,... | collective-permute-start | bytes 884744 | tf_op jit(solution)/shard_map/ppermute | solution.py:311
  14.4 11.4 %collective-permute-start.5 = (bf16[128,1024]{1,0:T(8,128)(2,1)S(1)}, bf16[128,1024]{1,0:T(8,128)(2,1)S(1)}, u32[]{:S(2)}, u32[]{:S(2)}) collective-permute-start(bf16[128,1024]{1,0:T(8,128)(2,1)S(1)} %get-tuple-element.35), channel_id=1, source_target_pairs={{0,6},{1,7},{2,4},{3,5},{4,2},{5,3},{6,0},{7,1},{8,14},{9,15},{10,... | collective-permute-start | bytes 786440 | tf_op jit(solution)/shard_map/ppermute | solution.py:311
  15.9 10.5 %collective-permute-start.4 = (bf16[128,1024]{1,0:T(8,128)(2,1)S(1)}, bf16[128,1024]{1,0:T(8,128)(2,1)S(1)}, u32[]{:S(2)}, u32[]{:S(2)}) collective-permute-start(bf16[128,1024]{1,0:T(8,128)(2,1)S(1)} %get-tuple-element.35), channel_id=1, source_target_pairs={{0,2},{1,3},{2,0},{3,1},{4,6},{5,7},{6,4},{7,5},{8,10},{9,11},{10,... | collective-permute-start | bytes 786440 | tf_op jit(solution)/shard_map/ppermute | solution.py:311
  18.4 9.2 %collective-permute-start.6 = (bf16[128,1152]{1,0:T(8,128)(2,1)S(1)}, bf16[128,1152]{1,0:T(8,128)(2,1)S(1)}, u32[]{:S(2)}, u32[]{:S(2)}) collective-permute-start(bf16[128,1152]{1,0:T(8,128)(2,1)S(1)} %get-tuple-element.33.refs_0_), channel_id=1, source_target_pairs={{0,1},{1,0},{2,3},{3,2},{4,5},{5,4},{6,7},{7,6},{8,9},{9,8},{10,11... | collective-permute-start | bytes 884744 | tf_op jit(solution)/shard_map/ppermute | solution.py:311
  25.9 2.3 %collective-permute-start.7 = (bf16[128,1152]{1,0:T(8,128)(2,1)S(1)}, bf16[128,1152]{1,0:T(8,128)(2,1)S(1)}, u32[]{:S(2)}, u32[]{:S(2)}) collective-permute-start(bf16[128,1152]{1,0:T(8,128)(2,1)S(1)} %collective-permute-done.3.refs_1_), channel_id=1, source_target_pairs={{0,1},{1,0},{2,3},{3,2},{4,5},{5,4},{6,7},{7,6},{8,9},{9,8},{10,11... | collective-permute-start | bytes 884744 | tf_op jit(solution)/shard_map/ppermute | solution.py:311
  25.9 2.0 %collective-permute-start.9 = (bf16[128,1024]{1,0:T(8,128)(2,1)S(1)}, bf16[128,1024]{1,0:T(8,128)(2,1)S(1)}, u32[]{:S(2)}, u32[]{:S(2)}) collective-permute-start(bf16[128,1024]{1,0:T(8,128)(2,1)S(1)} %collective-permute-done.5.refs_3_.refs_5_), channel_id=1, source_target_pairs={{0,1},{1,0},{2,3},{3,2},{4,5},{5,4},{6,7},{7,6},{8,9},{9,8},{10,11... | collective-permute-start | bytes 786440 | tf_op jit(solution)/shard_map/ppermute | solution.py:311
  26.4 1.8 %collective-permute-start.8 = (bf16[128,1024]{1,0:T(8,128)(2,1)S(1)}, bf16[128,1024]{1,0:T(8,128)(2,1)S(1)}, u32[]{:S(2)}, u32[]{:S(2)}) collective-permute-start(bf16[128,1024]{1,0:T(8,128)(2,1)S(1)} %collective-permute-done.4.refs_2_.refs_4_), channel_id=1, source_target_pairs={{0,1},{1,0},{2,3},{3,2},{4,5},{5,4},{6,7},{7,6},{8,9},{9,8},{10,11... | collective-permute-start | bytes 786440 | tf_op jit(solution)/shard_map/ppermute | solution.py:311
  44.4 2.0 %collective-permute-start.15 = (bf16[4,64,1024]{2,1,0:T(8,128)(2,1)S(1)}, bf16[4,64,1024]{2,1,0:T(8,128)(2,1)S(1)}, u32[]{:S(2)}, u32[]{:S(2)}) collective-permute-start(bf16[4,64,1024]{2,1,0:T(8,128)(2,1)S(1)} %get-tuple-element.51), channel_id=1, source_target_pairs={{0,1},{1,0},{2,3},{3,2},{4,5},{5,4},{6,7},{7,6},{8,9},{9,8},{10,11... | collective-permute-start | bytes 1572872 | tf_op jit(solution)/shard_map/ppermute | solution.py:311
  44.6 5.4 %collective-permute-start.10 = (bf16[4,64,1024]{2,1,0:T(8,128)(2,1)S(1)}, bf16[4,64,1024]{2,1,0:T(8,128)(2,1)S(1)}, u32[]{:S(2)}, u32[]{:S(2)}) collective-permute-start(bf16[4,64,1024]{2,1,0:T(8,128)(2,1)S(1)} %get-tuple-element.42), channel_id=1, source_target_pairs={{0,1},{1,0},{2,3},{3,2},{4,5},{5,4},{6,7},{7,6},{8,9},{9,8},{10,11... | collective-permute-start | bytes 1572872 | tf_op jit(solution)/shard_map/ppermute | solution.py:311
  46.5 5.6 %collective-permute-start.16 = (bf16[64,1024]{1,0:T(8,128)(2,1)S(1)}, bf16[64,1024]{1,0:T(8,128)(2,1)S(1)}, u32[]{:S(2)}, u32[]{:S(2)}) collective-permute-start(bf16[64,1024]{1,0:T(8,128)(2,1)S(1)} %get-tuple-element.53), channel_id=1, source_target_pairs={{0,4},{1,5},{2,6},{3,7},{4,0},{5,1},{6,2},{7,3},{8,12},{9,13},{10,... | collective-permute-start | bytes 393224 | tf_op jit(solution)/shard_map/ppermute | solution.py:311
  47.2 9.0 %collective-permute-start.17 = (bf16[64,1024]{1,0:T(8,128)(2,1)S(1)}, bf16[64,1024]{1,0:T(8,128)(2,1)S(1)}, u32[]{:S(2)}, u32[]{:S(2)}) collective-permute-start(bf16[64,1024]{1,0:T(8,128)(2,1)S(1)} %get-tuple-element.54), channel_id=1, source_target_pairs={{0,2},{1,3},{2,0},{3,1},{4,6},{5,7},{6,4},{7,5},{8,10},{9,11},{10,... | collective-permute-start | bytes 393224 | tf_op jit(solution)/shard_map/ppermute | solution.py:311
  47.9 9.3 %collective-permute-start.18 = (bf16[64,1024]{1,0:T(8,128)(2,1)S(1)}, bf16[64,1024]{1,0:T(8,128)(2,1)S(1)}, u32[]{:S(2)}, u32[]{:S(2)}) collective-permute-start(bf16[64,1024]{1,0:T(8,128)(2,1)S(1)} %get-tuple-element.55), channel_id=1, source_target_pairs={{0,6},{1,7},{2,4},{3,5},{4,2},{5,3},{6,0},{7,1},{8,14},{9,15},{10,... | collective-permute-start | bytes 393224 | tf_op jit(solution)/shard_map/ppermute | solution.py:311
  50.1 10.2 %collective-permute-start.11 = (bf16[64,1024]{1,0:T(8,128)(2,1)S(1)}, bf16[64,1024]{1,0:T(8,128)(2,1)S(1)}, u32[]{:S(2)}, u32[]{:S(2)}) collective-permute-start(bf16[64,1024]{1,0:T(8,128)(2,1)S(1)} %get-tuple-element.45), channel_id=1, source_target_pairs={{0,4},{1,5},{2,6},{3,7},{4,0},{5,1},{6,2},{7,3},{8,12},{9,13},{10,... | collective-permute-start | bytes 393224 | tf_op jit(solution)/shard_map/ppermute | solution.py:311
  50.8 9.5 %collective-permute-start.12 = (bf16[64,1024]{1,0:T(8,128)(2,1)S(1)}, bf16[64,1024]{1,0:T(8,128)(2,1)S(1)}, u32[]{:S(2)}, u32[]{:S(2)}) collective-permute-start(bf16[64,1024]{1,0:T(8,128)(2,1)S(1)} %get-tuple-element.46), channel_id=1, source_target_pairs={{0,2},{1,3},{2,0},{3,1},{4,6},{5,7},{6,4},{7,5},{8,10},{9,11},{10,... | collective-permute-start | bytes 393224 | tf_op jit(solution)/shard_map/ppermute | solution.py:311
  52.1 9.6 %collective-permute-start.13 = (bf16[64,1024]{1,0:T(8,128)(2,1)S(1)}, bf16[64,1024]{1,0:T(8,128)(2,1)S(1)}, u32[]{:S(2)}, u32[]{:S(2)}) collective-permute-start(bf16[64,1024]{1,0:T(8,128)(2,1)S(1)} %get-tuple-element.47), channel_id=1, source_target_pairs={{0,6},{1,7},{2,4},{3,5},{4,2},{5,3},{6,0},{7,1},{8,14},{9,15},{10,... | collective-permute-start | bytes 393224 | tf_op jit(solution)/shard_map/ppermute | solution.py:311
  57.3 5.9 %collective-permute-start.19 = (bf16[32,1024]{1,0:T(8,128)(2,1)S(1)}, bf16[32,1024]{1,0:T(8,128)(2,1)S(1)}, u32[]{:S(2)}, u32[]{:S(2)}) collective-permute-start(bf16[32,1024]{1,0:T(8,128)(2,1)S(1)} %get-tuple-element.56), channel_id=1, source_target_pairs={{0,16},{1,17},{2,18},{3,19},{4,20},{5,21},{6,22},{7,23},{8,24},{9,... | collective-permute-start | bytes 196616 | tf_op jit(solution)/shard_map/ppermute | solution.py:311
  58.1 6.6 %collective-permute-start.20 = (bf16[32,1024]{1,0:T(8,128)(2,1)S(1)}, bf16[32,1024]{1,0:T(8,128)(2,1)S(1)}, u32[]{:S(2)}, u32[]{:S(2)}) collective-permute-start(bf16[32,1024]{1,0:T(8,128)(2,1)S(1)} %get-tuple-element.57), channel_id=1, source_target_pairs={{0,24},{1,25},{2,26},{3,27},{4,28},{5,29},{6,30},{7,31},{8,16},{9,... | collective-permute-start | bytes 196616 | tf_op jit(solution)/shard_map/ppermute | solution.py:311
  61.8 4.3 %collective-permute-start.14 = (bf16[32,1024]{1,0:T(8,128)(2,1)S(1)}, bf16[32,1024]{1,0:T(8,128)(2,1)S(1)}, u32[]{:S(2)}, u32[]{:S(2)}) collective-permute-start(bf16[32,1024]{1,0:T(8,128)(2,1)S(1)} %get-tuple-element.49), channel_id=1, source_target_pairs={{0,8},{1,9},{2,10},{3,11},{4,12},{5,13},{6,14},{7,15},{8,0},{9,1},... | collective-permute-start | bytes 196616 | tf_op jit(solution)/shard_map/ppermute | solution.py:311

commit v10 on v9

--- a/solution.py
+++ b/solution.py
@@ -104,23 +104,29 @@
     rows[:, :width] = packed.astype(jnp.bfloat16)
 
 
-def join_kernel(order, *refs):
+def join_kernel(order, after, *refs):
     blocks, line, plain = refs[:-2], refs[-2], refs[-1]
     for place, block in zip(order, blocks):
         line[place * CAP:(place + 1) * CAP] = block[...]
         plain[place * CAP:(place + 1) * CAP] = block[:, :plain.shape[1]]
 
 
-def stage_kernel(line, weight, held, same, sems):
-    count = sems.shape[0]
-    height = weight.shape[0] // count
+def stage_kernel(blocks, after, weight, held, away, finished, sems):
+    rank = coordinates()[0]
+    width = weight.shape[0] // blocks
     copies = []
-    for place in range(count):
-        part = pl.ds(place * height, height)
-        copy = pltpu.make_async_copy(weight.at[part], held.at[part], sems.at[place])
-        copy.start()
-        copies.append(copy)
-    same[...] = line[...]
+    for block in list(range(1, blocks, 2)) + list(range(0, blocks, 2)):
+        start = pl.multiple_of((rank ^ block) * width, width)
+        targets = [held.at[pl.ds(start, width)]]
+        if block % 2:
+            targets.append(away.at[pl.ds(block // 2 * width, width)])
+        for target in targets:
+            copy = pltpu.make_async_copy(
+                weight.at[pl.ds(start, width)], target, sems.at[len(copies)]
+            )
+            copy.start()
+            copies.append(copy)
+    finished[...] = jnp.zeros_like(finished)
     for copy in copies:
         copy.wait()
 
@@ -199,60 +205,71 @@
     stats[...] = jnp.broadcast_to(line[None], stats.shape)
 
 
-def block_grads(blocks, rank, first, grad, weight, outs):
-    height = grad.shape[0] // 4
-    width = weight.shape[0] // blocks
-    for block in range(first, blocks, 2):
-        start = pl.multiple_of((rank ^ block) * width, width)
-        part = lax.dot_general(
-            grad,
-            weight[pl.ds(start, width), :],
-            (((1,), (1,)), ((), ())),
-            preferred_element_type=jnp.float32,
-        )
-        for quarter in range(4):
-            side, out = quarter // 2, outs[quarter % 2]
-            piece = part[quarter * height:(quarter + 1) * height]
-            out[block // 2 * 2 + side] = piece.astype(out.dtype)
-
-
-def grad_kernel(blocks, groups, info, logits, weight, stats, *refs):
-    away, (logit_grad, loss) = refs[:2], refs[2:]
-    rank, position, shard = coordinates()
-    height, columns = logits.shape
+def log_totals_kernel(groups, info, stats, columns, loss):
+    position = coordinates()[1]
+    height = info.shape[0]
     peaks, masses = stats[:, :, :height], stats[:, :, height:2 * height]
     peak = jnp.max(peaks, axis=0)
     mass = jnp.sum(masses * jnp.exp(peaks - peak[None]), axis=0)
     hit = jnp.sum(stats[:, :, 2 * height:], axis=0)
     log_total = jnp.broadcast_to(peak + jnp.log(mass), (8, height))
     log_total = reorder(log_total, position, groups)
-    log_total = jnp.transpose(jnp.concatenate([log_total] * 16, axis=0))[:, 0:1]
-    row_weight = info[:, 0:1]
-    loss[0, 0] = jnp.sum(row_weight * log_total) - hit[0, 0]
-    target = info[:, 1:2].astype(jnp.int32) - shard * columns
-    column = lax.broadcasted_iota(jnp.int32, logits.shape, 1)
-    probability = jnp.exp(logits[...] - log_total)
-    grad = (
-        grad_scale * row_weight * (probability - (column == target).astype(jnp.float32))
-    ).astype(jnp.bfloat16)
+    log_total = jnp.transpose(jnp.concatenate([log_total] * 16, axis=0))
+    loss[0, 0] = jnp.sum(info[:, 0:1] * log_total[:, 0:1]) - hit[0, 0]
+    columns[...] = log_total
+
+
+def grad_kernel(chunk, order, info, mine, theirs, weight, other_weight, table, *refs):
+    logit_grad, outs = refs[0], refs[1:]
+    rank, _, shard = coordinates()
+    height, columns = mine.shape
+    part = height // 4
+    quarters = [chunk, 2 + chunk]
+
+    def rows_of(ref):
+        return jnp.concatenate([ref[q * part:(q + 1) * part] for q in quarters], axis=0)
+
+    rows_info = rows_of(info)
+    log_total = rows_of(table)[:, 0:1]
+    row_weight, target = rows_info[:, 0:1], rows_info[:, 1:2].astype(jnp.int32)
+
+    def grad_of(logits, shard):
+        column = lax.broadcasted_iota(jnp.int32, (2 * part, columns), 1) + shard * columns
+        probability = jnp.exp(rows_of(logits) - log_total)
+        return (
+            grad_scale * row_weight * (probability - (column == target).astype(jnp.float32))
+        ).astype(jnp.bfloat16)
+
+    grad = grad_of(mine, shard)
     logit_grad[...] = grad
-    block_grads(blocks, rank, 1, grad, weight, away)
-
-
-def kept_kernel(blocks, logit_grad, weight, *kept):
-    block_grads(blocks, coordinates()[0], 0, logit_grad[...], weight, kept)
-
-
-def weight_kernel(blocks, after, logit_grad, *refs):
+    grads = (grad, grad_of(theirs, shard ^ 1))
+    width = outs[0].shape[1]
+    for x in reversed(range(len(outs) // 2)):
+        start = pl.multiple_of((rank ^ 2 * x) * width, width)
+        weights = (weight[pl.ds(start, width), :], other_weight[x * width:(x + 1) * width, :])
+        total = sum(
+            lax.dot_general(g, w, (((1,), (1,)), ((), ())), preferred_element_type=jnp.float32)
+            for g, w in zip(grads, weights)
+        )
+        for y in range(2):
+            out = outs[order.index(2 * x + y)]
+            out[...] = total[y * part:(y + 1) * part].astype(out.dtype)
+
+
+def weight_kernel(blocks, after, near_grad, far_grad, *refs):
     pieces, (out, finished, done, sems) = refs[:-4], refs[-4:]
     rank = coordinates()[0]
     finished[...] = jnp.zeros_like(finished)
+    part = near_grad.shape[0] // 2
+    logit_grad = jnp.concatenate(
+        [ref[y * part:(y + 1) * part] for y in range(2) for ref in (near_grad, far_grad)], axis=0
+    )
     width = done.shape[0] // blocks
     copies = []
     for block in range(blocks):
         done[block * width:(block + 1) * width] = lax.dot_general(
             all_rows(pieces, block, width),
-            logit_grad[...],
+            logit_grad,
             (((0,), (0,)), ((), ())),
             preferred_element_type=jnp.float32,
         ).astype(jnp.bfloat16)
@@ -264,12 +281,6 @@
         copies.append(copy)
     for copy in copies:
         copy.wait()
-
-
-def pair_kernel(order, kept, beside, *outs):
-    for place, out in zip(order, outs):
-        total = kept[place] + beside[place].astype(jnp.float32)
-        out[...] = total.astype(out.dtype)
 
 
 def corner_kernel(count, after, kept, *refs):
@@ -331,24 +342,29 @@
 
     line_order = [0, 1] + list(range(zs - 1, 1, -1))
     blocks = [send(packed, z=z) if z else packed for z in line_order]
+    held, away, finished = call(
+        functools.partial(stage_kernel, ranks),
+        (blocks[1], in_hbm(weight)),
+        [ANY, HBM],
+        (
+            shape((depth, columns), bf16),
+            shape((depth // 2, columns), bf16),
+            shape((8, 128), f32),
+        ),
+        (VMEM,) * 3,
+        [pltpu.SemaphoreType.DMA((ranks + xs,))],
+    )
+    other_held = send(away, core=1)
     line_rows = zs * CAP
     line, line_plain = call(
         functools.partial(join_kernel, line_order),
-        blocks,
-        [VMEM] * zs,
+        (finished, *blocks),
+        [ANY] + [VMEM] * zs,
         (shape((line_rows, width + IDS), bf16), shape((line_rows, width), bf16)),
         (VMEM, VMEM),
     )
     pieces = {(2 * x, y): send(line_plain if x else line, y=y, x=x) for y, x in square}
-    held, same = call(
-        stage_kernel,
-        (line, in_hbm(weight)),
-        [VMEM, HBM],
-        (shape((depth, columns), bf16), shape(line.shape, bf16)),
-        (VMEM, VMEM),
-        [pltpu.SemaphoreType.DMA((4,))],
-    )
-    pieces[0, 0] = same
+    pieces[0, 0] = line
     for b, y in list(pieces):
         pieces[b + 1, y] = send(pieces[b, y], core=1)
     rows = [pieces[b, y] for b in range(ranks) for y in range(2)]
@@ -381,50 +397,37 @@
         (VMEM, VMEM),
         flops=flops // 2,
     )
+    other_logits = send(logits, core=1)
     stats = lax.all_to_all(stats, AXES, 0, 0)
+    table, loss = call(
+        functools.partial(log_totals_kernel, dps),
+        (info, stats),
+        [VMEM] * 2,
+        (shape((total_rows, 128), f32), shape((1, 1), f32)),
+        (VMEM, SMEM),
+    )
 
     rows_part = total_rows // 4
-    whole = (ranks, rows_part, width)
-    *away, logit_grad, loss = call(
-        functools.partial(grad_kernel, ranks, dps),
-        (info, logits, held, stats),
-        [VMEM] * 4,
-        (shape(whole, bf16),) * 2 + (shape((total_rows, columns), bf16), shape((1, 1), f32)),
-        (VMEM,) * 3 + (SMEM,),
-        flops=flops // 2,
-    )
-    kept = call(
-        functools.partial(kept_kernel, ranks),
-        (logit_grad, held),
-        [VMEM] * 2,
-        (shape(whole, f32),) * 2,
-        (VMEM,) * 2,
-        flops=flops // 2,
-    )
-
-    ends = [None] * zs
-    besides = [None, None]
-    order = sorted(range(1, ranks), key=lambda place: (place % 2 + (place > 1), place))
+    order = sorted(range(1, ranks), key=lambda place: (place % 2 + (place > 1), place)) + [0]
+    ends, sums, grads = [None] * zs, [None, None], [None, None]
     for chunk in (1, 0):
-        besides[chunk] = send(away[chunk], core=1)
-    sums = [None, None]
-    for chunk in (1, 0):
-        part = shape((rows_part, width), bf16)
-        *going, corner = call(
-            functools.partial(pair_kernel, order + [0]),
-            (kept[chunk], besides[chunk]),
-            [VMEM, VMEM],
-            (part,) * (ranks - 1) + (shape((rows_part, width), f32),),
-            (VMEM,) * ranks,
-        )
-        arrived = []
-        for place, value in zip(order, going):
-            arrived.append(send(value, y=place % 2, x=place // 2))
-        sums[chunk] = (corner, *arrived)
+        grads[chunk], *going = call(
+            functools.partial(grad_kernel, chunk, order),
+            (info, logits, other_logits, held, other_held, table),
+            [VMEM] * 6,
+            (shape((total_rows // 2, columns), bf16),)
+            + (shape((rows_part, width), bf16),) * (ranks - 1)
+            + (shape((rows_part, width), f32),),
+            (VMEM,) * (ranks + 1),
+            flops=flops // 2,
+        )
+        sums[chunk] = [going[-1]]
+        for place, value in zip(order, going[:-1]):
+            sums[chunk].append(send(value, y=place % 2, x=place // 2))
     weight_grad, finished = call(
         functools.partial(weight_kernel, ranks),
-        (sums[0][0], logit_grad, *rows),
-        [ANY] + [VMEM] * (1 + len(rows)),
+        (sums[0][0], *grads, *rows),
+        [ANY] + [VMEM] * (2 + len(rows)),
         (shape((depth, columns), bf16), shape((8, 128), f32)),
         (HBM, VMEM),
         [pltpu.VMEM((depth, columns), bf16), pltpu.SemaphoreType.DMA((ranks,))],
@@ -434,7 +437,7 @@
         near = chunk * zs // 2
         parts_z = call(
             functools.partial(corner_kernel, ranks - 1),
-            (logit_grad if chunk else finished, *sums[chunk]),
+            (table if chunk else finished, *sums[chunk]),
             [ANY] + [VMEM] * ranks,
             tuple(shape((CAP, width), bf16 if near + z else f32) for z in range(zs // 2)),
             (VMEM,) * (zs // 2),

time: 67.2 us -> 74.9 us (1.11)
  waiting for transfers between devices: 20.3 us -> 23.1 us
  Pallas kernels: 11.4 us -> 14 us
  starting transfers between devices: 20.7 us -> 22.2 us
  blocking collectives: 13.9 us -> 14.7 us
    ppermute x21, waiting for transfers between devices: 20.3 us -> 23.1 us  [send(): return lax.ppermute(value, AXES, pairs)]
    pallas_call x14 -> x13, Pallas kernels: 11.4 us -> 14 us  [call(): pl.pallas_call(kernel, out_shape=out_shape, in_specs=in_specs, out_specs=...]
    ppermute x21, starting transfers between devices: 20.7 us -> 22.2 us  [send(): return lax.ppermute(value, AXES, pairs)]
    all_to_all x1, blocking collectives: 13.9 us -> 14.7 us  [body(): stats = lax.all_to_all(stats, AXES, 0, 0)]
  transfers between devices with their start and end apart: 21 -> 21, of which waited for: 13 -> 9; matrix products, arithmetic and copies ran while one was open for 0% -> 0% of each run, Pallas kernels for 10% -> 10%
where the time goes in v10:
time: 74.9 us; the launch traced here: 74.7 us
  waiting for transfers between devices  23.1 us (31%)
  starting transfers between devices  22.2 us (30%)
  blocking collectives  14.7 us (20%)
  Pallas kernels  14 us (19%)
  between operations  0.8 us (1%)
    ppermute x21, waiting for transfers between devices, send(): return lax.ppermute(value, AXES, pairs)  23.1 us
    ppermute x21, starting transfers between devices, send(): return lax.ppermute(value, AXES, pairs)  22.2 us
    all_to_all x1, blocking collectives, body(): stats = lax.all_to_all(stats, AXES, 0, 0)  14.7 us
    pallas_call x13, Pallas kernels, call(): pl.pallas_call(kernel, out_shape=out_shape, in_specs=in_specs, out_specs=...  14 us
  transfers between devices with their start and end apart: 21, of which 9 were waited for; matrix products, arithmetic and copies ran while one was open for 0% of the time, Pallas kernels for 10%

profile of v10, /device:TPU:0, one launch (start us, length us, event | category | flops | bytes accessed | tf_op | source)
XLA Modules:
  0.0 74.7 jit_solution(13096501220336367376)
XLA Ops:
  0.6 1.2 %shard_map.85 = (bf16[32,1152]{1,0:T(8,128)(2,1)S(1)}, bf16[32,128]{1,0:T(8,128)(2,1)S(1)}) custom-call(bf16[128,1024]{1,0:T(8,128)(2,1)} %hidden_hbm.1, s32[1,128]{1,0:T(1,128)} %bitcast.6, s32[1,128]{1,0:T(1,128)} %bitcast.7, s32[1,128]{1,0:T(1,128)} %bitcast.8), custom_call_target="tpu_custom_call" | custom-call | bytes 345600 | tf_op jit(solution)/shard_map/pallas_call | solution.py:32
  1.9 3.1 %collective-permute-start = (bf16[32,1152]{1,0:T(8,128)(2,1)S(1)}, bf16[32,1152]{1,0:T(8,128)(2,1)S(1)}, u32[]{:S(2)}, u32[]{:S(2)}) collective-permute-start(bf16[32,1152]{1,0:T(8,128)(2,1)S(1)} %get-tuple-element.30.refs_0_), channel_id=1, source_target_pairs={{0,8},{1,9},{2,10},{3,11},{4,12},{5,13},{6,14},{7,15},{8,0},{9,1},... | collective-permute-start | bytes 221192 | tf_op jit(solution)/shard_map/ppermute | solution.py:322
  5.0 2.3 %collective-permute-done.after.refs_1_ = bf16[32,1152]{1,0:T(8,128)(2,1)S(1)} collective-permute-done((bf16[32,1152]{1,0:T(8,128)(2,1)S(1)}, bf16[32,1152]{1,0:T(8,128)(2,1)S(1)}, u32[]{:S(2)}, u32[]{:S(2)}) %collective-permute-start) | collective-permute-done | bytes 73760 | tf_op jit(solution)/shard_map/ppermute | solution.py:322
  7.3 2.9 %shard_map.86 = (bf16[4096,512]{1,0:T(8,128)(2,1)S(1)}, bf16[2048,512]{1,0:T(8,128)(2,1)S(1)}, f32[8,128]{1,0:T(8,128)S(1)}) custom-call(bf16[32,1152]{1,0:T(8,128)(2,1)S(1)} %collective-permute-done.after.refs_1_, bf16[4096,512]{1,0:T(8,128)(2,1)} %weight.1), custom_call_target="tpu_custom_call" | custom-call | bytes 10563584 | tf_op jit(solution)/shard_map/pallas_call | solution.py:32
  10.2 3.1 %collective-permute-start.2 = (bf16[32,1152]{1,0:T(8,128)(2,1)S(1)}, bf16[32,1152]{1,0:T(8,128)(2,1)S(1)}, u32[]{:S(2)}, u32[]{:S(2)}) collective-permute-start(bf16[32,1152]{1,0:T(8,128)(2,1)S(1)} %get-tuple-element.30.refs_0_), channel_id=1, source_target_pairs={{0,16},{1,17},{2,18},{3,19},{4,20},{5,21},{6,22},{7,23},{8,24},{9,... | collective-permute-start | bytes 221192 | tf_op jit(solution)/shard_map/ppermute | solution.py:322
  13.3 1.3 %collective-permute-start.1 = (bf16[32,1152]{1,0:T(8,128)(2,1)S(1)}, bf16[32,1152]{1,0:T(8,128)(2,1)S(1)}, u32[]{:S(2)}, u32[]{:S(2)}) collective-permute-start(bf16[32,1152]{1,0:T(8,128)(2,1)S(1)} %get-tuple-element.30.refs_0_), channel_id=1, source_target_pairs={{0,24},{1,25},{2,26},{3,27},{4,28},{5,29},{6,30},{7,31},{8,16},{9,... | collective-permute-start | bytes 221192 | tf_op jit(solution)/shard_map/ppermute | solution.py:322
  14.7 4.9 %collective-permute-done.2.refs_3_ = bf16[32,1152]{1,0:T(8,128)(2,1)S(1)} collective-permute-done((bf16[32,1152]{1,0:T(8,128)(2,1)S(1)}, bf16[32,1152]{1,0:T(8,128)(2,1)S(1)}, u32[]{:S(2)}, u32[]{:S(2)}) %collective-permute-start.2) | collective-permute-done | bytes 73760 | tf_op jit(solution)/shard_map/ppermute | solution.py:322
  19.7 1.8 %collective-permute-start.3 = (bf16[128,1152]{1,0:T(8,128)(2,1)S(1)}, bf16[128,1152]{1,0:T(8,128)(2,1)S(1)}, u32[]{:S(2)}, u32[]{:S(2)}) collective-permute-start(bf16[128,1152]{1,0:T(8,128)(2,1)S(1)} %get-tuple-element.32.refs_0_), channel_id=1, source_target_pairs={{0,4},{1,5},{2,6},{3,7},{4,0},{5,1},{6,2},{7,3},{8,12},{9,13},{10,... | collective-permute-start | bytes 884744 | tf_op jit(solution)/shard_map/ppermute | solution.py:322
  21.5 1.4 %collective-permute-start.5 = (bf16[128,1024]{1,0:T(8,128)(2,1)S(1)}, bf16[128,1024]{1,0:T(8,128)(2,1)S(1)}, u32[]{:S(2)}, u32[]{:S(2)}) collective-permute-start(bf16[128,1024]{1,0:T(8,128)(2,1)S(1)} %get-tuple-element.34), channel_id=1, source_target_pairs={{0,6},{1,7},{2,4},{3,5},{4,2},{5,3},{6,0},{7,1},{8,14},{9,15},{10,... | collective-permute-start | bytes 786440 | tf_op jit(solution)/shard_map/ppermute | solution.py:322
  23.2 10.0 %collective-permute-done.3.refs_1_ = bf16[128,1152]{1,0:T(8,128)(2,1)S(1)} collective-permute-done((bf16[128,1152]{1,0:T(8,128)(2,1)S(1)}, bf16[128,1152]{1,0:T(8,128)(2,1)S(1)}, u32[]{:S(2)}, u32[]{:S(2)}) %collective-permute-start.3) | collective-permute-done | bytes 294944 | tf_op jit(solution)/shard_map/ppermute | solution.py:322
  33.2 0.5 collective-permute-start.9
  33.8 0.4 shard_map.88.info
  34.2 0.7 shard_map.89.partial
  35.6 1.2 %shard_map.90 = (f32[256,512]{1,0:T(8,128)S(1)}, f32[32,1,640]{2,1,0:T(1,128)S(1)}) custom-call(f32[256,128]{1,0:T(8,128)S(1)} %shard_map.88.info, f32[256,512]{1,0:T(8,128)S(1)} %shard_map.89.partial, bf16[4096,512]{1,0:T(8,128)(2,1)S(1)} %get-tuple-element.33.weight, bf16[128,1152]{1,0:T(8,128)(2,1)S(1)} %collective-permute-done.6.refs_0_.refs_2_, ...), custom_call_target="tpu_custom_call" | custom-call | flops 536870912 | bytes 6569984 | tf_op jit(solution)/shard_map/pallas_call | solution.py:32
  36.9 14.7 %all_to_all.5.stats = f32[32,1,640]{2,1,0:T(1,128)S(1)} all-to-all(f32[32,1,640]{2,1,0:T(1,128)S(1)} %get-tuple-element.35), channel_id=1, replica_groups=mesh['dp'=8,'vocab'=4] {'dp','vocab'}, dimensions={0} | all-to-all | bytes 163840 | tf_op jit(solution)/shard_map/all_to_all | solution.py:401
  51.7 1.0 %shard_map.91 = (f32[256,128]{1,0:T(8,128)S(1)}, f32[1,1]{1,0:T(1,128)}) custom-call(f32[256,128]{1,0:T(8,128)S(1)} %shard_map.88.info, f32[32,1,640]{2,1,0:T(1,128)S(1)} %all_to_all.5.stats), custom_call_target="tpu_custom_call" | custom-call | bytes 344068 | tf_op jit(solution)/shard_map/pallas_call | solution.py:32
  52.6 1.5 %shard_map.93 = (bf16[128,512]{1,0:T(8,128)(2,1)S(1)}, bf16[64,1024]{1,0:T(8,128)(2,1)S(1)}, bf16[64,1024]{1,0:T(8,128)(2,1)S(1)}, bf16[64,1024]{1,0:T(8,128)(2,1)S(1)}, f32[64,1024]{1,0:T(8,128)S(1)}) custom-call(f32[256,128]{1,0:T(8,128)S(1)} %shard_map.88.info, f32[256,512]{1,0:T(8,128)S(1)} %get-tuple-element.38.mine, ...), custom_call_target="tpu_custom_call" | custom-call | flops 536870912 | bytes 8388608 | tf_op jit(solution)/shard_map/pallas_call | solution.py:32
  54.2 0.7 collective-permute-start.16
  54.9 0.7 collective-permute-start.17
  55.6 2.2 %collective-permute-start.18 = (bf16[64,1024]{1,0:T(8,128)(2,1)S(1)}, bf16[64,1024]{1,0:T(8,128)(2,1)S(1)}, u32[]{:S(2)}, u32[]{:S(2)}) collective-permute-start(bf16[64,1024]{1,0:T(8,128)(2,1)S(1)} %get-tuple-element.53), channel_id=1, source_target_pairs={{0,6},{1,7},{2,4},{3,5},{4,2},{5,3},{6,0},{7,1},{8,14},{9,15},{10,... | collective-permute-start | bytes 393224 | tf_op jit(solution)/shard_map/ppermute | solution.py:322
  57.7 1.5 %shard_map.92 = (bf16[128,512]{1,0:T(8,128)(2,1)S(1)}, bf16[64,1024]{1,0:T(8,128)(2,1)S(1)}, bf16[64,1024]{1,0:T(8,128)(2,1)S(1)}, bf16[64,1024]{1,0:T(8,128)(2,1)S(1)}, f32[64,1024]{1,0:T(8,128)S(1)}) custom-call(f32[256,128]{1,0:T(8,128)S(1)} %shard_map.88.info, f32[256,512]{1,0:T(8,128)S(1)} %get-tuple-element.38.mine, ...), custom_call_target="tpu_custom_call" | custom-call | flops 536870912 | bytes 8388608 | tf_op jit(solution)/shard_map/pallas_call | solution.py:32
  59.3 0.7 collective-permute-start.12
  60.0 0.7 collective-permute-start.13
  60.7 2.2 %collective-permute-start.14 = (bf16[64,1024]{1,0:T(8,128)(2,1)S(1)}, bf16[64,1024]{1,0:T(8,128)(2,1)S(1)}, u32[]{:S(2)}, u32[]{:S(2)}) collective-permute-start(bf16[64,1024]{1,0:T(8,128)(2,1)S(1)} %get-tuple-element.47), channel_id=1, source_target_pairs={{0,6},{1,7},{2,4},{3,5},{4,2},{5,3},{6,0},{7,1},{8,14},{9,15},{10,... | collective-permute-start | bytes 393224 | tf_op jit(solution)/shard_map/ppermute | solution.py:322
  62.8 2.5 %shard_map.94 = (bf16[4096,512]{1,0:T(8,128)(2,1)}, f32[8,128]{1,0:T(8,128)S(1)}) custom-call(f32[64,1024]{1,0:T(8,128)S(1)} %get-tuple-element.41.after.kept, bf16[128,512]{1,0:T(8,128)(2,1)S(1)} %get-tuple-element.42.near_grad, bf16[128,512]{1,0:T(8,128)(2,1)S(1)} %get-tuple-element.43.far_grad, bf16[128,1152]{1,0:T(8,128)(2,1)S(1)} %get-tuple-element.32.refs_0_, ...), custom_call_target="tpu_custom_call" | custom-call | flops 1073741824 | bytes 6950912 | tf_op jit(solution)/shard_map/pallas_call | solution.py:32
  65.4 0.8 %collective-permute-start.19 = (bf16[32,1024]{1,0:T(8,128)(2,1)S(1)}, bf16[32,1024]{1,0:T(8,128)(2,1)S(1)}, u32[]{:S(2)}, u32[]{:S(2)}) collective-permute-start(bf16[32,1024]{1,0:T(8,128)(2,1)S(1)} %get-tuple-element.54), channel_id=1, source_target_pairs={{0,16},{1,17},{2,18},{3,19},{4,20},{5,21},{6,22},{7,23},{8,24},{9,... | collective-permute-start | bytes 196616 | tf_op jit(solution)/shard_map/ppermute | solution.py:322
  66.2 2.3 %collective-permute-start.20 = (bf16[32,1024]{1,0:T(8,128)(2,1)S(1)}, bf16[32,1024]{1,0:T(8,128)(2,1)S(1)}, u32[]{:S(2)}, u32[]{:S(2)}) collective-permute-start(bf16[32,1024]{1,0:T(8,128)(2,1)S(1)} %get-tuple-element.55), channel_id=1, source_target_pairs={{0,24},{1,25},{2,26},{3,27},{4,28},{5,29},{6,30},{7,31},{8,16},{9,... | collective-permute-start | bytes 196616 | tf_op jit(solution)/shard_map/ppermute | solution.py:322
  68.5 0.9 %collective-permute-done.14.refs_2_ = bf16[64,1024]{1,0:T(8,128)(2,1)S(1)} collective-permute-done((bf16[64,1024]{1,0:T(8,128)(2,1)S(1)}, bf16[64,1024]{1,0:T(8,128)(2,1)S(1)}, u32[]{:S(2)}, u32[]{:S(2)}) %collective-permute-start.14) | collective-permute-done | bytes 131104 | tf_op jit(solution)/shard_map/ppermute | solution.py:322
  69.5 1.9 %collective-permute-done.19.refs_2_ = bf16[32,1024]{1,0:T(8,128)(2,1)S(1)} collective-permute-done((bf16[32,1024]{1,0:T(8,128)(2,1)S(1)}, bf16[32,1024]{1,0:T(8,128)(2,1)S(1)}, u32[]{:S(2)}, u32[]{:S(2)}) %collective-permute-start.19) | collective-permute-done | bytes 65568 | tf_op jit(solution)/shard_map/ppermute | solution.py:322
  71.5 1.0 %collective-permute-done.20.refs_3_ = bf16[32,1024]{1,0:T(8,128)(2,1)S(1)} collective-permute-done((bf16[32,1024]{1,0:T(8,128)(2,1)S(1)}, bf16[32,1024]{1,0:T(8,128)(2,1)S(1)}, u32[]{:S(2)}, u32[]{:S(2)}) %collective-permute-start.20) | collective-permute-done | bytes 65568 | tf_op jit(solution)/shard_map/ppermute | solution.py:322
  72.4 1.3 %collective-permute-done.15.refs_1_ = bf16[32,1024]{1,0:T(8,128)(2,1)S(1)} collective-permute-done((bf16[32,1024]{1,0:T(8,128)(2,1)S(1)}, bf16[32,1024]{1,0:T(8,128)(2,1)S(1)}, u32[]{:S(2)}, u32[]{:S(2)}) %collective-permute-start.15) | collective-permute-done | bytes 65568 | tf_op jit(solution)/shard_map/ppermute | solution.py:322
  73.8 1.0 %shard_map.97 = bf16[128,1024]{1,0:T(8,128)(2,1)} custom-call(bf16[32,128]{1,0:T(8,128)(2,1)S(1)} %get-tuple-element.37.chosen, f32[32,1024]{1,0:T(8,128)S(1)} %get-tuple-element.48.refs_0_, bf16[32,1024]{1,0:T(8,128)(2,1)S(1)} %collective-permute-done.15.refs_1_, bf16[32,1024]{1,0:T(8,128)(2,1)S(1)} %collective-permute-done.19.refs_2_, ...), custom_call_target="tpu_custom_call" | custom-call | bytes 598016 | tf_op jit(solution)/shard_map/pallas_call | solution.py:32
  (26 shorter events, 1.5 us)
Async XLA Ops:
  0.6 33.2 %copy-start = (f32[32]{0:T(128)S(1)}, f32[32]{0:T(128)}, u32[]{:S(2)}) copy-start(f32[32]{0:T(128)} %param.11) | copy-start | bytes 388
  1.9 5.4 %collective-permute-start = (bf16[32,1152]{1,0:T(8,128)(2,1)S(1)}, bf16[32,1152]{1,0:T(8,128)(2,1)S(1)}, u32[]{:S(2)}, u32[]{:S(2)}) collective-permute-start(bf16[32,1152]{1,0:T(8,128)(2,1)S(1)} %get-tuple-element.30.refs_0_), channel_id=1, source_target_pairs={{0,8},{1,9},{2,10},{3,11},{4,12},{5,13},{6,14},{7,15},{8,0},{9,1},... | collective-permute-start | bytes 221192 | tf_op jit(solution)/shard_map/ppermute | solution.py:322
  10.2 42.5 %collective-permute-start.11 = (bf16[2048,512]{1,0:T(8,128)(2,1)S(1)}, bf16[2048,512]{1,0:T(8,128)(2,1)S(1)}, u32[]{:S(2)}, u32[]{:S(2)}) collective-permute-start(bf16[2048,512]{1,0:T(8,128)(2,1)S(1)} %get-tuple-element.39), channel_id=1, source_target_pairs={{0,1},{1,0},{2,3},{3,2},{4,5},{5,4},{6,7},{7,6},{8,9},{9,8},{10,11... | collective-permute-start | bytes 6291464 | tf_op jit(solution)/shard_map/ppermute | solution.py:322
  10.2 9.4 %collective-permute-start.2 = (bf16[32,1152]{1,0:T(8,128)(2,1)S(1)}, bf16[32,1152]{1,0:T(8,128)(2,1)S(1)}, u32[]{:S(2)}, u32[]{:S(2)}) collective-permute-start(bf16[32,1152]{1,0:T(8,128)(2,1)S(1)} %get-tuple-element.30.refs_0_), channel_id=1, source_target_pairs={{0,16},{1,17},{2,18},{3,19},{4,20},{5,21},{6,22},{7,23},{8,24},{9,... | collective-permute-start | bytes 221192 | tf_op jit(solution)/shard_map/ppermute | solution.py:322
  13.3 6.3 %collective-permute-start.1 = (bf16[32,1152]{1,0:T(8,128)(2,1)S(1)}, bf16[32,1152]{1,0:T(8,128)(2,1)S(1)}, u32[]{:S(2)}, u32[]{:S(2)}) collective-permute-start(bf16[32,1152]{1,0:T(8,128)(2,1)S(1)} %get-tuple-element.30.refs_0_), channel_id=1, source_target_pairs={{0,24},{1,25},{2,26},{3,27},{4,28},{5,29},{6,30},{7,31},{8,16},{9,... | collective-permute-start | bytes 221192 | tf_op jit(solution)/shard_map/ppermute | solution.py:322
  19.7 13.6 %collective-permute-start.3 = (bf16[128,1152]{1,0:T(8,128)(2,1)S(1)}, bf16[128,1152]{1,0:T(8,128)(2,1)S(1)}, u32[]{:S(2)}, u32[]{:S(2)}) collective-permute-start(bf16[128,1152]{1,0:T(8,128)(2,1)S(1)} %get-tuple-element.32.refs_0_), channel_id=1, source_target_pairs={{0,4},{1,5},{2,6},{3,7},{4,0},{5,1},{6,2},{7,3},{8,12},{9,13},{10,... | collective-permute-start | bytes 884744 | tf_op jit(solution)/shard_map/ppermute | solution.py:322
  21.5 11.7 %collective-permute-start.5 = (bf16[128,1024]{1,0:T(8,128)(2,1)S(1)}, bf16[128,1024]{1,0:T(8,128)(2,1)S(1)}, u32[]{:S(2)}, u32[]{:S(2)}) collective-permute-start(bf16[128,1024]{1,0:T(8,128)(2,1)S(1)} %get-tuple-element.34), channel_id=1, source_target_pairs={{0,6},{1,7},{2,4},{3,5},{4,2},{5,3},{6,0},{7,1},{8,14},{9,15},{10,... | collective-permute-start | bytes 786440 | tf_op jit(solution)/shard_map/ppermute | solution.py:322
  22.9 10.8 %collective-permute-start.4 = (bf16[128,1024]{1,0:T(8,128)(2,1)S(1)}, bf16[128,1024]{1,0:T(8,128)(2,1)S(1)}, u32[]{:S(2)}, u32[]{:S(2)}) collective-permute-start(bf16[128,1024]{1,0:T(8,128)(2,1)S(1)} %get-tuple-element.34), channel_id=1, source_target_pairs={{0,2},{1,3},{2,0},{3,1},{4,6},{5,7},{6,4},{7,5},{8,10},{9,11},{10,... | collective-permute-start | bytes 786440 | tf_op jit(solution)/shard_map/ppermute | solution.py:322
  23.2 11.7 %collective-permute-start.6 = (bf16[128,1152]{1,0:T(8,128)(2,1)S(1)}, bf16[128,1152]{1,0:T(8,128)(2,1)S(1)}, u32[]{:S(2)}, u32[]{:S(2)}) collective-permute-start(bf16[128,1152]{1,0:T(8,128)(2,1)S(1)} %get-tuple-element.32.refs_0_), channel_id=1, source_target_pairs={{0,1},{1,0},{2,3},{3,2},{4,5},{5,4},{6,7},{7,6},{8,9},{9,8},{10,11... | collective-permute-start | bytes 884744 | tf_op jit(solution)/shard_map/ppermute | solution.py:322
  33.2 2.3 %collective-permute-start.7 = (bf16[128,1152]{1,0:T(8,128)(2,1)S(1)}, bf16[128,1152]{1,0:T(8,128)(2,1)S(1)}, u32[]{:S(2)}, u32[]{:S(2)}) collective-permute-start(bf16[128,1152]{1,0:T(8,128)(2,1)S(1)} %collective-permute-done.3.refs_1_), channel_id=1, source_target_pairs={{0,1},{1,0},{2,3},{3,2},{4,5},{5,4},{6,7},{7,6},{8,9},{9,8},{10,11... | collective-permute-start | bytes 884744 | tf_op jit(solution)/shard_map/ppermute | solution.py:322
  33.2 2.0 %collective-permute-start.9 = (bf16[128,1024]{1,0:T(8,128)(2,1)S(1)}, bf16[128,1024]{1,0:T(8,128)(2,1)S(1)}, u32[]{:S(2)}, u32[]{:S(2)}) collective-permute-start(bf16[128,1024]{1,0:T(8,128)(2,1)S(1)} %collective-permute-done.5.refs_3_.refs_5_), channel_id=1, source_target_pairs={{0,1},{1,0},{2,3},{3,2},{4,5},{5,4},{6,7},{7,6},{8,9},{9,8},{10,11... | collective-permute-start | bytes 786440 | tf_op jit(solution)/shard_map/ppermute | solution.py:322
  33.8 1.8 %collective-permute-start.8 = (bf16[128,1024]{1,0:T(8,128)(2,1)S(1)}, bf16[128,1024]{1,0:T(8,128)(2,1)S(1)}, u32[]{:S(2)}, u32[]{:S(2)}) collective-permute-start(bf16[128,1024]{1,0:T(8,128)(2,1)S(1)} %collective-permute-done.4.refs_2_.refs_4_), channel_id=1, source_target_pairs={{0,1},{1,0},{2,3},{3,2},{4,5},{5,4},{6,7},{7,6},{8,9},{9,8},{10,11... | collective-permute-start | bytes 786440 | tf_op jit(solution)/shard_map/ppermute | solution.py:322
  36.7 15.9 %collective-permute-start.10 = (f32[256,512]{1,0:T(8,128)S(1)}, f32[256,512]{1,0:T(8,128)S(1)}, u32[]{:S(2)}, u32[]{:S(2)}) collective-permute-start(f32[256,512]{1,0:T(8,128)S(1)} %get-tuple-element.38.mine), channel_id=1, source_target_pairs={{0,1},{1,0},{2,3},{3,2},{4,5},{5,4},{6,7},{7,6},{8,9},{9,8},{10,11... | collective-permute-start | bytes 1572872 | tf_op jit(solution)/shard_map/ppermute | solution.py:322
  54.2 6.5 %collective-permute-start.16 = (bf16[64,1024]{1,0:T(8,128)(2,1)S(1)}, bf16[64,1024]{1,0:T(8,128)(2,1)S(1)}, u32[]{:S(2)}, u32[]{:S(2)}) collective-permute-start(bf16[64,1024]{1,0:T(8,128)(2,1)S(1)} %get-tuple-element.51), channel_id=1, source_target_pairs={{0,4},{1,5},{2,6},{3,7},{4,0},{5,1},{6,2},{7,3},{8,12},{9,13},{10,... | collective-permute-start | bytes 393224 | tf_op jit(solution)/shard_map/ppermute | solution.py:322
  54.9 10.5 %collective-permute-start.17 = (bf16[64,1024]{1,0:T(8,128)(2,1)S(1)}, bf16[64,1024]{1,0:T(8,128)(2,1)S(1)}, u32[]{:S(2)}, u32[]{:S(2)}) collective-permute-start(bf16[64,1024]{1,0:T(8,128)(2,1)S(1)} %get-tuple-element.52), channel_id=1, source_target_pairs={{0,2},{1,3},{2,0},{3,1},{4,6},{5,7},{6,4},{7,5},{8,10},{9,11},{10,... | collective-permute-start | bytes 393224 | tf_op jit(solution)/shard_map/ppermute | solution.py:322
  55.6 9.8 %collective-permute-start.18 = (bf16[64,1024]{1,0:T(8,128)(2,1)S(1)}, bf16[64,1024]{1,0:T(8,128)(2,1)S(1)}, u32[]{:S(2)}, u32[]{:S(2)}) collective-permute-start(bf16[64,1024]{1,0:T(8,128)(2,1)S(1)} %get-tuple-element.53), channel_id=1, source_target_pairs={{0,6},{1,7},{2,4},{3,5},{4,2},{5,3},{6,0},{7,1},{8,14},{9,15},{10,... | collective-permute-start | bytes 393224 | tf_op jit(solution)/shard_map/ppermute | solution.py:322
  59.3 9.2 %collective-permute-start.12 = (bf16[64,1024]{1,0:T(8,128)(2,1)S(1)}, bf16[64,1024]{1,0:T(8,128)(2,1)S(1)}, u32[]{:S(2)}, u32[]{:S(2)}) collective-permute-start(bf16[64,1024]{1,0:T(8,128)(2,1)S(1)} %get-tuple-element.45), channel_id=1, source_target_pairs={{0,4},{1,5},{2,6},{3,7},{4,0},{5,1},{6,2},{7,3},{8,12},{9,13},{10,... | collective-permute-start | bytes 393224 | tf_op jit(solution)/shard_map/ppermute | solution.py:322
  60.0 8.5 %collective-permute-start.13 = (bf16[64,1024]{1,0:T(8,128)(2,1)S(1)}, bf16[64,1024]{1,0:T(8,128)(2,1)S(1)}, u32[]{:S(2)}, u32[]{:S(2)}) collective-permute-start(bf16[64,1024]{1,0:T(8,128)(2,1)S(1)} %get-tuple-element.46), channel_id=1, source_target_pairs={{0,2},{1,3},{2,0},{3,1},{4,6},{5,7},{6,4},{7,5},{8,10},{9,11},{10,... | collective-permute-start | bytes 393224 | tf_op jit(solution)/shard_map/ppermute | solution.py:322
  60.7 8.7 %collective-permute-start.14 = (bf16[64,1024]{1,0:T(8,128)(2,1)S(1)}, bf16[64,1024]{1,0:T(8,128)(2,1)S(1)}, u32[]{:S(2)}, u32[]{:S(2)}) collective-permute-start(bf16[64,1024]{1,0:T(8,128)(2,1)S(1)} %get-tuple-element.47), channel_id=1, source_target_pairs={{0,6},{1,7},{2,4},{3,5},{4,2},{5,3},{6,0},{7,1},{8,14},{9,15},{10,... | collective-permute-start | bytes 393224 | tf_op jit(solution)/shard_map/ppermute | solution.py:322
  65.4 6.0 %collective-permute-start.19 = (bf16[32,1024]{1,0:T(8,128)(2,1)S(1)}, bf16[32,1024]{1,0:T(8,128)(2,1)S(1)}, u32[]{:S(2)}, u32[]{:S(2)}) collective-permute-start(bf16[32,1024]{1,0:T(8,128)(2,1)S(1)} %get-tuple-element.54), channel_id=1, source_target_pairs={{0,16},{1,17},{2,18},{3,19},{4,20},{5,21},{6,22},{7,23},{8,24},{9,... | collective-permute-start | bytes 196616 | tf_op jit(solution)/shard_map/ppermute | solution.py:322
  66.2 6.2 %collective-permute-start.20 = (bf16[32,1024]{1,0:T(8,128)(2,1)S(1)}, bf16[32,1024]{1,0:T(8,128)(2,1)S(1)}, u32[]{:S(2)}, u32[]{:S(2)}) collective-permute-start(bf16[32,1024]{1,0:T(8,128)(2,1)S(1)} %get-tuple-element.55), channel_id=1, source_target_pairs={{0,24},{1,25},{2,26},{3,27},{4,28},{5,29},{6,30},{7,31},{8,16},{9,... | collective-permute-start | bytes 196616 | tf_op jit(solution)/shard_map/ppermute | solution.py:322
  69.5 4.3 %collective-permute-start.15 = (bf16[32,1024]{1,0:T(8,128)(2,1)S(1)}, bf16[32,1024]{1,0:T(8,128)(2,1)S(1)}, u32[]{:S(2)}, u32[]{:S(2)}) collective-permute-start(bf16[32,1024]{1,0:T(8,128)(2,1)S(1)} %get-tuple-element.49), channel_id=1, source_target_pairs={{0,8},{1,9},{2,10},{3,11},{4,12},{5,13},{6,14},{7,15},{8,0},{9,1},... | collective-permute-start | bytes 196616 | tf_op jit(solution)/shard_map/ppermute | solution.py:322

commit v11 on v10

--- a/solution.py
+++ b/solution.py
@@ -104,14 +104,14 @@
     rows[:, :width] = packed.astype(jnp.bfloat16)
 
 
-def join_kernel(order, after, *refs):
+def join_kernel(order, *refs):
     blocks, line, plain = refs[:-2], refs[-2], refs[-1]
     for place, block in zip(order, blocks):
         line[place * CAP:(place + 1) * CAP] = block[...]
         plain[place * CAP:(place + 1) * CAP] = block[:, :plain.shape[1]]
 
 
-def stage_kernel(blocks, after, weight, held, away, finished, sems):
+def stage_kernel(blocks, line, weight, held, away, same, sems):
     rank = coordinates()[0]
     width = weight.shape[0] // blocks
     copies = []
@@ -126,9 +126,13 @@
             )
             copy.start()
             copies.append(copy)
-    finished[...] = jnp.zeros_like(finished)
+    same[...] = line[...]
     for copy in copies:
         copy.wait()
+
+
+def gate_kernel(value, after, same):
+    pass
 
 
 def info_kernel(*refs):
@@ -205,32 +209,32 @@
     stats[...] = jnp.broadcast_to(line[None], stats.shape)
 
 
-def log_totals_kernel(groups, info, stats, columns, loss):
-    position = coordinates()[1]
-    height = info.shape[0]
+def log_totals(groups, stats, height):
     peaks, masses = stats[:, :, :height], stats[:, :, height:2 * height]
     peak = jnp.max(peaks, axis=0)
     mass = jnp.sum(masses * jnp.exp(peaks - peak[None]), axis=0)
-    hit = jnp.sum(stats[:, :, 2 * height:], axis=0)
-    log_total = jnp.broadcast_to(peak + jnp.log(mass), (8, height))
-    log_total = reorder(log_total, position, groups)
-    log_total = jnp.transpose(jnp.concatenate([log_total] * 16, axis=0))
-    loss[0, 0] = jnp.sum(info[:, 0:1] * log_total[:, 0:1]) - hit[0, 0]
-    columns[...] = log_total
-
-
-def grad_kernel(chunk, order, info, mine, theirs, weight, other_weight, table, *refs):
-    logit_grad, outs = refs[0], refs[1:]
+    line = jnp.broadcast_to(peak + jnp.log(mass), (8, height))
+    line = reorder(line, coordinates()[1], groups)
+    return jnp.transpose(jnp.concatenate([line] * 16, axis=0))
+
+
+def grad_kernel(chunk, order, groups, info, mine, theirs, weight, other_weight, stats, *refs):
+    logit_grad, outs = refs[0], refs[1:len(order) + 1]
     rank, _, shard = coordinates()
     height, columns = mine.shape
     part = height // 4
     quarters = [chunk, 2 + chunk]
 
-    def rows_of(ref):
-        return jnp.concatenate([ref[q * part:(q + 1) * part] for q in quarters], axis=0)
-
+    def rows_of(value):
+        return jnp.concatenate([value[q * part:(q + 1) * part] for q in quarters], axis=0)
+
+    if chunk:
+        table = log_totals(groups, stats, height)
+        refs[-1][...] = table
+    else:
+        table = stats[...]
+    log_total = rows_of(table)[:, 0:1]
     rows_info = rows_of(info)
-    log_total = rows_of(table)[:, 0:1]
     row_weight, target = rows_info[:, 0:1], rows_info[:, 1:2].astype(jnp.int32)
 
     def grad_of(logits, shard):
@@ -256,29 +260,35 @@
             out[...] = total[y * part:(y + 1) * part].astype(out.dtype)
 
 
-def weight_kernel(blocks, after, near_grad, far_grad, *refs):
-    pieces, (out, finished, done, sems) = refs[:-4], refs[-4:]
+def weight_kernel(blocks, skipped, after, near_grad, far_grad, *refs):
+    pieces, (out, last, done, sems) = refs[skipped:-4], refs[-4:]
     rank = coordinates()[0]
-    finished[...] = jnp.zeros_like(finished)
     part = near_grad.shape[0] // 2
     logit_grad = jnp.concatenate(
         [ref[y * part:(y + 1) * part] for y in range(2) for ref in (near_grad, far_grad)], axis=0
     )
-    width = done.shape[0] // blocks
+    width = done.shape[0] // len(blocks)
     copies = []
-    for block in range(blocks):
-        done[block * width:(block + 1) * width] = lax.dot_general(
-            all_rows(pieces, block, width),
+    for place, block in enumerate(blocks):
+        done[place * width:(place + 1) * width] = lax.dot_general(
+            all_rows(pieces, place, width),
             logit_grad,
             (((0,), (0,)), ((), ())),
             preferred_element_type=jnp.float32,
         ).astype(jnp.bfloat16)
         start = pl.multiple_of((rank ^ block) * width, width)
         copy = pltpu.make_async_copy(
-            done.at[pl.ds(block * width, width)], out.at[pl.ds(start, width)], sems.at[block]
+            done.at[pl.ds(place * width, width)], out.at[pl.ds(start, width)], sems.at[place]
         )
         copy.start()
         copies.append(copy)
+    if skipped:
+        info, table, stats = refs[1:4]
+        hits = jnp.sum(stats[:, :, 2 * info.shape[0]:], axis=0)
+        loss = jnp.sum(info[:, 0:1] * table[:, 0:1]) - hits[0, 0]
+        last[...] = jnp.full(last.shape, loss, jnp.float32)
+    else:
+        last[...] = jnp.zeros_like(last)
     for copy in copies:
         copy.wait()
 
@@ -291,9 +301,10 @@
         out[...] = total[place * CAP:(place + 1) * CAP].astype(out.dtype)
 
 
-def unpack_kernel(chosen, *refs):
-    out = refs[-1]
-    total = sum(ref[...].astype(jnp.float32) for ref in refs[:-1])
+def unpack_kernel(last, chosen, *refs):
+    out, loss = refs[-2:]
+    loss[0, 0] = last[0, 0]
+    total = sum(ref[...].astype(jnp.float32) for ref in refs[:-2])
     out[...] = lax.dot_general(
         chosen[...],
         total.astype(jnp.bfloat16),
@@ -340,31 +351,30 @@
         + [pltpu.SemaphoreType.DMA((4,))],
     )
 
-    line_order = [0, 1] + list(range(zs - 1, 1, -1))
+    line_order = [0, *range(2, zs), 1]
     blocks = [send(packed, z=z) if z else packed for z in line_order]
-    held, away, finished = call(
+    line_rows = zs * CAP
+    line, line_plain = call(
+        functools.partial(join_kernel, line_order),
+        blocks,
+        [VMEM] * zs,
+        (shape((line_rows, width + IDS), bf16), shape((line_rows, width), bf16)),
+        (VMEM, VMEM),
+    )
+    pieces = {(2 * x, y): send(line_plain if x else line, y=y, x=x) for y, x in square}
+    held, away, same = call(
         functools.partial(stage_kernel, ranks),
-        (blocks[1], in_hbm(weight)),
-        [ANY, HBM],
+        (line, in_hbm(weight)),
+        [VMEM, HBM],
         (
             shape((depth, columns), bf16),
             shape((depth // 2, columns), bf16),
-            shape((8, 128), f32),
+            shape(line.shape, bf16),
         ),
         (VMEM,) * 3,
         [pltpu.SemaphoreType.DMA((ranks + xs,))],
     )
-    other_held = send(away, core=1)
-    line_rows = zs * CAP
-    line, line_plain = call(
-        functools.partial(join_kernel, line_order),
-        (finished, *blocks),
-        [ANY] + [VMEM] * zs,
-        (shape((line_rows, width + IDS), bf16), shape((line_rows, width), bf16)),
-        (VMEM, VMEM),
-    )
-    pieces = {(2 * x, y): send(line_plain if x else line, y=y, x=x) for y, x in square}
-    pieces[0, 0] = line
+    pieces[0, 0] = same
     for b, y in list(pieces):
         pieces[b + 1, y] = send(pieces[b, y], core=1)
     rows = [pieces[b, y] for b in range(ranks) for y in range(2)]
@@ -398,41 +408,52 @@
         flops=flops // 2,
     )
     other_logits = send(logits, core=1)
+    away = call(
+        gate_kernel, (away, stats), [ANY, ANY], shape(away.shape, bf16), ANY, aliases={0: 0}
+    )
+    other_held = send(away, core=1)
     stats = lax.all_to_all(stats, AXES, 0, 0)
-    table, loss = call(
-        functools.partial(log_totals_kernel, dps),
-        (info, stats),
-        [VMEM] * 2,
-        (shape((total_rows, 128), f32), shape((1, 1), f32)),
-        (VMEM, SMEM),
-    )
-
     rows_part = total_rows // 4
     order = sorted(range(1, ranks), key=lambda place: (place % 2 + (place > 1), place)) + [0]
     ends, sums, grads = [None] * zs, [None, None], [None, None]
     for chunk in (1, 0):
+        outs = (shape((total_rows // 2, columns), bf16),)
+        outs += (shape((rows_part, width), bf16),) * (ranks - 1) + (shape((rows_part, width), f32),)
+        if chunk:
+            outs += (shape((total_rows, 128), f32),)
         grads[chunk], *going = call(
-            functools.partial(grad_kernel, chunk, order),
-            (info, logits, other_logits, held, other_held, table),
+            functools.partial(grad_kernel, chunk, order, dps),
+            (info, logits, other_logits, held, other_held, stats if chunk else table),
             [VMEM] * 6,
-            (shape((total_rows // 2, columns), bf16),)
-            + (shape((rows_part, width), bf16),) * (ranks - 1)
-            + (shape((rows_part, width), f32),),
-            (VMEM,) * (ranks + 1),
+            outs,
+            (VMEM,) * len(outs),
             flops=flops // 2,
         )
+        if chunk:
+            table = going.pop()
         sums[chunk] = [going[-1]]
         for place, value in zip(order, going[:-1]):
             sums[chunk].append(send(value, y=place % 2, x=place // 2))
-    weight_grad, finished = call(
-        functools.partial(weight_kernel, ranks),
-        (sums[0][0], *grads, *rows),
-        [ANY] + [VMEM] * (2 + len(rows)),
-        (shape((depth, columns), bf16), shape((8, 128), f32)),
-        (HBM, VMEM),
-        [pltpu.VMEM((depth, columns), bf16), pltpu.SemaphoreType.DMA((ranks,))],
-        flops=flops,
-    )
+
+    def weight_part(first, after, *extra):
+        blocks = range(first, first + ranks // 2)
+        chosen_rows = rows[2 * first:2 * first + ranks]
+        return call(
+            functools.partial(weight_kernel, blocks, len(extra)),
+            (after, *grads, *extra, *chosen_rows),
+            [ANY] + [VMEM] * 2 + [HBM] * (len(extra) > 0)
+            + [VMEM] * (max(len(extra) - 1, 0) + len(chosen_rows)),
+            (shape((depth, columns), bf16), shape((8, 128), f32)),
+            (HBM, VMEM),
+            [
+                pltpu.VMEM((depth // 2, columns), bf16),
+                pltpu.SemaphoreType.DMA((ranks // 2,)),
+            ],
+            flops=flops // 2,
+            aliases={3: 0} if extra else {},
+        )
+
+    weight_grad, finished = weight_part(0, sums[0][0])
     for chunk in (1, 0):
         near = chunk * zs // 2
         parts_z = call(
@@ -444,12 +465,13 @@
         )
         for z, value in enumerate(parts_z):
             ends[near + z] = send(value, z=near + z) if near + z else value
-    hidden_grad = call(
+    weight_grad, last = weight_part(ranks // 2, parts_z[0], weight_grad, info, table, stats)
+    hidden_grad, loss = call(
         unpack_kernel,
-        (chosen, *ends),
-        [VMEM] * (1 + len(ends)),
-        shape((tokens, width), bf16),
-        VMEM,
+        (last, chosen, *ends),
+        [VMEM] * (2 + len(ends)),
+        (shape((tokens, width), bf16), shape((1, 1), f32)),
+        (VMEM, SMEM),
     )
     return loss[0, 0], hidden_grad, weight_grad
 

time: 74.9 us -> 66.2 us (0.88)
  waiting for transfers between devices: 23.1 us -> 16.9 us
  starting transfers between devices: 22.2 us -> 19.9 us
  blocking collectives: 14.7 us -> 13.9 us
    ppermute x21, waiting for transfers between devices: 23.1 us -> 16.9 us  [send(): return lax.ppermute(value, AXES, pairs)]
    ppermute x21, starting transfers between devices: 22.2 us -> 19.9 us  [send(): return lax.ppermute(value, AXES, pairs)]
    all_to_all x1, blocking collectives: 14.7 us -> 13.9 us  [body(): stats = lax.all_to_all(stats, AXES, 0, 0)]
    pallas_call x13 -> x14, Pallas kernels: 14 us -> 14.5 us  [call(): pl.pallas_call(kernel, out_shape=out_shape, in_specs=in_specs, out_specs=...]
  transfers between devices with their start and end apart: 21 -> 21, of which waited for: 9 -> 11; matrix products, arithmetic and copies ran while one was open for 0% -> 0% of each run, Pallas kernels for 10% -> 14%
where the time goes in v11:
time: 66.2 us; the launch traced here: 66 us
  starting transfers between devices  19.9 us (30%)
  waiting for transfers between devices  16.9 us (26%)
  Pallas kernels  14.5 us (22%)
  blocking collectives  13.9 us (21%)
  between operations  0.8 us (1%)
    ppermute x21, starting transfers between devices, send(): return lax.ppermute(value, AXES, pairs)  19.9 us
    ppermute x21, waiting for transfers between devices, send(): return lax.ppermute(value, AXES, pairs)  16.9 us
    pallas_call x14, Pallas kernels, call(): pl.pallas_call(kernel, out_shape=out_shape, in_specs=in_specs, out_specs=...  14.5 us
    all_to_all x1, blocking collectives, body(): stats = lax.all_to_all(stats, AXES, 0, 0)  13.9 us
  transfers between devices with their start and end apart: 21, of which 11 were waited for; matrix products, arithmetic and copies ran while one was open for 0% of the time, Pallas kernels for 14%

profile of v11, /device:TPU:0, one launch (start us, length us, event | category | flops | bytes accessed | tf_op | source)
XLA Modules:
  0.0 66.0 jit_solution(16951103368133738923)
XLA Ops:
  0.6 1.2 %shard_map.85 = (bf16[32,1152]{1,0:T(8,128)(2,1)S(1)}, bf16[32,128]{1,0:T(8,128)(2,1)S(1)}) custom-call(bf16[128,1024]{1,0:T(8,128)(2,1)} %hidden_hbm.1, s32[1,128]{1,0:T(1,128)} %bitcast.6, s32[1,128]{1,0:T(1,128)} %bitcast.7, s32[1,128]{1,0:T(1,128)} %bitcast.8), custom_call_target="tpu_custom_call" | custom-call | bytes 345600 | tf_op jit(solution)/shard_map/pallas_call | solution.py:32
  1.9 4.1 %collective-permute-start = (bf16[32,1152]{1,0:T(8,128)(2,1)S(1)}, bf16[32,1152]{1,0:T(8,128)(2,1)S(1)}, u32[]{:S(2)}, u32[]{:S(2)}) collective-permute-start(bf16[32,1152]{1,0:T(8,128)(2,1)S(1)} %get-tuple-element.33.refs_0_), channel_id=1, source_target_pairs={{0,16},{1,17},{2,18},{3,19},{4,20},{5,21},{6,22},{7,23},{8,24},{9,... | collective-permute-start | bytes 221192 | tf_op jit(solution)/shard_map/ppermute | solution.py:333
  6.0 1.3 %collective-permute-start.1 = (bf16[32,1152]{1,0:T(8,128)(2,1)S(1)}, bf16[32,1152]{1,0:T(8,128)(2,1)S(1)}, u32[]{:S(2)}, u32[]{:S(2)}) collective-permute-start(bf16[32,1152]{1,0:T(8,128)(2,1)S(1)} %get-tuple-element.33.refs_0_), channel_id=1, source_target_pairs={{0,24},{1,25},{2,26},{3,27},{4,28},{5,29},{6,30},{7,31},{8,16},{9,... | collective-permute-start | bytes 221192 | tf_op jit(solution)/shard_map/ppermute | solution.py:333
  7.5 3.3 %collective-permute-done.refs_1_ = bf16[32,1152]{1,0:T(8,128)(2,1)S(1)} collective-permute-done((bf16[32,1152]{1,0:T(8,128)(2,1)S(1)}, bf16[32,1152]{1,0:T(8,128)(2,1)S(1)}, u32[]{:S(2)}, u32[]{:S(2)}) %collective-permute-start) | collective-permute-done | bytes 73760 | tf_op jit(solution)/shard_map/ppermute | solution.py:333
  10.8 1.6 %collective-permute-done.1.refs_2_ = bf16[32,1152]{1,0:T(8,128)(2,1)S(1)} collective-permute-done((bf16[32,1152]{1,0:T(8,128)(2,1)S(1)}, bf16[32,1152]{1,0:T(8,128)(2,1)S(1)}, u32[]{:S(2)}, u32[]{:S(2)}) %collective-permute-start.1) | collective-permute-done | bytes 73760 | tf_op jit(solution)/shard_map/ppermute | solution.py:333
  12.6 1.8 %collective-permute-start.3 = (bf16[128,1152]{1,0:T(8,128)(2,1)S(1)}, bf16[128,1152]{1,0:T(8,128)(2,1)S(1)}, u32[]{:S(2)}, u32[]{:S(2)}) collective-permute-start(bf16[128,1152]{1,0:T(8,128)(2,1)S(1)} %get-tuple-element.34.line), channel_id=1, source_target_pairs={{0,4},{1,5},{2,6},{3,7},{4,0},{5,1},{6,2},{7,3},{8,12},{9,13},{10,... | collective-permute-start | bytes 884744 | tf_op jit(solution)/shard_map/ppermute | solution.py:333
  14.4 1.5 %collective-permute-start.4 = (bf16[128,1024]{1,0:T(8,128)(2,1)S(1)}, bf16[128,1024]{1,0:T(8,128)(2,1)S(1)}, u32[]{:S(2)}, u32[]{:S(2)}) collective-permute-start(bf16[128,1024]{1,0:T(8,128)(2,1)S(1)} %get-tuple-element.37), channel_id=1, source_target_pairs={{0,2},{1,3},{2,0},{3,1},{4,6},{5,7},{6,4},{7,5},{8,10},{9,11},{10,... | collective-permute-start | bytes 786440 | tf_op jit(solution)/shard_map/ppermute | solution.py:333
  16.2 2.9 %shard_map.87 = (bf16[4096,512]{1,0:T(8,128)(2,1)S(1)}, bf16[2048,512]{1,0:T(8,128)(2,1)S(1)}, bf16[128,1152]{1,0:T(8,128)(2,1)S(1)}) custom-call(bf16[128,1152]{1,0:T(8,128)(2,1)S(1)} %get-tuple-element.34.line, bf16[4096,512]{1,0:T(8,128)(2,1)} %weight.1), custom_call_target="tpu_custom_call" | custom-call | bytes 11075584 | tf_op jit(solution)/shard_map/pallas_call | solution.py:32
  19.2 3.3 %collective-permute-done.3.refs_1_ = bf16[128,1152]{1,0:T(8,128)(2,1)S(1)} collective-permute-done((bf16[128,1152]{1,0:T(8,128)(2,1)S(1)}, bf16[128,1152]{1,0:T(8,128)(2,1)S(1)}, u32[]{:S(2)}, u32[]{:S(2)}) %collective-permute-start.3) | collective-permute-done | bytes 294944 | tf_op jit(solution)/shard_map/ppermute | solution.py:333
  22.5 1.2 %collective-permute-done.4.refs_2_.refs_4_ = bf16[128,1024]{1,0:T(8,128)(2,1)S(1)} collective-permute-done((bf16[128,1024]{1,0:T(8,128)(2,1)S(1)}, bf16[128,1024]{1,0:T(8,128)(2,1)S(1)}, u32[]{:S(2)}, u32[]{:S(2)}) %collective-permute-start.4) | collective-permute-done | bytes 262176 | tf_op jit(solution)/shard_map/ppermute | solution.py:333
  23.7 2.6 %collective-permute-done.5.refs_3_.refs_5_ = bf16[128,1024]{1,0:T(8,128)(2,1)S(1)} collective-permute-done((bf16[128,1024]{1,0:T(8,128)(2,1)S(1)}, bf16[128,1024]{1,0:T(8,128)(2,1)S(1)}, u32[]{:S(2)}, u32[]{:S(2)}) %collective-permute-start.5) | collective-permute-done | bytes 262176 | tf_op jit(solution)/shard_map/ppermute | solution.py:333
  26.3 0.4 shard_map.88.info.refs_1_
  26.7 0.7 %shard_map.89.partial = f32[256,512]{1,0:T(8,128)S(1)} custom-call(bf16[4096,512]{1,0:T(8,128)(2,1)S(1)} %get-tuple-element.36.weight, bf16[128,1152]{1,0:T(8,128)(2,1)S(1)} %get-tuple-element.35.refs_0_, bf16[128,1152]{1,0:T(8,128)(2,1)S(1)} %collective-permute-done.3.refs_1_, bf16[128,1024]{1,0:T(8,128)(2,1)S(1)} %collective-permute-done.4.refs_2_.refs_4_, ...), custom_call_target="tpu_custom_call" | custom-call | flops 536870912 | bytes 5832704 | tf_op jit(solution)/shard_map/pallas_call | solution.py:32
  27.5 0.4 collective-permute-done.9.refs_3_.refs_7_
  27.9 1.2 %shard_map.90 = (f32[256,512]{1,0:T(8,128)S(1)}, f32[32,1,640]{2,1,0:T(1,128)S(1)}) custom-call(f32[256,128]{1,0:T(8,128)S(1)} %shard_map.88.info.refs_1_, f32[256,512]{1,0:T(8,128)S(1)} %shard_map.89.partial, bf16[4096,512]{1,0:T(8,128)(2,1)S(1)} %get-tuple-element.36.weight, bf16[128,1152]{1,0:T(8,128)(2,1)S(1)} %collective-permute-done.6.refs_0_.refs_2_, ...), custom_call_target="tpu_custom_call" | custom-call | flops 536870912 | bytes 6569984 | tf_op jit(solution)/shard_map/pallas_call | solution.py:32
  29.6 13.9 %all_to_all.5.stats.refs_3_ = f32[32,1,640]{2,1,0:T(1,128)S(1)} all-to-all(f32[32,1,640]{2,1,0:T(1,128)S(1)} %get-tuple-element.40.after), channel_id=1, replica_groups=mesh['dp'=8,'vocab'=4] {'dp','vocab'}, dimensions={0} | all-to-all | bytes 163840 | tf_op jit(solution)/shard_map/all_to_all | solution.py:415
  43.5 1.9 %shard_map.92 = (bf16[128,512]{1,0:T(8,128)(2,1)S(1)}, bf16[64,1024]{1,0:T(8,128)(2,1)S(1)}, bf16[64,1024]{1,0:T(8,128)(2,1)S(1)}, bf16[64,1024]{1,0:T(8,128)(2,...) custom-call(f32[256,128]{1,0:T(8,128)S(1)} %shard_map.88.info.refs_1_, f32[256,512]{1,0:T(8,128)S(1)} %get-tuple-element.38.mine, ...), custom_call_target="tpu_custom_call" | custom-call | flops 536870912 | bytes 8470528 | tf_op jit(solution)/shard_map/pallas_call | solution.py:32
  45.5 0.7 %collective-permute-start.16 = (bf16[64,1024]{1,0:T(8,128)(2,1)S(1)}, bf16[64,1024]{1,0:T(8,128)(2,1)S(1)}, u32[]{:S(2)}, u32[]{:S(2)}) collective-permute-start(bf16[64,1024]{1,0:T(8,128)(2,1)S(1)} %get-tuple-element.55), channel_id=1, source_target_pairs={{0,4},{1,5},{2,6},{3,7},{4,0},{5,1},{6,2},{7,3},{8,12},{9,13},{10,... | collective-permute-start | bytes 393224 | tf_op jit(solution)/shard_map/ppermute | solution.py:333
  46.1 0.7 %collective-permute-start.17 = (bf16[64,1024]{1,0:T(8,128)(2,1)S(1)}, bf16[64,1024]{1,0:T(8,128)(2,1)S(1)}, u32[]{:S(2)}, u32[]{:S(2)}) collective-permute-start(bf16[64,1024]{1,0:T(8,128)(2,1)S(1)} %get-tuple-element.56), channel_id=1, source_target_pairs={{0,2},{1,3},{2,0},{3,1},{4,6},{5,7},{6,4},{7,5},{8,10},{9,11},{10,... | collective-permute-start | bytes 393224 | tf_op jit(solution)/shard_map/ppermute | solution.py:333
  46.9 2.2 %collective-permute-start.18 = (bf16[64,1024]{1,0:T(8,128)(2,1)S(1)}, bf16[64,1024]{1,0:T(8,128)(2,1)S(1)}, u32[]{:S(2)}, u32[]{:S(2)}) collective-permute-start(bf16[64,1024]{1,0:T(8,128)(2,1)S(1)} %get-tuple-element.57), channel_id=1, source_target_pairs={{0,6},{1,7},{2,4},{3,5},{4,2},{5,3},{6,0},{7,1},{8,14},{9,15},{10,... | collective-permute-start | bytes 393224 | tf_op jit(solution)/shard_map/ppermute | solution.py:333
  49.0 1.5 %shard_map.93 = (bf16[128,512]{1,0:T(8,128)(2,1)S(1)}, bf16[64,1024]{1,0:T(8,128)(2,1)S(1)}, bf16[64,1024]{1,0:T(8,128)(2,1)S(1)}, bf16[64,1024]{1,0:T(8,128)(2,1)S(1)}, f32[64,1024]{1,0:T(8,128)S(1)}) custom-call(f32[256,128]{1,0:T(8,128)S(1)} %shard_map.88.info.refs_1_, f32[256,512]{1,0:T(8,128)S(1)} %get-tuple-element.38.mine, ...), custom_call_target="tpu_custom_call" | custom-call | flops 536870912 | bytes 8388608 | tf_op jit(solution)/shard_map/pallas_call | solution.py:32
  50.6 0.7 %collective-permute-start.12 = (bf16[64,1024]{1,0:T(8,128)(2,1)S(1)}, bf16[64,1024]{1,0:T(8,128)(2,1)S(1)}, u32[]{:S(2)}, u32[]{:S(2)}) collective-permute-start(bf16[64,1024]{1,0:T(8,128)(2,1)S(1)} %get-tuple-element.46), channel_id=1, source_target_pairs={{0,4},{1,5},{2,6},{3,7},{4,0},{5,1},{6,2},{7,3},{8,12},{9,13},{10,... | collective-permute-start | bytes 393224 | tf_op jit(solution)/shard_map/ppermute | solution.py:333
  51.2 0.7 %collective-permute-start.13 = (bf16[64,1024]{1,0:T(8,128)(2,1)S(1)}, bf16[64,1024]{1,0:T(8,128)(2,1)S(1)}, u32[]{:S(2)}, u32[]{:S(2)}) collective-permute-start(bf16[64,1024]{1,0:T(8,128)(2,1)S(1)} %get-tuple-element.47), channel_id=1, source_target_pairs={{0,2},{1,3},{2,0},{3,1},{4,6},{5,7},{6,4},{7,5},{8,10},{9,11},{10,... | collective-permute-start | bytes 393224 | tf_op jit(solution)/shard_map/ppermute | solution.py:333
  51.9 2.2 %collective-permute-start.14 = (bf16[64,1024]{1,0:T(8,128)(2,1)S(1)}, bf16[64,1024]{1,0:T(8,128)(2,1)S(1)}, u32[]{:S(2)}, u32[]{:S(2)}) collective-permute-start(bf16[64,1024]{1,0:T(8,128)(2,1)S(1)} %get-tuple-element.48), channel_id=1, source_target_pairs={{0,6},{1,7},{2,4},{3,5},{4,2},{5,3},{6,0},{7,1},{8,14},{9,15},{10,... | collective-permute-start | bytes 393224 | tf_op jit(solution)/shard_map/ppermute | solution.py:333
  54.1 1.8 %shard_map.94 = (bf16[4096,512]{1,0:T(8,128)(2,1)}, f32[8,128]{1,0:T(8,128)S(1)}) custom-call(f32[64,1024]{1,0:T(8,128)S(1)} %get-tuple-element.42.after.kept, bf16[128,512]{1,0:T(8,128)(2,1)S(1)} %get-tuple-element.43.near_grad, bf16[128,512]{1,0:T(8,128)(2,1)S(1)} %get-tuple-element.44.far_grad, bf16[128,1152]{1,0:T(8,128)(2,1)S(1)} %get-tuple-element.35.refs_0_, ...), custom_call_target="tpu_custom_call" | custom-call | flops 536870912 | bytes 5902336 | tf_op jit(solution)/shard_map/pallas_call | solution.py:32
  56.3 0.5 collective-permute-start.19
  56.8 2.3 %collective-permute-start.20 = (bf16[32,1024]{1,0:T(8,128)(2,1)S(1)}, bf16[32,1024]{1,0:T(8,128)(2,1)S(1)}, u32[]{:S(2)}, u32[]{:S(2)}) collective-permute-start(bf16[32,1024]{1,0:T(8,128)(2,1)S(1)} %get-tuple-element.59), channel_id=1, source_target_pairs={{0,24},{1,25},{2,26},{3,27},{4,28},{5,29},{6,30},{7,31},{8,16},{9,... | collective-permute-start | bytes 196616 | tf_op jit(solution)/shard_map/ppermute | solution.py:333
  59.1 1.6 %collective-permute-done.14.refs_2_ = bf16[64,1024]{1,0:T(8,128)(2,1)S(1)} collective-permute-done((bf16[64,1024]{1,0:T(8,128)(2,1)S(1)}, bf16[64,1024]{1,0:T(8,128)(2,1)S(1)}, u32[]{:S(2)}, u32[]{:S(2)}) %collective-permute-start.14) | collective-permute-done | bytes 131104 | tf_op jit(solution)/shard_map/ppermute | solution.py:333
  60.8 1.8 %shard_map.96 = (bf16[4096,512]{1,0:T(8,128)(2,1)}, f32[8,128]{1,0:T(8,128)S(1)}) custom-call(f32[32,1024]{1,0:T(8,128)S(1)} %get-tuple-element.49.after.refs_0_, bf16[128,512]{1,0:T(8,128)(2,1)S(1)} %get-tuple-element.43.near_grad, bf16[128,512]{1,0:T(8,128)(2,1)S(1)} %get-tuple-element.44.far_grad, ...), custom_call_target="tpu_custom_call", output_to_operand_aliasing={{0}: (3, {})} | custom-call | flops 536870912 | bytes 10178560 | tf_op jit(solution)/shard_map/pallas_call | solution.py:32
  62.6 0.5 collective-permute-done.20.refs_3_
  63.1 1.9 %collective-permute-done.15.refs_1_ = bf16[32,1024]{1,0:T(8,128)(2,1)S(1)} collective-permute-done((bf16[32,1024]{1,0:T(8,128)(2,1)S(1)}, bf16[32,1024]{1,0:T(8,128)(2,1)S(1)}, u32[]{:S(2)}, u32[]{:S(2)}) %collective-permute-start.15) | collective-permute-done | bytes 65568 | tf_op jit(solution)/shard_map/ppermute | solution.py:333
  65.1 1.0 %shard_map.98 = (bf16[128,1024]{1,0:T(8,128)(2,1)}, f32[1,1]{1,0:T(1,128)}) custom-call(f32[8,128]{1,0:T(8,128)S(1)} %get-tuple-element.51.last, bf16[32,128]{1,0:T(8,128)(2,1)S(1)} %get-tuple-element.52.chosen, f32[32,1024]{1,0:T(8,128)S(1)} %get-tuple-element.49.after.refs_0_, bf16[32,1024]{1,0:T(8,128)(2,1)S(1)} %collective-permute-done.15.refs_1_, ...), custom_call_target="tpu_custom_call" | custom-call | bytes 602116 | tf_op jit(solution)/shard_map/pallas_call | solution.py:32
  (27 shorter events, 1.8 us)
Async XLA Ops:
  0.6 25.7 %copy-start = (f32[32]{0:T(128)S(1)}, f32[32]{0:T(128)}, u32[]{:S(2)}) copy-start(f32[32]{0:T(128)} %param.11) | copy-start | bytes 388
  1.9 9.0 %collective-permute-start = (bf16[32,1152]{1,0:T(8,128)(2,1)S(1)}, bf16[32,1152]{1,0:T(8,128)(2,1)S(1)}, u32[]{:S(2)}, u32[]{:S(2)}) collective-permute-start(bf16[32,1152]{1,0:T(8,128)(2,1)S(1)} %get-tuple-element.33.refs_0_), channel_id=1, source_target_pairs={{0,16},{1,17},{2,18},{3,19},{4,20},{5,21},{6,22},{7,23},{8,24},{9,... | collective-permute-start | bytes 221192 | tf_op jit(solution)/shard_map/ppermute | solution.py:333
  6.0 6.5 %collective-permute-start.1 = (bf16[32,1152]{1,0:T(8,128)(2,1)S(1)}, bf16[32,1152]{1,0:T(8,128)(2,1)S(1)}, u32[]{:S(2)}, u32[]{:S(2)}) collective-permute-start(bf16[32,1152]{1,0:T(8,128)(2,1)S(1)} %get-tuple-element.33.refs_0_), channel_id=1, source_target_pairs={{0,24},{1,25},{2,26},{3,27},{4,28},{5,29},{6,30},{7,31},{8,16},{9,... | collective-permute-start | bytes 221192 | tf_op jit(solution)/shard_map/ppermute | solution.py:333
  7.3 5.3 %collective-permute-start.2 = (bf16[32,1152]{1,0:T(8,128)(2,1)S(1)}, bf16[32,1152]{1,0:T(8,128)(2,1)S(1)}, u32[]{:S(2)}, u32[]{:S(2)}) collective-permute-start(bf16[32,1152]{1,0:T(8,128)(2,1)S(1)} %get-tuple-element.33.refs_0_), channel_id=1, source_target_pairs={{0,8},{1,9},{2,10},{3,11},{4,12},{5,13},{6,14},{7,15},{8,0},{9,1},... | collective-permute-start | bytes 221192 | tf_op jit(solution)/shard_map/ppermute | solution.py:333
  12.6 9.8 %collective-permute-start.3 = (bf16[128,1152]{1,0:T(8,128)(2,1)S(1)}, bf16[128,1152]{1,0:T(8,128)(2,1)S(1)}, u32[]{:S(2)}, u32[]{:S(2)}) collective-permute-start(bf16[128,1152]{1,0:T(8,128)(2,1)S(1)} %get-tuple-element.34.line), channel_id=1, source_target_pairs={{0,4},{1,5},{2,6},{3,7},{4,0},{5,1},{6,2},{7,3},{8,12},{9,13},{10,... | collective-permute-start | bytes 884744 | tf_op jit(solution)/shard_map/ppermute | solution.py:333
  14.4 9.2 %collective-permute-start.4 = (bf16[128,1024]{1,0:T(8,128)(2,1)S(1)}, bf16[128,1024]{1,0:T(8,128)(2,1)S(1)}, u32[]{:S(2)}, u32[]{:S(2)}) collective-permute-start(bf16[128,1024]{1,0:T(8,128)(2,1)S(1)} %get-tuple-element.37), channel_id=1, source_target_pairs={{0,2},{1,3},{2,0},{3,1},{4,6},{5,7},{6,4},{7,5},{8,10},{9,11},{10,... | collective-permute-start | bytes 786440 | tf_op jit(solution)/shard_map/ppermute | solution.py:333
  15.9 10.4 %collective-permute-start.5 = (bf16[128,1024]{1,0:T(8,128)(2,1)S(1)}, bf16[128,1024]{1,0:T(8,128)(2,1)S(1)}, u32[]{:S(2)}, u32[]{:S(2)}) collective-permute-start(bf16[128,1024]{1,0:T(8,128)(2,1)S(1)} %get-tuple-element.37), channel_id=1, source_target_pairs={{0,6},{1,7},{2,4},{3,5},{4,2},{5,3},{6,0},{7,1},{8,14},{9,15},{10,... | collective-permute-start | bytes 786440 | tf_op jit(solution)/shard_map/ppermute | solution.py:333
  19.1 8.4 %collective-permute-start.6 = (bf16[128,1152]{1,0:T(8,128)(2,1)S(1)}, bf16[128,1152]{1,0:T(8,128)(2,1)S(1)}, u32[]{:S(2)}, u32[]{:S(2)}) collective-permute-start(bf16[128,1152]{1,0:T(8,128)(2,1)S(1)} %get-tuple-element.35.refs_0_), channel_id=1, source_target_pairs={{0,1},{1,0},{2,3},{3,2},{4,5},{5,4},{6,7},{7,6},{8,9},{9,8},{10,11... | collective-permute-start | bytes 884744 | tf_op jit(solution)/shard_map/ppermute | solution.py:333
  22.5 5.4 %collective-permute-start.7 = (bf16[128,1152]{1,0:T(8,128)(2,1)S(1)}, bf16[128,1152]{1,0:T(8,128)(2,1)S(1)}, u32[]{:S(2)}, u32[]{:S(2)}) collective-permute-start(bf16[128,1152]{1,0:T(8,128)(2,1)S(1)} %collective-permute-done.3.refs_1_), channel_id=1, source_target_pairs={{0,1},{1,0},{2,3},{3,2},{4,5},{5,4},{6,7},{7,6},{8,9},{9,8},{10,11... | collective-permute-start | bytes 884744 | tf_op jit(solution)/shard_map/ppermute | solution.py:333
  23.7 3.8 %collective-permute-start.8 = (bf16[128,1024]{1,0:T(8,128)(2,1)S(1)}, bf16[128,1024]{1,0:T(8,128)(2,1)S(1)}, u32[]{:S(2)}, u32[]{:S(2)}) collective-permute-start(bf16[128,1024]{1,0:T(8,128)(2,1)S(1)} %collective-permute-done.4.refs_2_.refs_4_), channel_id=1, source_target_pairs={{0,1},{1,0},{2,3},{3,2},{4,5},{5,4},{6,7},{7,6},{8,9},{9,8},{10,11... | collective-permute-start | bytes 786440 | tf_op jit(solution)/shard_map/ppermute | solution.py:333
  26.3 1.5 %collective-permute-start.9 = (bf16[128,1024]{1,0:T(8,128)(2,1)S(1)}, bf16[128,1024]{1,0:T(8,128)(2,1)S(1)}, u32[]{:S(2)}, u32[]{:S(2)}) collective-permute-start(bf16[128,1024]{1,0:T(8,128)(2,1)S(1)} %collective-permute-done.5.refs_3_.refs_5_), channel_id=1, source_target_pairs={{0,1},{1,0},{2,3},{3,2},{4,5},{5,4},{6,7},{7,6},{8,9},{9,8},{10,11... | collective-permute-start | bytes 786440 | tf_op jit(solution)/shard_map/ppermute | solution.py:333
  29.0 14.5 %collective-permute-start.11 = (bf16[2048,512]{1,0:T(8,128)(2,1)S(1)}, bf16[2048,512]{1,0:T(8,128)(2,1)S(1)}, u32[]{:S(2)}, u32[]{:S(2)}) collective-permute-start(bf16[2048,512]{1,0:T(8,128)(2,1)S(1)} %shard_map.91), channel_id=1, source_target_pairs={{0,1},{1,0},{2,3},{3,2},{4,5},{5,4},{6,7},{7,6},{8,9},{9,8},{10,11... | collective-permute-start | bytes 6291464 | tf_op jit(solution)/shard_map/ppermute | solution.py:333
  29.3 14.3 %collective-permute-start.10 = (f32[256,512]{1,0:T(8,128)S(1)}, f32[256,512]{1,0:T(8,128)S(1)}, u32[]{:S(2)}, u32[]{:S(2)}) collective-permute-start(f32[256,512]{1,0:T(8,128)S(1)} %get-tuple-element.38.mine), channel_id=1, source_target_pairs={{0,1},{1,0},{2,3},{3,2},{4,5},{5,4},{6,7},{7,6},{8,9},{9,8},{10,11... | collective-permute-start | bytes 1572872 | tf_op jit(solution)/shard_map/ppermute | solution.py:333
  45.5 6.5 %collective-permute-start.16 = (bf16[64,1024]{1,0:T(8,128)(2,1)S(1)}, bf16[64,1024]{1,0:T(8,128)(2,1)S(1)}, u32[]{:S(2)}, u32[]{:S(2)}) collective-permute-start(bf16[64,1024]{1,0:T(8,128)(2,1)S(1)} %get-tuple-element.55), channel_id=1, source_target_pairs={{0,4},{1,5},{2,6},{3,7},{4,0},{5,1},{6,2},{7,3},{8,12},{9,13},{10,... | collective-permute-start | bytes 393224 | tf_op jit(solution)/shard_map/ppermute | solution.py:333
  46.1 9.8 %collective-permute-start.17 = (bf16[64,1024]{1,0:T(8,128)(2,1)S(1)}, bf16[64,1024]{1,0:T(8,128)(2,1)S(1)}, u32[]{:S(2)}, u32[]{:S(2)}) collective-permute-start(bf16[64,1024]{1,0:T(8,128)(2,1)S(1)} %get-tuple-element.56), channel_id=1, source_target_pairs={{0,2},{1,3},{2,0},{3,1},{4,6},{5,7},{6,4},{7,5},{8,10},{9,11},{10,... | collective-permute-start | bytes 393224 | tf_op jit(solution)/shard_map/ppermute | solution.py:333
  46.9 9.3 %collective-permute-start.18 = (bf16[64,1024]{1,0:T(8,128)(2,1)S(1)}, bf16[64,1024]{1,0:T(8,128)(2,1)S(1)}, u32[]{:S(2)}, u32[]{:S(2)}) collective-permute-start(bf16[64,1024]{1,0:T(8,128)(2,1)S(1)} %get-tuple-element.57), channel_id=1, source_target_pairs={{0,6},{1,7},{2,4},{3,5},{4,2},{5,3},{6,0},{7,1},{8,14},{9,15},{10,... | collective-permute-start | bytes 393224 | tf_op jit(solution)/shard_map/ppermute | solution.py:333
  50.6 8.5 %collective-permute-start.12 = (bf16[64,1024]{1,0:T(8,128)(2,1)S(1)}, bf16[64,1024]{1,0:T(8,128)(2,1)S(1)}, u32[]{:S(2)}, u32[]{:S(2)}) collective-permute-start(bf16[64,1024]{1,0:T(8,128)(2,1)S(1)} %get-tuple-element.46), channel_id=1, source_target_pairs={{0,4},{1,5},{2,6},{3,7},{4,0},{5,1},{6,2},{7,3},{8,12},{9,13},{10,... | collective-permute-start | bytes 393224 | tf_op jit(solution)/shard_map/ppermute | solution.py:333
  51.2 7.8 %collective-permute-start.13 = (bf16[64,1024]{1,0:T(8,128)(2,1)S(1)}, bf16[64,1024]{1,0:T(8,128)(2,1)S(1)}, u32[]{:S(2)}, u32[]{:S(2)}) collective-permute-start(bf16[64,1024]{1,0:T(8,128)(2,1)S(1)} %get-tuple-element.47), channel_id=1, source_target_pairs={{0,2},{1,3},{2,0},{3,1},{4,6},{5,7},{6,4},{7,5},{8,10},{9,11},{10,... | collective-permute-start | bytes 393224 | tf_op jit(solution)/shard_map/ppermute | solution.py:333
  51.9 8.7 %collective-permute-start.14 = (bf16[64,1024]{1,0:T(8,128)(2,1)S(1)}, bf16[64,1024]{1,0:T(8,128)(2,1)S(1)}, u32[]{:S(2)}, u32[]{:S(2)}) collective-permute-start(bf16[64,1024]{1,0:T(8,128)(2,1)S(1)} %get-tuple-element.48), channel_id=1, source_target_pairs={{0,6},{1,7},{2,4},{3,5},{4,2},{5,3},{6,0},{7,1},{8,14},{9,15},{10,... | collective-permute-start | bytes 393224 | tf_op jit(solution)/shard_map/ppermute | solution.py:333
  56.3 6.4 %collective-permute-start.19 = (bf16[32,1024]{1,0:T(8,128)(2,1)S(1)}, bf16[32,1024]{1,0:T(8,128)(2,1)S(1)}, u32[]{:S(2)}, u32[]{:S(2)}) collective-permute-start(bf16[32,1024]{1,0:T(8,128)(2,1)S(1)} %get-tuple-element.58), channel_id=1, source_target_pairs={{0,16},{1,17},{2,18},{3,19},{4,20},{5,21},{6,22},{7,23},{8,24},{9,... | collective-permute-start | bytes 196616 | tf_op jit(solution)/shard_map/ppermute | solution.py:333
  56.8 6.3 %collective-permute-start.20 = (bf16[32,1024]{1,0:T(8,128)(2,1)S(1)}, bf16[32,1024]{1,0:T(8,128)(2,1)S(1)}, u32[]{:S(2)}, u32[]{:S(2)}) collective-permute-start(bf16[32,1024]{1,0:T(8,128)(2,1)S(1)} %get-tuple-element.59), channel_id=1, source_target_pairs={{0,24},{1,25},{2,26},{3,27},{4,28},{5,29},{6,30},{7,31},{8,16},{9,... | collective-permute-start | bytes 196616 | tf_op jit(solution)/shard_map/ppermute | solution.py:333
  60.7 4.3 %collective-permute-start.15 = (bf16[32,1024]{1,0:T(8,128)(2,1)S(1)}, bf16[32,1024]{1,0:T(8,128)(2,1)S(1)}, u32[]{:S(2)}, u32[]{:S(2)}) collective-permute-start(bf16[32,1024]{1,0:T(8,128)(2,1)S(1)} %get-tuple-element.53), channel_id=1, source_target_pairs={{0,8},{1,9},{2,10},{3,11},{4,12},{5,13},{6,14},{7,15},{8,0},{9,1},... | collective-permute-start | bytes 196616 | tf_op jit(solution)/shard_map/ppermute | solution.py:333

commit v12 on v11

--- a/solution.py
+++ b/solution.py
@@ -218,61 +218,86 @@
     return jnp.transpose(jnp.concatenate([line] * 16, axis=0))
 
 
-def grad_kernel(chunk, order, groups, info, mine, theirs, weight, other_weight, stats, *refs):
-    logit_grad, outs = refs[0], refs[1:len(order) + 1]
+def products_kernel(info, mine, theirs, weight, other_weight, columns, *refs):
+    sums, picks = refs[:2], refs[2:]
     rank, _, shard = coordinates()
-    height, columns = mine.shape
+    height, width_v = mine.shape
     part = height // 4
-    quarters = [chunk, 2 + chunk]
-
-    def rows_of(value):
-        return jnp.concatenate([value[q * part:(q + 1) * part] for q in quarters], axis=0)
-
-    if chunk:
-        table = log_totals(groups, stats, height)
-        refs[-1][...] = table
-    else:
-        table = stats[...]
-    log_total = rows_of(table)[:, 0:1]
-    rows_info = rows_of(info)
-    row_weight, target = rows_info[:, 0:1], rows_info[:, 1:2].astype(jnp.int32)
-
-    def grad_of(logits, shard):
-        column = lax.broadcasted_iota(jnp.int32, (2 * part, columns), 1) + shard * columns
-        probability = jnp.exp(rows_of(logits) - log_total)
-        return (
-            grad_scale * row_weight * (probability - (column == target).astype(jnp.float32))
-        ).astype(jnp.bfloat16)
-
-    grad = grad_of(mine, shard)
-    logit_grad[...] = grad
-    grads = (grad, grad_of(theirs, shard ^ 1))
-    width = outs[0].shape[1]
-    for x in reversed(range(len(outs) // 2)):
+    target = info[:, 1:2].astype(jnp.int32)
+    logits = (mine[...], theirs[...])
+    hits = [
+        lax.broadcasted_iota(jnp.int32, mine.shape, 1) + place * width_v == target
+        for place in (shard, shard ^ 1)
+    ]
+    peak = functools.reduce(
+        jnp.maximum, [jnp.max(value, axis=1, keepdims=True) for value in logits]
+    )
+    hit = sum(
+        jnp.sum(jnp.where(chosen, value - peak, 0.0), axis=1, keepdims=True)
+        for chosen, value in zip(hits, logits)
+    )
+    lane = lax.broadcasted_iota(jnp.int32, columns.shape, 1)
+    columns[...] = jnp.where(lane == 0, peak, hit + peak)
+    factors = [
+        jnp.where(chosen, 0.0, jnp.exp(value - peak)).astype(jnp.bfloat16)
+        for chosen, value in zip(hits, logits)
+    ]
+    one_hots = [chosen.astype(jnp.float32).astype(jnp.bfloat16) for chosen in hits]
+    width = sums[0].shape[2]
+    for x in range(sums[0].shape[0] // 2):
         start = pl.multiple_of((rank ^ 2 * x) * width, width)
         weights = (weight[pl.ds(start, width), :], other_weight[x * width:(x + 1) * width, :])
-        total = sum(
-            lax.dot_general(g, w, (((1,), (1,)), ((), ())), preferred_element_type=jnp.float32)
-            for g, w in zip(grads, weights)
-        )
-        for y in range(2):
-            out = outs[order.index(2 * x + y)]
-            out[...] = total[y * part:(y + 1) * part].astype(out.dtype)
-
-
-def weight_kernel(blocks, skipped, after, near_grad, far_grad, *refs):
+        for lefts, outs in ((factors, sums), (one_hots, picks)):
+            total = sum(
+                lax.dot_general(
+                    left, right, (((1,), (1,)), ((), ())), preferred_element_type=jnp.float32
+                )
+                for left, right in zip(lefts, weights)
+            )
+            for quarter in range(4):
+                out = outs[quarter % 2]
+                piece = total[quarter * part:(quarter + 1) * part]
+                out[2 * x + quarter // 2] = piece.astype(out.dtype)
+
+
+def chunk_grads(chunk, order, info, columns, log_total, sums, picks, outs):
+    part = sums.shape[1]
+    for place, out in zip(order, outs):
+        quarter = place % 2 * 2 + chunk
+        rows = slice(quarter * part, (quarter + 1) * part)
+        scale = grad_scale * info[rows, 0:1]
+        many = scale * jnp.exp(columns[rows, 0:1] - log_total[rows])
+        one = scale * (jnp.exp(columns[rows, 1:2] - log_total[rows]) - 1.0)
+        total = many * sums[place] + one * picks[place].astype(jnp.float32)
+        out[...] = total.astype(out.dtype)
+
+
+def far_kernel(order, groups, info, columns, stats, sums, picks, table, *outs):
+    log_total = log_totals(groups, stats, info.shape[0])
+    table[...] = log_total
+    chunk_grads(1, order, info, columns, log_total[:, 0:1], sums, picks, outs)
+
+
+def near_kernel(order, info, columns, table, sums, picks, logits, logit_grad, *outs):
+    log_total = table[:, 0:1]
+    chunk_grads(0, order, info, columns, log_total, sums, picks, outs)
+    target = info[:, 1:2].astype(jnp.int32) - coordinates()[2] * logits.shape[1]
+    column = lax.broadcasted_iota(jnp.int32, logits.shape, 1)
+    probability = jnp.exp(logits[...] - log_total)
+    logit_grad[...] = (
+        grad_scale * info[:, 0:1] * (probability - (column == target).astype(jnp.float32))
+    ).astype(jnp.bfloat16)
+
+
+def weight_kernel(blocks, skipped, after, logit_grad, *refs):
     pieces, (out, last, done, sems) = refs[skipped:-4], refs[-4:]
     rank = coordinates()[0]
-    part = near_grad.shape[0] // 2
-    logit_grad = jnp.concatenate(
-        [ref[y * part:(y + 1) * part] for y in range(2) for ref in (near_grad, far_grad)], axis=0
-    )
     width = done.shape[0] // len(blocks)
     copies = []
     for place, block in enumerate(blocks):
         done[place * width:(place + 1) * width] = lax.dot_general(
             all_rows(pieces, place, width),
-            logit_grad,
+            logit_grad[...],
             (((0,), (0,)), ((), ())),
             preferred_element_type=jnp.float32,
         ).astype(jnp.bfloat16)
@@ -414,23 +439,35 @@
     other_held = send(away, core=1)
     stats = lax.all_to_all(stats, AXES, 0, 0)
     rows_part = total_rows // 4
+    whole = (ranks, rows_part, width)
+    columns_shape = shape((total_rows, 128), f32)
+    pair_columns, *products = call(
+        products_kernel,
+        (info, logits, other_logits, held, other_held),
+        [VMEM] * 5,
+        (columns_shape,) + (shape(whole, f32),) * 2 + (shape(whole, bf16),) * 2,
+        (VMEM,) * 5,
+        flops=2 * flops,
+    )
+
     order = sorted(range(1, ranks), key=lambda place: (place % 2 + (place > 1), place)) + [0]
-    ends, sums, grads = [None] * zs, [None, None], [None, None]
-    for chunk in (1, 0):
-        outs = (shape((total_rows // 2, columns), bf16),)
-        outs += (shape((rows_part, width), bf16),) * (ranks - 1) + (shape((rows_part, width), f32),)
-        if chunk:
-            outs += (shape((total_rows, 128), f32),)
-        grads[chunk], *going = call(
-            functools.partial(grad_kernel, chunk, order, dps),
-            (info, logits, other_logits, held, other_held, stats if chunk else table),
-            [VMEM] * 6,
-            outs,
-            (VMEM,) * len(outs),
-            flops=flops // 2,
-        )
-        if chunk:
-            table = going.pop()
+    outs = (shape((rows_part, width), bf16),) * (ranks - 1) + (shape((rows_part, width), f32),)
+    ends, sums = [None] * zs, [None, None]
+    table, *going_far = call(
+        functools.partial(far_kernel, order, dps),
+        (info, pair_columns, stats, products[1], products[3]),
+        [VMEM] * 5,
+        (columns_shape, *outs),
+        (VMEM,) * (1 + ranks),
+    )
+    logit_grad, *going_near = call(
+        functools.partial(near_kernel, order),
+        (info, pair_columns, table, products[0], products[2], logits),
+        [VMEM] * 6,
+        (shape((total_rows, columns), bf16), *outs),
+        (VMEM,) * (1 + ranks),
+    )
+    for chunk, going in ((1, going_far), (0, going_near)):
         sums[chunk] = [going[-1]]
         for place, value in zip(order, going[:-1]):
             sums[chunk].append(send(value, y=place % 2, x=place // 2))
@@ -440,8 +477,8 @@
         chosen_rows = rows[2 * first:2 * first + ranks]
         return call(
             functools.partial(weight_kernel, blocks, len(extra)),
-            (after, *grads, *extra, *chosen_rows),
-            [ANY] + [VMEM] * 2 + [HBM] * (len(extra) > 0)
+            (after, logit_grad, *extra, *chosen_rows),
+            [ANY, VMEM] + [HBM] * (len(extra) > 0)
             + [VMEM] * (max(len(extra) - 1, 0) + len(chosen_rows)),
             (shape((depth, columns), bf16), shape((8, 128), f32)),
             (HBM, VMEM),
@@ -450,7 +487,7 @@
                 pltpu.SemaphoreType.DMA((ranks // 2,)),
             ],
             flops=flops // 2,
-            aliases={3: 0} if extra else {},
+            aliases={2: 0} if extra else {},
         )
 
     weight_grad, finished = weight_part(0, sums[0][0])

time: 66.2 us -> 71.5 us (1.080)
  blocking collectives: 13.9 us -> 0 us
  local copies, waits for them, and re-layouts: 0.01 us -> 6.9 us
  starting transfers between devices: 19.9 us -> 25.6 us
  Pallas kernels: 14.5 us -> 18.4 us
  waiting for transfers between devices: 16.9 us -> 19.4 us
    all_to_all x1 -> x0, blocking collectives: 13.9 us -> none  [body(): stats = lax.all_to_all(stats, AXES, 0, 0)]
    unnamed x2 -> x34, local copies, waits for them, and re-layouts: 0.01 us -> 6.9 us
    pallas_call x14 -> x15, Pallas kernels: 14.5 us -> 18.4 us  [call(): pl.pallas_call(kernel, out_shape=out_shape, in_specs=in_specs, out_specs=...]
    all_to_all x0 -> x1, starting transfers between devices: none -> 3.76 us  [body(): stats = lax.all_to_all(stats, AXES, 0, 0)]
    ppermute x21, waiting for transfers between devices: 16.9 us -> 19.4 us  [send(): return lax.ppermute(value, AXES, pairs)]
    ppermute x21, starting transfers between devices: 19.9 us -> 21.9 us  [send(): return lax.ppermute(value, AXES, pairs)]
  transfers between devices with their start and end apart: 21 -> 22, of which waited for: 11 -> 9; matrix products, arithmetic and copies ran while one was open for 0% -> 0% of each run, Pallas kernels for 14% -> 19%
where the time goes in v12:
time: 71.5 us; the launch traced here: 71.2 us
  starting transfers between devices  25.6 us (36%)
  waiting for transfers between devices  19.4 us (27%)
  Pallas kernels  18.4 us (26%)
  local copies, waits for them, and re-layouts  6.9 us (10%)
  between operations  0.87 us (1%)
    ppermute x21, starting transfers between devices, send(): return lax.ppermute(value, AXES, pairs)  21.9 us
    ppermute x21, waiting for transfers between devices, send(): return lax.ppermute(value, AXES, pairs)  19.4 us
    pallas_call x15, Pallas kernels, call(): pl.pallas_call(kernel, out_shape=out_shape, in_specs=in_specs, out_specs=...  18.4 us
    unnamed x34, local copies, waits for them, and re-layouts  6.9 us
    all_to_all x1, starting transfers between devices, body(): stats = lax.all_to_all(stats, AXES, 0, 0)  3.76 us
  transfers between devices with their start and end apart: 22, of which 9 were waited for; matrix products, arithmetic and copies ran while one was open for 0% of the time, Pallas kernels for 19%

profile of v12, /device:TPU:0, one launch (start us, length us, event | category | flops | bytes accessed | tf_op | source)
XLA Modules:
  0.0 71.2 jit_solution(17862010478121027827)
XLA Ops:
  0.6 1.2 %shard_map.85 = (bf16[32,1152]{1,0:T(8,128)(2,1)S(1)}, bf16[32,128]{1,0:T(8,128)(2,1)S(1)}) custom-call(bf16[128,1024]{1,0:T(8,128)(2,1)} %hidden_hbm.1, s32[1,128]{1,0:T(1,128)} %bitcast.6, s32[1,128]{1,0:T(1,128)} %bitcast.7, s32[1,128]{1,0:T(1,128)} %bitcast.8), custom_call_target="tpu_custom_call" | custom-call | bytes 345600 | tf_op jit(solution)/shard_map/pallas_call | solution.py:32
  2.5 3.0 %collective-permute-start.2 = (bf16[32,1152]{1,0:T(8,128)(2,1)S(1)}, bf16[32,1152]{1,0:T(8,128)(2,1)S(1)}, u32[]{:S(2)}, u32[]{:S(2)}) collective-permute-start(bf16[32,1152]{1,0:T(8,128)(2,1)S(1)} %get-tuple-element.37.refs_0_), channel_id=1, source_target_pairs={{0,8},{1,9},{2,10},{3,11},{4,12},{5,13},{6,14},{7,15},{8,0},{9,1},... | collective-permute-start | bytes 221192 | tf_op jit(solution)/shard_map/ppermute | solution.py:358
  5.5 2.5 %collective-permute-start.1 = (bf16[32,1152]{1,0:T(8,128)(2,1)S(1)}, bf16[32,1152]{1,0:T(8,128)(2,1)S(1)}, u32[]{:S(2)}, u32[]{:S(2)}) collective-permute-start(bf16[32,1152]{1,0:T(8,128)(2,1)S(1)} %get-tuple-element.37.refs_0_), channel_id=1, source_target_pairs={{0,24},{1,25},{2,26},{3,27},{4,28},{5,29},{6,30},{7,31},{8,16},{9,... | collective-permute-start | bytes 221192 | tf_op jit(solution)/shard_map/ppermute | solution.py:358
  8.1 4.6 %collective-permute-done.1.refs_2_ = bf16[32,1152]{1,0:T(8,128)(2,1)S(1)} collective-permute-done((bf16[32,1152]{1,0:T(8,128)(2,1)S(1)}, bf16[32,1152]{1,0:T(8,128)(2,1)S(1)}, u32[]{:S(2)}, u32[]{:S(2)}) %collective-permute-start.1) | collective-permute-done | bytes 73760 | tf_op jit(solution)/shard_map/ppermute | solution.py:358
  12.7 2.3 %collective-permute-done.refs_1_ = bf16[32,1152]{1,0:T(8,128)(2,1)S(1)} collective-permute-done((bf16[32,1152]{1,0:T(8,128)(2,1)S(1)}, bf16[32,1152]{1,0:T(8,128)(2,1)S(1)}, u32[]{:S(2)}, u32[]{:S(2)}) %collective-permute-start) | collective-permute-done | bytes 73760 | tf_op jit(solution)/shard_map/ppermute | solution.py:358
  15.1 1.6 %collective-permute-start.3 = (bf16[128,1152]{1,0:T(8,128)(2,1)S(1)}, bf16[128,1152]{1,0:T(8,128)(2,1)S(1)}, u32[]{:S(2)}, u32[]{:S(2)}) collective-permute-start(bf16[128,1152]{1,0:T(8,128)(2,1)S(1)} %get-tuple-element.38.line), channel_id=1, source_target_pairs={{0,4},{1,5},{2,6},{3,7},{4,0},{5,1},{6,2},{7,3},{8,12},{9,13},{10,... | collective-permute-start | bytes 884744 | tf_op jit(solution)/shard_map/ppermute | solution.py:358
  16.6 1.4 %collective-permute-start.5 = (bf16[128,1024]{1,0:T(8,128)(2,1)S(1)}, bf16[128,1024]{1,0:T(8,128)(2,1)S(1)}, u32[]{:S(2)}, u32[]{:S(2)}) collective-permute-start(bf16[128,1024]{1,0:T(8,128)(2,1)S(1)} %get-tuple-element.41), channel_id=1, source_target_pairs={{0,6},{1,7},{2,4},{3,5},{4,2},{5,3},{6,0},{7,1},{8,14},{9,15},{10,... | collective-permute-start | bytes 786440 | tf_op jit(solution)/shard_map/ppermute | solution.py:358
  18.6 2.9 %shard_map.87 = (bf16[4096,512]{1,0:T(8,128)(2,1)S(1)}, bf16[2048,512]{1,0:T(8,128)(2,1)S(1)}, bf16[128,1152]{1,0:T(8,128)(2,1)S(1)}) custom-call(bf16[128,1152]{1,0:T(8,128)(2,1)S(1)} %get-tuple-element.38.line, bf16[4096,512]{1,0:T(8,128)(2,1)} %weight.1), custom_call_target="tpu_custom_call" | custom-call | bytes 11075584 | tf_op jit(solution)/shard_map/pallas_call | solution.py:32
  21.6 8.0 %collective-permute-done.3.refs_1_ = bf16[128,1152]{1,0:T(8,128)(2,1)S(1)} collective-permute-done((bf16[128,1152]{1,0:T(8,128)(2,1)S(1)}, bf16[128,1152]{1,0:T(8,128)(2,1)S(1)}, u32[]{:S(2)}, u32[]{:S(2)}) %collective-permute-start.3) | collective-permute-done | bytes 294944 | tf_op jit(solution)/shard_map/ppermute | solution.py:358
  30.5 0.7 shard_map.89.partial
  31.9 1.8 %shard_map.90 = (f32[256,512]{1,0:T(8,128)}, f32[32,1,640]{2,1,0:T(1,128)}) custom-call(f32[256,128]{1,0:T(8,128)S(1)} %shard_map.88.info.refs_1_, f32[256,512]{1,0:T(8,128)S(1)} %shard_map.89.partial, bf16[4096,512]{1,0:T(8,128)(2,1)S(1)} %get-tuple-element.40.weight, bf16[128,1152]{1,0:T(8,128)(2,1)S(1)} %collective-permute-done.6.refs_0_.refs_2_, ...), custom_call_target="tpu_custom_call" | custom-call | flops 536870912 | bytes 6569984 | tf_op jit(solution)/shard_map/pallas_call | solution.py:32
  34.3 3.8 %all-to-all-start = ((f32[32,1,640]{2,1,0:T(1,128)}), f32[32,1,640]{2,1,0:T(1,128)S(1)}, u32[]{:S(2)}, u32[]{:S(2)}) async-start(f32[32,1,640]{2,1,0:T(1,128)} %get-tuple-element.44.after), calls=%async_computation | async-start | bytes 163840 | tf_op jit(solution)/shard_map/all_to_all | solution.py:440
  38.1 0.7 %collective-permute-done.10.theirs = f32[256,512]{1,0:T(8,128)} collective-permute-done((f32[256,512]{1,0:T(8,128)}, f32[256,512]{1,0:T(8,128)}, u32[]{:S(2)}, u32[]{:S(2)}) %collective-permute-start.10) | collective-permute-done | bytes 524320 | tf_op jit(solution)/shard_map/ppermute | solution.py:358
  38.8 2.2 %copy-done.1 = bf16[4096,512]{1,0:T(8,128)(2,1)S(1)} copy-done((bf16[4096,512]{1,0:T(8,128)(2,1)S(1)}, bf16[4096,512]{1,0:T(8,128)(2,1)}, u32[]{:S(2)}) %copy-start.1) | copy-done | bytes 4194328
  41.0 4.5 %shard_map.92 = (f32[256,128]{1,0:T(8,128)S(1)}, f32[4,64,1024]{2,1,0:T(8,128)S(1)}, f32[4,64,1024]{2,1,0:T(8,128)S(1)}, bf16[4,64,1024]{2,1,0:T(8,128)(2,1)S(1)}, bf16[4,64,1024]{2,1,0:T(8,128)(2,1)S(1)}) custom-call(f32[256,128]{1,0:T(8,128)S(1)} %shard_map.88.info.refs_1_, f32[256,512]{1,0:T(8,128)} %get-tuple-element.42.mine.logits, ...), custom_call_target="tpu_custom_call" | custom-call | flops 2147483648 | bytes 10747904 | tf_op jit(solution)/shard_map/pallas_call | solution.py:32
  45.6 1.0 %copy-done.6 = f32[4,64,1024]{2,1,0:T(8,128)} copy-done((f32[4,64,1024]{2,1,0:T(8,128)}, f32[4,64,1024]{2,1,0:T(8,128)S(1)}, u32[]{:S(2)}) %copy-start.6) | copy-done | bytes 1048600
  46.5 0.8 %copy-done.8 = bf16[4,64,1024]{2,1,0:T(8,128)(2,1)} copy-done((bf16[4,64,1024]{2,1,0:T(8,128)(2,1)}, bf16[4,64,1024]{2,1,0:T(8,128)(2,1)S(1)}, u32[]{:S(2)}) %copy-start.8) | copy-done | bytes 524312
  47.3 1.3 %copy-done.7 = f32[4,64,1024]{2,1,0:T(8,128)S(1)} copy-done((f32[4,64,1024]{2,1,0:T(8,128)S(1)}, f32[4,64,1024]{2,1,0:T(8,128)}, u32[]{:S(2)}) %copy-start.7) | copy-done | bytes 1048600
  48.6 1.0 %copy-done.9 = bf16[4,64,1024]{2,1,0:T(8,128)(2,1)S(1)} copy-done((bf16[4,64,1024]{2,1,0:T(8,128)(2,1)S(1)}, bf16[4,64,1024]{2,1,0:T(8,128)(2,1)}, u32[]{:S(2)}) %copy-start.9) | copy-done | bytes 524312
  50.3 1.6 %collective-permute-start.16 = (bf16[64,1024]{1,0:T(8,128)(2,1)S(1)}, bf16[64,1024]{1,0:T(8,128)(2,1)S(1)}, u32[]{:S(2)}, u32[]{:S(2)}) collective-permute-start(bf16[64,1024]{1,0:T(8,128)(2,1)S(1)} %get-tuple-element.63), channel_id=1, source_target_pairs={{0,4},{1,5},{2,6},{3,7},{4,0},{5,1},{6,2},{7,3},{8,12},{9,13},{10,... | collective-permute-start | bytes 393224 | tf_op jit(solution)/shard_map/ppermute | solution.py:358
  51.9 1.5 %collective-permute-start.17 = (bf16[64,1024]{1,0:T(8,128)(2,1)S(1)}, bf16[64,1024]{1,0:T(8,128)(2,1)S(1)}, u32[]{:S(2)}, u32[]{:S(2)}) collective-permute-start(bf16[64,1024]{1,0:T(8,128)(2,1)S(1)} %get-tuple-element.64), channel_id=1, source_target_pairs={{0,2},{1,3},{2,0},{3,1},{4,6},{5,7},{6,4},{7,5},{8,10},{9,11},{10,... | collective-permute-start | bytes 393224 | tf_op jit(solution)/shard_map/ppermute | solution.py:358
  53.9 1.5 %shard_map.94 = (bf16[256,512]{1,0:T(8,128)(2,1)S(1)}, bf16[64,1024]{1,0:T(8,128)(2,1)S(1)}, bf16[64,1024]{1,0:T(8,128)(2,1)S(1)}, bf16[64,1024]{1,0:T(8,128)(2,1)S(1)}, f32[64,1024]{1,0:T(8,128)S(1)}) custom-call(f32[256,128]{1,0:T(8,128)S(1)} %shard_map.88.info.refs_1_, f32[256,128]{1,0:T(8,128)S(1)} %get-tuple-element.45.columns, ...), custom_call_target="tpu_custom_call" | custom-call | bytes 3407872 | tf_op jit(solution)/shard_map/pallas_call | solution.py:32
  55.4 1.6 %collective-permute-start.12 = (bf16[64,1024]{1,0:T(8,128)(2,1)S(1)}, bf16[64,1024]{1,0:T(8,128)(2,1)S(1)}, u32[]{:S(2)}, u32[]{:S(2)}) collective-permute-start(bf16[64,1024]{1,0:T(8,128)(2,1)S(1)} %get-tuple-element.54), channel_id=1, source_target_pairs={{0,4},{1,5},{2,6},{3,7},{4,0},{5,1},{6,2},{7,3},{8,12},{9,13},{10,... | collective-permute-start | bytes 393224 | tf_op jit(solution)/shard_map/ppermute | solution.py:358
  57.0 1.5 %collective-permute-start.13 = (bf16[64,1024]{1,0:T(8,128)(2,1)S(1)}, bf16[64,1024]{1,0:T(8,128)(2,1)S(1)}, u32[]{:S(2)}, u32[]{:S(2)}) collective-permute-start(bf16[64,1024]{1,0:T(8,128)(2,1)S(1)} %get-tuple-element.55), channel_id=1, source_target_pairs={{0,2},{1,3},{2,0},{3,1},{4,6},{5,7},{6,4},{7,5},{8,10},{9,11},{10,... | collective-permute-start | bytes 393224 | tf_op jit(solution)/shard_map/ppermute | solution.py:358
  59.0 1.8 %shard_map.95 = (bf16[4096,512]{1,0:T(8,128)(2,1)}, f32[8,128]{1,0:T(8,128)S(1)}) custom-call(f32[64,1024]{1,0:T(8,128)S(1)} %get-tuple-element.51.after.kept, bf16[256,512]{1,0:T(8,128)(2,1)S(1)} %get-tuple-element.52.logit_grad, bf16[128,1152]{1,0:T(8,128)(2,1)S(1)} %get-tuple-element.39.refs_0_, bf16[128,1152]{1,0:T(8,128)(2,1)S(1)} %collective-permute-done.3.refs_1_, ...), custom_call_target="tpu_custom_call" | custom-call | flops 536870912 | bytes 5902336 | tf_op jit(solution)/shard_map/pallas_call | solution.py:32
  60.9 2.0 %collective-permute-start.19 = (bf16[32,1024]{1,0:T(8,128)(2,1)S(1)}, bf16[32,1024]{1,0:T(8,128)(2,1)S(1)}, u32[]{:S(2)}, u32[]{:S(2)}) collective-permute-start(bf16[32,1024]{1,0:T(8,128)(2,1)S(1)} %get-tuple-element.66), channel_id=1, source_target_pairs={{0,16},{1,17},{2,18},{3,19},{4,20},{5,21},{6,22},{7,23},{8,24},{9,... | collective-permute-start | bytes 196616 | tf_op jit(solution)/shard_map/ppermute | solution.py:358
  62.9 1.5 %collective-permute-start.20 = (bf16[32,1024]{1,0:T(8,128)(2,1)S(1)}, bf16[32,1024]{1,0:T(8,128)(2,1)S(1)}, u32[]{:S(2)}, u32[]{:S(2)}) collective-permute-start(bf16[32,1024]{1,0:T(8,128)(2,1)S(1)} %get-tuple-element.67), channel_id=1, source_target_pairs={{0,24},{1,25},{2,26},{3,27},{4,28},{5,29},{6,30},{7,31},{8,16},{9,... | collective-permute-start | bytes 196616 | tf_op jit(solution)/shard_map/ppermute | solution.py:358
  64.3 1.4 %collective-permute-done.14.refs_2_ = bf16[64,1024]{1,0:T(8,128)(2,1)S(1)} collective-permute-done((bf16[64,1024]{1,0:T(8,128)(2,1)S(1)}, bf16[64,1024]{1,0:T(8,128)(2,1)S(1)}, u32[]{:S(2)}, u32[]{:S(2)}) %collective-permute-start.14) | collective-permute-done | bytes 131104 | tf_op jit(solution)/shard_map/ppermute | solution.py:358
  65.9 0.9 %collective-permute-start.15 = (bf16[32,1024]{1,0:T(8,128)(2,1)S(1)}, bf16[32,1024]{1,0:T(8,128)(2,1)S(1)}, u32[]{:S(2)}, u32[]{:S(2)}) collective-permute-start(bf16[32,1024]{1,0:T(8,128)(2,1)S(1)} %get-tuple-element.61), channel_id=1, source_target_pairs={{0,8},{1,9},{2,10},{3,11},{4,12},{5,13},{6,14},{7,15},{8,0},{9,1},... | collective-permute-start | bytes 196616 | tf_op jit(solution)/shard_map/ppermute | solution.py:358
  66.8 1.8 %shard_map.97 = (bf16[4096,512]{1,0:T(8,128)(2,1)}, f32[8,128]{1,0:T(8,128)S(1)}) custom-call(f32[32,1024]{1,0:T(8,128)S(1)} %get-tuple-element.57.after.refs_0_, bf16[256,512]{1,0:T(8,128)(2,1)S(1)} %get-tuple-element.52.logit_grad, bf16[4096,512]{1,0:T(8,128)(2,1)} %get-tuple-element.58.refs_0_, ...), custom_call_target="tpu_custom_call", output_to_operand_aliasing={{0}: (2, {})} | custom-call | flops 536870912 | bytes 10178560 | tf_op jit(solution)/shard_map/pallas_call | solution.py:32
  69.0 1.1 %collective-permute-done.15.refs_1_ = bf16[32,1024]{1,0:T(8,128)(2,1)S(1)} collective-permute-done((bf16[32,1024]{1,0:T(8,128)(2,1)S(1)}, bf16[32,1024]{1,0:T(8,128)(2,1)S(1)}, u32[]{:S(2)}, u32[]{:S(2)}) %collective-permute-start.15) | collective-permute-done | bytes 65568 | tf_op jit(solution)/shard_map/ppermute | solution.py:358
  70.2 1.0 %shard_map.99 = (bf16[128,1024]{1,0:T(8,128)(2,1)}, f32[1,1]{1,0:T(1,128)}) custom-call(f32[8,128]{1,0:T(8,128)S(1)} %get-tuple-element.59.last, bf16[32,128]{1,0:T(8,128)(2,1)S(1)} %copy-done.15, f32[32,1024]{1,0:T(8,128)S(1)} %get-tuple-element.57.after.refs_0_, bf16[32,1024]{1,0:T(8,128)(2,1)S(1)} %collective-permute-done.15.refs_1_, ...), custom_call_target="tpu_custom_call" | custom-call | bytes 602116 | tf_op jit(solution)/shard_map/pallas_call | solution.py:32
  (61 shorter events, 5.8 us)
Async XLA Ops:
  0.6 29.5 %copy-start.16 = (f32[32]{0:T(128)S(1)}, f32[32]{0:T(128)}, u32[]{:S(2)}) copy-start(f32[32]{0:T(128)} %param.11) | copy-start | bytes 388
  2.5 5.6 %collective-permute-start.2 = (bf16[32,1152]{1,0:T(8,128)(2,1)S(1)}, bf16[32,1152]{1,0:T(8,128)(2,1)S(1)}, u32[]{:S(2)}, u32[]{:S(2)}) collective-permute-start(bf16[32,1152]{1,0:T(8,128)(2,1)S(1)} %get-tuple-element.37.refs_0_), channel_id=1, source_target_pairs={{0,8},{1,9},{2,10},{3,11},{4,12},{5,13},{6,14},{7,15},{8,0},{9,1},... | collective-permute-start | bytes 221192 | tf_op jit(solution)/shard_map/ppermute | solution.py:358
  5.5 7.2 %collective-permute-start.1 = (bf16[32,1152]{1,0:T(8,128)(2,1)S(1)}, bf16[32,1152]{1,0:T(8,128)(2,1)S(1)}, u32[]{:S(2)}, u32[]{:S(2)}) collective-permute-start(bf16[32,1152]{1,0:T(8,128)(2,1)S(1)} %get-tuple-element.37.refs_0_), channel_id=1, source_target_pairs={{0,24},{1,25},{2,26},{3,27},{4,28},{5,29},{6,30},{7,31},{8,16},{9,... | collective-permute-start | bytes 221192 | tf_op jit(solution)/shard_map/ppermute | solution.py:358
  8.0 7.1 %collective-permute-start = (bf16[32,1152]{1,0:T(8,128)(2,1)S(1)}, bf16[32,1152]{1,0:T(8,128)(2,1)S(1)}, u32[]{:S(2)}, u32[]{:S(2)}) collective-permute-start(bf16[32,1152]{1,0:T(8,128)(2,1)S(1)} %get-tuple-element.37.refs_0_), channel_id=1, source_target_pairs={{0,16},{1,17},{2,18},{3,19},{4,20},{5,21},{6,22},{7,23},{8,24},{9,... | collective-permute-start | bytes 221192 | tf_op jit(solution)/shard_map/ppermute | solution.py:358
  15.1 14.5 %collective-permute-start.3 = (bf16[128,1152]{1,0:T(8,128)(2,1)S(1)}, bf16[128,1152]{1,0:T(8,128)(2,1)S(1)}, u32[]{:S(2)}, u32[]{:S(2)}) collective-permute-start(bf16[128,1152]{1,0:T(8,128)(2,1)S(1)} %get-tuple-element.38.line), channel_id=1, source_target_pairs={{0,4},{1,5},{2,6},{3,7},{4,0},{5,1},{6,2},{7,3},{8,12},{9,13},{10,... | collective-permute-start | bytes 884744 | tf_op jit(solution)/shard_map/ppermute | solution.py:358
  16.6 12.9 %collective-permute-start.5 = (bf16[128,1024]{1,0:T(8,128)(2,1)S(1)}, bf16[128,1024]{1,0:T(8,128)(2,1)S(1)}, u32[]{:S(2)}, u32[]{:S(2)}) collective-permute-start(bf16[128,1024]{1,0:T(8,128)(2,1)S(1)} %get-tuple-element.41), channel_id=1, source_target_pairs={{0,6},{1,7},{2,4},{3,5},{4,2},{5,3},{6,0},{7,1},{8,14},{9,15},{10,... | collective-permute-start | bytes 786440 | tf_op jit(solution)/shard_map/ppermute | solution.py:358
  18.1 12.0 %collective-permute-start.4 = (bf16[128,1024]{1,0:T(8,128)(2,1)S(1)}, bf16[128,1024]{1,0:T(8,128)(2,1)S(1)}, u32[]{:S(2)}, u32[]{:S(2)}) collective-permute-start(bf16[128,1024]{1,0:T(8,128)(2,1)S(1)} %get-tuple-element.41), channel_id=1, source_target_pairs={{0,2},{1,3},{2,0},{3,1},{4,6},{5,7},{6,4},{7,5},{8,10},{9,11},{10,... | collective-permute-start | bytes 786440 | tf_op jit(solution)/shard_map/ppermute | solution.py:358
  21.5 12.2 %copy-start = (bf16[4096,512]{1,0:T(8,128)(2,1)}, bf16[4096,512]{1,0:T(8,128)(2,1)S(1)}, u32[]{:S(2)}) copy-start(bf16[4096,512]{1,0:T(8,128)(2,1)S(1)} %get-tuple-element.40.weight) | copy-start | bytes 12582916
  21.5 9.8 %collective-permute-start.6 = (bf16[128,1152]{1,0:T(8,128)(2,1)S(1)}, bf16[128,1152]{1,0:T(8,128)(2,1)S(1)}, u32[]{:S(2)}, u32[]{:S(2)}) collective-permute-start(bf16[128,1152]{1,0:T(8,128)(2,1)S(1)} %get-tuple-element.39.refs_0_), channel_id=1, source_target_pairs={{0,1},{1,0},{2,3},{3,2},{4,5},{5,4},{6,7},{7,6},{8,9},{9,8},{10,11... | collective-permute-start | bytes 884744 | tf_op jit(solution)/shard_map/ppermute | solution.py:358
  29.6 2.3 %collective-permute-start.7 = (bf16[128,1152]{1,0:T(8,128)(2,1)S(1)}, bf16[128,1152]{1,0:T(8,128)(2,1)S(1)}, u32[]{:S(2)}, u32[]{:S(2)}) collective-permute-start(bf16[128,1152]{1,0:T(8,128)(2,1)S(1)} %collective-permute-done.3.refs_1_), channel_id=1, source_target_pairs={{0,1},{1,0},{2,3},{3,2},{4,5},{5,4},{6,7},{7,6},{8,9},{9,8},{10,11... | collective-permute-start | bytes 884744 | tf_op jit(solution)/shard_map/ppermute | solution.py:358
  29.6 2.0 %collective-permute-start.9 = (bf16[128,1024]{1,0:T(8,128)(2,1)S(1)}, bf16[128,1024]{1,0:T(8,128)(2,1)S(1)}, u32[]{:S(2)}, u32[]{:S(2)}) collective-permute-start(bf16[128,1024]{1,0:T(8,128)(2,1)S(1)} %collective-permute-done.5.refs_3_.refs_5_), channel_id=1, source_target_pairs={{0,1},{1,0},{2,3},{3,2},{4,5},{5,4},{6,7},{7,6},{8,9},{9,8},{10,11... | collective-permute-start | bytes 786440 | tf_op jit(solution)/shard_map/ppermute | solution.py:358
  30.1 1.8 %collective-permute-start.8 = (bf16[128,1024]{1,0:T(8,128)(2,1)S(1)}, bf16[128,1024]{1,0:T(8,128)(2,1)S(1)}, u32[]{:S(2)}, u32[]{:S(2)}) collective-permute-start(bf16[128,1024]{1,0:T(8,128)(2,1)S(1)} %collective-permute-done.4.refs_2_.refs_4_), channel_id=1, source_target_pairs={{0,1},{1,0},{2,3},{3,2},{4,5},{5,4},{6,7},{7,6},{8,9},{9,8},{10,11... | collective-permute-start | bytes 786440 | tf_op jit(solution)/shard_map/ppermute | solution.py:358
  31.3 2.4 %copy-start.10 = (bf16[128,1152]{1,0:T(8,128)(2,1)}, bf16[128,1152]{1,0:T(8,128)(2,1)S(1)}, u32[]{:S(2)}) copy-start(bf16[128,1152]{1,0:T(8,128)(2,1)S(1)} %collective-permute-done.6.refs_0_.refs_2_) | copy-start | bytes 884740
  31.5 2.2 %copy-start.2 = (bf16[128,1024]{1,0:T(8,128)(2,1)}, bf16[128,1024]{1,0:T(8,128)(2,1)S(1)}, u32[]{:S(2)}) copy-start(bf16[128,1024]{1,0:T(8,128)(2,1)S(1)} %collective-permute-done.9.refs_3_.refs_7_) | copy-start | bytes 786436
  33.7 5.1 %collective-permute-start.11 = (bf16[2048,512]{1,0:T(8,128)(2,1)S(1)}, bf16[2048,512]{1,0:T(8,128)(2,1)}, u32[]{:S(2)}, u32[]{:S(2)}) collective-permute-start(bf16[2048,512]{1,0:T(8,128)(2,1)S(1)} %shard_map.91), channel_id=1, source_target_pairs={{0,1},{1,0},{2,3},{3,2},{4,5},{5,4},{6,7},{7,6},{8,9},{9,8},{10,11... | collective-permute-start | bytes 6291464 | tf_op jit(solution)/shard_map/ppermute | solution.py:358
  33.9 4.9 %collective-permute-start.10 = (f32[256,512]{1,0:T(8,128)}, f32[256,512]{1,0:T(8,128)}, u32[]{:S(2)}, u32[]{:S(2)}) collective-permute-start(f32[256,512]{1,0:T(8,128)} %get-tuple-element.42.mine.logits), channel_id=1, source_target_pairs={{0,1},{1,0},{2,3},{3,2},{4,5},{5,4},{6,7},{7,6},{8,9},{9,8},{10,11... | collective-permute-start | bytes 1572872 | tf_op jit(solution)/shard_map/ppermute | solution.py:358
  34.3 13.1 %all-to-all-start = ((f32[32,1,640]{2,1,0:T(1,128)}), f32[32,1,640]{2,1,0:T(1,128)S(1)}, u32[]{:S(2)}, u32[]{:S(2)}) async-start(f32[32,1,640]{2,1,0:T(1,128)} %get-tuple-element.44.after), calls=%async_computation | async-start | bytes 163840 | tf_op jit(solution)/shard_map/all_to_all | solution.py:440
  38.8 2.2 %copy-start.1 = (bf16[4096,512]{1,0:T(8,128)(2,1)S(1)}, bf16[4096,512]{1,0:T(8,128)(2,1)}, u32[]{:S(2)}) copy-start(bf16[4096,512]{1,0:T(8,128)(2,1)} %copy-done) | copy-start | bytes 12582916
  47.3 19.4 %copy-start.3 = (bf16[128,1024]{1,0:T(8,128)(2,1)S(1)}, bf16[128,1024]{1,0:T(8,128)(2,1)}, u32[]{:S(2)}) copy-start(bf16[128,1024]{1,0:T(8,128)(2,1)} %copy-done.2) | copy-start | bytes 786436
  47.3 19.4 %copy-start.5 = (bf16[128,1024]{1,0:T(8,128)(2,1)S(1)}, bf16[128,1024]{1,0:T(8,128)(2,1)}, u32[]{:S(2)}) copy-start(bf16[128,1024]{1,0:T(8,128)(2,1)} %copy-done.4) | copy-start | bytes 786436
  49.7 9.3 %copy-start.11 = (bf16[128,1152]{1,0:T(8,128)(2,1)S(1)}, bf16[128,1152]{1,0:T(8,128)(2,1)}, u32[]{:S(2)}) copy-start(bf16[128,1152]{1,0:T(8,128)(2,1)} %copy-done.10) | copy-start | bytes 884740
  49.7 9.3 %copy-start.13 = (bf16[128,1152]{1,0:T(8,128)(2,1)S(1)}, bf16[128,1152]{1,0:T(8,128)(2,1)}, u32[]{:S(2)}) copy-start(bf16[128,1152]{1,0:T(8,128)(2,1)} %copy-done.12) | copy-start | bytes 884740
  50.3 8.2 %collective-permute-start.16 = (bf16[64,1024]{1,0:T(8,128)(2,1)S(1)}, bf16[64,1024]{1,0:T(8,128)(2,1)S(1)}, u32[]{:S(2)}, u32[]{:S(2)}) collective-permute-start(bf16[64,1024]{1,0:T(8,128)(2,1)S(1)} %get-tuple-element.63), channel_id=1, source_target_pairs={{0,4},{1,5},{2,6},{3,7},{4,0},{5,1},{6,2},{7,3},{8,12},{9,13},{10,... | collective-permute-start | bytes 393224 | tf_op jit(solution)/shard_map/ppermute | solution.py:358
  51.9 8.9 %collective-permute-start.17 = (bf16[64,1024]{1,0:T(8,128)(2,1)S(1)}, bf16[64,1024]{1,0:T(8,128)(2,1)S(1)}, u32[]{:S(2)}, u32[]{:S(2)}) collective-permute-start(bf16[64,1024]{1,0:T(8,128)(2,1)S(1)} %get-tuple-element.64), channel_id=1, source_target_pairs={{0,2},{1,3},{2,0},{3,1},{4,6},{5,7},{6,4},{7,5},{8,10},{9,11},{10,... | collective-permute-start | bytes 393224 | tf_op jit(solution)/shard_map/ppermute | solution.py:358
  53.4 7.4 %collective-permute-start.18 = (bf16[64,1024]{1,0:T(8,128)(2,1)S(1)}, bf16[64,1024]{1,0:T(8,128)(2,1)S(1)}, u32[]{:S(2)}, u32[]{:S(2)}) collective-permute-start(bf16[64,1024]{1,0:T(8,128)(2,1)S(1)} %get-tuple-element.65), channel_id=1, source_target_pairs={{0,6},{1,7},{2,4},{3,5},{4,2},{5,3},{6,0},{7,1},{8,14},{9,15},{10,... | collective-permute-start | bytes 393224 | tf_op jit(solution)/shard_map/ppermute | solution.py:358
  55.4 8.9 %collective-permute-start.12 = (bf16[64,1024]{1,0:T(8,128)(2,1)S(1)}, bf16[64,1024]{1,0:T(8,128)(2,1)S(1)}, u32[]{:S(2)}, u32[]{:S(2)}) collective-permute-start(bf16[64,1024]{1,0:T(8,128)(2,1)S(1)} %get-tuple-element.54), channel_id=1, source_target_pairs={{0,4},{1,5},{2,6},{3,7},{4,0},{5,1},{6,2},{7,3},{8,12},{9,13},{10,... | collective-permute-start | bytes 393224 | tf_op jit(solution)/shard_map/ppermute | solution.py:358
  57.0 7.4 %collective-permute-start.13 = (bf16[64,1024]{1,0:T(8,128)(2,1)S(1)}, bf16[64,1024]{1,0:T(8,128)(2,1)S(1)}, u32[]{:S(2)}, u32[]{:S(2)}) collective-permute-start(bf16[64,1024]{1,0:T(8,128)(2,1)S(1)} %get-tuple-element.55), channel_id=1, source_target_pairs={{0,2},{1,3},{2,0},{3,1},{4,6},{5,7},{6,4},{7,5},{8,10},{9,11},{10,... | collective-permute-start | bytes 393224 | tf_op jit(solution)/shard_map/ppermute | solution.py:358
  58.5 7.3 %collective-permute-start.14 = (bf16[64,1024]{1,0:T(8,128)(2,1)S(1)}, bf16[64,1024]{1,0:T(8,128)(2,1)S(1)}, u32[]{:S(2)}, u32[]{:S(2)}) collective-permute-start(bf16[64,1024]{1,0:T(8,128)(2,1)S(1)} %get-tuple-element.56), channel_id=1, source_target_pairs={{0,6},{1,7},{2,4},{3,5},{4,2},{5,3},{6,0},{7,1},{8,14},{9,15},{10,... | collective-permute-start | bytes 393224 | tf_op jit(solution)/shard_map/ppermute | solution.py:358
  60.8 9.4 %copy-start.15 = (bf16[32,128]{1,0:T(8,128)(2,1)S(1)}, bf16[32,128]{1,0:T(8,128)(2,1)}, u32[]{:S(2)}) copy-start(bf16[32,128]{1,0:T(8,128)(2,1)} %copy-done.14) | copy-start | bytes 24580
  60.9 7.7 %collective-permute-start.19 = (bf16[32,1024]{1,0:T(8,128)(2,1)S(1)}, bf16[32,1024]{1,0:T(8,128)(2,1)S(1)}, u32[]{:S(2)}, u32[]{:S(2)}) collective-permute-start(bf16[32,1024]{1,0:T(8,128)(2,1)S(1)} %get-tuple-element.66), channel_id=1, source_target_pairs={{0,16},{1,17},{2,18},{3,19},{4,20},{5,21},{6,22},{7,23},{8,24},{9,... | collective-permute-start | bytes 196616 | tf_op jit(solution)/shard_map/ppermute | solution.py:358
  62.9 6.2 %collective-permute-start.20 = (bf16[32,1024]{1,0:T(8,128)(2,1)S(1)}, bf16[32,1024]{1,0:T(8,128)(2,1)S(1)}, u32[]{:S(2)}, u32[]{:S(2)}) collective-permute-start(bf16[32,1024]{1,0:T(8,128)(2,1)S(1)} %get-tuple-element.67), channel_id=1, source_target_pairs={{0,24},{1,25},{2,26},{3,27},{4,28},{5,29},{6,30},{7,31},{8,16},{9,... | collective-permute-start | bytes 196616 | tf_op jit(solution)/shard_map/ppermute | solution.py:358
  65.9 4.3 %collective-permute-start.15 = (bf16[32,1024]{1,0:T(8,128)(2,1)S(1)}, bf16[32,1024]{1,0:T(8,128)(2,1)S(1)}, u32[]{:S(2)}, u32[]{:S(2)}) collective-permute-start(bf16[32,1024]{1,0:T(8,128)(2,1)S(1)} %get-tuple-element.61), channel_id=1, source_target_pairs={{0,8},{1,9},{2,10},{3,11},{4,12},{5,13},{6,14},{7,15},{8,0},{9,1},... | collective-permute-start | bytes 196616 | tf_op jit(solution)/shard_map/ppermute | solution.py:358
  (7 other events, 8.3 us)

commit v13 on v11

--- a/solution.py
+++ b/solution.py
@@ -218,28 +218,19 @@
     return jnp.transpose(jnp.concatenate([line] * 16, axis=0))
 
 
-def grad_kernel(chunk, order, groups, info, mine, theirs, weight, other_weight, stats, *refs):
-    logit_grad, outs = refs[0], refs[1:len(order) + 1]
+def grad_kernel(order, groups, info, mine, theirs, weight, other_weight, stats, *refs):
+    logit_grad, table, outs = refs[0], refs[1], refs[2:]
+    chunks = (outs[len(order):], outs[:len(order)])
     rank, _, shard = coordinates()
     height, columns = mine.shape
     part = height // 4
-    quarters = [chunk, 2 + chunk]
-
-    def rows_of(value):
-        return jnp.concatenate([value[q * part:(q + 1) * part] for q in quarters], axis=0)
-
-    if chunk:
-        table = log_totals(groups, stats, height)
-        refs[-1][...] = table
-    else:
-        table = stats[...]
-    log_total = rows_of(table)[:, 0:1]
-    rows_info = rows_of(info)
-    row_weight, target = rows_info[:, 0:1], rows_info[:, 1:2].astype(jnp.int32)
+    table[...] = log_totals(groups, stats, height)
+    log_total = table[:, 0:1]
+    row_weight, target = info[:, 0:1], info[:, 1:2].astype(jnp.int32)
 
     def grad_of(logits, shard):
-        column = lax.broadcasted_iota(jnp.int32, (2 * part, columns), 1) + shard * columns
-        probability = jnp.exp(rows_of(logits) - log_total)
+        column = lax.broadcasted_iota(jnp.int32, (height, columns), 1) + shard * columns
+        probability = jnp.exp(logits[...] - log_total)
         return (
             grad_scale * row_weight * (probability - (column == target).astype(jnp.float32))
         ).astype(jnp.bfloat16)
@@ -248,31 +239,27 @@
     logit_grad[...] = grad
     grads = (grad, grad_of(theirs, shard ^ 1))
     width = outs[0].shape[1]
-    for x in reversed(range(len(outs) // 2)):
+    for x in range(len(order) // 2):
         start = pl.multiple_of((rank ^ 2 * x) * width, width)
         weights = (weight[pl.ds(start, width), :], other_weight[x * width:(x + 1) * width, :])
         total = sum(
             lax.dot_general(g, w, (((1,), (1,)), ((), ())), preferred_element_type=jnp.float32)
             for g, w in zip(grads, weights)
         )
-        for y in range(2):
-            out = outs[order.index(2 * x + y)]
-            out[...] = total[y * part:(y + 1) * part].astype(out.dtype)
-
-
-def weight_kernel(blocks, skipped, after, near_grad, far_grad, *refs):
+        for quarter in range(4):
+            out = chunks[quarter % 2][order.index(2 * x + quarter // 2)]
+            out[...] = total[quarter * part:(quarter + 1) * part].astype(out.dtype)
+
+
+def weight_kernel(blocks, skipped, after, logit_grad, *refs):
     pieces, (out, last, done, sems) = refs[skipped:-4], refs[-4:]
     rank = coordinates()[0]
-    part = near_grad.shape[0] // 2
-    logit_grad = jnp.concatenate(
-        [ref[y * part:(y + 1) * part] for y in range(2) for ref in (near_grad, far_grad)], axis=0
-    )
     width = done.shape[0] // len(blocks)
     copies = []
     for place, block in enumerate(blocks):
         done[place * width:(place + 1) * width] = lax.dot_general(
             all_rows(pieces, place, width),
-            logit_grad,
+            logit_grad[...],
             (((0,), (0,)), ((), ())),
             preferred_element_type=jnp.float32,
         ).astype(jnp.bfloat16)
@@ -415,24 +402,20 @@
     stats = lax.all_to_all(stats, AXES, 0, 0)
     rows_part = total_rows // 4
     order = sorted(range(1, ranks), key=lambda place: (place % 2 + (place > 1), place)) + [0]
-    ends, sums, grads = [None] * zs, [None, None], [None, None]
+    outs = (shape((rows_part, width), bf16),) * (ranks - 1) + (shape((rows_part, width), f32),)
+    logit_grad, table, *going = call(
+        functools.partial(grad_kernel, order, dps),
+        (info, logits, other_logits, held, other_held, stats),
+        [VMEM] * 6,
+        (shape((total_rows, columns), bf16), shape((total_rows, 128), f32)) + outs * 2,
+        (VMEM,) * (2 + 2 * ranks),
+        flops=flops,
+    )
+    ends, sums = [None] * zs, [None, None]
     for chunk in (1, 0):
-        outs = (shape((total_rows // 2, columns), bf16),)
-        outs += (shape((rows_part, width), bf16),) * (ranks - 1) + (shape((rows_part, width), f32),)
-        if chunk:
-            outs += (shape((total_rows, 128), f32),)
-        grads[chunk], *going = call(
-            functools.partial(grad_kernel, chunk, order, dps),
-            (info, logits, other_logits, held, other_held, stats if chunk else table),
-            [VMEM] * 6,
-            outs,
-            (VMEM,) * len(outs),
-            flops=flops // 2,
-        )
-        if chunk:
-            table = going.pop()
-        sums[chunk] = [going[-1]]
-        for place, value in zip(order, going[:-1]):
+        *values, corner = going[(1 - chunk) * ranks:(2 - chunk) * ranks]
+        sums[chunk] = [corner]
+        for place, value in zip(order, values):
             sums[chunk].append(send(value, y=place % 2, x=place // 2))
 
     def weight_part(first, after, *extra):
@@ -440,8 +423,8 @@
         chosen_rows = rows[2 * first:2 * first + ranks]
         return call(
             functools.partial(weight_kernel, blocks, len(extra)),
-            (after, *grads, *extra, *chosen_rows),
-            [ANY] + [VMEM] * 2 + [HBM] * (len(extra) > 0)
+            (after, logit_grad, *extra, *chosen_rows),
+            [ANY, VMEM] + [HBM] * (len(extra) > 0)
             + [VMEM] * (max(len(extra) - 1, 0) + len(chosen_rows)),
             (shape((depth, columns), bf16), shape((8, 128), f32)),
             (HBM, VMEM),
@@ -450,7 +433,7 @@
                 pltpu.SemaphoreType.DMA((ranks // 2,)),
             ],
             flops=flops // 2,
-            aliases={3: 0} if extra else {},
+            aliases={2: 0} if extra else {},
         )
 
     weight_grad, finished = weight_part(0, sums[0][0])

time: 66.2 us -> 66 us (level)
  waiting for transfers between devices: 16.9 us -> 19 us
  Pallas kernels: 14.5 us -> 12.9 us
    ppermute x21, waiting for transfers between devices: 16.9 us -> 19 us  [send(): return lax.ppermute(value, AXES, pairs)]
    pallas_call x14 -> x13, Pallas kernels: 14.5 us -> 12.9 us  [call(): pl.pallas_call(kernel, out_shape=out_shape, in_specs=in_specs, out_specs=...]
  transfers between devices with their start and end apart: 21 -> 21, of which waited for: 11 -> 12; matrix products, arithmetic and copies ran while one was open for 0% -> 0% of each run, Pallas kernels for 14% -> 12%
where the time goes in v13:
time: 66 us; the launch traced here: 65.9 us
  starting transfers between devices  19.3 us (29%)
  waiting for transfers between devices  19 us (29%)
  blocking collectives  13.9 us (21%)
  Pallas kernels  12.9 us (20%)
  between operations  0.79 us (1%)
    ppermute x21, starting transfers between devices, send(): return lax.ppermute(value, AXES, pairs)  19.3 us
    ppermute x21, waiting for transfers between devices, send(): return lax.ppermute(value, AXES, pairs)  19 us
    all_to_all x1, blocking collectives, body(): stats = lax.all_to_all(stats, AXES, 0, 0)  13.9 us
    pallas_call x13, Pallas kernels, call(): pl.pallas_call(kernel, out_shape=out_shape, in_specs=in_specs, out_specs=...  12.9 us
  transfers between devices with their start and end apart: 21, of which 12 were waited for; matrix products, arithmetic and copies ran while one was open for 0% of the time, Pallas kernels for 12%

profile of v13, /device:TPU:0, one launch (start us, length us, event | category | flops | bytes accessed | tf_op | source)
XLA Modules:
  0.0 65.9 jit_solution(1168899143593075232)
XLA Ops:
  0.6 1.2 %shard_map.85 = (bf16[32,1152]{1,0:T(8,128)(2,1)S(1)}, bf16[32,128]{1,0:T(8,128)(2,1)S(1)}) custom-call(bf16[128,1024]{1,0:T(8,128)(2,1)} %hidden_hbm.1, s32[1,128]{1,0:T(1,128)} %bitcast.6, s32[1,128]{1,0:T(1,128)} %bitcast.7, s32[1,128]{1,0:T(1,128)} %bitcast.8), custom_call_target="tpu_custom_call" | custom-call | bytes 345600 | tf_op jit(solution)/shard_map/pallas_call | solution.py:32
  1.9 4.1 %collective-permute-start = (bf16[32,1152]{1,0:T(8,128)(2,1)S(1)}, bf16[32,1152]{1,0:T(8,128)(2,1)S(1)}, u32[]{:S(2)}, u32[]{:S(2)}) collective-permute-start(bf16[32,1152]{1,0:T(8,128)(2,1)S(1)} %get-tuple-element.32.refs_0_), channel_id=1, source_target_pairs={{0,16},{1,17},{2,18},{3,19},{4,20},{5,21},{6,22},{7,23},{8,24},{9,... | collective-permute-start | bytes 221192 | tf_op jit(solution)/shard_map/ppermute | solution.py:320
  6.0 1.3 %collective-permute-start.1 = (bf16[32,1152]{1,0:T(8,128)(2,1)S(1)}, bf16[32,1152]{1,0:T(8,128)(2,1)S(1)}, u32[]{:S(2)}, u32[]{:S(2)}) collective-permute-start(bf16[32,1152]{1,0:T(8,128)(2,1)S(1)} %get-tuple-element.32.refs_0_), channel_id=1, source_target_pairs={{0,24},{1,25},{2,26},{3,27},{4,28},{5,29},{6,30},{7,31},{8,16},{9,... | collective-permute-start | bytes 221192 | tf_op jit(solution)/shard_map/ppermute | solution.py:320
  7.5 3.3 %collective-permute-done.refs_1_ = bf16[32,1152]{1,0:T(8,128)(2,1)S(1)} collective-permute-done((bf16[32,1152]{1,0:T(8,128)(2,1)S(1)}, bf16[32,1152]{1,0:T(8,128)(2,1)S(1)}, u32[]{:S(2)}, u32[]{:S(2)}) %collective-permute-start) | collective-permute-done | bytes 73760 | tf_op jit(solution)/shard_map/ppermute | solution.py:320
  10.8 1.6 %collective-permute-done.1.refs_2_ = bf16[32,1152]{1,0:T(8,128)(2,1)S(1)} collective-permute-done((bf16[32,1152]{1,0:T(8,128)(2,1)S(1)}, bf16[32,1152]{1,0:T(8,128)(2,1)S(1)}, u32[]{:S(2)}, u32[]{:S(2)}) %collective-permute-start.1) | collective-permute-done | bytes 73760 | tf_op jit(solution)/shard_map/ppermute | solution.py:320
  12.6 1.8 %collective-permute-start.3 = (bf16[128,1152]{1,0:T(8,128)(2,1)S(1)}, bf16[128,1152]{1,0:T(8,128)(2,1)S(1)}, u32[]{:S(2)}, u32[]{:S(2)}) collective-permute-start(bf16[128,1152]{1,0:T(8,128)(2,1)S(1)} %get-tuple-element.33.line), channel_id=1, source_target_pairs={{0,4},{1,5},{2,6},{3,7},{4,0},{5,1},{6,2},{7,3},{8,12},{9,13},{10,... | collective-permute-start | bytes 884744 | tf_op jit(solution)/shard_map/ppermute | solution.py:320
  14.4 1.5 %collective-permute-start.4 = (bf16[128,1024]{1,0:T(8,128)(2,1)S(1)}, bf16[128,1024]{1,0:T(8,128)(2,1)S(1)}, u32[]{:S(2)}, u32[]{:S(2)}) collective-permute-start(bf16[128,1024]{1,0:T(8,128)(2,1)S(1)} %get-tuple-element.36), channel_id=1, source_target_pairs={{0,2},{1,3},{2,0},{3,1},{4,6},{5,7},{6,4},{7,5},{8,10},{9,11},{10,... | collective-permute-start | bytes 786440 | tf_op jit(solution)/shard_map/ppermute | solution.py:320
  16.2 2.9 %shard_map.87 = (bf16[4096,512]{1,0:T(8,128)(2,1)S(1)}, bf16[2048,512]{1,0:T(8,128)(2,1)S(1)}, bf16[128,1152]{1,0:T(8,128)(2,1)S(1)}) custom-call(bf16[128,1152]{1,0:T(8,128)(2,1)S(1)} %get-tuple-element.33.line, bf16[4096,512]{1,0:T(8,128)(2,1)} %weight.1), custom_call_target="tpu_custom_call" | custom-call | bytes 11075584 | tf_op jit(solution)/shard_map/pallas_call | solution.py:32
  19.2 3.3 %collective-permute-done.3.refs_1_ = bf16[128,1152]{1,0:T(8,128)(2,1)S(1)} collective-permute-done((bf16[128,1152]{1,0:T(8,128)(2,1)S(1)}, bf16[128,1152]{1,0:T(8,128)(2,1)S(1)}, u32[]{:S(2)}, u32[]{:S(2)}) %collective-permute-start.3) | collective-permute-done | bytes 294944 | tf_op jit(solution)/shard_map/ppermute | solution.py:320
  22.5 1.2 %collective-permute-done.4.refs_2_.refs_4_ = bf16[128,1024]{1,0:T(8,128)(2,1)S(1)} collective-permute-done((bf16[128,1024]{1,0:T(8,128)(2,1)S(1)}, bf16[128,1024]{1,0:T(8,128)(2,1)S(1)}, u32[]{:S(2)}, u32[]{:S(2)}) %collective-permute-start.4) | collective-permute-done | bytes 262176 | tf_op jit(solution)/shard_map/ppermute | solution.py:320
  23.7 2.6 %collective-permute-done.5.refs_3_.refs_5_ = bf16[128,1024]{1,0:T(8,128)(2,1)S(1)} collective-permute-done((bf16[128,1024]{1,0:T(8,128)(2,1)S(1)}, bf16[128,1024]{1,0:T(8,128)(2,1)S(1)}, u32[]{:S(2)}, u32[]{:S(2)}) %collective-permute-start.5) | collective-permute-done | bytes 262176 | tf_op jit(solution)/shard_map/ppermute | solution.py:320
  26.3 0.4 shard_map.88.info.refs_1_
  26.7 0.7 %shard_map.89.partial = f32[256,512]{1,0:T(8,128)S(1)} custom-call(bf16[4096,512]{1,0:T(8,128)(2,1)S(1)} %get-tuple-element.35.weight, bf16[128,1152]{1,0:T(8,128)(2,1)S(1)} %get-tuple-element.34.refs_0_, bf16[128,1152]{1,0:T(8,128)(2,1)S(1)} %collective-permute-done.3.refs_1_, bf16[128,1024]{1,0:T(8,128)(2,1)S(1)} %collective-permute-done.4.refs_2_.refs_4_, ...), custom_call_target="tpu_custom_call" | custom-call | flops 536870912 | bytes 5832704 | tf_op jit(solution)/shard_map/pallas_call | solution.py:32
  27.9 1.2 %shard_map.90 = (f32[256,512]{1,0:T(8,128)S(1)}, f32[32,1,640]{2,1,0:T(1,128)S(1)}) custom-call(f32[256,128]{1,0:T(8,128)S(1)} %shard_map.88.info.refs_1_, f32[256,512]{1,0:T(8,128)S(1)} %shard_map.89.partial, bf16[4096,512]{1,0:T(8,128)(2,1)S(1)} %get-tuple-element.35.weight, bf16[128,1152]{1,0:T(8,128)(2,1)S(1)} %collective-permute-done.6.refs_0_.refs_2_, ...), custom_call_target="tpu_custom_call" | custom-call | flops 536870912 | bytes 6569984 | tf_op jit(solution)/shard_map/pallas_call | solution.py:32
  29.6 13.9 %all_to_all.5.stats.refs_3_ = f32[32,1,640]{2,1,0:T(1,128)S(1)} all-to-all(f32[32,1,640]{2,1,0:T(1,128)S(1)} %get-tuple-element.39.after), channel_id=1, replica_groups=mesh['dp'=8,'vocab'=4] {'dp','vocab'}, dimensions={0} | all-to-all | bytes 163840 | tf_op jit(solution)/shard_map/all_to_all | solution.py:402
  43.5 1.8 %shard_map.92 = (bf16[256,512]{1,0:T(8,128)(2,1)S(1)}, f32[256,128]{1,0:T(8,128)S(1)}, bf16[64,1024]{1,0:T(8,128)(2,1)S(1)}, bf16[64,1024]{1,0:T(8,128)(2,1)S(1)...) custom-call(f32[256,128]{1,0:T(8,128)S(1)} %shard_map.88.info.refs_1, ...), custom_call_target="tpu_custom_call" | custom-call | flops 1073741824 | bytes 9256960 | tf_op jit(solution)/shard_map/pallas_call | solution.py:32
  45.3 0.7 %collective-permute-start.16 = (bf16[64,1024]{1,0:T(8,128)(2,1)S(1)}, bf16[64,1024]{1,0:T(8,128)(2,1)S(1)}, u32[]{:S(2)}, u32[]{:S(2)}) collective-permute-start(bf16[64,1024]{1,0:T(8,128)(2,1)S(1)} %get-tuple-element.53), channel_id=1, source_target_pairs={{0,4},{1,5},{2,6},{3,7},{4,0},{5,1},{6,2},{7,3},{8,12},{9,13},{10,... | collective-permute-start | bytes 393224 | tf_op jit(solution)/shard_map/ppermute | solution.py:320
  46.0 0.7 %collective-permute-start.17 = (bf16[64,1024]{1,0:T(8,128)(2,1)S(1)}, bf16[64,1024]{1,0:T(8,128)(2,1)S(1)}, u32[]{:S(2)}, u32[]{:S(2)}) collective-permute-start(bf16[64,1024]{1,0:T(8,128)(2,1)S(1)} %get-tuple-element.54), channel_id=1, source_target_pairs={{0,2},{1,3},{2,0},{3,1},{4,6},{5,7},{6,4},{7,5},{8,10},{9,11},{10,... | collective-permute-start | bytes 393224 | tf_op jit(solution)/shard_map/ppermute | solution.py:320
  46.7 2.2 %collective-permute-start.18 = (bf16[64,1024]{1,0:T(8,128)(2,1)S(1)}, bf16[64,1024]{1,0:T(8,128)(2,1)S(1)}, u32[]{:S(2)}, u32[]{:S(2)}) collective-permute-start(bf16[64,1024]{1,0:T(8,128)(2,1)S(1)} %get-tuple-element.55), channel_id=1, source_target_pairs={{0,6},{1,7},{2,4},{3,5},{4,2},{5,3},{6,0},{7,1},{8,14},{9,15},{10,... | collective-permute-start | bytes 393224 | tf_op jit(solution)/shard_map/ppermute | solution.py:320
  48.9 0.6 collective-permute-start.12
  49.5 0.7 %collective-permute-start.13 = (bf16[64,1024]{1,0:T(8,128)(2,1)S(1)}, bf16[64,1024]{1,0:T(8,128)(2,1)S(1)}, u32[]{:S(2)}, u32[]{:S(2)}) collective-permute-start(bf16[64,1024]{1,0:T(8,128)(2,1)S(1)} %get-tuple-element.44), channel_id=1, source_target_pairs={{0,2},{1,3},{2,0},{3,1},{4,6},{5,7},{6,4},{7,5},{8,10},{9,11},{10,... | collective-permute-start | bytes 393224 | tf_op jit(solution)/shard_map/ppermute | solution.py:320
  50.2 0.9 %collective-permute-done.16.refs_0_ = bf16[64,1024]{1,0:T(8,128)(2,1)S(1)} collective-permute-done((bf16[64,1024]{1,0:T(8,128)(2,1)S(1)}, bf16[64,1024]{1,0:T(8,128)(2,1)S(1)}, u32[]{:S(2)}, u32[]{:S(2)}) %collective-permute-start.16) | collective-permute-done | bytes 131104 | tf_op jit(solution)/shard_map/ppermute | solution.py:320
  51.1 1.3 %collective-permute-start.14 = (bf16[64,1024]{1,0:T(8,128)(2,1)S(1)}, bf16[64,1024]{1,0:T(8,128)(2,1)S(1)}, u32[]{:S(2)}, u32[]{:S(2)}) collective-permute-start(bf16[64,1024]{1,0:T(8,128)(2,1)S(1)} %get-tuple-element.45), channel_id=1, source_target_pairs={{0,6},{1,7},{2,4},{3,5},{4,2},{5,3},{6,0},{7,1},{8,14},{9,15},{10,... | collective-permute-start | bytes 393224 | tf_op jit(solution)/shard_map/ppermute | solution.py:320
  52.4 1.8 %shard_map.93 = (bf16[4096,512]{1,0:T(8,128)(2,1)}, f32[8,128]{1,0:T(8,128)S(1)}) custom-call(f32[64,1024]{1,0:T(8,128)S(1)} %get-tuple-element.40.after.kept, bf16[256,512]{1,0:T(8,128)(2,1)S(1)} %get-tuple-element.41.logit_grad, bf16[128,1152]{1,0:T(8,128)(2,1)S(1)} %get-tuple-element.34.refs_0_, bf16[128,1152]{1,0:T(8,128)(2,1)S(1)} %collective-permute-done.3.refs_1_, ...), custom_call_target="tpu_custom_call" | custom-call | flops 536870912 | bytes 5902336 | tf_op jit(solution)/shard_map/pallas_call | solution.py:32
  54.2 1.9 %collective-permute-done.18.refs_2_ = bf16[64,1024]{1,0:T(8,128)(2,1)S(1)} collective-permute-done((bf16[64,1024]{1,0:T(8,128)(2,1)S(1)}, bf16[64,1024]{1,0:T(8,128)(2,1)S(1)}, u32[]{:S(2)}, u32[]{:S(2)}) %collective-permute-start.18) | collective-permute-done | bytes 131104 | tf_op jit(solution)/shard_map/ppermute | solution.py:320
  56.1 0.9 %collective-permute-start.19 = (bf16[32,1024]{1,0:T(8,128)(2,1)S(1)}, bf16[32,1024]{1,0:T(8,128)(2,1)S(1)}, u32[]{:S(2)}, u32[]{:S(2)}) collective-permute-start(bf16[32,1024]{1,0:T(8,128)(2,1)S(1)} %get-tuple-element.56), channel_id=1, source_target_pairs={{0,16},{1,17},{2,18},{3,19},{4,20},{5,21},{6,22},{7,23},{8,24},{9,... | collective-permute-start | bytes 196616 | tf_op jit(solution)/shard_map/ppermute | solution.py:320
  57.0 2.3 %collective-permute-start.20 = (bf16[32,1024]{1,0:T(8,128)(2,1)S(1)}, bf16[32,1024]{1,0:T(8,128)(2,1)S(1)}, u32[]{:S(2)}, u32[]{:S(2)}) collective-permute-start(bf16[32,1024]{1,0:T(8,128)(2,1)S(1)} %get-tuple-element.57), channel_id=1, source_target_pairs={{0,24},{1,25},{2,26},{3,27},{4,28},{5,29},{6,30},{7,31},{8,16},{9,... | collective-permute-start | bytes 196616 | tf_op jit(solution)/shard_map/ppermute | solution.py:320
  59.3 1.2 %collective-permute-done.14.refs_2_ = bf16[64,1024]{1,0:T(8,128)(2,1)S(1)} collective-permute-done((bf16[64,1024]{1,0:T(8,128)(2,1)S(1)}, bf16[64,1024]{1,0:T(8,128)(2,1)S(1)}, u32[]{:S(2)}, u32[]{:S(2)}) %collective-permute-start.14) | collective-permute-done | bytes 131104 | tf_op jit(solution)/shard_map/ppermute | solution.py:320
  60.7 1.8 %shard_map.95 = (bf16[4096,512]{1,0:T(8,128)(2,1)}, f32[8,128]{1,0:T(8,128)S(1)}) custom-call(f32[32,1024]{1,0:T(8,128)S(1)} %get-tuple-element.46.after.refs_0_, bf16[256,512]{1,0:T(8,128)(2,1)S(1)} %get-tuple-element.41.logit_grad, bf16[4096,512]{1,0:T(8,128)(2,1)} %get-tuple-element.47.refs_0_, ...), custom_call_target="tpu_custom_call", output_to_operand_aliasing={{0}: (2, {})} | custom-call | flops 536870912 | bytes 10178560 | tf_op jit(solution)/shard_map/pallas_call | solution.py:32
  62.5 0.7 %collective-permute-done.20.refs_3_ = bf16[32,1024]{1,0:T(8,128)(2,1)S(1)} collective-permute-done((bf16[32,1024]{1,0:T(8,128)(2,1)S(1)}, bf16[32,1024]{1,0:T(8,128)(2,1)S(1)}, u32[]{:S(2)}, u32[]{:S(2)}) %collective-permute-start.20) | collective-permute-done | bytes 65568 | tf_op jit(solution)/shard_map/ppermute | solution.py:320
  63.2 1.7 %collective-permute-done.15.refs_1_ = bf16[32,1024]{1,0:T(8,128)(2,1)S(1)} collective-permute-done((bf16[32,1024]{1,0:T(8,128)(2,1)S(1)}, bf16[32,1024]{1,0:T(8,128)(2,1)S(1)}, u32[]{:S(2)}, u32[]{:S(2)}) %collective-permute-start.15) | collective-permute-done | bytes 65568 | tf_op jit(solution)/shard_map/ppermute | solution.py:320
  64.9 1.0 %shard_map.97 = (bf16[128,1024]{1,0:T(8,128)(2,1)}, f32[1,1]{1,0:T(1,128)}) custom-call(f32[8,128]{1,0:T(8,128)S(1)} %get-tuple-element.49.last, bf16[32,128]{1,0:T(8,128)(2,1)S(1)} %get-tuple-element.50.chosen, f32[32,1024]{1,0:T(8,128)S(1)} %get-tuple-element.46.after.refs_0_, bf16[32,1024]{1,0:T(8,128)(2,1)S(1)} %collective-permute-done.15.refs_1_, ...), custom_call_target="tpu_custom_call" | custom-call | bytes 602116 | tf_op jit(solution)/shard_map/pallas_call | solution.py:32
  (26 shorter events, 2.0 us)
Async XLA Ops:
  0.6 25.7 %copy-start = (f32[32]{0:T(128)S(1)}, f32[32]{0:T(128)}, u32[]{:S(2)}) copy-start(f32[32]{0:T(128)} %param.11) | copy-start | bytes 388
  1.9 9.0 %collective-permute-start = (bf16[32,1152]{1,0:T(8,128)(2,1)S(1)}, bf16[32,1152]{1,0:T(8,128)(2,1)S(1)}, u32[]{:S(2)}, u32[]{:S(2)}) collective-permute-start(bf16[32,1152]{1,0:T(8,128)(2,1)S(1)} %get-tuple-element.32.refs_0_), channel_id=1, source_target_pairs={{0,16},{1,17},{2,18},{3,19},{4,20},{5,21},{6,22},{7,23},{8,24},{9,... | collective-permute-start | bytes 221192 | tf_op jit(solution)/shard_map/ppermute | solution.py:320
  6.0 6.5 %collective-permute-start.1 = (bf16[32,1152]{1,0:T(8,128)(2,1)S(1)}, bf16[32,1152]{1,0:T(8,128)(2,1)S(1)}, u32[]{:S(2)}, u32[]{:S(2)}) collective-permute-start(bf16[32,1152]{1,0:T(8,128)(2,1)S(1)} %get-tuple-element.32.refs_0_), channel_id=1, source_target_pairs={{0,24},{1,25},{2,26},{3,27},{4,28},{5,29},{6,30},{7,31},{8,16},{9,... | collective-permute-start | bytes 221192 | tf_op jit(solution)/shard_map/ppermute | solution.py:320
  7.3 5.3 %collective-permute-start.2 = (bf16[32,1152]{1,0:T(8,128)(2,1)S(1)}, bf16[32,1152]{1,0:T(8,128)(2,1)S(1)}, u32[]{:S(2)}, u32[]{:S(2)}) collective-permute-start(bf16[32,1152]{1,0:T(8,128)(2,1)S(1)} %get-tuple-element.32.refs_0_), channel_id=1, source_target_pairs={{0,8},{1,9},{2,10},{3,11},{4,12},{5,13},{6,14},{7,15},{8,0},{9,1},... | collective-permute-start | bytes 221192 | tf_op jit(solution)/shard_map/ppermute | solution.py:320
  12.6 9.8 %collective-permute-start.3 = (bf16[128,1152]{1,0:T(8,128)(2,1)S(1)}, bf16[128,1152]{1,0:T(8,128)(2,1)S(1)}, u32[]{:S(2)}, u32[]{:S(2)}) collective-permute-start(bf16[128,1152]{1,0:T(8,128)(2,1)S(1)} %get-tuple-element.33.line), channel_id=1, source_target_pairs={{0,4},{1,5},{2,6},{3,7},{4,0},{5,1},{6,2},{7,3},{8,12},{9,13},{10,... | collective-permute-start | bytes 884744 | tf_op jit(solution)/shard_map/ppermute | solution.py:320
  14.4 9.2 %collective-permute-start.4 = (bf16[128,1024]{1,0:T(8,128)(2,1)S(1)}, bf16[128,1024]{1,0:T(8,128)(2,1)S(1)}, u32[]{:S(2)}, u32[]{:S(2)}) collective-permute-start(bf16[128,1024]{1,0:T(8,128)(2,1)S(1)} %get-tuple-element.36), channel_id=1, source_target_pairs={{0,2},{1,3},{2,0},{3,1},{4,6},{5,7},{6,4},{7,5},{8,10},{9,11},{10,... | collective-permute-start | bytes 786440 | tf_op jit(solution)/shard_map/ppermute | solution.py:320
  15.9 10.4 %collective-permute-start.5 = (bf16[128,1024]{1,0:T(8,128)(2,1)S(1)}, bf16[128,1024]{1,0:T(8,128)(2,1)S(1)}, u32[]{:S(2)}, u32[]{:S(2)}) collective-permute-start(bf16[128,1024]{1,0:T(8,128)(2,1)S(1)} %get-tuple-element.36), channel_id=1, source_target_pairs={{0,6},{1,7},{2,4},{3,5},{4,2},{5,3},{6,0},{7,1},{8,14},{9,15},{10,... | collective-permute-start | bytes 786440 | tf_op jit(solution)/shard_map/ppermute | solution.py:320
  19.1 8.4 %collective-permute-start.6 = (bf16[128,1152]{1,0:T(8,128)(2,1)S(1)}, bf16[128,1152]{1,0:T(8,128)(2,1)S(1)}, u32[]{:S(2)}, u32[]{:S(2)}) collective-permute-start(bf16[128,1152]{1,0:T(8,128)(2,1)S(1)} %get-tuple-element.34.refs_0_), channel_id=1, source_target_pairs={{0,1},{1,0},{2,3},{3,2},{4,5},{5,4},{6,7},{7,6},{8,9},{9,8},{10,11... | collective-permute-start | bytes 884744 | tf_op jit(solution)/shard_map/ppermute | solution.py:320
  22.5 5.4 %collective-permute-start.7 = (bf16[128,1152]{1,0:T(8,128)(2,1)S(1)}, bf16[128,1152]{1,0:T(8,128)(2,1)S(1)}, u32[]{:S(2)}, u32[]{:S(2)}) collective-permute-start(bf16[128,1152]{1,0:T(8,128)(2,1)S(1)} %collective-permute-done.3.refs_1_), channel_id=1, source_target_pairs={{0,1},{1,0},{2,3},{3,2},{4,5},{5,4},{6,7},{7,6},{8,9},{9,8},{10,11... | collective-permute-start | bytes 884744 | tf_op jit(solution)/shard_map/ppermute | solution.py:320
  23.7 3.8 %collective-permute-start.8 = (bf16[128,1024]{1,0:T(8,128)(2,1)S(1)}, bf16[128,1024]{1,0:T(8,128)(2,1)S(1)}, u32[]{:S(2)}, u32[]{:S(2)}) collective-permute-start(bf16[128,1024]{1,0:T(8,128)(2,1)S(1)} %collective-permute-done.4.refs_2_.refs_4_), channel_id=1, source_target_pairs={{0,1},{1,0},{2,3},{3,2},{4,5},{5,4},{6,7},{7,6},{8,9},{9,8},{10,11... | collective-permute-start | bytes 786440 | tf_op jit(solution)/shard_map/ppermute | solution.py:320
  26.3 1.5 %collective-permute-start.9 = (bf16[128,1024]{1,0:T(8,128)(2,1)S(1)}, bf16[128,1024]{1,0:T(8,128)(2,1)S(1)}, u32[]{:S(2)}, u32[]{:S(2)}) collective-permute-start(bf16[128,1024]{1,0:T(8,128)(2,1)S(1)} %collective-permute-done.5.refs_3_.refs_5_), channel_id=1, source_target_pairs={{0,1},{1,0},{2,3},{3,2},{4,5},{5,4},{6,7},{7,6},{8,9},{9,8},{10,11... | collective-permute-start | bytes 786440 | tf_op jit(solution)/shard_map/ppermute | solution.py:320
  29.0 14.5 %collective-permute-start.11 = (bf16[2048,512]{1,0:T(8,128)(2,1)S(1)}, bf16[2048,512]{1,0:T(8,128)(2,1)S(1)}, u32[]{:S(2)}, u32[]{:S(2)}) collective-permute-start(bf16[2048,512]{1,0:T(8,128)(2,1)S(1)} %shard_map.91), channel_id=1, source_target_pairs={{0,1},{1,0},{2,3},{3,2},{4,5},{5,4},{6,7},{7,6},{8,9},{9,8},{10,11... | collective-permute-start | bytes 6291464 | tf_op jit(solution)/shard_map/ppermute | solution.py:320
  29.3 14.3 %collective-permute-start.10 = (f32[256,512]{1,0:T(8,128)S(1)}, f32[256,512]{1,0:T(8,128)S(1)}, u32[]{:S(2)}, u32[]{:S(2)}) collective-permute-start(f32[256,512]{1,0:T(8,128)S(1)} %get-tuple-element.37.mine), channel_id=1, source_target_pairs={{0,1},{1,0},{2,3},{3,2},{4,5},{5,4},{6,7},{7,6},{8,9},{9,8},{10,11... | collective-permute-start | bytes 1572872 | tf_op jit(solution)/shard_map/ppermute | solution.py:320
  45.3 5.7 %collective-permute-start.16 = (bf16[64,1024]{1,0:T(8,128)(2,1)S(1)}, bf16[64,1024]{1,0:T(8,128)(2,1)S(1)}, u32[]{:S(2)}, u32[]{:S(2)}) collective-permute-start(bf16[64,1024]{1,0:T(8,128)(2,1)S(1)} %get-tuple-element.53), channel_id=1, source_target_pairs={{0,4},{1,5},{2,6},{3,7},{4,0},{5,1},{6,2},{7,3},{8,12},{9,13},{10,... | collective-permute-start | bytes 393224 | tf_op jit(solution)/shard_map/ppermute | solution.py:320
  46.0 8.2 %collective-permute-start.17 = (bf16[64,1024]{1,0:T(8,128)(2,1)S(1)}, bf16[64,1024]{1,0:T(8,128)(2,1)S(1)}, u32[]{:S(2)}, u32[]{:S(2)}) collective-permute-start(bf16[64,1024]{1,0:T(8,128)(2,1)S(1)} %get-tuple-element.54), channel_id=1, source_target_pairs={{0,2},{1,3},{2,0},{3,1},{4,6},{5,7},{6,4},{7,5},{8,10},{9,11},{10,... | collective-permute-start | bytes 393224 | tf_op jit(solution)/shard_map/ppermute | solution.py:320
  46.7 9.3 %collective-permute-start.18 = (bf16[64,1024]{1,0:T(8,128)(2,1)S(1)}, bf16[64,1024]{1,0:T(8,128)(2,1)S(1)}, u32[]{:S(2)}, u32[]{:S(2)}) collective-permute-start(bf16[64,1024]{1,0:T(8,128)(2,1)S(1)} %get-tuple-element.55), channel_id=1, source_target_pairs={{0,6},{1,7},{2,4},{3,5},{4,2},{5,3},{6,0},{7,1},{8,14},{9,15},{10,... | collective-permute-start | bytes 393224 | tf_op jit(solution)/shard_map/ppermute | solution.py:320
  48.9 10.4 %collective-permute-start.12 = (bf16[64,1024]{1,0:T(8,128)(2,1)S(1)}, bf16[64,1024]{1,0:T(8,128)(2,1)S(1)}, u32[]{:S(2)}, u32[]{:S(2)}) collective-permute-start(bf16[64,1024]{1,0:T(8,128)(2,1)S(1)} %get-tuple-element.43), channel_id=1, source_target_pairs={{0,4},{1,5},{2,6},{3,7},{4,0},{5,1},{6,2},{7,3},{8,12},{9,13},{10,... | collective-permute-start | bytes 393224 | tf_op jit(solution)/shard_map/ppermute | solution.py:320
  49.5 9.8 %collective-permute-start.13 = (bf16[64,1024]{1,0:T(8,128)(2,1)S(1)}, bf16[64,1024]{1,0:T(8,128)(2,1)S(1)}, u32[]{:S(2)}, u32[]{:S(2)}) collective-permute-start(bf16[64,1024]{1,0:T(8,128)(2,1)S(1)} %get-tuple-element.44), channel_id=1, source_target_pairs={{0,2},{1,3},{2,0},{3,1},{4,6},{5,7},{6,4},{7,5},{8,10},{9,11},{10,... | collective-permute-start | bytes 393224 | tf_op jit(solution)/shard_map/ppermute | solution.py:320
  51.1 9.5 %collective-permute-start.14 = (bf16[64,1024]{1,0:T(8,128)(2,1)S(1)}, bf16[64,1024]{1,0:T(8,128)(2,1)S(1)}, u32[]{:S(2)}, u32[]{:S(2)}) collective-permute-start(bf16[64,1024]{1,0:T(8,128)(2,1)S(1)} %get-tuple-element.45), channel_id=1, source_target_pairs={{0,6},{1,7},{2,4},{3,5},{4,2},{5,3},{6,0},{7,1},{8,14},{9,15},{10,... | collective-permute-start | bytes 393224 | tf_op jit(solution)/shard_map/ppermute | solution.py:320
  56.1 6.4 %collective-permute-start.19 = (bf16[32,1024]{1,0:T(8,128)(2,1)S(1)}, bf16[32,1024]{1,0:T(8,128)(2,1)S(1)}, u32[]{:S(2)}, u32[]{:S(2)}) collective-permute-start(bf16[32,1024]{1,0:T(8,128)(2,1)S(1)} %get-tuple-element.56), channel_id=1, source_target_pairs={{0,16},{1,17},{2,18},{3,19},{4,20},{5,21},{6,22},{7,23},{8,24},{9,... | collective-permute-start | bytes 196616 | tf_op jit(solution)/shard_map/ppermute | solution.py:320
  57.0 6.2 %collective-permute-start.20 = (bf16[32,1024]{1,0:T(8,128)(2,1)S(1)}, bf16[32,1024]{1,0:T(8,128)(2,1)S(1)}, u32[]{:S(2)}, u32[]{:S(2)}) collective-permute-start(bf16[32,1024]{1,0:T(8,128)(2,1)S(1)} %get-tuple-element.57), channel_id=1, source_target_pairs={{0,24},{1,25},{2,26},{3,27},{4,28},{5,29},{6,30},{7,31},{8,16},{9,... | collective-permute-start | bytes 196616 | tf_op jit(solution)/shard_map/ppermute | solution.py:320
  60.6 4.3 %collective-permute-start.15 = (bf16[32,1024]{1,0:T(8,128)(2,1)S(1)}, bf16[32,1024]{1,0:T(8,128)(2,1)S(1)}, u32[]{:S(2)}, u32[]{:S(2)}) collective-permute-start(bf16[32,1024]{1,0:T(8,128)(2,1)S(1)} %get-tuple-element.51), channel_id=1, source_target_pairs={{0,8},{1,9},{2,10},{3,11},{4,12},{5,13},{6,14},{7,15},{8,0},{9,1},... | collective-permute-start | bytes 196616 | tf_op jit(solution)/shard_map/ppermute | solution.py:320

commit v14 on v13

--- a/solution.py
+++ b/solution.py
@@ -9,8 +9,9 @@
 from jax.sharding import PartitionSpec as P
 
 CAP = 32
+LANES = 128
+SUB = 16
 MOST_VMEM = 56 * 1024 * 1024
-IDS = 128
 grad_scale = 16384.0
 AXES = ("dp", "vocab")
 SMEM = pl.BlockSpec(memory_space=pltpu.SMEM)
@@ -69,7 +70,22 @@
     return (slot.astype(jnp.int32) == grid) & (mask == 1)
 
 
-def pack_kernel(hidden_hbm, mask_hbm, target_hbm, turn_hbm, rows, chosen_out, *scratch):
+def payload_rows(width):
+    return CAP * width // LANES + SUB
+
+
+def tiles(width):
+    count = width // LANES
+    for high in range(CAP // SUB):
+        for low in range(count):
+            yield (
+                (high * count + low) * SUB,
+                slice(high * SUB, (high + 1) * SUB),
+                slice(low * LANES, (low + 1) * LANES),
+            )
+
+
+def pack_kernel(hidden_hbm, mask_hbm, target_hbm, turn_hbm, payload, chosen_out, *scratch):
     hidden, mask, target, turn, sems = scratch
     copies = []
     for place, (source, held) in enumerate(
@@ -81,8 +97,7 @@
     for copy in copies[:3]:
         copy.wait()
     width = hidden.shape[1]
-    chosen = choose(mask[...])
-    one_hot = chosen.astype(jnp.float32).astype(jnp.bfloat16)
+    one_hot = choose(mask[...]).astype(jnp.float32).astype(jnp.bfloat16)
     chosen_out[...] = one_hot
     turns, targets = turn[...], target[...]
     fields = (
@@ -93,22 +108,41 @@
         (targets >> 8) & 255,
         targets >> 16,
     )
-    lane = lax.broadcasted_iota(jnp.int32, (CAP, IDS), 1)
-    table = jnp.zeros((CAP, IDS), jnp.float32)
-    for place, field in enumerate(fields):
-        picked = jnp.where(chosen, field.astype(jnp.float32), 0.0)
-        table = jnp.where(lane == place, jnp.sum(picked, axis=1, keepdims=True), table)
-    rows[:, width:] = table.astype(jnp.bfloat16)
+    fields += (jnp.zeros_like(turns),) * (SUB - len(fields))
+    fields = jnp.concatenate([field.astype(jnp.float32) for field in fields], axis=0)
+    slots = jnp.concatenate([one_hot] + [jnp.zeros_like(one_hot)] * (LANES // CAP - 1), axis=0)
+    ids = lax.dot_general(
+        fields.astype(jnp.bfloat16),
+        slots,
+        (((1,), (1,)), ((), ())),
+        preferred_element_type=jnp.float32,
+    )
+    payload[payload.shape[0] - SUB:] = ids.astype(jnp.bfloat16)
     copies[3].wait()
     packed = jnp.dot(one_hot, hidden[...], preferred_element_type=jnp.float32)
-    rows[:, :width] = packed.astype(jnp.bfloat16)
+    packed = packed.astype(jnp.bfloat16)
+    for start, rows, lanes in tiles(width):
+        payload[start:start + SUB] = packed[rows, lanes]
+
+
+def unroll(payload, first, plain, place):
+    for start, rows, lanes in tiles(plain.shape[1]):
+        target = slice(place * CAP + rows.start, place * CAP + rows.stop)
+        plain[target, lanes] = payload[first + start:first + start + SUB]
 
 
 def join_kernel(order, *refs):
     blocks, line, plain = refs[:-2], refs[-2], refs[-1]
     for place, block in zip(order, blocks):
-        line[place * CAP:(place + 1) * CAP] = block[...]
-        plain[place * CAP:(place + 1) * CAP] = block[:, :plain.shape[1]]
+        height = block.shape[0]
+        line[place * height:(place + 1) * height] = block[...]
+        unroll(block, 0, plain, place)
+
+
+def rows_kernel(after, line, plain):
+    height = payload_rows(plain.shape[1])
+    for place in range(line.shape[0] // height):
+        unroll(line, place * height, plain, place)
 
 
 def stage_kernel(blocks, line, weight, held, away, same, sems):
@@ -135,10 +169,14 @@
     pass
 
 
-def info_kernel(*refs):
-    advantages, info = refs[-2:]
-    start = refs[0].shape[1] - IDS
-    table = jnp.concatenate([ref[:, start:] for ref in refs[:-2]], axis=0).astype(jnp.float32)
+def info_kernel(height, own, other, advantages, info):
+    tables = []
+    for line in (own, other):
+        for end in range(height, line.shape[0] + 1, height):
+            ids = line[end - SUB:end].astype(jnp.float32)
+            ids = jnp.concatenate([ids] * (LANES // SUB), axis=0)
+            tables.append(jnp.transpose(ids)[:CAP])
+    table = jnp.concatenate(tables, axis=0)
     valid = table[:, 0:1]
     turn = table[:, 1:2] + 256.0 * table[:, 2:3]
     target = table[:, 3:4] + 256.0 * table[:, 4:5] + 65536.0 * table[:, 5:6]
@@ -168,8 +206,8 @@
     return stats
 
 
-def all_rows(pieces, block, width):
-    return jnp.concatenate([ref[:, :width] for ref in pieces[2 * block:2 * block + 2]], axis=0)
+def all_rows(pieces, block):
+    return jnp.concatenate([ref[...] for ref in pieces[2 * block:2 * block + 2]], axis=0)
 
 
 def some_logits(blocks, first, pieces, weight):
@@ -178,7 +216,7 @@
     for place, block in enumerate(range(first, blocks, 2)):
         start = pl.multiple_of((rank ^ block) * width, width)
         part = jnp.dot(
-            all_rows(pieces, place, width),
+            all_rows(pieces, place),
             weight[pl.ds(start, width), :],
             preferred_element_type=jnp.float32,
         )
@@ -258,7 +296,7 @@
     copies = []
     for place, block in enumerate(blocks):
         done[place * width:(place + 1) * width] = lax.dot_general(
-            all_rows(pieces, place, width),
+            all_rows(pieces, place),
             logit_grad[...],
             (((0,), (0,)), ((), ())),
             preferred_element_type=jnp.float32,
@@ -329,7 +367,7 @@
         ),
         [HBM] * 4,
         (
-            shape((CAP, width + IDS), bf16),
+            shape((payload_rows(width), LANES), bf16),
             shape((CAP, tokens), bf16),
         ),
         (VMEM,) * 2,
@@ -340,35 +378,43 @@
 
     line_order = [0, *range(2, zs), 1]
     blocks = [send(packed, z=z) if z else packed for z in line_order]
-    line_rows = zs * CAP
+    height = payload_rows(width)
     line, line_plain = call(
         functools.partial(join_kernel, line_order),
         blocks,
         [VMEM] * zs,
-        (shape((line_rows, width + IDS), bf16), shape((line_rows, width), bf16)),
+        (shape((zs * height, LANES), bf16), shape((zs * CAP, width), bf16)),
         (VMEM, VMEM),
     )
     pieces = {(2 * x, y): send(line_plain if x else line, y=y, x=x) for y, x in square}
+    across = pieces[0, 1]
     held, away, same = call(
         functools.partial(stage_kernel, ranks),
-        (line, in_hbm(weight)),
+        (line_plain, in_hbm(weight)),
         [VMEM, HBM],
         (
             shape((depth, columns), bf16),
             shape((depth // 2, columns), bf16),
-            shape(line.shape, bf16),
+            shape(line_plain.shape, bf16),
         ),
         (VMEM,) * 3,
         [pltpu.SemaphoreType.DMA((ranks + xs,))],
     )
+    plain = shape((zs * CAP, width), bf16)
+    pieces[0, 1] = call(rows_kernel, (same, across), [ANY, VMEM], plain, VMEM)
+    pieces[1, 1] = send(pieces[0, 1], core=1)
+    for x in range(1, xs):
+        operands = (pieces[2 * x, 1], pieces[1, 1])
+        pieces[2 * x, 1] = call(gate_kernel, operands, [ANY] * 2, plain, ANY, aliases={0: 0})
     pieces[0, 0] = same
     for b, y in list(pieces):
-        pieces[b + 1, y] = send(pieces[b, y], core=1)
+        if b % 2 == 0 and (b + 1, y) not in pieces:
+            pieces[b + 1, y] = send(pieces[b, y], core=1)
     rows = [pieces[b, y] for b in range(ranks) for y in range(2)]
 
     info = call(
-        info_kernel,
-        (*rows[:2], advantages.reshape(1, -1)),
+        functools.partial(info_kernel, height),
+        (line, across, advantages.reshape(1, -1)),
         [VMEM] * 3,
         shape((total_rows, 128), f32),
         VMEM,

time: 66 us -> 66.5 us (level)
  starting transfers between devices: 19.3 us -> 20 us
    pallas_call x13 -> x15, Pallas kernels: 12.9 us -> 13 us  [call(): pl.pallas_call(kernel, out_shape=out_shape, in_specs=in_specs, out_specs=...]
where the time goes in v14:
time: 66.5 us; the launch traced here: 66.3 us
  starting transfers between devices  20 us (30%)
  waiting for transfers between devices  18.8 us (28%)
  blocking collectives  13.7 us (21%)
  Pallas kernels  13 us (20%)
  between operations  0.79 us (1%)
    ppermute x21, starting transfers between devices, send(): return lax.ppermute(value, AXES, pairs)  20 us
    ppermute x21, waiting for transfers between devices, send(): return lax.ppermute(value, AXES, pairs)  18.8 us
    all_to_all x1, blocking collectives, body(): stats = lax.all_to_all(stats, AXES, 0, 0)  13.7 us
    pallas_call x15, Pallas kernels, call(): pl.pallas_call(kernel, out_shape=out_shape, in_specs=in_specs, out_specs=...  13 us
  transfers between devices with their start and end apart: 21, of which 12 were waited for; matrix products, arithmetic and copies ran while one was open for 0% of the time, Pallas kernels for 12%

profile of v14, /device:TPU:0, one launch (start us, length us, event | category | flops | bytes accessed | tf_op | source)
XLA Modules:
  0.0 66.3 jit_solution(8676088596704866712)
XLA Ops:
  0.6 1.2 %shard_map.85 = (bf16[272,128]{1,0:T(8,128)(2,1)S(1)}, bf16[32,128]{1,0:T(8,128)(2,1)S(1)}) custom-call(bf16[128,1024]{1,0:T(8,128)(2,1)} %hidden_hbm.1, s32[1,128]{1,0:T(1,128)} %bitcast.6, s32[1,128]{1,0:T(1,128)} %bitcast.7, s32[1,128]{1,0:T(1,128)} %bitcast.8), custom_call_target="tpu_custom_call" | custom-call | bytes 341504 | tf_op jit(solution)/shard_map/pallas_call | solution.py:33
  1.9 4.1 %collective-permute-start = (bf16[272,128]{1,0:T(8,128)(2,1)S(1)}, bf16[272,128]{1,0:T(8,128)(2,1)S(1)}, u32[]{:S(2)}, u32[]{:S(2)}) collective-permute-start(bf16[272,128]{1,0:T(8,128)(2,1)S(1)} %get-tuple-element.32.refs_0_), channel_id=1, source_target_pairs={{0,16},{1,17},{2,18},{3,19},{4,20},{5,21},{6,22},{7,23},{8,24},{9,... | collective-permute-start | bytes 208904 | tf_op jit(solution)/shard_map/ppermute | solution.py:358
  6.0 1.3 %collective-permute-start.1 = (bf16[272,128]{1,0:T(8,128)(2,1)S(1)}, bf16[272,128]{1,0:T(8,128)(2,1)S(1)}, u32[]{:S(2)}, u32[]{:S(2)}) collective-permute-start(bf16[272,128]{1,0:T(8,128)(2,1)S(1)} %get-tuple-element.32.refs_0_), channel_id=1, source_target_pairs={{0,24},{1,25},{2,26},{3,27},{4,28},{5,29},{6,30},{7,31},{8,16},{9,... | collective-permute-start | bytes 208904 | tf_op jit(solution)/shard_map/ppermute | solution.py:358
  7.5 2.3 %collective-permute-done.refs_1_ = bf16[272,128]{1,0:T(8,128)(2,1)S(1)} collective-permute-done((bf16[272,128]{1,0:T(8,128)(2,1)S(1)}, bf16[272,128]{1,0:T(8,128)(2,1)S(1)}, u32[]{:S(2)}, u32[]{:S(2)}) %collective-permute-start) | collective-permute-done | bytes 69664 | tf_op jit(solution)/shard_map/ppermute | solution.py:358
  9.8 2.5 %collective-permute-done.1.refs_2_ = bf16[272,128]{1,0:T(8,128)(2,1)S(1)} collective-permute-done((bf16[272,128]{1,0:T(8,128)(2,1)S(1)}, bf16[272,128]{1,0:T(8,128)(2,1)S(1)}, u32[]{:S(2)}, u32[]{:S(2)}) %collective-permute-start.1) | collective-permute-done | bytes 69664 | tf_op jit(solution)/shard_map/ppermute | solution.py:358
  12.4 1.8 %collective-permute-start.3 = (bf16[1088,128]{1,0:T(8,128)(2,1)S(1)}, bf16[1088,128]{1,0:T(8,128)(2,1)S(1)}, u32[]{:S(2)}, u32[]{:S(2)}) collective-permute-start(bf16[1088,128]{1,0:T(8,128)(2,1)S(1)} %get-tuple-element.33.own), channel_id=1, source_target_pairs={{0,4},{1,5},{2,6},{3,7},{4,0},{5,1},{6,2},{7,3},{8,12},{9,13},{10,... | collective-permute-start | bytes 835592 | tf_op jit(solution)/shard_map/ppermute | solution.py:358
  14.2 1.4 %collective-permute-start.5 = (bf16[128,1024]{1,0:T(8,128)(2,1)S(1)}, bf16[128,1024]{1,0:T(8,128)(2,1)S(1)}, u32[]{:S(2)}, u32[]{:S(2)}) collective-permute-start(bf16[128,1024]{1,0:T(8,128)(2,1)S(1)} %get-tuple-element.34.line), channel_id=1, source_target_pairs={{0,6},{1,7},{2,4},{3,5},{4,2},{5,3},{6,0},{7,1},{8,14},{9,15},{10,... | collective-permute-start | bytes 786440 | tf_op jit(solution)/shard_map/ppermute | solution.py:358
  16.0 2.9 %shard_map.88 = (bf16[4096,512]{1,0:T(8,128)(2,1)S(1)}, bf16[2048,512]{1,0:T(8,128)(2,1)S(1)}, bf16[128,1024]{1,0:T(8,128)(2,1)S(1)}) custom-call(bf16[128,1024]{1,0:T(8,128)(2,1)S(1)} %get-tuple-element.34.line, bf16[4096,512]{1,0:T(8,128)(2,1)} %weight.1), custom_call_target="tpu_custom_call" | custom-call | bytes 11010048 | tf_op jit(solution)/shard_map/pallas_call | solution.py:33
  18.9 6.4 %collective-permute-done.3.other.line = bf16[1088,128]{1,0:T(8,128)(2,1)S(1)} collective-permute-done((bf16[1088,128]{1,0:T(8,128)(2,1)S(1)}, bf16[1088,128]{1,0:T(8,128)(2,1)S(1)}, u32[]{:S(2)}, u32[]{:S(2)}) %collective-permute-start.3) | collective-permute-done | bytes 278560 | tf_op jit(solution)/shard_map/ppermute | solution.py:358
  25.4 0.5 collective-permute-start.7
  26.3 0.7 %collective-permute-done.6.after.refs_1_.refs_3_ = bf16[128,1024]{1,0:T(8,128)(2,1)S(1)} collective-permute-done((bf16[128,1024]{1,0:T(8,128)(2,1)S(1)}, bf16[128,1024]{1,0:T(8,128)(2,1)S(1)}, u32[]{:S(2)}, u32[]{:S(2)}) %collective-permute-start.6) | collective-permute-done | bytes 262176 | tf_op jit(solution)/shard_map/ppermute | solution.py:358
  27.1 0.5 shard_map.87.info.refs_1_
  27.6 0.7 %shard_map.91.partial = f32[256,512]{1,0:T(8,128)S(1)} custom-call(bf16[4096,512]{1,0:T(8,128)(2,1)S(1)} %get-tuple-element.35.weight, bf16[128,1024]{1,0:T(8,128)(2,1)S(1)} %get-tuple-element.36.after.refs_0_, bf16[128,1024]{1,0:T(8,128)(2,1)S(1)} %shard_map.89.refs_1_, bf16[128,1024]{1,0:T(8,128)(2,1)S(1)} %collective-permute-done.4.refs_2_.refs_4_, ...), custom_call_target="tpu_custom_call" | custom-call | flops 536870912 | bytes 5767168 | tf_op jit(solution)/shard_map/pallas_call | solution.py:33
  28.5 1.1 %shard_map.92 = (f32[256,512]{1,0:T(8,128)S(1)}, f32[32,1,640]{2,1,0:T(1,128)S(1)}) custom-call(f32[256,128]{1,0:T(8,128)S(1)} %shard_map.87.info.refs_1_, f32[256,512]{1,0:T(8,128)S(1)} %shard_map.91.partial, bf16[4096,512]{1,0:T(8,128)(2,1)S(1)} %get-tuple-element.35.weight, bf16[128,1024]{1,0:T(8,128)(2,1)S(1)} %collective-permute-done.7.refs_0_.refs_2_, ...), custom_call_target="tpu_custom_call" | custom-call | flops 536870912 | bytes 6504448 | tf_op jit(solution)/shard_map/pallas_call | solution.py:33
  30.2 13.7 %all_to_all.5.stats.refs_3_ = f32[32,1,640]{2,1,0:T(1,128)S(1)} all-to-all(f32[32,1,640]{2,1,0:T(1,128)S(1)} %get-tuple-element.39.after), channel_id=1, replica_groups=mesh['dp'=8,'vocab'=4] {'dp','vocab'}, dimensions={0} | all-to-all | bytes 163840 | tf_op jit(solution)/shard_map/all_to_all | solution.py:448
  44.0 1.8 %shard_map.94 = (bf16[256,512]{1,0:T(8,128)(2,1)S(1)}, f32[256,128]{1,0:T(8,128)S(1)}, bf16[64,1024]{1,0:T(8,128)(2,1)S(1)}, bf16[64,1024]{1,0:T(8,128)(2,1)S(1)...) custom-call(f32[256,128]{1,0:T(8,128)S(1)} %shard_map.87.info.refs_1, ...), custom_call_target="tpu_custom_call" | custom-call | flops 1073741824 | bytes 9256960 | tf_op jit(solution)/shard_map/pallas_call | solution.py:33
  45.7 0.7 %collective-permute-start.16 = (bf16[64,1024]{1,0:T(8,128)(2,1)S(1)}, bf16[64,1024]{1,0:T(8,128)(2,1)S(1)}, u32[]{:S(2)}, u32[]{:S(2)}) collective-permute-start(bf16[64,1024]{1,0:T(8,128)(2,1)S(1)} %get-tuple-element.53), channel_id=1, source_target_pairs={{0,4},{1,5},{2,6},{3,7},{4,0},{5,1},{6,2},{7,3},{8,12},{9,13},{10,... | collective-permute-start | bytes 393224 | tf_op jit(solution)/shard_map/ppermute | solution.py:358
  46.4 0.7 %collective-permute-start.17 = (bf16[64,1024]{1,0:T(8,128)(2,1)S(1)}, bf16[64,1024]{1,0:T(8,128)(2,1)S(1)}, u32[]{:S(2)}, u32[]{:S(2)}) collective-permute-start(bf16[64,1024]{1,0:T(8,128)(2,1)S(1)} %get-tuple-element.54), channel_id=1, source_target_pairs={{0,2},{1,3},{2,0},{3,1},{4,6},{5,7},{6,4},{7,5},{8,10},{9,11},{10,... | collective-permute-start | bytes 393224 | tf_op jit(solution)/shard_map/ppermute | solution.py:358
  47.1 2.2 %collective-permute-start.18 = (bf16[64,1024]{1,0:T(8,128)(2,1)S(1)}, bf16[64,1024]{1,0:T(8,128)(2,1)S(1)}, u32[]{:S(2)}, u32[]{:S(2)}) collective-permute-start(bf16[64,1024]{1,0:T(8,128)(2,1)S(1)} %get-tuple-element.55), channel_id=1, source_target_pairs={{0,6},{1,7},{2,4},{3,5},{4,2},{5,3},{6,0},{7,1},{8,14},{9,15},{10,... | collective-permute-start | bytes 393224 | tf_op jit(solution)/shard_map/ppermute | solution.py:358
  49.3 0.6 collective-permute-start.12
  49.9 0.7 %collective-permute-start.13 = (bf16[64,1024]{1,0:T(8,128)(2,1)S(1)}, bf16[64,1024]{1,0:T(8,128)(2,1)S(1)}, u32[]{:S(2)}, u32[]{:S(2)}) collective-permute-start(bf16[64,1024]{1,0:T(8,128)(2,1)S(1)} %get-tuple-element.44), channel_id=1, source_target_pairs={{0,2},{1,3},{2,0},{3,1},{4,6},{5,7},{6,4},{7,5},{8,10},{9,11},{10,... | collective-permute-start | bytes 393224 | tf_op jit(solution)/shard_map/ppermute | solution.py:358
  50.6 0.8 %collective-permute-done.16.refs_0_ = bf16[64,1024]{1,0:T(8,128)(2,1)S(1)} collective-permute-done((bf16[64,1024]{1,0:T(8,128)(2,1)S(1)}, bf16[64,1024]{1,0:T(8,128)(2,1)S(1)}, u32[]{:S(2)}, u32[]{:S(2)}) %collective-permute-start.16) | collective-permute-done | bytes 131104 | tf_op jit(solution)/shard_map/ppermute | solution.py:358
  51.5 1.3 %collective-permute-start.14 = (bf16[64,1024]{1,0:T(8,128)(2,1)S(1)}, bf16[64,1024]{1,0:T(8,128)(2,1)S(1)}, u32[]{:S(2)}, u32[]{:S(2)}) collective-permute-start(bf16[64,1024]{1,0:T(8,128)(2,1)S(1)} %get-tuple-element.45), channel_id=1, source_target_pairs={{0,6},{1,7},{2,4},{3,5},{4,2},{5,3},{6,0},{7,1},{8,14},{9,15},{10,... | collective-permute-start | bytes 393224 | tf_op jit(solution)/shard_map/ppermute | solution.py:358
  52.8 1.8 %shard_map.95 = (bf16[4096,512]{1,0:T(8,128)(2,1)}, f32[8,128]{1,0:T(8,128)S(1)}) custom-call(f32[64,1024]{1,0:T(8,128)S(1)} %get-tuple-element.40.after.kept, bf16[256,512]{1,0:T(8,128)(2,1)S(1)} %get-tuple-element.41.logit_grad, bf16[128,1024]{1,0:T(8,128)(2,1)S(1)} %get-tuple-element.36.after.refs_0_, bf16[128,1024]{1,0:T(8,128)(2,1)S(1)} %shard_map.89.refs_1_, ...), custom_call_target="tpu_custom_call" | custom-call | flops 536870912 | bytes 5771264 | tf_op jit(solution)/shard_map/pallas_call | solution.py:33
  54.6 1.9 %collective-permute-done.18.refs_2_ = bf16[64,1024]{1,0:T(8,128)(2,1)S(1)} collective-permute-done((bf16[64,1024]{1,0:T(8,128)(2,1)S(1)}, bf16[64,1024]{1,0:T(8,128)(2,1)S(1)}, u32[]{:S(2)}, u32[]{:S(2)}) %collective-permute-start.18) | collective-permute-done | bytes 131104 | tf_op jit(solution)/shard_map/ppermute | solution.py:358
  56.5 0.9 %collective-permute-start.19 = (bf16[32,1024]{1,0:T(8,128)(2,1)S(1)}, bf16[32,1024]{1,0:T(8,128)(2,1)S(1)}, u32[]{:S(2)}, u32[]{:S(2)}) collective-permute-start(bf16[32,1024]{1,0:T(8,128)(2,1)S(1)} %get-tuple-element.56), channel_id=1, source_target_pairs={{0,16},{1,17},{2,18},{3,19},{4,20},{5,21},{6,22},{7,23},{8,24},{9,... | collective-permute-start | bytes 196616 | tf_op jit(solution)/shard_map/ppermute | solution.py:358
  57.5 2.3 %collective-permute-start.20 = (bf16[32,1024]{1,0:T(8,128)(2,1)S(1)}, bf16[32,1024]{1,0:T(8,128)(2,1)S(1)}, u32[]{:S(2)}, u32[]{:S(2)}) collective-permute-start(bf16[32,1024]{1,0:T(8,128)(2,1)S(1)} %get-tuple-element.57), channel_id=1, source_target_pairs={{0,24},{1,25},{2,26},{3,27},{4,28},{5,29},{6,30},{7,31},{8,16},{9,... | collective-permute-start | bytes 196616 | tf_op jit(solution)/shard_map/ppermute | solution.py:358
  59.7 1.2 %collective-permute-done.14.refs_2_ = bf16[64,1024]{1,0:T(8,128)(2,1)S(1)} collective-permute-done((bf16[64,1024]{1,0:T(8,128)(2,1)S(1)}, bf16[64,1024]{1,0:T(8,128)(2,1)S(1)}, u32[]{:S(2)}, u32[]{:S(2)}) %collective-permute-start.14) | collective-permute-done | bytes 131104 | tf_op jit(solution)/shard_map/ppermute | solution.py:358
  61.1 1.8 %shard_map.97 = (bf16[4096,512]{1,0:T(8,128)(2,1)}, f32[8,128]{1,0:T(8,128)S(1)}) custom-call(f32[32,1024]{1,0:T(8,128)S(1)} %get-tuple-element.46.after.refs_0_, bf16[256,512]{1,0:T(8,128)(2,1)S(1)} %get-tuple-element.41.logit_grad, bf16[4096,512]{1,0:T(8,128)(2,1)} %get-tuple-element.47.refs_0_, ...), custom_call_target="tpu_custom_call", output_to_operand_aliasing={{0}: (2, {})} | custom-call | flops 536870912 | bytes 10178560 | tf_op jit(solution)/shard_map/pallas_call | solution.py:33
  62.9 0.7 %collective-permute-done.20.refs_3_ = bf16[32,1024]{1,0:T(8,128)(2,1)S(1)} collective-permute-done((bf16[32,1024]{1,0:T(8,128)(2,1)S(1)}, bf16[32,1024]{1,0:T(8,128)(2,1)S(1)}, u32[]{:S(2)}, u32[]{:S(2)}) %collective-permute-start.20) | collective-permute-done | bytes 65568 | tf_op jit(solution)/shard_map/ppermute | solution.py:358
  63.6 1.7 %collective-permute-done.15.refs_1_ = bf16[32,1024]{1,0:T(8,128)(2,1)S(1)} collective-permute-done((bf16[32,1024]{1,0:T(8,128)(2,1)S(1)}, bf16[32,1024]{1,0:T(8,128)(2,1)S(1)}, u32[]{:S(2)}, u32[]{:S(2)}) %collective-permute-start.15) | collective-permute-done | bytes 65568 | tf_op jit(solution)/shard_map/ppermute | solution.py:358
  65.3 1.0 %shard_map.99 = (bf16[128,1024]{1,0:T(8,128)(2,1)}, f32[1,1]{1,0:T(1,128)}) custom-call(f32[8,128]{1,0:T(8,128)S(1)} %get-tuple-element.49.last, bf16[32,128]{1,0:T(8,128)(2,1)S(1)} %get-tuple-element.50.chosen, f32[32,1024]{1,0:T(8,128)S(1)} %get-tuple-element.46.after.refs_0_, bf16[32,1024]{1,0:T(8,128)(2,1)S(1)} %collective-permute-done.15.refs_1_, ...), custom_call_target="tpu_custom_call" | custom-call | bytes 602116 | tf_op jit(solution)/shard_map/pallas_call | solution.py:33
  (28 shorter events, 2.3 us)
Async XLA Ops:
  0.6 26.5 %copy-start = (f32[32]{0:T(128)S(1)}, f32[32]{0:T(128)}, u32[]{:S(2)}) copy-start(f32[32]{0:T(128)} %param.11) | copy-start | bytes 388
  1.9 8.0 %collective-permute-start = (bf16[272,128]{1,0:T(8,128)(2,1)S(1)}, bf16[272,128]{1,0:T(8,128)(2,1)S(1)}, u32[]{:S(2)}, u32[]{:S(2)}) collective-permute-start(bf16[272,128]{1,0:T(8,128)(2,1)S(1)} %get-tuple-element.32.refs_0_), channel_id=1, source_target_pairs={{0,16},{1,17},{2,18},{3,19},{4,20},{5,21},{6,22},{7,23},{8,24},{9,... | collective-permute-start | bytes 208904 | tf_op jit(solution)/shard_map/ppermute | solution.py:358
  6.0 6.3 %collective-permute-start.1 = (bf16[272,128]{1,0:T(8,128)(2,1)S(1)}, bf16[272,128]{1,0:T(8,128)(2,1)S(1)}, u32[]{:S(2)}, u32[]{:S(2)}) collective-permute-start(bf16[272,128]{1,0:T(8,128)(2,1)S(1)} %get-tuple-element.32.refs_0_), channel_id=1, source_target_pairs={{0,24},{1,25},{2,26},{3,27},{4,28},{5,29},{6,30},{7,31},{8,16},{9,... | collective-permute-start | bytes 208904 | tf_op jit(solution)/shard_map/ppermute | solution.py:358
  7.3 5.1 %collective-permute-start.2 = (bf16[272,128]{1,0:T(8,128)(2,1)S(1)}, bf16[272,128]{1,0:T(8,128)(2,1)S(1)}, u32[]{:S(2)}, u32[]{:S(2)}) collective-permute-start(bf16[272,128]{1,0:T(8,128)(2,1)S(1)} %get-tuple-element.32.refs_0_), channel_id=1, source_target_pairs={{0,8},{1,9},{2,10},{3,11},{4,12},{5,13},{6,14},{7,15},{8,0},{9,1},... | collective-permute-start | bytes 208904 | tf_op jit(solution)/shard_map/ppermute | solution.py:358
  12.4 12.9 %collective-permute-start.3 = (bf16[1088,128]{1,0:T(8,128)(2,1)S(1)}, bf16[1088,128]{1,0:T(8,128)(2,1)S(1)}, u32[]{:S(2)}, u32[]{:S(2)}) collective-permute-start(bf16[1088,128]{1,0:T(8,128)(2,1)S(1)} %get-tuple-element.33.own), channel_id=1, source_target_pairs={{0,4},{1,5},{2,6},{3,7},{4,0},{5,1},{6,2},{7,3},{8,12},{9,13},{10,... | collective-permute-start | bytes 835592 | tf_op jit(solution)/shard_map/ppermute | solution.py:358
  14.2 12.1 %collective-permute-start.5 = (bf16[128,1024]{1,0:T(8,128)(2,1)S(1)}, bf16[128,1024]{1,0:T(8,128)(2,1)S(1)}, u32[]{:S(2)}, u32[]{:S(2)}) collective-permute-start(bf16[128,1024]{1,0:T(8,128)(2,1)S(1)} %get-tuple-element.34.line), channel_id=1, source_target_pairs={{0,6},{1,7},{2,4},{3,5},{4,2},{5,3},{6,0},{7,1},{8,14},{9,15},{10,... | collective-permute-start | bytes 786440 | tf_op jit(solution)/shard_map/ppermute | solution.py:358
  15.6 10.6 %collective-permute-start.4 = (bf16[128,1024]{1,0:T(8,128)(2,1)S(1)}, bf16[128,1024]{1,0:T(8,128)(2,1)S(1)}, u32[]{:S(2)}, u32[]{:S(2)}) collective-permute-start(bf16[128,1024]{1,0:T(8,128)(2,1)S(1)} %get-tuple-element.34.line), channel_id=1, source_target_pairs={{0,2},{1,3},{2,0},{3,1},{4,6},{5,7},{6,4},{7,5},{8,10},{9,11},{10,... | collective-permute-start | bytes 786440 | tf_op jit(solution)/shard_map/ppermute | solution.py:358
  25.3 1.6 %collective-permute-start.6 = (bf16[128,1024]{1,0:T(8,128)(2,1)S(1)}, bf16[128,1024]{1,0:T(8,128)(2,1)S(1)}, u32[]{:S(2)}, u32[]{:S(2)}) collective-permute-start(bf16[128,1024]{1,0:T(8,128)(2,1)S(1)} %shard_map.89.refs_1_), channel_id=1, source_target_pairs={{0,1},{1,0},{2,3},{3,2},{4,5},{5,4},{6,7},{7,6},{8,9},{9,8},{10,11... | collective-permute-start | bytes 786440 | tf_op jit(solution)/shard_map/ppermute | solution.py:358
  25.4 2.9 %collective-permute-start.7 = (bf16[128,1024]{1,0:T(8,128)(2,1)S(1)}, bf16[128,1024]{1,0:T(8,128)(2,1)S(1)}, u32[]{:S(2)}, u32[]{:S(2)}) collective-permute-start(bf16[128,1024]{1,0:T(8,128)(2,1)S(1)} %get-tuple-element.36.after.refs_0_), channel_id=1, source_target_pairs={{0,1},{1,0},{2,3},{3,2},{4,5},{5,4},{6,7},{7,6},{8,9},{9,8},{10,11... | collective-permute-start | bytes 786440 | tf_op jit(solution)/shard_map/ppermute | solution.py:358
  26.2 2.1 %collective-permute-start.8 = (bf16[128,1024]{1,0:T(8,128)(2,1)S(1)}, bf16[128,1024]{1,0:T(8,128)(2,1)S(1)}, u32[]{:S(2)}, u32[]{:S(2)}) collective-permute-start(bf16[128,1024]{1,0:T(8,128)(2,1)S(1)} %collective-permute-done.4.refs_2_.refs_4_), channel_id=1, source_target_pairs={{0,1},{1,0},{2,3},{3,2},{4,5},{5,4},{6,7},{7,6},{8,9},{9,8},{10,11... | collective-permute-start | bytes 786440 | tf_op jit(solution)/shard_map/ppermute | solution.py:358
  26.9 1.5 %collective-permute-start.9 = (bf16[128,1024]{1,0:T(8,128)(2,1)S(1)}, bf16[128,1024]{1,0:T(8,128)(2,1)S(1)}, u32[]{:S(2)}, u32[]{:S(2)}) collective-permute-start(bf16[128,1024]{1,0:T(8,128)(2,1)S(1)} %shard_map.90.refs_3_.refs_5_), channel_id=1, source_target_pairs={{0,1},{1,0},{2,3},{3,2},{4,5},{5,4},{6,7},{7,6},{8,9},{9,8},{10,11... | collective-permute-start | bytes 786440 | tf_op jit(solution)/shard_map/ppermute | solution.py:358
  29.7 14.3 %collective-permute-start.11 = (bf16[2048,512]{1,0:T(8,128)(2,1)S(1)}, bf16[2048,512]{1,0:T(8,128)(2,1)S(1)}, u32[]{:S(2)}, u32[]{:S(2)}) collective-permute-start(bf16[2048,512]{1,0:T(8,128)(2,1)S(1)} %shard_map.93), channel_id=1, source_target_pairs={{0,1},{1,0},{2,3},{3,2},{4,5},{5,4},{6,7},{7,6},{8,9},{9,8},{10,11... | collective-permute-start | bytes 6291464 | tf_op jit(solution)/shard_map/ppermute | solution.py:358
  29.9 14.0 %collective-permute-start.10 = (f32[256,512]{1,0:T(8,128)S(1)}, f32[256,512]{1,0:T(8,128)S(1)}, u32[]{:S(2)}, u32[]{:S(2)}) collective-permute-start(f32[256,512]{1,0:T(8,128)S(1)} %get-tuple-element.37.mine), channel_id=1, source_target_pairs={{0,1},{1,0},{2,3},{3,2},{4,5},{5,4},{6,7},{7,6},{8,9},{9,8},{10,11... | collective-permute-start | bytes 1572872 | tf_op jit(solution)/shard_map/ppermute | solution.py:358
  45.7 5.7 %collective-permute-start.16 = (bf16[64,1024]{1,0:T(8,128)(2,1)S(1)}, bf16[64,1024]{1,0:T(8,128)(2,1)S(1)}, u32[]{:S(2)}, u32[]{:S(2)}) collective-permute-start(bf16[64,1024]{1,0:T(8,128)(2,1)S(1)} %get-tuple-element.53), channel_id=1, source_target_pairs={{0,4},{1,5},{2,6},{3,7},{4,0},{5,1},{6,2},{7,3},{8,12},{9,13},{10,... | collective-permute-start | bytes 393224 | tf_op jit(solution)/shard_map/ppermute | solution.py:358
  46.4 8.2 %collective-permute-start.17 = (bf16[64,1024]{1,0:T(8,128)(2,1)S(1)}, bf16[64,1024]{1,0:T(8,128)(2,1)S(1)}, u32[]{:S(2)}, u32[]{:S(2)}) collective-permute-start(bf16[64,1024]{1,0:T(8,128)(2,1)S(1)} %get-tuple-element.54), channel_id=1, source_target_pairs={{0,2},{1,3},{2,0},{3,1},{4,6},{5,7},{6,4},{7,5},{8,10},{9,11},{10,... | collective-permute-start | bytes 393224 | tf_op jit(solution)/shard_map/ppermute | solution.py:358
  47.1 9.3 %collective-permute-start.18 = (bf16[64,1024]{1,0:T(8,128)(2,1)S(1)}, bf16[64,1024]{1,0:T(8,128)(2,1)S(1)}, u32[]{:S(2)}, u32[]{:S(2)}) collective-permute-start(bf16[64,1024]{1,0:T(8,128)(2,1)S(1)} %get-tuple-element.55), channel_id=1, source_target_pairs={{0,6},{1,7},{2,4},{3,5},{4,2},{5,3},{6,0},{7,1},{8,14},{9,15},{10,... | collective-permute-start | bytes 393224 | tf_op jit(solution)/shard_map/ppermute | solution.py:358
  49.3 10.4 %collective-permute-start.12 = (bf16[64,1024]{1,0:T(8,128)(2,1)S(1)}, bf16[64,1024]{1,0:T(8,128)(2,1)S(1)}, u32[]{:S(2)}, u32[]{:S(2)}) collective-permute-start(bf16[64,1024]{1,0:T(8,128)(2,1)S(1)} %get-tuple-element.43), channel_id=1, source_target_pairs={{0,4},{1,5},{2,6},{3,7},{4,0},{5,1},{6,2},{7,3},{8,12},{9,13},{10,... | collective-permute-start | bytes 393224 | tf_op jit(solution)/shard_map/ppermute | solution.py:358
  49.9 9.8 %collective-permute-start.13 = (bf16[64,1024]{1,0:T(8,128)(2,1)S(1)}, bf16[64,1024]{1,0:T(8,128)(2,1)S(1)}, u32[]{:S(2)}, u32[]{:S(2)}) collective-permute-start(bf16[64,1024]{1,0:T(8,128)(2,1)S(1)} %get-tuple-element.44), channel_id=1, source_target_pairs={{0,2},{1,3},{2,0},{3,1},{4,6},{5,7},{6,4},{7,5},{8,10},{9,11},{10,... | collective-permute-start | bytes 393224 | tf_op jit(solution)/shard_map/ppermute | solution.py:358
  51.5 9.5 %collective-permute-start.14 = (bf16[64,1024]{1,0:T(8,128)(2,1)S(1)}, bf16[64,1024]{1,0:T(8,128)(2,1)S(1)}, u32[]{:S(2)}, u32[]{:S(2)}) collective-permute-start(bf16[64,1024]{1,0:T(8,128)(2,1)S(1)} %get-tuple-element.45), channel_id=1, source_target_pairs={{0,6},{1,7},{2,4},{3,5},{4,2},{5,3},{6,0},{7,1},{8,14},{9,15},{10,... | collective-permute-start | bytes 393224 | tf_op jit(solution)/shard_map/ppermute | solution.py:358
  56.5 6.4 %collective-permute-start.19 = (bf16[32,1024]{1,0:T(8,128)(2,1)S(1)}, bf16[32,1024]{1,0:T(8,128)(2,1)S(1)}, u32[]{:S(2)}, u32[]{:S(2)}) collective-permute-start(bf16[32,1024]{1,0:T(8,128)(2,1)S(1)} %get-tuple-element.56), channel_id=1, source_target_pairs={{0,16},{1,17},{2,18},{3,19},{4,20},{5,21},{6,22},{7,23},{8,24},{9,... | collective-permute-start | bytes 196616 | tf_op jit(solution)/shard_map/ppermute | solution.py:358
  57.5 6.2 %collective-permute-start.20 = (bf16[32,1024]{1,0:T(8,128)(2,1)S(1)}, bf16[32,1024]{1,0:T(8,128)(2,1)S(1)}, u32[]{:S(2)}, u32[]{:S(2)}) collective-permute-start(bf16[32,1024]{1,0:T(8,128)(2,1)S(1)} %get-tuple-element.57), channel_id=1, source_target_pairs={{0,24},{1,25},{2,26},{3,27},{4,28},{5,29},{6,30},{7,31},{8,16},{9,... | collective-permute-start | bytes 196616 | tf_op jit(solution)/shard_map/ppermute | solution.py:358
  61.0 4.3 %collective-permute-start.15 = (bf16[32,1024]{1,0:T(8,128)(2,1)S(1)}, bf16[32,1024]{1,0:T(8,128)(2,1)S(1)}, u32[]{:S(2)}, u32[]{:S(2)}) collective-permute-start(bf16[32,1024]{1,0:T(8,128)(2,1)S(1)} %get-tuple-element.51), channel_id=1, source_target_pairs={{0,8},{1,9},{2,10},{3,11},{4,12},{5,13},{6,14},{7,15},{8,0},{9,1},... | collective-permute-start | bytes 196616 | tf_op jit(solution)/shard_map/ppermute | solution.py:358

commit v15 on v13

--- a/solution.py
+++ b/solution.py
@@ -69,7 +69,7 @@
     return (slot.astype(jnp.int32) == grid) & (mask == 1)
 
 
-def pack_kernel(hidden_hbm, mask_hbm, target_hbm, turn_hbm, rows, chosen_out, *scratch):
+def pack_kernel(hidden_hbm, mask_hbm, target_hbm, turn_hbm, rows, plain, chosen_out, *scratch):
     hidden, mask, target, turn, sems = scratch
     copies = []
     for place, (source, held) in enumerate(
@@ -101,14 +101,20 @@
     rows[:, width:] = table.astype(jnp.bfloat16)
     copies[3].wait()
     packed = jnp.dot(one_hot, hidden[...], preferred_element_type=jnp.float32)
-    rows[:, :width] = packed.astype(jnp.bfloat16)
+    packed = packed.astype(jnp.bfloat16)
+    rows[:, :width] = packed
+    plain[...] = packed
 
 
 def join_kernel(order, *refs):
-    blocks, line, plain = refs[:-2], refs[-2], refs[-1]
+    blocks, (line, plain, far) = refs[:len(order) - 1] + refs[-4:-3], refs[-3:]
+    width = plain.shape[1]
     for place, block in zip(order, blocks):
-        line[place * CAP:(place + 1) * CAP] = block[...]
-        plain[place * CAP:(place + 1) * CAP] = block[:, :plain.shape[1]]
+        rows = slice(place * CAP, (place + 1) * CAP)
+        line[rows] = block[...]
+        plain[rows] = block[:, :width]
+        if place:
+            far[(place - 1) * CAP:place * CAP] = block[:, :width]
 
 
 def stage_kernel(blocks, line, weight, held, away, same, sems):
@@ -168,17 +174,19 @@
     return stats
 
 
-def all_rows(pieces, block, width):
-    return jnp.concatenate([ref[:, :width] for ref in pieces[2 * block:2 * block + 2]], axis=0)
-
-
-def some_logits(blocks, first, pieces, weight):
+def all_rows(pieces, counts, place, width):
+    start = sum(counts[:place])
+    return jnp.concatenate([ref[:, :width] for ref in pieces[start:start + counts[place]]], axis=0)
+
+
+def some_logits(counts, first, pieces, weight):
+    blocks = 2 * len(counts)
     width = weight.shape[0] // blocks
     rank, total = coordinates()[0], None
     for place, block in enumerate(range(first, blocks, 2)):
         start = pl.multiple_of((rank ^ block) * width, width)
         part = jnp.dot(
-            all_rows(pieces, place, width),
+            all_rows(pieces, counts, place, width),
             weight[pl.ds(start, width), :],
             preferred_element_type=jnp.float32,
         )
@@ -186,14 +194,14 @@
     return total
 
 
-def first_kernel(blocks, weight, *refs):
-    refs[-1][...] = some_logits(blocks, 0, refs[:-1], weight)
-
-
-def logits_kernel(blocks, groups, info, partial, weight, *refs):
+def first_kernel(counts, weight, *refs):
+    refs[-1][...] = some_logits(counts, 0, refs[:-1], weight)
+
+
+def logits_kernel(counts, groups, info, partial, weight, *refs):
     pieces, (logits, stats) = refs[:-2], refs[-2:]
     _, position, shard = coordinates()
-    total = partial[...] + some_logits(blocks, 1, pieces, weight)
+    total = partial[...] + some_logits(counts, 1, pieces, weight)
     logits[...] = total
     height, columns = total.shape
     target = info[:, 1:2].astype(jnp.int32) - shard * columns
@@ -251,14 +259,14 @@
             out[...] = total[quarter * part:(quarter + 1) * part].astype(out.dtype)
 
 
-def weight_kernel(blocks, skipped, after, logit_grad, *refs):
+def weight_kernel(blocks, counts, skipped, after, logit_grad, *refs):
     pieces, (out, last, done, sems) = refs[skipped:-4], refs[-4:]
     rank = coordinates()[0]
     width = done.shape[0] // len(blocks)
     copies = []
     for place, block in enumerate(blocks):
         done[place * width:(place + 1) * width] = lax.dot_general(
-            all_rows(pieces, place, width),
+            all_rows(pieces, counts, place, width),
             logit_grad[...],
             (((0,), (0,)), ((), ())),
             preferred_element_type=jnp.float32,
@@ -307,7 +315,6 @@
     total_rows = dps * CAP
     bf16, f32, i32 = jnp.bfloat16, jnp.float32, jnp.int32
     shape = jax.ShapeDtypeStruct
-    square = [(y, x) for x in reversed(range(xs)) for y in (1, 0) if x or y]
     flops = 2 * total_rows * depth * columns
 
     def send(value, z=0, y=0, x=0, core=0):
@@ -319,7 +326,7 @@
         ]
         return lax.ppermute(value, AXES, pairs)
 
-    packed, chosen = call(
+    packed, own, chosen = call(
         pack_kernel,
         (
             in_hbm(hidden),
@@ -330,25 +337,36 @@
         [HBM] * 4,
         (
             shape((CAP, width + IDS), bf16),
+            shape((CAP, width), bf16),
             shape((CAP, tokens), bf16),
         ),
-        (VMEM,) * 2,
+        (VMEM,) * 3,
         [pltpu.VMEM((tokens, width), bf16)]
         + [pltpu.VMEM((1, tokens), i32)] * 3
         + [pltpu.SemaphoreType.DMA((4,))],
     )
 
     line_order = [0, *range(2, zs), 1]
-    blocks = [send(packed, z=z) if z else packed for z in line_order]
+    blocks = [send(packed, z=z) if z else packed for z in line_order[:-1]]
+    corners = {x: send(own, y=1, x=x) for x in range(1, xs)}
+    blocks.append(send(packed, z=1))
     line_rows = zs * CAP
-    line, line_plain = call(
+    line, line_plain, far = call(
         functools.partial(join_kernel, line_order),
-        blocks,
-        [VMEM] * zs,
-        (shape((line_rows, width + IDS), bf16), shape((line_rows, width), bf16)),
-        (VMEM, VMEM),
-    )
-    pieces = {(2 * x, y): send(line_plain if x else line, y=y, x=x) for y, x in square}
+        (*blocks[:-1], *corners.values(), blocks[-1]),
+        [VMEM] * (zs - 1) + [ANY] * len(corners) + [VMEM],
+        (
+            shape((line_rows, width + IDS), bf16),
+            shape((line_rows, width), bf16),
+            shape((line_rows - CAP, width), bf16),
+        ),
+        (VMEM,) * 3,
+    )
+    pieces = {(0, 1, 0): send(line, y=1)}
+    for x in range(1, xs):
+        pieces[2 * x, 0, 0] = send(line_plain, x=x)
+        pieces[2 * x, 1, 0] = corners[x]
+        pieces[2 * x, 1, 1] = send(far, y=1, x=x)
     held, away, same = call(
         functools.partial(stage_kernel, ranks),
         (line, in_hbm(weight)),
@@ -361,32 +379,38 @@
         (VMEM,) * 3,
         [pltpu.SemaphoreType.DMA((ranks + xs,))],
     )
-    pieces[0, 0] = same
-    for b, y in list(pieces):
-        pieces[b + 1, y] = send(pieces[b, y], core=1)
-    rows = [pieces[b, y] for b in range(ranks) for y in range(2)]
+    pieces[0, 0, 0] = same
+    for b, y, part in list(pieces):
+        pieces[b + 1, y, part] = send(pieces[b, y, part], core=1)
+    parted = [[pieces[key] for key in sorted(pieces) if key[0] == b] for b in range(ranks)]
+
+    def rows_of(blocks):
+        return [piece for b in blocks for piece in parted[b]]
+
+    def counts_of(blocks):
+        return [len(parted[b]) for b in blocks]
 
     info = call(
         info_kernel,
-        (*rows[:2], advantages.reshape(1, -1)),
-        [VMEM] * 3,
+        (*parted[0], advantages.reshape(1, -1)),
+        [VMEM] * (1 + len(parted[0])),
         shape((total_rows, 128), f32),
         VMEM,
     )
-    near = [pieces[b, y] for b in range(0, ranks, 2) for y in range(2)]
+    near = range(0, ranks, 2)
     partial = call(
-        functools.partial(first_kernel, ranks),
-        (held, *near),
-        [VMEM] * (1 + len(near)),
+        functools.partial(first_kernel, counts_of(near)),
+        (held, *rows_of(near)),
+        [VMEM] * (1 + sum(counts_of(near))),
         shape((total_rows, columns), f32),
         VMEM,
         flops=flops // 2,
     )
-    beside = [pieces[b, y] for b in range(1, ranks, 2) for y in range(2)]
+    beside = range(1, ranks, 2)
     logits, stats = call(
-        functools.partial(logits_kernel, ranks, dps),
-        (info, partial, held, *beside),
-        [VMEM] * (3 + len(beside)),
+        functools.partial(logits_kernel, counts_of(beside), dps),
+        (info, partial, held, *rows_of(beside)),
+        [VMEM] * (3 + sum(counts_of(beside))),
         (
             shape((total_rows, columns), f32),
             shape((dps * ranks, 1, 2 * total_rows + 128), f32),
@@ -420,9 +444,9 @@
 
     def weight_part(first, after, *extra):
         blocks = range(first, first + ranks // 2)
-        chosen_rows = rows[2 * first:2 * first + ranks]
+        chosen_rows = rows_of(blocks)
         return call(
-            functools.partial(weight_kernel, blocks, len(extra)),
+            functools.partial(weight_kernel, blocks, counts_of(blocks), len(extra)),
             (after, logit_grad, *extra, *chosen_rows),
             [ANY, VMEM] + [HBM] * (len(extra) > 0)
             + [VMEM] * (max(len(extra) - 1, 0) + len(chosen_rows)),

time: 66 us -> 64.8 us (0.982)
  waiting for transfers between devices: 19 us -> 14.7 us
  starting transfers between devices: 19.3 us -> 22.3 us
    ppermute x21 -> x23, waiting for transfers between devices: 19 us -> 14.7 us  [send(): return lax.ppermute(value, AXES, pairs)]
    ppermute x21 -> x23, starting transfers between devices: 19.3 us -> 22.3 us  [send(): return lax.ppermute(value, AXES, pairs)]
  transfers between devices with their start and end apart: 21 -> 23, of which waited for: 12 -> 9; matrix products, arithmetic and copies ran while one was open for 0% -> 0% of each run, Pallas kernels for 12% -> 12%
where the time goes in v15:
time: 64.8 us; the launch traced here: 64.6 us
  starting transfers between devices  22.3 us (34%)
  waiting for transfers between devices  14.7 us (23%)
  blocking collectives  13.9 us (21%)
  Pallas kernels  12.9 us (20%)
  between operations  0.82 us (1%)
    ppermute x23, starting transfers between devices, send(): return lax.ppermute(value, AXES, pairs)  22.3 us
    ppermute x23, waiting for transfers between devices, send(): return lax.ppermute(value, AXES, pairs)  14.7 us
    all_to_all x1, blocking collectives, body(): stats = lax.all_to_all(stats, AXES, 0, 0)  13.9 us
    pallas_call x13, Pallas kernels, call(): pl.pallas_call(kernel, out_shape=out_shape, in_specs=in_specs, out_specs=...  12.9 us
  transfers between devices with their start and end apart: 23, of which 9 were waited for; matrix products, arithmetic and copies ran while one was open for 0% of the time, Pallas kernels for 12%

profile of v15, /device:TPU:0, one launch (start us, length us, event | category | flops | bytes accessed | tf_op | source)
XLA Modules:
  0.0 64.6 jit_solution(18355500725784361844)
XLA Ops:
  0.6 1.2 %shard_map.85 = (bf16[32,1152]{1,0:T(8,128)(2,1)S(1)}, bf16[32,1024]{1,0:T(8,128)(2,1)S(1)}, bf16[32,128]{1,0:T(8,128)(2,1)S(1)}) custom-call(bf16[128,1024]{1,0:T(8,128)(2,1)} %hidden_hbm.1, s32[1,128]{1,0:T(1,128)} %bitcast.6, s32[1,128]{1,0:T(1,128)} %bitcast.7, s32[1,128]{1,0:T(1,128)} %bitcast.8), custom_call_target="tpu_custom_call" | custom-call | bytes 411136 | tf_op jit(solution)/shard_map/pallas_call | solution.py:32
  1.9 4.1 %collective-permute-start = (bf16[32,1152]{1,0:T(8,128)(2,1)S(1)}, bf16[32,1152]{1,0:T(8,128)(2,1)S(1)}, u32[]{:S(2)}, u32[]{:S(2)}) collective-permute-start(bf16[32,1152]{1,0:T(8,128)(2,1)S(1)} %get-tuple-element.34.refs_0_), channel_id=1, source_target_pairs={{0,16},{1,17},{2,18},{3,19},{4,20},{5,21},{6,22},{7,23},{8,24},{9,... | collective-permute-start | bytes 221192 | tf_op jit(solution)/shard_map/ppermute | solution.py:327
  6.0 1.3 %collective-permute-start.1 = (bf16[32,1152]{1,0:T(8,128)(2,1)S(1)}, bf16[32,1152]{1,0:T(8,128)(2,1)S(1)}, u32[]{:S(2)}, u32[]{:S(2)}) collective-permute-start(bf16[32,1152]{1,0:T(8,128)(2,1)S(1)} %get-tuple-element.34.refs_0_), channel_id=1, source_target_pairs={{0,24},{1,25},{2,26},{3,27},{4,28},{5,29},{6,30},{7,31},{8,16},{9,... | collective-permute-start | bytes 221192 | tf_op jit(solution)/shard_map/ppermute | solution.py:327
  7.5 2.4 %collective-permute-start.2 = (bf16[32,1024]{1,0:T(8,128)(2,1)S(1)}, bf16[32,1024]{1,0:T(8,128)(2,1)S(1)}, u32[]{:S(2)}, u32[]{:S(2)}) collective-permute-start(bf16[32,1024]{1,0:T(8,128)(2,1)S(1)} %get-tuple-element.35), channel_id=1, source_target_pairs={{0,6},{1,7},{2,4},{3,5},{4,2},{5,3},{6,0},{7,1},{8,14},{9,15},{10,... | collective-permute-start | bytes 196616 | tf_op jit(solution)/shard_map/ppermute | solution.py:327
  10.0 2.7 %collective-permute-done.2.refs_3_.refs_5_ = bf16[32,1024]{1,0:T(8,128)(2,1)S(1)} collective-permute-done((bf16[32,1024]{1,0:T(8,128)(2,1)S(1)}, bf16[32,1024]{1,0:T(8,128)(2,1)S(1)}, u32[]{:S(2)}, u32[]{:S(2)}) %collective-permute-start.2) | collective-permute-done | bytes 65568 | tf_op jit(solution)/shard_map/ppermute | solution.py:327
  12.8 1.7 %collective-permute-start.4 = (bf16[128,1152]{1,0:T(8,128)(2,1)S(1)}, bf16[128,1152]{1,0:T(8,128)(2,1)S(1)}, u32[]{:S(2)}, u32[]{:S(2)}) collective-permute-start(bf16[128,1152]{1,0:T(8,128)(2,1)S(1)} %get-tuple-element.36.line), channel_id=1, source_target_pairs={{0,4},{1,5},{2,6},{3,7},{4,0},{5,1},{6,2},{7,3},{8,12},{9,13},{10,... | collective-permute-start | bytes 884744 | tf_op jit(solution)/shard_map/ppermute | solution.py:327
  14.5 1.5 %collective-permute-start.5 = (bf16[128,1024]{1,0:T(8,128)(2,1)S(1)}, bf16[128,1024]{1,0:T(8,128)(2,1)S(1)}, u32[]{:S(2)}, u32[]{:S(2)}) collective-permute-start(bf16[128,1024]{1,0:T(8,128)(2,1)S(1)} %get-tuple-element.39), channel_id=1, source_target_pairs={{0,2},{1,3},{2,0},{3,1},{4,6},{5,7},{6,4},{7,5},{8,10},{9,11},{10,... | collective-permute-start | bytes 786440 | tf_op jit(solution)/shard_map/ppermute | solution.py:327
  16.3 2.9 %shard_map.87 = (bf16[4096,512]{1,0:T(8,128)(2,1)S(1)}, bf16[2048,512]{1,0:T(8,128)(2,1)S(1)}, bf16[128,1152]{1,0:T(8,128)(2,1)S(1)}) custom-call(bf16[128,1152]{1,0:T(8,128)(2,1)S(1)} %get-tuple-element.36.line, bf16[4096,512]{1,0:T(8,128)(2,1)} %weight.1), custom_call_target="tpu_custom_call" | custom-call | bytes 11075584 | tf_op jit(solution)/shard_map/pallas_call | solution.py:32
  19.3 3.1 %collective-permute-done.4.refs_1_ = bf16[128,1152]{1,0:T(8,128)(2,1)S(1)} collective-permute-done((bf16[128,1152]{1,0:T(8,128)(2,1)S(1)}, bf16[128,1152]{1,0:T(8,128)(2,1)S(1)}, u32[]{:S(2)}, u32[]{:S(2)}) %collective-permute-start.4) | collective-permute-done | bytes 294944 | tf_op jit(solution)/shard_map/ppermute | solution.py:327
  22.4 0.7 %collective-permute-done.5.refs_2_.refs_4_ = bf16[128,1024]{1,0:T(8,128)(2,1)S(1)} collective-permute-done((bf16[128,1024]{1,0:T(8,128)(2,1)S(1)}, bf16[128,1024]{1,0:T(8,128)(2,1)S(1)}, u32[]{:S(2)}, u32[]{:S(2)}) %collective-permute-start.5) | collective-permute-done | bytes 262176 | tf_op jit(solution)/shard_map/ppermute | solution.py:327
  23.0 1.9 %collective-permute-done.6.refs_4_.refs_6_ = bf16[96,1024]{1,0:T(8,128)(2,1)S(1)} collective-permute-done((bf16[96,1024]{1,0:T(8,128)(2,1)S(1)}, bf16[96,1024]{1,0:T(8,128)(2,1)S(1)}, u32[]{:S(2)}, u32[]{:S(2)}) %collective-permute-start.6) | collective-permute-done | bytes 196640 | tf_op jit(solution)/shard_map/ppermute | solution.py:327
  24.9 0.5 collective-permute-start.10
  25.9 0.7 %shard_map.89.partial = f32[256,512]{1,0:T(8,128)S(1)} custom-call(bf16[4096,512]{1,0:T(8,128)(2,1)S(1)} %get-tuple-element.38.weight, bf16[128,1152]{1,0:T(8,128)(2,1)S(1)} %get-tuple-element.37.refs_0_, bf16[128,1152]{1,0:T(8,128)(2,1)S(1)} %collective-permute-done.4.refs_1_, bf16[128,1024]{1,0:T(8,128)(2,1)S(1)} %collective-permute-done.5.refs_2_.refs_4_, ...), custom_call_target="tpu_custom_call" | custom-call | flops 536870912 | bytes 5832704 | tf_op jit(solution)/shard_map/pallas_call | solution.py:32
  26.6 1.2 %shard_map.90 = (f32[256,512]{1,0:T(8,128)S(1)}, f32[32,1,640]{2,1,0:T(1,128)S(1)}) custom-call(f32[256,128]{1,0:T(8,128)S(1)} %shard_map.88.info.refs_1_, f32[256,512]{1,0:T(8,128)S(1)} %shard_map.89.partial, bf16[4096,512]{1,0:T(8,128)(2,1)S(1)} %get-tuple-element.38.weight, bf16[128,1152]{1,0:T(8,128)(2,1)S(1)} %collective-permute-done.7.refs_0_.refs_2_, ...), custom_call_target="tpu_custom_call" | custom-call | flops 536870912 | bytes 6569984 | tf_op jit(solution)/shard_map/pallas_call | solution.py:32
  28.4 13.9 %all_to_all.5.stats.refs_3_ = f32[32,1,640]{2,1,0:T(1,128)S(1)} all-to-all(f32[32,1,640]{2,1,0:T(1,128)S(1)} %get-tuple-element.43.after), channel_id=1, replica_groups=mesh['dp'=8,'vocab'=4] {'dp','vocab'}, dimensions={0} | all-to-all | bytes 163840 | tf_op jit(solution)/shard_map/all_to_all | solution.py:426
  42.3 1.8 %shard_map.92 = (bf16[256,512]{1,0:T(8,128)(2,1)S(1)}, f32[256,128]{1,0:T(8,128)S(1)}, bf16[64,1024]{1,0:T(8,128)(2,1)S(1)}, bf16[64,1024]{1,0:T(8,128)(2,1)S(1)...) custom-call(f32[256,128]{1,0:T(8,128)S(1)} %shard_map.88.info.refs_1, ...), custom_call_target="tpu_custom_call" | custom-call | flops 1073741824 | bytes 9256960 | tf_op jit(solution)/shard_map/pallas_call | solution.py:32
  44.1 0.7 %collective-permute-start.18 = (bf16[64,1024]{1,0:T(8,128)(2,1)S(1)}, bf16[64,1024]{1,0:T(8,128)(2,1)S(1)}, u32[]{:S(2)}, u32[]{:S(2)}) collective-permute-start(bf16[64,1024]{1,0:T(8,128)(2,1)S(1)} %get-tuple-element.57), channel_id=1, source_target_pairs={{0,4},{1,5},{2,6},{3,7},{4,0},{5,1},{6,2},{7,3},{8,12},{9,13},{10,... | collective-permute-start | bytes 393224 | tf_op jit(solution)/shard_map/ppermute | solution.py:327
  44.8 0.7 %collective-permute-start.19 = (bf16[64,1024]{1,0:T(8,128)(2,1)S(1)}, bf16[64,1024]{1,0:T(8,128)(2,1)S(1)}, u32[]{:S(2)}, u32[]{:S(2)}) collective-permute-start(bf16[64,1024]{1,0:T(8,128)(2,1)S(1)} %get-tuple-element.58), channel_id=1, source_target_pairs={{0,2},{1,3},{2,0},{3,1},{4,6},{5,7},{6,4},{7,5},{8,10},{9,11},{10,... | collective-permute-start | bytes 393224 | tf_op jit(solution)/shard_map/ppermute | solution.py:327
  45.5 2.2 %collective-permute-start.20 = (bf16[64,1024]{1,0:T(8,128)(2,1)S(1)}, bf16[64,1024]{1,0:T(8,128)(2,1)S(1)}, u32[]{:S(2)}, u32[]{:S(2)}) collective-permute-start(bf16[64,1024]{1,0:T(8,128)(2,1)S(1)} %get-tuple-element.59), channel_id=1, source_target_pairs={{0,6},{1,7},{2,4},{3,5},{4,2},{5,3},{6,0},{7,1},{8,14},{9,15},{10,... | collective-permute-start | bytes 393224 | tf_op jit(solution)/shard_map/ppermute | solution.py:327
  47.6 0.6 collective-permute-start.14
  48.3 0.7 %collective-permute-start.15 = (bf16[64,1024]{1,0:T(8,128)(2,1)S(1)}, bf16[64,1024]{1,0:T(8,128)(2,1)S(1)}, u32[]{:S(2)}, u32[]{:S(2)}) collective-permute-start(bf16[64,1024]{1,0:T(8,128)(2,1)S(1)} %get-tuple-element.48), channel_id=1, source_target_pairs={{0,2},{1,3},{2,0},{3,1},{4,6},{5,7},{6,4},{7,5},{8,10},{9,11},{10,... | collective-permute-start | bytes 393224 | tf_op jit(solution)/shard_map/ppermute | solution.py:327
  49.0 0.8 %collective-permute-done.18.refs_0_ = bf16[64,1024]{1,0:T(8,128)(2,1)S(1)} collective-permute-done((bf16[64,1024]{1,0:T(8,128)(2,1)S(1)}, bf16[64,1024]{1,0:T(8,128)(2,1)S(1)}, u32[]{:S(2)}, u32[]{:S(2)}) %collective-permute-start.18) | collective-permute-done | bytes 131104 | tf_op jit(solution)/shard_map/ppermute | solution.py:327
  49.8 1.3 %collective-permute-start.16 = (bf16[64,1024]{1,0:T(8,128)(2,1)S(1)}, bf16[64,1024]{1,0:T(8,128)(2,1)S(1)}, u32[]{:S(2)}, u32[]{:S(2)}) collective-permute-start(bf16[64,1024]{1,0:T(8,128)(2,1)S(1)} %get-tuple-element.49), channel_id=1, source_target_pairs={{0,6},{1,7},{2,4},{3,5},{4,2},{5,3},{6,0},{7,1},{8,14},{9,15},{10,... | collective-permute-start | bytes 393224 | tf_op jit(solution)/shard_map/ppermute | solution.py:327
  51.1 1.8 %shard_map.93 = (bf16[4096,512]{1,0:T(8,128)(2,1)}, f32[8,128]{1,0:T(8,128)S(1)}) custom-call(f32[64,1024]{1,0:T(8,128)S(1)} %get-tuple-element.44.after.kept, bf16[256,512]{1,0:T(8,128)(2,1)S(1)} %get-tuple-element.45.logit_grad, bf16[128,1152]{1,0:T(8,128)(2,1)S(1)} %get-tuple-element.37.refs_0_, bf16[128,1152]{1,0:T(8,128)(2,1)S(1)} %collective-permute-done.4.refs_1_, ...), custom_call_target="tpu_custom_call" | custom-call | flops 536870912 | bytes 5902336 | tf_op jit(solution)/shard_map/pallas_call | solution.py:32
  52.9 1.9 %collective-permute-done.20.refs_2_ = bf16[64,1024]{1,0:T(8,128)(2,1)S(1)} collective-permute-done((bf16[64,1024]{1,0:T(8,128)(2,1)S(1)}, bf16[64,1024]{1,0:T(8,128)(2,1)S(1)}, u32[]{:S(2)}, u32[]{:S(2)}) %collective-permute-start.20) | collective-permute-done | bytes 131104 | tf_op jit(solution)/shard_map/ppermute | solution.py:327
  54.9 0.9 %collective-permute-start.21 = (bf16[32,1024]{1,0:T(8,128)(2,1)S(1)}, bf16[32,1024]{1,0:T(8,128)(2,1)S(1)}, u32[]{:S(2)}, u32[]{:S(2)}) collective-permute-start(bf16[32,1024]{1,0:T(8,128)(2,1)S(1)} %get-tuple-element.60), channel_id=1, source_target_pairs={{0,16},{1,17},{2,18},{3,19},{4,20},{5,21},{6,22},{7,23},{8,24},{9,... | collective-permute-start | bytes 196616 | tf_op jit(solution)/shard_map/ppermute | solution.py:327
  55.8 2.3 %collective-permute-start.22 = (bf16[32,1024]{1,0:T(8,128)(2,1)S(1)}, bf16[32,1024]{1,0:T(8,128)(2,1)S(1)}, u32[]{:S(2)}, u32[]{:S(2)}) collective-permute-start(bf16[32,1024]{1,0:T(8,128)(2,1)S(1)} %get-tuple-element.61), channel_id=1, source_target_pairs={{0,24},{1,25},{2,26},{3,27},{4,28},{5,29},{6,30},{7,31},{8,16},{9,... | collective-permute-start | bytes 196616 | tf_op jit(solution)/shard_map/ppermute | solution.py:327
  58.1 1.2 %collective-permute-done.16.refs_2_ = bf16[64,1024]{1,0:T(8,128)(2,1)S(1)} collective-permute-done((bf16[64,1024]{1,0:T(8,128)(2,1)S(1)}, bf16[64,1024]{1,0:T(8,128)(2,1)S(1)}, u32[]{:S(2)}, u32[]{:S(2)}) %collective-permute-start.16) | collective-permute-done | bytes 131104 | tf_op jit(solution)/shard_map/ppermute | solution.py:327
  59.4 1.8 %shard_map.95 = (bf16[4096,512]{1,0:T(8,128)(2,1)}, f32[8,128]{1,0:T(8,128)S(1)}) custom-call(f32[32,1024]{1,0:T(8,128)S(1)} %get-tuple-element.50.after.refs_0_, bf16[256,512]{1,0:T(8,128)(2,1)S(1)} %get-tuple-element.45.logit_grad, bf16[4096,512]{1,0:T(8,128)(2,1)} %get-tuple-element.51.refs_0_, ...), custom_call_target="tpu_custom_call", output_to_operand_aliasing={{0}: (2, {})} | custom-call | flops 536870912 | bytes 10178560 | tf_op jit(solution)/shard_map/pallas_call | solution.py:32
  61.2 0.7 %collective-permute-done.22.refs_3_ = bf16[32,1024]{1,0:T(8,128)(2,1)S(1)} collective-permute-done((bf16[32,1024]{1,0:T(8,128)(2,1)S(1)}, bf16[32,1024]{1,0:T(8,128)(2,1)S(1)}, u32[]{:S(2)}, u32[]{:S(2)}) %collective-permute-start.22) | collective-permute-done | bytes 65568 | tf_op jit(solution)/shard_map/ppermute | solution.py:327
  62.0 1.7 %collective-permute-done.17.refs_1_ = bf16[32,1024]{1,0:T(8,128)(2,1)S(1)} collective-permute-done((bf16[32,1024]{1,0:T(8,128)(2,1)S(1)}, bf16[32,1024]{1,0:T(8,128)(2,1)S(1)}, u32[]{:S(2)}, u32[]{:S(2)}) %collective-permute-start.17) | collective-permute-done | bytes 65568 | tf_op jit(solution)/shard_map/ppermute | solution.py:327
  63.7 1.0 %shard_map.97 = (bf16[128,1024]{1,0:T(8,128)(2,1)}, f32[1,1]{1,0:T(1,128)}) custom-call(f32[8,128]{1,0:T(8,128)S(1)} %get-tuple-element.53.last, bf16[32,128]{1,0:T(8,128)(2,1)S(1)} %get-tuple-element.54.chosen, f32[32,1024]{1,0:T(8,128)S(1)} %get-tuple-element.50.after.refs_0_, bf16[32,1024]{1,0:T(8,128)(2,1)S(1)} %collective-permute-done.17.refs_1_, ...), custom_call_target="tpu_custom_call" | custom-call | bytes 602116 | tf_op jit(solution)/shard_map/pallas_call | solution.py:32
  (30 shorter events, 2.0 us)
Async XLA Ops:
  0.6 24.8 %copy-start = (f32[32]{0:T(128)S(1)}, f32[32]{0:T(128)}, u32[]{:S(2)}) copy-start(f32[32]{0:T(128)} %param.11) | copy-start | bytes 388
  1.9 10.8 %collective-permute-start = (bf16[32,1152]{1,0:T(8,128)(2,1)S(1)}, bf16[32,1152]{1,0:T(8,128)(2,1)S(1)}, u32[]{:S(2)}, u32[]{:S(2)}) collective-permute-start(bf16[32,1152]{1,0:T(8,128)(2,1)S(1)} %get-tuple-element.34.refs_0_), channel_id=1, source_target_pairs={{0,16},{1,17},{2,18},{3,19},{4,20},{5,21},{6,22},{7,23},{8,24},{9,... | collective-permute-start | bytes 221192 | tf_op jit(solution)/shard_map/ppermute | solution.py:327
  6.0 6.8 %collective-permute-start.1 = (bf16[32,1152]{1,0:T(8,128)(2,1)S(1)}, bf16[32,1152]{1,0:T(8,128)(2,1)S(1)}, u32[]{:S(2)}, u32[]{:S(2)}) collective-permute-start(bf16[32,1152]{1,0:T(8,128)(2,1)S(1)} %get-tuple-element.34.refs_0_), channel_id=1, source_target_pairs={{0,24},{1,25},{2,26},{3,27},{4,28},{5,29},{6,30},{7,31},{8,16},{9,... | collective-permute-start | bytes 221192 | tf_op jit(solution)/shard_map/ppermute | solution.py:327
  7.3 5.4 %collective-permute-start.3 = (bf16[32,1152]{1,0:T(8,128)(2,1)S(1)}, bf16[32,1152]{1,0:T(8,128)(2,1)S(1)}, u32[]{:S(2)}, u32[]{:S(2)}) collective-permute-start(bf16[32,1152]{1,0:T(8,128)(2,1)S(1)} %get-tuple-element.34.refs_0_), channel_id=1, source_target_pairs={{0,8},{1,9},{2,10},{3,11},{4,12},{5,13},{6,14},{7,15},{8,0},{9,1},... | collective-permute-start | bytes 221192 | tf_op jit(solution)/shard_map/ppermute | solution.py:327
  7.5 5.2 %collective-permute-start.2 = (bf16[32,1024]{1,0:T(8,128)(2,1)S(1)}, bf16[32,1024]{1,0:T(8,128)(2,1)S(1)}, u32[]{:S(2)}, u32[]{:S(2)}) collective-permute-start(bf16[32,1024]{1,0:T(8,128)(2,1)S(1)} %get-tuple-element.35), channel_id=1, source_target_pairs={{0,6},{1,7},{2,4},{3,5},{4,2},{5,3},{6,0},{7,1},{8,14},{9,15},{10,... | collective-permute-start | bytes 196616 | tf_op jit(solution)/shard_map/ppermute | solution.py:327
  12.8 9.6 %collective-permute-start.4 = (bf16[128,1152]{1,0:T(8,128)(2,1)S(1)}, bf16[128,1152]{1,0:T(8,128)(2,1)S(1)}, u32[]{:S(2)}, u32[]{:S(2)}) collective-permute-start(bf16[128,1152]{1,0:T(8,128)(2,1)S(1)} %get-tuple-element.36.line), channel_id=1, source_target_pairs={{0,4},{1,5},{2,6},{3,7},{4,0},{5,1},{6,2},{7,3},{8,12},{9,13},{10,... | collective-permute-start | bytes 884744 | tf_op jit(solution)/shard_map/ppermute | solution.py:327
  14.5 8.6 %collective-permute-start.5 = (bf16[128,1024]{1,0:T(8,128)(2,1)S(1)}, bf16[128,1024]{1,0:T(8,128)(2,1)S(1)}, u32[]{:S(2)}, u32[]{:S(2)}) collective-permute-start(bf16[128,1024]{1,0:T(8,128)(2,1)S(1)} %get-tuple-element.39), channel_id=1, source_target_pairs={{0,2},{1,3},{2,0},{3,1},{4,6},{5,7},{6,4},{7,5},{8,10},{9,11},{10,... | collective-permute-start | bytes 786440 | tf_op jit(solution)/shard_map/ppermute | solution.py:327
  15.9 9.0 %collective-permute-start.6 = (bf16[96,1024]{1,0:T(8,128)(2,1)S(1)}, bf16[96,1024]{1,0:T(8,128)(2,1)S(1)}, u32[]{:S(2)}, u32[]{:S(2)}) collective-permute-start(bf16[96,1024]{1,0:T(8,128)(2,1)S(1)} %get-tuple-element.40), channel_id=1, source_target_pairs={{0,6},{1,7},{2,4},{3,5},{4,2},{5,3},{6,0},{7,1},{8,14},{9,15},{10,... | collective-permute-start | bytes 589832 | tf_op jit(solution)/shard_map/ppermute | solution.py:327
  19.2 7.4 %collective-permute-start.7 = (bf16[128,1152]{1,0:T(8,128)(2,1)S(1)}, bf16[128,1152]{1,0:T(8,128)(2,1)S(1)}, u32[]{:S(2)}, u32[]{:S(2)}) collective-permute-start(bf16[128,1152]{1,0:T(8,128)(2,1)S(1)} %get-tuple-element.37.refs_0_), channel_id=1, source_target_pairs={{0,1},{1,0},{2,3},{3,2},{4,5},{5,4},{6,7},{7,6},{8,9},{9,8},{10,11... | collective-permute-start | bytes 884744 | tf_op jit(solution)/shard_map/ppermute | solution.py:327
  22.4 4.3 %collective-permute-start.8 = (bf16[128,1152]{1,0:T(8,128)(2,1)S(1)}, bf16[128,1152]{1,0:T(8,128)(2,1)S(1)}, u32[]{:S(2)}, u32[]{:S(2)}) collective-permute-start(bf16[128,1152]{1,0:T(8,128)(2,1)S(1)} %collective-permute-done.4.refs_1_), channel_id=1, source_target_pairs={{0,1},{1,0},{2,3},{3,2},{4,5},{5,4},{6,7},{7,6},{8,9},{9,8},{10,11... | collective-permute-start | bytes 884744 | tf_op jit(solution)/shard_map/ppermute | solution.py:327
  23.0 3.6 %collective-permute-start.9 = (bf16[128,1024]{1,0:T(8,128)(2,1)S(1)}, bf16[128,1024]{1,0:T(8,128)(2,1)S(1)}, u32[]{:S(2)}, u32[]{:S(2)}) collective-permute-start(bf16[128,1024]{1,0:T(8,128)(2,1)S(1)} %collective-permute-done.5.refs_2_.refs_4_), channel_id=1, source_target_pairs={{0,1},{1,0},{2,3},{3,2},{4,5},{5,4},{6,7},{7,6},{8,9},{9,8},{10,11... | collective-permute-start | bytes 786440 | tf_op jit(solution)/shard_map/ppermute | solution.py:327
  24.9 1.7 %collective-permute-start.11 = (bf16[96,1024]{1,0:T(8,128)(2,1)S(1)}, bf16[96,1024]{1,0:T(8,128)(2,1)S(1)}, u32[]{:S(2)}, u32[]{:S(2)}) collective-permute-start(bf16[96,1024]{1,0:T(8,128)(2,1)S(1)} %collective-permute-done.6.refs_4_.refs_6_), channel_id=1, source_target_pairs={{0,1},{1,0},{2,3},{3,2},{4,5},{5,4},{6,7},{7,6},{8,9},{9,8},{10,11... | collective-permute-start | bytes 589832 | tf_op jit(solution)/shard_map/ppermute | solution.py:327
  24.9 1.6 %collective-permute-start.10 = (bf16[32,1024]{1,0:T(8,128)(2,1)S(1)}, bf16[32,1024]{1,0:T(8,128)(2,1)S(1)}, u32[]{:S(2)}, u32[]{:S(2)}) collective-permute-start(bf16[32,1024]{1,0:T(8,128)(2,1)S(1)} %collective-permute-done.2.refs_3_.refs_5_), channel_id=1, source_target_pairs={{0,1},{1,0},{2,3},{3,2},{4,5},{5,4},{6,7},{7,6},{8,9},{9,8},{10,11... | collective-permute-start | bytes 196616 | tf_op jit(solution)/shard_map/ppermute | solution.py:327
  27.8 14.5 %collective-permute-start.13 = (bf16[2048,512]{1,0:T(8,128)(2,1)S(1)}, bf16[2048,512]{1,0:T(8,128)(2,1)S(1)}, u32[]{:S(2)}, u32[]{:S(2)}) collective-permute-start(bf16[2048,512]{1,0:T(8,128)(2,1)S(1)} %shard_map.91), channel_id=1, source_target_pairs={{0,1},{1,0},{2,3},{3,2},{4,5},{5,4},{6,7},{7,6},{8,9},{9,8},{10,11... | collective-permute-start | bytes 6291464 | tf_op jit(solution)/shard_map/ppermute | solution.py:327
  28.0 14.3 %collective-permute-start.12 = (f32[256,512]{1,0:T(8,128)S(1)}, f32[256,512]{1,0:T(8,128)S(1)}, u32[]{:S(2)}, u32[]{:S(2)}) collective-permute-start(f32[256,512]{1,0:T(8,128)S(1)} %get-tuple-element.41.mine), channel_id=1, source_target_pairs={{0,1},{1,0},{2,3},{3,2},{4,5},{5,4},{6,7},{7,6},{8,9},{9,8},{10,11... | collective-permute-start | bytes 1572872 | tf_op jit(solution)/shard_map/ppermute | solution.py:327
  44.1 5.7 %collective-permute-start.18 = (bf16[64,1024]{1,0:T(8,128)(2,1)S(1)}, bf16[64,1024]{1,0:T(8,128)(2,1)S(1)}, u32[]{:S(2)}, u32[]{:S(2)}) collective-permute-start(bf16[64,1024]{1,0:T(8,128)(2,1)S(1)} %get-tuple-element.57), channel_id=1, source_target_pairs={{0,4},{1,5},{2,6},{3,7},{4,0},{5,1},{6,2},{7,3},{8,12},{9,13},{10,... | collective-permute-start | bytes 393224 | tf_op jit(solution)/shard_map/ppermute | solution.py:327
  44.8 8.2 %collective-permute-start.19 = (bf16[64,1024]{1,0:T(8,128)(2,1)S(1)}, bf16[64,1024]{1,0:T(8,128)(2,1)S(1)}, u32[]{:S(2)}, u32[]{:S(2)}) collective-permute-start(bf16[64,1024]{1,0:T(8,128)(2,1)S(1)} %get-tuple-element.58), channel_id=1, source_target_pairs={{0,2},{1,3},{2,0},{3,1},{4,6},{5,7},{6,4},{7,5},{8,10},{9,11},{10,... | collective-permute-start | bytes 393224 | tf_op jit(solution)/shard_map/ppermute | solution.py:327
  45.5 9.3 %collective-permute-start.20 = (bf16[64,1024]{1,0:T(8,128)(2,1)S(1)}, bf16[64,1024]{1,0:T(8,128)(2,1)S(1)}, u32[]{:S(2)}, u32[]{:S(2)}) collective-permute-start(bf16[64,1024]{1,0:T(8,128)(2,1)S(1)} %get-tuple-element.59), channel_id=1, source_target_pairs={{0,6},{1,7},{2,4},{3,5},{4,2},{5,3},{6,0},{7,1},{8,14},{9,15},{10,... | collective-permute-start | bytes 393224 | tf_op jit(solution)/shard_map/ppermute | solution.py:327
  47.6 10.4 %collective-permute-start.14 = (bf16[64,1024]{1,0:T(8,128)(2,1)S(1)}, bf16[64,1024]{1,0:T(8,128)(2,1)S(1)}, u32[]{:S(2)}, u32[]{:S(2)}) collective-permute-start(bf16[64,1024]{1,0:T(8,128)(2,1)S(1)} %get-tuple-element.47), channel_id=1, source_target_pairs={{0,4},{1,5},{2,6},{3,7},{4,0},{5,1},{6,2},{7,3},{8,12},{9,13},{10,... | collective-permute-start | bytes 393224 | tf_op jit(solution)/shard_map/ppermute | solution.py:327
  48.3 9.8 %collective-permute-start.15 = (bf16[64,1024]{1,0:T(8,128)(2,1)S(1)}, bf16[64,1024]{1,0:T(8,128)(2,1)S(1)}, u32[]{:S(2)}, u32[]{:S(2)}) collective-permute-start(bf16[64,1024]{1,0:T(8,128)(2,1)S(1)} %get-tuple-element.48), channel_id=1, source_target_pairs={{0,2},{1,3},{2,0},{3,1},{4,6},{5,7},{6,4},{7,5},{8,10},{9,11},{10,... | collective-permute-start | bytes 393224 | tf_op jit(solution)/shard_map/ppermute | solution.py:327
  49.8 9.5 %collective-permute-start.16 = (bf16[64,1024]{1,0:T(8,128)(2,1)S(1)}, bf16[64,1024]{1,0:T(8,128)(2,1)S(1)}, u32[]{:S(2)}, u32[]{:S(2)}) collective-permute-start(bf16[64,1024]{1,0:T(8,128)(2,1)S(1)} %get-tuple-element.49), channel_id=1, source_target_pairs={{0,6},{1,7},{2,4},{3,5},{4,2},{5,3},{6,0},{7,1},{8,14},{9,15},{10,... | collective-permute-start | bytes 393224 | tf_op jit(solution)/shard_map/ppermute | solution.py:327
  54.9 6.4 %collective-permute-start.21 = (bf16[32,1024]{1,0:T(8,128)(2,1)S(1)}, bf16[32,1024]{1,0:T(8,128)(2,1)S(1)}, u32[]{:S(2)}, u32[]{:S(2)}) collective-permute-start(bf16[32,1024]{1,0:T(8,128)(2,1)S(1)} %get-tuple-element.60), channel_id=1, source_target_pairs={{0,16},{1,17},{2,18},{3,19},{4,20},{5,21},{6,22},{7,23},{8,24},{9,... | collective-permute-start | bytes 196616 | tf_op jit(solution)/shard_map/ppermute | solution.py:327
  55.8 6.2 %collective-permute-start.22 = (bf16[32,1024]{1,0:T(8,128)(2,1)S(1)}, bf16[32,1024]{1,0:T(8,128)(2,1)S(1)}, u32[]{:S(2)}, u32[]{:S(2)}) collective-permute-start(bf16[32,1024]{1,0:T(8,128)(2,1)S(1)} %get-tuple-element.61), channel_id=1, source_target_pairs={{0,24},{1,25},{2,26},{3,27},{4,28},{5,29},{6,30},{7,31},{8,16},{9,... | collective-permute-start | bytes 196616 | tf_op jit(solution)/shard_map/ppermute | solution.py:327
  59.3 4.3 %collective-permute-start.17 = (bf16[32,1024]{1,0:T(8,128)(2,1)S(1)}, bf16[32,1024]{1,0:T(8,128)(2,1)S(1)}, u32[]{:S(2)}, u32[]{:S(2)}) collective-permute-start(bf16[32,1024]{1,0:T(8,128)(2,1)S(1)} %get-tuple-element.55), channel_id=1, source_target_pairs={{0,8},{1,9},{2,10},{3,11},{4,12},{5,13},{6,14},{7,15},{8,0},{9,1},... | collective-permute-start | bytes 196616 | tf_op jit(solution)/shard_map/ppermute | solution.py:327

commit v16 on v15

--- a/solution.py
+++ b/solution.py
@@ -11,6 +11,7 @@
 CAP = 32
 MOST_VMEM = 56 * 1024 * 1024
 IDS = 128
+LANES = 128
 grad_scale = 16384.0
 AXES = ("dp", "vocab")
 SMEM = pl.BlockSpec(memory_space=pltpu.SMEM)
@@ -213,16 +214,24 @@
     lane = lax.broadcasted_iota(jnp.int32, (height, 128), 1)
     table = jnp.where(lane == 0, peak, jnp.where(lane == 1, mass, hit))
     table = reorder(jnp.transpose(table)[0:8], position, groups)
-    line = jnp.concatenate([table[0:1], table[1:2], table[2:3, :128]], axis=1)
-    stats[...] = jnp.broadcast_to(line[None], stats.shape)
+    lines = [
+        table[row:row + 1, start:start + LANES]
+        for row in range(2)
+        for start in range(0, height, LANES)
+    ]
+    lines.append(table[2:3, :LANES])
+    lines += [jnp.zeros_like(lines[0])] * (stats.shape[1] - len(lines))
+    stats[...] = jnp.broadcast_to(jnp.concatenate(lines, axis=0)[None], stats.shape)
 
 
 def log_totals(groups, stats, height):
-    peaks, masses = stats[:, :, :height], stats[:, :, height:2 * height]
+    count = height // LANES
+    peaks, masses = stats[:, :count, :], stats[:, count:2 * count, :]
     peak = jnp.max(peaks, axis=0)
     mass = jnp.sum(masses * jnp.exp(peaks - peak[None]), axis=0)
-    line = jnp.broadcast_to(peak + jnp.log(mass), (8, height))
-    line = reorder(line, coordinates()[1], groups)
+    total = peak + jnp.log(mass)
+    line = jnp.concatenate([total[row:row + 1] for row in range(count)], axis=1)
+    line = reorder(jnp.broadcast_to(line, (8, height)), coordinates()[1], groups)
     return jnp.transpose(jnp.concatenate([line] * 16, axis=0))
 
 
@@ -279,7 +288,8 @@
         copies.append(copy)
     if skipped:
         info, table, stats = refs[1:4]
-        hits = jnp.sum(stats[:, :, 2 * info.shape[0]:], axis=0)
+        first = 2 * info.shape[0] // LANES
+        hits = jnp.sum(stats[:, first:first + 1, :], axis=0)
         loss = jnp.sum(info[:, 0:1] * table[:, 0:1]) - hits[0, 0]
         last[...] = jnp.full(last.shape, loss, jnp.float32)
     else:
@@ -380,8 +390,25 @@
         [pltpu.SemaphoreType.DMA((ranks + xs,))],
     )
     pieces[0, 0, 0] = same
+    info = call(
+        info_kernel,
+        (same, pieces[0, 1, 0], advantages.reshape(1, -1)),
+        [VMEM] * 3,
+        shape((total_rows, 128), f32),
+        VMEM,
+    )
+
+    def hold(value, after):
+        like = shape(value.shape, value.dtype)
+        return call(gate_kernel, (value, after), [ANY, ANY], like, ANY, aliases={0: 0})
+
+    for x in range(1, xs):
+        pieces[2 * x + 1, 1, 0] = send(pieces[2 * x, 1, 0], core=1)
+        pieces[2 * x, 0, 0] = hold(pieces[2 * x, 0, 0], info)
+        pieces[2 * x, 1, 1] = hold(pieces[2 * x, 1, 1], pieces[2 * x + 1, 1, 0])
     for b, y, part in list(pieces):
-        pieces[b + 1, y, part] = send(pieces[b, y, part], core=1)
+        if b % 2 == 0 and (b + 1, y, part) not in pieces:
+            pieces[b + 1, y, part] = send(pieces[b, y, part], core=1)
     parted = [[pieces[key] for key in sorted(pieces) if key[0] == b] for b in range(ranks)]
 
     def rows_of(blocks):
@@ -390,14 +417,8 @@
     def counts_of(blocks):
         return [len(parted[b]) for b in blocks]
 
-    info = call(
-        info_kernel,
-        (*parted[0], advantages.reshape(1, -1)),
-        [VMEM] * (1 + len(parted[0])),
-        shape((total_rows, 128), f32),
-        VMEM,
-    )
     near = range(0, ranks, 2)
+    stat_rows = (2 * total_rows // LANES + 1 + 7) // 8 * 8
     partial = call(
         functools.partial(first_kernel, counts_of(near)),
         (held, *rows_of(near)),
@@ -413,16 +434,13 @@
         [VMEM] * (3 + sum(counts_of(beside))),
         (
             shape((total_rows, columns), f32),
-            shape((dps * ranks, 1, 2 * total_rows + 128), f32),
+            shape((dps * ranks, stat_rows, LANES), f32),
         ),
         (VMEM, VMEM),
         flops=flops // 2,
     )
     other_logits = send(logits, core=1)
-    away = call(
-        gate_kernel, (away, stats), [ANY, ANY], shape(away.shape, bf16), ANY, aliases={0: 0}
-    )
-    other_held = send(away, core=1)
+    other_held = send(hold(away, stats), core=1)
     stats = lax.all_to_all(stats, AXES, 0, 0)
     rows_part = total_rows // 4
     order = sorted(range(1, ranks), key=lambda place: (place % 2 + (place > 1), place)) + [0]

time: 64.8 us -> 65.3 us (level)
    pallas_call x13 -> x15, Pallas kernels: 12.9 us -> 12.8 us  [call(): pl.pallas_call(kernel, out_shape=out_shape, in_specs=in_specs, out_specs=...]
  transfers between devices with their start and end apart: 23 -> 23, of which waited for: 9 -> 10; matrix products, arithmetic and copies ran while one was open for 0% -> 0% of each run, Pallas kernels for 12% -> 12%
where the time goes in v16:
time: 65.3 us; the launch traced here: 65.1 us
  starting transfers between devices  22.5 us (34%)
  blocking collectives  14.5 us (22%)
  waiting for transfers between devices  14.4 us (22%)
  Pallas kernels  12.8 us (20%)
  between operations  0.81 us (1%)
    ppermute x23, starting transfers between devices, send(): return lax.ppermute(value, AXES, pairs)  22.5 us
    all_to_all x1, blocking collectives, body(): stats = lax.all_to_all(stats, AXES, 0, 0)  14.5 us
    ppermute x23, waiting for transfers between devices, send(): return lax.ppermute(value, AXES, pairs)  14.4 us
    pallas_call x15, Pallas kernels, call(): pl.pallas_call(kernel, out_shape=out_shape, in_specs=in_specs, out_specs=...  12.8 us
  transfers between devices with their start and end apart: 23, of which 10 were waited for; matrix products, arithmetic and copies ran while one was open for 0% of the time, Pallas kernels for 12%

profile of v16, /device:TPU:0, one launch (start us, length us, event | category | flops | bytes accessed | tf_op | source)
XLA Modules:
  0.0 65.1 jit_solution(6841788351649028068)
XLA Ops:
  0.6 1.2 %shard_map.85 = (bf16[32,1152]{1,0:T(8,128)(2,1)S(1)}, bf16[32,1024]{1,0:T(8,128)(2,1)S(1)}, bf16[32,128]{1,0:T(8,128)(2,1)S(1)}) custom-call(bf16[128,1024]{1,0:T(8,128)(2,1)} %hidden_hbm.1, s32[1,128]{1,0:T(1,128)} %bitcast.6, s32[1,128]{1,0:T(1,128)} %bitcast.7, s32[1,128]{1,0:T(1,128)} %bitcast.8), custom_call_target="tpu_custom_call" | custom-call | bytes 411136 | tf_op jit(solution)/shard_map/pallas_call | solution.py:33
  1.9 4.1 %collective-permute-start = (bf16[32,1152]{1,0:T(8,128)(2,1)S(1)}, bf16[32,1152]{1,0:T(8,128)(2,1)S(1)}, u32[]{:S(2)}, u32[]{:S(2)}) collective-permute-start(bf16[32,1152]{1,0:T(8,128)(2,1)S(1)} %get-tuple-element.34.refs_0_), channel_id=1, source_target_pairs={{0,16},{1,17},{2,18},{3,19},{4,20},{5,21},{6,22},{7,23},{8,24},{9,... | collective-permute-start | bytes 221192 | tf_op jit(solution)/shard_map/ppermute | solution.py:337
  6.0 1.3 %collective-permute-start.1 = (bf16[32,1152]{1,0:T(8,128)(2,1)S(1)}, bf16[32,1152]{1,0:T(8,128)(2,1)S(1)}, u32[]{:S(2)}, u32[]{:S(2)}) collective-permute-start(bf16[32,1152]{1,0:T(8,128)(2,1)S(1)} %get-tuple-element.34.refs_0_), channel_id=1, source_target_pairs={{0,24},{1,25},{2,26},{3,27},{4,28},{5,29},{6,30},{7,31},{8,16},{9,... | collective-permute-start | bytes 221192 | tf_op jit(solution)/shard_map/ppermute | solution.py:337
  7.5 2.4 %collective-permute-start.2 = (bf16[32,1024]{1,0:T(8,128)(2,1)S(1)}, bf16[32,1024]{1,0:T(8,128)(2,1)S(1)}, u32[]{:S(2)}, u32[]{:S(2)}) collective-permute-start(bf16[32,1024]{1,0:T(8,128)(2,1)S(1)} %get-tuple-element.35), channel_id=1, source_target_pairs={{0,6},{1,7},{2,4},{3,5},{4,2},{5,3},{6,0},{7,1},{8,14},{9,15},{10,... | collective-permute-start | bytes 196616 | tf_op jit(solution)/shard_map/ppermute | solution.py:337
  10.0 2.7 %collective-permute-done.2.refs_3_.refs_5_ = bf16[32,1024]{1,0:T(8,128)(2,1)S(1)} collective-permute-done((bf16[32,1024]{1,0:T(8,128)(2,1)S(1)}, bf16[32,1024]{1,0:T(8,128)(2,1)S(1)}, u32[]{:S(2)}, u32[]{:S(2)}) %collective-permute-start.2) | collective-permute-done | bytes 65568 | tf_op jit(solution)/shard_map/ppermute | solution.py:337
  12.8 1.7 %collective-permute-start.4 = (bf16[128,1152]{1,0:T(8,128)(2,1)S(1)}, bf16[128,1152]{1,0:T(8,128)(2,1)S(1)}, u32[]{:S(2)}, u32[]{:S(2)}) collective-permute-start(bf16[128,1152]{1,0:T(8,128)(2,1)S(1)} %get-tuple-element.36.line), channel_id=1, source_target_pairs={{0,4},{1,5},{2,6},{3,7},{4,0},{5,1},{6,2},{7,3},{8,12},{9,13},{10,... | collective-permute-start | bytes 884744 | tf_op jit(solution)/shard_map/ppermute | solution.py:337
  14.5 1.5 %collective-permute-start.5 = (bf16[128,1024]{1,0:T(8,128)(2,1)S(1)}, bf16[128,1024]{1,0:T(8,128)(2,1)S(1)}, u32[]{:S(2)}, u32[]{:S(2)}) collective-permute-start(bf16[128,1024]{1,0:T(8,128)(2,1)S(1)} %get-tuple-element.39), channel_id=1, source_target_pairs={{0,2},{1,3},{2,0},{3,1},{4,6},{5,7},{6,4},{7,5},{8,10},{9,11},{10,... | collective-permute-start | bytes 786440 | tf_op jit(solution)/shard_map/ppermute | solution.py:337
  16.3 2.9 %shard_map.87 = (bf16[4096,512]{1,0:T(8,128)(2,1)S(1)}, bf16[2048,512]{1,0:T(8,128)(2,1)S(1)}, bf16[128,1152]{1,0:T(8,128)(2,1)S(1)}) custom-call(bf16[128,1152]{1,0:T(8,128)(2,1)S(1)} %get-tuple-element.36.line, bf16[4096,512]{1,0:T(8,128)(2,1)} %weight.1), custom_call_target="tpu_custom_call" | custom-call | bytes 11075584 | tf_op jit(solution)/shard_map/pallas_call | solution.py:33
  19.3 3.1 %collective-permute-done.4.refs_1_ = bf16[128,1152]{1,0:T(8,128)(2,1)S(1)} collective-permute-done((bf16[128,1152]{1,0:T(8,128)(2,1)S(1)}, bf16[128,1152]{1,0:T(8,128)(2,1)S(1)}, u32[]{:S(2)}, u32[]{:S(2)}) %collective-permute-start.4) | collective-permute-done | bytes 294944 | tf_op jit(solution)/shard_map/ppermute | solution.py:337
  23.4 0.7 %collective-permute-done.7.after.refs_3_.refs_8_ = bf16[32,1024]{1,0:T(8,128)(2,1)S(1)} collective-permute-done((bf16[32,1024]{1,0:T(8,128)(2,1)S(1)}, bf16[32,1024]{1,0:T(8,128)(2,1)S(1)}, u32[]{:S(2)}, u32[]{:S(2)}) %collective-permute-start.7) | collective-permute-done | bytes 65568 | tf_op jit(solution)/shard_map/ppermute | solution.py:337
  24.0 0.9 %collective-permute-done.6.value = bf16[96,1024]{1,0:T(8,128)(2,1)S(1)} collective-permute-done((bf16[96,1024]{1,0:T(8,128)(2,1)S(1)}, bf16[96,1024]{1,0:T(8,128)(2,1)S(1)}, u32[]{:S(2)}, u32[]{:S(2)}) %collective-permute-start.6) | collective-permute-done | bytes 196640 | tf_op jit(solution)/shard_map/ppermute | solution.py:337
  24.9 0.7 %shard_map.91.partial = f32[256,512]{1,0:T(8,128)S(1)} custom-call(bf16[4096,512]{1,0:T(8,128)(2,1)S(1)} %get-tuple-element.38.weight, bf16[128,1152]{1,0:T(8,128)(2,1)S(1)} %get-tuple-element.37.refs_0_, bf16[128,1152]{1,0:T(8,128)(2,1)S(1)} %collective-permute-done.4.refs_1_, bf16[128,1024]{1,0:T(8,128)(2,1)S(1)} %shard_map.89.refs_2_.refs_4_, ...), custom_call_target="tpu_custom_call" | custom-call | flops 536870912 | bytes 5832704 | tf_op jit(solution)/shard_map/pallas_call | solution.py:33
  25.7 0.7 %collective-permute-done.11.refs_4_.refs_9_ = bf16[96,1024]{1,0:T(8,128)(2,1)S(1)} collective-permute-done((bf16[96,1024]{1,0:T(8,128)(2,1)S(1)}, bf16[96,1024]{1,0:T(8,128)(2,1)S(1)}, u32[]{:S(2)}, u32[]{:S(2)}) %collective-permute-start.11) | collective-permute-done | bytes 196640 | tf_op jit(solution)/shard_map/ppermute | solution.py:337
  26.4 1.2 %shard_map.92 = (f32[256,512]{1,0:T(8,128)S(1)}, f32[32,8,128]{2,1,0:T(8,128)S(1)}) custom-call(f32[256,128]{1,0:T(8,128)S(1)} %shard_map.88.after.info.refs_1_, f32[256,512]{1,0:T(8,128)S(1)} %shard_map.91.partial, bf16[4096,512]{1,0:T(8,128)(2,1)S(1)} %get-tuple-element.38.weight, bf16[128,1152]{1,0:T(8,128)(2,1)S(1)} %collective-permute-done.8.refs_0_.refs_2_, ...), custom_call_target="tpu_custom_call" | custom-call | flops 536870912 | bytes 6619136 | tf_op jit(solution)/shard_map/pallas_call | solution.py:33
  28.1 14.5 %all_to_all.5.stats.refs_3_ = f32[32,8,128]{2,1,0:T(8,128)S(1)} all-to-all(f32[32,8,128]{2,1,0:T(8,128)S(1)} %get-tuple-element.43.after), channel_id=1, replica_groups=mesh['dp'=8,'vocab'=4] {'dp','vocab'}, dimensions={0} | all-to-all | bytes 262144 | tf_op jit(solution)/shard_map/all_to_all | solution.py:444
  42.7 1.8 %shard_map.94 = (bf16[256,512]{1,0:T(8,128)(2,1)S(1)}, f32[256,128]{1,0:T(8,128)S(1)}, bf16[64,1024]{1,0:T(8,128)(2,1)S(1)}, bf16[64,1024]{1,0:T(8,128)(2,1)S(1)...) custom-call(f32[256,128]{1,0:T(8,128)S(1)} %shard_map.88.after.info., ...), custom_call_target="tpu_custom_call" | custom-call | flops 1073741824 | bytes 9306112 | tf_op jit(solution)/shard_map/pallas_call | solution.py:33
  44.5 0.7 %collective-permute-start.18 = (bf16[64,1024]{1,0:T(8,128)(2,1)S(1)}, bf16[64,1024]{1,0:T(8,128)(2,1)S(1)}, u32[]{:S(2)}, u32[]{:S(2)}) collective-permute-start(bf16[64,1024]{1,0:T(8,128)(2,1)S(1)} %get-tuple-element.57), channel_id=1, source_target_pairs={{0,4},{1,5},{2,6},{3,7},{4,0},{5,1},{6,2},{7,3},{8,12},{9,13},{10,... | collective-permute-start | bytes 393224 | tf_op jit(solution)/shard_map/ppermute | solution.py:337
  45.2 0.8 %collective-permute-start.19 = (bf16[64,1024]{1,0:T(8,128)(2,1)S(1)}, bf16[64,1024]{1,0:T(8,128)(2,1)S(1)}, u32[]{:S(2)}, u32[]{:S(2)}) collective-permute-start(bf16[64,1024]{1,0:T(8,128)(2,1)S(1)} %get-tuple-element.58), channel_id=1, source_target_pairs={{0,2},{1,3},{2,0},{3,1},{4,6},{5,7},{6,4},{7,5},{8,10},{9,11},{10,... | collective-permute-start | bytes 393224 | tf_op jit(solution)/shard_map/ppermute | solution.py:337
  46.0 2.1 %collective-permute-start.20 = (bf16[64,1024]{1,0:T(8,128)(2,1)S(1)}, bf16[64,1024]{1,0:T(8,128)(2,1)S(1)}, u32[]{:S(2)}, u32[]{:S(2)}) collective-permute-start(bf16[64,1024]{1,0:T(8,128)(2,1)S(1)} %get-tuple-element.59), channel_id=1, source_target_pairs={{0,6},{1,7},{2,4},{3,5},{4,2},{5,3},{6,0},{7,1},{8,14},{9,15},{10,... | collective-permute-start | bytes 393224 | tf_op jit(solution)/shard_map/ppermute | solution.py:337
  48.0 0.7 %collective-permute-start.14 = (bf16[64,1024]{1,0:T(8,128)(2,1)S(1)}, bf16[64,1024]{1,0:T(8,128)(2,1)S(1)}, u32[]{:S(2)}, u32[]{:S(2)}) collective-permute-start(bf16[64,1024]{1,0:T(8,128)(2,1)S(1)} %get-tuple-element.47), channel_id=1, source_target_pairs={{0,4},{1,5},{2,6},{3,7},{4,0},{5,1},{6,2},{7,3},{8,12},{9,13},{10,... | collective-permute-start | bytes 393224 | tf_op jit(solution)/shard_map/ppermute | solution.py:337
  48.7 0.8 %collective-permute-start.15 = (bf16[64,1024]{1,0:T(8,128)(2,1)S(1)}, bf16[64,1024]{1,0:T(8,128)(2,1)S(1)}, u32[]{:S(2)}, u32[]{:S(2)}) collective-permute-start(bf16[64,1024]{1,0:T(8,128)(2,1)S(1)} %get-tuple-element.48), channel_id=1, source_target_pairs={{0,2},{1,3},{2,0},{3,1},{4,6},{5,7},{6,4},{7,5},{8,10},{9,11},{10,... | collective-permute-start | bytes 393224 | tf_op jit(solution)/shard_map/ppermute | solution.py:337
  49.4 0.8 %collective-permute-done.18.refs_0_ = bf16[64,1024]{1,0:T(8,128)(2,1)S(1)} collective-permute-done((bf16[64,1024]{1,0:T(8,128)(2,1)S(1)}, bf16[64,1024]{1,0:T(8,128)(2,1)S(1)}, u32[]{:S(2)}, u32[]{:S(2)}) %collective-permute-start.18) | collective-permute-done | bytes 131104 | tf_op jit(solution)/shard_map/ppermute | solution.py:337
  50.2 1.3 %collective-permute-start.16 = (bf16[64,1024]{1,0:T(8,128)(2,1)S(1)}, bf16[64,1024]{1,0:T(8,128)(2,1)S(1)}, u32[]{:S(2)}, u32[]{:S(2)}) collective-permute-start(bf16[64,1024]{1,0:T(8,128)(2,1)S(1)} %get-tuple-element.49), channel_id=1, source_target_pairs={{0,6},{1,7},{2,4},{3,5},{4,2},{5,3},{6,0},{7,1},{8,14},{9,15},{10,... | collective-permute-start | bytes 393224 | tf_op jit(solution)/shard_map/ppermute | solution.py:337
  51.5 1.8 %shard_map.95 = (bf16[4096,512]{1,0:T(8,128)(2,1)}, f32[8,128]{1,0:T(8,128)S(1)}) custom-call(f32[64,1024]{1,0:T(8,128)S(1)} %get-tuple-element.44.after.kept, bf16[256,512]{1,0:T(8,128)(2,1)S(1)} %get-tuple-element.45.logit_grad, bf16[128,1152]{1,0:T(8,128)(2,1)S(1)} %get-tuple-element.37.refs_0_, bf16[128,1152]{1,0:T(8,128)(2,1)S(1)} %collective-permute-done.4.refs_1_, ...), custom_call_target="tpu_custom_call" | custom-call | flops 536870912 | bytes 5902336 | tf_op jit(solution)/shard_map/pallas_call | solution.py:33
  53.3 1.8 %collective-permute-done.20.refs_2_ = bf16[64,1024]{1,0:T(8,128)(2,1)S(1)} collective-permute-done((bf16[64,1024]{1,0:T(8,128)(2,1)S(1)}, bf16[64,1024]{1,0:T(8,128)(2,1)S(1)}, u32[]{:S(2)}, u32[]{:S(2)}) %collective-permute-start.20) | collective-permute-done | bytes 131104 | tf_op jit(solution)/shard_map/ppermute | solution.py:337
  55.2 1.0 %collective-permute-start.21 = (bf16[32,1024]{1,0:T(8,128)(2,1)S(1)}, bf16[32,1024]{1,0:T(8,128)(2,1)S(1)}, u32[]{:S(2)}, u32[]{:S(2)}) collective-permute-start(bf16[32,1024]{1,0:T(8,128)(2,1)S(1)} %get-tuple-element.60), channel_id=1, source_target_pairs={{0,16},{1,17},{2,18},{3,19},{4,20},{5,21},{6,22},{7,23},{8,24},{9,... | collective-permute-start | bytes 196616 | tf_op jit(solution)/shard_map/ppermute | solution.py:337
  56.2 2.3 %collective-permute-start.22 = (bf16[32,1024]{1,0:T(8,128)(2,1)S(1)}, bf16[32,1024]{1,0:T(8,128)(2,1)S(1)}, u32[]{:S(2)}, u32[]{:S(2)}) collective-permute-start(bf16[32,1024]{1,0:T(8,128)(2,1)S(1)} %get-tuple-element.61), channel_id=1, source_target_pairs={{0,24},{1,25},{2,26},{3,27},{4,28},{5,29},{6,30},{7,31},{8,16},{9,... | collective-permute-start | bytes 196616 | tf_op jit(solution)/shard_map/ppermute | solution.py:337
  58.5 1.3 %collective-permute-done.16.refs_2_ = bf16[64,1024]{1,0:T(8,128)(2,1)S(1)} collective-permute-done((bf16[64,1024]{1,0:T(8,128)(2,1)S(1)}, bf16[64,1024]{1,0:T(8,128)(2,1)S(1)}, u32[]{:S(2)}, u32[]{:S(2)}) %collective-permute-start.16) | collective-permute-done | bytes 131104 | tf_op jit(solution)/shard_map/ppermute | solution.py:337
  59.9 1.8 %shard_map.97 = (bf16[4096,512]{1,0:T(8,128)(2,1)}, f32[8,128]{1,0:T(8,128)S(1)}) custom-call(f32[32,1024]{1,0:T(8,128)S(1)} %get-tuple-element.50.after.refs_0_, bf16[256,512]{1,0:T(8,128)(2,1)S(1)} %get-tuple-element.45.logit_grad, bf16[4096,512]{1,0:T(8,128)(2,1)} %get-tuple-element.51.refs_0_, ...), custom_call_target="tpu_custom_call", output_to_operand_aliasing={{0}: (2, {})} | custom-call | flops 536870912 | bytes 10227712 | tf_op jit(solution)/shard_map/pallas_call | solution.py:33
  61.7 0.6 collective-permute-done.22.refs_3_
  62.4 1.8 %collective-permute-done.17.refs_1_ = bf16[32,1024]{1,0:T(8,128)(2,1)S(1)} collective-permute-done((bf16[32,1024]{1,0:T(8,128)(2,1)S(1)}, bf16[32,1024]{1,0:T(8,128)(2,1)S(1)}, u32[]{:S(2)}, u32[]{:S(2)}) %collective-permute-start.17) | collective-permute-done | bytes 65568 | tf_op jit(solution)/shard_map/ppermute | solution.py:337
  64.1 1.0 %shard_map.99 = (bf16[128,1024]{1,0:T(8,128)(2,1)}, f32[1,1]{1,0:T(1,128)}) custom-call(f32[8,128]{1,0:T(8,128)S(1)} %get-tuple-element.53.last, bf16[32,128]{1,0:T(8,128)(2,1)S(1)} %get-tuple-element.54.chosen, f32[32,1024]{1,0:T(8,128)S(1)} %get-tuple-element.50.after.refs_0_, bf16[32,1024]{1,0:T(8,128)(2,1)S(1)} %collective-permute-done.17.refs_1_, ...), custom_call_target="tpu_custom_call" | custom-call | bytes 602116 | tf_op jit(solution)/shard_map/pallas_call | solution.py:33
  (32 shorter events, 2.5 us)
Async XLA Ops:
  0.6 22.2 %copy-start = (f32[32]{0:T(128)S(1)}, f32[32]{0:T(128)}, u32[]{:S(2)}) copy-start(f32[32]{0:T(128)} %param.11) | copy-start | bytes 388
  1.9 10.8 %collective-permute-start = (bf16[32,1152]{1,0:T(8,128)(2,1)S(1)}, bf16[32,1152]{1,0:T(8,128)(2,1)S(1)}, u32[]{:S(2)}, u32[]{:S(2)}) collective-permute-start(bf16[32,1152]{1,0:T(8,128)(2,1)S(1)} %get-tuple-element.34.refs_0_), channel_id=1, source_target_pairs={{0,16},{1,17},{2,18},{3,19},{4,20},{5,21},{6,22},{7,23},{8,24},{9,... | collective-permute-start | bytes 221192 | tf_op jit(solution)/shard_map/ppermute | solution.py:337
  6.0 6.8 %collective-permute-start.1 = (bf16[32,1152]{1,0:T(8,128)(2,1)S(1)}, bf16[32,1152]{1,0:T(8,128)(2,1)S(1)}, u32[]{:S(2)}, u32[]{:S(2)}) collective-permute-start(bf16[32,1152]{1,0:T(8,128)(2,1)S(1)} %get-tuple-element.34.refs_0_), channel_id=1, source_target_pairs={{0,24},{1,25},{2,26},{3,27},{4,28},{5,29},{6,30},{7,31},{8,16},{9,... | collective-permute-start | bytes 221192 | tf_op jit(solution)/shard_map/ppermute | solution.py:337
  7.3 5.4 %collective-permute-start.3 = (bf16[32,1152]{1,0:T(8,128)(2,1)S(1)}, bf16[32,1152]{1,0:T(8,128)(2,1)S(1)}, u32[]{:S(2)}, u32[]{:S(2)}) collective-permute-start(bf16[32,1152]{1,0:T(8,128)(2,1)S(1)} %get-tuple-element.34.refs_0_), channel_id=1, source_target_pairs={{0,8},{1,9},{2,10},{3,11},{4,12},{5,13},{6,14},{7,15},{8,0},{9,1},... | collective-permute-start | bytes 221192 | tf_op jit(solution)/shard_map/ppermute | solution.py:337
  7.5 5.2 %collective-permute-start.2 = (bf16[32,1024]{1,0:T(8,128)(2,1)S(1)}, bf16[32,1024]{1,0:T(8,128)(2,1)S(1)}, u32[]{:S(2)}, u32[]{:S(2)}) collective-permute-start(bf16[32,1024]{1,0:T(8,128)(2,1)S(1)} %get-tuple-element.35), channel_id=1, source_target_pairs={{0,6},{1,7},{2,4},{3,5},{4,2},{5,3},{6,0},{7,1},{8,14},{9,15},{10,... | collective-permute-start | bytes 196616 | tf_op jit(solution)/shard_map/ppermute | solution.py:337
  12.8 9.6 %collective-permute-start.4 = (bf16[128,1152]{1,0:T(8,128)(2,1)S(1)}, bf16[128,1152]{1,0:T(8,128)(2,1)S(1)}, u32[]{:S(2)}, u32[]{:S(2)}) collective-permute-start(bf16[128,1152]{1,0:T(8,128)(2,1)S(1)} %get-tuple-element.36.line), channel_id=1, source_target_pairs={{0,4},{1,5},{2,6},{3,7},{4,0},{5,1},{6,2},{7,3},{8,12},{9,13},{10,... | collective-permute-start | bytes 884744 | tf_op jit(solution)/shard_map/ppermute | solution.py:337
  14.5 8.8 %collective-permute-start.5 = (bf16[128,1024]{1,0:T(8,128)(2,1)S(1)}, bf16[128,1024]{1,0:T(8,128)(2,1)S(1)}, u32[]{:S(2)}, u32[]{:S(2)}) collective-permute-start(bf16[128,1024]{1,0:T(8,128)(2,1)S(1)} %get-tuple-element.39), channel_id=1, source_target_pairs={{0,2},{1,3},{2,0},{3,1},{4,6},{5,7},{6,4},{7,5},{8,10},{9,11},{10,... | collective-permute-start | bytes 786440 | tf_op jit(solution)/shard_map/ppermute | solution.py:337
  15.9 9.0 %collective-permute-start.6 = (bf16[96,1024]{1,0:T(8,128)(2,1)S(1)}, bf16[96,1024]{1,0:T(8,128)(2,1)S(1)}, u32[]{:S(2)}, u32[]{:S(2)}) collective-permute-start(bf16[96,1024]{1,0:T(8,128)(2,1)S(1)} %get-tuple-element.40), channel_id=1, source_target_pairs={{0,6},{1,7},{2,4},{3,5},{4,2},{5,3},{6,0},{7,1},{8,14},{9,15},{10,... | collective-permute-start | bytes 589832 | tf_op jit(solution)/shard_map/ppermute | solution.py:337
  19.2 6.4 %collective-permute-start.8 = (bf16[128,1152]{1,0:T(8,128)(2,1)S(1)}, bf16[128,1152]{1,0:T(8,128)(2,1)S(1)}, u32[]{:S(2)}, u32[]{:S(2)}) collective-permute-start(bf16[128,1152]{1,0:T(8,128)(2,1)S(1)} %get-tuple-element.37.refs_0_), channel_id=1, source_target_pairs={{0,1},{1,0},{2,3},{3,2},{4,5},{5,4},{6,7},{7,6},{8,9},{9,8},{10,11... | collective-permute-start | bytes 884744 | tf_op jit(solution)/shard_map/ppermute | solution.py:337
  22.4 4.0 %collective-permute-start.9 = (bf16[128,1152]{1,0:T(8,128)(2,1)S(1)}, bf16[128,1152]{1,0:T(8,128)(2,1)S(1)}, u32[]{:S(2)}, u32[]{:S(2)}) collective-permute-start(bf16[128,1152]{1,0:T(8,128)(2,1)S(1)} %collective-permute-done.4.refs_1_), channel_id=1, source_target_pairs={{0,1},{1,0},{2,3},{3,2},{4,5},{5,4},{6,7},{7,6},{8,9},{9,8},{10,11... | collective-permute-start | bytes 884744 | tf_op jit(solution)/shard_map/ppermute | solution.py:337
  22.4 1.7 %collective-permute-start.7 = (bf16[32,1024]{1,0:T(8,128)(2,1)S(1)}, bf16[32,1024]{1,0:T(8,128)(2,1)S(1)}, u32[]{:S(2)}, u32[]{:S(2)}) collective-permute-start(bf16[32,1024]{1,0:T(8,128)(2,1)S(1)} %collective-permute-done.2.refs_3_.refs_5_), channel_id=1, source_target_pairs={{0,1},{1,0},{2,3},{3,2},{4,5},{5,4},{6,7},{7,6},{8,9},{9,8},{10,11... | collective-permute-start | bytes 196616 | tf_op jit(solution)/shard_map/ppermute | solution.py:337
  23.3 3.1 %collective-permute-start.10 = (bf16[128,1024]{1,0:T(8,128)(2,1)S(1)}, bf16[128,1024]{1,0:T(8,128)(2,1)S(1)}, u32[]{:S(2)}, u32[]{:S(2)}) collective-permute-start(bf16[128,1024]{1,0:T(8,128)(2,1)S(1)} %shard_map.89.refs_2_.refs_4_), channel_id=1, source_target_pairs={{0,1},{1,0},{2,3},{3,2},{4,5},{5,4},{6,7},{7,6},{8,9},{9,8},{10,11... | collective-permute-start | bytes 786440 | tf_op jit(solution)/shard_map/ppermute | solution.py:337
  24.9 1.4 %collective-permute-start.11 = (bf16[96,1024]{1,0:T(8,128)(2,1)S(1)}, bf16[96,1024]{1,0:T(8,128)(2,1)S(1)}, u32[]{:S(2)}, u32[]{:S(2)}) collective-permute-start(bf16[96,1024]{1,0:T(8,128)(2,1)S(1)} %shard_map.90.refs_4_.refs_6_), channel_id=1, source_target_pairs={{0,1},{1,0},{2,3},{3,2},{4,5},{5,4},{6,7},{7,6},{8,9},{9,8},{10,11... | collective-permute-start | bytes 589832 | tf_op jit(solution)/shard_map/ppermute | solution.py:337
  27.6 15.1 %collective-permute-start.13 = (bf16[2048,512]{1,0:T(8,128)(2,1)S(1)}, bf16[2048,512]{1,0:T(8,128)(2,1)S(1)}, u32[]{:S(2)}, u32[]{:S(2)}) collective-permute-start(bf16[2048,512]{1,0:T(8,128)(2,1)S(1)} %shard_map.93), channel_id=1, source_target_pairs={{0,1},{1,0},{2,3},{3,2},{4,5},{5,4},{6,7},{7,6},{8,9},{9,8},{10,11... | collective-permute-start | bytes 6291464 | tf_op jit(solution)/shard_map/ppermute | solution.py:337
  27.8 14.9 %collective-permute-start.12 = (f32[256,512]{1,0:T(8,128)S(1)}, f32[256,512]{1,0:T(8,128)S(1)}, u32[]{:S(2)}, u32[]{:S(2)}) collective-permute-start(f32[256,512]{1,0:T(8,128)S(1)} %get-tuple-element.41.mine), channel_id=1, source_target_pairs={{0,1},{1,0},{2,3},{3,2},{4,5},{5,4},{6,7},{7,6},{8,9},{9,8},{10,11... | collective-permute-start | bytes 1572872 | tf_op jit(solution)/shard_map/ppermute | solution.py:337
  44.5 5.8 %collective-permute-start.18 = (bf16[64,1024]{1,0:T(8,128)(2,1)S(1)}, bf16[64,1024]{1,0:T(8,128)(2,1)S(1)}, u32[]{:S(2)}, u32[]{:S(2)}) collective-permute-start(bf16[64,1024]{1,0:T(8,128)(2,1)S(1)} %get-tuple-element.57), channel_id=1, source_target_pairs={{0,4},{1,5},{2,6},{3,7},{4,0},{5,1},{6,2},{7,3},{8,12},{9,13},{10,... | collective-permute-start | bytes 393224 | tf_op jit(solution)/shard_map/ppermute | solution.py:337
  45.2 8.1 %collective-permute-start.19 = (bf16[64,1024]{1,0:T(8,128)(2,1)S(1)}, bf16[64,1024]{1,0:T(8,128)(2,1)S(1)}, u32[]{:S(2)}, u32[]{:S(2)}) collective-permute-start(bf16[64,1024]{1,0:T(8,128)(2,1)S(1)} %get-tuple-element.58), channel_id=1, source_target_pairs={{0,2},{1,3},{2,0},{3,1},{4,6},{5,7},{6,4},{7,5},{8,10},{9,11},{10,... | collective-permute-start | bytes 393224 | tf_op jit(solution)/shard_map/ppermute | solution.py:337
  46.0 9.2 %collective-permute-start.20 = (bf16[64,1024]{1,0:T(8,128)(2,1)S(1)}, bf16[64,1024]{1,0:T(8,128)(2,1)S(1)}, u32[]{:S(2)}, u32[]{:S(2)}) collective-permute-start(bf16[64,1024]{1,0:T(8,128)(2,1)S(1)} %get-tuple-element.59), channel_id=1, source_target_pairs={{0,6},{1,7},{2,4},{3,5},{4,2},{5,3},{6,0},{7,1},{8,14},{9,15},{10,... | collective-permute-start | bytes 393224 | tf_op jit(solution)/shard_map/ppermute | solution.py:337
  48.0 10.5 %collective-permute-start.14 = (bf16[64,1024]{1,0:T(8,128)(2,1)S(1)}, bf16[64,1024]{1,0:T(8,128)(2,1)S(1)}, u32[]{:S(2)}, u32[]{:S(2)}) collective-permute-start(bf16[64,1024]{1,0:T(8,128)(2,1)S(1)} %get-tuple-element.47), channel_id=1, source_target_pairs={{0,4},{1,5},{2,6},{3,7},{4,0},{5,1},{6,2},{7,3},{8,12},{9,13},{10,... | collective-permute-start | bytes 393224 | tf_op jit(solution)/shard_map/ppermute | solution.py:337
  48.7 9.8 %collective-permute-start.15 = (bf16[64,1024]{1,0:T(8,128)(2,1)S(1)}, bf16[64,1024]{1,0:T(8,128)(2,1)S(1)}, u32[]{:S(2)}, u32[]{:S(2)}) collective-permute-start(bf16[64,1024]{1,0:T(8,128)(2,1)S(1)} %get-tuple-element.48), channel_id=1, source_target_pairs={{0,2},{1,3},{2,0},{3,1},{4,6},{5,7},{6,4},{7,5},{8,10},{9,11},{10,... | collective-permute-start | bytes 393224 | tf_op jit(solution)/shard_map/ppermute | solution.py:337
  50.2 9.5 %collective-permute-start.16 = (bf16[64,1024]{1,0:T(8,128)(2,1)S(1)}, bf16[64,1024]{1,0:T(8,128)(2,1)S(1)}, u32[]{:S(2)}, u32[]{:S(2)}) collective-permute-start(bf16[64,1024]{1,0:T(8,128)(2,1)S(1)} %get-tuple-element.49), channel_id=1, source_target_pairs={{0,6},{1,7},{2,4},{3,5},{4,2},{5,3},{6,0},{7,1},{8,14},{9,15},{10,... | collective-permute-start | bytes 393224 | tf_op jit(solution)/shard_map/ppermute | solution.py:337
  55.2 6.5 %collective-permute-start.21 = (bf16[32,1024]{1,0:T(8,128)(2,1)S(1)}, bf16[32,1024]{1,0:T(8,128)(2,1)S(1)}, u32[]{:S(2)}, u32[]{:S(2)}) collective-permute-start(bf16[32,1024]{1,0:T(8,128)(2,1)S(1)} %get-tuple-element.60), channel_id=1, source_target_pairs={{0,16},{1,17},{2,18},{3,19},{4,20},{5,21},{6,22},{7,23},{8,24},{9,... | collective-permute-start | bytes 196616 | tf_op jit(solution)/shard_map/ppermute | solution.py:337
  56.2 6.2 %collective-permute-start.22 = (bf16[32,1024]{1,0:T(8,128)(2,1)S(1)}, bf16[32,1024]{1,0:T(8,128)(2,1)S(1)}, u32[]{:S(2)}, u32[]{:S(2)}) collective-permute-start(bf16[32,1024]{1,0:T(8,128)(2,1)S(1)} %get-tuple-element.61), channel_id=1, source_target_pairs={{0,24},{1,25},{2,26},{3,27},{4,28},{5,29},{6,30},{7,31},{8,16},{9,... | collective-permute-start | bytes 196616 | tf_op jit(solution)/shard_map/ppermute | solution.py:337
  59.8 4.3 %collective-permute-start.17 = (bf16[32,1024]{1,0:T(8,128)(2,1)S(1)}, bf16[32,1024]{1,0:T(8,128)(2,1)S(1)}, u32[]{:S(2)}, u32[]{:S(2)}) collective-permute-start(bf16[32,1024]{1,0:T(8,128)(2,1)S(1)} %get-tuple-element.55), channel_id=1, source_target_pairs={{0,8},{1,9},{2,10},{3,11},{4,12},{5,13},{6,14},{7,15},{8,0},{9,1},... | collective-permute-start | bytes 196616 | tf_op jit(solution)/shard_map/ppermute | solution.py:337

commit v17 on v16

--- a/solution.py
+++ b/solution.py
@@ -212,25 +212,16 @@
     peak = jnp.max(total, axis=1, keepdims=True)
     mass = jnp.sum(jnp.exp(total - peak), axis=1, keepdims=True)
     lane = lax.broadcasted_iota(jnp.int32, (height, 128), 1)
-    table = jnp.where(lane == 0, peak, jnp.where(lane == 1, mass, hit))
+    table = jnp.where(lane == 0, peak + jnp.log(mass), hit)
     table = reorder(jnp.transpose(table)[0:8], position, groups)
-    lines = [
-        table[row:row + 1, start:start + LANES]
-        for row in range(2)
-        for start in range(0, height, LANES)
-    ]
-    lines.append(table[2:3, :LANES])
-    lines += [jnp.zeros_like(lines[0])] * (stats.shape[1] - len(lines))
-    stats[...] = jnp.broadcast_to(jnp.concatenate(lines, axis=0)[None], stats.shape)
+    line = jnp.concatenate([table[0:1], table[1:2, :LANES]], axis=1)
+    stats[...] = jnp.broadcast_to(line[None], stats.shape)
 
 
 def log_totals(groups, stats, height):
-    count = height // LANES
-    peaks, masses = stats[:, :count, :], stats[:, count:2 * count, :]
-    peak = jnp.max(peaks, axis=0)
-    mass = jnp.sum(masses * jnp.exp(peaks - peak[None]), axis=0)
-    total = peak + jnp.log(mass)
-    line = jnp.concatenate([total[row:row + 1] for row in range(count)], axis=1)
+    parts = stats[:, :, :height]
+    peak = jnp.max(parts, axis=0)
+    line = peak + jnp.log(jnp.sum(jnp.exp(parts - peak[None]), axis=0))
     line = reorder(jnp.broadcast_to(line, (8, height)), coordinates()[1], groups)
     return jnp.transpose(jnp.concatenate([line] * 16, axis=0))
 
@@ -288,8 +279,7 @@
         copies.append(copy)
     if skipped:
         info, table, stats = refs[1:4]
-        first = 2 * info.shape[0] // LANES
-        hits = jnp.sum(stats[:, first:first + 1, :], axis=0)
+        hits = jnp.sum(stats[:, :, info.shape[0]:], axis=0)
         loss = jnp.sum(info[:, 0:1] * table[:, 0:1]) - hits[0, 0]
         last[...] = jnp.full(last.shape, loss, jnp.float32)
     else:
@@ -418,7 +408,6 @@
         return [len(parted[b]) for b in blocks]
 
     near = range(0, ranks, 2)
-    stat_rows = (2 * total_rows // LANES + 1 + 7) // 8 * 8
     partial = call(
         functools.partial(first_kernel, counts_of(near)),
         (held, *rows_of(near)),
@@ -434,7 +423,7 @@
         [VMEM] * (3 + sum(counts_of(beside))),
         (
             shape((total_rows, columns), f32),
-            shape((dps * ranks, stat_rows, LANES), f32),
+            shape((dps * ranks, 1, total_rows + LANES), f32),
         ),
         (VMEM, VMEM),
         flops=flops // 2,

time: 65.3 us -> 64.3 us (0.985)
  blocking collectives: 14.5 us -> 13.6 us
    all_to_all x1, blocking collectives: 14.5 us -> 13.6 us  [body(): stats = lax.all_to_all(stats, AXES, 0, 0)]
where the time goes in v17:
time: 64.3 us; the launch traced here: 64.1 us
  starting transfers between devices  22.3 us (35%)
  waiting for transfers between devices  14.5 us (23%)
  blocking collectives  13.6 us (21%)
  Pallas kernels  12.8 us (20%)
  between operations  0.81 us (1%)
    ppermute x23, starting transfers between devices, send(): return lax.ppermute(value, AXES, pairs)  22.3 us
    ppermute x23, waiting for transfers between devices, send(): return lax.ppermute(value, AXES, pairs)  14.5 us
    all_to_all x1, blocking collectives, body(): stats = lax.all_to_all(stats, AXES, 0, 0)  13.6 us
    pallas_call x15, Pallas kernels, call(): pl.pallas_call(kernel, out_shape=out_shape, in_specs=in_specs, out_specs=...  12.8 us
  transfers between devices with their start and end apart: 23, of which 10 were waited for; matrix products, arithmetic and copies ran while one was open for 0% of the time, Pallas kernels for 12%

profile of v17, /device:TPU:0, one launch (start us, length us, event | category | flops | bytes accessed | tf_op | source)
XLA Modules:
  0.0 64.1 jit_solution(7437778131484461156)
XLA Ops:
  0.6 1.2 %shard_map.85 = (bf16[32,1152]{1,0:T(8,128)(2,1)S(1)}, bf16[32,1024]{1,0:T(8,128)(2,1)S(1)}, bf16[32,128]{1,0:T(8,128)(2,1)S(1)}) custom-call(bf16[128,1024]{1,0:T(8,128)(2,1)} %hidden_hbm.1, s32[1,128]{1,0:T(1,128)} %bitcast.6, s32[1,128]{1,0:T(1,128)} %bitcast.7, s32[1,128]{1,0:T(1,128)} %bitcast.8), custom_call_target="tpu_custom_call" | custom-call | bytes 411136 | tf_op jit(solution)/shard_map/pallas_call | solution.py:33
  1.9 4.1 %collective-permute-start = (bf16[32,1152]{1,0:T(8,128)(2,1)S(1)}, bf16[32,1152]{1,0:T(8,128)(2,1)S(1)}, u32[]{:S(2)}, u32[]{:S(2)}) collective-permute-start(bf16[32,1152]{1,0:T(8,128)(2,1)S(1)} %get-tuple-element.34.refs_0_), channel_id=1, source_target_pairs={{0,16},{1,17},{2,18},{3,19},{4,20},{5,21},{6,22},{7,23},{8,24},{9,... | collective-permute-start | bytes 221192 | tf_op jit(solution)/shard_map/ppermute | solution.py:327
  6.0 1.3 %collective-permute-start.1 = (bf16[32,1152]{1,0:T(8,128)(2,1)S(1)}, bf16[32,1152]{1,0:T(8,128)(2,1)S(1)}, u32[]{:S(2)}, u32[]{:S(2)}) collective-permute-start(bf16[32,1152]{1,0:T(8,128)(2,1)S(1)} %get-tuple-element.34.refs_0_), channel_id=1, source_target_pairs={{0,24},{1,25},{2,26},{3,27},{4,28},{5,29},{6,30},{7,31},{8,16},{9,... | collective-permute-start | bytes 221192 | tf_op jit(solution)/shard_map/ppermute | solution.py:327
  7.5 2.4 %collective-permute-start.2 = (bf16[32,1024]{1,0:T(8,128)(2,1)S(1)}, bf16[32,1024]{1,0:T(8,128)(2,1)S(1)}, u32[]{:S(2)}, u32[]{:S(2)}) collective-permute-start(bf16[32,1024]{1,0:T(8,128)(2,1)S(1)} %get-tuple-element.35), channel_id=1, source_target_pairs={{0,6},{1,7},{2,4},{3,5},{4,2},{5,3},{6,0},{7,1},{8,14},{9,15},{10,... | collective-permute-start | bytes 196616 | tf_op jit(solution)/shard_map/ppermute | solution.py:327
  10.0 2.7 %collective-permute-done.2.refs_3_.refs_5_ = bf16[32,1024]{1,0:T(8,128)(2,1)S(1)} collective-permute-done((bf16[32,1024]{1,0:T(8,128)(2,1)S(1)}, bf16[32,1024]{1,0:T(8,128)(2,1)S(1)}, u32[]{:S(2)}, u32[]{:S(2)}) %collective-permute-start.2) | collective-permute-done | bytes 65568 | tf_op jit(solution)/shard_map/ppermute | solution.py:327
  12.8 1.7 %collective-permute-start.4 = (bf16[128,1152]{1,0:T(8,128)(2,1)S(1)}, bf16[128,1152]{1,0:T(8,128)(2,1)S(1)}, u32[]{:S(2)}, u32[]{:S(2)}) collective-permute-start(bf16[128,1152]{1,0:T(8,128)(2,1)S(1)} %get-tuple-element.36.line), channel_id=1, source_target_pairs={{0,4},{1,5},{2,6},{3,7},{4,0},{5,1},{6,2},{7,3},{8,12},{9,13},{10,... | collective-permute-start | bytes 884744 | tf_op jit(solution)/shard_map/ppermute | solution.py:327
  14.5 1.5 %collective-permute-start.5 = (bf16[128,1024]{1,0:T(8,128)(2,1)S(1)}, bf16[128,1024]{1,0:T(8,128)(2,1)S(1)}, u32[]{:S(2)}, u32[]{:S(2)}) collective-permute-start(bf16[128,1024]{1,0:T(8,128)(2,1)S(1)} %get-tuple-element.39), channel_id=1, source_target_pairs={{0,2},{1,3},{2,0},{3,1},{4,6},{5,7},{6,4},{7,5},{8,10},{9,11},{10,... | collective-permute-start | bytes 786440 | tf_op jit(solution)/shard_map/ppermute | solution.py:327
  16.3 2.9 %shard_map.87 = (bf16[4096,512]{1,0:T(8,128)(2,1)S(1)}, bf16[2048,512]{1,0:T(8,128)(2,1)S(1)}, bf16[128,1152]{1,0:T(8,128)(2,1)S(1)}) custom-call(bf16[128,1152]{1,0:T(8,128)(2,1)S(1)} %get-tuple-element.36.line, bf16[4096,512]{1,0:T(8,128)(2,1)} %weight.1), custom_call_target="tpu_custom_call" | custom-call | bytes 11075584 | tf_op jit(solution)/shard_map/pallas_call | solution.py:33
  19.3 3.1 %collective-permute-done.4.refs_1_ = bf16[128,1152]{1,0:T(8,128)(2,1)S(1)} collective-permute-done((bf16[128,1152]{1,0:T(8,128)(2,1)S(1)}, bf16[128,1152]{1,0:T(8,128)(2,1)S(1)}, u32[]{:S(2)}, u32[]{:S(2)}) %collective-permute-start.4) | collective-permute-done | bytes 294944 | tf_op jit(solution)/shard_map/ppermute | solution.py:327
  23.4 0.7 %collective-permute-done.7.after.refs_3_.refs_8_ = bf16[32,1024]{1,0:T(8,128)(2,1)S(1)} collective-permute-done((bf16[32,1024]{1,0:T(8,128)(2,1)S(1)}, bf16[32,1024]{1,0:T(8,128)(2,1)S(1)}, u32[]{:S(2)}, u32[]{:S(2)}) %collective-permute-start.7) | collective-permute-done | bytes 65568 | tf_op jit(solution)/shard_map/ppermute | solution.py:327
  24.0 0.9 %collective-permute-done.6.value = bf16[96,1024]{1,0:T(8,128)(2,1)S(1)} collective-permute-done((bf16[96,1024]{1,0:T(8,128)(2,1)S(1)}, bf16[96,1024]{1,0:T(8,128)(2,1)S(1)}, u32[]{:S(2)}, u32[]{:S(2)}) %collective-permute-start.6) | collective-permute-done | bytes 196640 | tf_op jit(solution)/shard_map/ppermute | solution.py:327
  24.9 0.7 %shard_map.91.partial = f32[256,512]{1,0:T(8,128)S(1)} custom-call(bf16[4096,512]{1,0:T(8,128)(2,1)S(1)} %get-tuple-element.38.weight, bf16[128,1152]{1,0:T(8,128)(2,1)S(1)} %get-tuple-element.37.refs_0_, bf16[128,1152]{1,0:T(8,128)(2,1)S(1)} %collective-permute-done.4.refs_1_, bf16[128,1024]{1,0:T(8,128)(2,1)S(1)} %shard_map.89.refs_2_.refs_4_, ...), custom_call_target="tpu_custom_call" | custom-call | flops 536870912 | bytes 5832704 | tf_op jit(solution)/shard_map/pallas_call | solution.py:33
  25.7 0.7 %collective-permute-done.11.refs_4_.refs_9_ = bf16[96,1024]{1,0:T(8,128)(2,1)S(1)} collective-permute-done((bf16[96,1024]{1,0:T(8,128)(2,1)S(1)}, bf16[96,1024]{1,0:T(8,128)(2,1)S(1)}, u32[]{:S(2)}, u32[]{:S(2)}) %collective-permute-start.11) | collective-permute-done | bytes 196640 | tf_op jit(solution)/shard_map/ppermute | solution.py:327
  26.4 1.1 %shard_map.92 = (f32[256,512]{1,0:T(8,128)S(1)}, f32[32,1,384]{2,1,0:T(1,128)S(1)}) custom-call(f32[256,128]{1,0:T(8,128)S(1)} %shard_map.88.after.info.refs_1_, f32[256,512]{1,0:T(8,128)S(1)} %shard_map.91.partial, bf16[4096,512]{1,0:T(8,128)(2,1)S(1)} %get-tuple-element.38.weight, bf16[128,1152]{1,0:T(8,128)(2,1)S(1)} %collective-permute-done.8.refs_0_.refs_2_, ...), custom_call_target="tpu_custom_call" | custom-call | flops 536870912 | bytes 6537216 | tf_op jit(solution)/shard_map/pallas_call | solution.py:33
  28.1 13.6 %all_to_all.5.stats.refs_3_ = f32[32,1,384]{2,1,0:T(1,128)S(1)} all-to-all(f32[32,1,384]{2,1,0:T(1,128)S(1)} %get-tuple-element.43.after), channel_id=1, replica_groups=mesh['dp'=8,'vocab'=4] {'dp','vocab'}, dimensions={0} | all-to-all | bytes 98304 | tf_op jit(solution)/shard_map/all_to_all | solution.py:433
  41.8 1.8 %shard_map.94 = (bf16[256,512]{1,0:T(8,128)(2,1)S(1)}, f32[256,128]{1,0:T(8,128)S(1)}, bf16[64,1024]{1,0:T(8,128)(2,1)S(1)}, bf16[64,1024]{1,0:T(8,128)(2,1)S(1)...) custom-call(f32[256,128]{1,0:T(8,128)S(1)} %shard_map.88.after.info., ...), custom_call_target="tpu_custom_call" | custom-call | flops 1073741824 | bytes 9224192 | tf_op jit(solution)/shard_map/pallas_call | solution.py:33
  43.6 0.6 %collective-permute-start.18 = (bf16[64,1024]{1,0:T(8,128)(2,1)S(1)}, bf16[64,1024]{1,0:T(8,128)(2,1)S(1)}, u32[]{:S(2)}, u32[]{:S(2)}) collective-permute-start(bf16[64,1024]{1,0:T(8,128)(2,1)S(1)} %get-tuple-element.57), channel_id=1, source_target_pairs={{0,4},{1,5},{2,6},{3,7},{4,0},{5,1},{6,2},{7,3},{8,12},{9,13},{10,... | collective-permute-start | bytes 393224 | tf_op jit(solution)/shard_map/ppermute | solution.py:327
  44.2 0.7 %collective-permute-start.19 = (bf16[64,1024]{1,0:T(8,128)(2,1)S(1)}, bf16[64,1024]{1,0:T(8,128)(2,1)S(1)}, u32[]{:S(2)}, u32[]{:S(2)}) collective-permute-start(bf16[64,1024]{1,0:T(8,128)(2,1)S(1)} %get-tuple-element.58), channel_id=1, source_target_pairs={{0,2},{1,3},{2,0},{3,1},{4,6},{5,7},{6,4},{7,5},{8,10},{9,11},{10,... | collective-permute-start | bytes 393224 | tf_op jit(solution)/shard_map/ppermute | solution.py:327
  44.9 2.2 %collective-permute-start.20 = (bf16[64,1024]{1,0:T(8,128)(2,1)S(1)}, bf16[64,1024]{1,0:T(8,128)(2,1)S(1)}, u32[]{:S(2)}, u32[]{:S(2)}) collective-permute-start(bf16[64,1024]{1,0:T(8,128)(2,1)S(1)} %get-tuple-element.59), channel_id=1, source_target_pairs={{0,6},{1,7},{2,4},{3,5},{4,2},{5,3},{6,0},{7,1},{8,14},{9,15},{10,... | collective-permute-start | bytes 393224 | tf_op jit(solution)/shard_map/ppermute | solution.py:327
  47.1 0.6 collective-permute-start.14
  47.7 0.7 %collective-permute-start.15 = (bf16[64,1024]{1,0:T(8,128)(2,1)S(1)}, bf16[64,1024]{1,0:T(8,128)(2,1)S(1)}, u32[]{:S(2)}, u32[]{:S(2)}) collective-permute-start(bf16[64,1024]{1,0:T(8,128)(2,1)S(1)} %get-tuple-element.48), channel_id=1, source_target_pairs={{0,2},{1,3},{2,0},{3,1},{4,6},{5,7},{6,4},{7,5},{8,10},{9,11},{10,... | collective-permute-start | bytes 393224 | tf_op jit(solution)/shard_map/ppermute | solution.py:327
  48.4 0.9 %collective-permute-done.18.refs_0_ = bf16[64,1024]{1,0:T(8,128)(2,1)S(1)} collective-permute-done((bf16[64,1024]{1,0:T(8,128)(2,1)S(1)}, bf16[64,1024]{1,0:T(8,128)(2,1)S(1)}, u32[]{:S(2)}, u32[]{:S(2)}) %collective-permute-start.18) | collective-permute-done | bytes 131104 | tf_op jit(solution)/shard_map/ppermute | solution.py:327
  49.3 1.3 %collective-permute-start.16 = (bf16[64,1024]{1,0:T(8,128)(2,1)S(1)}, bf16[64,1024]{1,0:T(8,128)(2,1)S(1)}, u32[]{:S(2)}, u32[]{:S(2)}) collective-permute-start(bf16[64,1024]{1,0:T(8,128)(2,1)S(1)} %get-tuple-element.49), channel_id=1, source_target_pairs={{0,6},{1,7},{2,4},{3,5},{4,2},{5,3},{6,0},{7,1},{8,14},{9,15},{10,... | collective-permute-start | bytes 393224 | tf_op jit(solution)/shard_map/ppermute | solution.py:327
  50.6 1.8 %shard_map.95 = (bf16[4096,512]{1,0:T(8,128)(2,1)}, f32[8,128]{1,0:T(8,128)S(1)}) custom-call(f32[64,1024]{1,0:T(8,128)S(1)} %get-tuple-element.44.after.kept, bf16[256,512]{1,0:T(8,128)(2,1)S(1)} %get-tuple-element.45.logit_grad, bf16[128,1152]{1,0:T(8,128)(2,1)S(1)} %get-tuple-element.37.refs_0_, bf16[128,1152]{1,0:T(8,128)(2,1)S(1)} %collective-permute-done.4.refs_1_, ...), custom_call_target="tpu_custom_call" | custom-call | flops 536870912 | bytes 5902336 | tf_op jit(solution)/shard_map/pallas_call | solution.py:33
  52.4 1.9 %collective-permute-done.20.refs_2_ = bf16[64,1024]{1,0:T(8,128)(2,1)S(1)} collective-permute-done((bf16[64,1024]{1,0:T(8,128)(2,1)S(1)}, bf16[64,1024]{1,0:T(8,128)(2,1)S(1)}, u32[]{:S(2)}, u32[]{:S(2)}) %collective-permute-start.20) | collective-permute-done | bytes 131104 | tf_op jit(solution)/shard_map/ppermute | solution.py:327
  54.4 0.9 %collective-permute-start.21 = (bf16[32,1024]{1,0:T(8,128)(2,1)S(1)}, bf16[32,1024]{1,0:T(8,128)(2,1)S(1)}, u32[]{:S(2)}, u32[]{:S(2)}) collective-permute-start(bf16[32,1024]{1,0:T(8,128)(2,1)S(1)} %get-tuple-element.60), channel_id=1, source_target_pairs={{0,16},{1,17},{2,18},{3,19},{4,20},{5,21},{6,22},{7,23},{8,24},{9,... | collective-permute-start | bytes 196616 | tf_op jit(solution)/shard_map/ppermute | solution.py:327
  55.2 2.3 %collective-permute-start.22 = (bf16[32,1024]{1,0:T(8,128)(2,1)S(1)}, bf16[32,1024]{1,0:T(8,128)(2,1)S(1)}, u32[]{:S(2)}, u32[]{:S(2)}) collective-permute-start(bf16[32,1024]{1,0:T(8,128)(2,1)S(1)} %get-tuple-element.61), channel_id=1, source_target_pairs={{0,24},{1,25},{2,26},{3,27},{4,28},{5,29},{6,30},{7,31},{8,16},{9,... | collective-permute-start | bytes 196616 | tf_op jit(solution)/shard_map/ppermute | solution.py:327
  57.5 1.2 %collective-permute-done.16.refs_2_ = bf16[64,1024]{1,0:T(8,128)(2,1)S(1)} collective-permute-done((bf16[64,1024]{1,0:T(8,128)(2,1)S(1)}, bf16[64,1024]{1,0:T(8,128)(2,1)S(1)}, u32[]{:S(2)}, u32[]{:S(2)}) %collective-permute-start.16) | collective-permute-done | bytes 131104 | tf_op jit(solution)/shard_map/ppermute | solution.py:327
  58.9 1.8 %shard_map.97 = (bf16[4096,512]{1,0:T(8,128)(2,1)}, f32[8,128]{1,0:T(8,128)S(1)}) custom-call(f32[32,1024]{1,0:T(8,128)S(1)} %get-tuple-element.50.after.refs_0_, bf16[256,512]{1,0:T(8,128)(2,1)S(1)} %get-tuple-element.45.logit_grad, bf16[4096,512]{1,0:T(8,128)(2,1)} %get-tuple-element.51.refs_0_, ...), custom_call_target="tpu_custom_call", output_to_operand_aliasing={{0}: (2, {})} | custom-call | flops 536870912 | bytes 10145792 | tf_op jit(solution)/shard_map/pallas_call | solution.py:33
  60.8 0.6 collective-permute-done.22.refs_3_
  61.4 1.8 %collective-permute-done.17.refs_1_ = bf16[32,1024]{1,0:T(8,128)(2,1)S(1)} collective-permute-done((bf16[32,1024]{1,0:T(8,128)(2,1)S(1)}, bf16[32,1024]{1,0:T(8,128)(2,1)S(1)}, u32[]{:S(2)}, u32[]{:S(2)}) %collective-permute-start.17) | collective-permute-done | bytes 65568 | tf_op jit(solution)/shard_map/ppermute | solution.py:327
  63.1 1.0 %shard_map.99 = (bf16[128,1024]{1,0:T(8,128)(2,1)}, f32[1,1]{1,0:T(1,128)}) custom-call(f32[8,128]{1,0:T(8,128)S(1)} %get-tuple-element.53.last, bf16[32,128]{1,0:T(8,128)(2,1)S(1)} %get-tuple-element.54.chosen, f32[32,1024]{1,0:T(8,128)S(1)} %get-tuple-element.50.after.refs_0_, bf16[32,1024]{1,0:T(8,128)(2,1)S(1)} %collective-permute-done.17.refs_1_, ...), custom_call_target="tpu_custom_call" | custom-call | bytes 602116 | tf_op jit(solution)/shard_map/pallas_call | solution.py:33
  (32 shorter events, 2.6 us)
Async XLA Ops:
  0.6 22.2 %copy-start = (f32[32]{0:T(128)S(1)}, f32[32]{0:T(128)}, u32[]{:S(2)}) copy-start(f32[32]{0:T(128)} %param.11) | copy-start | bytes 388
  1.9 10.8 %collective-permute-start = (bf16[32,1152]{1,0:T(8,128)(2,1)S(1)}, bf16[32,1152]{1,0:T(8,128)(2,1)S(1)}, u32[]{:S(2)}, u32[]{:S(2)}) collective-permute-start(bf16[32,1152]{1,0:T(8,128)(2,1)S(1)} %get-tuple-element.34.refs_0_), channel_id=1, source_target_pairs={{0,16},{1,17},{2,18},{3,19},{4,20},{5,21},{6,22},{7,23},{8,24},{9,... | collective-permute-start | bytes 221192 | tf_op jit(solution)/shard_map/ppermute | solution.py:327
  6.0 6.8 %collective-permute-start.1 = (bf16[32,1152]{1,0:T(8,128)(2,1)S(1)}, bf16[32,1152]{1,0:T(8,128)(2,1)S(1)}, u32[]{:S(2)}, u32[]{:S(2)}) collective-permute-start(bf16[32,1152]{1,0:T(8,128)(2,1)S(1)} %get-tuple-element.34.refs_0_), channel_id=1, source_target_pairs={{0,24},{1,25},{2,26},{3,27},{4,28},{5,29},{6,30},{7,31},{8,16},{9,... | collective-permute-start | bytes 221192 | tf_op jit(solution)/shard_map/ppermute | solution.py:327
  7.3 5.4 %collective-permute-start.3 = (bf16[32,1152]{1,0:T(8,128)(2,1)S(1)}, bf16[32,1152]{1,0:T(8,128)(2,1)S(1)}, u32[]{:S(2)}, u32[]{:S(2)}) collective-permute-start(bf16[32,1152]{1,0:T(8,128)(2,1)S(1)} %get-tuple-element.34.refs_0_), channel_id=1, source_target_pairs={{0,8},{1,9},{2,10},{3,11},{4,12},{5,13},{6,14},{7,15},{8,0},{9,1},... | collective-permute-start | bytes 221192 | tf_op jit(solution)/shard_map/ppermute | solution.py:327
  7.5 5.2 %collective-permute-start.2 = (bf16[32,1024]{1,0:T(8,128)(2,1)S(1)}, bf16[32,1024]{1,0:T(8,128)(2,1)S(1)}, u32[]{:S(2)}, u32[]{:S(2)}) collective-permute-start(bf16[32,1024]{1,0:T(8,128)(2,1)S(1)} %get-tuple-element.35), channel_id=1, source_target_pairs={{0,6},{1,7},{2,4},{3,5},{4,2},{5,3},{6,0},{7,1},{8,14},{9,15},{10,... | collective-permute-start | bytes 196616 | tf_op jit(solution)/shard_map/ppermute | solution.py:327
  12.8 9.6 %collective-permute-start.4 = (bf16[128,1152]{1,0:T(8,128)(2,1)S(1)}, bf16[128,1152]{1,0:T(8,128)(2,1)S(1)}, u32[]{:S(2)}, u32[]{:S(2)}) collective-permute-start(bf16[128,1152]{1,0:T(8,128)(2,1)S(1)} %get-tuple-element.36.line), channel_id=1, source_target_pairs={{0,4},{1,5},{2,6},{3,7},{4,0},{5,1},{6,2},{7,3},{8,12},{9,13},{10,... | collective-permute-start | bytes 884744 | tf_op jit(solution)/shard_map/ppermute | solution.py:327
  14.5 8.8 %collective-permute-start.5 = (bf16[128,1024]{1,0:T(8,128)(2,1)S(1)}, bf16[128,1024]{1,0:T(8,128)(2,1)S(1)}, u32[]{:S(2)}, u32[]{:S(2)}) collective-permute-start(bf16[128,1024]{1,0:T(8,128)(2,1)S(1)} %get-tuple-element.39), channel_id=1, source_target_pairs={{0,2},{1,3},{2,0},{3,1},{4,6},{5,7},{6,4},{7,5},{8,10},{9,11},{10,... | collective-permute-start | bytes 786440 | tf_op jit(solution)/shard_map/ppermute | solution.py:327
  15.9 9.0 %collective-permute-start.6 = (bf16[96,1024]{1,0:T(8,128)(2,1)S(1)}, bf16[96,1024]{1,0:T(8,128)(2,1)S(1)}, u32[]{:S(2)}, u32[]{:S(2)}) collective-permute-start(bf16[96,1024]{1,0:T(8,128)(2,1)S(1)} %get-tuple-element.40), channel_id=1, source_target_pairs={{0,6},{1,7},{2,4},{3,5},{4,2},{5,3},{6,0},{7,1},{8,14},{9,15},{10,... | collective-permute-start | bytes 589832 | tf_op jit(solution)/shard_map/ppermute | solution.py:327
  19.2 6.4 %collective-permute-start.8 = (bf16[128,1152]{1,0:T(8,128)(2,1)S(1)}, bf16[128,1152]{1,0:T(8,128)(2,1)S(1)}, u32[]{:S(2)}, u32[]{:S(2)}) collective-permute-start(bf16[128,1152]{1,0:T(8,128)(2,1)S(1)} %get-tuple-element.37.refs_0_), channel_id=1, source_target_pairs={{0,1},{1,0},{2,3},{3,2},{4,5},{5,4},{6,7},{7,6},{8,9},{9,8},{10,11... | collective-permute-start | bytes 884744 | tf_op jit(solution)/shard_map/ppermute | solution.py:327
  22.4 4.0 %collective-permute-start.9 = (bf16[128,1152]{1,0:T(8,128)(2,1)S(1)}, bf16[128,1152]{1,0:T(8,128)(2,1)S(1)}, u32[]{:S(2)}, u32[]{:S(2)}) collective-permute-start(bf16[128,1152]{1,0:T(8,128)(2,1)S(1)} %collective-permute-done.4.refs_1_), channel_id=1, source_target_pairs={{0,1},{1,0},{2,3},{3,2},{4,5},{5,4},{6,7},{7,6},{8,9},{9,8},{10,11... | collective-permute-start | bytes 884744 | tf_op jit(solution)/shard_map/ppermute | solution.py:327
  22.4 1.7 %collective-permute-start.7 = (bf16[32,1024]{1,0:T(8,128)(2,1)S(1)}, bf16[32,1024]{1,0:T(8,128)(2,1)S(1)}, u32[]{:S(2)}, u32[]{:S(2)}) collective-permute-start(bf16[32,1024]{1,0:T(8,128)(2,1)S(1)} %collective-permute-done.2.refs_3_.refs_5_), channel_id=1, source_target_pairs={{0,1},{1,0},{2,3},{3,2},{4,5},{5,4},{6,7},{7,6},{8,9},{9,8},{10,11... | collective-permute-start | bytes 196616 | tf_op jit(solution)/shard_map/ppermute | solution.py:327
  23.3 3.1 %collective-permute-start.10 = (bf16[128,1024]{1,0:T(8,128)(2,1)S(1)}, bf16[128,1024]{1,0:T(8,128)(2,1)S(1)}, u32[]{:S(2)}, u32[]{:S(2)}) collective-permute-start(bf16[128,1024]{1,0:T(8,128)(2,1)S(1)} %shard_map.89.refs_2_.refs_4_), channel_id=1, source_target_pairs={{0,1},{1,0},{2,3},{3,2},{4,5},{5,4},{6,7},{7,6},{8,9},{9,8},{10,11... | collective-permute-start | bytes 786440 | tf_op jit(solution)/shard_map/ppermute | solution.py:327
  24.9 1.4 %collective-permute-start.11 = (bf16[96,1024]{1,0:T(8,128)(2,1)S(1)}, bf16[96,1024]{1,0:T(8,128)(2,1)S(1)}, u32[]{:S(2)}, u32[]{:S(2)}) collective-permute-start(bf16[96,1024]{1,0:T(8,128)(2,1)S(1)} %shard_map.90.refs_4_.refs_6_), channel_id=1, source_target_pairs={{0,1},{1,0},{2,3},{3,2},{4,5},{5,4},{6,7},{7,6},{8,9},{9,8},{10,11... | collective-permute-start | bytes 589832 | tf_op jit(solution)/shard_map/ppermute | solution.py:327
  27.6 14.2 %collective-permute-start.13 = (bf16[2048,512]{1,0:T(8,128)(2,1)S(1)}, bf16[2048,512]{1,0:T(8,128)(2,1)S(1)}, u32[]{:S(2)}, u32[]{:S(2)}) collective-permute-start(bf16[2048,512]{1,0:T(8,128)(2,1)S(1)} %shard_map.93), channel_id=1, source_target_pairs={{0,1},{1,0},{2,3},{3,2},{4,5},{5,4},{6,7},{7,6},{8,9},{9,8},{10,11... | collective-permute-start | bytes 6291464 | tf_op jit(solution)/shard_map/ppermute | solution.py:327
  27.8 14.0 %collective-permute-start.12 = (f32[256,512]{1,0:T(8,128)S(1)}, f32[256,512]{1,0:T(8,128)S(1)}, u32[]{:S(2)}, u32[]{:S(2)}) collective-permute-start(f32[256,512]{1,0:T(8,128)S(1)} %get-tuple-element.41.mine), channel_id=1, source_target_pairs={{0,1},{1,0},{2,3},{3,2},{4,5},{5,4},{6,7},{7,6},{8,9},{9,8},{10,11... | collective-permute-start | bytes 1572872 | tf_op jit(solution)/shard_map/ppermute | solution.py:327
  43.6 5.7 %collective-permute-start.18 = (bf16[64,1024]{1,0:T(8,128)(2,1)S(1)}, bf16[64,1024]{1,0:T(8,128)(2,1)S(1)}, u32[]{:S(2)}, u32[]{:S(2)}) collective-permute-start(bf16[64,1024]{1,0:T(8,128)(2,1)S(1)} %get-tuple-element.57), channel_id=1, source_target_pairs={{0,4},{1,5},{2,6},{3,7},{4,0},{5,1},{6,2},{7,3},{8,12},{9,13},{10,... | collective-permute-start | bytes 393224 | tf_op jit(solution)/shard_map/ppermute | solution.py:327
  44.2 8.2 %collective-permute-start.19 = (bf16[64,1024]{1,0:T(8,128)(2,1)S(1)}, bf16[64,1024]{1,0:T(8,128)(2,1)S(1)}, u32[]{:S(2)}, u32[]{:S(2)}) collective-permute-start(bf16[64,1024]{1,0:T(8,128)(2,1)S(1)} %get-tuple-element.58), channel_id=1, source_target_pairs={{0,2},{1,3},{2,0},{3,1},{4,6},{5,7},{6,4},{7,5},{8,10},{9,11},{10,... | collective-permute-start | bytes 393224 | tf_op jit(solution)/shard_map/ppermute | solution.py:327
  44.9 9.4 %collective-permute-start.20 = (bf16[64,1024]{1,0:T(8,128)(2,1)S(1)}, bf16[64,1024]{1,0:T(8,128)(2,1)S(1)}, u32[]{:S(2)}, u32[]{:S(2)}) collective-permute-start(bf16[64,1024]{1,0:T(8,128)(2,1)S(1)} %get-tuple-element.59), channel_id=1, source_target_pairs={{0,6},{1,7},{2,4},{3,5},{4,2},{5,3},{6,0},{7,1},{8,14},{9,15},{10,... | collective-permute-start | bytes 393224 | tf_op jit(solution)/shard_map/ppermute | solution.py:327
  47.1 10.4 %collective-permute-start.14 = (bf16[64,1024]{1,0:T(8,128)(2,1)S(1)}, bf16[64,1024]{1,0:T(8,128)(2,1)S(1)}, u32[]{:S(2)}, u32[]{:S(2)}) collective-permute-start(bf16[64,1024]{1,0:T(8,128)(2,1)S(1)} %get-tuple-element.47), channel_id=1, source_target_pairs={{0,4},{1,5},{2,6},{3,7},{4,0},{5,1},{6,2},{7,3},{8,12},{9,13},{10,... | collective-permute-start | bytes 393224 | tf_op jit(solution)/shard_map/ppermute | solution.py:327
  47.7 9.8 %collective-permute-start.15 = (bf16[64,1024]{1,0:T(8,128)(2,1)S(1)}, bf16[64,1024]{1,0:T(8,128)(2,1)S(1)}, u32[]{:S(2)}, u32[]{:S(2)}) collective-permute-start(bf16[64,1024]{1,0:T(8,128)(2,1)S(1)} %get-tuple-element.48), channel_id=1, source_target_pairs={{0,2},{1,3},{2,0},{3,1},{4,6},{5,7},{6,4},{7,5},{8,10},{9,11},{10,... | collective-permute-start | bytes 393224 | tf_op jit(solution)/shard_map/ppermute | solution.py:327
  49.3 9.5 %collective-permute-start.16 = (bf16[64,1024]{1,0:T(8,128)(2,1)S(1)}, bf16[64,1024]{1,0:T(8,128)(2,1)S(1)}, u32[]{:S(2)}, u32[]{:S(2)}) collective-permute-start(bf16[64,1024]{1,0:T(8,128)(2,1)S(1)} %get-tuple-element.49), channel_id=1, source_target_pairs={{0,6},{1,7},{2,4},{3,5},{4,2},{5,3},{6,0},{7,1},{8,14},{9,15},{10,... | collective-permute-start | bytes 393224 | tf_op jit(solution)/shard_map/ppermute | solution.py:327
  54.4 6.4 %collective-permute-start.21 = (bf16[32,1024]{1,0:T(8,128)(2,1)S(1)}, bf16[32,1024]{1,0:T(8,128)(2,1)S(1)}, u32[]{:S(2)}, u32[]{:S(2)}) collective-permute-start(bf16[32,1024]{1,0:T(8,128)(2,1)S(1)} %get-tuple-element.60), channel_id=1, source_target_pairs={{0,16},{1,17},{2,18},{3,19},{4,20},{5,21},{6,22},{7,23},{8,24},{9,... | collective-permute-start | bytes 196616 | tf_op jit(solution)/shard_map/ppermute | solution.py:327
  55.2 6.2 %collective-permute-start.22 = (bf16[32,1024]{1,0:T(8,128)(2,1)S(1)}, bf16[32,1024]{1,0:T(8,128)(2,1)S(1)}, u32[]{:S(2)}, u32[]{:S(2)}) collective-permute-start(bf16[32,1024]{1,0:T(8,128)(2,1)S(1)} %get-tuple-element.61), channel_id=1, source_target_pairs={{0,24},{1,25},{2,26},{3,27},{4,28},{5,29},{6,30},{7,31},{8,16},{9,... | collective-permute-start | bytes 196616 | tf_op jit(solution)/shard_map/ppermute | solution.py:327
  58.8 4.3 %collective-permute-start.17 = (bf16[32,1024]{1,0:T(8,128)(2,1)S(1)}, bf16[32,1024]{1,0:T(8,128)(2,1)S(1)}, u32[]{:S(2)}, u32[]{:S(2)}) collective-permute-start(bf16[32,1024]{1,0:T(8,128)(2,1)S(1)} %get-tuple-element.55), channel_id=1, source_target_pairs={{0,8},{1,9},{2,10},{3,11},{4,12},{5,13},{6,14},{7,15},{8,0},{9,1},... | collective-permute-start | bytes 196616 | tf_op jit(solution)/shard_map/ppermute | solution.py:327

commit v18 on v17

--- a/solution.py
+++ b/solution.py
@@ -10,8 +10,8 @@
 
 CAP = 32
 MOST_VMEM = 56 * 1024 * 1024
-IDS = 128
 LANES = 128
+SUB = 16
 grad_scale = 16384.0
 AXES = ("dp", "vocab")
 SMEM = pl.BlockSpec(memory_space=pltpu.SMEM)
@@ -70,7 +70,22 @@
     return (slot.astype(jnp.int32) == grid) & (mask == 1)
 
 
-def pack_kernel(hidden_hbm, mask_hbm, target_hbm, turn_hbm, rows, plain, chosen_out, *scratch):
+def payload_rows(width):
+    return CAP * width // LANES + SUB
+
+
+def tiles(width):
+    count = width // LANES
+    for high in range(CAP // SUB):
+        for low in range(count):
+            yield (
+                (high * count + low) * SUB,
+                slice(high * SUB, (high + 1) * SUB),
+                slice(low * LANES, (low + 1) * LANES),
+            )
+
+
+def pack_kernel(hidden_hbm, mask_hbm, target_hbm, turn_hbm, payload, plain, chosen_out, *scratch):
     hidden, mask, target, turn, sems = scratch
     copies = []
     for place, (source, held) in enumerate(
@@ -82,8 +97,7 @@
     for copy in copies[:3]:
         copy.wait()
     width = hidden.shape[1]
-    chosen = choose(mask[...])
-    one_hot = chosen.astype(jnp.float32).astype(jnp.bfloat16)
+    one_hot = choose(mask[...]).astype(jnp.float32).astype(jnp.bfloat16)
     chosen_out[...] = one_hot
     turns, targets = turn[...], target[...]
     fields = (
@@ -94,28 +108,44 @@
         (targets >> 8) & 255,
         targets >> 16,
     )
-    lane = lax.broadcasted_iota(jnp.int32, (CAP, IDS), 1)
-    table = jnp.zeros((CAP, IDS), jnp.float32)
-    for place, field in enumerate(fields):
-        picked = jnp.where(chosen, field.astype(jnp.float32), 0.0)
-        table = jnp.where(lane == place, jnp.sum(picked, axis=1, keepdims=True), table)
-    rows[:, width:] = table.astype(jnp.bfloat16)
+    fields += (jnp.zeros_like(turns),) * (SUB - len(fields))
+    fields = jnp.concatenate([field.astype(jnp.float32) for field in fields], axis=0)
+    slots = jnp.concatenate([one_hot] + [jnp.zeros_like(one_hot)] * (LANES // CAP - 1), axis=0)
+    ids = lax.dot_general(
+        fields.astype(jnp.bfloat16),
+        slots,
+        (((1,), (1,)), ((), ())),
+        preferred_element_type=jnp.float32,
+    )
+    payload[payload.shape[0] - SUB:] = ids.astype(jnp.bfloat16)
     copies[3].wait()
     packed = jnp.dot(one_hot, hidden[...], preferred_element_type=jnp.float32)
     packed = packed.astype(jnp.bfloat16)
-    rows[:, :width] = packed
     plain[...] = packed
+    for start, rows, lanes in tiles(width):
+        payload[start:start + SUB] = packed[rows, lanes]
+
+
+def unroll(payload, first, plain, place):
+    for start, rows, lanes in tiles(plain.shape[1]):
+        target = slice(place * CAP + rows.start, place * CAP + rows.stop)
+        plain[target, lanes] = payload[first + start:first + start + SUB]
 
 
 def join_kernel(order, *refs):
     blocks, (line, plain, far) = refs[:len(order) - 1] + refs[-4:-3], refs[-3:]
-    width = plain.shape[1]
     for place, block in zip(order, blocks):
-        rows = slice(place * CAP, (place + 1) * CAP)
-        line[rows] = block[...]
-        plain[rows] = block[:, :width]
+        height = block.shape[0]
+        line[place * height:(place + 1) * height] = block[...]
+        unroll(block, 0, plain, place)
         if place:
-            far[(place - 1) * CAP:place * CAP] = block[:, :width]
+            unroll(block, 0, far, place - 1)
+
+
+def rows_kernel(line, plain):
+    height = payload_rows(plain.shape[1])
+    for place in range(line.shape[0] // height):
+        unroll(line, place * height, plain, place)
 
 
 def stage_kernel(blocks, line, weight, held, away, same, sems):
@@ -142,10 +172,14 @@
     pass
 
 
-def info_kernel(*refs):
-    advantages, info = refs[-2:]
-    start = refs[0].shape[1] - IDS
-    table = jnp.concatenate([ref[:, start:] for ref in refs[:-2]], axis=0).astype(jnp.float32)
+def info_kernel(height, own, other, advantages, info):
+    tables = []
+    for line in (own, other):
+        for end in range(height, line.shape[0] + 1, height):
+            ids = line[end - SUB:end].astype(jnp.float32)
+            ids = jnp.concatenate([ids] * (LANES // SUB), axis=0)
+            tables.append(jnp.transpose(ids)[:CAP])
+    table = jnp.concatenate(tables, axis=0)
     valid = table[:, 0:1]
     turn = table[:, 1:2] + 256.0 * table[:, 2:3]
     target = table[:, 3:4] + 256.0 * table[:, 4:5] + 65536.0 * table[:, 5:6]
@@ -175,9 +209,9 @@
     return stats
 
 
-def all_rows(pieces, counts, place, width):
+def all_rows(pieces, counts, place):
     start = sum(counts[:place])
-    return jnp.concatenate([ref[:, :width] for ref in pieces[start:start + counts[place]]], axis=0)
+    return jnp.concatenate([ref[...] for ref in pieces[start:start + counts[place]]], axis=0)
 
 
 def some_logits(counts, first, pieces, weight):
@@ -187,7 +221,7 @@
     for place, block in enumerate(range(first, blocks, 2)):
         start = pl.multiple_of((rank ^ block) * width, width)
         part = jnp.dot(
-            all_rows(pieces, counts, place, width),
+            all_rows(pieces, counts, place),
             weight[pl.ds(start, width), :],
             preferred_element_type=jnp.float32,
         )
@@ -266,7 +300,7 @@
     copies = []
     for place, block in enumerate(blocks):
         done[place * width:(place + 1) * width] = lax.dot_general(
-            all_rows(pieces, counts, place, width),
+            all_rows(pieces, counts, place),
             logit_grad[...],
             (((0,), (0,)), ((), ())),
             preferred_element_type=jnp.float32,
@@ -336,7 +370,7 @@
         ),
         [HBM] * 4,
         (
-            shape((CAP, width + IDS), bf16),
+            shape((payload_rows(width), LANES), bf16),
             shape((CAP, width), bf16),
             shape((CAP, tokens), bf16),
         ),
@@ -350,39 +384,40 @@
     blocks = [send(packed, z=z) if z else packed for z in line_order[:-1]]
     corners = {x: send(own, y=1, x=x) for x in range(1, xs)}
     blocks.append(send(packed, z=1))
-    line_rows = zs * CAP
+    line_rows, height = zs * CAP, payload_rows(width)
     line, line_plain, far = call(
         functools.partial(join_kernel, line_order),
         (*blocks[:-1], *corners.values(), blocks[-1]),
         [VMEM] * (zs - 1) + [ANY] * len(corners) + [VMEM],
         (
-            shape((line_rows, width + IDS), bf16),
+            shape((zs * height, LANES), bf16),
             shape((line_rows, width), bf16),
             shape((line_rows - CAP, width), bf16),
         ),
         (VMEM,) * 3,
     )
-    pieces = {(0, 1, 0): send(line, y=1)}
+    across = send(line, y=1)
+    pieces = {(0, 1, 0): call(rows_kernel, (across,), [VMEM], shape((line_rows, width), bf16), VMEM)}
     for x in range(1, xs):
         pieces[2 * x, 0, 0] = send(line_plain, x=x)
         pieces[2 * x, 1, 0] = corners[x]
         pieces[2 * x, 1, 1] = send(far, y=1, x=x)
     held, away, same = call(
         functools.partial(stage_kernel, ranks),
-        (line, in_hbm(weight)),
+        (line_plain, in_hbm(weight)),
         [VMEM, HBM],
         (
             shape((depth, columns), bf16),
             shape((depth // 2, columns), bf16),
-            shape(line.shape, bf16),
+            shape(line_plain.shape, bf16),
         ),
         (VMEM,) * 3,
         [pltpu.SemaphoreType.DMA((ranks + xs,))],
     )
     pieces[0, 0, 0] = same
     info = call(
-        info_kernel,
-        (same, pieces[0, 1, 0], advantages.reshape(1, -1)),
+        functools.partial(info_kernel, height),
+        (line, across, advantages.reshape(1, -1)),
         [VMEM] * 3,
         shape((total_rows, 128), f32),
         VMEM,

time: 64.3 us -> 63.9 us (level)
  waiting for transfers between devices: 14.5 us -> 13.7 us
    ppermute x23, waiting for transfers between devices: 14.5 us -> 13.7 us  [send(): return lax.ppermute(value, AXES, pairs)]
    pallas_call x15 -> x16, Pallas kernels: 12.8 us -> 13 us  [call(): pl.pallas_call(kernel, out_shape=out_shape, in_specs=in_specs, out_specs=...]
where the time goes in v18:
time: 63.9 us; the launch traced here: 63.8 us
  starting transfers between devices  22.8 us (36%)
  waiting for transfers between devices  13.7 us (21%)
  blocking collectives  13.4 us (21%)
  Pallas kernels  13 us (20%)
  between operations  0.78 us (1%)
    ppermute x23, starting transfers between devices, send(): return lax.ppermute(value, AXES, pairs)  22.8 us
    ppermute x23, waiting for transfers between devices, send(): return lax.ppermute(value, AXES, pairs)  13.7 us
    all_to_all x1, blocking collectives, body(): stats = lax.all_to_all(stats, AXES, 0, 0)  13.4 us
    pallas_call x16, Pallas kernels, call(): pl.pallas_call(kernel, out_shape=out_shape, in_specs=in_specs, out_specs=...  13 us
  transfers between devices with their start and end apart: 23, of which 10 were waited for; matrix products, arithmetic and copies ran while one was open for 0% of the time, Pallas kernels for 12%

profile of v18, /device:TPU:0, one launch (start us, length us, event | category | flops | bytes accessed | tf_op | source)
XLA Modules:
  0.0 63.8 jit_solution(4784074471772456789)
XLA Ops:
  0.6 1.2 %shard_map.85 = (bf16[272,128]{1,0:T(8,128)(2,1)S(1)}, bf16[32,1024]{1,0:T(8,128)(2,1)S(1)}, bf16[32,128]{1,0:T(8,128)(2,1)S(1)}) custom-call(bf16[128,1024]{1,0:T(8,128)(2,1)} %hidden_hbm.1, s32[1,128]{1,0:T(1,128)} %bitcast.6, s32[1,128]{1,0:T(1,128)} %bitcast.7, s32[1,128]{1,0:T(1,128)} %bitcast.8), custom_call_target="tpu_custom_call" | custom-call | bytes 407040 | tf_op jit(solution)/shard_map/pallas_call | solution.py:33
  1.9 4.1 %collective-permute-start = (bf16[272,128]{1,0:T(8,128)(2,1)S(1)}, bf16[272,128]{1,0:T(8,128)(2,1)S(1)}, u32[]{:S(2)}, u32[]{:S(2)}) collective-permute-start(bf16[272,128]{1,0:T(8,128)(2,1)S(1)} %get-tuple-element.34.refs_0_), channel_id=1, source_target_pairs={{0,16},{1,17},{2,18},{3,19},{4,20},{5,21},{6,22},{7,23},{8,24},{9,... | collective-permute-start | bytes 208904 | tf_op jit(solution)/shard_map/ppermute | solution.py:361
  6.0 1.3 %collective-permute-start.1 = (bf16[272,128]{1,0:T(8,128)(2,1)S(1)}, bf16[272,128]{1,0:T(8,128)(2,1)S(1)}, u32[]{:S(2)}, u32[]{:S(2)}) collective-permute-start(bf16[272,128]{1,0:T(8,128)(2,1)S(1)} %get-tuple-element.34.refs_0_), channel_id=1, source_target_pairs={{0,24},{1,25},{2,26},{3,27},{4,28},{5,29},{6,30},{7,31},{8,16},{9,... | collective-permute-start | bytes 208904 | tf_op jit(solution)/shard_map/ppermute | solution.py:361
  7.5 2.4 %collective-permute-start.2 = (bf16[32,1024]{1,0:T(8,128)(2,1)S(1)}, bf16[32,1024]{1,0:T(8,128)(2,1)S(1)}, u32[]{:S(2)}, u32[]{:S(2)}) collective-permute-start(bf16[32,1024]{1,0:T(8,128)(2,1)S(1)} %get-tuple-element.35), channel_id=1, source_target_pairs={{0,6},{1,7},{2,4},{3,5},{4,2},{5,3},{6,0},{7,1},{8,14},{9,15},{10,... | collective-permute-start | bytes 196616 | tf_op jit(solution)/shard_map/ppermute | solution.py:361
  10.0 2.7 %collective-permute-done.2.refs_3_.refs_5_ = bf16[32,1024]{1,0:T(8,128)(2,1)S(1)} collective-permute-done((bf16[32,1024]{1,0:T(8,128)(2,1)S(1)}, bf16[32,1024]{1,0:T(8,128)(2,1)S(1)}, u32[]{:S(2)}, u32[]{:S(2)}) %collective-permute-start.2) | collective-permute-done | bytes 65568 | tf_op jit(solution)/shard_map/ppermute | solution.py:361
  12.8 1.6 %collective-permute-start.4 = (bf16[1088,128]{1,0:T(8,128)(2,1)S(1)}, bf16[1088,128]{1,0:T(8,128)(2,1)S(1)}, u32[]{:S(2)}, u32[]{:S(2)}) collective-permute-start(bf16[1088,128]{1,0:T(8,128)(2,1)S(1)} %get-tuple-element.36.own), channel_id=1, source_target_pairs={{0,4},{1,5},{2,6},{3,7},{4,0},{5,1},{6,2},{7,3},{8,12},{9,13},{10,... | collective-permute-start | bytes 835592 | tf_op jit(solution)/shard_map/ppermute | solution.py:361
  14.4 1.5 %collective-permute-start.5 = (bf16[128,1024]{1,0:T(8,128)(2,1)S(1)}, bf16[128,1024]{1,0:T(8,128)(2,1)S(1)}, u32[]{:S(2)}, u32[]{:S(2)}) collective-permute-start(bf16[128,1024]{1,0:T(8,128)(2,1)S(1)} %get-tuple-element.37.line), channel_id=1, source_target_pairs={{0,2},{1,3},{2,0},{3,1},{4,6},{5,7},{6,4},{7,5},{8,10},{9,11},{10,... | collective-permute-start | bytes 786440 | tf_op jit(solution)/shard_map/ppermute | solution.py:361
  16.4 2.9 %shard_map.88 = (bf16[4096,512]{1,0:T(8,128)(2,1)S(1)}, bf16[2048,512]{1,0:T(8,128)(2,1)S(1)}, bf16[128,1024]{1,0:T(8,128)(2,1)S(1)}) custom-call(bf16[128,1024]{1,0:T(8,128)(2,1)S(1)} %get-tuple-element.37.line, bf16[4096,512]{1,0:T(8,128)(2,1)} %weight.1), custom_call_target="tpu_custom_call" | custom-call | bytes 11010048 | tf_op jit(solution)/shard_map/pallas_call | solution.py:33
  19.3 0.6 collective-permute-start.8
  19.9 1.9 %collective-permute-done.4.other.line = bf16[1088,128]{1,0:T(8,128)(2,1)S(1)} collective-permute-done((bf16[1088,128]{1,0:T(8,128)(2,1)S(1)}, bf16[1088,128]{1,0:T(8,128)(2,1)S(1)}, u32[]{:S(2)}, u32[]{:S(2)}) %collective-permute-start.4) | collective-permute-done | bytes 278560 | tf_op jit(solution)/shard_map/ppermute | solution.py:361
  22.3 0.6 %collective-permute-done.5.value = bf16[128,1024]{1,0:T(8,128)(2,1)S(1)} collective-permute-done((bf16[128,1024]{1,0:T(8,128)(2,1)S(1)}, bf16[128,1024]{1,0:T(8,128)(2,1)S(1)}, u32[]{:S(2)}, u32[]{:S(2)}) %collective-permute-start.5) | collective-permute-done | bytes 262176 | tf_op jit(solution)/shard_map/ppermute | solution.py:361
  23.5 1.3 %collective-permute-done.6.value = bf16[96,1024]{1,0:T(8,128)(2,1)S(1)} collective-permute-done((bf16[96,1024]{1,0:T(8,128)(2,1)S(1)}, bf16[96,1024]{1,0:T(8,128)(2,1)S(1)}, u32[]{:S(2)}, u32[]{:S(2)}) %collective-permute-start.6) | collective-permute-done | bytes 196640 | tf_op jit(solution)/shard_map/ppermute | solution.py:361
  24.8 0.7 %shard_map.92.partial = f32[256,512]{1,0:T(8,128)S(1)} custom-call(bf16[4096,512]{1,0:T(8,128)(2,1)S(1)} %get-tuple-element.38.weight, bf16[128,1024]{1,0:T(8,128)(2,1)S(1)} %get-tuple-element.39.refs_0_, bf16[128,1024]{1,0:T(8,128)(2,1)S(1)} %shard_map.89.refs_1_, bf16[128,1024]{1,0:T(8,128)(2,1)S(1)} %shard_map.90.refs_2_.refs_4_, ...), custom_call_target="tpu_custom_call" | custom-call | flops 536870912 | bytes 5767168 | tf_op jit(solution)/shard_map/pallas_call | solution.py:33
  25.5 0.7 %collective-permute-done.11.refs_4_.refs_9_ = bf16[96,1024]{1,0:T(8,128)(2,1)S(1)} collective-permute-done((bf16[96,1024]{1,0:T(8,128)(2,1)S(1)}, bf16[96,1024]{1,0:T(8,128)(2,1)S(1)}, u32[]{:S(2)}, u32[]{:S(2)}) %collective-permute-start.11) | collective-permute-done | bytes 196640 | tf_op jit(solution)/shard_map/ppermute | solution.py:361
  26.3 1.1 %shard_map.93 = (f32[256,512]{1,0:T(8,128)S(1)}, f32[32,1,384]{2,1,0:T(1,128)S(1)}) custom-call(f32[256,128]{1,0:T(8,128)S(1)} %shard_map.87.after.info.refs_1_, f32[256,512]{1,0:T(8,128)S(1)} %shard_map.92.partial, bf16[4096,512]{1,0:T(8,128)(2,1)S(1)} %get-tuple-element.38.weight, bf16[128,1024]{1,0:T(8,128)(2,1)S(1)} %collective-permute-done.8.refs_0_.refs_2_, ...), custom_call_target="tpu_custom_call" | custom-call | flops 536870912 | bytes 6471680 | tf_op jit(solution)/shard_map/pallas_call | solution.py:33
  28.0 13.4 %all_to_all.5.stats.refs_3_ = f32[32,1,384]{2,1,0:T(1,128)S(1)} all-to-all(f32[32,1,384]{2,1,0:T(1,128)S(1)} %get-tuple-element.43.after), channel_id=1, replica_groups=mesh['dp'=8,'vocab'=4] {'dp','vocab'}, dimensions={0} | all-to-all | bytes 98304 | tf_op jit(solution)/shard_map/all_to_all | solution.py:468
  41.4 1.8 %shard_map.95 = (bf16[256,512]{1,0:T(8,128)(2,1)S(1)}, f32[256,128]{1,0:T(8,128)S(1)}, bf16[64,1024]{1,0:T(8,128)(2,1)S(1)}, bf16[64,1024]{1,0:T(8,128)(2,1)S(1)...) custom-call(f32[256,128]{1,0:T(8,128)S(1)} %shard_map.87.after.info., ...), custom_call_target="tpu_custom_call" | custom-call | flops 1073741824 | bytes 9224192 | tf_op jit(solution)/shard_map/pallas_call | solution.py:33
  43.2 0.6 %collective-permute-start.18 = (bf16[64,1024]{1,0:T(8,128)(2,1)S(1)}, bf16[64,1024]{1,0:T(8,128)(2,1)S(1)}, u32[]{:S(2)}, u32[]{:S(2)}) collective-permute-start(bf16[64,1024]{1,0:T(8,128)(2,1)S(1)} %get-tuple-element.57), channel_id=1, source_target_pairs={{0,4},{1,5},{2,6},{3,7},{4,0},{5,1},{6,2},{7,3},{8,12},{9,13},{10,... | collective-permute-start | bytes 393224 | tf_op jit(solution)/shard_map/ppermute | solution.py:361
  43.8 0.7 %collective-permute-start.19 = (bf16[64,1024]{1,0:T(8,128)(2,1)S(1)}, bf16[64,1024]{1,0:T(8,128)(2,1)S(1)}, u32[]{:S(2)}, u32[]{:S(2)}) collective-permute-start(bf16[64,1024]{1,0:T(8,128)(2,1)S(1)} %get-tuple-element.58), channel_id=1, source_target_pairs={{0,2},{1,3},{2,0},{3,1},{4,6},{5,7},{6,4},{7,5},{8,10},{9,11},{10,... | collective-permute-start | bytes 393224 | tf_op jit(solution)/shard_map/ppermute | solution.py:361
  44.5 2.2 %collective-permute-start.20 = (bf16[64,1024]{1,0:T(8,128)(2,1)S(1)}, bf16[64,1024]{1,0:T(8,128)(2,1)S(1)}, u32[]{:S(2)}, u32[]{:S(2)}) collective-permute-start(bf16[64,1024]{1,0:T(8,128)(2,1)S(1)} %get-tuple-element.59), channel_id=1, source_target_pairs={{0,6},{1,7},{2,4},{3,5},{4,2},{5,3},{6,0},{7,1},{8,14},{9,15},{10,... | collective-permute-start | bytes 393224 | tf_op jit(solution)/shard_map/ppermute | solution.py:361
  47.3 0.7 %collective-permute-start.15 = (bf16[64,1024]{1,0:T(8,128)(2,1)S(1)}, bf16[64,1024]{1,0:T(8,128)(2,1)S(1)}, u32[]{:S(2)}, u32[]{:S(2)}) collective-permute-start(bf16[64,1024]{1,0:T(8,128)(2,1)S(1)} %get-tuple-element.48), channel_id=1, source_target_pairs={{0,2},{1,3},{2,0},{3,1},{4,6},{5,7},{6,4},{7,5},{8,10},{9,11},{10,... | collective-permute-start | bytes 393224 | tf_op jit(solution)/shard_map/ppermute | solution.py:361
  48.0 0.9 %collective-permute-done.18.refs_0_ = bf16[64,1024]{1,0:T(8,128)(2,1)S(1)} collective-permute-done((bf16[64,1024]{1,0:T(8,128)(2,1)S(1)}, bf16[64,1024]{1,0:T(8,128)(2,1)S(1)}, u32[]{:S(2)}, u32[]{:S(2)}) %collective-permute-start.18) | collective-permute-done | bytes 131104 | tf_op jit(solution)/shard_map/ppermute | solution.py:361
  48.9 1.3 %collective-permute-start.16 = (bf16[64,1024]{1,0:T(8,128)(2,1)S(1)}, bf16[64,1024]{1,0:T(8,128)(2,1)S(1)}, u32[]{:S(2)}, u32[]{:S(2)}) collective-permute-start(bf16[64,1024]{1,0:T(8,128)(2,1)S(1)} %get-tuple-element.49), channel_id=1, source_target_pairs={{0,6},{1,7},{2,4},{3,5},{4,2},{5,3},{6,0},{7,1},{8,14},{9,15},{10,... | collective-permute-start | bytes 393224 | tf_op jit(solution)/shard_map/ppermute | solution.py:361
  50.2 1.8 %shard_map.96 = (bf16[4096,512]{1,0:T(8,128)(2,1)}, f32[8,128]{1,0:T(8,128)S(1)}) custom-call(f32[64,1024]{1,0:T(8,128)S(1)} %get-tuple-element.44.after.kept, bf16[256,512]{1,0:T(8,128)(2,1)S(1)} %get-tuple-element.45.logit_grad, bf16[128,1024]{1,0:T(8,128)(2,1)S(1)} %get-tuple-element.39.refs_0_, bf16[128,1024]{1,0:T(8,128)(2,1)S(1)} %shard_map.89.refs_1_, ...), custom_call_target="tpu_custom_call" | custom-call | flops 536870912 | bytes 5771264 | tf_op jit(solution)/shard_map/pallas_call | solution.py:33
  52.1 1.9 %collective-permute-done.20.refs_2_ = bf16[64,1024]{1,0:T(8,128)(2,1)S(1)} collective-permute-done((bf16[64,1024]{1,0:T(8,128)(2,1)S(1)}, bf16[64,1024]{1,0:T(8,128)(2,1)S(1)}, u32[]{:S(2)}, u32[]{:S(2)}) %collective-permute-start.20) | collective-permute-done | bytes 131104 | tf_op jit(solution)/shard_map/ppermute | solution.py:361
  54.0 0.9 %collective-permute-start.21 = (bf16[32,1024]{1,0:T(8,128)(2,1)S(1)}, bf16[32,1024]{1,0:T(8,128)(2,1)S(1)}, u32[]{:S(2)}, u32[]{:S(2)}) collective-permute-start(bf16[32,1024]{1,0:T(8,128)(2,1)S(1)} %get-tuple-element.60), channel_id=1, source_target_pairs={{0,16},{1,17},{2,18},{3,19},{4,20},{5,21},{6,22},{7,23},{8,24},{9,... | collective-permute-start | bytes 196616 | tf_op jit(solution)/shard_map/ppermute | solution.py:361
  54.9 2.3 %collective-permute-start.22 = (bf16[32,1024]{1,0:T(8,128)(2,1)S(1)}, bf16[32,1024]{1,0:T(8,128)(2,1)S(1)}, u32[]{:S(2)}, u32[]{:S(2)}) collective-permute-start(bf16[32,1024]{1,0:T(8,128)(2,1)S(1)} %get-tuple-element.61), channel_id=1, source_target_pairs={{0,24},{1,25},{2,26},{3,27},{4,28},{5,29},{6,30},{7,31},{8,16},{9,... | collective-permute-start | bytes 196616 | tf_op jit(solution)/shard_map/ppermute | solution.py:361
  57.2 1.2 %collective-permute-done.16.refs_2_ = bf16[64,1024]{1,0:T(8,128)(2,1)S(1)} collective-permute-done((bf16[64,1024]{1,0:T(8,128)(2,1)S(1)}, bf16[64,1024]{1,0:T(8,128)(2,1)S(1)}, u32[]{:S(2)}, u32[]{:S(2)}) %collective-permute-start.16) | collective-permute-done | bytes 131104 | tf_op jit(solution)/shard_map/ppermute | solution.py:361
  58.6 1.8 %shard_map.98 = (bf16[4096,512]{1,0:T(8,128)(2,1)}, f32[8,128]{1,0:T(8,128)S(1)}) custom-call(f32[32,1024]{1,0:T(8,128)S(1)} %get-tuple-element.50.after.refs_0_, bf16[256,512]{1,0:T(8,128)(2,1)S(1)} %get-tuple-element.45.logit_grad, bf16[4096,512]{1,0:T(8,128)(2,1)} %get-tuple-element.51.refs_0_, ...), custom_call_target="tpu_custom_call", output_to_operand_aliasing={{0}: (2, {})} | custom-call | flops 536870912 | bytes 10145792 | tf_op jit(solution)/shard_map/pallas_call | solution.py:33
  60.4 0.6 collective-permute-done.22.refs_3_
  61.0 1.8 %collective-permute-done.17.refs_1_ = bf16[32,1024]{1,0:T(8,128)(2,1)S(1)} collective-permute-done((bf16[32,1024]{1,0:T(8,128)(2,1)S(1)}, bf16[32,1024]{1,0:T(8,128)(2,1)S(1)}, u32[]{:S(2)}, u32[]{:S(2)}) %collective-permute-start.17) | collective-permute-done | bytes 65568 | tf_op jit(solution)/shard_map/ppermute | solution.py:361
  62.8 1.0 %shard_map.100 = (bf16[128,1024]{1,0:T(8,128)(2,1)}, f32[1,1]{1,0:T(1,128)}) custom-call(f32[8,128]{1,0:T(8,128)S(1)} %get-tuple-element.53.last, bf16[32,128]{1,0:T(8,128)(2,1)S(1)} %get-tuple-element.54.chosen, f32[32,1024]{1,0:T(8,128)S(1)} %get-tuple-element.50.after.refs_0_, bf16[32,1024]{1,0:T(8,128)(2,1)S(1)} %collective-permute-done.17.refs_1_, ...), custom_call_target="tpu_custom_call" | custom-call | bytes 602116 | tf_op jit(solution)/shard_map/pallas_call | solution.py:33
  (33 shorter events, 3.3 us)
Async XLA Ops:
  0.6 21.2 %copy-start = (f32[32]{0:T(128)S(1)}, f32[32]{0:T(128)}, u32[]{:S(2)}) copy-start(f32[32]{0:T(128)} %param.11) | copy-start | bytes 388
  1.9 10.8 %collective-permute-start = (bf16[272,128]{1,0:T(8,128)(2,1)S(1)}, bf16[272,128]{1,0:T(8,128)(2,1)S(1)}, u32[]{:S(2)}, u32[]{:S(2)}) collective-permute-start(bf16[272,128]{1,0:T(8,128)(2,1)S(1)} %get-tuple-element.34.refs_0_), channel_id=1, source_target_pairs={{0,16},{1,17},{2,18},{3,19},{4,20},{5,21},{6,22},{7,23},{8,24},{9,... | collective-permute-start | bytes 208904 | tf_op jit(solution)/shard_map/ppermute | solution.py:361
  6.0 6.8 %collective-permute-start.1 = (bf16[272,128]{1,0:T(8,128)(2,1)S(1)}, bf16[272,128]{1,0:T(8,128)(2,1)S(1)}, u32[]{:S(2)}, u32[]{:S(2)}) collective-permute-start(bf16[272,128]{1,0:T(8,128)(2,1)S(1)} %get-tuple-element.34.refs_0_), channel_id=1, source_target_pairs={{0,24},{1,25},{2,26},{3,27},{4,28},{5,29},{6,30},{7,31},{8,16},{9,... | collective-permute-start | bytes 208904 | tf_op jit(solution)/shard_map/ppermute | solution.py:361
  7.3 5.4 %collective-permute-start.3 = (bf16[272,128]{1,0:T(8,128)(2,1)S(1)}, bf16[272,128]{1,0:T(8,128)(2,1)S(1)}, u32[]{:S(2)}, u32[]{:S(2)}) collective-permute-start(bf16[272,128]{1,0:T(8,128)(2,1)S(1)} %get-tuple-element.34.refs_0_), channel_id=1, source_target_pairs={{0,8},{1,9},{2,10},{3,11},{4,12},{5,13},{6,14},{7,15},{8,0},{9,1},... | collective-permute-start | bytes 208904 | tf_op jit(solution)/shard_map/ppermute | solution.py:361
  7.5 5.2 %collective-permute-start.2 = (bf16[32,1024]{1,0:T(8,128)(2,1)S(1)}, bf16[32,1024]{1,0:T(8,128)(2,1)S(1)}, u32[]{:S(2)}, u32[]{:S(2)}) collective-permute-start(bf16[32,1024]{1,0:T(8,128)(2,1)S(1)} %get-tuple-element.35), channel_id=1, source_target_pairs={{0,6},{1,7},{2,4},{3,5},{4,2},{5,3},{6,0},{7,1},{8,14},{9,15},{10,... | collective-permute-start | bytes 196616 | tf_op jit(solution)/shard_map/ppermute | solution.py:361
  12.8 9.0 %collective-permute-start.4 = (bf16[1088,128]{1,0:T(8,128)(2,1)S(1)}, bf16[1088,128]{1,0:T(8,128)(2,1)S(1)}, u32[]{:S(2)}, u32[]{:S(2)}) collective-permute-start(bf16[1088,128]{1,0:T(8,128)(2,1)S(1)} %get-tuple-element.36.own), channel_id=1, source_target_pairs={{0,4},{1,5},{2,6},{3,7},{4,0},{5,1},{6,2},{7,3},{8,12},{9,13},{10,... | collective-permute-start | bytes 835592 | tf_op jit(solution)/shard_map/ppermute | solution.py:361
  14.4 8.5 %collective-permute-start.5 = (bf16[128,1024]{1,0:T(8,128)(2,1)S(1)}, bf16[128,1024]{1,0:T(8,128)(2,1)S(1)}, u32[]{:S(2)}, u32[]{:S(2)}) collective-permute-start(bf16[128,1024]{1,0:T(8,128)(2,1)S(1)} %get-tuple-element.37.line), channel_id=1, source_target_pairs={{0,2},{1,3},{2,0},{3,1},{4,6},{5,7},{6,4},{7,5},{8,10},{9,11},{10,... | collective-permute-start | bytes 786440 | tf_op jit(solution)/shard_map/ppermute | solution.py:361
  15.9 8.9 %collective-permute-start.6 = (bf16[96,1024]{1,0:T(8,128)(2,1)S(1)}, bf16[96,1024]{1,0:T(8,128)(2,1)S(1)}, u32[]{:S(2)}, u32[]{:S(2)}) collective-permute-start(bf16[96,1024]{1,0:T(8,128)(2,1)S(1)} %get-tuple-element.40), channel_id=1, source_target_pairs={{0,6},{1,7},{2,4},{3,5},{4,2},{5,3},{6,0},{7,1},{8,14},{9,15},{10,... | collective-permute-start | bytes 589832 | tf_op jit(solution)/shard_map/ppermute | solution.py:361
  16.4 7.2 %collective-permute-start.7 = (bf16[32,1024]{1,0:T(8,128)(2,1)S(1)}, bf16[32,1024]{1,0:T(8,128)(2,1)S(1)}, u32[]{:S(2)}, u32[]{:S(2)}) collective-permute-start(bf16[32,1024]{1,0:T(8,128)(2,1)S(1)} %collective-permute-done.2.refs_3_.refs_5_), channel_id=1, source_target_pairs={{0,1},{1,0},{2,3},{3,2},{4,5},{5,4},{6,7},{7,6},{8,9},{9,8},{10,11... | collective-permute-start | bytes 196616 | tf_op jit(solution)/shard_map/ppermute | solution.py:361
  19.3 6.3 %collective-permute-start.8 = (bf16[128,1024]{1,0:T(8,128)(2,1)S(1)}, bf16[128,1024]{1,0:T(8,128)(2,1)S(1)}, u32[]{:S(2)}, u32[]{:S(2)}) collective-permute-start(bf16[128,1024]{1,0:T(8,128)(2,1)S(1)} %get-tuple-element.39.refs_0_), channel_id=1, source_target_pairs={{0,1},{1,0},{2,3},{3,2},{4,5},{5,4},{6,7},{7,6},{8,9},{9,8},{10,11... | collective-permute-start | bytes 786440 | tf_op jit(solution)/shard_map/ppermute | solution.py:361
  22.9 3.3 %collective-permute-start.10 = (bf16[128,1024]{1,0:T(8,128)(2,1)S(1)}, bf16[128,1024]{1,0:T(8,128)(2,1)S(1)}, u32[]{:S(2)}, u32[]{:S(2)}) collective-permute-start(bf16[128,1024]{1,0:T(8,128)(2,1)S(1)} %shard_map.90.refs_2_.refs_4_), channel_id=1, source_target_pairs={{0,1},{1,0},{2,3},{3,2},{4,5},{5,4},{6,7},{7,6},{8,9},{9,8},{10,11... | collective-permute-start | bytes 786440 | tf_op jit(solution)/shard_map/ppermute | solution.py:361
  23.0 3.3 %collective-permute-start.9 = (bf16[128,1024]{1,0:T(8,128)(2,1)S(1)}, bf16[128,1024]{1,0:T(8,128)(2,1)S(1)}, u32[]{:S(2)}, u32[]{:S(2)}) collective-permute-start(bf16[128,1024]{1,0:T(8,128)(2,1)S(1)} %shard_map.89.refs_1_), channel_id=1, source_target_pairs={{0,1},{1,0},{2,3},{3,2},{4,5},{5,4},{6,7},{7,6},{8,9},{9,8},{10,11... | collective-permute-start | bytes 786440 | tf_op jit(solution)/shard_map/ppermute | solution.py:361
  24.8 1.4 %collective-permute-start.11 = (bf16[96,1024]{1,0:T(8,128)(2,1)S(1)}, bf16[96,1024]{1,0:T(8,128)(2,1)S(1)}, u32[]{:S(2)}, u32[]{:S(2)}) collective-permute-start(bf16[96,1024]{1,0:T(8,128)(2,1)S(1)} %shard_map.91.refs_4_.refs_6_), channel_id=1, source_target_pairs={{0,1},{1,0},{2,3},{3,2},{4,5},{5,4},{6,7},{7,6},{8,9},{9,8},{10,11... | collective-permute-start | bytes 589832 | tf_op jit(solution)/shard_map/ppermute | solution.py:361
  27.4 14.0 %collective-permute-start.13 = (bf16[2048,512]{1,0:T(8,128)(2,1)S(1)}, bf16[2048,512]{1,0:T(8,128)(2,1)S(1)}, u32[]{:S(2)}, u32[]{:S(2)}) collective-permute-start(bf16[2048,512]{1,0:T(8,128)(2,1)S(1)} %shard_map.94), channel_id=1, source_target_pairs={{0,1},{1,0},{2,3},{3,2},{4,5},{5,4},{6,7},{7,6},{8,9},{9,8},{10,11... | collective-permute-start | bytes 6291464 | tf_op jit(solution)/shard_map/ppermute | solution.py:361
  27.6 13.8 %collective-permute-start.12 = (f32[256,512]{1,0:T(8,128)S(1)}, f32[256,512]{1,0:T(8,128)S(1)}, u32[]{:S(2)}, u32[]{:S(2)}) collective-permute-start(f32[256,512]{1,0:T(8,128)S(1)} %get-tuple-element.41.mine), channel_id=1, source_target_pairs={{0,1},{1,0},{2,3},{3,2},{4,5},{5,4},{6,7},{7,6},{8,9},{9,8},{10,11... | collective-permute-start | bytes 1572872 | tf_op jit(solution)/shard_map/ppermute | solution.py:361
  43.2 5.7 %collective-permute-start.18 = (bf16[64,1024]{1,0:T(8,128)(2,1)S(1)}, bf16[64,1024]{1,0:T(8,128)(2,1)S(1)}, u32[]{:S(2)}, u32[]{:S(2)}) collective-permute-start(bf16[64,1024]{1,0:T(8,128)(2,1)S(1)} %get-tuple-element.57), channel_id=1, source_target_pairs={{0,4},{1,5},{2,6},{3,7},{4,0},{5,1},{6,2},{7,3},{8,12},{9,13},{10,... | collective-permute-start | bytes 393224 | tf_op jit(solution)/shard_map/ppermute | solution.py:361
  43.8 8.2 %collective-permute-start.19 = (bf16[64,1024]{1,0:T(8,128)(2,1)S(1)}, bf16[64,1024]{1,0:T(8,128)(2,1)S(1)}, u32[]{:S(2)}, u32[]{:S(2)}) collective-permute-start(bf16[64,1024]{1,0:T(8,128)(2,1)S(1)} %get-tuple-element.58), channel_id=1, source_target_pairs={{0,2},{1,3},{2,0},{3,1},{4,6},{5,7},{6,4},{7,5},{8,10},{9,11},{10,... | collective-permute-start | bytes 393224 | tf_op jit(solution)/shard_map/ppermute | solution.py:361
  44.5 9.4 %collective-permute-start.20 = (bf16[64,1024]{1,0:T(8,128)(2,1)S(1)}, bf16[64,1024]{1,0:T(8,128)(2,1)S(1)}, u32[]{:S(2)}, u32[]{:S(2)}) collective-permute-start(bf16[64,1024]{1,0:T(8,128)(2,1)S(1)} %get-tuple-element.59), channel_id=1, source_target_pairs={{0,6},{1,7},{2,4},{3,5},{4,2},{5,3},{6,0},{7,1},{8,14},{9,15},{10,... | collective-permute-start | bytes 393224 | tf_op jit(solution)/shard_map/ppermute | solution.py:361
  46.8 10.4 %collective-permute-start.14 = (bf16[64,1024]{1,0:T(8,128)(2,1)S(1)}, bf16[64,1024]{1,0:T(8,128)(2,1)S(1)}, u32[]{:S(2)}, u32[]{:S(2)}) collective-permute-start(bf16[64,1024]{1,0:T(8,128)(2,1)S(1)} %get-tuple-element.47), channel_id=1, source_target_pairs={{0,4},{1,5},{2,6},{3,7},{4,0},{5,1},{6,2},{7,3},{8,12},{9,13},{10,... | collective-permute-start | bytes 393224 | tf_op jit(solution)/shard_map/ppermute | solution.py:361
  47.3 9.8 %collective-permute-start.15 = (bf16[64,1024]{1,0:T(8,128)(2,1)S(1)}, bf16[64,1024]{1,0:T(8,128)(2,1)S(1)}, u32[]{:S(2)}, u32[]{:S(2)}) collective-permute-start(bf16[64,1024]{1,0:T(8,128)(2,1)S(1)} %get-tuple-element.48), channel_id=1, source_target_pairs={{0,2},{1,3},{2,0},{3,1},{4,6},{5,7},{6,4},{7,5},{8,10},{9,11},{10,... | collective-permute-start | bytes 393224 | tf_op jit(solution)/shard_map/ppermute | solution.py:361
  48.9 9.5 %collective-permute-start.16 = (bf16[64,1024]{1,0:T(8,128)(2,1)S(1)}, bf16[64,1024]{1,0:T(8,128)(2,1)S(1)}, u32[]{:S(2)}, u32[]{:S(2)}) collective-permute-start(bf16[64,1024]{1,0:T(8,128)(2,1)S(1)} %get-tuple-element.49), channel_id=1, source_target_pairs={{0,6},{1,7},{2,4},{3,5},{4,2},{5,3},{6,0},{7,1},{8,14},{9,15},{10,... | collective-permute-start | bytes 393224 | tf_op jit(solution)/shard_map/ppermute | solution.py:361
  54.0 6.4 %collective-permute-start.21 = (bf16[32,1024]{1,0:T(8,128)(2,1)S(1)}, bf16[32,1024]{1,0:T(8,128)(2,1)S(1)}, u32[]{:S(2)}, u32[]{:S(2)}) collective-permute-start(bf16[32,1024]{1,0:T(8,128)(2,1)S(1)} %get-tuple-element.60), channel_id=1, source_target_pairs={{0,16},{1,17},{2,18},{3,19},{4,20},{5,21},{6,22},{7,23},{8,24},{9,... | collective-permute-start | bytes 196616 | tf_op jit(solution)/shard_map/ppermute | solution.py:361
  54.9 6.2 %collective-permute-start.22 = (bf16[32,1024]{1,0:T(8,128)(2,1)S(1)}, bf16[32,1024]{1,0:T(8,128)(2,1)S(1)}, u32[]{:S(2)}, u32[]{:S(2)}) collective-permute-start(bf16[32,1024]{1,0:T(8,128)(2,1)S(1)} %get-tuple-element.61), channel_id=1, source_target_pairs={{0,24},{1,25},{2,26},{3,27},{4,28},{5,29},{6,30},{7,31},{8,16},{9,... | collective-permute-start | bytes 196616 | tf_op jit(solution)/shard_map/ppermute | solution.py:361
  58.5 4.3 %collective-permute-start.17 = (bf16[32,1024]{1,0:T(8,128)(2,1)S(1)}, bf16[32,1024]{1,0:T(8,128)(2,1)S(1)}, u32[]{:S(2)}, u32[]{:S(2)}) collective-permute-start(bf16[32,1024]{1,0:T(8,128)(2,1)S(1)} %get-tuple-element.55), channel_id=1, source_target_pairs={{0,8},{1,9},{2,10},{3,11},{4,12},{5,13},{6,14},{7,15},{8,0},{9,1},... | collective-permute-start | bytes 196616 | tf_op jit(solution)/shard_map/ppermute | solution.py:361

commit v19 on v17

--- a/solution.py
+++ b/solution.py
@@ -138,7 +138,7 @@
         copy.wait()
 
 
-def gate_kernel(value, after, same):
+def gate_kernel(*refs):
     pass
 
 
@@ -442,13 +442,6 @@
         (VMEM,) * (2 + 2 * ranks),
         flops=flops,
     )
-    ends, sums = [None] * zs, [None, None]
-    for chunk in (1, 0):
-        *values, corner = going[(1 - chunk) * ranks:(2 - chunk) * ranks]
-        sums[chunk] = [corner]
-        for place, value in zip(order, values):
-            sums[chunk].append(send(value, y=place % 2, x=place // 2))
-
     def weight_part(first, after, *extra):
         blocks = range(first, first + ranks // 2)
         chosen_rows = rows_of(blocks)
@@ -467,12 +460,27 @@
             aliases={2: 0} if extra else {},
         )
 
-    weight_grad, finished = weight_part(0, sums[0][0])
+    far_values, near_values = list(going[:ranks]), list(going[ranks:])
+    weight_grad, finished = weight_part(0, far_values[-1])
+    near_values[:-1] = call(
+        gate_kernel,
+        (*near_values[:-1], finished),
+        [ANY] * ranks,
+        outs[:-1],
+        (ANY,) * (ranks - 1),
+        aliases={place: place for place in range(ranks - 1)},
+    )
+    ends, sums = [None] * zs, [None, None]
+    for chunk, values in ((1, far_values), (0, near_values)):
+        sums[chunk] = [values[-1]]
+        for place, value in zip(order, values):
+            if place:
+                sums[chunk].append(send(value, y=place % 2, x=place // 2))
     for chunk in (1, 0):
         near = chunk * zs // 2
         parts_z = call(
             functools.partial(corner_kernel, ranks - 1),
-            (table if chunk else finished, *sums[chunk]),
+            (table, *sums[chunk]),
             [ANY] + [VMEM] * ranks,
             tuple(shape((CAP, width), bf16 if near + z else f32) for z in range(zs // 2)),
             (VMEM,) * (zs // 2),

time: 64.3 us -> 64.3 us (level)
    pallas_call x15 -> x16, Pallas kernels: 12.8 us -> 12.8 us  [call(): pl.pallas_call(kernel, out_shape=out_shape, in_specs=in_specs, out_specs=...]
  transfers between devices with their start and end apart: 23 -> 23, of which waited for: 10 -> 9; matrix products, arithmetic and copies ran while one was open for 0% -> 0% of each run, Pallas kernels for 12% -> 12%
where the time goes in v19:
time: 64.3 us; the launch traced here: 64.1 us
  starting transfers between devices  22.6 us (35%)
  waiting for transfers between devices  14.2 us (22%)
  blocking collectives  13.6 us (21%)
  Pallas kernels  12.8 us (20%)
  between operations  0.81 us (1%)
    ppermute x23, starting transfers between devices, send(): return lax.ppermute(value, AXES, pairs)  22.6 us
    ppermute x23, waiting for transfers between devices, send(): return lax.ppermute(value, AXES, pairs)  14.2 us
    all_to_all x1, blocking collectives, body(): stats = lax.all_to_all(stats, AXES, 0, 0)  13.6 us
    pallas_call x16, Pallas kernels, call(): pl.pallas_call(kernel, out_shape=out_shape, in_specs=in_specs, out_specs=...  12.8 us
  transfers between devices with their start and end apart: 23, of which 9 were waited for; matrix products, arithmetic and copies ran while one was open for 0% of the time, Pallas kernels for 12%

profile of v19, /device:TPU:0, one launch (start us, length us, event | category | flops | bytes accessed | tf_op | source)
XLA Modules:
  0.0 64.1 jit_solution(4179911067705647437)
XLA Ops:
  0.6 1.2 %shard_map.85 = (bf16[32,1152]{1,0:T(8,128)(2,1)S(1)}, bf16[32,1024]{1,0:T(8,128)(2,1)S(1)}, bf16[32,128]{1,0:T(8,128)(2,1)S(1)}) custom-call(bf16[128,1024]{1,0:T(8,128)(2,1)} %hidden_hbm.1, s32[1,128]{1,0:T(1,128)} %bitcast.6, s32[1,128]{1,0:T(1,128)} %bitcast.7, s32[1,128]{1,0:T(1,128)} %bitcast.8), custom_call_target="tpu_custom_call" | custom-call | bytes 411136 | tf_op jit(solution)/shard_map/pallas_call | solution.py:33
  1.9 4.1 %collective-permute-start = (bf16[32,1152]{1,0:T(8,128)(2,1)S(1)}, bf16[32,1152]{1,0:T(8,128)(2,1)S(1)}, u32[]{:S(2)}, u32[]{:S(2)}) collective-permute-start(bf16[32,1152]{1,0:T(8,128)(2,1)S(1)} %get-tuple-element.37.refs_0_), channel_id=1, source_target_pairs={{0,16},{1,17},{2,18},{3,19},{4,20},{5,21},{6,22},{7,23},{8,24},{9,... | collective-permute-start | bytes 221192 | tf_op jit(solution)/shard_map/ppermute | solution.py:327
  6.0 1.3 %collective-permute-start.1 = (bf16[32,1152]{1,0:T(8,128)(2,1)S(1)}, bf16[32,1152]{1,0:T(8,128)(2,1)S(1)}, u32[]{:S(2)}, u32[]{:S(2)}) collective-permute-start(bf16[32,1152]{1,0:T(8,128)(2,1)S(1)} %get-tuple-element.37.refs_0_), channel_id=1, source_target_pairs={{0,24},{1,25},{2,26},{3,27},{4,28},{5,29},{6,30},{7,31},{8,16},{9,... | collective-permute-start | bytes 221192 | tf_op jit(solution)/shard_map/ppermute | solution.py:327
  7.5 2.4 %collective-permute-start.2 = (bf16[32,1024]{1,0:T(8,128)(2,1)S(1)}, bf16[32,1024]{1,0:T(8,128)(2,1)S(1)}, u32[]{:S(2)}, u32[]{:S(2)}) collective-permute-start(bf16[32,1024]{1,0:T(8,128)(2,1)S(1)} %get-tuple-element.38), channel_id=1, source_target_pairs={{0,6},{1,7},{2,4},{3,5},{4,2},{5,3},{6,0},{7,1},{8,14},{9,15},{10,... | collective-permute-start | bytes 196616 | tf_op jit(solution)/shard_map/ppermute | solution.py:327
  10.0 2.7 %collective-permute-done.2.refs_3_.refs_5_ = bf16[32,1024]{1,0:T(8,128)(2,1)S(1)} collective-permute-done((bf16[32,1024]{1,0:T(8,128)(2,1)S(1)}, bf16[32,1024]{1,0:T(8,128)(2,1)S(1)}, u32[]{:S(2)}, u32[]{:S(2)}) %collective-permute-start.2) | collective-permute-done | bytes 65568 | tf_op jit(solution)/shard_map/ppermute | solution.py:327
  12.8 1.7 %collective-permute-start.4 = (bf16[128,1152]{1,0:T(8,128)(2,1)S(1)}, bf16[128,1152]{1,0:T(8,128)(2,1)S(1)}, u32[]{:S(2)}, u32[]{:S(2)}) collective-permute-start(bf16[128,1152]{1,0:T(8,128)(2,1)S(1)} %get-tuple-element.39.line), channel_id=1, source_target_pairs={{0,4},{1,5},{2,6},{3,7},{4,0},{5,1},{6,2},{7,3},{8,12},{9,13},{10,... | collective-permute-start | bytes 884744 | tf_op jit(solution)/shard_map/ppermute | solution.py:327
  14.5 1.5 %collective-permute-start.5 = (bf16[128,1024]{1,0:T(8,128)(2,1)S(1)}, bf16[128,1024]{1,0:T(8,128)(2,1)S(1)}, u32[]{:S(2)}, u32[]{:S(2)}) collective-permute-start(bf16[128,1024]{1,0:T(8,128)(2,1)S(1)} %get-tuple-element.42), channel_id=1, source_target_pairs={{0,2},{1,3},{2,0},{3,1},{4,6},{5,7},{6,4},{7,5},{8,10},{9,11},{10,... | collective-permute-start | bytes 786440 | tf_op jit(solution)/shard_map/ppermute | solution.py:327
  15.9 0.4 collective-permute-start.6
  16.3 2.9 %shard_map.87 = (bf16[4096,512]{1,0:T(8,128)(2,1)S(1)}, bf16[2048,512]{1,0:T(8,128)(2,1)S(1)}, bf16[128,1152]{1,0:T(8,128)(2,1)S(1)}) custom-call(bf16[128,1152]{1,0:T(8,128)(2,1)S(1)} %get-tuple-element.39.line, bf16[4096,512]{1,0:T(8,128)(2,1)} %weight.1), custom_call_target="tpu_custom_call" | custom-call | bytes 11075584 | tf_op jit(solution)/shard_map/pallas_call | solution.py:33
  19.3 3.1 %collective-permute-done.4.refs_1_ = bf16[128,1152]{1,0:T(8,128)(2,1)S(1)} collective-permute-done((bf16[128,1152]{1,0:T(8,128)(2,1)S(1)}, bf16[128,1152]{1,0:T(8,128)(2,1)S(1)}, u32[]{:S(2)}, u32[]{:S(2)}) %collective-permute-start.4) | collective-permute-done | bytes 294944 | tf_op jit(solution)/shard_map/ppermute | solution.py:327
  22.4 0.5 collective-permute-start.7
  22.9 0.4 shard_map.88.refs_1_.info
  23.4 0.7 %collective-permute-done.7.refs_1_.refs_3_.refs_8_ = bf16[32,1024]{1,0:T(8,128)(2,1)S(1)} collective-permute-done((bf16[32,1024]{1,0:T(8,128)(2,1)S(1)}, bf16[32,1024]{1,0:T(8,128)(2,1)S(1)}, u32[]{:S(2)}, u32[]{:S(2)}) %collective-permute-start.7) | collective-permute-done | bytes 65568 | tf_op jit(solution)/shard_map/ppermute | solution.py:327
  24.0 0.9 %collective-permute-done.6.refs_0_ = bf16[96,1024]{1,0:T(8,128)(2,1)S(1)} collective-permute-done((bf16[96,1024]{1,0:T(8,128)(2,1)S(1)}, bf16[96,1024]{1,0:T(8,128)(2,1)S(1)}, u32[]{:S(2)}, u32[]{:S(2)}) %collective-permute-start.6) | collective-permute-done | bytes 196640 | tf_op jit(solution)/shard_map/ppermute | solution.py:327
  24.9 0.7 %shard_map.91.partial = f32[256,512]{1,0:T(8,128)S(1)} custom-call(bf16[4096,512]{1,0:T(8,128)(2,1)S(1)} %get-tuple-element.41.weight, bf16[128,1152]{1,0:T(8,128)(2,1)S(1)} %get-tuple-element.40.refs_0_, bf16[128,1152]{1,0:T(8,128)(2,1)S(1)} %collective-permute-done.4.refs_1_, bf16[128,1024]{1,0:T(8,128)(2,1)S(1)} %shard_map.89.refs_2_.refs_4_, ...), custom_call_target="tpu_custom_call" | custom-call | flops 536870912 | bytes 5832704 | tf_op jit(solution)/shard_map/pallas_call | solution.py:33
  25.7 0.7 %collective-permute-done.11.refs_4_.refs_9_ = bf16[96,1024]{1,0:T(8,128)(2,1)S(1)} collective-permute-done((bf16[96,1024]{1,0:T(8,128)(2,1)S(1)}, bf16[96,1024]{1,0:T(8,128)(2,1)S(1)}, u32[]{:S(2)}, u32[]{:S(2)}) %collective-permute-start.11) | collective-permute-done | bytes 196640 | tf_op jit(solution)/shard_map/ppermute | solution.py:327
  26.4 1.1 %shard_map.92 = (f32[256,512]{1,0:T(8,128)S(1)}, f32[32,1,384]{2,1,0:T(1,128)S(1)}) custom-call(f32[256,128]{1,0:T(8,128)S(1)} %shard_map.88.refs_1_.info, f32[256,512]{1,0:T(8,128)S(1)} %shard_map.91.partial, bf16[4096,512]{1,0:T(8,128)(2,1)S(1)} %get-tuple-element.41.weight, bf16[128,1152]{1,0:T(8,128)(2,1)S(1)} %collective-permute-done.8.refs_0_.refs_2_, ...), custom_call_target="tpu_custom_call" | custom-call | flops 536870912 | bytes 6537216 | tf_op jit(solution)/shard_map/pallas_call | solution.py:33
  28.1 13.6 %all_to_all.5.stats.refs_3_ = f32[32,1,384]{2,1,0:T(1,128)S(1)} all-to-all(f32[32,1,384]{2,1,0:T(1,128)S(1)} %get-tuple-element.46.refs_1_), channel_id=1, replica_groups=mesh['dp'=8,'vocab'=4] {'dp','vocab'}, dimensions={0} | all-to-all | bytes 98304 | tf_op jit(solution)/shard_map/all_to_all | solution.py:433
  41.8 1.8 %shard_map.94 = (bf16[256,512]{1,0:T(8,128)(2,1)S(1)}, f32[256,128]{1,0:T(8,128)S(1)}, bf16[64,1024]{1,0:T(8,128)(2,1)S(1)}, bf16[64,1024]{1,0:T(8,128)(2,1)S(1)...) custom-call(f32[256,128]{1,0:T(8,128)S(1)} %shard_map.88.refs_1_.inf, ...), custom_call_target="tpu_custom_call" | custom-call | flops 1073741824 | bytes 9224192 | tf_op jit(solution)/shard_map/pallas_call | solution.py:33
  43.6 0.6 %collective-permute-start.18 = (bf16[64,1024]{1,0:T(8,128)(2,1)S(1)}, bf16[64,1024]{1,0:T(8,128)(2,1)S(1)}, u32[]{:S(2)}, u32[]{:S(2)}) collective-permute-start(bf16[64,1024]{1,0:T(8,128)(2,1)S(1)} %get-tuple-element.63), channel_id=1, source_target_pairs={{0,4},{1,5},{2,6},{3,7},{4,0},{5,1},{6,2},{7,3},{8,12},{9,13},{10,... | collective-permute-start | bytes 393224 | tf_op jit(solution)/shard_map/ppermute | solution.py:327
  44.2 0.7 %collective-permute-start.19 = (bf16[64,1024]{1,0:T(8,128)(2,1)S(1)}, bf16[64,1024]{1,0:T(8,128)(2,1)S(1)}, u32[]{:S(2)}, u32[]{:S(2)}) collective-permute-start(bf16[64,1024]{1,0:T(8,128)(2,1)S(1)} %get-tuple-element.64), channel_id=1, source_target_pairs={{0,2},{1,3},{2,0},{3,1},{4,6},{5,7},{6,4},{7,5},{8,10},{9,11},{10,... | collective-permute-start | bytes 393224 | tf_op jit(solution)/shard_map/ppermute | solution.py:327
  44.9 2.2 %collective-permute-start.20 = (bf16[64,1024]{1,0:T(8,128)(2,1)S(1)}, bf16[64,1024]{1,0:T(8,128)(2,1)S(1)}, u32[]{:S(2)}, u32[]{:S(2)}) collective-permute-start(bf16[64,1024]{1,0:T(8,128)(2,1)S(1)} %get-tuple-element.65), channel_id=1, source_target_pairs={{0,6},{1,7},{2,4},{3,5},{4,2},{5,3},{6,0},{7,1},{8,14},{9,15},{10,... | collective-permute-start | bytes 393224 | tf_op jit(solution)/shard_map/ppermute | solution.py:327
  47.1 1.8 %shard_map.95 = (bf16[4096,512]{1,0:T(8,128)(2,1)}, f32[8,128]{1,0:T(8,128)S(1)}) custom-call(f32[64,1024]{1,0:T(8,128)S(1)} %get-tuple-element.52.after.kept, bf16[256,512]{1,0:T(8,128)(2,1)S(1)} %get-tuple-element.53.logit_grad, bf16[128,1152]{1,0:T(8,128)(2,1)S(1)} %get-tuple-element.40.refs_0_, bf16[128,1152]{1,0:T(8,128)(2,1)S(1)} %collective-permute-done.4.refs_1_, ...), custom_call_target="tpu_custom_call" | custom-call | flops 536870912 | bytes 5902336 | tf_op jit(solution)/shard_map/pallas_call | solution.py:33
  48.9 0.6 %collective-permute-start.14 = (bf16[64,1024]{1,0:T(8,128)(2,1)S(1)}, bf16[64,1024]{1,0:T(8,128)(2,1)S(1)}, u32[]{:S(2)}, u32[]{:S(2)}) collective-permute-start(bf16[64,1024]{1,0:T(8,128)(2,1)S(1)} %get-tuple-element.55), channel_id=1, source_target_pairs={{0,4},{1,5},{2,6},{3,7},{4,0},{5,1},{6,2},{7,3},{8,12},{9,13},{10,... | collective-permute-start | bytes 393224 | tf_op jit(solution)/shard_map/ppermute | solution.py:327
  49.6 0.7 %collective-permute-start.15 = (bf16[64,1024]{1,0:T(8,128)(2,1)S(1)}, bf16[64,1024]{1,0:T(8,128)(2,1)S(1)}, u32[]{:S(2)}, u32[]{:S(2)}) collective-permute-start(bf16[64,1024]{1,0:T(8,128)(2,1)S(1)} %get-tuple-element.56), channel_id=1, source_target_pairs={{0,2},{1,3},{2,0},{3,1},{4,6},{5,7},{6,4},{7,5},{8,10},{9,11},{10,... | collective-permute-start | bytes 393224 | tf_op jit(solution)/shard_map/ppermute | solution.py:327
  50.2 2.2 %collective-permute-start.16 = (bf16[64,1024]{1,0:T(8,128)(2,1)S(1)}, bf16[64,1024]{1,0:T(8,128)(2,1)S(1)}, u32[]{:S(2)}, u32[]{:S(2)}) collective-permute-start(bf16[64,1024]{1,0:T(8,128)(2,1)S(1)} %get-tuple-element.57), channel_id=1, source_target_pairs={{0,6},{1,7},{2,4},{3,5},{4,2},{5,3},{6,0},{7,1},{8,14},{9,15},{10,... | collective-permute-start | bytes 393224 | tf_op jit(solution)/shard_map/ppermute | solution.py:327
  52.5 1.7 %collective-permute-done.20.refs_2_ = bf16[64,1024]{1,0:T(8,128)(2,1)S(1)} collective-permute-done((bf16[64,1024]{1,0:T(8,128)(2,1)S(1)}, bf16[64,1024]{1,0:T(8,128)(2,1)S(1)}, u32[]{:S(2)}, u32[]{:S(2)}) %collective-permute-start.20) | collective-permute-done | bytes 131104 | tf_op jit(solution)/shard_map/ppermute | solution.py:327
  54.4 2.3 %collective-permute-start.22 = (bf16[32,1024]{1,0:T(8,128)(2,1)S(1)}, bf16[32,1024]{1,0:T(8,128)(2,1)S(1)}, u32[]{:S(2)}, u32[]{:S(2)}) collective-permute-start(bf16[32,1024]{1,0:T(8,128)(2,1)S(1)} %get-tuple-element.67), channel_id=1, source_target_pairs={{0,24},{1,25},{2,26},{3,27},{4,28},{5,29},{6,30},{7,31},{8,16},{9,... | collective-permute-start | bytes 196616 | tf_op jit(solution)/shard_map/ppermute | solution.py:327
  56.7 2.0 %collective-permute-done.16.refs_2_ = bf16[64,1024]{1,0:T(8,128)(2,1)S(1)} collective-permute-done((bf16[64,1024]{1,0:T(8,128)(2,1)S(1)}, bf16[64,1024]{1,0:T(8,128)(2,1)S(1)}, u32[]{:S(2)}, u32[]{:S(2)}) %collective-permute-start.16) | collective-permute-done | bytes 131104 | tf_op jit(solution)/shard_map/ppermute | solution.py:327
  58.9 1.8 %shard_map.98 = (bf16[4096,512]{1,0:T(8,128)(2,1)}, f32[8,128]{1,0:T(8,128)S(1)}) custom-call(f32[32,1024]{1,0:T(8,128)S(1)} %get-tuple-element.58.after.refs_0_, bf16[256,512]{1,0:T(8,128)(2,1)S(1)} %get-tuple-element.53.logit_grad, bf16[4096,512]{1,0:T(8,128)(2,1)} %get-tuple-element.59.refs_0_, ...), custom_call_target="tpu_custom_call", output_to_operand_aliasing={{0}: (2, {})} | custom-call | flops 536870912 | bytes 10145792 | tf_op jit(solution)/shard_map/pallas_call | solution.py:33
  60.9 2.3 %collective-permute-done.17.refs_1_ = bf16[32,1024]{1,0:T(8,128)(2,1)S(1)} collective-permute-done((bf16[32,1024]{1,0:T(8,128)(2,1)S(1)}, bf16[32,1024]{1,0:T(8,128)(2,1)S(1)}, u32[]{:S(2)}, u32[]{:S(2)}) %collective-permute-start.17) | collective-permute-done | bytes 65568 | tf_op jit(solution)/shard_map/ppermute | solution.py:327
  63.1 1.0 %shard_map.100 = (bf16[128,1024]{1,0:T(8,128)(2,1)}, f32[1,1]{1,0:T(1,128)}) custom-call(f32[8,128]{1,0:T(8,128)S(1)} %get-tuple-element.60.last, bf16[32,128]{1,0:T(8,128)(2,1)S(1)} %get-tuple-element.61.chosen, f32[32,1024]{1,0:T(8,128)S(1)} %get-tuple-element.58.after.refs_0_, bf16[32,1024]{1,0:T(8,128)(2,1)S(1)} %collective-permute-done.17.refs_1_, ...), custom_call_target="tpu_custom_call" | custom-call | bytes 602116 | tf_op jit(solution)/shard_map/pallas_call | solution.py:33
  (33 shorter events, 1.6 us)
Async XLA Ops:
  0.6 22.2 %copy-start = (f32[32]{0:T(128)S(1)}, f32[32]{0:T(128)}, u32[]{:S(2)}) copy-start(f32[32]{0:T(128)} %param.11) | copy-start | bytes 388
  1.9 10.8 %collective-permute-start = (bf16[32,1152]{1,0:T(8,128)(2,1)S(1)}, bf16[32,1152]{1,0:T(8,128)(2,1)S(1)}, u32[]{:S(2)}, u32[]{:S(2)}) collective-permute-start(bf16[32,1152]{1,0:T(8,128)(2,1)S(1)} %get-tuple-element.37.refs_0_), channel_id=1, source_target_pairs={{0,16},{1,17},{2,18},{3,19},{4,20},{5,21},{6,22},{7,23},{8,24},{9,... | collective-permute-start | bytes 221192 | tf_op jit(solution)/shard_map/ppermute | solution.py:327
  6.0 6.8 %collective-permute-start.1 = (bf16[32,1152]{1,0:T(8,128)(2,1)S(1)}, bf16[32,1152]{1,0:T(8,128)(2,1)S(1)}, u32[]{:S(2)}, u32[]{:S(2)}) collective-permute-start(bf16[32,1152]{1,0:T(8,128)(2,1)S(1)} %get-tuple-element.37.refs_0_), channel_id=1, source_target_pairs={{0,24},{1,25},{2,26},{3,27},{4,28},{5,29},{6,30},{7,31},{8,16},{9,... | collective-permute-start | bytes 221192 | tf_op jit(solution)/shard_map/ppermute | solution.py:327
  7.3 5.4 %collective-permute-start.3 = (bf16[32,1152]{1,0:T(8,128)(2,1)S(1)}, bf16[32,1152]{1,0:T(8,128)(2,1)S(1)}, u32[]{:S(2)}, u32[]{:S(2)}) collective-permute-start(bf16[32,1152]{1,0:T(8,128)(2,1)S(1)} %get-tuple-element.37.refs_0_), channel_id=1, source_target_pairs={{0,8},{1,9},{2,10},{3,11},{4,12},{5,13},{6,14},{7,15},{8,0},{9,1},... | collective-permute-start | bytes 221192 | tf_op jit(solution)/shard_map/ppermute | solution.py:327
  7.5 5.2 %collective-permute-start.2 = (bf16[32,1024]{1,0:T(8,128)(2,1)S(1)}, bf16[32,1024]{1,0:T(8,128)(2,1)S(1)}, u32[]{:S(2)}, u32[]{:S(2)}) collective-permute-start(bf16[32,1024]{1,0:T(8,128)(2,1)S(1)} %get-tuple-element.38), channel_id=1, source_target_pairs={{0,6},{1,7},{2,4},{3,5},{4,2},{5,3},{6,0},{7,1},{8,14},{9,15},{10,... | collective-permute-start | bytes 196616 | tf_op jit(solution)/shard_map/ppermute | solution.py:327
  12.8 9.6 %collective-permute-start.4 = (bf16[128,1152]{1,0:T(8,128)(2,1)S(1)}, bf16[128,1152]{1,0:T(8,128)(2,1)S(1)}, u32[]{:S(2)}, u32[]{:S(2)}) collective-permute-start(bf16[128,1152]{1,0:T(8,128)(2,1)S(1)} %get-tuple-element.39.line), channel_id=1, source_target_pairs={{0,4},{1,5},{2,6},{3,7},{4,0},{5,1},{6,2},{7,3},{8,12},{9,13},{10,... | collective-permute-start | bytes 884744 | tf_op jit(solution)/shard_map/ppermute | solution.py:327
  14.5 8.8 %collective-permute-start.5 = (bf16[128,1024]{1,0:T(8,128)(2,1)S(1)}, bf16[128,1024]{1,0:T(8,128)(2,1)S(1)}, u32[]{:S(2)}, u32[]{:S(2)}) collective-permute-start(bf16[128,1024]{1,0:T(8,128)(2,1)S(1)} %get-tuple-element.42), channel_id=1, source_target_pairs={{0,2},{1,3},{2,0},{3,1},{4,6},{5,7},{6,4},{7,5},{8,10},{9,11},{10,... | collective-permute-start | bytes 786440 | tf_op jit(solution)/shard_map/ppermute | solution.py:327
  15.9 9.0 %collective-permute-start.6 = (bf16[96,1024]{1,0:T(8,128)(2,1)S(1)}, bf16[96,1024]{1,0:T(8,128)(2,1)S(1)}, u32[]{:S(2)}, u32[]{:S(2)}) collective-permute-start(bf16[96,1024]{1,0:T(8,128)(2,1)S(1)} %get-tuple-element.43), channel_id=1, source_target_pairs={{0,6},{1,7},{2,4},{3,5},{4,2},{5,3},{6,0},{7,1},{8,14},{9,15},{10,... | collective-permute-start | bytes 589832 | tf_op jit(solution)/shard_map/ppermute | solution.py:327
  19.2 6.4 %collective-permute-start.8 = (bf16[128,1152]{1,0:T(8,128)(2,1)S(1)}, bf16[128,1152]{1,0:T(8,128)(2,1)S(1)}, u32[]{:S(2)}, u32[]{:S(2)}) collective-permute-start(bf16[128,1152]{1,0:T(8,128)(2,1)S(1)} %get-tuple-element.40.refs_0_), channel_id=1, source_target_pairs={{0,1},{1,0},{2,3},{3,2},{4,5},{5,4},{6,7},{7,6},{8,9},{9,8},{10,11... | collective-permute-start | bytes 884744 | tf_op jit(solution)/shard_map/ppermute | solution.py:327
  22.4 4.0 %collective-permute-start.9 = (bf16[128,1152]{1,0:T(8,128)(2,1)S(1)}, bf16[128,1152]{1,0:T(8,128)(2,1)S(1)}, u32[]{:S(2)}, u32[]{:S(2)}) collective-permute-start(bf16[128,1152]{1,0:T(8,128)(2,1)S(1)} %collective-permute-done.4.refs_1_), channel_id=1, source_target_pairs={{0,1},{1,0},{2,3},{3,2},{4,5},{5,4},{6,7},{7,6},{8,9},{9,8},{10,11... | collective-permute-start | bytes 884744 | tf_op jit(solution)/shard_map/ppermute | solution.py:327
  22.4 1.7 %collective-permute-start.7 = (bf16[32,1024]{1,0:T(8,128)(2,1)S(1)}, bf16[32,1024]{1,0:T(8,128)(2,1)S(1)}, u32[]{:S(2)}, u32[]{:S(2)}) collective-permute-start(bf16[32,1024]{1,0:T(8,128)(2,1)S(1)} %collective-permute-done.2.refs_3_.refs_5_), channel_id=1, source_target_pairs={{0,1},{1,0},{2,3},{3,2},{4,5},{5,4},{6,7},{7,6},{8,9},{9,8},{10,11... | collective-permute-start | bytes 196616 | tf_op jit(solution)/shard_map/ppermute | solution.py:327
  23.3 3.1 %collective-permute-start.10 = (bf16[128,1024]{1,0:T(8,128)(2,1)S(1)}, bf16[128,1024]{1,0:T(8,128)(2,1)S(1)}, u32[]{:S(2)}, u32[]{:S(2)}) collective-permute-start(bf16[128,1024]{1,0:T(8,128)(2,1)S(1)} %shard_map.89.refs_2_.refs_4_), channel_id=1, source_target_pairs={{0,1},{1,0},{2,3},{3,2},{4,5},{5,4},{6,7},{7,6},{8,9},{9,8},{10,11... | collective-permute-start | bytes 786440 | tf_op jit(solution)/shard_map/ppermute | solution.py:327
  24.9 1.4 %collective-permute-start.11 = (bf16[96,1024]{1,0:T(8,128)(2,1)S(1)}, bf16[96,1024]{1,0:T(8,128)(2,1)S(1)}, u32[]{:S(2)}, u32[]{:S(2)}) collective-permute-start(bf16[96,1024]{1,0:T(8,128)(2,1)S(1)} %shard_map.90.refs_4_.refs_6_), channel_id=1, source_target_pairs={{0,1},{1,0},{2,3},{3,2},{4,5},{5,4},{6,7},{7,6},{8,9},{9,8},{10,11... | collective-permute-start | bytes 589832 | tf_op jit(solution)/shard_map/ppermute | solution.py:327
  27.6 14.2 %collective-permute-start.13 = (bf16[2048,512]{1,0:T(8,128)(2,1)S(1)}, bf16[2048,512]{1,0:T(8,128)(2,1)S(1)}, u32[]{:S(2)}, u32[]{:S(2)}) collective-permute-start(bf16[2048,512]{1,0:T(8,128)(2,1)S(1)} %shard_map.93), channel_id=1, source_target_pairs={{0,1},{1,0},{2,3},{3,2},{4,5},{5,4},{6,7},{7,6},{8,9},{9,8},{10,11... | collective-permute-start | bytes 6291464 | tf_op jit(solution)/shard_map/ppermute | solution.py:327
  27.8 14.0 %collective-permute-start.12 = (f32[256,512]{1,0:T(8,128)S(1)}, f32[256,512]{1,0:T(8,128)S(1)}, u32[]{:S(2)}, u32[]{:S(2)}) collective-permute-start(f32[256,512]{1,0:T(8,128)S(1)} %get-tuple-element.44.mine), channel_id=1, source_target_pairs={{0,1},{1,0},{2,3},{3,2},{4,5},{5,4},{6,7},{7,6},{8,9},{9,8},{10,11... | collective-permute-start | bytes 1572872 | tf_op jit(solution)/shard_map/ppermute | solution.py:327
  43.6 6.7 %collective-permute-start.18 = (bf16[64,1024]{1,0:T(8,128)(2,1)S(1)}, bf16[64,1024]{1,0:T(8,128)(2,1)S(1)}, u32[]{:S(2)}, u32[]{:S(2)}) collective-permute-start(bf16[64,1024]{1,0:T(8,128)(2,1)S(1)} %get-tuple-element.63), channel_id=1, source_target_pairs={{0,4},{1,5},{2,6},{3,7},{4,0},{5,1},{6,2},{7,3},{8,12},{9,13},{10,... | collective-permute-start | bytes 393224 | tf_op jit(solution)/shard_map/ppermute | solution.py:327
  44.2 8.3 %collective-permute-start.19 = (bf16[64,1024]{1,0:T(8,128)(2,1)S(1)}, bf16[64,1024]{1,0:T(8,128)(2,1)S(1)}, u32[]{:S(2)}, u32[]{:S(2)}) collective-permute-start(bf16[64,1024]{1,0:T(8,128)(2,1)S(1)} %get-tuple-element.64), channel_id=1, source_target_pairs={{0,2},{1,3},{2,0},{3,1},{4,6},{5,7},{6,4},{7,5},{8,10},{9,11},{10,... | collective-permute-start | bytes 393224 | tf_op jit(solution)/shard_map/ppermute | solution.py:327
  44.9 9.3 %collective-permute-start.20 = (bf16[64,1024]{1,0:T(8,128)(2,1)S(1)}, bf16[64,1024]{1,0:T(8,128)(2,1)S(1)}, u32[]{:S(2)}, u32[]{:S(2)}) collective-permute-start(bf16[64,1024]{1,0:T(8,128)(2,1)S(1)} %get-tuple-element.65), channel_id=1, source_target_pairs={{0,6},{1,7},{2,4},{3,5},{4,2},{5,3},{6,0},{7,1},{8,14},{9,15},{10,... | collective-permute-start | bytes 393224 | tf_op jit(solution)/shard_map/ppermute | solution.py:327
  48.9 7.8 %collective-permute-start.14 = (bf16[64,1024]{1,0:T(8,128)(2,1)S(1)}, bf16[64,1024]{1,0:T(8,128)(2,1)S(1)}, u32[]{:S(2)}, u32[]{:S(2)}) collective-permute-start(bf16[64,1024]{1,0:T(8,128)(2,1)S(1)} %get-tuple-element.55), channel_id=1, source_target_pairs={{0,4},{1,5},{2,6},{3,7},{4,0},{5,1},{6,2},{7,3},{8,12},{9,13},{10,... | collective-permute-start | bytes 393224 | tf_op jit(solution)/shard_map/ppermute | solution.py:327
  49.6 7.1 %collective-permute-start.15 = (bf16[64,1024]{1,0:T(8,128)(2,1)S(1)}, bf16[64,1024]{1,0:T(8,128)(2,1)S(1)}, u32[]{:S(2)}, u32[]{:S(2)}) collective-permute-start(bf16[64,1024]{1,0:T(8,128)(2,1)S(1)} %get-tuple-element.56), channel_id=1, source_target_pairs={{0,2},{1,3},{2,0},{3,1},{4,6},{5,7},{6,4},{7,5},{8,10},{9,11},{10,... | collective-permute-start | bytes 393224 | tf_op jit(solution)/shard_map/ppermute | solution.py:327
  50.2 8.5 %collective-permute-start.16 = (bf16[64,1024]{1,0:T(8,128)(2,1)S(1)}, bf16[64,1024]{1,0:T(8,128)(2,1)S(1)}, u32[]{:S(2)}, u32[]{:S(2)}) collective-permute-start(bf16[64,1024]{1,0:T(8,128)(2,1)S(1)} %get-tuple-element.57), channel_id=1, source_target_pairs={{0,6},{1,7},{2,4},{3,5},{4,2},{5,3},{6,0},{7,1},{8,14},{9,15},{10,... | collective-permute-start | bytes 393224 | tf_op jit(solution)/shard_map/ppermute | solution.py:327
  54.2 6.5 %collective-permute-start.21 = (bf16[32,1024]{1,0:T(8,128)(2,1)S(1)}, bf16[32,1024]{1,0:T(8,128)(2,1)S(1)}, u32[]{:S(2)}, u32[]{:S(2)}) collective-permute-start(bf16[32,1024]{1,0:T(8,128)(2,1)S(1)} %get-tuple-element.66), channel_id=1, source_target_pairs={{0,16},{1,17},{2,18},{3,19},{4,20},{5,21},{6,22},{7,23},{8,24},{9,... | collective-permute-start | bytes 196616 | tf_op jit(solution)/shard_map/ppermute | solution.py:327
  54.4 6.5 %collective-permute-start.22 = (bf16[32,1024]{1,0:T(8,128)(2,1)S(1)}, bf16[32,1024]{1,0:T(8,128)(2,1)S(1)}, u32[]{:S(2)}, u32[]{:S(2)}) collective-permute-start(bf16[32,1024]{1,0:T(8,128)(2,1)S(1)} %get-tuple-element.67), channel_id=1, source_target_pairs={{0,24},{1,25},{2,26},{3,27},{4,28},{5,29},{6,30},{7,31},{8,16},{9,... | collective-permute-start | bytes 196616 | tf_op jit(solution)/shard_map/ppermute | solution.py:327
  58.8 4.3 %collective-permute-start.17 = (bf16[32,1024]{1,0:T(8,128)(2,1)S(1)}, bf16[32,1024]{1,0:T(8,128)(2,1)S(1)}, u32[]{:S(2)}, u32[]{:S(2)}) collective-permute-start(bf16[32,1024]{1,0:T(8,128)(2,1)S(1)} %get-tuple-element.62), channel_id=1, source_target_pairs={{0,8},{1,9},{2,10},{3,11},{4,12},{5,13},{6,14},{7,15},{8,0},{9,1},... | collective-permute-start | bytes 196616 | tf_op jit(solution)/shard_map/ppermute | solution.py:327

commit v20 on v19

--- a/solution.py
+++ b/solution.py
@@ -432,7 +432,7 @@
     other_held = send(hold(away, stats), core=1)
     stats = lax.all_to_all(stats, AXES, 0, 0)
     rows_part = total_rows // 4
-    order = sorted(range(1, ranks), key=lambda place: (place % 2 + (place > 1), place)) + [0]
+    order = sorted(range(1, ranks), key=lambda place: (-(place % 2 + (place > 1)), place)) + [0]
     outs = (shape((rows_part, width), bf16),) * (ranks - 1) + (shape((rows_part, width), f32),)
     logit_grad, table, *going = call(
         functools.partial(grad_kernel, order, dps),

time: 64.3 us -> 63.4 us (0.986)
  waiting for transfers between devices: 14.2 us -> 12.1 us
  starting transfers between devices: 22.6 us -> 23.8 us
    ppermute x23, waiting for transfers between devices: 14.2 us -> 12.1 us  [send(): return lax.ppermute(value, AXES, pairs)]
    ppermute x23, starting transfers between devices: 22.6 us -> 23.8 us  [send(): return lax.ppermute(value, AXES, pairs)]
where the time goes in v20:
time: 63.4 us; the launch traced here: 63.2 us
  starting transfers between devices  23.8 us (38%)
  blocking collectives  13.6 us (21%)
  Pallas kernels  12.8 us (20%)
  waiting for transfers between devices  12.1 us (19%)
  between operations  0.81 us (1%)
    ppermute x23, starting transfers between devices, send(): return lax.ppermute(value, AXES, pairs)  23.8 us
    all_to_all x1, blocking collectives, body(): stats = lax.all_to_all(stats, AXES, 0, 0)  13.6 us
    pallas_call x16, Pallas kernels, call(): pl.pallas_call(kernel, out_shape=out_shape, in_specs=in_specs, out_specs=...  12.8 us
    ppermute x23, waiting for transfers between devices, send(): return lax.ppermute(value, AXES, pairs)  12.1 us
  transfers between devices with their start and end apart: 23, of which 9 were waited for; matrix products, arithmetic and copies ran while one was open for 0% of the time, Pallas kernels for 12%

profile of v20, /device:TPU:0, one launch (start us, length us, event | category | flops | bytes accessed | tf_op | source)
XLA Modules:
  0.0 63.2 jit_solution(14170010644615385569)
XLA Ops:
  0.6 1.2 %shard_map.85 = (bf16[32,1152]{1,0:T(8,128)(2,1)S(1)}, bf16[32,1024]{1,0:T(8,128)(2,1)S(1)}, bf16[32,128]{1,0:T(8,128)(2,1)S(1)}) custom-call(bf16[128,1024]{1,0:T(8,128)(2,1)} %hidden_hbm.1, s32[1,128]{1,0:T(1,128)} %bitcast.6, s32[1,128]{1,0:T(1,128)} %bitcast.7, s32[1,128]{1,0:T(1,128)} %bitcast.8), custom_call_target="tpu_custom_call" | custom-call | bytes 411136 | tf_op jit(solution)/shard_map/pallas_call | solution.py:33
  1.9 4.1 %collective-permute-start = (bf16[32,1152]{1,0:T(8,128)(2,1)S(1)}, bf16[32,1152]{1,0:T(8,128)(2,1)S(1)}, u32[]{:S(2)}, u32[]{:S(2)}) collective-permute-start(bf16[32,1152]{1,0:T(8,128)(2,1)S(1)} %get-tuple-element.37.refs_0_), channel_id=1, source_target_pairs={{0,16},{1,17},{2,18},{3,19},{4,20},{5,21},{6,22},{7,23},{8,24},{9,... | collective-permute-start | bytes 221192 | tf_op jit(solution)/shard_map/ppermute | solution.py:327
  6.0 1.3 %collective-permute-start.1 = (bf16[32,1152]{1,0:T(8,128)(2,1)S(1)}, bf16[32,1152]{1,0:T(8,128)(2,1)S(1)}, u32[]{:S(2)}, u32[]{:S(2)}) collective-permute-start(bf16[32,1152]{1,0:T(8,128)(2,1)S(1)} %get-tuple-element.37.refs_0_), channel_id=1, source_target_pairs={{0,24},{1,25},{2,26},{3,27},{4,28},{5,29},{6,30},{7,31},{8,16},{9,... | collective-permute-start | bytes 221192 | tf_op jit(solution)/shard_map/ppermute | solution.py:327
  7.5 2.4 %collective-permute-start.2 = (bf16[32,1024]{1,0:T(8,128)(2,1)S(1)}, bf16[32,1024]{1,0:T(8,128)(2,1)S(1)}, u32[]{:S(2)}, u32[]{:S(2)}) collective-permute-start(bf16[32,1024]{1,0:T(8,128)(2,1)S(1)} %get-tuple-element.38), channel_id=1, source_target_pairs={{0,6},{1,7},{2,4},{3,5},{4,2},{5,3},{6,0},{7,1},{8,14},{9,15},{10,... | collective-permute-start | bytes 196616 | tf_op jit(solution)/shard_map/ppermute | solution.py:327
  10.0 2.7 %collective-permute-done.2.refs_3_.refs_5_ = bf16[32,1024]{1,0:T(8,128)(2,1)S(1)} collective-permute-done((bf16[32,1024]{1,0:T(8,128)(2,1)S(1)}, bf16[32,1024]{1,0:T(8,128)(2,1)S(1)}, u32[]{:S(2)}, u32[]{:S(2)}) %collective-permute-start.2) | collective-permute-done | bytes 65568 | tf_op jit(solution)/shard_map/ppermute | solution.py:327
  12.8 1.7 %collective-permute-start.4 = (bf16[128,1152]{1,0:T(8,128)(2,1)S(1)}, bf16[128,1152]{1,0:T(8,128)(2,1)S(1)}, u32[]{:S(2)}, u32[]{:S(2)}) collective-permute-start(bf16[128,1152]{1,0:T(8,128)(2,1)S(1)} %get-tuple-element.39.line), channel_id=1, source_target_pairs={{0,4},{1,5},{2,6},{3,7},{4,0},{5,1},{6,2},{7,3},{8,12},{9,13},{10,... | collective-permute-start | bytes 884744 | tf_op jit(solution)/shard_map/ppermute | solution.py:327
  14.5 1.5 %collective-permute-start.5 = (bf16[128,1024]{1,0:T(8,128)(2,1)S(1)}, bf16[128,1024]{1,0:T(8,128)(2,1)S(1)}, u32[]{:S(2)}, u32[]{:S(2)}) collective-permute-start(bf16[128,1024]{1,0:T(8,128)(2,1)S(1)} %get-tuple-element.42), channel_id=1, source_target_pairs={{0,2},{1,3},{2,0},{3,1},{4,6},{5,7},{6,4},{7,5},{8,10},{9,11},{10,... | collective-permute-start | bytes 786440 | tf_op jit(solution)/shard_map/ppermute | solution.py:327
  16.3 2.9 %shard_map.87 = (bf16[4096,512]{1,0:T(8,128)(2,1)S(1)}, bf16[2048,512]{1,0:T(8,128)(2,1)S(1)}, bf16[128,1152]{1,0:T(8,128)(2,1)S(1)}) custom-call(bf16[128,1152]{1,0:T(8,128)(2,1)S(1)} %get-tuple-element.39.line, bf16[4096,512]{1,0:T(8,128)(2,1)} %weight.1), custom_call_target="tpu_custom_call" | custom-call | bytes 11075584 | tf_op jit(solution)/shard_map/pallas_call | solution.py:33
  19.3 3.1 %collective-permute-done.4.refs_1_ = bf16[128,1152]{1,0:T(8,128)(2,1)S(1)} collective-permute-done((bf16[128,1152]{1,0:T(8,128)(2,1)S(1)}, bf16[128,1152]{1,0:T(8,128)(2,1)S(1)}, u32[]{:S(2)}, u32[]{:S(2)}) %collective-permute-start.4) | collective-permute-done | bytes 294944 | tf_op jit(solution)/shard_map/ppermute | solution.py:327
  23.4 0.7 %collective-permute-done.7.refs_1_.refs_3_.refs_8_ = bf16[32,1024]{1,0:T(8,128)(2,1)S(1)} collective-permute-done((bf16[32,1024]{1,0:T(8,128)(2,1)S(1)}, bf16[32,1024]{1,0:T(8,128)(2,1)S(1)}, u32[]{:S(2)}, u32[]{:S(2)}) %collective-permute-start.7) | collective-permute-done | bytes 65568 | tf_op jit(solution)/shard_map/ppermute | solution.py:327
  24.0 0.9 %collective-permute-done.6.refs_0_ = bf16[96,1024]{1,0:T(8,128)(2,1)S(1)} collective-permute-done((bf16[96,1024]{1,0:T(8,128)(2,1)S(1)}, bf16[96,1024]{1,0:T(8,128)(2,1)S(1)}, u32[]{:S(2)}, u32[]{:S(2)}) %collective-permute-start.6) | collective-permute-done | bytes 196640 | tf_op jit(solution)/shard_map/ppermute | solution.py:327
  24.9 0.7 %shard_map.91.partial = f32[256,512]{1,0:T(8,128)S(1)} custom-call(bf16[4096,512]{1,0:T(8,128)(2,1)S(1)} %get-tuple-element.41.weight, bf16[128,1152]{1,0:T(8,128)(2,1)S(1)} %get-tuple-element.40.refs_0_, bf16[128,1152]{1,0:T(8,128)(2,1)S(1)} %collective-permute-done.4.refs_1_, bf16[128,1024]{1,0:T(8,128)(2,1)S(1)} %shard_map.89.refs_2_.refs_4_, ...), custom_call_target="tpu_custom_call" | custom-call | flops 536870912 | bytes 5832704 | tf_op jit(solution)/shard_map/pallas_call | solution.py:33
  25.7 0.7 %collective-permute-done.11.refs_4_.refs_9_ = bf16[96,1024]{1,0:T(8,128)(2,1)S(1)} collective-permute-done((bf16[96,1024]{1,0:T(8,128)(2,1)S(1)}, bf16[96,1024]{1,0:T(8,128)(2,1)S(1)}, u32[]{:S(2)}, u32[]{:S(2)}) %collective-permute-start.11) | collective-permute-done | bytes 196640 | tf_op jit(solution)/shard_map/ppermute | solution.py:327
  26.4 1.1 %shard_map.92 = (f32[256,512]{1,0:T(8,128)S(1)}, f32[32,1,384]{2,1,0:T(1,128)S(1)}) custom-call(f32[256,128]{1,0:T(8,128)S(1)} %shard_map.88.refs_1_.info, f32[256,512]{1,0:T(8,128)S(1)} %shard_map.91.partial, bf16[4096,512]{1,0:T(8,128)(2,1)S(1)} %get-tuple-element.41.weight, bf16[128,1152]{1,0:T(8,128)(2,1)S(1)} %collective-permute-done.8.refs_0_.refs_2_, ...), custom_call_target="tpu_custom_call" | custom-call | flops 536870912 | bytes 6537216 | tf_op jit(solution)/shard_map/pallas_call | solution.py:33
  28.1 13.6 %all_to_all.5.stats.refs_3_ = f32[32,1,384]{2,1,0:T(1,128)S(1)} all-to-all(f32[32,1,384]{2,1,0:T(1,128)S(1)} %get-tuple-element.46.refs_1_), channel_id=1, replica_groups=mesh['dp'=8,'vocab'=4] {'dp','vocab'}, dimensions={0} | all-to-all | bytes 98304 | tf_op jit(solution)/shard_map/all_to_all | solution.py:433
  41.8 1.8 %shard_map.94 = (bf16[256,512]{1,0:T(8,128)(2,1)S(1)}, f32[256,128]{1,0:T(8,128)S(1)}, bf16[64,1024]{1,0:T(8,128)(2,1)S(1)}, bf16[64,1024]{1,0:T(8,128)(2,1)S(1)...) custom-call(f32[256,128]{1,0:T(8,128)S(1)} %shard_map.88.refs_1_.inf, ...), custom_call_target="tpu_custom_call" | custom-call | flops 1073741824 | bytes 9224192 | tf_op jit(solution)/shard_map/pallas_call | solution.py:33
  43.6 0.7 %collective-permute-start.18 = (bf16[64,1024]{1,0:T(8,128)(2,1)S(1)}, bf16[64,1024]{1,0:T(8,128)(2,1)S(1)}, u32[]{:S(2)}, u32[]{:S(2)}) collective-permute-start(bf16[64,1024]{1,0:T(8,128)(2,1)S(1)} %get-tuple-element.63), channel_id=1, source_target_pairs={{0,6},{1,7},{2,4},{3,5},{4,2},{5,3},{6,0},{7,1},{8,14},{9,15},{10,... | collective-permute-start | bytes 393224 | tf_op jit(solution)/shard_map/ppermute | solution.py:327
  44.3 1.2 %collective-permute-start.19 = (bf16[64,1024]{1,0:T(8,128)(2,1)S(1)}, bf16[64,1024]{1,0:T(8,128)(2,1)S(1)}, u32[]{:S(2)}, u32[]{:S(2)}) collective-permute-start(bf16[64,1024]{1,0:T(8,128)(2,1)S(1)} %get-tuple-element.64), channel_id=1, source_target_pairs={{0,4},{1,5},{2,6},{3,7},{4,0},{5,1},{6,2},{7,3},{8,12},{9,13},{10,... | collective-permute-start | bytes 393224 | tf_op jit(solution)/shard_map/ppermute | solution.py:327
  45.6 1.6 %collective-permute-start.20 = (bf16[64,1024]{1,0:T(8,128)(2,1)S(1)}, bf16[64,1024]{1,0:T(8,128)(2,1)S(1)}, u32[]{:S(2)}, u32[]{:S(2)}) collective-permute-start(bf16[64,1024]{1,0:T(8,128)(2,1)S(1)} %get-tuple-element.65), channel_id=1, source_target_pairs={{0,2},{1,3},{2,0},{3,1},{4,6},{5,7},{6,4},{7,5},{8,10},{9,11},{10,... | collective-permute-start | bytes 393224 | tf_op jit(solution)/shard_map/ppermute | solution.py:327
  47.1 1.8 %shard_map.95 = (bf16[4096,512]{1,0:T(8,128)(2,1)}, f32[8,128]{1,0:T(8,128)S(1)}) custom-call(f32[64,1024]{1,0:T(8,128)S(1)} %get-tuple-element.52.after.kept, bf16[256,512]{1,0:T(8,128)(2,1)S(1)} %get-tuple-element.53.logit_grad, bf16[128,1152]{1,0:T(8,128)(2,1)S(1)} %get-tuple-element.40.refs_0_, bf16[128,1152]{1,0:T(8,128)(2,1)S(1)} %collective-permute-done.4.refs_1_, ...), custom_call_target="tpu_custom_call" | custom-call | flops 536870912 | bytes 5902336 | tf_op jit(solution)/shard_map/pallas_call | solution.py:33
  48.9 0.7 %collective-permute-start.14 = (bf16[64,1024]{1,0:T(8,128)(2,1)S(1)}, bf16[64,1024]{1,0:T(8,128)(2,1)S(1)}, u32[]{:S(2)}, u32[]{:S(2)}) collective-permute-start(bf16[64,1024]{1,0:T(8,128)(2,1)S(1)} %get-tuple-element.55), channel_id=1, source_target_pairs={{0,6},{1,7},{2,4},{3,5},{4,2},{5,3},{6,0},{7,1},{8,14},{9,15},{10,... | collective-permute-start | bytes 393224 | tf_op jit(solution)/shard_map/ppermute | solution.py:327
  49.7 1.2 %collective-permute-start.15 = (bf16[64,1024]{1,0:T(8,128)(2,1)S(1)}, bf16[64,1024]{1,0:T(8,128)(2,1)S(1)}, u32[]{:S(2)}, u32[]{:S(2)}) collective-permute-start(bf16[64,1024]{1,0:T(8,128)(2,1)S(1)} %get-tuple-element.56), channel_id=1, source_target_pairs={{0,4},{1,5},{2,6},{3,7},{4,0},{5,1},{6,2},{7,3},{8,12},{9,13},{10,... | collective-permute-start | bytes 393224 | tf_op jit(solution)/shard_map/ppermute | solution.py:327
  50.9 1.6 %collective-permute-start.16 = (bf16[64,1024]{1,0:T(8,128)(2,1)S(1)}, bf16[64,1024]{1,0:T(8,128)(2,1)S(1)}, u32[]{:S(2)}, u32[]{:S(2)}) collective-permute-start(bf16[64,1024]{1,0:T(8,128)(2,1)S(1)} %get-tuple-element.57), channel_id=1, source_target_pairs={{0,2},{1,3},{2,0},{3,1},{4,6},{5,7},{6,4},{7,5},{8,10},{9,11},{10,... | collective-permute-start | bytes 393224 | tf_op jit(solution)/shard_map/ppermute | solution.py:327
  52.5 1.3 %collective-permute-done.19.refs_1_ = bf16[64,1024]{1,0:T(8,128)(2,1)S(1)} collective-permute-done((bf16[64,1024]{1,0:T(8,128)(2,1)S(1)}, bf16[64,1024]{1,0:T(8,128)(2,1)S(1)}, u32[]{:S(2)}, u32[]{:S(2)}) %collective-permute-start.19) | collective-permute-done | bytes 131104 | tf_op jit(solution)/shard_map/ppermute | solution.py:327
  53.9 0.8 %collective-permute-start.21 = (bf16[32,1024]{1,0:T(8,128)(2,1)S(1)}, bf16[32,1024]{1,0:T(8,128)(2,1)S(1)}, u32[]{:S(2)}, u32[]{:S(2)}) collective-permute-start(bf16[32,1024]{1,0:T(8,128)(2,1)S(1)} %get-tuple-element.66), channel_id=1, source_target_pairs={{0,16},{1,17},{2,18},{3,19},{4,20},{5,21},{6,22},{7,23},{8,24},{9,... | collective-permute-start | bytes 196616 | tf_op jit(solution)/shard_map/ppermute | solution.py:327
  54.7 2.3 %collective-permute-start.22 = (bf16[32,1024]{1,0:T(8,128)(2,1)S(1)}, bf16[32,1024]{1,0:T(8,128)(2,1)S(1)}, u32[]{:S(2)}, u32[]{:S(2)}) collective-permute-start(bf16[32,1024]{1,0:T(8,128)(2,1)S(1)} %get-tuple-element.67), channel_id=1, source_target_pairs={{0,24},{1,25},{2,26},{3,27},{4,28},{5,29},{6,30},{7,31},{8,16},{9,... | collective-permute-start | bytes 196616 | tf_op jit(solution)/shard_map/ppermute | solution.py:327
  57.0 0.9 %collective-permute-done.15.refs_1_ = bf16[64,1024]{1,0:T(8,128)(2,1)S(1)} collective-permute-done((bf16[64,1024]{1,0:T(8,128)(2,1)S(1)}, bf16[64,1024]{1,0:T(8,128)(2,1)S(1)}, u32[]{:S(2)}, u32[]{:S(2)}) %collective-permute-start.15) | collective-permute-done | bytes 131104 | tf_op jit(solution)/shard_map/ppermute | solution.py:327
  57.9 0.7 %collective-permute-start.17 = (bf16[32,1024]{1,0:T(8,128)(2,1)S(1)}, bf16[32,1024]{1,0:T(8,128)(2,1)S(1)}, u32[]{:S(2)}, u32[]{:S(2)}) collective-permute-start(bf16[32,1024]{1,0:T(8,128)(2,1)S(1)} %get-tuple-element.62), channel_id=1, source_target_pairs={{0,8},{1,9},{2,10},{3,11},{4,12},{5,13},{6,14},{7,15},{8,0},{9,1},... | collective-permute-start | bytes 196616 | tf_op jit(solution)/shard_map/ppermute | solution.py:327
  58.6 1.8 %shard_map.98 = (bf16[4096,512]{1,0:T(8,128)(2,1)}, f32[8,128]{1,0:T(8,128)S(1)}) custom-call(f32[32,1024]{1,0:T(8,128)S(1)} %get-tuple-element.58.after.refs_0_, bf16[256,512]{1,0:T(8,128)(2,1)S(1)} %get-tuple-element.53.logit_grad, bf16[4096,512]{1,0:T(8,128)(2,1)} %get-tuple-element.59.refs_0_, ...), custom_call_target="tpu_custom_call", output_to_operand_aliasing={{0}: (2, {})} | custom-call | flops 536870912 | bytes 10145792 | tf_op jit(solution)/shard_map/pallas_call | solution.py:33
  60.4 0.8 %collective-permute-done.22.refs_3_ = bf16[32,1024]{1,0:T(8,128)(2,1)S(1)} collective-permute-done((bf16[32,1024]{1,0:T(8,128)(2,1)S(1)}, bf16[32,1024]{1,0:T(8,128)(2,1)S(1)}, u32[]{:S(2)}, u32[]{:S(2)}) %collective-permute-start.22) | collective-permute-done | bytes 65568 | tf_op jit(solution)/shard_map/ppermute | solution.py:327
  61.2 1.1 %collective-permute-done.17.refs_1_ = bf16[32,1024]{1,0:T(8,128)(2,1)S(1)} collective-permute-done((bf16[32,1024]{1,0:T(8,128)(2,1)S(1)}, bf16[32,1024]{1,0:T(8,128)(2,1)S(1)}, u32[]{:S(2)}, u32[]{:S(2)}) %collective-permute-start.17) | collective-permute-done | bytes 65568 | tf_op jit(solution)/shard_map/ppermute | solution.py:327
  62.3 1.0 %shard_map.100 = (bf16[128,1024]{1,0:T(8,128)(2,1)}, f32[1,1]{1,0:T(1,128)}) custom-call(f32[8,128]{1,0:T(8,128)S(1)} %get-tuple-element.60.last, bf16[32,128]{1,0:T(8,128)(2,1)S(1)} %get-tuple-element.61.chosen, f32[32,1024]{1,0:T(8,128)S(1)} %get-tuple-element.58.after.refs_0_, bf16[32,1024]{1,0:T(8,128)(2,1)S(1)} %collective-permute-done.17.refs_1_, ...), custom_call_target="tpu_custom_call" | custom-call | bytes 602116 | tf_op jit(solution)/shard_map/pallas_call | solution.py:33
  (33 shorter events, 2.5 us)
Async XLA Ops:
  0.6 22.2 %copy-start = (f32[32]{0:T(128)S(1)}, f32[32]{0:T(128)}, u32[]{:S(2)}) copy-start(f32[32]{0:T(128)} %param.11) | copy-start | bytes 388
  1.9 10.8 %collective-permute-start = (bf16[32,1152]{1,0:T(8,128)(2,1)S(1)}, bf16[32,1152]{1,0:T(8,128)(2,1)S(1)}, u32[]{:S(2)}, u32[]{:S(2)}) collective-permute-start(bf16[32,1152]{1,0:T(8,128)(2,1)S(1)} %get-tuple-element.37.refs_0_), channel_id=1, source_target_pairs={{0,16},{1,17},{2,18},{3,19},{4,20},{5,21},{6,22},{7,23},{8,24},{9,... | collective-permute-start | bytes 221192 | tf_op jit(solution)/shard_map/ppermute | solution.py:327
  6.0 6.8 %collective-permute-start.1 = (bf16[32,1152]{1,0:T(8,128)(2,1)S(1)}, bf16[32,1152]{1,0:T(8,128)(2,1)S(1)}, u32[]{:S(2)}, u32[]{:S(2)}) collective-permute-start(bf16[32,1152]{1,0:T(8,128)(2,1)S(1)} %get-tuple-element.37.refs_0_), channel_id=1, source_target_pairs={{0,24},{1,25},{2,26},{3,27},{4,28},{5,29},{6,30},{7,31},{8,16},{9,... | collective-permute-start | bytes 221192 | tf_op jit(solution)/shard_map/ppermute | solution.py:327
  7.3 5.4 %collective-permute-start.3 = (bf16[32,1152]{1,0:T(8,128)(2,1)S(1)}, bf16[32,1152]{1,0:T(8,128)(2,1)S(1)}, u32[]{:S(2)}, u32[]{:S(2)}) collective-permute-start(bf16[32,1152]{1,0:T(8,128)(2,1)S(1)} %get-tuple-element.37.refs_0_), channel_id=1, source_target_pairs={{0,8},{1,9},{2,10},{3,11},{4,12},{5,13},{6,14},{7,15},{8,0},{9,1},... | collective-permute-start | bytes 221192 | tf_op jit(solution)/shard_map/ppermute | solution.py:327
  7.5 5.2 %collective-permute-start.2 = (bf16[32,1024]{1,0:T(8,128)(2,1)S(1)}, bf16[32,1024]{1,0:T(8,128)(2,1)S(1)}, u32[]{:S(2)}, u32[]{:S(2)}) collective-permute-start(bf16[32,1024]{1,0:T(8,128)(2,1)S(1)} %get-tuple-element.38), channel_id=1, source_target_pairs={{0,6},{1,7},{2,4},{3,5},{4,2},{5,3},{6,0},{7,1},{8,14},{9,15},{10,... | collective-permute-start | bytes 196616 | tf_op jit(solution)/shard_map/ppermute | solution.py:327
  12.8 9.6 %collective-permute-start.4 = (bf16[128,1152]{1,0:T(8,128)(2,1)S(1)}, bf16[128,1152]{1,0:T(8,128)(2,1)S(1)}, u32[]{:S(2)}, u32[]{:S(2)}) collective-permute-start(bf16[128,1152]{1,0:T(8,128)(2,1)S(1)} %get-tuple-element.39.line), channel_id=1, source_target_pairs={{0,4},{1,5},{2,6},{3,7},{4,0},{5,1},{6,2},{7,3},{8,12},{9,13},{10,... | collective-permute-start | bytes 884744 | tf_op jit(solution)/shard_map/ppermute | solution.py:327
  14.5 8.8 %collective-permute-start.5 = (bf16[128,1024]{1,0:T(8,128)(2,1)S(1)}, bf16[128,1024]{1,0:T(8,128)(2,1)S(1)}, u32[]{:S(2)}, u32[]{:S(2)}) collective-permute-start(bf16[128,1024]{1,0:T(8,128)(2,1)S(1)} %get-tuple-element.42), channel_id=1, source_target_pairs={{0,2},{1,3},{2,0},{3,1},{4,6},{5,7},{6,4},{7,5},{8,10},{9,11},{10,... | collective-permute-start | bytes 786440 | tf_op jit(solution)/shard_map/ppermute | solution.py:327
  15.9 9.0 %collective-permute-start.6 = (bf16[96,1024]{1,0:T(8,128)(2,1)S(1)}, bf16[96,1024]{1,0:T(8,128)(2,1)S(1)}, u32[]{:S(2)}, u32[]{:S(2)}) collective-permute-start(bf16[96,1024]{1,0:T(8,128)(2,1)S(1)} %get-tuple-element.43), channel_id=1, source_target_pairs={{0,6},{1,7},{2,4},{3,5},{4,2},{5,3},{6,0},{7,1},{8,14},{9,15},{10,... | collective-permute-start | bytes 589832 | tf_op jit(solution)/shard_map/ppermute | solution.py:327
  19.2 6.4 %collective-permute-start.8 = (bf16[128,1152]{1,0:T(8,128)(2,1)S(1)}, bf16[128,1152]{1,0:T(8,128)(2,1)S(1)}, u32[]{:S(2)}, u32[]{:S(2)}) collective-permute-start(bf16[128,1152]{1,0:T(8,128)(2,1)S(1)} %get-tuple-element.40.refs_0_), channel_id=1, source_target_pairs={{0,1},{1,0},{2,3},{3,2},{4,5},{5,4},{6,7},{7,6},{8,9},{9,8},{10,11... | collective-permute-start | bytes 884744 | tf_op jit(solution)/shard_map/ppermute | solution.py:327
  22.4 4.0 %collective-permute-start.9 = (bf16[128,1152]{1,0:T(8,128)(2,1)S(1)}, bf16[128,1152]{1,0:T(8,128)(2,1)S(1)}, u32[]{:S(2)}, u32[]{:S(2)}) collective-permute-start(bf16[128,1152]{1,0:T(8,128)(2,1)S(1)} %collective-permute-done.4.refs_1_), channel_id=1, source_target_pairs={{0,1},{1,0},{2,3},{3,2},{4,5},{5,4},{6,7},{7,6},{8,9},{9,8},{10,11... | collective-permute-start | bytes 884744 | tf_op jit(solution)/shard_map/ppermute | solution.py:327
  22.4 1.7 %collective-permute-start.7 = (bf16[32,1024]{1,0:T(8,128)(2,1)S(1)}, bf16[32,1024]{1,0:T(8,128)(2,1)S(1)}, u32[]{:S(2)}, u32[]{:S(2)}) collective-permute-start(bf16[32,1024]{1,0:T(8,128)(2,1)S(1)} %collective-permute-done.2.refs_3_.refs_5_), channel_id=1, source_target_pairs={{0,1},{1,0},{2,3},{3,2},{4,5},{5,4},{6,7},{7,6},{8,9},{9,8},{10,11... | collective-permute-start | bytes 196616 | tf_op jit(solution)/shard_map/ppermute | solution.py:327
  23.3 3.1 %collective-permute-start.10 = (bf16[128,1024]{1,0:T(8,128)(2,1)S(1)}, bf16[128,1024]{1,0:T(8,128)(2,1)S(1)}, u32[]{:S(2)}, u32[]{:S(2)}) collective-permute-start(bf16[128,1024]{1,0:T(8,128)(2,1)S(1)} %shard_map.89.refs_2_.refs_4_), channel_id=1, source_target_pairs={{0,1},{1,0},{2,3},{3,2},{4,5},{5,4},{6,7},{7,6},{8,9},{9,8},{10,11... | collective-permute-start | bytes 786440 | tf_op jit(solution)/shard_map/ppermute | solution.py:327
  24.9 1.4 %collective-permute-start.11 = (bf16[96,1024]{1,0:T(8,128)(2,1)S(1)}, bf16[96,1024]{1,0:T(8,128)(2,1)S(1)}, u32[]{:S(2)}, u32[]{:S(2)}) collective-permute-start(bf16[96,1024]{1,0:T(8,128)(2,1)S(1)} %shard_map.90.refs_4_.refs_6_), channel_id=1, source_target_pairs={{0,1},{1,0},{2,3},{3,2},{4,5},{5,4},{6,7},{7,6},{8,9},{9,8},{10,11... | collective-permute-start | bytes 589832 | tf_op jit(solution)/shard_map/ppermute | solution.py:327
  27.6 14.2 %collective-permute-start.13 = (bf16[2048,512]{1,0:T(8,128)(2,1)S(1)}, bf16[2048,512]{1,0:T(8,128)(2,1)S(1)}, u32[]{:S(2)}, u32[]{:S(2)}) collective-permute-start(bf16[2048,512]{1,0:T(8,128)(2,1)S(1)} %shard_map.93), channel_id=1, source_target_pairs={{0,1},{1,0},{2,3},{3,2},{4,5},{5,4},{6,7},{7,6},{8,9},{9,8},{10,11... | collective-permute-start | bytes 6291464 | tf_op jit(solution)/shard_map/ppermute | solution.py:327
  27.8 14.0 %collective-permute-start.12 = (f32[256,512]{1,0:T(8,128)S(1)}, f32[256,512]{1,0:T(8,128)S(1)}, u32[]{:S(2)}, u32[]{:S(2)}) collective-permute-start(f32[256,512]{1,0:T(8,128)S(1)} %get-tuple-element.44.mine), channel_id=1, source_target_pairs={{0,1},{1,0},{2,3},{3,2},{4,5},{5,4},{6,7},{7,6},{8,9},{9,8},{10,11... | collective-permute-start | bytes 1572872 | tf_op jit(solution)/shard_map/ppermute | solution.py:327
  43.6 7.4 %collective-permute-start.18 = (bf16[64,1024]{1,0:T(8,128)(2,1)S(1)}, bf16[64,1024]{1,0:T(8,128)(2,1)S(1)}, u32[]{:S(2)}, u32[]{:S(2)}) collective-permute-start(bf16[64,1024]{1,0:T(8,128)(2,1)S(1)} %get-tuple-element.63), channel_id=1, source_target_pairs={{0,6},{1,7},{2,4},{3,5},{4,2},{5,3},{6,0},{7,1},{8,14},{9,15},{10,... | collective-permute-start | bytes 393224 | tf_op jit(solution)/shard_map/ppermute | solution.py:327
  44.3 9.5 %collective-permute-start.19 = (bf16[64,1024]{1,0:T(8,128)(2,1)S(1)}, bf16[64,1024]{1,0:T(8,128)(2,1)S(1)}, u32[]{:S(2)}, u32[]{:S(2)}) collective-permute-start(bf16[64,1024]{1,0:T(8,128)(2,1)S(1)} %get-tuple-element.64), channel_id=1, source_target_pairs={{0,4},{1,5},{2,6},{3,7},{4,0},{5,1},{6,2},{7,3},{8,12},{9,13},{10,... | collective-permute-start | bytes 393224 | tf_op jit(solution)/shard_map/ppermute | solution.py:327
  45.6 8.3 %collective-permute-start.20 = (bf16[64,1024]{1,0:T(8,128)(2,1)S(1)}, bf16[64,1024]{1,0:T(8,128)(2,1)S(1)}, u32[]{:S(2)}, u32[]{:S(2)}) collective-permute-start(bf16[64,1024]{1,0:T(8,128)(2,1)S(1)} %get-tuple-element.65), channel_id=1, source_target_pairs={{0,2},{1,3},{2,0},{3,1},{4,6},{5,7},{6,4},{7,5},{8,10},{9,11},{10,... | collective-permute-start | bytes 393224 | tf_op jit(solution)/shard_map/ppermute | solution.py:327
  48.9 8.1 %collective-permute-start.14 = (bf16[64,1024]{1,0:T(8,128)(2,1)S(1)}, bf16[64,1024]{1,0:T(8,128)(2,1)S(1)}, u32[]{:S(2)}, u32[]{:S(2)}) collective-permute-start(bf16[64,1024]{1,0:T(8,128)(2,1)S(1)} %get-tuple-element.55), channel_id=1, source_target_pairs={{0,6},{1,7},{2,4},{3,5},{4,2},{5,3},{6,0},{7,1},{8,14},{9,15},{10,... | collective-permute-start | bytes 393224 | tf_op jit(solution)/shard_map/ppermute | solution.py:327
  49.7 8.2 %collective-permute-start.15 = (bf16[64,1024]{1,0:T(8,128)(2,1)S(1)}, bf16[64,1024]{1,0:T(8,128)(2,1)S(1)}, u32[]{:S(2)}, u32[]{:S(2)}) collective-permute-start(bf16[64,1024]{1,0:T(8,128)(2,1)S(1)} %get-tuple-element.56), channel_id=1, source_target_pairs={{0,4},{1,5},{2,6},{3,7},{4,0},{5,1},{6,2},{7,3},{8,12},{9,13},{10,... | collective-permute-start | bytes 393224 | tf_op jit(solution)/shard_map/ppermute | solution.py:327
  50.9 6.9 %collective-permute-start.16 = (bf16[64,1024]{1,0:T(8,128)(2,1)S(1)}, bf16[64,1024]{1,0:T(8,128)(2,1)S(1)}, u32[]{:S(2)}, u32[]{:S(2)}) collective-permute-start(bf16[64,1024]{1,0:T(8,128)(2,1)S(1)} %get-tuple-element.57), channel_id=1, source_target_pairs={{0,2},{1,3},{2,0},{3,1},{4,6},{5,7},{6,4},{7,5},{8,10},{9,11},{10,... | collective-permute-start | bytes 393224 | tf_op jit(solution)/shard_map/ppermute | solution.py:327
  53.9 6.5 %collective-permute-start.21 = (bf16[32,1024]{1,0:T(8,128)(2,1)S(1)}, bf16[32,1024]{1,0:T(8,128)(2,1)S(1)}, u32[]{:S(2)}, u32[]{:S(2)}) collective-permute-start(bf16[32,1024]{1,0:T(8,128)(2,1)S(1)} %get-tuple-element.66), channel_id=1, source_target_pairs={{0,16},{1,17},{2,18},{3,19},{4,20},{5,21},{6,22},{7,23},{8,24},{9,... | collective-permute-start | bytes 196616 | tf_op jit(solution)/shard_map/ppermute | solution.py:327
  54.7 6.5 %collective-permute-start.22 = (bf16[32,1024]{1,0:T(8,128)(2,1)S(1)}, bf16[32,1024]{1,0:T(8,128)(2,1)S(1)}, u32[]{:S(2)}, u32[]{:S(2)}) collective-permute-start(bf16[32,1024]{1,0:T(8,128)(2,1)S(1)} %get-tuple-element.67), channel_id=1, source_target_pairs={{0,24},{1,25},{2,26},{3,27},{4,28},{5,29},{6,30},{7,31},{8,16},{9,... | collective-permute-start | bytes 196616 | tf_op jit(solution)/shard_map/ppermute | solution.py:327
  57.9 4.3 %collective-permute-start.17 = (bf16[32,1024]{1,0:T(8,128)(2,1)S(1)}, bf16[32,1024]{1,0:T(8,128)(2,1)S(1)}, u32[]{:S(2)}, u32[]{:S(2)}) collective-permute-start(bf16[32,1024]{1,0:T(8,128)(2,1)S(1)} %get-tuple-element.62), channel_id=1, source_target_pairs={{0,8},{1,9},{2,10},{3,11},{4,12},{5,13},{6,14},{7,15},{8,0},{9,1},... | collective-permute-start | bytes 196616 | tf_op jit(solution)/shard_map/ppermute | solution.py:327

commit v21 on v20

--- a/solution.py
+++ b/solution.py
@@ -180,11 +180,10 @@
     return jnp.concatenate([ref[:, :width] for ref in pieces[start:start + counts[place]]], axis=0)
 
 
-def some_logits(counts, first, pieces, weight):
-    blocks = 2 * len(counts)
-    width = weight.shape[0] // blocks
+def some_logits(blocks, counts, ranks, pieces, weight):
+    width = weight.shape[0] // ranks
     rank, total = coordinates()[0], None
-    for place, block in enumerate(range(first, blocks, 2)):
+    for place, block in enumerate(blocks):
         start = pl.multiple_of((rank ^ block) * width, width)
         part = jnp.dot(
             all_rows(pieces, counts, place, width),
@@ -195,14 +194,14 @@
     return total
 
 
-def first_kernel(counts, weight, *refs):
-    refs[-1][...] = some_logits(counts, 0, refs[:-1], weight)
-
-
-def logits_kernel(counts, groups, info, partial, weight, *refs):
+def first_kernel(blocks, counts, ranks, weight, *refs):
+    refs[-1][...] = some_logits(blocks, counts, ranks, refs[:-1], weight)
+
+
+def logits_kernel(blocks, counts, ranks, groups, info, partial, weight, *refs):
     pieces, (logits, stats) = refs[:-2], refs[-2:]
     _, position, shard = coordinates()
-    total = partial[...] + some_logits(counts, 1, pieces, weight)
+    total = partial[...] + some_logits(blocks, counts, ranks, pieces, weight)
     logits[...] = total
     height, columns = total.shape
     target = info[:, 1:2].astype(jnp.int32) - shard * columns
@@ -392,6 +391,18 @@
         like = shape(value.shape, value.dtype)
         return call(gate_kernel, (value, after), [ANY, ANY], like, ANY, aliases={0: 0})
 
+    def part_logits(kernel, blocks, operands, out_shapes):
+        parts = [[pieces[key] for key in sorted(pieces) if key[0] == b] for b in blocks]
+        operands = (*operands, held, *(piece for part in parts for piece in part))
+        return call(
+            functools.partial(kernel, blocks, [len(part) for part in parts], ranks),
+            operands,
+            [VMEM] * len(operands),
+            out_shapes,
+            jax.tree.map(lambda _: VMEM, out_shapes),
+            flops=flops * len(blocks) // ranks,
+        )
+
     for x in range(1, xs):
         pieces[2 * x + 1, 1, 0] = send(pieces[2 * x, 1, 0], core=1)
         pieces[2 * x, 0, 0] = hold(pieces[2 * x, 0, 0], info)
@@ -399,6 +410,15 @@
     for b, y, part in list(pieces):
         if b % 2 == 0 and (b + 1, y, part) not in pieces:
             pieces[b + 1, y, part] = send(pieces[b, y, part], core=1)
+
+    logits_shape = shape((total_rows, columns), f32)
+    partial = part_logits(first_kernel, [*range(0, ranks, 2), 1], (), logits_shape)
+    logits, stats = part_logits(
+        lambda blocks, counts, ranks, *refs: logits_kernel(blocks, counts, ranks, dps, *refs),
+        list(range(3, ranks, 2)),
+        (info, partial),
+        (logits_shape, shape((dps * ranks, 1, total_rows + LANES), f32)),
+    )
     parted = [[pieces[key] for key in sorted(pieces) if key[0] == b] for b in range(ranks)]
 
     def rows_of(blocks):
@@ -407,27 +427,6 @@
     def counts_of(blocks):
         return [len(parted[b]) for b in blocks]
 
-    near = range(0, ranks, 2)
-    partial = call(
-        functools.partial(first_kernel, counts_of(near)),
-        (held, *rows_of(near)),
-        [VMEM] * (1 + sum(counts_of(near))),
-        shape((total_rows, columns), f32),
-        VMEM,
-        flops=flops // 2,
-    )
-    beside = range(1, ranks, 2)
-    logits, stats = call(
-        functools.partial(logits_kernel, counts_of(beside), dps),
-        (info, partial, held, *rows_of(beside)),
-        [VMEM] * (3 + sum(counts_of(beside))),
-        (
-            shape((total_rows, columns), f32),
-            shape((dps * ranks, 1, total_rows + LANES), f32),
-        ),
-        (VMEM, VMEM),
-        flops=flops // 2,
-    )
     other_logits = send(logits, core=1)
     other_held = send(hold(away, stats), core=1)
     stats = lax.all_to_all(stats, AXES, 0, 0)

time: 63.4 us -> 63.1 us (level)
  transfers between devices with their start and end apart: 23 -> 23, of which waited for: 9 -> 9; matrix products, arithmetic and copies ran while one was open for 0% -> 0% of each run, Pallas kernels for 12% -> 13%
where the time goes in v21:
time: 63.1 us; the launch traced here: 63 us
  starting transfers between devices  23.8 us (38%)
  blocking collectives  13.6 us (22%)
  Pallas kernels  12.9 us (20%)
  waiting for transfers between devices  11.8 us (19%)
  between operations  0.8 us (1%)
    ppermute x23, starting transfers between devices, send(): return lax.ppermute(value, AXES, pairs)  23.8 us
    all_to_all x1, blocking collectives, body(): stats = lax.all_to_all(stats, AXES, 0, 0)  13.6 us
    pallas_call x16, Pallas kernels, call(): pl.pallas_call(kernel, out_shape=out_shape, in_specs=in_specs, out_specs=...  12.9 us
    ppermute x23, waiting for transfers between devices, send(): return lax.ppermute(value, AXES, pairs)  11.8 us
  transfers between devices with their start and end apart: 23, of which 9 were waited for; matrix products, arithmetic and copies ran while one was open for 0% of the time, Pallas kernels for 13%

profile of v21, /device:TPU:0, one launch (start us, length us, event | category | flops | bytes accessed | tf_op | source)
XLA Modules:
  0.0 63.0 jit_solution(7732683669047599236)
XLA Ops:
  0.6 1.2 %shard_map.85 = (bf16[32,1152]{1,0:T(8,128)(2,1)S(1)}, bf16[32,1024]{1,0:T(8,128)(2,1)S(1)}, bf16[32,128]{1,0:T(8,128)(2,1)S(1)}) custom-call(bf16[128,1024]{1,0:T(8,128)(2,1)} %hidden_hbm.1, s32[1,128]{1,0:T(1,128)} %bitcast.6, s32[1,128]{1,0:T(1,128)} %bitcast.7, s32[1,128]{1,0:T(1,128)} %bitcast.8), custom_call_target="tpu_custom_call" | custom-call | bytes 411136 | tf_op jit(solution)/shard_map/pallas_call | solution.py:33
  1.9 4.1 %collective-permute-start = (bf16[32,1152]{1,0:T(8,128)(2,1)S(1)}, bf16[32,1152]{1,0:T(8,128)(2,1)S(1)}, u32[]{:S(2)}, u32[]{:S(2)}) collective-permute-start(bf16[32,1152]{1,0:T(8,128)(2,1)S(1)} %get-tuple-element.37.refs_0_), channel_id=1, source_target_pairs={{0,16},{1,17},{2,18},{3,19},{4,20},{5,21},{6,22},{7,23},{8,24},{9,... | collective-permute-start | bytes 221192 | tf_op jit(solution)/shard_map/ppermute | solution.py:326
  6.0 1.3 %collective-permute-start.1 = (bf16[32,1152]{1,0:T(8,128)(2,1)S(1)}, bf16[32,1152]{1,0:T(8,128)(2,1)S(1)}, u32[]{:S(2)}, u32[]{:S(2)}) collective-permute-start(bf16[32,1152]{1,0:T(8,128)(2,1)S(1)} %get-tuple-element.37.refs_0_), channel_id=1, source_target_pairs={{0,24},{1,25},{2,26},{3,27},{4,28},{5,29},{6,30},{7,31},{8,16},{9,... | collective-permute-start | bytes 221192 | tf_op jit(solution)/shard_map/ppermute | solution.py:326
  7.5 2.4 %collective-permute-start.2 = (bf16[32,1024]{1,0:T(8,128)(2,1)S(1)}, bf16[32,1024]{1,0:T(8,128)(2,1)S(1)}, u32[]{:S(2)}, u32[]{:S(2)}) collective-permute-start(bf16[32,1024]{1,0:T(8,128)(2,1)S(1)} %get-tuple-element.38), channel_id=1, source_target_pairs={{0,6},{1,7},{2,4},{3,5},{4,2},{5,3},{6,0},{7,1},{8,14},{9,15},{10,... | collective-permute-start | bytes 196616 | tf_op jit(solution)/shard_map/ppermute | solution.py:326
  10.0 2.7 %collective-permute-done.2.refs_3_.refs_5_ = bf16[32,1024]{1,0:T(8,128)(2,1)S(1)} collective-permute-done((bf16[32,1024]{1,0:T(8,128)(2,1)S(1)}, bf16[32,1024]{1,0:T(8,128)(2,1)S(1)}, u32[]{:S(2)}, u32[]{:S(2)}) %collective-permute-start.2) | collective-permute-done | bytes 65568 | tf_op jit(solution)/shard_map/ppermute | solution.py:326
  12.8 1.7 %collective-permute-start.4 = (bf16[128,1152]{1,0:T(8,128)(2,1)S(1)}, bf16[128,1152]{1,0:T(8,128)(2,1)S(1)}, u32[]{:S(2)}, u32[]{:S(2)}) collective-permute-start(bf16[128,1152]{1,0:T(8,128)(2,1)S(1)} %get-tuple-element.39.line), channel_id=1, source_target_pairs={{0,4},{1,5},{2,6},{3,7},{4,0},{5,1},{6,2},{7,3},{8,12},{9,13},{10,... | collective-permute-start | bytes 884744 | tf_op jit(solution)/shard_map/ppermute | solution.py:326
  14.5 1.5 %collective-permute-start.5 = (bf16[128,1024]{1,0:T(8,128)(2,1)S(1)}, bf16[128,1024]{1,0:T(8,128)(2,1)S(1)}, u32[]{:S(2)}, u32[]{:S(2)}) collective-permute-start(bf16[128,1024]{1,0:T(8,128)(2,1)S(1)} %get-tuple-element.42), channel_id=1, source_target_pairs={{0,2},{1,3},{2,0},{3,1},{4,6},{5,7},{6,4},{7,5},{8,10},{9,11},{10,... | collective-permute-start | bytes 786440 | tf_op jit(solution)/shard_map/ppermute | solution.py:326
  16.3 2.9 %shard_map.87 = (bf16[4096,512]{1,0:T(8,128)(2,1)S(1)}, bf16[2048,512]{1,0:T(8,128)(2,1)S(1)}, bf16[128,1152]{1,0:T(8,128)(2,1)S(1)}) custom-call(bf16[128,1152]{1,0:T(8,128)(2,1)S(1)} %get-tuple-element.39.line, bf16[4096,512]{1,0:T(8,128)(2,1)} %weight.1), custom_call_target="tpu_custom_call" | custom-call | bytes 11075584 | tf_op jit(solution)/shard_map/pallas_call | solution.py:33
  19.3 3.1 %collective-permute-done.4.refs_1_ = bf16[128,1152]{1,0:T(8,128)(2,1)S(1)} collective-permute-done((bf16[128,1152]{1,0:T(8,128)(2,1)S(1)}, bf16[128,1152]{1,0:T(8,128)(2,1)S(1)}, u32[]{:S(2)}, u32[]{:S(2)}) %collective-permute-start.4) | collective-permute-done | bytes 294944 | tf_op jit(solution)/shard_map/ppermute | solution.py:326
  22.4 0.5 collective-permute-start.7
  23.4 0.7 %collective-permute-done.7.refs_1_.refs_4_.refs_8_ = bf16[32,1024]{1,0:T(8,128)(2,1)S(1)} collective-permute-done((bf16[32,1024]{1,0:T(8,128)(2,1)S(1)}, bf16[32,1024]{1,0:T(8,128)(2,1)S(1)}, u32[]{:S(2)}, u32[]{:S(2)}) %collective-permute-start.7) | collective-permute-done | bytes 65568 | tf_op jit(solution)/shard_map/ppermute | solution.py:326
  24.0 0.9 %collective-permute-done.6.refs_0_ = bf16[96,1024]{1,0:T(8,128)(2,1)S(1)} collective-permute-done((bf16[96,1024]{1,0:T(8,128)(2,1)S(1)}, bf16[96,1024]{1,0:T(8,128)(2,1)S(1)}, u32[]{:S(2)}, u32[]{:S(2)}) %collective-permute-start.6) | collective-permute-done | bytes 196640 | tf_op jit(solution)/shard_map/ppermute | solution.py:326
  25.0 1.0 %shard_map.91.refs_1_ = f32[256,512]{1,0:T(8,128)S(1)} custom-call(bf16[4096,512]{1,0:T(8,128)(2,1)S(1)} %get-tuple-element.41.weight.refs_2_, bf16[128,1152]{1,0:T(8,128)(2,1)S(1)} %get-tuple-element.40.refs_0_, bf16[128,1152]{1,0:T(8,128)(2,1)S(1)} %collective-permute-done.4.refs_1_, bf16[128,1024]{1,0:T(8,128)(2,1)S(1)} %shard_map.89.refs_2_.refs_4_, ...), custom_call_target="tpu_custom_call" | custom-call | flops 805306368 | bytes 6422528 | tf_op jit(solution)/shard_map/pallas_call | solution.py:33
  26.4 0.9 %shard_map.92 = (f32[256,512]{1,0:T(8,128)S(1)}, f32[32,1,384]{2,1,0:T(1,128)S(1)}) custom-call(f32[256,128]{1,0:T(8,128)S(1)} %shard_map.88.refs_1_.refs_0_.info, f32[256,512]{1,0:T(8,128)S(1)} %shard_map.91.refs_1_, bf16[4096,512]{1,0:T(8,128)(2,1)S(1)} %get-tuple-element.41.weight.refs_2_, bf16[128,1024]{1,0:T(8,128)(2,1)S(1)} %collective-permute-done.10.refs_3_.refs_7_, ...), custom_call_target="tpu_custom_call" | custom-call | flops 268435456 | bytes 5947392 | tf_op jit(solution)/shard_map/pallas_call | solution.py:33
  27.9 13.6 %all_to_all.5.stats.refs_3_ = f32[32,1,384]{2,1,0:T(1,128)S(1)} all-to-all(f32[32,1,384]{2,1,0:T(1,128)S(1)} %get-tuple-element.46.refs_1_), channel_id=1, replica_groups=mesh['dp'=8,'vocab'=4] {'dp','vocab'}, dimensions={0} | all-to-all | bytes 98304 | tf_op jit(solution)/shard_map/all_to_all | solution.py:432
  41.5 1.8 %shard_map.94 = (bf16[256,512]{1,0:T(8,128)(2,1)S(1)}, f32[256,128]{1,0:T(8,128)S(1)}, bf16[64,1024]{1,0:T(8,128)(2,1)S(1)}, bf16[64,1024]{1,0:T(8,128)(2,1)S(1)...) custom-call(f32[256,128]{1,0:T(8,128)S(1)} %shard_map.88.refs_1_.ref, ...), custom_call_target="tpu_custom_call" | custom-call | flops 1073741824 | bytes 9224192 | tf_op jit(solution)/shard_map/pallas_call | solution.py:33
  43.3 0.7 %collective-permute-start.18 = (bf16[64,1024]{1,0:T(8,128)(2,1)S(1)}, bf16[64,1024]{1,0:T(8,128)(2,1)S(1)}, u32[]{:S(2)}, u32[]{:S(2)}) collective-permute-start(bf16[64,1024]{1,0:T(8,128)(2,1)S(1)} %get-tuple-element.63), channel_id=1, source_target_pairs={{0,6},{1,7},{2,4},{3,5},{4,2},{5,3},{6,0},{7,1},{8,14},{9,15},{10,... | collective-permute-start | bytes 393224 | tf_op jit(solution)/shard_map/ppermute | solution.py:326
  44.0 1.2 %collective-permute-start.19 = (bf16[64,1024]{1,0:T(8,128)(2,1)S(1)}, bf16[64,1024]{1,0:T(8,128)(2,1)S(1)}, u32[]{:S(2)}, u32[]{:S(2)}) collective-permute-start(bf16[64,1024]{1,0:T(8,128)(2,1)S(1)} %get-tuple-element.64), channel_id=1, source_target_pairs={{0,4},{1,5},{2,6},{3,7},{4,0},{5,1},{6,2},{7,3},{8,12},{9,13},{10,... | collective-permute-start | bytes 393224 | tf_op jit(solution)/shard_map/ppermute | solution.py:326
  45.3 1.6 %collective-permute-start.20 = (bf16[64,1024]{1,0:T(8,128)(2,1)S(1)}, bf16[64,1024]{1,0:T(8,128)(2,1)S(1)}, u32[]{:S(2)}, u32[]{:S(2)}) collective-permute-start(bf16[64,1024]{1,0:T(8,128)(2,1)S(1)} %get-tuple-element.65), channel_id=1, source_target_pairs={{0,2},{1,3},{2,0},{3,1},{4,6},{5,7},{6,4},{7,5},{8,10},{9,11},{10,... | collective-permute-start | bytes 393224 | tf_op jit(solution)/shard_map/ppermute | solution.py:326
  46.8 1.8 %shard_map.95 = (bf16[4096,512]{1,0:T(8,128)(2,1)}, f32[8,128]{1,0:T(8,128)S(1)}) custom-call(f32[64,1024]{1,0:T(8,128)S(1)} %get-tuple-element.52.after.kept, bf16[256,512]{1,0:T(8,128)(2,1)S(1)} %get-tuple-element.53.logit_grad, bf16[128,1152]{1,0:T(8,128)(2,1)S(1)} %get-tuple-element.40.refs_0_, bf16[128,1152]{1,0:T(8,128)(2,1)S(1)} %collective-permute-done.4.refs_1_, ...), custom_call_target="tpu_custom_call" | custom-call | flops 536870912 | bytes 5902336 | tf_op jit(solution)/shard_map/pallas_call | solution.py:33
  48.7 0.7 %collective-permute-start.14 = (bf16[64,1024]{1,0:T(8,128)(2,1)S(1)}, bf16[64,1024]{1,0:T(8,128)(2,1)S(1)}, u32[]{:S(2)}, u32[]{:S(2)}) collective-permute-start(bf16[64,1024]{1,0:T(8,128)(2,1)S(1)} %get-tuple-element.55), channel_id=1, source_target_pairs={{0,6},{1,7},{2,4},{3,5},{4,2},{5,3},{6,0},{7,1},{8,14},{9,15},{10,... | collective-permute-start | bytes 393224 | tf_op jit(solution)/shard_map/ppermute | solution.py:326
  49.4 1.2 %collective-permute-start.15 = (bf16[64,1024]{1,0:T(8,128)(2,1)S(1)}, bf16[64,1024]{1,0:T(8,128)(2,1)S(1)}, u32[]{:S(2)}, u32[]{:S(2)}) collective-permute-start(bf16[64,1024]{1,0:T(8,128)(2,1)S(1)} %get-tuple-element.56), channel_id=1, source_target_pairs={{0,4},{1,5},{2,6},{3,7},{4,0},{5,1},{6,2},{7,3},{8,12},{9,13},{10,... | collective-permute-start | bytes 393224 | tf_op jit(solution)/shard_map/ppermute | solution.py:326
  50.7 1.6 %collective-permute-start.16 = (bf16[64,1024]{1,0:T(8,128)(2,1)S(1)}, bf16[64,1024]{1,0:T(8,128)(2,1)S(1)}, u32[]{:S(2)}, u32[]{:S(2)}) collective-permute-start(bf16[64,1024]{1,0:T(8,128)(2,1)S(1)} %get-tuple-element.57), channel_id=1, source_target_pairs={{0,2},{1,3},{2,0},{3,1},{4,6},{5,7},{6,4},{7,5},{8,10},{9,11},{10,... | collective-permute-start | bytes 393224 | tf_op jit(solution)/shard_map/ppermute | solution.py:326
  52.2 1.3 %collective-permute-done.19.refs_1_ = bf16[64,1024]{1,0:T(8,128)(2,1)S(1)} collective-permute-done((bf16[64,1024]{1,0:T(8,128)(2,1)S(1)}, bf16[64,1024]{1,0:T(8,128)(2,1)S(1)}, u32[]{:S(2)}, u32[]{:S(2)}) %collective-permute-start.19) | collective-permute-done | bytes 131104 | tf_op jit(solution)/shard_map/ppermute | solution.py:326
  53.6 0.8 %collective-permute-start.21 = (bf16[32,1024]{1,0:T(8,128)(2,1)S(1)}, bf16[32,1024]{1,0:T(8,128)(2,1)S(1)}, u32[]{:S(2)}, u32[]{:S(2)}) collective-permute-start(bf16[32,1024]{1,0:T(8,128)(2,1)S(1)} %get-tuple-element.66), channel_id=1, source_target_pairs={{0,16},{1,17},{2,18},{3,19},{4,20},{5,21},{6,22},{7,23},{8,24},{9,... | collective-permute-start | bytes 196616 | tf_op jit(solution)/shard_map/ppermute | solution.py:326
  54.4 2.3 %collective-permute-start.22 = (bf16[32,1024]{1,0:T(8,128)(2,1)S(1)}, bf16[32,1024]{1,0:T(8,128)(2,1)S(1)}, u32[]{:S(2)}, u32[]{:S(2)}) collective-permute-start(bf16[32,1024]{1,0:T(8,128)(2,1)S(1)} %get-tuple-element.67), channel_id=1, source_target_pairs={{0,24},{1,25},{2,26},{3,27},{4,28},{5,29},{6,30},{7,31},{8,16},{9,... | collective-permute-start | bytes 196616 | tf_op jit(solution)/shard_map/ppermute | solution.py:326
  56.7 0.9 %collective-permute-done.15.refs_1_ = bf16[64,1024]{1,0:T(8,128)(2,1)S(1)} collective-permute-done((bf16[64,1024]{1,0:T(8,128)(2,1)S(1)}, bf16[64,1024]{1,0:T(8,128)(2,1)S(1)}, u32[]{:S(2)}, u32[]{:S(2)}) %collective-permute-start.15) | collective-permute-done | bytes 131104 | tf_op jit(solution)/shard_map/ppermute | solution.py:326
  57.7 0.7 %collective-permute-start.17 = (bf16[32,1024]{1,0:T(8,128)(2,1)S(1)}, bf16[32,1024]{1,0:T(8,128)(2,1)S(1)}, u32[]{:S(2)}, u32[]{:S(2)}) collective-permute-start(bf16[32,1024]{1,0:T(8,128)(2,1)S(1)} %get-tuple-element.62), channel_id=1, source_target_pairs={{0,8},{1,9},{2,10},{3,11},{4,12},{5,13},{6,14},{7,15},{8,0},{9,1},... | collective-permute-start | bytes 196616 | tf_op jit(solution)/shard_map/ppermute | solution.py:326
  58.3 1.8 %shard_map.98 = (bf16[4096,512]{1,0:T(8,128)(2,1)}, f32[8,128]{1,0:T(8,128)S(1)}) custom-call(f32[32,1024]{1,0:T(8,128)S(1)} %get-tuple-element.58.after.refs_0_, bf16[256,512]{1,0:T(8,128)(2,1)S(1)} %get-tuple-element.53.logit_grad, bf16[4096,512]{1,0:T(8,128)(2,1)} %get-tuple-element.59.refs_0_, ...), custom_call_target="tpu_custom_call", output_to_operand_aliasing={{0}: (2, {})} | custom-call | flops 536870912 | bytes 10145792 | tf_op jit(solution)/shard_map/pallas_call | solution.py:33
  60.2 0.7 %collective-permute-done.22.refs_3_ = bf16[32,1024]{1,0:T(8,128)(2,1)S(1)} collective-permute-done((bf16[32,1024]{1,0:T(8,128)(2,1)S(1)}, bf16[32,1024]{1,0:T(8,128)(2,1)S(1)}, u32[]{:S(2)}, u32[]{:S(2)}) %collective-permute-start.22) | collective-permute-done | bytes 65568 | tf_op jit(solution)/shard_map/ppermute | solution.py:326
  60.9 1.1 %collective-permute-done.17.refs_1_ = bf16[32,1024]{1,0:T(8,128)(2,1)S(1)} collective-permute-done((bf16[32,1024]{1,0:T(8,128)(2,1)S(1)}, bf16[32,1024]{1,0:T(8,128)(2,1)S(1)}, u32[]{:S(2)}, u32[]{:S(2)}) %collective-permute-start.17) | collective-permute-done | bytes 65568 | tf_op jit(solution)/shard_map/ppermute | solution.py:326
  62.0 1.0 %shard_map.100 = (bf16[128,1024]{1,0:T(8,128)(2,1)}, f32[1,1]{1,0:T(1,128)}) custom-call(f32[8,128]{1,0:T(8,128)S(1)} %get-tuple-element.60.last, bf16[32,128]{1,0:T(8,128)(2,1)S(1)} %get-tuple-element.61.chosen, f32[32,1024]{1,0:T(8,128)S(1)} %get-tuple-element.58.after.refs_0_, bf16[32,1024]{1,0:T(8,128)(2,1)S(1)} %collective-permute-done.17.refs_1_, ...), custom_call_target="tpu_custom_call" | custom-call | bytes 602116 | tf_op jit(solution)/shard_map/pallas_call | solution.py:33
  (33 shorter events, 2.4 us)
Async XLA Ops:
  0.6 22.2 %copy-start = (f32[32]{0:T(128)S(1)}, f32[32]{0:T(128)}, u32[]{:S(2)}) copy-start(f32[32]{0:T(128)} %param.11) | copy-start | bytes 388
  1.9 10.8 %collective-permute-start = (bf16[32,1152]{1,0:T(8,128)(2,1)S(1)}, bf16[32,1152]{1,0:T(8,128)(2,1)S(1)}, u32[]{:S(2)}, u32[]{:S(2)}) collective-permute-start(bf16[32,1152]{1,0:T(8,128)(2,1)S(1)} %get-tuple-element.37.refs_0_), channel_id=1, source_target_pairs={{0,16},{1,17},{2,18},{3,19},{4,20},{5,21},{6,22},{7,23},{8,24},{9,... | collective-permute-start | bytes 221192 | tf_op jit(solution)/shard_map/ppermute | solution.py:326
  6.0 6.8 %collective-permute-start.1 = (bf16[32,1152]{1,0:T(8,128)(2,1)S(1)}, bf16[32,1152]{1,0:T(8,128)(2,1)S(1)}, u32[]{:S(2)}, u32[]{:S(2)}) collective-permute-start(bf16[32,1152]{1,0:T(8,128)(2,1)S(1)} %get-tuple-element.37.refs_0_), channel_id=1, source_target_pairs={{0,24},{1,25},{2,26},{3,27},{4,28},{5,29},{6,30},{7,31},{8,16},{9,... | collective-permute-start | bytes 221192 | tf_op jit(solution)/shard_map/ppermute | solution.py:326
  7.3 5.4 %collective-permute-start.3 = (bf16[32,1152]{1,0:T(8,128)(2,1)S(1)}, bf16[32,1152]{1,0:T(8,128)(2,1)S(1)}, u32[]{:S(2)}, u32[]{:S(2)}) collective-permute-start(bf16[32,1152]{1,0:T(8,128)(2,1)S(1)} %get-tuple-element.37.refs_0_), channel_id=1, source_target_pairs={{0,8},{1,9},{2,10},{3,11},{4,12},{5,13},{6,14},{7,15},{8,0},{9,1},... | collective-permute-start | bytes 221192 | tf_op jit(solution)/shard_map/ppermute | solution.py:326
  7.5 5.2 %collective-permute-start.2 = (bf16[32,1024]{1,0:T(8,128)(2,1)S(1)}, bf16[32,1024]{1,0:T(8,128)(2,1)S(1)}, u32[]{:S(2)}, u32[]{:S(2)}) collective-permute-start(bf16[32,1024]{1,0:T(8,128)(2,1)S(1)} %get-tuple-element.38), channel_id=1, source_target_pairs={{0,6},{1,7},{2,4},{3,5},{4,2},{5,3},{6,0},{7,1},{8,14},{9,15},{10,... | collective-permute-start | bytes 196616 | tf_op jit(solution)/shard_map/ppermute | solution.py:326
  12.8 9.6 %collective-permute-start.4 = (bf16[128,1152]{1,0:T(8,128)(2,1)S(1)}, bf16[128,1152]{1,0:T(8,128)(2,1)S(1)}, u32[]{:S(2)}, u32[]{:S(2)}) collective-permute-start(bf16[128,1152]{1,0:T(8,128)(2,1)S(1)} %get-tuple-element.39.line), channel_id=1, source_target_pairs={{0,4},{1,5},{2,6},{3,7},{4,0},{5,1},{6,2},{7,3},{8,12},{9,13},{10,... | collective-permute-start | bytes 884744 | tf_op jit(solution)/shard_map/ppermute | solution.py:326
  14.5 8.8 %collective-permute-start.5 = (bf16[128,1024]{1,0:T(8,128)(2,1)S(1)}, bf16[128,1024]{1,0:T(8,128)(2,1)S(1)}, u32[]{:S(2)}, u32[]{:S(2)}) collective-permute-start(bf16[128,1024]{1,0:T(8,128)(2,1)S(1)} %get-tuple-element.42), channel_id=1, source_target_pairs={{0,2},{1,3},{2,0},{3,1},{4,6},{5,7},{6,4},{7,5},{8,10},{9,11},{10,... | collective-permute-start | bytes 786440 | tf_op jit(solution)/shard_map/ppermute | solution.py:326
  15.9 9.0 %collective-permute-start.6 = (bf16[96,1024]{1,0:T(8,128)(2,1)S(1)}, bf16[96,1024]{1,0:T(8,128)(2,1)S(1)}, u32[]{:S(2)}, u32[]{:S(2)}) collective-permute-start(bf16[96,1024]{1,0:T(8,128)(2,1)S(1)} %get-tuple-element.43), channel_id=1, source_target_pairs={{0,6},{1,7},{2,4},{3,5},{4,2},{5,3},{6,0},{7,1},{8,14},{9,15},{10,... | collective-permute-start | bytes 589832 | tf_op jit(solution)/shard_map/ppermute | solution.py:326
  19.2 5.7 %collective-permute-start.8 = (bf16[128,1152]{1,0:T(8,128)(2,1)S(1)}, bf16[128,1152]{1,0:T(8,128)(2,1)S(1)}, u32[]{:S(2)}, u32[]{:S(2)}) collective-permute-start(bf16[128,1152]{1,0:T(8,128)(2,1)S(1)} %get-tuple-element.40.refs_0_), channel_id=1, source_target_pairs={{0,1},{1,0},{2,3},{3,2},{4,5},{5,4},{6,7},{7,6},{8,9},{9,8},{10,11... | collective-permute-start | bytes 884744 | tf_op jit(solution)/shard_map/ppermute | solution.py:326
  22.4 2.6 %collective-permute-start.9 = (bf16[128,1152]{1,0:T(8,128)(2,1)S(1)}, bf16[128,1152]{1,0:T(8,128)(2,1)S(1)}, u32[]{:S(2)}, u32[]{:S(2)}) collective-permute-start(bf16[128,1152]{1,0:T(8,128)(2,1)S(1)} %collective-permute-done.4.refs_1_), channel_id=1, source_target_pairs={{0,1},{1,0},{2,3},{3,2},{4,5},{5,4},{6,7},{7,6},{8,9},{9,8},{10,11... | collective-permute-start | bytes 884744 | tf_op jit(solution)/shard_map/ppermute | solution.py:326
  22.4 1.7 %collective-permute-start.7 = (bf16[32,1024]{1,0:T(8,128)(2,1)S(1)}, bf16[32,1024]{1,0:T(8,128)(2,1)S(1)}, u32[]{:S(2)}, u32[]{:S(2)}) collective-permute-start(bf16[32,1024]{1,0:T(8,128)(2,1)S(1)} %collective-permute-done.2.refs_3_.refs_5_), channel_id=1, source_target_pairs={{0,1},{1,0},{2,3},{3,2},{4,5},{5,4},{6,7},{7,6},{8,9},{9,8},{10,11... | collective-permute-start | bytes 196616 | tf_op jit(solution)/shard_map/ppermute | solution.py:326
  23.3 3.1 %collective-permute-start.10 = (bf16[128,1024]{1,0:T(8,128)(2,1)S(1)}, bf16[128,1024]{1,0:T(8,128)(2,1)S(1)}, u32[]{:S(2)}, u32[]{:S(2)}) collective-permute-start(bf16[128,1024]{1,0:T(8,128)(2,1)S(1)} %shard_map.89.refs_2_.refs_4_), channel_id=1, source_target_pairs={{0,1},{1,0},{2,3},{3,2},{4,5},{5,4},{6,7},{7,6},{8,9},{9,8},{10,11... | collective-permute-start | bytes 786440 | tf_op jit(solution)/shard_map/ppermute | solution.py:326
  24.9 1.4 %collective-permute-start.11 = (bf16[96,1024]{1,0:T(8,128)(2,1)S(1)}, bf16[96,1024]{1,0:T(8,128)(2,1)S(1)}, u32[]{:S(2)}, u32[]{:S(2)}) collective-permute-start(bf16[96,1024]{1,0:T(8,128)(2,1)S(1)} %shard_map.90.refs_4_.refs_6_), channel_id=1, source_target_pairs={{0,1},{1,0},{2,3},{3,2},{4,5},{5,4},{6,7},{7,6},{8,9},{9,8},{10,11... | collective-permute-start | bytes 589832 | tf_op jit(solution)/shard_map/ppermute | solution.py:326
  27.3 14.2 %collective-permute-start.13 = (bf16[2048,512]{1,0:T(8,128)(2,1)S(1)}, bf16[2048,512]{1,0:T(8,128)(2,1)S(1)}, u32[]{:S(2)}, u32[]{:S(2)}) collective-permute-start(bf16[2048,512]{1,0:T(8,128)(2,1)S(1)} %shard_map.93), channel_id=1, source_target_pairs={{0,1},{1,0},{2,3},{3,2},{4,5},{5,4},{6,7},{7,6},{8,9},{9,8},{10,11... | collective-permute-start | bytes 6291464 | tf_op jit(solution)/shard_map/ppermute | solution.py:326
  27.5 14.0 %collective-permute-start.12 = (f32[256,512]{1,0:T(8,128)S(1)}, f32[256,512]{1,0:T(8,128)S(1)}, u32[]{:S(2)}, u32[]{:S(2)}) collective-permute-start(f32[256,512]{1,0:T(8,128)S(1)} %get-tuple-element.44.mine), channel_id=1, source_target_pairs={{0,1},{1,0},{2,3},{3,2},{4,5},{5,4},{6,7},{7,6},{8,9},{9,8},{10,11... | collective-permute-start | bytes 1572872 | tf_op jit(solution)/shard_map/ppermute | solution.py:326
  43.3 7.4 %collective-permute-start.18 = (bf16[64,1024]{1,0:T(8,128)(2,1)S(1)}, bf16[64,1024]{1,0:T(8,128)(2,1)S(1)}, u32[]{:S(2)}, u32[]{:S(2)}) collective-permute-start(bf16[64,1024]{1,0:T(8,128)(2,1)S(1)} %get-tuple-element.63), channel_id=1, source_target_pairs={{0,6},{1,7},{2,4},{3,5},{4,2},{5,3},{6,0},{7,1},{8,14},{9,15},{10,... | collective-permute-start | bytes 393224 | tf_op jit(solution)/shard_map/ppermute | solution.py:326
  44.0 9.5 %collective-permute-start.19 = (bf16[64,1024]{1,0:T(8,128)(2,1)S(1)}, bf16[64,1024]{1,0:T(8,128)(2,1)S(1)}, u32[]{:S(2)}, u32[]{:S(2)}) collective-permute-start(bf16[64,1024]{1,0:T(8,128)(2,1)S(1)} %get-tuple-element.64), channel_id=1, source_target_pairs={{0,4},{1,5},{2,6},{3,7},{4,0},{5,1},{6,2},{7,3},{8,12},{9,13},{10,... | collective-permute-start | bytes 393224 | tf_op jit(solution)/shard_map/ppermute | solution.py:326
  45.3 8.3 %collective-permute-start.20 = (bf16[64,1024]{1,0:T(8,128)(2,1)S(1)}, bf16[64,1024]{1,0:T(8,128)(2,1)S(1)}, u32[]{:S(2)}, u32[]{:S(2)}) collective-permute-start(bf16[64,1024]{1,0:T(8,128)(2,1)S(1)} %get-tuple-element.65), channel_id=1, source_target_pairs={{0,2},{1,3},{2,0},{3,1},{4,6},{5,7},{6,4},{7,5},{8,10},{9,11},{10,... | collective-permute-start | bytes 393224 | tf_op jit(solution)/shard_map/ppermute | solution.py:326
  48.7 8.1 %collective-permute-start.14 = (bf16[64,1024]{1,0:T(8,128)(2,1)S(1)}, bf16[64,1024]{1,0:T(8,128)(2,1)S(1)}, u32[]{:S(2)}, u32[]{:S(2)}) collective-permute-start(bf16[64,1024]{1,0:T(8,128)(2,1)S(1)} %get-tuple-element.55), channel_id=1, source_target_pairs={{0,6},{1,7},{2,4},{3,5},{4,2},{5,3},{6,0},{7,1},{8,14},{9,15},{10,... | collective-permute-start | bytes 393224 | tf_op jit(solution)/shard_map/ppermute | solution.py:326
  49.4 8.2 %collective-permute-start.15 = (bf16[64,1024]{1,0:T(8,128)(2,1)S(1)}, bf16[64,1024]{1,0:T(8,128)(2,1)S(1)}, u32[]{:S(2)}, u32[]{:S(2)}) collective-permute-start(bf16[64,1024]{1,0:T(8,128)(2,1)S(1)} %get-tuple-element.56), channel_id=1, source_target_pairs={{0,4},{1,5},{2,6},{3,7},{4,0},{5,1},{6,2},{7,3},{8,12},{9,13},{10,... | collective-permute-start | bytes 393224 | tf_op jit(solution)/shard_map/ppermute | solution.py:326
  50.7 6.9 %collective-permute-start.16 = (bf16[64,1024]{1,0:T(8,128)(2,1)S(1)}, bf16[64,1024]{1,0:T(8,128)(2,1)S(1)}, u32[]{:S(2)}, u32[]{:S(2)}) collective-permute-start(bf16[64,1024]{1,0:T(8,128)(2,1)S(1)} %get-tuple-element.57), channel_id=1, source_target_pairs={{0,2},{1,3},{2,0},{3,1},{4,6},{5,7},{6,4},{7,5},{8,10},{9,11},{10,... | collective-permute-start | bytes 393224 | tf_op jit(solution)/shard_map/ppermute | solution.py:326
  53.6 6.5 %collective-permute-start.21 = (bf16[32,1024]{1,0:T(8,128)(2,1)S(1)}, bf16[32,1024]{1,0:T(8,128)(2,1)S(1)}, u32[]{:S(2)}, u32[]{:S(2)}) collective-permute-start(bf16[32,1024]{1,0:T(8,128)(2,1)S(1)} %get-tuple-element.66), channel_id=1, source_target_pairs={{0,16},{1,17},{2,18},{3,19},{4,20},{5,21},{6,22},{7,23},{8,24},{9,... | collective-permute-start | bytes 196616 | tf_op jit(solution)/shard_map/ppermute | solution.py:326
  54.4 6.5 %collective-permute-start.22 = (bf16[32,1024]{1,0:T(8,128)(2,1)S(1)}, bf16[32,1024]{1,0:T(8,128)(2,1)S(1)}, u32[]{:S(2)}, u32[]{:S(2)}) collective-permute-start(bf16[32,1024]{1,0:T(8,128)(2,1)S(1)} %get-tuple-element.67), channel_id=1, source_target_pairs={{0,24},{1,25},{2,26},{3,27},{4,28},{5,29},{6,30},{7,31},{8,16},{9,... | collective-permute-start | bytes 196616 | tf_op jit(solution)/shard_map/ppermute | solution.py:326
  57.7 4.3 %collective-permute-start.17 = (bf16[32,1024]{1,0:T(8,128)(2,1)S(1)}, bf16[32,1024]{1,0:T(8,128)(2,1)S(1)}, u32[]{:S(2)}, u32[]{:S(2)}) collective-permute-start(bf16[32,1024]{1,0:T(8,128)(2,1)S(1)} %get-tuple-element.62), channel_id=1, source_target_pairs={{0,8},{1,9},{2,10},{3,11},{4,12},{5,13},{6,14},{7,15},{8,0},{9,1},... | collective-permute-start | bytes 196616 | tf_op jit(solution)/shard_map/ppermute | solution.py:326

commit v22 on v21

--- a/solution.py
+++ b/solution.py
@@ -259,7 +259,8 @@
 
 
 def weight_kernel(blocks, counts, skipped, after, logit_grad, *refs):
-    pieces, (out, last, done, sems) = refs[skipped:-4], refs[-4:]
+    results = 5 if skipped else 4
+    pieces, (out, last, *loss, done, sems) = refs[skipped:-results], refs[-results:]
     rank = coordinates()[0]
     width = done.shape[0] // len(blocks)
     copies = []
@@ -279,10 +280,8 @@
     if skipped:
         info, table, stats = refs[1:4]
         hits = jnp.sum(stats[:, :, info.shape[0]:], axis=0)
-        loss = jnp.sum(info[:, 0:1] * table[:, 0:1]) - hits[0, 0]
-        last[...] = jnp.full(last.shape, loss, jnp.float32)
-    else:
-        last[...] = jnp.zeros_like(last)
+        loss[0][0, 0] = jnp.sum(info[:, 0:1] * table[:, 0:1]) - hits[0, 0]
+    last[...] = jnp.zeros_like(last)
     for copy in copies:
         copy.wait()
 
@@ -295,16 +294,24 @@
         out[...] = total[place * CAP:(place + 1) * CAP].astype(out.dtype)
 
 
-def unpack_kernel(last, chosen, *refs):
-    out, loss = refs[-2:]
-    loss[0, 0] = last[0, 0]
-    total = sum(ref[...].astype(jnp.float32) for ref in refs[:-2])
-    out[...] = lax.dot_general(
-        chosen[...],
-        total.astype(jnp.bfloat16),
-        (((0,), (0,)), ((), ())),
-        preferred_element_type=jnp.float32,
-    ).astype(jnp.bfloat16)
+def unpack_kernel(after, chosen, *refs):
+    ends, (out, held, sems) = refs[:-3], refs[-3:]
+    half = held.shape[1] // 2
+    copies = []
+    for place in range(2):
+        lanes = pl.ds(place * half, half)
+        total = sum(ref[:, lanes].astype(jnp.float32) for ref in ends)
+        held[:, lanes] = lax.dot_general(
+            chosen[...],
+            total.astype(jnp.bfloat16),
+            (((0,), (0,)), ((), ())),
+            preferred_element_type=jnp.float32,
+        ).astype(jnp.bfloat16)
+        copy = pltpu.make_async_copy(held.at[:, lanes], out.at[:, lanes], sems.at[place])
+        copy.start()
+        copies.append(copy)
+    for copy in copies:
+        copy.wait()
 
 
 def body(dps, ranks, hidden, weight, loss_mask, target_ids, turn_ids, advantages):
@@ -449,8 +456,9 @@
             (after, logit_grad, *extra, *chosen_rows),
             [ANY, VMEM] + [HBM] * (len(extra) > 0)
             + [VMEM] * (max(len(extra) - 1, 0) + len(chosen_rows)),
-            (shape((depth, columns), bf16), shape((8, 128), f32)),
-            (HBM, VMEM),
+            (shape((depth, columns), bf16), shape((8, 128), f32))
+            + (shape((1, 1), f32),) * (len(extra) > 0),
+            (HBM, VMEM) + (SMEM,) * (len(extra) > 0),
             [
                 pltpu.VMEM((depth // 2, columns), bf16),
                 pltpu.SemaphoreType.DMA((ranks // 2,)),
@@ -486,13 +494,14 @@
         )
         for z, value in enumerate(parts_z):
             ends[near + z] = send(value, z=near + z) if near + z else value
-    weight_grad, last = weight_part(ranks // 2, parts_z[0], weight_grad, info, table, stats)
-    hidden_grad, loss = call(
+    weight_grad, last, loss = weight_part(ranks // 2, parts_z[0], weight_grad, info, table, stats)
+    hidden_grad = call(
         unpack_kernel,
         (last, chosen, *ends),
-        [VMEM] * (2 + len(ends)),
-        (shape((tokens, width), bf16), shape((1, 1), f32)),
-        (VMEM, SMEM),
+        [ANY] + [VMEM] * (1 + len(ends)),
+        shape((tokens, width), bf16),
+        HBM,
+        [pltpu.VMEM((tokens, width), bf16), pltpu.SemaphoreType.DMA((2,))],
     )
     return loss[0, 0], hidden_grad, weight_grad
 

time: 63.1 us -> 63.1 us (level)
  no operation moved by 1% of the time
where the time goes in v22:
time: 63.1 us; the launch traced here: 62.9 us
  starting transfers between devices  23.8 us (38%)
  blocking collectives  13.6 us (22%)
  Pallas kernels  13.3 us (21%)
  waiting for transfers between devices  11.3 us (18%)
  between operations  0.8 us (1%)
    ppermute x23, starting transfers between devices, send(): return lax.ppermute(value, AXES, pairs)  23.8 us
    all_to_all x1, blocking collectives, body(): stats = lax.all_to_all(stats, AXES, 0, 0)  13.6 us
    pallas_call x16, Pallas kernels, call(): pl.pallas_call(kernel, out_shape=out_shape, in_specs=in_specs, out_specs=...  13.3 us
    ppermute x23, waiting for transfers between devices, send(): return lax.ppermute(value, AXES, pairs)  11.3 us
  transfers between devices with their start and end apart: 23, of which 9 were waited for; matrix products, arithmetic and copies ran while one was open for 0% of the time, Pallas kernels for 13%

profile of v22, /device:TPU:0, one launch (start us, length us, event | category | flops | bytes accessed | tf_op | source)
XLA Modules:
  0.0 62.9 jit_solution(14840142244382346590)
XLA Ops:
  0.6 1.2 %shard_map.85 = (bf16[32,1152]{1,0:T(8,128)(2,1)S(1)}, bf16[32,1024]{1,0:T(8,128)(2,1)S(1)}, bf16[32,128]{1,0:T(8,128)(2,1)S(1)}) custom-call(bf16[128,1024]{1,0:T(8,128)(2,1)} %hidden_hbm.1, s32[1,128]{1,0:T(1,128)} %bitcast.6, s32[1,128]{1,0:T(1,128)} %bitcast.7, s32[1,128]{1,0:T(1,128)} %bitcast.8), custom_call_target="tpu_custom_call" | custom-call | bytes 411136 | tf_op jit(solution)/shard_map/pallas_call | solution.py:33
  1.9 4.1 %collective-permute-start = (bf16[32,1152]{1,0:T(8,128)(2,1)S(1)}, bf16[32,1152]{1,0:T(8,128)(2,1)S(1)}, u32[]{:S(2)}, u32[]{:S(2)}) collective-permute-start(bf16[32,1152]{1,0:T(8,128)(2,1)S(1)} %get-tuple-element.36.refs_0_), channel_id=1, source_target_pairs={{0,16},{1,17},{2,18},{3,19},{4,20},{5,21},{6,22},{7,23},{8,24},{9,... | collective-permute-start | bytes 221192 | tf_op jit(solution)/shard_map/ppermute | solution.py:333
  6.0 1.3 %collective-permute-start.1 = (bf16[32,1152]{1,0:T(8,128)(2,1)S(1)}, bf16[32,1152]{1,0:T(8,128)(2,1)S(1)}, u32[]{:S(2)}, u32[]{:S(2)}) collective-permute-start(bf16[32,1152]{1,0:T(8,128)(2,1)S(1)} %get-tuple-element.36.refs_0_), channel_id=1, source_target_pairs={{0,24},{1,25},{2,26},{3,27},{4,28},{5,29},{6,30},{7,31},{8,16},{9,... | collective-permute-start | bytes 221192 | tf_op jit(solution)/shard_map/ppermute | solution.py:333
  7.5 2.4 %collective-permute-start.2 = (bf16[32,1024]{1,0:T(8,128)(2,1)S(1)}, bf16[32,1024]{1,0:T(8,128)(2,1)S(1)}, u32[]{:S(2)}, u32[]{:S(2)}) collective-permute-start(bf16[32,1024]{1,0:T(8,128)(2,1)S(1)} %get-tuple-element.37), channel_id=1, source_target_pairs={{0,6},{1,7},{2,4},{3,5},{4,2},{5,3},{6,0},{7,1},{8,14},{9,15},{10,... | collective-permute-start | bytes 196616 | tf_op jit(solution)/shard_map/ppermute | solution.py:333
  10.0 2.7 %collective-permute-done.2.refs_3_.refs_5_ = bf16[32,1024]{1,0:T(8,128)(2,1)S(1)} collective-permute-done((bf16[32,1024]{1,0:T(8,128)(2,1)S(1)}, bf16[32,1024]{1,0:T(8,128)(2,1)S(1)}, u32[]{:S(2)}, u32[]{:S(2)}) %collective-permute-start.2) | collective-permute-done | bytes 65568 | tf_op jit(solution)/shard_map/ppermute | solution.py:333
  12.8 1.7 %collective-permute-start.4 = (bf16[128,1152]{1,0:T(8,128)(2,1)S(1)}, bf16[128,1152]{1,0:T(8,128)(2,1)S(1)}, u32[]{:S(2)}, u32[]{:S(2)}) collective-permute-start(bf16[128,1152]{1,0:T(8,128)(2,1)S(1)} %get-tuple-element.38.line), channel_id=1, source_target_pairs={{0,4},{1,5},{2,6},{3,7},{4,0},{5,1},{6,2},{7,3},{8,12},{9,13},{10,... | collective-permute-start | bytes 884744 | tf_op jit(solution)/shard_map/ppermute | solution.py:333
  14.5 1.5 %collective-permute-start.5 = (bf16[128,1024]{1,0:T(8,128)(2,1)S(1)}, bf16[128,1024]{1,0:T(8,128)(2,1)S(1)}, u32[]{:S(2)}, u32[]{:S(2)}) collective-permute-start(bf16[128,1024]{1,0:T(8,128)(2,1)S(1)} %get-tuple-element.41), channel_id=1, source_target_pairs={{0,2},{1,3},{2,0},{3,1},{4,6},{5,7},{6,4},{7,5},{8,10},{9,11},{10,... | collective-permute-start | bytes 786440 | tf_op jit(solution)/shard_map/ppermute | solution.py:333
  16.3 2.9 %shard_map.87 = (bf16[4096,512]{1,0:T(8,128)(2,1)S(1)}, bf16[2048,512]{1,0:T(8,128)(2,1)S(1)}, bf16[128,1152]{1,0:T(8,128)(2,1)S(1)}) custom-call(bf16[128,1152]{1,0:T(8,128)(2,1)S(1)} %get-tuple-element.38.line, bf16[4096,512]{1,0:T(8,128)(2,1)} %weight.1), custom_call_target="tpu_custom_call" | custom-call | bytes 11075584 | tf_op jit(solution)/shard_map/pallas_call | solution.py:33
  19.3 3.1 %collective-permute-done.4.refs_1_ = bf16[128,1152]{1,0:T(8,128)(2,1)S(1)} collective-permute-done((bf16[128,1152]{1,0:T(8,128)(2,1)S(1)}, bf16[128,1152]{1,0:T(8,128)(2,1)S(1)}, u32[]{:S(2)}, u32[]{:S(2)}) %collective-permute-start.4) | collective-permute-done | bytes 294944 | tf_op jit(solution)/shard_map/ppermute | solution.py:333
  22.4 0.5 collective-permute-start.7
  23.4 0.7 %collective-permute-done.7.refs_1_.refs_4_.refs_8_ = bf16[32,1024]{1,0:T(8,128)(2,1)S(1)} collective-permute-done((bf16[32,1024]{1,0:T(8,128)(2,1)S(1)}, bf16[32,1024]{1,0:T(8,128)(2,1)S(1)}, u32[]{:S(2)}, u32[]{:S(2)}) %collective-permute-start.7) | collective-permute-done | bytes 65568 | tf_op jit(solution)/shard_map/ppermute | solution.py:333
  24.0 0.9 %collective-permute-done.6.refs_0_ = bf16[96,1024]{1,0:T(8,128)(2,1)S(1)} collective-permute-done((bf16[96,1024]{1,0:T(8,128)(2,1)S(1)}, bf16[96,1024]{1,0:T(8,128)(2,1)S(1)}, u32[]{:S(2)}, u32[]{:S(2)}) %collective-permute-start.6) | collective-permute-done | bytes 196640 | tf_op jit(solution)/shard_map/ppermute | solution.py:333
  25.0 1.0 %shard_map.91.refs_1_ = f32[256,512]{1,0:T(8,128)S(1)} custom-call(bf16[4096,512]{1,0:T(8,128)(2,1)S(1)} %get-tuple-element.40.weight.refs_2_, bf16[128,1152]{1,0:T(8,128)(2,1)S(1)} %get-tuple-element.39.refs_0_, bf16[128,1152]{1,0:T(8,128)(2,1)S(1)} %collective-permute-done.4.refs_1_, bf16[128,1024]{1,0:T(8,128)(2,1)S(1)} %shard_map.89.refs_2_.refs_4_, ...), custom_call_target="tpu_custom_call" | custom-call | flops 805306368 | bytes 6422528 | tf_op jit(solution)/shard_map/pallas_call | solution.py:33
  25.9 0.4 collective-permute-done.11.refs_5_.refs_9_
  26.4 0.9 %shard_map.92 = (f32[256,512]{1,0:T(8,128)S(1)}, f32[32,1,384]{2,1,0:T(1,128)S(1)}) custom-call(f32[256,128]{1,0:T(8,128)S(1)} %shard_map.88.refs_1_.refs_0_.info, f32[256,512]{1,0:T(8,128)S(1)} %shard_map.91.refs_1_, bf16[4096,512]{1,0:T(8,128)(2,1)S(1)} %get-tuple-element.40.weight.refs_2_, bf16[128,1024]{1,0:T(8,128)(2,1)S(1)} %collective-permute-done.10.refs_3_.refs_7_, ...), custom_call_target="tpu_custom_call" | custom-call | flops 268435456 | bytes 5947392 | tf_op jit(solution)/shard_map/pallas_call | solution.py:33
  27.9 13.6 %all_to_all.5.stats.refs_3_ = f32[32,1,384]{2,1,0:T(1,128)S(1)} all-to-all(f32[32,1,384]{2,1,0:T(1,128)S(1)} %get-tuple-element.45.refs_1_), channel_id=1, replica_groups=mesh['dp'=8,'vocab'=4] {'dp','vocab'}, dimensions={0} | all-to-all | bytes 98304 | tf_op jit(solution)/shard_map/all_to_all | solution.py:439
  41.5 1.8 %shard_map.94 = (bf16[256,512]{1,0:T(8,128)(2,1)S(1)}, f32[256,128]{1,0:T(8,128)S(1)}, bf16[64,1024]{1,0:T(8,128)(2,1)S(1)}, bf16[64,1024]{1,0:T(8,128)(2,1)S(1)...) custom-call(f32[256,128]{1,0:T(8,128)S(1)} %shard_map.88.refs_1_.ref, ...), custom_call_target="tpu_custom_call" | custom-call | flops 1073741824 | bytes 9224192 | tf_op jit(solution)/shard_map/pallas_call | solution.py:33
  43.3 0.7 %collective-permute-start.18 = (bf16[64,1024]{1,0:T(8,128)(2,1)S(1)}, bf16[64,1024]{1,0:T(8,128)(2,1)S(1)}, u32[]{:S(2)}, u32[]{:S(2)}) collective-permute-start(bf16[64,1024]{1,0:T(8,128)(2,1)S(1)} %get-tuple-element.63), channel_id=1, source_target_pairs={{0,6},{1,7},{2,4},{3,5},{4,2},{5,3},{6,0},{7,1},{8,14},{9,15},{10,... | collective-permute-start | bytes 393224 | tf_op jit(solution)/shard_map/ppermute | solution.py:333
  44.0 1.2 %collective-permute-start.19 = (bf16[64,1024]{1,0:T(8,128)(2,1)S(1)}, bf16[64,1024]{1,0:T(8,128)(2,1)S(1)}, u32[]{:S(2)}, u32[]{:S(2)}) collective-permute-start(bf16[64,1024]{1,0:T(8,128)(2,1)S(1)} %get-tuple-element.64), channel_id=1, source_target_pairs={{0,4},{1,5},{2,6},{3,7},{4,0},{5,1},{6,2},{7,3},{8,12},{9,13},{10,... | collective-permute-start | bytes 393224 | tf_op jit(solution)/shard_map/ppermute | solution.py:333
  45.3 1.6 %collective-permute-start.20 = (bf16[64,1024]{1,0:T(8,128)(2,1)S(1)}, bf16[64,1024]{1,0:T(8,128)(2,1)S(1)}, u32[]{:S(2)}, u32[]{:S(2)}) collective-permute-start(bf16[64,1024]{1,0:T(8,128)(2,1)S(1)} %get-tuple-element.65), channel_id=1, source_target_pairs={{0,2},{1,3},{2,0},{3,1},{4,6},{5,7},{6,4},{7,5},{8,10},{9,11},{10,... | collective-permute-start | bytes 393224 | tf_op jit(solution)/shard_map/ppermute | solution.py:333
  46.8 1.8 %shard_map.95 = (bf16[4096,512]{1,0:T(8,128)(2,1)}, f32[8,128]{1,0:T(8,128)S(1)}) custom-call(f32[64,1024]{1,0:T(8,128)S(1)} %get-tuple-element.51.after.kept, bf16[256,512]{1,0:T(8,128)(2,1)S(1)} %get-tuple-element.52.logit_grad, bf16[128,1152]{1,0:T(8,128)(2,1)S(1)} %get-tuple-element.39.refs_0_, bf16[128,1152]{1,0:T(8,128)(2,1)S(1)} %collective-permute-done.4.refs_1_, ...), custom_call_target="tpu_custom_call" | custom-call | flops 536870912 | bytes 5902336 | tf_op jit(solution)/shard_map/pallas_call | solution.py:33
  48.7 0.7 %collective-permute-start.14 = (bf16[64,1024]{1,0:T(8,128)(2,1)S(1)}, bf16[64,1024]{1,0:T(8,128)(2,1)S(1)}, u32[]{:S(2)}, u32[]{:S(2)}) collective-permute-start(bf16[64,1024]{1,0:T(8,128)(2,1)S(1)} %get-tuple-element.54), channel_id=1, source_target_pairs={{0,6},{1,7},{2,4},{3,5},{4,2},{5,3},{6,0},{7,1},{8,14},{9,15},{10,... | collective-permute-start | bytes 393224 | tf_op jit(solution)/shard_map/ppermute | solution.py:333
  49.4 1.2 %collective-permute-start.15 = (bf16[64,1024]{1,0:T(8,128)(2,1)S(1)}, bf16[64,1024]{1,0:T(8,128)(2,1)S(1)}, u32[]{:S(2)}, u32[]{:S(2)}) collective-permute-start(bf16[64,1024]{1,0:T(8,128)(2,1)S(1)} %get-tuple-element.55), channel_id=1, source_target_pairs={{0,4},{1,5},{2,6},{3,7},{4,0},{5,1},{6,2},{7,3},{8,12},{9,13},{10,... | collective-permute-start | bytes 393224 | tf_op jit(solution)/shard_map/ppermute | solution.py:333
  50.7 1.6 %collective-permute-start.16 = (bf16[64,1024]{1,0:T(8,128)(2,1)S(1)}, bf16[64,1024]{1,0:T(8,128)(2,1)S(1)}, u32[]{:S(2)}, u32[]{:S(2)}) collective-permute-start(bf16[64,1024]{1,0:T(8,128)(2,1)S(1)} %get-tuple-element.56), channel_id=1, source_target_pairs={{0,2},{1,3},{2,0},{3,1},{4,6},{5,7},{6,4},{7,5},{8,10},{9,11},{10,... | collective-permute-start | bytes 393224 | tf_op jit(solution)/shard_map/ppermute | solution.py:333
  52.2 1.3 %collective-permute-done.19.refs_1_ = bf16[64,1024]{1,0:T(8,128)(2,1)S(1)} collective-permute-done((bf16[64,1024]{1,0:T(8,128)(2,1)S(1)}, bf16[64,1024]{1,0:T(8,128)(2,1)S(1)}, u32[]{:S(2)}, u32[]{:S(2)}) %collective-permute-start.19) | collective-permute-done | bytes 131104 | tf_op jit(solution)/shard_map/ppermute | solution.py:333
  53.6 0.8 %collective-permute-start.21 = (bf16[32,1024]{1,0:T(8,128)(2,1)S(1)}, bf16[32,1024]{1,0:T(8,128)(2,1)S(1)}, u32[]{:S(2)}, u32[]{:S(2)}) collective-permute-start(bf16[32,1024]{1,0:T(8,128)(2,1)S(1)} %get-tuple-element.66), channel_id=1, source_target_pairs={{0,16},{1,17},{2,18},{3,19},{4,20},{5,21},{6,22},{7,23},{8,24},{9,... | collective-permute-start | bytes 196616 | tf_op jit(solution)/shard_map/ppermute | solution.py:333
  54.4 2.3 %collective-permute-start.22 = (bf16[32,1024]{1,0:T(8,128)(2,1)S(1)}, bf16[32,1024]{1,0:T(8,128)(2,1)S(1)}, u32[]{:S(2)}, u32[]{:S(2)}) collective-permute-start(bf16[32,1024]{1,0:T(8,128)(2,1)S(1)} %get-tuple-element.67), channel_id=1, source_target_pairs={{0,24},{1,25},{2,26},{3,27},{4,28},{5,29},{6,30},{7,31},{8,16},{9,... | collective-permute-start | bytes 196616 | tf_op jit(solution)/shard_map/ppermute | solution.py:333
  56.7 0.9 %collective-permute-done.15.refs_1_ = bf16[64,1024]{1,0:T(8,128)(2,1)S(1)} collective-permute-done((bf16[64,1024]{1,0:T(8,128)(2,1)S(1)}, bf16[64,1024]{1,0:T(8,128)(2,1)S(1)}, u32[]{:S(2)}, u32[]{:S(2)}) %collective-permute-start.15) | collective-permute-done | bytes 131104 | tf_op jit(solution)/shard_map/ppermute | solution.py:333
  57.7 0.7 %collective-permute-start.17 = (bf16[32,1024]{1,0:T(8,128)(2,1)S(1)}, bf16[32,1024]{1,0:T(8,128)(2,1)S(1)}, u32[]{:S(2)}, u32[]{:S(2)}) collective-permute-start(bf16[32,1024]{1,0:T(8,128)(2,1)S(1)} %get-tuple-element.62), channel_id=1, source_target_pairs={{0,8},{1,9},{2,10},{3,11},{4,12},{5,13},{6,14},{7,15},{8,0},{9,1},... | collective-permute-start | bytes 196616 | tf_op jit(solution)/shard_map/ppermute | solution.py:333
  58.3 2.3 %shard_map.98 = (bf16[4096,512]{1,0:T(8,128)(2,1)}, f32[8,128]{1,0:T(8,128)S(1)}, f32[1,1]{1,0:T(1,128)}) custom-call(f32[32,1024]{1,0:T(8,128)S(1)} %get-tuple-element.57.after.refs_0_, bf16[256,512]{1,0:T(8,128)(2,1)S(1)} %get-tuple-element.52.logit_grad, bf16[4096,512]{1,0:T(8,128)(2,1)} %get-tuple-element.58.refs_0_, ...), custom_call_target="tpu_custom_call", output_to_operand_aliasing={{0}: (2, {})} | custom-call | flops 536870912 | bytes 10145796 | tf_op jit(solution)/shard_map/pallas_call | solution.py:33
  60.9 1.1 %collective-permute-done.17.refs_1_ = bf16[32,1024]{1,0:T(8,128)(2,1)S(1)} collective-permute-done((bf16[32,1024]{1,0:T(8,128)(2,1)S(1)}, bf16[32,1024]{1,0:T(8,128)(2,1)S(1)}, u32[]{:S(2)}, u32[]{:S(2)}) %collective-permute-start.17) | collective-permute-done | bytes 65568 | tf_op jit(solution)/shard_map/ppermute | solution.py:333
  62.0 0.9 %shard_map.100 = bf16[128,1024]{1,0:T(8,128)(2,1)} custom-call(f32[8,128]{1,0:T(8,128)S(1)} %get-tuple-element.60.after, bf16[32,128]{1,0:T(8,128)(2,1)S(1)} %get-tuple-element.61.chosen, f32[32,1024]{1,0:T(8,128)S(1)} %get-tuple-element.57.after.refs_0_, bf16[32,1024]{1,0:T(8,128)(2,1)S(1)} %collective-permute-done.17.refs_1_, ...), custom_call_target="tpu_custom_call" | custom-call | bytes 602112 | tf_op jit(solution)/shard_map/pallas_call | solution.py:33
  (33 shorter events, 2.2 us)
Async XLA Ops:
  0.6 22.2 %copy-start = (f32[32]{0:T(128)S(1)}, f32[32]{0:T(128)}, u32[]{:S(2)}) copy-start(f32[32]{0:T(128)} %param.11) | copy-start | bytes 388
  1.9 10.8 %collective-permute-start = (bf16[32,1152]{1,0:T(8,128)(2,1)S(1)}, bf16[32,1152]{1,0:T(8,128)(2,1)S(1)}, u32[]{:S(2)}, u32[]{:S(2)}) collective-permute-start(bf16[32,1152]{1,0:T(8,128)(2,1)S(1)} %get-tuple-element.36.refs_0_), channel_id=1, source_target_pairs={{0,16},{1,17},{2,18},{3,19},{4,20},{5,21},{6,22},{7,23},{8,24},{9,... | collective-permute-start | bytes 221192 | tf_op jit(solution)/shard_map/ppermute | solution.py:333
  6.0 6.8 %collective-permute-start.1 = (bf16[32,1152]{1,0:T(8,128)(2,1)S(1)}, bf16[32,1152]{1,0:T(8,128)(2,1)S(1)}, u32[]{:S(2)}, u32[]{:S(2)}) collective-permute-start(bf16[32,1152]{1,0:T(8,128)(2,1)S(1)} %get-tuple-element.36.refs_0_), channel_id=1, source_target_pairs={{0,24},{1,25},{2,26},{3,27},{4,28},{5,29},{6,30},{7,31},{8,16},{9,... | collective-permute-start | bytes 221192 | tf_op jit(solution)/shard_map/ppermute | solution.py:333
  7.3 5.4 %collective-permute-start.3 = (bf16[32,1152]{1,0:T(8,128)(2,1)S(1)}, bf16[32,1152]{1,0:T(8,128)(2,1)S(1)}, u32[]{:S(2)}, u32[]{:S(2)}) collective-permute-start(bf16[32,1152]{1,0:T(8,128)(2,1)S(1)} %get-tuple-element.36.refs_0_), channel_id=1, source_target_pairs={{0,8},{1,9},{2,10},{3,11},{4,12},{5,13},{6,14},{7,15},{8,0},{9,1},... | collective-permute-start | bytes 221192 | tf_op jit(solution)/shard_map/ppermute | solution.py:333
  7.5 5.2 %collective-permute-start.2 = (bf16[32,1024]{1,0:T(8,128)(2,1)S(1)}, bf16[32,1024]{1,0:T(8,128)(2,1)S(1)}, u32[]{:S(2)}, u32[]{:S(2)}) collective-permute-start(bf16[32,1024]{1,0:T(8,128)(2,1)S(1)} %get-tuple-element.37), channel_id=1, source_target_pairs={{0,6},{1,7},{2,4},{3,5},{4,2},{5,3},{6,0},{7,1},{8,14},{9,15},{10,... | collective-permute-start | bytes 196616 | tf_op jit(solution)/shard_map/ppermute | solution.py:333
  12.8 9.6 %collective-permute-start.4 = (bf16[128,1152]{1,0:T(8,128)(2,1)S(1)}, bf16[128,1152]{1,0:T(8,128)(2,1)S(1)}, u32[]{:S(2)}, u32[]{:S(2)}) collective-permute-start(bf16[128,1152]{1,0:T(8,128)(2,1)S(1)} %get-tuple-element.38.line), channel_id=1, source_target_pairs={{0,4},{1,5},{2,6},{3,7},{4,0},{5,1},{6,2},{7,3},{8,12},{9,13},{10,... | collective-permute-start | bytes 884744 | tf_op jit(solution)/shard_map/ppermute | solution.py:333
  14.5 8.8 %collective-permute-start.5 = (bf16[128,1024]{1,0:T(8,128)(2,1)S(1)}, bf16[128,1024]{1,0:T(8,128)(2,1)S(1)}, u32[]{:S(2)}, u32[]{:S(2)}) collective-permute-start(bf16[128,1024]{1,0:T(8,128)(2,1)S(1)} %get-tuple-element.41), channel_id=1, source_target_pairs={{0,2},{1,3},{2,0},{3,1},{4,6},{5,7},{6,4},{7,5},{8,10},{9,11},{10,... | collective-permute-start | bytes 786440 | tf_op jit(solution)/shard_map/ppermute | solution.py:333
  15.9 9.0 %collective-permute-start.6 = (bf16[96,1024]{1,0:T(8,128)(2,1)S(1)}, bf16[96,1024]{1,0:T(8,128)(2,1)S(1)}, u32[]{:S(2)}, u32[]{:S(2)}) collective-permute-start(bf16[96,1024]{1,0:T(8,128)(2,1)S(1)} %get-tuple-element.42), channel_id=1, source_target_pairs={{0,6},{1,7},{2,4},{3,5},{4,2},{5,3},{6,0},{7,1},{8,14},{9,15},{10,... | collective-permute-start | bytes 589832 | tf_op jit(solution)/shard_map/ppermute | solution.py:333
  19.2 5.7 %collective-permute-start.8 = (bf16[128,1152]{1,0:T(8,128)(2,1)S(1)}, bf16[128,1152]{1,0:T(8,128)(2,1)S(1)}, u32[]{:S(2)}, u32[]{:S(2)}) collective-permute-start(bf16[128,1152]{1,0:T(8,128)(2,1)S(1)} %get-tuple-element.39.refs_0_), channel_id=1, source_target_pairs={{0,1},{1,0},{2,3},{3,2},{4,5},{5,4},{6,7},{7,6},{8,9},{9,8},{10,11... | collective-permute-start | bytes 884744 | tf_op jit(solution)/shard_map/ppermute | solution.py:333
  22.4 2.6 %collective-permute-start.9 = (bf16[128,1152]{1,0:T(8,128)(2,1)S(1)}, bf16[128,1152]{1,0:T(8,128)(2,1)S(1)}, u32[]{:S(2)}, u32[]{:S(2)}) collective-permute-start(bf16[128,1152]{1,0:T(8,128)(2,1)S(1)} %collective-permute-done.4.refs_1_), channel_id=1, source_target_pairs={{0,1},{1,0},{2,3},{3,2},{4,5},{5,4},{6,7},{7,6},{8,9},{9,8},{10,11... | collective-permute-start | bytes 884744 | tf_op jit(solution)/shard_map/ppermute | solution.py:333
  22.4 1.7 %collective-permute-start.7 = (bf16[32,1024]{1,0:T(8,128)(2,1)S(1)}, bf16[32,1024]{1,0:T(8,128)(2,1)S(1)}, u32[]{:S(2)}, u32[]{:S(2)}) collective-permute-start(bf16[32,1024]{1,0:T(8,128)(2,1)S(1)} %collective-permute-done.2.refs_3_.refs_5_), channel_id=1, source_target_pairs={{0,1},{1,0},{2,3},{3,2},{4,5},{5,4},{6,7},{7,6},{8,9},{9,8},{10,11... | collective-permute-start | bytes 196616 | tf_op jit(solution)/shard_map/ppermute | solution.py:333
  23.3 3.1 %collective-permute-start.10 = (bf16[128,1024]{1,0:T(8,128)(2,1)S(1)}, bf16[128,1024]{1,0:T(8,128)(2,1)S(1)}, u32[]{:S(2)}, u32[]{:S(2)}) collective-permute-start(bf16[128,1024]{1,0:T(8,128)(2,1)S(1)} %shard_map.89.refs_2_.refs_4_), channel_id=1, source_target_pairs={{0,1},{1,0},{2,3},{3,2},{4,5},{5,4},{6,7},{7,6},{8,9},{9,8},{10,11... | collective-permute-start | bytes 786440 | tf_op jit(solution)/shard_map/ppermute | solution.py:333
  24.9 1.4 %collective-permute-start.11 = (bf16[96,1024]{1,0:T(8,128)(2,1)S(1)}, bf16[96,1024]{1,0:T(8,128)(2,1)S(1)}, u32[]{:S(2)}, u32[]{:S(2)}) collective-permute-start(bf16[96,1024]{1,0:T(8,128)(2,1)S(1)} %shard_map.90.refs_4_.refs_6_), channel_id=1, source_target_pairs={{0,1},{1,0},{2,3},{3,2},{4,5},{5,4},{6,7},{7,6},{8,9},{9,8},{10,11... | collective-permute-start | bytes 589832 | tf_op jit(solution)/shard_map/ppermute | solution.py:333
  27.3 14.2 %collective-permute-start.13 = (bf16[2048,512]{1,0:T(8,128)(2,1)S(1)}, bf16[2048,512]{1,0:T(8,128)(2,1)S(1)}, u32[]{:S(2)}, u32[]{:S(2)}) collective-permute-start(bf16[2048,512]{1,0:T(8,128)(2,1)S(1)} %shard_map.93), channel_id=1, source_target_pairs={{0,1},{1,0},{2,3},{3,2},{4,5},{5,4},{6,7},{7,6},{8,9},{9,8},{10,11... | collective-permute-start | bytes 6291464 | tf_op jit(solution)/shard_map/ppermute | solution.py:333
  27.5 14.0 %collective-permute-start.12 = (f32[256,512]{1,0:T(8,128)S(1)}, f32[256,512]{1,0:T(8,128)S(1)}, u32[]{:S(2)}, u32[]{:S(2)}) collective-permute-start(f32[256,512]{1,0:T(8,128)S(1)} %get-tuple-element.43.mine), channel_id=1, source_target_pairs={{0,1},{1,0},{2,3},{3,2},{4,5},{5,4},{6,7},{7,6},{8,9},{9,8},{10,11... | collective-permute-start | bytes 1572872 | tf_op jit(solution)/shard_map/ppermute | solution.py:333
  43.3 7.4 %collective-permute-start.18 = (bf16[64,1024]{1,0:T(8,128)(2,1)S(1)}, bf16[64,1024]{1,0:T(8,128)(2,1)S(1)}, u32[]{:S(2)}, u32[]{:S(2)}) collective-permute-start(bf16[64,1024]{1,0:T(8,128)(2,1)S(1)} %get-tuple-element.63), channel_id=1, source_target_pairs={{0,6},{1,7},{2,4},{3,5},{4,2},{5,3},{6,0},{7,1},{8,14},{9,15},{10,... | collective-permute-start | bytes 393224 | tf_op jit(solution)/shard_map/ppermute | solution.py:333
  44.0 9.5 %collective-permute-start.19 = (bf16[64,1024]{1,0:T(8,128)(2,1)S(1)}, bf16[64,1024]{1,0:T(8,128)(2,1)S(1)}, u32[]{:S(2)}, u32[]{:S(2)}) collective-permute-start(bf16[64,1024]{1,0:T(8,128)(2,1)S(1)} %get-tuple-element.64), channel_id=1, source_target_pairs={{0,4},{1,5},{2,6},{3,7},{4,0},{5,1},{6,2},{7,3},{8,12},{9,13},{10,... | collective-permute-start | bytes 393224 | tf_op jit(solution)/shard_map/ppermute | solution.py:333
  45.3 8.3 %collective-permute-start.20 = (bf16[64,1024]{1,0:T(8,128)(2,1)S(1)}, bf16[64,1024]{1,0:T(8,128)(2,1)S(1)}, u32[]{:S(2)}, u32[]{:S(2)}) collective-permute-start(bf16[64,1024]{1,0:T(8,128)(2,1)S(1)} %get-tuple-element.65), channel_id=1, source_target_pairs={{0,2},{1,3},{2,0},{3,1},{4,6},{5,7},{6,4},{7,5},{8,10},{9,11},{10,... | collective-permute-start | bytes 393224 | tf_op jit(solution)/shard_map/ppermute | solution.py:333
  48.7 8.1 %collective-permute-start.14 = (bf16[64,1024]{1,0:T(8,128)(2,1)S(1)}, bf16[64,1024]{1,0:T(8,128)(2,1)S(1)}, u32[]{:S(2)}, u32[]{:S(2)}) collective-permute-start(bf16[64,1024]{1,0:T(8,128)(2,1)S(1)} %get-tuple-element.54), channel_id=1, source_target_pairs={{0,6},{1,7},{2,4},{3,5},{4,2},{5,3},{6,0},{7,1},{8,14},{9,15},{10,... | collective-permute-start | bytes 393224 | tf_op jit(solution)/shard_map/ppermute | solution.py:333
  49.4 8.2 %collective-permute-start.15 = (bf16[64,1024]{1,0:T(8,128)(2,1)S(1)}, bf16[64,1024]{1,0:T(8,128)(2,1)S(1)}, u32[]{:S(2)}, u32[]{:S(2)}) collective-permute-start(bf16[64,1024]{1,0:T(8,128)(2,1)S(1)} %get-tuple-element.55), channel_id=1, source_target_pairs={{0,4},{1,5},{2,6},{3,7},{4,0},{5,1},{6,2},{7,3},{8,12},{9,13},{10,... | collective-permute-start | bytes 393224 | tf_op jit(solution)/shard_map/ppermute | solution.py:333
  50.7 6.9 %collective-permute-start.16 = (bf16[64,1024]{1,0:T(8,128)(2,1)S(1)}, bf16[64,1024]{1,0:T(8,128)(2,1)S(1)}, u32[]{:S(2)}, u32[]{:S(2)}) collective-permute-start(bf16[64,1024]{1,0:T(8,128)(2,1)S(1)} %get-tuple-element.56), channel_id=1, source_target_pairs={{0,2},{1,3},{2,0},{3,1},{4,6},{5,7},{6,4},{7,5},{8,10},{9,11},{10,... | collective-permute-start | bytes 393224 | tf_op jit(solution)/shard_map/ppermute | solution.py:333
  53.6 7.1 %collective-permute-start.21 = (bf16[32,1024]{1,0:T(8,128)(2,1)S(1)}, bf16[32,1024]{1,0:T(8,128)(2,1)S(1)}, u32[]{:S(2)}, u32[]{:S(2)}) collective-permute-start(bf16[32,1024]{1,0:T(8,128)(2,1)S(1)} %get-tuple-element.66), channel_id=1, source_target_pairs={{0,16},{1,17},{2,18},{3,19},{4,20},{5,21},{6,22},{7,23},{8,24},{9,... | collective-permute-start | bytes 196616 | tf_op jit(solution)/shard_map/ppermute | solution.py:333
  54.4 6.5 %collective-permute-start.22 = (bf16[32,1024]{1,0:T(8,128)(2,1)S(1)}, bf16[32,1024]{1,0:T(8,128)(2,1)S(1)}, u32[]{:S(2)}, u32[]{:S(2)}) collective-permute-start(bf16[32,1024]{1,0:T(8,128)(2,1)S(1)} %get-tuple-element.67), channel_id=1, source_target_pairs={{0,24},{1,25},{2,26},{3,27},{4,28},{5,29},{6,30},{7,31},{8,16},{9,... | collective-permute-start | bytes 196616 | tf_op jit(solution)/shard_map/ppermute | solution.py:333
  57.7 4.3 %collective-permute-start.17 = (bf16[32,1024]{1,0:T(8,128)(2,1)S(1)}, bf16[32,1024]{1,0:T(8,128)(2,1)S(1)}, u32[]{:S(2)}, u32[]{:S(2)}) collective-permute-start(bf16[32,1024]{1,0:T(8,128)(2,1)S(1)} %get-tuple-element.62), channel_id=1, source_target_pairs={{0,8},{1,9},{2,10},{3,11},{4,12},{5,13},{6,14},{7,15},{8,0},{9,1},... | collective-permute-start | bytes 196616 | tf_op jit(solution)/shard_map/ppermute | solution.py:333

commit v23 on v21

--- a/solution.py
+++ b/solution.py
@@ -441,8 +441,7 @@
         (VMEM,) * (2 + 2 * ranks),
         flops=flops,
     )
-    def weight_part(first, after, *extra):
-        blocks = range(first, first + ranks // 2)
+    def weight_part(blocks, after, *extra):
         chosen_rows = rows_of(blocks)
         return call(
             functools.partial(weight_kernel, blocks, counts_of(blocks), len(extra)),
@@ -452,15 +451,15 @@
             (shape((depth, columns), bf16), shape((8, 128), f32)),
             (HBM, VMEM),
             [
-                pltpu.VMEM((depth // 2, columns), bf16),
-                pltpu.SemaphoreType.DMA((ranks // 2,)),
+                pltpu.VMEM((len(blocks) * width, columns), bf16),
+                pltpu.SemaphoreType.DMA((len(blocks),)),
             ],
-            flops=flops // 2,
+            flops=flops * len(blocks) // ranks,
             aliases={2: 0} if extra else {},
         )
 
     far_values, near_values = list(going[:ranks]), list(going[ranks:])
-    weight_grad, finished = weight_part(0, far_values[-1])
+    weight_grad, finished = weight_part(range(ranks // 4), far_values[-1])
     near_values[:-1] = call(
         gate_kernel,
         (*near_values[:-1], finished),
@@ -486,7 +485,9 @@
         )
         for z, value in enumerate(parts_z):
             ends[near + z] = send(value, z=near + z) if near + z else value
-    weight_grad, last = weight_part(ranks // 2, parts_z[0], weight_grad, info, table, stats)
+    weight_grad, last = weight_part(
+        range(ranks // 4, ranks), parts_z[0], weight_grad, info, table, stats
+    )
     hidden_grad, loss = call(
         unpack_kernel,
         (last, chosen, *ends),

time: 63.1 us -> 63.1 us (level)
  transfers between devices with their start and end apart: 23 -> 23, of which waited for: 9 -> 10; matrix products, arithmetic and copies ran while one was open for 0% -> 0% of each run, Pallas kernels for 13% -> 13%
where the time goes in v23:
time: 63.1 us; the launch traced here: 63 us
  starting transfers between devices  23.4 us (37%)
  blocking collectives  13.6 us (22%)
  Pallas kernels  12.9 us (20%)
  waiting for transfers between devices  12.2 us (19%)
  between operations  0.8 us (1%)
    ppermute x23, starting transfers between devices, send(): return lax.ppermute(value, AXES, pairs)  23.4 us
    all_to_all x1, blocking collectives, body(): stats = lax.all_to_all(stats, AXES, 0, 0)  13.6 us
    pallas_call x16, Pallas kernels, call(): pl.pallas_call(kernel, out_shape=out_shape, in_specs=in_specs, out_specs=...  12.9 us
    ppermute x23, waiting for transfers between devices, send(): return lax.ppermute(value, AXES, pairs)  12.2 us
  transfers between devices with their start and end apart: 23, of which 10 were waited for; matrix products, arithmetic and copies ran while one was open for 0% of the time, Pallas kernels for 13%

profile of v23, /device:TPU:0, one launch (start us, length us, event | category | flops | bytes accessed | tf_op | source)
XLA Modules:
  0.0 63.0 jit_solution(48438775546485904)
XLA Ops:
  0.6 1.2 %shard_map.85 = (bf16[32,1152]{1,0:T(8,128)(2,1)S(1)}, bf16[32,1024]{1,0:T(8,128)(2,1)S(1)}, bf16[32,128]{1,0:T(8,128)(2,1)S(1)}) custom-call(bf16[128,1024]{1,0:T(8,128)(2,1)} %hidden_hbm.1, s32[1,128]{1,0:T(1,128)} %bitcast.6, s32[1,128]{1,0:T(1,128)} %bitcast.7, s32[1,128]{1,0:T(1,128)} %bitcast.8), custom_call_target="tpu_custom_call" | custom-call | bytes 411136 | tf_op jit(solution)/shard_map/pallas_call | solution.py:33
  1.9 4.1 %collective-permute-start = (bf16[32,1152]{1,0:T(8,128)(2,1)S(1)}, bf16[32,1152]{1,0:T(8,128)(2,1)S(1)}, u32[]{:S(2)}, u32[]{:S(2)}) collective-permute-start(bf16[32,1152]{1,0:T(8,128)(2,1)S(1)} %get-tuple-element.37.refs_0_), channel_id=1, source_target_pairs={{0,16},{1,17},{2,18},{3,19},{4,20},{5,21},{6,22},{7,23},{8,24},{9,... | collective-permute-start | bytes 221192 | tf_op jit(solution)/shard_map/ppermute | solution.py:326
  6.0 1.3 %collective-permute-start.1 = (bf16[32,1152]{1,0:T(8,128)(2,1)S(1)}, bf16[32,1152]{1,0:T(8,128)(2,1)S(1)}, u32[]{:S(2)}, u32[]{:S(2)}) collective-permute-start(bf16[32,1152]{1,0:T(8,128)(2,1)S(1)} %get-tuple-element.37.refs_0_), channel_id=1, source_target_pairs={{0,24},{1,25},{2,26},{3,27},{4,28},{5,29},{6,30},{7,31},{8,16},{9,... | collective-permute-start | bytes 221192 | tf_op jit(solution)/shard_map/ppermute | solution.py:326
  7.5 2.4 %collective-permute-start.2 = (bf16[32,1024]{1,0:T(8,128)(2,1)S(1)}, bf16[32,1024]{1,0:T(8,128)(2,1)S(1)}, u32[]{:S(2)}, u32[]{:S(2)}) collective-permute-start(bf16[32,1024]{1,0:T(8,128)(2,1)S(1)} %get-tuple-element.38), channel_id=1, source_target_pairs={{0,6},{1,7},{2,4},{3,5},{4,2},{5,3},{6,0},{7,1},{8,14},{9,15},{10,... | collective-permute-start | bytes 196616 | tf_op jit(solution)/shard_map/ppermute | solution.py:326
  10.0 2.7 %collective-permute-done.2.refs_3_.refs_7_ = bf16[32,1024]{1,0:T(8,128)(2,1)S(1)} collective-permute-done((bf16[32,1024]{1,0:T(8,128)(2,1)S(1)}, bf16[32,1024]{1,0:T(8,128)(2,1)S(1)}, u32[]{:S(2)}, u32[]{:S(2)}) %collective-permute-start.2) | collective-permute-done | bytes 65568 | tf_op jit(solution)/shard_map/ppermute | solution.py:326
  12.8 1.7 %collective-permute-start.4 = (bf16[128,1152]{1,0:T(8,128)(2,1)S(1)}, bf16[128,1152]{1,0:T(8,128)(2,1)S(1)}, u32[]{:S(2)}, u32[]{:S(2)}) collective-permute-start(bf16[128,1152]{1,0:T(8,128)(2,1)S(1)} %get-tuple-element.39.line), channel_id=1, source_target_pairs={{0,4},{1,5},{2,6},{3,7},{4,0},{5,1},{6,2},{7,3},{8,12},{9,13},{10,... | collective-permute-start | bytes 884744 | tf_op jit(solution)/shard_map/ppermute | solution.py:326
  14.5 1.5 %collective-permute-start.5 = (bf16[128,1024]{1,0:T(8,128)(2,1)S(1)}, bf16[128,1024]{1,0:T(8,128)(2,1)S(1)}, u32[]{:S(2)}, u32[]{:S(2)}) collective-permute-start(bf16[128,1024]{1,0:T(8,128)(2,1)S(1)} %get-tuple-element.42), channel_id=1, source_target_pairs={{0,2},{1,3},{2,0},{3,1},{4,6},{5,7},{6,4},{7,5},{8,10},{9,11},{10,... | collective-permute-start | bytes 786440 | tf_op jit(solution)/shard_map/ppermute | solution.py:326
  16.3 2.9 %shard_map.87 = (bf16[4096,512]{1,0:T(8,128)(2,1)S(1)}, bf16[2048,512]{1,0:T(8,128)(2,1)S(1)}, bf16[128,1152]{1,0:T(8,128)(2,1)S(1)}) custom-call(bf16[128,1152]{1,0:T(8,128)(2,1)S(1)} %get-tuple-element.39.line, bf16[4096,512]{1,0:T(8,128)(2,1)} %weight.1), custom_call_target="tpu_custom_call" | custom-call | bytes 11075584 | tf_op jit(solution)/shard_map/pallas_call | solution.py:33
  19.3 3.1 %collective-permute-done.4.refs_1_ = bf16[128,1152]{1,0:T(8,128)(2,1)S(1)} collective-permute-done((bf16[128,1152]{1,0:T(8,128)(2,1)S(1)}, bf16[128,1152]{1,0:T(8,128)(2,1)S(1)}, u32[]{:S(2)}, u32[]{:S(2)}) %collective-permute-start.4) | collective-permute-done | bytes 294944 | tf_op jit(solution)/shard_map/ppermute | solution.py:326
  22.4 0.5 collective-permute-start.7
  23.4 0.7 %collective-permute-done.7.refs_1_.refs_4_.refs_10_ = bf16[32,1024]{1,0:T(8,128)(2,1)S(1)} collective-permute-done((bf16[32,1024]{1,0:T(8,128)(2,1)S(1)}, bf16[32,1024]{1,0:T(8,128)(2,1)S(1)}, u32[]{:S(2)}, u32[]{:S(2)}) %collective-permute-start.7) | collective-permute-done | bytes 65568 | tf_op jit(solution)/shard_map/ppermute | solution.py:326
  24.0 0.9 %collective-permute-done.6.refs_0_ = bf16[96,1024]{1,0:T(8,128)(2,1)S(1)} collective-permute-done((bf16[96,1024]{1,0:T(8,128)(2,1)S(1)}, bf16[96,1024]{1,0:T(8,128)(2,1)S(1)}, u32[]{:S(2)}, u32[]{:S(2)}) %collective-permute-start.6) | collective-permute-done | bytes 196640 | tf_op jit(solution)/shard_map/ppermute | solution.py:326
  25.0 1.0 %shard_map.91.refs_1_ = f32[256,512]{1,0:T(8,128)S(1)} custom-call(bf16[4096,512]{1,0:T(8,128)(2,1)S(1)} %get-tuple-element.41.weight.refs_2_, bf16[128,1152]{1,0:T(8,128)(2,1)S(1)} %get-tuple-element.40.refs_0_, bf16[128,1152]{1,0:T(8,128)(2,1)S(1)} %collective-permute-done.4.refs_1_, bf16[128,1024]{1,0:T(8,128)(2,1)S(1)} %shard_map.89.refs_2_.refs_6_, ...), custom_call_target="tpu_custom_call" | custom-call | flops 805306368 | bytes 6422528 | tf_op jit(solution)/shard_map/pallas_call | solution.py:33
  25.9 0.4 collective-permute-done.11.refs_5_.refs_11_
  26.4 0.9 %shard_map.92 = (f32[256,512]{1,0:T(8,128)S(1)}, f32[32,1,384]{2,1,0:T(1,128)S(1)}) custom-call(f32[256,128]{1,0:T(8,128)S(1)} %shard_map.88.refs_1_.refs_0_.info, f32[256,512]{1,0:T(8,128)S(1)} %shard_map.91.refs_1_, bf16[4096,512]{1,0:T(8,128)(2,1)S(1)} %get-tuple-element.41.weight.refs_2_, bf16[128,1024]{1,0:T(8,128)(2,1)S(1)} %collective-permute-done.10.refs_3_.refs_9_, ...), custom_call_target="tpu_custom_call" | custom-call | flops 268435456 | bytes 5947392 | tf_op jit(solution)/shard_map/pallas_call | solution.py:33
  27.9 13.6 %all_to_all.5.stats.refs_3_ = f32[32,1,384]{2,1,0:T(1,128)S(1)} all-to-all(f32[32,1,384]{2,1,0:T(1,128)S(1)} %get-tuple-element.46.refs_1_), channel_id=1, replica_groups=mesh['dp'=8,'vocab'=4] {'dp','vocab'}, dimensions={0} | all-to-all | bytes 98304 | tf_op jit(solution)/shard_map/all_to_all | solution.py:432
  41.5 1.8 %shard_map.94 = (bf16[256,512]{1,0:T(8,128)(2,1)S(1)}, f32[256,128]{1,0:T(8,128)S(1)}, bf16[64,1024]{1,0:T(8,128)(2,1)S(1)}, bf16[64,1024]{1,0:T(8,128)(2,1)S(1)...) custom-call(f32[256,128]{1,0:T(8,128)S(1)} %shard_map.88.refs_1_.ref, ...), custom_call_target="tpu_custom_call" | custom-call | flops 1073741824 | bytes 9224192 | tf_op jit(solution)/shard_map/pallas_call | solution.py:33
  43.3 0.7 %collective-permute-start.18 = (bf16[64,1024]{1,0:T(8,128)(2,1)S(1)}, bf16[64,1024]{1,0:T(8,128)(2,1)S(1)}, u32[]{:S(2)}, u32[]{:S(2)}) collective-permute-start(bf16[64,1024]{1,0:T(8,128)(2,1)S(1)} %get-tuple-element.63), channel_id=1, source_target_pairs={{0,6},{1,7},{2,4},{3,5},{4,2},{5,3},{6,0},{7,1},{8,14},{9,15},{10,... | collective-permute-start | bytes 393224 | tf_op jit(solution)/shard_map/ppermute | solution.py:326
  44.0 1.2 %collective-permute-start.19 = (bf16[64,1024]{1,0:T(8,128)(2,1)S(1)}, bf16[64,1024]{1,0:T(8,128)(2,1)S(1)}, u32[]{:S(2)}, u32[]{:S(2)}) collective-permute-start(bf16[64,1024]{1,0:T(8,128)(2,1)S(1)} %get-tuple-element.64), channel_id=1, source_target_pairs={{0,4},{1,5},{2,6},{3,7},{4,0},{5,1},{6,2},{7,3},{8,12},{9,13},{10,... | collective-permute-start | bytes 393224 | tf_op jit(solution)/shard_map/ppermute | solution.py:326
  45.3 1.6 %collective-permute-start.20 = (bf16[64,1024]{1,0:T(8,128)(2,1)S(1)}, bf16[64,1024]{1,0:T(8,128)(2,1)S(1)}, u32[]{:S(2)}, u32[]{:S(2)}) collective-permute-start(bf16[64,1024]{1,0:T(8,128)(2,1)S(1)} %get-tuple-element.65), channel_id=1, source_target_pairs={{0,2},{1,3},{2,0},{3,1},{4,6},{5,7},{6,4},{7,5},{8,10},{9,11},{10,... | collective-permute-start | bytes 393224 | tf_op jit(solution)/shard_map/ppermute | solution.py:326
  46.8 1.4 %shard_map.95 = (bf16[4096,512]{1,0:T(8,128)(2,1)}, f32[8,128]{1,0:T(8,128)S(1)}) custom-call(f32[64,1024]{1,0:T(8,128)S(1)} %get-tuple-element.52.after.kept, bf16[256,512]{1,0:T(8,128)(2,1)S(1)} %get-tuple-element.53.logit_grad, bf16[128,1152]{1,0:T(8,128)(2,1)S(1)} %get-tuple-element.40.refs_0_, bf16[128,1152]{1,0:T(8,128)(2,1)S(1)} %collective-permute-done.4.refs_1_), custom_call_target="tpu_custom_call" | custom-call | flops 268435456 | bytes 5312512 | tf_op jit(solution)/shard_map/pallas_call | solution.py:33
  48.3 0.7 %collective-permute-start.14 = (bf16[64,1024]{1,0:T(8,128)(2,1)S(1)}, bf16[64,1024]{1,0:T(8,128)(2,1)S(1)}, u32[]{:S(2)}, u32[]{:S(2)}) collective-permute-start(bf16[64,1024]{1,0:T(8,128)(2,1)S(1)} %get-tuple-element.55), channel_id=1, source_target_pairs={{0,6},{1,7},{2,4},{3,5},{4,2},{5,3},{6,0},{7,1},{8,14},{9,15},{10,... | collective-permute-start | bytes 393224 | tf_op jit(solution)/shard_map/ppermute | solution.py:326
  49.0 1.2 %collective-permute-start.15 = (bf16[64,1024]{1,0:T(8,128)(2,1)S(1)}, bf16[64,1024]{1,0:T(8,128)(2,1)S(1)}, u32[]{:S(2)}, u32[]{:S(2)}) collective-permute-start(bf16[64,1024]{1,0:T(8,128)(2,1)S(1)} %get-tuple-element.56), channel_id=1, source_target_pairs={{0,4},{1,5},{2,6},{3,7},{4,0},{5,1},{6,2},{7,3},{8,12},{9,13},{10,... | collective-permute-start | bytes 393224 | tf_op jit(solution)/shard_map/ppermute | solution.py:326
  50.6 1.2 %collective-permute-start.16 = (bf16[64,1024]{1,0:T(8,128)(2,1)S(1)}, bf16[64,1024]{1,0:T(8,128)(2,1)S(1)}, u32[]{:S(2)}, u32[]{:S(2)}) collective-permute-start(bf16[64,1024]{1,0:T(8,128)(2,1)S(1)} %get-tuple-element.57), channel_id=1, source_target_pairs={{0,2},{1,3},{2,0},{3,1},{4,6},{5,7},{6,4},{7,5},{8,10},{9,11},{10,... | collective-permute-start | bytes 393224 | tf_op jit(solution)/shard_map/ppermute | solution.py:326
  51.9 1.7 %collective-permute-done.19.refs_1_ = bf16[64,1024]{1,0:T(8,128)(2,1)S(1)} collective-permute-done((bf16[64,1024]{1,0:T(8,128)(2,1)S(1)}, bf16[64,1024]{1,0:T(8,128)(2,1)S(1)}, u32[]{:S(2)}, u32[]{:S(2)}) %collective-permute-start.19) | collective-permute-done | bytes 131104 | tf_op jit(solution)/shard_map/ppermute | solution.py:326
  53.6 0.7 %collective-permute-start.21 = (bf16[32,1024]{1,0:T(8,128)(2,1)S(1)}, bf16[32,1024]{1,0:T(8,128)(2,1)S(1)}, u32[]{:S(2)}, u32[]{:S(2)}) collective-permute-start(bf16[32,1024]{1,0:T(8,128)(2,1)S(1)} %get-tuple-element.66), channel_id=1, source_target_pairs={{0,16},{1,17},{2,18},{3,19},{4,20},{5,21},{6,22},{7,23},{8,24},{9,... | collective-permute-start | bytes 196616 | tf_op jit(solution)/shard_map/ppermute | solution.py:326
  54.3 2.3 %collective-permute-start.22 = (bf16[32,1024]{1,0:T(8,128)(2,1)S(1)}, bf16[32,1024]{1,0:T(8,128)(2,1)S(1)}, u32[]{:S(2)}, u32[]{:S(2)}) collective-permute-start(bf16[32,1024]{1,0:T(8,128)(2,1)S(1)} %get-tuple-element.67), channel_id=1, source_target_pairs={{0,24},{1,25},{2,26},{3,27},{4,28},{5,29},{6,30},{7,31},{8,16},{9,... | collective-permute-start | bytes 196616 | tf_op jit(solution)/shard_map/ppermute | solution.py:326
  56.7 0.9 %collective-permute-done.15.refs_1_ = bf16[64,1024]{1,0:T(8,128)(2,1)S(1)} collective-permute-done((bf16[64,1024]{1,0:T(8,128)(2,1)S(1)}, bf16[64,1024]{1,0:T(8,128)(2,1)S(1)}, u32[]{:S(2)}, u32[]{:S(2)}) %collective-permute-start.15) | collective-permute-done | bytes 131104 | tf_op jit(solution)/shard_map/ppermute | solution.py:326
  57.7 0.7 %collective-permute-start.17 = (bf16[32,1024]{1,0:T(8,128)(2,1)S(1)}, bf16[32,1024]{1,0:T(8,128)(2,1)S(1)}, u32[]{:S(2)}, u32[]{:S(2)}) collective-permute-start(bf16[32,1024]{1,0:T(8,128)(2,1)S(1)} %get-tuple-element.62), channel_id=1, source_target_pairs={{0,8},{1,9},{2,10},{3,11},{4,12},{5,13},{6,14},{7,15},{8,0},{9,1},... | collective-permute-start | bytes 196616 | tf_op jit(solution)/shard_map/ppermute | solution.py:326
  58.3 2.2 %shard_map.98 = (bf16[4096,512]{1,0:T(8,128)(2,1)}, f32[8,128]{1,0:T(8,128)S(1)}) custom-call(f32[32,1024]{1,0:T(8,128)S(1)} %get-tuple-element.58.after.refs_0_, bf16[256,512]{1,0:T(8,128)(2,1)S(1)} %get-tuple-element.53.logit_grad, bf16[4096,512]{1,0:T(8,128)(2,1)} %get-tuple-element.59.refs_0_, ...), custom_call_target="tpu_custom_call", output_to_operand_aliasing={{0}: (2, {})} | custom-call | flops 805306368 | bytes 10735616 | tf_op jit(solution)/shard_map/pallas_call | solution.py:33
  60.8 1.2 %collective-permute-done.17.refs_1_ = bf16[32,1024]{1,0:T(8,128)(2,1)S(1)} collective-permute-done((bf16[32,1024]{1,0:T(8,128)(2,1)S(1)}, bf16[32,1024]{1,0:T(8,128)(2,1)S(1)}, u32[]{:S(2)}, u32[]{:S(2)}) %collective-permute-start.17) | collective-permute-done | bytes 65568 | tf_op jit(solution)/shard_map/ppermute | solution.py:326
  62.0 1.0 %shard_map.100 = (bf16[128,1024]{1,0:T(8,128)(2,1)}, f32[1,1]{1,0:T(1,128)}) custom-call(f32[8,128]{1,0:T(8,128)S(1)} %get-tuple-element.60.last, bf16[32,128]{1,0:T(8,128)(2,1)S(1)} %get-tuple-element.61.chosen, f32[32,1024]{1,0:T(8,128)S(1)} %get-tuple-element.58.after.refs_0_, bf16[32,1024]{1,0:T(8,128)(2,1)S(1)} %collective-permute-done.17.refs_1_, ...), custom_call_target="tpu_custom_call" | custom-call | bytes 602116 | tf_op jit(solution)/shard_map/pallas_call | solution.py:33
  (33 shorter events, 2.6 us)
Async XLA Ops:
  0.6 22.2 %copy-start = (f32[32]{0:T(128)S(1)}, f32[32]{0:T(128)}, u32[]{:S(2)}) copy-start(f32[32]{0:T(128)} %param.11) | copy-start | bytes 388
  1.9 10.8 %collective-permute-start = (bf16[32,1152]{1,0:T(8,128)(2,1)S(1)}, bf16[32,1152]{1,0:T(8,128)(2,1)S(1)}, u32[]{:S(2)}, u32[]{:S(2)}) collective-permute-start(bf16[32,1152]{1,0:T(8,128)(2,1)S(1)} %get-tuple-element.37.refs_0_), channel_id=1, source_target_pairs={{0,16},{1,17},{2,18},{3,19},{4,20},{5,21},{6,22},{7,23},{8,24},{9,... | collective-permute-start | bytes 221192 | tf_op jit(solution)/shard_map/ppermute | solution.py:326
  6.0 6.8 %collective-permute-start.1 = (bf16[32,1152]{1,0:T(8,128)(2,1)S(1)}, bf16[32,1152]{1,0:T(8,128)(2,1)S(1)}, u32[]{:S(2)}, u32[]{:S(2)}) collective-permute-start(bf16[32,1152]{1,0:T(8,128)(2,1)S(1)} %get-tuple-element.37.refs_0_), channel_id=1, source_target_pairs={{0,24},{1,25},{2,26},{3,27},{4,28},{5,29},{6,30},{7,31},{8,16},{9,... | collective-permute-start | bytes 221192 | tf_op jit(solution)/shard_map/ppermute | solution.py:326
  7.3 5.4 %collective-permute-start.3 = (bf16[32,1152]{1,0:T(8,128)(2,1)S(1)}, bf16[32,1152]{1,0:T(8,128)(2,1)S(1)}, u32[]{:S(2)}, u32[]{:S(2)}) collective-permute-start(bf16[32,1152]{1,0:T(8,128)(2,1)S(1)} %get-tuple-element.37.refs_0_), channel_id=1, source_target_pairs={{0,8},{1,9},{2,10},{3,11},{4,12},{5,13},{6,14},{7,15},{8,0},{9,1},... | collective-permute-start | bytes 221192 | tf_op jit(solution)/shard_map/ppermute | solution.py:326
  7.5 5.2 %collective-permute-start.2 = (bf16[32,1024]{1,0:T(8,128)(2,1)S(1)}, bf16[32,1024]{1,0:T(8,128)(2,1)S(1)}, u32[]{:S(2)}, u32[]{:S(2)}) collective-permute-start(bf16[32,1024]{1,0:T(8,128)(2,1)S(1)} %get-tuple-element.38), channel_id=1, source_target_pairs={{0,6},{1,7},{2,4},{3,5},{4,2},{5,3},{6,0},{7,1},{8,14},{9,15},{10,... | collective-permute-start | bytes 196616 | tf_op jit(solution)/shard_map/ppermute | solution.py:326
  12.8 9.6 %collective-permute-start.4 = (bf16[128,1152]{1,0:T(8,128)(2,1)S(1)}, bf16[128,1152]{1,0:T(8,128)(2,1)S(1)}, u32[]{:S(2)}, u32[]{:S(2)}) collective-permute-start(bf16[128,1152]{1,0:T(8,128)(2,1)S(1)} %get-tuple-element.39.line), channel_id=1, source_target_pairs={{0,4},{1,5},{2,6},{3,7},{4,0},{5,1},{6,2},{7,3},{8,12},{9,13},{10,... | collective-permute-start | bytes 884744 | tf_op jit(solution)/shard_map/ppermute | solution.py:326
  14.5 8.8 %collective-permute-start.5 = (bf16[128,1024]{1,0:T(8,128)(2,1)S(1)}, bf16[128,1024]{1,0:T(8,128)(2,1)S(1)}, u32[]{:S(2)}, u32[]{:S(2)}) collective-permute-start(bf16[128,1024]{1,0:T(8,128)(2,1)S(1)} %get-tuple-element.42), channel_id=1, source_target_pairs={{0,2},{1,3},{2,0},{3,1},{4,6},{5,7},{6,4},{7,5},{8,10},{9,11},{10,... | collective-permute-start | bytes 786440 | tf_op jit(solution)/shard_map/ppermute | solution.py:326
  15.9 9.0 %collective-permute-start.6 = (bf16[96,1024]{1,0:T(8,128)(2,1)S(1)}, bf16[96,1024]{1,0:T(8,128)(2,1)S(1)}, u32[]{:S(2)}, u32[]{:S(2)}) collective-permute-start(bf16[96,1024]{1,0:T(8,128)(2,1)S(1)} %get-tuple-element.43), channel_id=1, source_target_pairs={{0,6},{1,7},{2,4},{3,5},{4,2},{5,3},{6,0},{7,1},{8,14},{9,15},{10,... | collective-permute-start | bytes 589832 | tf_op jit(solution)/shard_map/ppermute | solution.py:326
  19.2 5.7 %collective-permute-start.8 = (bf16[128,1152]{1,0:T(8,128)(2,1)S(1)}, bf16[128,1152]{1,0:T(8,128)(2,1)S(1)}, u32[]{:S(2)}, u32[]{:S(2)}) collective-permute-start(bf16[128,1152]{1,0:T(8,128)(2,1)S(1)} %get-tuple-element.40.refs_0_), channel_id=1, source_target_pairs={{0,1},{1,0},{2,3},{3,2},{4,5},{5,4},{6,7},{7,6},{8,9},{9,8},{10,11... | collective-permute-start | bytes 884744 | tf_op jit(solution)/shard_map/ppermute | solution.py:326
  22.4 2.6 %collective-permute-start.9 = (bf16[128,1152]{1,0:T(8,128)(2,1)S(1)}, bf16[128,1152]{1,0:T(8,128)(2,1)S(1)}, u32[]{:S(2)}, u32[]{:S(2)}) collective-permute-start(bf16[128,1152]{1,0:T(8,128)(2,1)S(1)} %collective-permute-done.4.refs_1_), channel_id=1, source_target_pairs={{0,1},{1,0},{2,3},{3,2},{4,5},{5,4},{6,7},{7,6},{8,9},{9,8},{10,11... | collective-permute-start | bytes 884744 | tf_op jit(solution)/shard_map/ppermute | solution.py:326
  22.4 1.7 %collective-permute-start.7 = (bf16[32,1024]{1,0:T(8,128)(2,1)S(1)}, bf16[32,1024]{1,0:T(8,128)(2,1)S(1)}, u32[]{:S(2)}, u32[]{:S(2)}) collective-permute-start(bf16[32,1024]{1,0:T(8,128)(2,1)S(1)} %collective-permute-done.2.refs_3_.refs_7_), channel_id=1, source_target_pairs={{0,1},{1,0},{2,3},{3,2},{4,5},{5,4},{6,7},{7,6},{8,9},{9,8},{10,11... | collective-permute-start | bytes 196616 | tf_op jit(solution)/shard_map/ppermute | solution.py:326
  23.3 3.1 %collective-permute-start.10 = (bf16[128,1024]{1,0:T(8,128)(2,1)S(1)}, bf16[128,1024]{1,0:T(8,128)(2,1)S(1)}, u32[]{:S(2)}, u32[]{:S(2)}) collective-permute-start(bf16[128,1024]{1,0:T(8,128)(2,1)S(1)} %shard_map.89.refs_2_.refs_6_), channel_id=1, source_target_pairs={{0,1},{1,0},{2,3},{3,2},{4,5},{5,4},{6,7},{7,6},{8,9},{9,8},{10,11... | collective-permute-start | bytes 786440 | tf_op jit(solution)/shard_map/ppermute | solution.py:326
  24.9 1.4 %collective-permute-start.11 = (bf16[96,1024]{1,0:T(8,128)(2,1)S(1)}, bf16[96,1024]{1,0:T(8,128)(2,1)S(1)}, u32[]{:S(2)}, u32[]{:S(2)}) collective-permute-start(bf16[96,1024]{1,0:T(8,128)(2,1)S(1)} %shard_map.90.refs_4_.refs_8_), channel_id=1, source_target_pairs={{0,1},{1,0},{2,3},{3,2},{4,5},{5,4},{6,7},{7,6},{8,9},{9,8},{10,11... | collective-permute-start | bytes 589832 | tf_op jit(solution)/shard_map/ppermute | solution.py:326
  27.3 14.2 %collective-permute-start.13 = (bf16[2048,512]{1,0:T(8,128)(2,1)S(1)}, bf16[2048,512]{1,0:T(8,128)(2,1)S(1)}, u32[]{:S(2)}, u32[]{:S(2)}) collective-permute-start(bf16[2048,512]{1,0:T(8,128)(2,1)S(1)} %shard_map.93), channel_id=1, source_target_pairs={{0,1},{1,0},{2,3},{3,2},{4,5},{5,4},{6,7},{7,6},{8,9},{9,8},{10,11... | collective-permute-start | bytes 6291464 | tf_op jit(solution)/shard_map/ppermute | solution.py:326
  27.5 14.0 %collective-permute-start.12 = (f32[256,512]{1,0:T(8,128)S(1)}, f32[256,512]{1,0:T(8,128)S(1)}, u32[]{:S(2)}, u32[]{:S(2)}) collective-permute-start(f32[256,512]{1,0:T(8,128)S(1)} %get-tuple-element.44.mine), channel_id=1, source_target_pairs={{0,1},{1,0},{2,3},{3,2},{4,5},{5,4},{6,7},{7,6},{8,9},{9,8},{10,11... | collective-permute-start | bytes 1572872 | tf_op jit(solution)/shard_map/ppermute | solution.py:326
  43.3 7.4 %collective-permute-start.18 = (bf16[64,1024]{1,0:T(8,128)(2,1)S(1)}, bf16[64,1024]{1,0:T(8,128)(2,1)S(1)}, u32[]{:S(2)}, u32[]{:S(2)}) collective-permute-start(bf16[64,1024]{1,0:T(8,128)(2,1)S(1)} %get-tuple-element.63), channel_id=1, source_target_pairs={{0,6},{1,7},{2,4},{3,5},{4,2},{5,3},{6,0},{7,1},{8,14},{9,15},{10,... | collective-permute-start | bytes 393224 | tf_op jit(solution)/shard_map/ppermute | solution.py:326
  44.0 9.5 %collective-permute-start.19 = (bf16[64,1024]{1,0:T(8,128)(2,1)S(1)}, bf16[64,1024]{1,0:T(8,128)(2,1)S(1)}, u32[]{:S(2)}, u32[]{:S(2)}) collective-permute-start(bf16[64,1024]{1,0:T(8,128)(2,1)S(1)} %get-tuple-element.64), channel_id=1, source_target_pairs={{0,4},{1,5},{2,6},{3,7},{4,0},{5,1},{6,2},{7,3},{8,12},{9,13},{10,... | collective-permute-start | bytes 393224 | tf_op jit(solution)/shard_map/ppermute | solution.py:326
  45.3 8.3 %collective-permute-start.20 = (bf16[64,1024]{1,0:T(8,128)(2,1)S(1)}, bf16[64,1024]{1,0:T(8,128)(2,1)S(1)}, u32[]{:S(2)}, u32[]{:S(2)}) collective-permute-start(bf16[64,1024]{1,0:T(8,128)(2,1)S(1)} %get-tuple-element.65), channel_id=1, source_target_pairs={{0,2},{1,3},{2,0},{3,1},{4,6},{5,7},{6,4},{7,5},{8,10},{9,11},{10,... | collective-permute-start | bytes 393224 | tf_op jit(solution)/shard_map/ppermute | solution.py:326
  48.3 8.4 %collective-permute-start.14 = (bf16[64,1024]{1,0:T(8,128)(2,1)S(1)}, bf16[64,1024]{1,0:T(8,128)(2,1)S(1)}, u32[]{:S(2)}, u32[]{:S(2)}) collective-permute-start(bf16[64,1024]{1,0:T(8,128)(2,1)S(1)} %get-tuple-element.55), channel_id=1, source_target_pairs={{0,6},{1,7},{2,4},{3,5},{4,2},{5,3},{6,0},{7,1},{8,14},{9,15},{10,... | collective-permute-start | bytes 393224 | tf_op jit(solution)/shard_map/ppermute | solution.py:326
  49.0 8.5 %collective-permute-start.15 = (bf16[64,1024]{1,0:T(8,128)(2,1)S(1)}, bf16[64,1024]{1,0:T(8,128)(2,1)S(1)}, u32[]{:S(2)}, u32[]{:S(2)}) collective-permute-start(bf16[64,1024]{1,0:T(8,128)(2,1)S(1)} %get-tuple-element.56), channel_id=1, source_target_pairs={{0,4},{1,5},{2,6},{3,7},{4,0},{5,1},{6,2},{7,3},{8,12},{9,13},{10,... | collective-permute-start | bytes 393224 | tf_op jit(solution)/shard_map/ppermute | solution.py:326
  50.6 6.9 %collective-permute-start.16 = (bf16[64,1024]{1,0:T(8,128)(2,1)S(1)}, bf16[64,1024]{1,0:T(8,128)(2,1)S(1)}, u32[]{:S(2)}, u32[]{:S(2)}) collective-permute-start(bf16[64,1024]{1,0:T(8,128)(2,1)S(1)} %get-tuple-element.57), channel_id=1, source_target_pairs={{0,2},{1,3},{2,0},{3,1},{4,6},{5,7},{6,4},{7,5},{8,10},{9,11},{10,... | collective-permute-start | bytes 393224 | tf_op jit(solution)/shard_map/ppermute | solution.py:326
  53.6 6.9 %collective-permute-start.21 = (bf16[32,1024]{1,0:T(8,128)(2,1)S(1)}, bf16[32,1024]{1,0:T(8,128)(2,1)S(1)}, u32[]{:S(2)}, u32[]{:S(2)}) collective-permute-start(bf16[32,1024]{1,0:T(8,128)(2,1)S(1)} %get-tuple-element.66), channel_id=1, source_target_pairs={{0,16},{1,17},{2,18},{3,19},{4,20},{5,21},{6,22},{7,23},{8,24},{9,... | collective-permute-start | bytes 196616 | tf_op jit(solution)/shard_map/ppermute | solution.py:326
  54.3 6.5 %collective-permute-start.22 = (bf16[32,1024]{1,0:T(8,128)(2,1)S(1)}, bf16[32,1024]{1,0:T(8,128)(2,1)S(1)}, u32[]{:S(2)}, u32[]{:S(2)}) collective-permute-start(bf16[32,1024]{1,0:T(8,128)(2,1)S(1)} %get-tuple-element.67), channel_id=1, source_target_pairs={{0,24},{1,25},{2,26},{3,27},{4,28},{5,29},{6,30},{7,31},{8,16},{9,... | collective-permute-start | bytes 196616 | tf_op jit(solution)/shard_map/ppermute | solution.py:326
  57.7 4.3 %collective-permute-start.17 = (bf16[32,1024]{1,0:T(8,128)(2,1)S(1)}, bf16[32,1024]{1,0:T(8,128)(2,1)S(1)}, u32[]{:S(2)}, u32[]{:S(2)}) collective-permute-start(bf16[32,1024]{1,0:T(8,128)(2,1)S(1)} %get-tuple-element.62), channel_id=1, source_target_pairs={{0,8},{1,9},{2,10},{3,11},{4,12},{5,13},{6,14},{7,15},{8,0},{9,1},... | collective-permute-start | bytes 196616 | tf_op jit(solution)/shard_map/ppermute | solution.py:326

commit v24 on v21

--- a/solution.py
+++ b/solution.py
@@ -431,7 +431,7 @@
     other_held = send(hold(away, stats), core=1)
     stats = lax.all_to_all(stats, AXES, 0, 0)
     rows_part = total_rows // 4
-    order = sorted(range(1, ranks), key=lambda place: (-(place % 2 + (place > 1)), place)) + [0]
+    order = sorted(range(1, ranks), key=lambda place: (place > 1, -(place % 2), place)) + [0]
     outs = (shape((rows_part, width), bf16),) * (ranks - 1) + (shape((rows_part, width), f32),)
     logit_grad, table, *going = call(
         functools.partial(grad_kernel, order, dps),

time: 63.1 us -> 64.1 us (1.016)
  waiting for transfers between devices: 11.8 us -> 15.5 us
  starting transfers between devices: 23.8 us -> 21.1 us
    ppermute x23, waiting for transfers between devices: 11.8 us -> 15.5 us  [send(): return lax.ppermute(value, AXES, pairs)]
    ppermute x23, starting transfers between devices: 23.8 us -> 21.1 us  [send(): return lax.ppermute(value, AXES, pairs)]
  transfers between devices with their start and end apart: 23 -> 23, of which waited for: 9 -> 11; matrix products, arithmetic and copies ran while one was open for 0% -> 0% of each run, Pallas kernels for 13% -> 12%
where the time goes in v24:
time: 64.1 us; the launch traced here: 63.9 us
  starting transfers between devices  21.1 us (33%)
  waiting for transfers between devices  15.5 us (24%)
  blocking collectives  13.6 us (21%)
  Pallas kernels  12.9 us (20%)
  between operations  0.8 us (1%)
    ppermute x23, starting transfers between devices, send(): return lax.ppermute(value, AXES, pairs)  21.1 us
    ppermute x23, waiting for transfers between devices, send(): return lax.ppermute(value, AXES, pairs)  15.5 us
    all_to_all x1, blocking collectives, body(): stats = lax.all_to_all(stats, AXES, 0, 0)  13.6 us
    pallas_call x16, Pallas kernels, call(): pl.pallas_call(kernel, out_shape=out_shape, in_specs=in_specs, out_specs=...  12.9 us
  transfers between devices with their start and end apart: 23, of which 11 were waited for; matrix products, arithmetic and copies ran while one was open for 0% of the time, Pallas kernels for 12%

profile of v24, /device:TPU:0, one launch (start us, length us, event | category | flops | bytes accessed | tf_op | source)
XLA Modules:
  0.0 63.9 jit_solution(14705230890475347749)
XLA Ops:
  0.6 1.2 %shard_map.85 = (bf16[32,1152]{1,0:T(8,128)(2,1)S(1)}, bf16[32,1024]{1,0:T(8,128)(2,1)S(1)}, bf16[32,128]{1,0:T(8,128)(2,1)S(1)}) custom-call(bf16[128,1024]{1,0:T(8,128)(2,1)} %hidden_hbm.1, s32[1,128]{1,0:T(1,128)} %bitcast.6, s32[1,128]{1,0:T(1,128)} %bitcast.7, s32[1,128]{1,0:T(1,128)} %bitcast.8), custom_call_target="tpu_custom_call" | custom-call | bytes 411136 | tf_op jit(solution)/shard_map/pallas_call | solution.py:33
  1.9 4.1 %collective-permute-start = (bf16[32,1152]{1,0:T(8,128)(2,1)S(1)}, bf16[32,1152]{1,0:T(8,128)(2,1)S(1)}, u32[]{:S(2)}, u32[]{:S(2)}) collective-permute-start(bf16[32,1152]{1,0:T(8,128)(2,1)S(1)} %get-tuple-element.37.refs_0_), channel_id=1, source_target_pairs={{0,16},{1,17},{2,18},{3,19},{4,20},{5,21},{6,22},{7,23},{8,24},{9,... | collective-permute-start | bytes 221192 | tf_op jit(solution)/shard_map/ppermute | solution.py:326
  6.0 1.3 %collective-permute-start.1 = (bf16[32,1152]{1,0:T(8,128)(2,1)S(1)}, bf16[32,1152]{1,0:T(8,128)(2,1)S(1)}, u32[]{:S(2)}, u32[]{:S(2)}) collective-permute-start(bf16[32,1152]{1,0:T(8,128)(2,1)S(1)} %get-tuple-element.37.refs_0_), channel_id=1, source_target_pairs={{0,24},{1,25},{2,26},{3,27},{4,28},{5,29},{6,30},{7,31},{8,16},{9,... | collective-permute-start | bytes 221192 | tf_op jit(solution)/shard_map/ppermute | solution.py:326
  7.5 2.4 %collective-permute-start.2 = (bf16[32,1024]{1,0:T(8,128)(2,1)S(1)}, bf16[32,1024]{1,0:T(8,128)(2,1)S(1)}, u32[]{:S(2)}, u32[]{:S(2)}) collective-permute-start(bf16[32,1024]{1,0:T(8,128)(2,1)S(1)} %get-tuple-element.38), channel_id=1, source_target_pairs={{0,6},{1,7},{2,4},{3,5},{4,2},{5,3},{6,0},{7,1},{8,14},{9,15},{10,... | collective-permute-start | bytes 196616 | tf_op jit(solution)/shard_map/ppermute | solution.py:326
  10.0 2.7 %collective-permute-done.2.refs_3_.refs_5_ = bf16[32,1024]{1,0:T(8,128)(2,1)S(1)} collective-permute-done((bf16[32,1024]{1,0:T(8,128)(2,1)S(1)}, bf16[32,1024]{1,0:T(8,128)(2,1)S(1)}, u32[]{:S(2)}, u32[]{:S(2)}) %collective-permute-start.2) | collective-permute-done | bytes 65568 | tf_op jit(solution)/shard_map/ppermute | solution.py:326
  12.8 1.7 %collective-permute-start.4 = (bf16[128,1152]{1,0:T(8,128)(2,1)S(1)}, bf16[128,1152]{1,0:T(8,128)(2,1)S(1)}, u32[]{:S(2)}, u32[]{:S(2)}) collective-permute-start(bf16[128,1152]{1,0:T(8,128)(2,1)S(1)} %get-tuple-element.39.line), channel_id=1, source_target_pairs={{0,4},{1,5},{2,6},{3,7},{4,0},{5,1},{6,2},{7,3},{8,12},{9,13},{10,... | collective-permute-start | bytes 884744 | tf_op jit(solution)/shard_map/ppermute | solution.py:326
  14.5 1.5 %collective-permute-start.5 = (bf16[128,1024]{1,0:T(8,128)(2,1)S(1)}, bf16[128,1024]{1,0:T(8,128)(2,1)S(1)}, u32[]{:S(2)}, u32[]{:S(2)}) collective-permute-start(bf16[128,1024]{1,0:T(8,128)(2,1)S(1)} %get-tuple-element.42), channel_id=1, source_target_pairs={{0,2},{1,3},{2,0},{3,1},{4,6},{5,7},{6,4},{7,5},{8,10},{9,11},{10,... | collective-permute-start | bytes 786440 | tf_op jit(solution)/shard_map/ppermute | solution.py:326
  16.3 2.9 %shard_map.87 = (bf16[4096,512]{1,0:T(8,128)(2,1)S(1)}, bf16[2048,512]{1,0:T(8,128)(2,1)S(1)}, bf16[128,1152]{1,0:T(8,128)(2,1)S(1)}) custom-call(bf16[128,1152]{1,0:T(8,128)(2,1)S(1)} %get-tuple-element.39.line, bf16[4096,512]{1,0:T(8,128)(2,1)} %weight.1), custom_call_target="tpu_custom_call" | custom-call | bytes 11075584 | tf_op jit(solution)/shard_map/pallas_call | solution.py:33
  19.3 3.1 %collective-permute-done.4.refs_1_ = bf16[128,1152]{1,0:T(8,128)(2,1)S(1)} collective-permute-done((bf16[128,1152]{1,0:T(8,128)(2,1)S(1)}, bf16[128,1152]{1,0:T(8,128)(2,1)S(1)}, u32[]{:S(2)}, u32[]{:S(2)}) %collective-permute-start.4) | collective-permute-done | bytes 294944 | tf_op jit(solution)/shard_map/ppermute | solution.py:326
  22.4 0.5 collective-permute-start.7
  23.4 0.7 %collective-permute-done.7.refs_1_.refs_4_.refs_8_ = bf16[32,1024]{1,0:T(8,128)(2,1)S(1)} collective-permute-done((bf16[32,1024]{1,0:T(8,128)(2,1)S(1)}, bf16[32,1024]{1,0:T(8,128)(2,1)S(1)}, u32[]{:S(2)}, u32[]{:S(2)}) %collective-permute-start.7) | collective-permute-done | bytes 65568 | tf_op jit(solution)/shard_map/ppermute | solution.py:326
  24.0 0.9 %collective-permute-done.6.refs_0_ = bf16[96,1024]{1,0:T(8,128)(2,1)S(1)} collective-permute-done((bf16[96,1024]{1,0:T(8,128)(2,1)S(1)}, bf16[96,1024]{1,0:T(8,128)(2,1)S(1)}, u32[]{:S(2)}, u32[]{:S(2)}) %collective-permute-start.6) | collective-permute-done | bytes 196640 | tf_op jit(solution)/shard_map/ppermute | solution.py:326
  25.0 1.0 %shard_map.91.refs_1_ = f32[256,512]{1,0:T(8,128)S(1)} custom-call(bf16[4096,512]{1,0:T(8,128)(2,1)S(1)} %get-tuple-element.41.weight.refs_2_, bf16[128,1152]{1,0:T(8,128)(2,1)S(1)} %get-tuple-element.40.refs_0_, bf16[128,1152]{1,0:T(8,128)(2,1)S(1)} %collective-permute-done.4.refs_1_, bf16[128,1024]{1,0:T(8,128)(2,1)S(1)} %shard_map.89.refs_2_.refs_4_, ...), custom_call_target="tpu_custom_call" | custom-call | flops 805306368 | bytes 6422528 | tf_op jit(solution)/shard_map/pallas_call | solution.py:33
  25.9 0.4 collective-permute-done.11.refs_5_.refs_9_
  26.4 0.9 %shard_map.92 = (f32[256,512]{1,0:T(8,128)S(1)}, f32[32,1,384]{2,1,0:T(1,128)S(1)}) custom-call(f32[256,128]{1,0:T(8,128)S(1)} %shard_map.88.refs_1_.refs_0_.info, f32[256,512]{1,0:T(8,128)S(1)} %shard_map.91.refs_1_, bf16[4096,512]{1,0:T(8,128)(2,1)S(1)} %get-tuple-element.41.weight.refs_2_, bf16[128,1024]{1,0:T(8,128)(2,1)S(1)} %collective-permute-done.10.refs_3_.refs_7_, ...), custom_call_target="tpu_custom_call" | custom-call | flops 268435456 | bytes 5947392 | tf_op jit(solution)/shard_map/pallas_call | solution.py:33
  27.9 13.6 %all_to_all.5.stats.refs_3_ = f32[32,1,384]{2,1,0:T(1,128)S(1)} all-to-all(f32[32,1,384]{2,1,0:T(1,128)S(1)} %get-tuple-element.46.refs_1_), channel_id=1, replica_groups=mesh['dp'=8,'vocab'=4] {'dp','vocab'}, dimensions={0} | all-to-all | bytes 98304 | tf_op jit(solution)/shard_map/all_to_all | solution.py:432
  41.5 1.8 %shard_map.94 = (bf16[256,512]{1,0:T(8,128)(2,1)S(1)}, f32[256,128]{1,0:T(8,128)S(1)}, bf16[64,1024]{1,0:T(8,128)(2,1)S(1)}, bf16[64,1024]{1,0:T(8,128)(2,1)S(1)...) custom-call(f32[256,128]{1,0:T(8,128)S(1)} %shard_map.88.refs_1_.ref, ...), custom_call_target="tpu_custom_call" | custom-call | flops 1073741824 | bytes 9224192 | tf_op jit(solution)/shard_map/pallas_call | solution.py:33
  43.3 0.6 %collective-permute-start.18 = (bf16[64,1024]{1,0:T(8,128)(2,1)S(1)}, bf16[64,1024]{1,0:T(8,128)(2,1)S(1)}, u32[]{:S(2)}, u32[]{:S(2)}) collective-permute-start(bf16[64,1024]{1,0:T(8,128)(2,1)S(1)} %get-tuple-element.63), channel_id=1, source_target_pairs={{0,4},{1,5},{2,6},{3,7},{4,0},{5,1},{6,2},{7,3},{8,12},{9,13},{10,... | collective-permute-start | bytes 393224 | tf_op jit(solution)/shard_map/ppermute | solution.py:326
  43.9 1.3 %collective-permute-start.19 = (bf16[64,1024]{1,0:T(8,128)(2,1)S(1)}, bf16[64,1024]{1,0:T(8,128)(2,1)S(1)}, u32[]{:S(2)}, u32[]{:S(2)}) collective-permute-start(bf16[64,1024]{1,0:T(8,128)(2,1)S(1)} %get-tuple-element.64), channel_id=1, source_target_pairs={{0,6},{1,7},{2,4},{3,5},{4,2},{5,3},{6,0},{7,1},{8,14},{9,15},{10,... | collective-permute-start | bytes 393224 | tf_op jit(solution)/shard_map/ppermute | solution.py:326
  45.3 1.6 %collective-permute-start.20 = (bf16[64,1024]{1,0:T(8,128)(2,1)S(1)}, bf16[64,1024]{1,0:T(8,128)(2,1)S(1)}, u32[]{:S(2)}, u32[]{:S(2)}) collective-permute-start(bf16[64,1024]{1,0:T(8,128)(2,1)S(1)} %get-tuple-element.65), channel_id=1, source_target_pairs={{0,2},{1,3},{2,0},{3,1},{4,6},{5,7},{6,4},{7,5},{8,10},{9,11},{10,... | collective-permute-start | bytes 393224 | tf_op jit(solution)/shard_map/ppermute | solution.py:326
  46.8 1.8 %shard_map.95 = (bf16[4096,512]{1,0:T(8,128)(2,1)}, f32[8,128]{1,0:T(8,128)S(1)}) custom-call(f32[64,1024]{1,0:T(8,128)S(1)} %get-tuple-element.52.after.kept, bf16[256,512]{1,0:T(8,128)(2,1)S(1)} %get-tuple-element.53.logit_grad, bf16[128,1152]{1,0:T(8,128)(2,1)S(1)} %get-tuple-element.40.refs_0_, bf16[128,1152]{1,0:T(8,128)(2,1)S(1)} %collective-permute-done.4.refs_1_, ...), custom_call_target="tpu_custom_call" | custom-call | flops 536870912 | bytes 5902336 | tf_op jit(solution)/shard_map/pallas_call | solution.py:33
  48.7 0.6 %collective-permute-start.14 = (bf16[64,1024]{1,0:T(8,128)(2,1)S(1)}, bf16[64,1024]{1,0:T(8,128)(2,1)S(1)}, u32[]{:S(2)}, u32[]{:S(2)}) collective-permute-start(bf16[64,1024]{1,0:T(8,128)(2,1)S(1)} %get-tuple-element.55), channel_id=1, source_target_pairs={{0,4},{1,5},{2,6},{3,7},{4,0},{5,1},{6,2},{7,3},{8,12},{9,13},{10,... | collective-permute-start | bytes 393224 | tf_op jit(solution)/shard_map/ppermute | solution.py:326
  49.3 1.4 %collective-permute-start.15 = (bf16[64,1024]{1,0:T(8,128)(2,1)S(1)}, bf16[64,1024]{1,0:T(8,128)(2,1)S(1)}, u32[]{:S(2)}, u32[]{:S(2)}) collective-permute-start(bf16[64,1024]{1,0:T(8,128)(2,1)S(1)} %get-tuple-element.56), channel_id=1, source_target_pairs={{0,6},{1,7},{2,4},{3,5},{4,2},{5,3},{6,0},{7,1},{8,14},{9,15},{10,... | collective-permute-start | bytes 393224 | tf_op jit(solution)/shard_map/ppermute | solution.py:326
  50.7 2.3 %collective-permute-done.18.refs_0_ = bf16[64,1024]{1,0:T(8,128)(2,1)S(1)} collective-permute-done((bf16[64,1024]{1,0:T(8,128)(2,1)S(1)}, bf16[64,1024]{1,0:T(8,128)(2,1)S(1)}, u32[]{:S(2)}, u32[]{:S(2)}) %collective-permute-start.18) | collective-permute-done | bytes 131104 | tf_op jit(solution)/shard_map/ppermute | solution.py:326
  53.1 0.9 %collective-permute-done.20.refs_2_ = bf16[64,1024]{1,0:T(8,128)(2,1)S(1)} collective-permute-done((bf16[64,1024]{1,0:T(8,128)(2,1)S(1)}, bf16[64,1024]{1,0:T(8,128)(2,1)S(1)}, u32[]{:S(2)}, u32[]{:S(2)}) %collective-permute-start.20) | collective-permute-done | bytes 131104 | tf_op jit(solution)/shard_map/ppermute | solution.py:326
  54.2 2.3 %collective-permute-start.22 = (bf16[32,1024]{1,0:T(8,128)(2,1)S(1)}, bf16[32,1024]{1,0:T(8,128)(2,1)S(1)}, u32[]{:S(2)}, u32[]{:S(2)}) collective-permute-start(bf16[32,1024]{1,0:T(8,128)(2,1)S(1)} %get-tuple-element.67), channel_id=1, source_target_pairs={{0,24},{1,25},{2,26},{3,27},{4,28},{5,29},{6,30},{7,31},{8,16},{9,... | collective-permute-start | bytes 196616 | tf_op jit(solution)/shard_map/ppermute | solution.py:326
  56.5 0.8 %collective-permute-done.14.refs_0_ = bf16[64,1024]{1,0:T(8,128)(2,1)S(1)} collective-permute-done((bf16[64,1024]{1,0:T(8,128)(2,1)S(1)}, bf16[64,1024]{1,0:T(8,128)(2,1)S(1)}, u32[]{:S(2)}, u32[]{:S(2)}) %collective-permute-start.14) | collective-permute-done | bytes 131104 | tf_op jit(solution)/shard_map/ppermute | solution.py:326
  57.3 1.2 %collective-permute-done.16.refs_2_ = bf16[64,1024]{1,0:T(8,128)(2,1)S(1)} collective-permute-done((bf16[64,1024]{1,0:T(8,128)(2,1)S(1)}, bf16[64,1024]{1,0:T(8,128)(2,1)S(1)}, u32[]{:S(2)}, u32[]{:S(2)}) %collective-permute-start.16) | collective-permute-done | bytes 131104 | tf_op jit(solution)/shard_map/ppermute | solution.py:326
  58.7 1.8 %shard_map.98 = (bf16[4096,512]{1,0:T(8,128)(2,1)}, f32[8,128]{1,0:T(8,128)S(1)}) custom-call(f32[32,1024]{1,0:T(8,128)S(1)} %get-tuple-element.58.after.refs_0_, bf16[256,512]{1,0:T(8,128)(2,1)S(1)} %get-tuple-element.53.logit_grad, bf16[4096,512]{1,0:T(8,128)(2,1)} %get-tuple-element.59.refs_0_, ...), custom_call_target="tpu_custom_call", output_to_operand_aliasing={{0}: (2, {})} | custom-call | flops 536870912 | bytes 10145792 | tf_op jit(solution)/shard_map/pallas_call | solution.py:33
  60.5 0.4 collective-permute-done.22.refs_3_
  61.0 2.0 %collective-permute-done.17.refs_1_ = bf16[32,1024]{1,0:T(8,128)(2,1)S(1)} collective-permute-done((bf16[32,1024]{1,0:T(8,128)(2,1)S(1)}, bf16[32,1024]{1,0:T(8,128)(2,1)S(1)}, u32[]{:S(2)}, u32[]{:S(2)}) %collective-permute-start.17) | collective-permute-done | bytes 65568 | tf_op jit(solution)/shard_map/ppermute | solution.py:326
  62.9 1.0 %shard_map.100 = (bf16[128,1024]{1,0:T(8,128)(2,1)}, f32[1,1]{1,0:T(1,128)}) custom-call(f32[8,128]{1,0:T(8,128)S(1)} %get-tuple-element.60.last, bf16[32,128]{1,0:T(8,128)(2,1)S(1)} %get-tuple-element.61.chosen, f32[32,1024]{1,0:T(8,128)S(1)} %get-tuple-element.58.after.refs_0_, bf16[32,1024]{1,0:T(8,128)(2,1)S(1)} %collective-permute-done.17.refs_1_, ...), custom_call_target="tpu_custom_call" | custom-call | bytes 602116 | tf_op jit(solution)/shard_map/pallas_call | solution.py:33
  (33 shorter events, 2.3 us)
Async XLA Ops:
  0.6 22.2 %copy-start = (f32[32]{0:T(128)S(1)}, f32[32]{0:T(128)}, u32[]{:S(2)}) copy-start(f32[32]{0:T(128)} %param.11) | copy-start | bytes 388
  1.9 10.8 %collective-permute-start = (bf16[32,1152]{1,0:T(8,128)(2,1)S(1)}, bf16[32,1152]{1,0:T(8,128)(2,1)S(1)}, u32[]{:S(2)}, u32[]{:S(2)}) collective-permute-start(bf16[32,1152]{1,0:T(8,128)(2,1)S(1)} %get-tuple-element.37.refs_0_), channel_id=1, source_target_pairs={{0,16},{1,17},{2,18},{3,19},{4,20},{5,21},{6,22},{7,23},{8,24},{9,... | collective-permute-start | bytes 221192 | tf_op jit(solution)/shard_map/ppermute | solution.py:326
  6.0 6.8 %collective-permute-start.1 = (bf16[32,1152]{1,0:T(8,128)(2,1)S(1)}, bf16[32,1152]{1,0:T(8,128)(2,1)S(1)}, u32[]{:S(2)}, u32[]{:S(2)}) collective-permute-start(bf16[32,1152]{1,0:T(8,128)(2,1)S(1)} %get-tuple-element.37.refs_0_), channel_id=1, source_target_pairs={{0,24},{1,25},{2,26},{3,27},{4,28},{5,29},{6,30},{7,31},{8,16},{9,... | collective-permute-start | bytes 221192 | tf_op jit(solution)/shard_map/ppermute | solution.py:326
  7.3 5.4 %collective-permute-start.3 = (bf16[32,1152]{1,0:T(8,128)(2,1)S(1)}, bf16[32,1152]{1,0:T(8,128)(2,1)S(1)}, u32[]{:S(2)}, u32[]{:S(2)}) collective-permute-start(bf16[32,1152]{1,0:T(8,128)(2,1)S(1)} %get-tuple-element.37.refs_0_), channel_id=1, source_target_pairs={{0,8},{1,9},{2,10},{3,11},{4,12},{5,13},{6,14},{7,15},{8,0},{9,1},... | collective-permute-start | bytes 221192 | tf_op jit(solution)/shard_map/ppermute | solution.py:326
  7.5 5.2 %collective-permute-start.2 = (bf16[32,1024]{1,0:T(8,128)(2,1)S(1)}, bf16[32,1024]{1,0:T(8,128)(2,1)S(1)}, u32[]{:S(2)}, u32[]{:S(2)}) collective-permute-start(bf16[32,1024]{1,0:T(8,128)(2,1)S(1)} %get-tuple-element.38), channel_id=1, source_target_pairs={{0,6},{1,7},{2,4},{3,5},{4,2},{5,3},{6,0},{7,1},{8,14},{9,15},{10,... | collective-permute-start | bytes 196616 | tf_op jit(solution)/shard_map/ppermute | solution.py:326
  12.8 9.6 %collective-permute-start.4 = (bf16[128,1152]{1,0:T(8,128)(2,1)S(1)}, bf16[128,1152]{1,0:T(8,128)(2,1)S(1)}, u32[]{:S(2)}, u32[]{:S(2)}) collective-permute-start(bf16[128,1152]{1,0:T(8,128)(2,1)S(1)} %get-tuple-element.39.line), channel_id=1, source_target_pairs={{0,4},{1,5},{2,6},{3,7},{4,0},{5,1},{6,2},{7,3},{8,12},{9,13},{10,... | collective-permute-start | bytes 884744 | tf_op jit(solution)/shard_map/ppermute | solution.py:326
  14.5 8.8 %collective-permute-start.5 = (bf16[128,1024]{1,0:T(8,128)(2,1)S(1)}, bf16[128,1024]{1,0:T(8,128)(2,1)S(1)}, u32[]{:S(2)}, u32[]{:S(2)}) collective-permute-start(bf16[128,1024]{1,0:T(8,128)(2,1)S(1)} %get-tuple-element.42), channel_id=1, source_target_pairs={{0,2},{1,3},{2,0},{3,1},{4,6},{5,7},{6,4},{7,5},{8,10},{9,11},{10,... | collective-permute-start | bytes 786440 | tf_op jit(solution)/shard_map/ppermute | solution.py:326
  15.9 9.0 %collective-permute-start.6 = (bf16[96,1024]{1,0:T(8,128)(2,1)S(1)}, bf16[96,1024]{1,0:T(8,128)(2,1)S(1)}, u32[]{:S(2)}, u32[]{:S(2)}) collective-permute-start(bf16[96,1024]{1,0:T(8,128)(2,1)S(1)} %get-tuple-element.43), channel_id=1, source_target_pairs={{0,6},{1,7},{2,4},{3,5},{4,2},{5,3},{6,0},{7,1},{8,14},{9,15},{10,... | collective-permute-start | bytes 589832 | tf_op jit(solution)/shard_map/ppermute | solution.py:326
  19.2 5.7 %collective-permute-start.8 = (bf16[128,1152]{1,0:T(8,128)(2,1)S(1)}, bf16[128,1152]{1,0:T(8,128)(2,1)S(1)}, u32[]{:S(2)}, u32[]{:S(2)}) collective-permute-start(bf16[128,1152]{1,0:T(8,128)(2,1)S(1)} %get-tuple-element.40.refs_0_), channel_id=1, source_target_pairs={{0,1},{1,0},{2,3},{3,2},{4,5},{5,4},{6,7},{7,6},{8,9},{9,8},{10,11... | collective-permute-start | bytes 884744 | tf_op jit(solution)/shard_map/ppermute | solution.py:326
  22.4 2.6 %collective-permute-start.9 = (bf16[128,1152]{1,0:T(8,128)(2,1)S(1)}, bf16[128,1152]{1,0:T(8,128)(2,1)S(1)}, u32[]{:S(2)}, u32[]{:S(2)}) collective-permute-start(bf16[128,1152]{1,0:T(8,128)(2,1)S(1)} %collective-permute-done.4.refs_1_), channel_id=1, source_target_pairs={{0,1},{1,0},{2,3},{3,2},{4,5},{5,4},{6,7},{7,6},{8,9},{9,8},{10,11... | collective-permute-start | bytes 884744 | tf_op jit(solution)/shard_map/ppermute | solution.py:326
  22.4 1.7 %collective-permute-start.7 = (bf16[32,1024]{1,0:T(8,128)(2,1)S(1)}, bf16[32,1024]{1,0:T(8,128)(2,1)S(1)}, u32[]{:S(2)}, u32[]{:S(2)}) collective-permute-start(bf16[32,1024]{1,0:T(8,128)(2,1)S(1)} %collective-permute-done.2.refs_3_.refs_5_), channel_id=1, source_target_pairs={{0,1},{1,0},{2,3},{3,2},{4,5},{5,4},{6,7},{7,6},{8,9},{9,8},{10,11... | collective-permute-start | bytes 196616 | tf_op jit(solution)/shard_map/ppermute | solution.py:326
  23.3 3.1 %collective-permute-start.10 = (bf16[128,1024]{1,0:T(8,128)(2,1)S(1)}, bf16[128,1024]{1,0:T(8,128)(2,1)S(1)}, u32[]{:S(2)}, u32[]{:S(2)}) collective-permute-start(bf16[128,1024]{1,0:T(8,128)(2,1)S(1)} %shard_map.89.refs_2_.refs_4_), channel_id=1, source_target_pairs={{0,1},{1,0},{2,3},{3,2},{4,5},{5,4},{6,7},{7,6},{8,9},{9,8},{10,11... | collective-permute-start | bytes 786440 | tf_op jit(solution)/shard_map/ppermute | solution.py:326
  24.9 1.4 %collective-permute-start.11 = (bf16[96,1024]{1,0:T(8,128)(2,1)S(1)}, bf16[96,1024]{1,0:T(8,128)(2,1)S(1)}, u32[]{:S(2)}, u32[]{:S(2)}) collective-permute-start(bf16[96,1024]{1,0:T(8,128)(2,1)S(1)} %shard_map.90.refs_4_.refs_6_), channel_id=1, source_target_pairs={{0,1},{1,0},{2,3},{3,2},{4,5},{5,4},{6,7},{7,6},{8,9},{9,8},{10,11... | collective-permute-start | bytes 589832 | tf_op jit(solution)/shard_map/ppermute | solution.py:326
  27.3 14.2 %collective-permute-start.13 = (bf16[2048,512]{1,0:T(8,128)(2,1)S(1)}, bf16[2048,512]{1,0:T(8,128)(2,1)S(1)}, u32[]{:S(2)}, u32[]{:S(2)}) collective-permute-start(bf16[2048,512]{1,0:T(8,128)(2,1)S(1)} %shard_map.93), channel_id=1, source_target_pairs={{0,1},{1,0},{2,3},{3,2},{4,5},{5,4},{6,7},{7,6},{8,9},{9,8},{10,11... | collective-permute-start | bytes 6291464 | tf_op jit(solution)/shard_map/ppermute | solution.py:326
  27.5 14.0 %collective-permute-start.12 = (f32[256,512]{1,0:T(8,128)S(1)}, f32[256,512]{1,0:T(8,128)S(1)}, u32[]{:S(2)}, u32[]{:S(2)}) collective-permute-start(f32[256,512]{1,0:T(8,128)S(1)} %get-tuple-element.44.mine), channel_id=1, source_target_pairs={{0,1},{1,0},{2,3},{3,2},{4,5},{5,4},{6,7},{7,6},{8,9},{9,8},{10,11... | collective-permute-start | bytes 1572872 | tf_op jit(solution)/shard_map/ppermute | solution.py:326
  43.3 9.7 %collective-permute-start.18 = (bf16[64,1024]{1,0:T(8,128)(2,1)S(1)}, bf16[64,1024]{1,0:T(8,128)(2,1)S(1)}, u32[]{:S(2)}, u32[]{:S(2)}) collective-permute-start(bf16[64,1024]{1,0:T(8,128)(2,1)S(1)} %get-tuple-element.63), channel_id=1, source_target_pairs={{0,4},{1,5},{2,6},{3,7},{4,0},{5,1},{6,2},{7,3},{8,12},{9,13},{10,... | collective-permute-start | bytes 393224 | tf_op jit(solution)/shard_map/ppermute | solution.py:326
  43.9 9.1 %collective-permute-start.19 = (bf16[64,1024]{1,0:T(8,128)(2,1)S(1)}, bf16[64,1024]{1,0:T(8,128)(2,1)S(1)}, u32[]{:S(2)}, u32[]{:S(2)}) collective-permute-start(bf16[64,1024]{1,0:T(8,128)(2,1)S(1)} %get-tuple-element.64), channel_id=1, source_target_pairs={{0,6},{1,7},{2,4},{3,5},{4,2},{5,3},{6,0},{7,1},{8,14},{9,15},{10,... | collective-permute-start | bytes 393224 | tf_op jit(solution)/shard_map/ppermute | solution.py:326
  45.3 8.7 %collective-permute-start.20 = (bf16[64,1024]{1,0:T(8,128)(2,1)S(1)}, bf16[64,1024]{1,0:T(8,128)(2,1)S(1)}, u32[]{:S(2)}, u32[]{:S(2)}) collective-permute-start(bf16[64,1024]{1,0:T(8,128)(2,1)S(1)} %get-tuple-element.65), channel_id=1, source_target_pairs={{0,2},{1,3},{2,0},{3,1},{4,6},{5,7},{6,4},{7,5},{8,10},{9,11},{10,... | collective-permute-start | bytes 393224 | tf_op jit(solution)/shard_map/ppermute | solution.py:326
  48.7 8.6 %collective-permute-start.14 = (bf16[64,1024]{1,0:T(8,128)(2,1)S(1)}, bf16[64,1024]{1,0:T(8,128)(2,1)S(1)}, u32[]{:S(2)}, u32[]{:S(2)}) collective-permute-start(bf16[64,1024]{1,0:T(8,128)(2,1)S(1)} %get-tuple-element.55), channel_id=1, source_target_pairs={{0,4},{1,5},{2,6},{3,7},{4,0},{5,1},{6,2},{7,3},{8,12},{9,13},{10,... | collective-permute-start | bytes 393224 | tf_op jit(solution)/shard_map/ppermute | solution.py:326
  49.3 8.0 %collective-permute-start.15 = (bf16[64,1024]{1,0:T(8,128)(2,1)S(1)}, bf16[64,1024]{1,0:T(8,128)(2,1)S(1)}, u32[]{:S(2)}, u32[]{:S(2)}) collective-permute-start(bf16[64,1024]{1,0:T(8,128)(2,1)S(1)} %get-tuple-element.56), channel_id=1, source_target_pairs={{0,6},{1,7},{2,4},{3,5},{4,2},{5,3},{6,0},{7,1},{8,14},{9,15},{10,... | collective-permute-start | bytes 393224 | tf_op jit(solution)/shard_map/ppermute | solution.py:326
  53.0 5.6 %collective-permute-start.16 = (bf16[64,1024]{1,0:T(8,128)(2,1)S(1)}, bf16[64,1024]{1,0:T(8,128)(2,1)S(1)}, u32[]{:S(2)}, u32[]{:S(2)}) collective-permute-start(bf16[64,1024]{1,0:T(8,128)(2,1)S(1)} %get-tuple-element.57), channel_id=1, source_target_pairs={{0,2},{1,3},{2,0},{3,1},{4,6},{5,7},{6,4},{7,5},{8,10},{9,11},{10,... | collective-permute-start | bytes 393224 | tf_op jit(solution)/shard_map/ppermute | solution.py:326
  54.1 6.4 %collective-permute-start.21 = (bf16[32,1024]{1,0:T(8,128)(2,1)S(1)}, bf16[32,1024]{1,0:T(8,128)(2,1)S(1)}, u32[]{:S(2)}, u32[]{:S(2)}) collective-permute-start(bf16[32,1024]{1,0:T(8,128)(2,1)S(1)} %get-tuple-element.66), channel_id=1, source_target_pairs={{0,16},{1,17},{2,18},{3,19},{4,20},{5,21},{6,22},{7,23},{8,24},{9,... | collective-permute-start | bytes 196616 | tf_op jit(solution)/shard_map/ppermute | solution.py:326
  54.2 6.8 %collective-permute-start.22 = (bf16[32,1024]{1,0:T(8,128)(2,1)S(1)}, bf16[32,1024]{1,0:T(8,128)(2,1)S(1)}, u32[]{:S(2)}, u32[]{:S(2)}) collective-permute-start(bf16[32,1024]{1,0:T(8,128)(2,1)S(1)} %get-tuple-element.67), channel_id=1, source_target_pairs={{0,24},{1,25},{2,26},{3,27},{4,28},{5,29},{6,30},{7,31},{8,16},{9,... | collective-permute-start | bytes 196616 | tf_op jit(solution)/shard_map/ppermute | solution.py:326
  58.6 4.3 %collective-permute-start.17 = (bf16[32,1024]{1,0:T(8,128)(2,1)S(1)}, bf16[32,1024]{1,0:T(8,128)(2,1)S(1)}, u32[]{:S(2)}, u32[]{:S(2)}) collective-permute-start(bf16[32,1024]{1,0:T(8,128)(2,1)S(1)} %get-tuple-element.62), channel_id=1, source_target_pairs={{0,8},{1,9},{2,10},{3,11},{4,12},{5,13},{6,14},{7,15},{8,0},{9,1},... | collective-permute-start | bytes 196616 | tf_op jit(solution)/shard_map/ppermute | solution.py:326

commit v25 on v21

--- a/solution.py
+++ b/solution.py
@@ -489,7 +489,7 @@
     weight_grad, last = weight_part(ranks // 2, parts_z[0], weight_grad, info, table, stats)
     hidden_grad, loss = call(
         unpack_kernel,
-        (last, chosen, *ends),
+        (last, chosen, *ends[:zs // 2], *reversed(ends[zs // 2:])),
         [VMEM] * (2 + len(ends)),
         (shape((tokens, width), bf16), shape((1, 1), f32)),
         (VMEM, SMEM),

time: 63.1 us -> 63.1 us (level)
  starting transfers between devices: 23.8 us -> 22.9 us
  waiting for transfers between devices: 11.8 us -> 12.7 us
    ppermute x23, waiting for transfers between devices: 11.8 us -> 12.7 us  [send(): return lax.ppermute(value, AXES, pairs)]
    ppermute x23, starting transfers between devices: 23.8 us -> 22.9 us  [send(): return lax.ppermute(value, AXES, pairs)]
  transfers between devices with their start and end apart: 23 -> 23, of which waited for: 9 -> 10; matrix products, arithmetic and copies ran while one was open for 0% -> 0% of each run, Pallas kernels for 13% -> 13%
where the time goes in v25:
time: 63.1 us; the launch traced here: 63 us
  starting transfers between devices  22.9 us (36%)
  blocking collectives  13.6 us (22%)
  Pallas kernels  12.9 us (20%)
  waiting for transfers between devices  12.7 us (20%)
  between operations  0.8 us (1%)
    ppermute x23, starting transfers between devices, send(): return lax.ppermute(value, AXES, pairs)  22.9 us
    all_to_all x1, blocking collectives, body(): stats = lax.all_to_all(stats, AXES, 0, 0)  13.6 us
    pallas_call x16, Pallas kernels, call(): pl.pallas_call(kernel, out_shape=out_shape, in_specs=in_specs, out_specs=...  12.9 us
    ppermute x23, waiting for transfers between devices, send(): return lax.ppermute(value, AXES, pairs)  12.7 us
  transfers between devices with their start and end apart: 23, of which 10 were waited for; matrix products, arithmetic and copies ran while one was open for 0% of the time, Pallas kernels for 13%

profile of v25, /device:TPU:0, one launch (start us, length us, event | category | flops | bytes accessed | tf_op | source)
XLA Modules:
  0.0 63.0 jit_solution(2406343009661771379)
XLA Ops:
  0.6 1.2 %shard_map.85 = (bf16[32,1152]{1,0:T(8,128)(2,1)S(1)}, bf16[32,1024]{1,0:T(8,128)(2,1)S(1)}, bf16[32,128]{1,0:T(8,128)(2,1)S(1)}) custom-call(bf16[128,1024]{1,0:T(8,128)(2,1)} %hidden_hbm.1, s32[1,128]{1,0:T(1,128)} %bitcast.6, s32[1,128]{1,0:T(1,128)} %bitcast.7, s32[1,128]{1,0:T(1,128)} %bitcast.8), custom_call_target="tpu_custom_call" | custom-call | bytes 411136 | tf_op jit(solution)/shard_map/pallas_call | solution.py:33
  1.9 4.1 %collective-permute-start = (bf16[32,1152]{1,0:T(8,128)(2,1)S(1)}, bf16[32,1152]{1,0:T(8,128)(2,1)S(1)}, u32[]{:S(2)}, u32[]{:S(2)}) collective-permute-start(bf16[32,1152]{1,0:T(8,128)(2,1)S(1)} %get-tuple-element.37.refs_0_), channel_id=1, source_target_pairs={{0,16},{1,17},{2,18},{3,19},{4,20},{5,21},{6,22},{7,23},{8,24},{9,... | collective-permute-start | bytes 221192 | tf_op jit(solution)/shard_map/ppermute | solution.py:326
  6.0 1.3 %collective-permute-start.1 = (bf16[32,1152]{1,0:T(8,128)(2,1)S(1)}, bf16[32,1152]{1,0:T(8,128)(2,1)S(1)}, u32[]{:S(2)}, u32[]{:S(2)}) collective-permute-start(bf16[32,1152]{1,0:T(8,128)(2,1)S(1)} %get-tuple-element.37.refs_0_), channel_id=1, source_target_pairs={{0,24},{1,25},{2,26},{3,27},{4,28},{5,29},{6,30},{7,31},{8,16},{9,... | collective-permute-start | bytes 221192 | tf_op jit(solution)/shard_map/ppermute | solution.py:326
  7.5 2.4 %collective-permute-start.2 = (bf16[32,1024]{1,0:T(8,128)(2,1)S(1)}, bf16[32,1024]{1,0:T(8,128)(2,1)S(1)}, u32[]{:S(2)}, u32[]{:S(2)}) collective-permute-start(bf16[32,1024]{1,0:T(8,128)(2,1)S(1)} %get-tuple-element.38), channel_id=1, source_target_pairs={{0,6},{1,7},{2,4},{3,5},{4,2},{5,3},{6,0},{7,1},{8,14},{9,15},{10,... | collective-permute-start | bytes 196616 | tf_op jit(solution)/shard_map/ppermute | solution.py:326
  10.0 2.7 %collective-permute-done.2.refs_3_.refs_5_ = bf16[32,1024]{1,0:T(8,128)(2,1)S(1)} collective-permute-done((bf16[32,1024]{1,0:T(8,128)(2,1)S(1)}, bf16[32,1024]{1,0:T(8,128)(2,1)S(1)}, u32[]{:S(2)}, u32[]{:S(2)}) %collective-permute-start.2) | collective-permute-done | bytes 65568 | tf_op jit(solution)/shard_map/ppermute | solution.py:326
  12.8 1.7 %collective-permute-start.4 = (bf16[128,1152]{1,0:T(8,128)(2,1)S(1)}, bf16[128,1152]{1,0:T(8,128)(2,1)S(1)}, u32[]{:S(2)}, u32[]{:S(2)}) collective-permute-start(bf16[128,1152]{1,0:T(8,128)(2,1)S(1)} %get-tuple-element.39.line), channel_id=1, source_target_pairs={{0,4},{1,5},{2,6},{3,7},{4,0},{5,1},{6,2},{7,3},{8,12},{9,13},{10,... | collective-permute-start | bytes 884744 | tf_op jit(solution)/shard_map/ppermute | solution.py:326
  14.5 1.5 %collective-permute-start.5 = (bf16[128,1024]{1,0:T(8,128)(2,1)S(1)}, bf16[128,1024]{1,0:T(8,128)(2,1)S(1)}, u32[]{:S(2)}, u32[]{:S(2)}) collective-permute-start(bf16[128,1024]{1,0:T(8,128)(2,1)S(1)} %get-tuple-element.42), channel_id=1, source_target_pairs={{0,2},{1,3},{2,0},{3,1},{4,6},{5,7},{6,4},{7,5},{8,10},{9,11},{10,... | collective-permute-start | bytes 786440 | tf_op jit(solution)/shard_map/ppermute | solution.py:326
  16.3 2.9 %shard_map.87 = (bf16[4096,512]{1,0:T(8,128)(2,1)S(1)}, bf16[2048,512]{1,0:T(8,128)(2,1)S(1)}, bf16[128,1152]{1,0:T(8,128)(2,1)S(1)}) custom-call(bf16[128,1152]{1,0:T(8,128)(2,1)S(1)} %get-tuple-element.39.line, bf16[4096,512]{1,0:T(8,128)(2,1)} %weight.1), custom_call_target="tpu_custom_call" | custom-call | bytes 11075584 | tf_op jit(solution)/shard_map/pallas_call | solution.py:33
  19.3 3.1 %collective-permute-done.4.refs_1_ = bf16[128,1152]{1,0:T(8,128)(2,1)S(1)} collective-permute-done((bf16[128,1152]{1,0:T(8,128)(2,1)S(1)}, bf16[128,1152]{1,0:T(8,128)(2,1)S(1)}, u32[]{:S(2)}, u32[]{:S(2)}) %collective-permute-start.4) | collective-permute-done | bytes 294944 | tf_op jit(solution)/shard_map/ppermute | solution.py:326
  22.4 0.5 collective-permute-start.7
  23.4 0.7 %collective-permute-done.7.refs_1_.refs_4_.refs_8_ = bf16[32,1024]{1,0:T(8,128)(2,1)S(1)} collective-permute-done((bf16[32,1024]{1,0:T(8,128)(2,1)S(1)}, bf16[32,1024]{1,0:T(8,128)(2,1)S(1)}, u32[]{:S(2)}, u32[]{:S(2)}) %collective-permute-start.7) | collective-permute-done | bytes 65568 | tf_op jit(solution)/shard_map/ppermute | solution.py:326
  24.0 0.9 %collective-permute-done.6.refs_0_ = bf16[96,1024]{1,0:T(8,128)(2,1)S(1)} collective-permute-done((bf16[96,1024]{1,0:T(8,128)(2,1)S(1)}, bf16[96,1024]{1,0:T(8,128)(2,1)S(1)}, u32[]{:S(2)}, u32[]{:S(2)}) %collective-permute-start.6) | collective-permute-done | bytes 196640 | tf_op jit(solution)/shard_map/ppermute | solution.py:326
  25.0 1.0 %shard_map.91.refs_1_ = f32[256,512]{1,0:T(8,128)S(1)} custom-call(bf16[4096,512]{1,0:T(8,128)(2,1)S(1)} %get-tuple-element.41.weight.refs_2_, bf16[128,1152]{1,0:T(8,128)(2,1)S(1)} %get-tuple-element.40.refs_0_, bf16[128,1152]{1,0:T(8,128)(2,1)S(1)} %collective-permute-done.4.refs_1_, bf16[128,1024]{1,0:T(8,128)(2,1)S(1)} %shard_map.89.refs_2_.refs_4_, ...), custom_call_target="tpu_custom_call" | custom-call | flops 805306368 | bytes 6422528 | tf_op jit(solution)/shard_map/pallas_call | solution.py:33
  26.4 0.9 %shard_map.92 = (f32[256,512]{1,0:T(8,128)S(1)}, f32[32,1,384]{2,1,0:T(1,128)S(1)}) custom-call(f32[256,128]{1,0:T(8,128)S(1)} %shard_map.88.refs_1_.refs_0_.info, f32[256,512]{1,0:T(8,128)S(1)} %shard_map.91.refs_1_, bf16[4096,512]{1,0:T(8,128)(2,1)S(1)} %get-tuple-element.41.weight.refs_2_, bf16[128,1024]{1,0:T(8,128)(2,1)S(1)} %collective-permute-done.10.refs_3_.refs_7_, ...), custom_call_target="tpu_custom_call" | custom-call | flops 268435456 | bytes 5947392 | tf_op jit(solution)/shard_map/pallas_call | solution.py:33
  27.9 13.6 %all_to_all.5.stats.refs_3_ = f32[32,1,384]{2,1,0:T(1,128)S(1)} all-to-all(f32[32,1,384]{2,1,0:T(1,128)S(1)} %get-tuple-element.46.refs_1_), channel_id=1, replica_groups=mesh['dp'=8,'vocab'=4] {'dp','vocab'}, dimensions={0} | all-to-all | bytes 98304 | tf_op jit(solution)/shard_map/all_to_all | solution.py:432
  41.5 1.8 %shard_map.94 = (bf16[256,512]{1,0:T(8,128)(2,1)S(1)}, f32[256,128]{1,0:T(8,128)S(1)}, bf16[64,1024]{1,0:T(8,128)(2,1)S(1)}, bf16[64,1024]{1,0:T(8,128)(2,1)S(1)...) custom-call(f32[256,128]{1,0:T(8,128)S(1)} %shard_map.88.refs_1_.ref, ...), custom_call_target="tpu_custom_call" | custom-call | flops 1073741824 | bytes 9224192 | tf_op jit(solution)/shard_map/pallas_call | solution.py:33
  43.3 0.7 %collective-permute-start.18 = (bf16[64,1024]{1,0:T(8,128)(2,1)S(1)}, bf16[64,1024]{1,0:T(8,128)(2,1)S(1)}, u32[]{:S(2)}, u32[]{:S(2)}) collective-permute-start(bf16[64,1024]{1,0:T(8,128)(2,1)S(1)} %get-tuple-element.63), channel_id=1, source_target_pairs={{0,6},{1,7},{2,4},{3,5},{4,2},{5,3},{6,0},{7,1},{8,14},{9,15},{10,... | collective-permute-start | bytes 393224 | tf_op jit(solution)/shard_map/ppermute | solution.py:326
  44.0 1.2 %collective-permute-start.19 = (bf16[64,1024]{1,0:T(8,128)(2,1)S(1)}, bf16[64,1024]{1,0:T(8,128)(2,1)S(1)}, u32[]{:S(2)}, u32[]{:S(2)}) collective-permute-start(bf16[64,1024]{1,0:T(8,128)(2,1)S(1)} %get-tuple-element.64), channel_id=1, source_target_pairs={{0,4},{1,5},{2,6},{3,7},{4,0},{5,1},{6,2},{7,3},{8,12},{9,13},{10,... | collective-permute-start | bytes 393224 | tf_op jit(solution)/shard_map/ppermute | solution.py:326
  45.3 1.6 %collective-permute-start.20 = (bf16[64,1024]{1,0:T(8,128)(2,1)S(1)}, bf16[64,1024]{1,0:T(8,128)(2,1)S(1)}, u32[]{:S(2)}, u32[]{:S(2)}) collective-permute-start(bf16[64,1024]{1,0:T(8,128)(2,1)S(1)} %get-tuple-element.65), channel_id=1, source_target_pairs={{0,2},{1,3},{2,0},{3,1},{4,6},{5,7},{6,4},{7,5},{8,10},{9,11},{10,... | collective-permute-start | bytes 393224 | tf_op jit(solution)/shard_map/ppermute | solution.py:326
  46.8 1.8 %shard_map.95 = (bf16[4096,512]{1,0:T(8,128)(2,1)}, f32[8,128]{1,0:T(8,128)S(1)}) custom-call(f32[64,1024]{1,0:T(8,128)S(1)} %get-tuple-element.52.after.kept, bf16[256,512]{1,0:T(8,128)(2,1)S(1)} %get-tuple-element.53.logit_grad, bf16[128,1152]{1,0:T(8,128)(2,1)S(1)} %get-tuple-element.40.refs_0_, bf16[128,1152]{1,0:T(8,128)(2,1)S(1)} %collective-permute-done.4.refs_1_, ...), custom_call_target="tpu_custom_call" | custom-call | flops 536870912 | bytes 5902336 | tf_op jit(solution)/shard_map/pallas_call | solution.py:33
  48.7 0.7 %collective-permute-start.14 = (bf16[64,1024]{1,0:T(8,128)(2,1)S(1)}, bf16[64,1024]{1,0:T(8,128)(2,1)S(1)}, u32[]{:S(2)}, u32[]{:S(2)}) collective-permute-start(bf16[64,1024]{1,0:T(8,128)(2,1)S(1)} %get-tuple-element.55), channel_id=1, source_target_pairs={{0,6},{1,7},{2,4},{3,5},{4,2},{5,3},{6,0},{7,1},{8,14},{9,15},{10,... | collective-permute-start | bytes 393224 | tf_op jit(solution)/shard_map/ppermute | solution.py:326
  49.4 1.2 %collective-permute-start.15 = (bf16[64,1024]{1,0:T(8,128)(2,1)S(1)}, bf16[64,1024]{1,0:T(8,128)(2,1)S(1)}, u32[]{:S(2)}, u32[]{:S(2)}) collective-permute-start(bf16[64,1024]{1,0:T(8,128)(2,1)S(1)} %get-tuple-element.56), channel_id=1, source_target_pairs={{0,4},{1,5},{2,6},{3,7},{4,0},{5,1},{6,2},{7,3},{8,12},{9,13},{10,... | collective-permute-start | bytes 393224 | tf_op jit(solution)/shard_map/ppermute | solution.py:326
  50.7 1.6 %collective-permute-start.16 = (bf16[64,1024]{1,0:T(8,128)(2,1)S(1)}, bf16[64,1024]{1,0:T(8,128)(2,1)S(1)}, u32[]{:S(2)}, u32[]{:S(2)}) collective-permute-start(bf16[64,1024]{1,0:T(8,128)(2,1)S(1)} %get-tuple-element.57), channel_id=1, source_target_pairs={{0,2},{1,3},{2,0},{3,1},{4,6},{5,7},{6,4},{7,5},{8,10},{9,11},{10,... | collective-permute-start | bytes 393224 | tf_op jit(solution)/shard_map/ppermute | solution.py:326
  52.2 1.3 %collective-permute-done.19.refs_1_ = bf16[64,1024]{1,0:T(8,128)(2,1)S(1)} collective-permute-done((bf16[64,1024]{1,0:T(8,128)(2,1)S(1)}, bf16[64,1024]{1,0:T(8,128)(2,1)S(1)}, u32[]{:S(2)}, u32[]{:S(2)}) %collective-permute-start.19) | collective-permute-done | bytes 131104 | tf_op jit(solution)/shard_map/ppermute | solution.py:326
  53.6 0.7 %collective-permute-start.21 = (bf16[32,1024]{1,0:T(8,128)(2,1)S(1)}, bf16[32,1024]{1,0:T(8,128)(2,1)S(1)}, u32[]{:S(2)}, u32[]{:S(2)}) collective-permute-start(bf16[32,1024]{1,0:T(8,128)(2,1)S(1)} %get-tuple-element.66), channel_id=1, source_target_pairs={{0,24},{1,25},{2,26},{3,27},{4,28},{5,29},{6,30},{7,31},{8,16},{9,... | collective-permute-start | bytes 196616 | tf_op jit(solution)/shard_map/ppermute | solution.py:326
  54.3 1.5 %collective-permute-start.22 = (bf16[32,1024]{1,0:T(8,128)(2,1)S(1)}, bf16[32,1024]{1,0:T(8,128)(2,1)S(1)}, u32[]{:S(2)}, u32[]{:S(2)}) collective-permute-start(bf16[32,1024]{1,0:T(8,128)(2,1)S(1)} %get-tuple-element.67), channel_id=1, source_target_pairs={{0,16},{1,17},{2,18},{3,19},{4,20},{5,21},{6,22},{7,23},{8,24},{9,... | collective-permute-start | bytes 196616 | tf_op jit(solution)/shard_map/ppermute | solution.py:326
  56.3 1.3 %collective-permute-done.15.refs_1_ = bf16[64,1024]{1,0:T(8,128)(2,1)S(1)} collective-permute-done((bf16[64,1024]{1,0:T(8,128)(2,1)S(1)}, bf16[64,1024]{1,0:T(8,128)(2,1)S(1)}, u32[]{:S(2)}, u32[]{:S(2)}) %collective-permute-start.15) | collective-permute-done | bytes 131104 | tf_op jit(solution)/shard_map/ppermute | solution.py:326
  57.7 0.7 %collective-permute-start.17 = (bf16[32,1024]{1,0:T(8,128)(2,1)S(1)}, bf16[32,1024]{1,0:T(8,128)(2,1)S(1)}, u32[]{:S(2)}, u32[]{:S(2)}) collective-permute-start(bf16[32,1024]{1,0:T(8,128)(2,1)S(1)} %get-tuple-element.62), channel_id=1, source_target_pairs={{0,8},{1,9},{2,10},{3,11},{4,12},{5,13},{6,14},{7,15},{8,0},{9,1},... | collective-permute-start | bytes 196616 | tf_op jit(solution)/shard_map/ppermute | solution.py:326
  58.3 1.8 %shard_map.98 = (bf16[4096,512]{1,0:T(8,128)(2,1)}, f32[8,128]{1,0:T(8,128)S(1)}) custom-call(f32[32,1024]{1,0:T(8,128)S(1)} %get-tuple-element.58.after.refs_0_, bf16[256,512]{1,0:T(8,128)(2,1)S(1)} %get-tuple-element.53.logit_grad, bf16[4096,512]{1,0:T(8,128)(2,1)} %get-tuple-element.59.refs_0_, ...), custom_call_target="tpu_custom_call", output_to_operand_aliasing={{0}: (2, {})} | custom-call | flops 536870912 | bytes 10145792 | tf_op jit(solution)/shard_map/pallas_call | solution.py:33
  60.2 1.0 %collective-permute-done.22.refs_3_ = bf16[32,1024]{1,0:T(8,128)(2,1)S(1)} collective-permute-done((bf16[32,1024]{1,0:T(8,128)(2,1)S(1)}, bf16[32,1024]{1,0:T(8,128)(2,1)S(1)}, u32[]{:S(2)}, u32[]{:S(2)}) %collective-permute-start.22) | collective-permute-done | bytes 65568 | tf_op jit(solution)/shard_map/ppermute | solution.py:326
  61.2 0.8 %collective-permute-done.17.refs_1_ = bf16[32,1024]{1,0:T(8,128)(2,1)S(1)} collective-permute-done((bf16[32,1024]{1,0:T(8,128)(2,1)S(1)}, bf16[32,1024]{1,0:T(8,128)(2,1)S(1)}, u32[]{:S(2)}, u32[]{:S(2)}) %collective-permute-start.17) | collective-permute-done | bytes 65568 | tf_op jit(solution)/shard_map/ppermute | solution.py:326
  62.0 1.0 %shard_map.100 = (bf16[128,1024]{1,0:T(8,128)(2,1)}, f32[1,1]{1,0:T(1,128)}) custom-call(f32[8,128]{1,0:T(8,128)S(1)} %get-tuple-element.60.last, bf16[32,128]{1,0:T(8,128)(2,1)S(1)} %get-tuple-element.61.chosen, f32[32,1024]{1,0:T(8,128)S(1)} %get-tuple-element.58.after.refs_0_, bf16[32,1024]{1,0:T(8,128)(2,1)S(1)} %collective-permute-done.17.refs_1_, ...), custom_call_target="tpu_custom_call" | custom-call | bytes 602116 | tf_op jit(solution)/shard_map/pallas_call | solution.py:33
  (33 shorter events, 2.9 us)
Async XLA Ops:
  0.6 22.2 %copy-start = (f32[32]{0:T(128)S(1)}, f32[32]{0:T(128)}, u32[]{:S(2)}) copy-start(f32[32]{0:T(128)} %param.11) | copy-start | bytes 388
  1.9 10.8 %collective-permute-start = (bf16[32,1152]{1,0:T(8,128)(2,1)S(1)}, bf16[32,1152]{1,0:T(8,128)(2,1)S(1)}, u32[]{:S(2)}, u32[]{:S(2)}) collective-permute-start(bf16[32,1152]{1,0:T(8,128)(2,1)S(1)} %get-tuple-element.37.refs_0_), channel_id=1, source_target_pairs={{0,16},{1,17},{2,18},{3,19},{4,20},{5,21},{6,22},{7,23},{8,24},{9,... | collective-permute-start | bytes 221192 | tf_op jit(solution)/shard_map/ppermute | solution.py:326
  6.0 6.8 %collective-permute-start.1 = (bf16[32,1152]{1,0:T(8,128)(2,1)S(1)}, bf16[32,1152]{1,0:T(8,128)(2,1)S(1)}, u32[]{:S(2)}, u32[]{:S(2)}) collective-permute-start(bf16[32,1152]{1,0:T(8,128)(2,1)S(1)} %get-tuple-element.37.refs_0_), channel_id=1, source_target_pairs={{0,24},{1,25},{2,26},{3,27},{4,28},{5,29},{6,30},{7,31},{8,16},{9,... | collective-permute-start | bytes 221192 | tf_op jit(solution)/shard_map/ppermute | solution.py:326
  7.3 5.4 %collective-permute-start.3 = (bf16[32,1152]{1,0:T(8,128)(2,1)S(1)}, bf16[32,1152]{1,0:T(8,128)(2,1)S(1)}, u32[]{:S(2)}, u32[]{:S(2)}) collective-permute-start(bf16[32,1152]{1,0:T(8,128)(2,1)S(1)} %get-tuple-element.37.refs_0_), channel_id=1, source_target_pairs={{0,8},{1,9},{2,10},{3,11},{4,12},{5,13},{6,14},{7,15},{8,0},{9,1},... | collective-permute-start | bytes 221192 | tf_op jit(solution)/shard_map/ppermute | solution.py:326
  7.5 5.2 %collective-permute-start.2 = (bf16[32,1024]{1,0:T(8,128)(2,1)S(1)}, bf16[32,1024]{1,0:T(8,128)(2,1)S(1)}, u32[]{:S(2)}, u32[]{:S(2)}) collective-permute-start(bf16[32,1024]{1,0:T(8,128)(2,1)S(1)} %get-tuple-element.38), channel_id=1, source_target_pairs={{0,6},{1,7},{2,4},{3,5},{4,2},{5,3},{6,0},{7,1},{8,14},{9,15},{10,... | collective-permute-start | bytes 196616 | tf_op jit(solution)/shard_map/ppermute | solution.py:326
  12.8 9.6 %collective-permute-start.4 = (bf16[128,1152]{1,0:T(8,128)(2,1)S(1)}, bf16[128,1152]{1,0:T(8,128)(2,1)S(1)}, u32[]{:S(2)}, u32[]{:S(2)}) collective-permute-start(bf16[128,1152]{1,0:T(8,128)(2,1)S(1)} %get-tuple-element.39.line), channel_id=1, source_target_pairs={{0,4},{1,5},{2,6},{3,7},{4,0},{5,1},{6,2},{7,3},{8,12},{9,13},{10,... | collective-permute-start | bytes 884744 | tf_op jit(solution)/shard_map/ppermute | solution.py:326
  14.5 8.8 %collective-permute-start.5 = (bf16[128,1024]{1,0:T(8,128)(2,1)S(1)}, bf16[128,1024]{1,0:T(8,128)(2,1)S(1)}, u32[]{:S(2)}, u32[]{:S(2)}) collective-permute-start(bf16[128,1024]{1,0:T(8,128)(2,1)S(1)} %get-tuple-element.42), channel_id=1, source_target_pairs={{0,2},{1,3},{2,0},{3,1},{4,6},{5,7},{6,4},{7,5},{8,10},{9,11},{10,... | collective-permute-start | bytes 786440 | tf_op jit(solution)/shard_map/ppermute | solution.py:326
  15.9 9.0 %collective-permute-start.6 = (bf16[96,1024]{1,0:T(8,128)(2,1)S(1)}, bf16[96,1024]{1,0:T(8,128)(2,1)S(1)}, u32[]{:S(2)}, u32[]{:S(2)}) collective-permute-start(bf16[96,1024]{1,0:T(8,128)(2,1)S(1)} %get-tuple-element.43), channel_id=1, source_target_pairs={{0,6},{1,7},{2,4},{3,5},{4,2},{5,3},{6,0},{7,1},{8,14},{9,15},{10,... | collective-permute-start | bytes 589832 | tf_op jit(solution)/shard_map/ppermute | solution.py:326
  19.2 5.7 %collective-permute-start.8 = (bf16[128,1152]{1,0:T(8,128)(2,1)S(1)}, bf16[128,1152]{1,0:T(8,128)(2,1)S(1)}, u32[]{:S(2)}, u32[]{:S(2)}) collective-permute-start(bf16[128,1152]{1,0:T(8,128)(2,1)S(1)} %get-tuple-element.40.refs_0_), channel_id=1, source_target_pairs={{0,1},{1,0},{2,3},{3,2},{4,5},{5,4},{6,7},{7,6},{8,9},{9,8},{10,11... | collective-permute-start | bytes 884744 | tf_op jit(solution)/shard_map/ppermute | solution.py:326
  22.4 2.6 %collective-permute-start.9 = (bf16[128,1152]{1,0:T(8,128)(2,1)S(1)}, bf16[128,1152]{1,0:T(8,128)(2,1)S(1)}, u32[]{:S(2)}, u32[]{:S(2)}) collective-permute-start(bf16[128,1152]{1,0:T(8,128)(2,1)S(1)} %collective-permute-done.4.refs_1_), channel_id=1, source_target_pairs={{0,1},{1,0},{2,3},{3,2},{4,5},{5,4},{6,7},{7,6},{8,9},{9,8},{10,11... | collective-permute-start | bytes 884744 | tf_op jit(solution)/shard_map/ppermute | solution.py:326
  22.4 1.7 %collective-permute-start.7 = (bf16[32,1024]{1,0:T(8,128)(2,1)S(1)}, bf16[32,1024]{1,0:T(8,128)(2,1)S(1)}, u32[]{:S(2)}, u32[]{:S(2)}) collective-permute-start(bf16[32,1024]{1,0:T(8,128)(2,1)S(1)} %collective-permute-done.2.refs_3_.refs_5_), channel_id=1, source_target_pairs={{0,1},{1,0},{2,3},{3,2},{4,5},{5,4},{6,7},{7,6},{8,9},{9,8},{10,11... | collective-permute-start | bytes 196616 | tf_op jit(solution)/shard_map/ppermute | solution.py:326
  23.3 3.1 %collective-permute-start.10 = (bf16[128,1024]{1,0:T(8,128)(2,1)S(1)}, bf16[128,1024]{1,0:T(8,128)(2,1)S(1)}, u32[]{:S(2)}, u32[]{:S(2)}) collective-permute-start(bf16[128,1024]{1,0:T(8,128)(2,1)S(1)} %shard_map.89.refs_2_.refs_4_), channel_id=1, source_target_pairs={{0,1},{1,0},{2,3},{3,2},{4,5},{5,4},{6,7},{7,6},{8,9},{9,8},{10,11... | collective-permute-start | bytes 786440 | tf_op jit(solution)/shard_map/ppermute | solution.py:326
  24.9 1.4 %collective-permute-start.11 = (bf16[96,1024]{1,0:T(8,128)(2,1)S(1)}, bf16[96,1024]{1,0:T(8,128)(2,1)S(1)}, u32[]{:S(2)}, u32[]{:S(2)}) collective-permute-start(bf16[96,1024]{1,0:T(8,128)(2,1)S(1)} %shard_map.90.refs_4_.refs_6_), channel_id=1, source_target_pairs={{0,1},{1,0},{2,3},{3,2},{4,5},{5,4},{6,7},{7,6},{8,9},{9,8},{10,11... | collective-permute-start | bytes 589832 | tf_op jit(solution)/shard_map/ppermute | solution.py:326
  27.3 14.2 %collective-permute-start.13 = (bf16[2048,512]{1,0:T(8,128)(2,1)S(1)}, bf16[2048,512]{1,0:T(8,128)(2,1)S(1)}, u32[]{:S(2)}, u32[]{:S(2)}) collective-permute-start(bf16[2048,512]{1,0:T(8,128)(2,1)S(1)} %shard_map.93), channel_id=1, source_target_pairs={{0,1},{1,0},{2,3},{3,2},{4,5},{5,4},{6,7},{7,6},{8,9},{9,8},{10,11... | collective-permute-start | bytes 6291464 | tf_op jit(solution)/shard_map/ppermute | solution.py:326
  27.5 14.0 %collective-permute-start.12 = (f32[256,512]{1,0:T(8,128)S(1)}, f32[256,512]{1,0:T(8,128)S(1)}, u32[]{:S(2)}, u32[]{:S(2)}) collective-permute-start(f32[256,512]{1,0:T(8,128)S(1)} %get-tuple-element.44.mine), channel_id=1, source_target_pairs={{0,1},{1,0},{2,3},{3,2},{4,5},{5,4},{6,7},{7,6},{8,9},{9,8},{10,11... | collective-permute-start | bytes 1572872 | tf_op jit(solution)/shard_map/ppermute | solution.py:326
  43.3 7.4 %collective-permute-start.18 = (bf16[64,1024]{1,0:T(8,128)(2,1)S(1)}, bf16[64,1024]{1,0:T(8,128)(2,1)S(1)}, u32[]{:S(2)}, u32[]{:S(2)}) collective-permute-start(bf16[64,1024]{1,0:T(8,128)(2,1)S(1)} %get-tuple-element.63), channel_id=1, source_target_pairs={{0,6},{1,7},{2,4},{3,5},{4,2},{5,3},{6,0},{7,1},{8,14},{9,15},{10,... | collective-permute-start | bytes 393224 | tf_op jit(solution)/shard_map/ppermute | solution.py:326
  44.0 9.5 %collective-permute-start.19 = (bf16[64,1024]{1,0:T(8,128)(2,1)S(1)}, bf16[64,1024]{1,0:T(8,128)(2,1)S(1)}, u32[]{:S(2)}, u32[]{:S(2)}) collective-permute-start(bf16[64,1024]{1,0:T(8,128)(2,1)S(1)} %get-tuple-element.64), channel_id=1, source_target_pairs={{0,4},{1,5},{2,6},{3,7},{4,0},{5,1},{6,2},{7,3},{8,12},{9,13},{10,... | collective-permute-start | bytes 393224 | tf_op jit(solution)/shard_map/ppermute | solution.py:326
  45.3 8.3 %collective-permute-start.20 = (bf16[64,1024]{1,0:T(8,128)(2,1)S(1)}, bf16[64,1024]{1,0:T(8,128)(2,1)S(1)}, u32[]{:S(2)}, u32[]{:S(2)}) collective-permute-start(bf16[64,1024]{1,0:T(8,128)(2,1)S(1)} %get-tuple-element.65), channel_id=1, source_target_pairs={{0,2},{1,3},{2,0},{3,1},{4,6},{5,7},{6,4},{7,5},{8,10},{9,11},{10,... | collective-permute-start | bytes 393224 | tf_op jit(solution)/shard_map/ppermute | solution.py:326
  48.7 7.6 %collective-permute-start.14 = (bf16[64,1024]{1,0:T(8,128)(2,1)S(1)}, bf16[64,1024]{1,0:T(8,128)(2,1)S(1)}, u32[]{:S(2)}, u32[]{:S(2)}) collective-permute-start(bf16[64,1024]{1,0:T(8,128)(2,1)S(1)} %get-tuple-element.55), channel_id=1, source_target_pairs={{0,6},{1,7},{2,4},{3,5},{4,2},{5,3},{6,0},{7,1},{8,14},{9,15},{10,... | collective-permute-start | bytes 393224 | tf_op jit(solution)/shard_map/ppermute | solution.py:326
  49.4 8.2 %collective-permute-start.15 = (bf16[64,1024]{1,0:T(8,128)(2,1)S(1)}, bf16[64,1024]{1,0:T(8,128)(2,1)S(1)}, u32[]{:S(2)}, u32[]{:S(2)}) collective-permute-start(bf16[64,1024]{1,0:T(8,128)(2,1)S(1)} %get-tuple-element.56), channel_id=1, source_target_pairs={{0,4},{1,5},{2,6},{3,7},{4,0},{5,1},{6,2},{7,3},{8,12},{9,13},{10,... | collective-permute-start | bytes 393224 | tf_op jit(solution)/shard_map/ppermute | solution.py:326
  50.7 6.9 %collective-permute-start.16 = (bf16[64,1024]{1,0:T(8,128)(2,1)S(1)}, bf16[64,1024]{1,0:T(8,128)(2,1)S(1)}, u32[]{:S(2)}, u32[]{:S(2)}) collective-permute-start(bf16[64,1024]{1,0:T(8,128)(2,1)S(1)} %get-tuple-element.57), channel_id=1, source_target_pairs={{0,2},{1,3},{2,0},{3,1},{4,6},{5,7},{6,4},{7,5},{8,10},{9,11},{10,... | collective-permute-start | bytes 393224 | tf_op jit(solution)/shard_map/ppermute | solution.py:326
  53.6 6.5 %collective-permute-start.21 = (bf16[32,1024]{1,0:T(8,128)(2,1)S(1)}, bf16[32,1024]{1,0:T(8,128)(2,1)S(1)}, u32[]{:S(2)}, u32[]{:S(2)}) collective-permute-start(bf16[32,1024]{1,0:T(8,128)(2,1)S(1)} %get-tuple-element.66), channel_id=1, source_target_pairs={{0,24},{1,25},{2,26},{3,27},{4,28},{5,29},{6,30},{7,31},{8,16},{9,... | collective-permute-start | bytes 196616 | tf_op jit(solution)/shard_map/ppermute | solution.py:326
  54.3 6.9 %collective-permute-start.22 = (bf16[32,1024]{1,0:T(8,128)(2,1)S(1)}, bf16[32,1024]{1,0:T(8,128)(2,1)S(1)}, u32[]{:S(2)}, u32[]{:S(2)}) collective-permute-start(bf16[32,1024]{1,0:T(8,128)(2,1)S(1)} %get-tuple-element.67), channel_id=1, source_target_pairs={{0,16},{1,17},{2,18},{3,19},{4,20},{5,21},{6,22},{7,23},{8,24},{9,... | collective-permute-start | bytes 196616 | tf_op jit(solution)/shard_map/ppermute | solution.py:326
  57.7 4.3 %collective-permute-start.17 = (bf16[32,1024]{1,0:T(8,128)(2,1)S(1)}, bf16[32,1024]{1,0:T(8,128)(2,1)S(1)}, u32[]{:S(2)}, u32[]{:S(2)}) collective-permute-start(bf16[32,1024]{1,0:T(8,128)(2,1)S(1)} %get-tuple-element.62), channel_id=1, source_target_pairs={{0,8},{1,9},{2,10},{3,11},{4,12},{5,13},{6,14},{7,15},{8,0},{9,1},... | collective-permute-start | bytes 196616 | tf_op jit(solution)/shard_map/ppermute | solution.py:326

commit v26 on v21

--- a/solution.py
+++ b/solution.py
@@ -460,15 +460,7 @@
         )
 
     far_values, near_values = list(going[:ranks]), list(going[ranks:])
-    weight_grad, finished = weight_part(0, far_values[-1])
-    near_values[:-1] = call(
-        gate_kernel,
-        (*near_values[:-1], finished),
-        [ANY] * ranks,
-        outs[:-1],
-        (ANY,) * (ranks - 1),
-        aliases={place: place for place in range(ranks - 1)},
-    )
+    weight_grad, finished = weight_part(0, near_values[-1])
     ends, sums = [None] * zs, [None, None]
     for chunk, values in ((1, far_values), (0, near_values)):
         sums[chunk] = [values[-1]]
@@ -479,7 +471,7 @@
         near = chunk * zs // 2
         parts_z = call(
             functools.partial(corner_kernel, ranks - 1),
-            (table, *sums[chunk]),
+            (table if chunk else finished, *sums[chunk]),
             [ANY] + [VMEM] * ranks,
             tuple(shape((CAP, width), bf16 if near + z else f32) for z in range(zs // 2)),
             (VMEM,) * (zs // 2),

time: 63.1 us -> 63.1 us (level)
  waiting for transfers between devices: 11.8 us -> 13.1 us
  starting transfers between devices: 23.8 us -> 22.6 us
    ppermute x23, waiting for transfers between devices: 11.8 us -> 13.1 us  [send(): return lax.ppermute(value, AXES, pairs)]
    ppermute x23, starting transfers between devices: 23.8 us -> 22.6 us  [send(): return lax.ppermute(value, AXES, pairs)]
    pallas_call x16 -> x15, Pallas kernels: 12.9 us -> 12.9 us  [call(): pl.pallas_call(kernel, out_shape=out_shape, in_specs=in_specs, out_specs=...]
  transfers between devices with their start and end apart: 23 -> 23, of which waited for: 9 -> 10; matrix products, arithmetic and copies ran while one was open for 0% -> 0% of each run, Pallas kernels for 13% -> 13%
where the time goes in v26:
time: 63.1 us; the launch traced here: 63 us
  starting transfers between devices  22.6 us (36%)
  blocking collectives  13.6 us (22%)
  waiting for transfers between devices  13.1 us (21%)
  Pallas kernels  12.9 us (20%)
  between operations  0.8 us (1%)
    ppermute x23, starting transfers between devices, send(): return lax.ppermute(value, AXES, pairs)  22.6 us
    all_to_all x1, blocking collectives, body(): stats = lax.all_to_all(stats, AXES, 0, 0)  13.6 us
    ppermute x23, waiting for transfers between devices, send(): return lax.ppermute(value, AXES, pairs)  13.1 us
    pallas_call x15, Pallas kernels, call(): pl.pallas_call(kernel, out_shape=out_shape, in_specs=in_specs, out_specs=...  12.9 us
  transfers between devices with their start and end apart: 23, of which 10 were waited for; matrix products, arithmetic and copies ran while one was open for 0% of the time, Pallas kernels for 13%

profile of v26, /device:TPU:0, one launch (start us, length us, event | category | flops | bytes accessed | tf_op | source)
XLA Modules:
  0.0 63.0 jit_solution(1314984350626971267)
XLA Ops:
  0.6 1.2 %shard_map.85 = (bf16[32,1152]{1,0:T(8,128)(2,1)S(1)}, bf16[32,1024]{1,0:T(8,128)(2,1)S(1)}, bf16[32,128]{1,0:T(8,128)(2,1)S(1)}) custom-call(bf16[128,1024]{1,0:T(8,128)(2,1)} %hidden_hbm.1, s32[1,128]{1,0:T(1,128)} %bitcast.6, s32[1,128]{1,0:T(1,128)} %bitcast.7, s32[1,128]{1,0:T(1,128)} %bitcast.8), custom_call_target="tpu_custom_call" | custom-call | bytes 411136 | tf_op jit(solution)/shard_map/pallas_call | solution.py:33
  1.9 4.1 %collective-permute-start = (bf16[32,1152]{1,0:T(8,128)(2,1)S(1)}, bf16[32,1152]{1,0:T(8,128)(2,1)S(1)}, u32[]{:S(2)}, u32[]{:S(2)}) collective-permute-start(bf16[32,1152]{1,0:T(8,128)(2,1)S(1)} %get-tuple-element.34.refs_0_), channel_id=1, source_target_pairs={{0,16},{1,17},{2,18},{3,19},{4,20},{5,21},{6,22},{7,23},{8,24},{9,... | collective-permute-start | bytes 221192 | tf_op jit(solution)/shard_map/ppermute | solution.py:326
  6.0 1.3 %collective-permute-start.1 = (bf16[32,1152]{1,0:T(8,128)(2,1)S(1)}, bf16[32,1152]{1,0:T(8,128)(2,1)S(1)}, u32[]{:S(2)}, u32[]{:S(2)}) collective-permute-start(bf16[32,1152]{1,0:T(8,128)(2,1)S(1)} %get-tuple-element.34.refs_0_), channel_id=1, source_target_pairs={{0,24},{1,25},{2,26},{3,27},{4,28},{5,29},{6,30},{7,31},{8,16},{9,... | collective-permute-start | bytes 221192 | tf_op jit(solution)/shard_map/ppermute | solution.py:326
  7.5 2.4 %collective-permute-start.2 = (bf16[32,1024]{1,0:T(8,128)(2,1)S(1)}, bf16[32,1024]{1,0:T(8,128)(2,1)S(1)}, u32[]{:S(2)}, u32[]{:S(2)}) collective-permute-start(bf16[32,1024]{1,0:T(8,128)(2,1)S(1)} %get-tuple-element.35), channel_id=1, source_target_pairs={{0,6},{1,7},{2,4},{3,5},{4,2},{5,3},{6,0},{7,1},{8,14},{9,15},{10,... | collective-permute-start | bytes 196616 | tf_op jit(solution)/shard_map/ppermute | solution.py:326
  10.0 2.7 %collective-permute-done.2.refs_3_.refs_5_ = bf16[32,1024]{1,0:T(8,128)(2,1)S(1)} collective-permute-done((bf16[32,1024]{1,0:T(8,128)(2,1)S(1)}, bf16[32,1024]{1,0:T(8,128)(2,1)S(1)}, u32[]{:S(2)}, u32[]{:S(2)}) %collective-permute-start.2) | collective-permute-done | bytes 65568 | tf_op jit(solution)/shard_map/ppermute | solution.py:326
  12.8 1.7 %collective-permute-start.4 = (bf16[128,1152]{1,0:T(8,128)(2,1)S(1)}, bf16[128,1152]{1,0:T(8,128)(2,1)S(1)}, u32[]{:S(2)}, u32[]{:S(2)}) collective-permute-start(bf16[128,1152]{1,0:T(8,128)(2,1)S(1)} %get-tuple-element.36.line), channel_id=1, source_target_pairs={{0,4},{1,5},{2,6},{3,7},{4,0},{5,1},{6,2},{7,3},{8,12},{9,13},{10,... | collective-permute-start | bytes 884744 | tf_op jit(solution)/shard_map/ppermute | solution.py:326
  14.5 1.5 %collective-permute-start.5 = (bf16[128,1024]{1,0:T(8,128)(2,1)S(1)}, bf16[128,1024]{1,0:T(8,128)(2,1)S(1)}, u32[]{:S(2)}, u32[]{:S(2)}) collective-permute-start(bf16[128,1024]{1,0:T(8,128)(2,1)S(1)} %get-tuple-element.39), channel_id=1, source_target_pairs={{0,2},{1,3},{2,0},{3,1},{4,6},{5,7},{6,4},{7,5},{8,10},{9,11},{10,... | collective-permute-start | bytes 786440 | tf_op jit(solution)/shard_map/ppermute | solution.py:326
  16.3 2.9 %shard_map.87 = (bf16[4096,512]{1,0:T(8,128)(2,1)S(1)}, bf16[2048,512]{1,0:T(8,128)(2,1)S(1)}, bf16[128,1152]{1,0:T(8,128)(2,1)S(1)}) custom-call(bf16[128,1152]{1,0:T(8,128)(2,1)S(1)} %get-tuple-element.36.line, bf16[4096,512]{1,0:T(8,128)(2,1)} %weight.1), custom_call_target="tpu_custom_call" | custom-call | bytes 11075584 | tf_op jit(solution)/shard_map/pallas_call | solution.py:33
  19.3 3.1 %collective-permute-done.4.refs_1_ = bf16[128,1152]{1,0:T(8,128)(2,1)S(1)} collective-permute-done((bf16[128,1152]{1,0:T(8,128)(2,1)S(1)}, bf16[128,1152]{1,0:T(8,128)(2,1)S(1)}, u32[]{:S(2)}, u32[]{:S(2)}) %collective-permute-start.4) | collective-permute-done | bytes 294944 | tf_op jit(solution)/shard_map/ppermute | solution.py:326
  22.4 0.5 collective-permute-start.7
  23.4 0.7 %collective-permute-done.7.refs_1_.refs_4_.refs_8_ = bf16[32,1024]{1,0:T(8,128)(2,1)S(1)} collective-permute-done((bf16[32,1024]{1,0:T(8,128)(2,1)S(1)}, bf16[32,1024]{1,0:T(8,128)(2,1)S(1)}, u32[]{:S(2)}, u32[]{:S(2)}) %collective-permute-start.7) | collective-permute-done | bytes 65568 | tf_op jit(solution)/shard_map/ppermute | solution.py:326
  24.0 0.9 %collective-permute-done.6.refs_0_ = bf16[96,1024]{1,0:T(8,128)(2,1)S(1)} collective-permute-done((bf16[96,1024]{1,0:T(8,128)(2,1)S(1)}, bf16[96,1024]{1,0:T(8,128)(2,1)S(1)}, u32[]{:S(2)}, u32[]{:S(2)}) %collective-permute-start.6) | collective-permute-done | bytes 196640 | tf_op jit(solution)/shard_map/ppermute | solution.py:326
  25.0 1.0 %shard_map.91.refs_1_ = f32[256,512]{1,0:T(8,128)S(1)} custom-call(bf16[4096,512]{1,0:T(8,128)(2,1)S(1)} %get-tuple-element.38.weight.refs_2_, bf16[128,1152]{1,0:T(8,128)(2,1)S(1)} %get-tuple-element.37.refs_0_, bf16[128,1152]{1,0:T(8,128)(2,1)S(1)} %collective-permute-done.4.refs_1_, bf16[128,1024]{1,0:T(8,128)(2,1)S(1)} %shard_map.89.refs_2_.refs_4_, ...), custom_call_target="tpu_custom_call" | custom-call | flops 805306368 | bytes 6422528 | tf_op jit(solution)/shard_map/pallas_call | solution.py:33
  26.4 0.9 %shard_map.92 = (f32[256,512]{1,0:T(8,128)S(1)}, f32[32,1,384]{2,1,0:T(1,128)S(1)}) custom-call(f32[256,128]{1,0:T(8,128)S(1)} %shard_map.88.refs_1_.refs_0_.info, f32[256,512]{1,0:T(8,128)S(1)} %shard_map.91.refs_1_, bf16[4096,512]{1,0:T(8,128)(2,1)S(1)} %get-tuple-element.38.weight.refs_2_, bf16[128,1024]{1,0:T(8,128)(2,1)S(1)} %collective-permute-done.10.refs_3_.refs_7_, ...), custom_call_target="tpu_custom_call" | custom-call | flops 268435456 | bytes 5947392 | tf_op jit(solution)/shard_map/pallas_call | solution.py:33
  27.9 13.6 %all_to_all.5.stats.refs_3_ = f32[32,1,384]{2,1,0:T(1,128)S(1)} all-to-all(f32[32,1,384]{2,1,0:T(1,128)S(1)} %get-tuple-element.43.refs_1_), channel_id=1, replica_groups=mesh['dp'=8,'vocab'=4] {'dp','vocab'}, dimensions={0} | all-to-all | bytes 98304 | tf_op jit(solution)/shard_map/all_to_all | solution.py:432
  41.5 1.8 %shard_map.94 = (bf16[256,512]{1,0:T(8,128)(2,1)S(1)}, f32[256,128]{1,0:T(8,128)S(1)}, bf16[64,1024]{1,0:T(8,128)(2,1)S(1)}, bf16[64,1024]{1,0:T(8,128)(2,1)S(1)...) custom-call(f32[256,128]{1,0:T(8,128)S(1)} %shard_map.88.refs_1_.ref, ...), custom_call_target="tpu_custom_call" | custom-call | flops 1073741824 | bytes 9224192 | tf_op jit(solution)/shard_map/pallas_call | solution.py:33
  43.3 0.7 %collective-permute-start.18 = (bf16[64,1024]{1,0:T(8,128)(2,1)S(1)}, bf16[64,1024]{1,0:T(8,128)(2,1)S(1)}, u32[]{:S(2)}, u32[]{:S(2)}) collective-permute-start(bf16[64,1024]{1,0:T(8,128)(2,1)S(1)} %get-tuple-element.57), channel_id=1, source_target_pairs={{0,6},{1,7},{2,4},{3,5},{4,2},{5,3},{6,0},{7,1},{8,14},{9,15},{10,... | collective-permute-start | bytes 393224 | tf_op jit(solution)/shard_map/ppermute | solution.py:326
  44.0 1.2 %collective-permute-start.19 = (bf16[64,1024]{1,0:T(8,128)(2,1)S(1)}, bf16[64,1024]{1,0:T(8,128)(2,1)S(1)}, u32[]{:S(2)}, u32[]{:S(2)}) collective-permute-start(bf16[64,1024]{1,0:T(8,128)(2,1)S(1)} %get-tuple-element.58), channel_id=1, source_target_pairs={{0,4},{1,5},{2,6},{3,7},{4,0},{5,1},{6,2},{7,3},{8,12},{9,13},{10,... | collective-permute-start | bytes 393224 | tf_op jit(solution)/shard_map/ppermute | solution.py:326
  45.3 1.6 %collective-permute-start.20 = (bf16[64,1024]{1,0:T(8,128)(2,1)S(1)}, bf16[64,1024]{1,0:T(8,128)(2,1)S(1)}, u32[]{:S(2)}, u32[]{:S(2)}) collective-permute-start(bf16[64,1024]{1,0:T(8,128)(2,1)S(1)} %get-tuple-element.59), channel_id=1, source_target_pairs={{0,2},{1,3},{2,0},{3,1},{4,6},{5,7},{6,4},{7,5},{8,10},{9,11},{10,... | collective-permute-start | bytes 393224 | tf_op jit(solution)/shard_map/ppermute | solution.py:326
  46.8 0.7 %collective-permute-start.14 = (bf16[64,1024]{1,0:T(8,128)(2,1)S(1)}, bf16[64,1024]{1,0:T(8,128)(2,1)S(1)}, u32[]{:S(2)}, u32[]{:S(2)}) collective-permute-start(bf16[64,1024]{1,0:T(8,128)(2,1)S(1)} %get-tuple-element.47), channel_id=1, source_target_pairs={{0,6},{1,7},{2,4},{3,5},{4,2},{5,3},{6,0},{7,1},{8,14},{9,15},{10,... | collective-permute-start | bytes 393224 | tf_op jit(solution)/shard_map/ppermute | solution.py:326
  47.5 1.2 %collective-permute-start.15 = (bf16[64,1024]{1,0:T(8,128)(2,1)S(1)}, bf16[64,1024]{1,0:T(8,128)(2,1)S(1)}, u32[]{:S(2)}, u32[]{:S(2)}) collective-permute-start(bf16[64,1024]{1,0:T(8,128)(2,1)S(1)} %get-tuple-element.48), channel_id=1, source_target_pairs={{0,4},{1,5},{2,6},{3,7},{4,0},{5,1},{6,2},{7,3},{8,12},{9,13},{10,... | collective-permute-start | bytes 393224 | tf_op jit(solution)/shard_map/ppermute | solution.py:326
  48.8 1.9 %collective-permute-done.18.refs_0_ = bf16[64,1024]{1,0:T(8,128)(2,1)S(1)} collective-permute-done((bf16[64,1024]{1,0:T(8,128)(2,1)S(1)}, bf16[64,1024]{1,0:T(8,128)(2,1)S(1)}, u32[]{:S(2)}, u32[]{:S(2)}) %collective-permute-start.18) | collective-permute-done | bytes 131104 | tf_op jit(solution)/shard_map/ppermute | solution.py:326
  51.1 1.8 %shard_map.95 = (bf16[4096,512]{1,0:T(8,128)(2,1)}, f32[8,128]{1,0:T(8,128)S(1)}) custom-call(f32[64,1024]{1,0:T(8,128)S(1)} %get-tuple-element.44.after.kept, bf16[256,512]{1,0:T(8,128)(2,1)S(1)} %get-tuple-element.45.logit_grad, bf16[128,1152]{1,0:T(8,128)(2,1)S(1)} %get-tuple-element.37.refs_0_, bf16[128,1152]{1,0:T(8,128)(2,1)S(1)} %collective-permute-done.4.refs_1_, ...), custom_call_target="tpu_custom_call" | custom-call | flops 536870912 | bytes 5902336 | tf_op jit(solution)/shard_map/pallas_call | solution.py:33
  52.9 0.7 %collective-permute-done.19.refs_1_ = bf16[64,1024]{1,0:T(8,128)(2,1)S(1)} collective-permute-done((bf16[64,1024]{1,0:T(8,128)(2,1)S(1)}, bf16[64,1024]{1,0:T(8,128)(2,1)S(1)}, u32[]{:S(2)}, u32[]{:S(2)}) %collective-permute-start.19) | collective-permute-done | bytes 131104 | tf_op jit(solution)/shard_map/ppermute | solution.py:326
  53.6 0.7 %collective-permute-start.21 = (bf16[32,1024]{1,0:T(8,128)(2,1)S(1)}, bf16[32,1024]{1,0:T(8,128)(2,1)S(1)}, u32[]{:S(2)}, u32[]{:S(2)}) collective-permute-start(bf16[32,1024]{1,0:T(8,128)(2,1)S(1)} %get-tuple-element.60), channel_id=1, source_target_pairs={{0,16},{1,17},{2,18},{3,19},{4,20},{5,21},{6,22},{7,23},{8,24},{9,... | collective-permute-start | bytes 196616 | tf_op jit(solution)/shard_map/ppermute | solution.py:326
  54.3 2.3 %collective-permute-start.22 = (bf16[32,1024]{1,0:T(8,128)(2,1)S(1)}, bf16[32,1024]{1,0:T(8,128)(2,1)S(1)}, u32[]{:S(2)}, u32[]{:S(2)}) collective-permute-start(bf16[32,1024]{1,0:T(8,128)(2,1)S(1)} %get-tuple-element.61), channel_id=1, source_target_pairs={{0,24},{1,25},{2,26},{3,27},{4,28},{5,29},{6,30},{7,31},{8,16},{9,... | collective-permute-start | bytes 196616 | tf_op jit(solution)/shard_map/ppermute | solution.py:326
  56.7 0.9 %collective-permute-done.15.refs_1_ = bf16[64,1024]{1,0:T(8,128)(2,1)S(1)} collective-permute-done((bf16[64,1024]{1,0:T(8,128)(2,1)S(1)}, bf16[64,1024]{1,0:T(8,128)(2,1)S(1)}, u32[]{:S(2)}, u32[]{:S(2)}) %collective-permute-start.15) | collective-permute-done | bytes 131104 | tf_op jit(solution)/shard_map/ppermute | solution.py:326
  57.7 0.7 %collective-permute-start.17 = (bf16[32,1024]{1,0:T(8,128)(2,1)S(1)}, bf16[32,1024]{1,0:T(8,128)(2,1)S(1)}, u32[]{:S(2)}, u32[]{:S(2)}) collective-permute-start(bf16[32,1024]{1,0:T(8,128)(2,1)S(1)} %get-tuple-element.55), channel_id=1, source_target_pairs={{0,8},{1,9},{2,10},{3,11},{4,12},{5,13},{6,14},{7,15},{8,0},{9,1},... | collective-permute-start | bytes 196616 | tf_op jit(solution)/shard_map/ppermute | solution.py:326
  58.3 1.8 %shard_map.97 = (bf16[4096,512]{1,0:T(8,128)(2,1)}, f32[8,128]{1,0:T(8,128)S(1)}) custom-call(f32[32,1024]{1,0:T(8,128)S(1)} %get-tuple-element.50.after.refs_0_, bf16[256,512]{1,0:T(8,128)(2,1)S(1)} %get-tuple-element.45.logit_grad, bf16[4096,512]{1,0:T(8,128)(2,1)} %get-tuple-element.51.refs_0_, ...), custom_call_target="tpu_custom_call", output_to_operand_aliasing={{0}: (2, {})} | custom-call | flops 536870912 | bytes 10145792 | tf_op jit(solution)/shard_map/pallas_call | solution.py:33
  60.2 0.7 %collective-permute-done.22.refs_3_ = bf16[32,1024]{1,0:T(8,128)(2,1)S(1)} collective-permute-done((bf16[32,1024]{1,0:T(8,128)(2,1)S(1)}, bf16[32,1024]{1,0:T(8,128)(2,1)S(1)}, u32[]{:S(2)}, u32[]{:S(2)}) %collective-permute-start.22) | collective-permute-done | bytes 65568 | tf_op jit(solution)/shard_map/ppermute | solution.py:326
  60.8 1.2 %collective-permute-done.17.refs_1_ = bf16[32,1024]{1,0:T(8,128)(2,1)S(1)} collective-permute-done((bf16[32,1024]{1,0:T(8,128)(2,1)S(1)}, bf16[32,1024]{1,0:T(8,128)(2,1)S(1)}, u32[]{:S(2)}, u32[]{:S(2)}) %collective-permute-start.17) | collective-permute-done | bytes 65568 | tf_op jit(solution)/shard_map/ppermute | solution.py:326
  62.0 1.0 %shard_map.99 = (bf16[128,1024]{1,0:T(8,128)(2,1)}, f32[1,1]{1,0:T(1,128)}) custom-call(f32[8,128]{1,0:T(8,128)S(1)} %get-tuple-element.53.last, bf16[32,128]{1,0:T(8,128)(2,1)S(1)} %get-tuple-element.54.chosen, f32[32,1024]{1,0:T(8,128)S(1)} %get-tuple-element.50.after.refs_0_, bf16[32,1024]{1,0:T(8,128)(2,1)S(1)} %collective-permute-done.17.refs_1_, ...), custom_call_target="tpu_custom_call" | custom-call | bytes 602116 | tf_op jit(solution)/shard_map/pallas_call | solution.py:33
  (32 shorter events, 2.8 us)
Async XLA Ops:
  0.6 22.2 %copy-start = (f32[32]{0:T(128)S(1)}, f32[32]{0:T(128)}, u32[]{:S(2)}) copy-start(f32[32]{0:T(128)} %param.11) | copy-start | bytes 388
  1.9 10.8 %collective-permute-start = (bf16[32,1152]{1,0:T(8,128)(2,1)S(1)}, bf16[32,1152]{1,0:T(8,128)(2,1)S(1)}, u32[]{:S(2)}, u32[]{:S(2)}) collective-permute-start(bf16[32,1152]{1,0:T(8,128)(2,1)S(1)} %get-tuple-element.34.refs_0_), channel_id=1, source_target_pairs={{0,16},{1,17},{2,18},{3,19},{4,20},{5,21},{6,22},{7,23},{8,24},{9,... | collective-permute-start | bytes 221192 | tf_op jit(solution)/shard_map/ppermute | solution.py:326
  6.0 6.8 %collective-permute-start.1 = (bf16[32,1152]{1,0:T(8,128)(2,1)S(1)}, bf16[32,1152]{1,0:T(8,128)(2,1)S(1)}, u32[]{:S(2)}, u32[]{:S(2)}) collective-permute-start(bf16[32,1152]{1,0:T(8,128)(2,1)S(1)} %get-tuple-element.34.refs_0_), channel_id=1, source_target_pairs={{0,24},{1,25},{2,26},{3,27},{4,28},{5,29},{6,30},{7,31},{8,16},{9,... | collective-permute-start | bytes 221192 | tf_op jit(solution)/shard_map/ppermute | solution.py:326
  7.3 5.4 %collective-permute-start.3 = (bf16[32,1152]{1,0:T(8,128)(2,1)S(1)}, bf16[32,1152]{1,0:T(8,128)(2,1)S(1)}, u32[]{:S(2)}, u32[]{:S(2)}) collective-permute-start(bf16[32,1152]{1,0:T(8,128)(2,1)S(1)} %get-tuple-element.34.refs_0_), channel_id=1, source_target_pairs={{0,8},{1,9},{2,10},{3,11},{4,12},{5,13},{6,14},{7,15},{8,0},{9,1},... | collective-permute-start | bytes 221192 | tf_op jit(solution)/shard_map/ppermute | solution.py:326
  7.5 5.2 %collective-permute-start.2 = (bf16[32,1024]{1,0:T(8,128)(2,1)S(1)}, bf16[32,1024]{1,0:T(8,128)(2,1)S(1)}, u32[]{:S(2)}, u32[]{:S(2)}) collective-permute-start(bf16[32,1024]{1,0:T(8,128)(2,1)S(1)} %get-tuple-element.35), channel_id=1, source_target_pairs={{0,6},{1,7},{2,4},{3,5},{4,2},{5,3},{6,0},{7,1},{8,14},{9,15},{10,... | collective-permute-start | bytes 196616 | tf_op jit(solution)/shard_map/ppermute | solution.py:326
  12.8 9.6 %collective-permute-start.4 = (bf16[128,1152]{1,0:T(8,128)(2,1)S(1)}, bf16[128,1152]{1,0:T(8,128)(2,1)S(1)}, u32[]{:S(2)}, u32[]{:S(2)}) collective-permute-start(bf16[128,1152]{1,0:T(8,128)(2,1)S(1)} %get-tuple-element.36.line), channel_id=1, source_target_pairs={{0,4},{1,5},{2,6},{3,7},{4,0},{5,1},{6,2},{7,3},{8,12},{9,13},{10,... | collective-permute-start | bytes 884744 | tf_op jit(solution)/shard_map/ppermute | solution.py:326
  14.5 8.8 %collective-permute-start.5 = (bf16[128,1024]{1,0:T(8,128)(2,1)S(1)}, bf16[128,1024]{1,0:T(8,128)(2,1)S(1)}, u32[]{:S(2)}, u32[]{:S(2)}) collective-permute-start(bf16[128,1024]{1,0:T(8,128)(2,1)S(1)} %get-tuple-element.39), channel_id=1, source_target_pairs={{0,2},{1,3},{2,0},{3,1},{4,6},{5,7},{6,4},{7,5},{8,10},{9,11},{10,... | collective-permute-start | bytes 786440 | tf_op jit(solution)/shard_map/ppermute | solution.py:326
  15.9 9.0 %collective-permute-start.6 = (bf16[96,1024]{1,0:T(8,128)(2,1)S(1)}, bf16[96,1024]{1,0:T(8,128)(2,1)S(1)}, u32[]{:S(2)}, u32[]{:S(2)}) collective-permute-start(bf16[96,1024]{1,0:T(8,128)(2,1)S(1)} %get-tuple-element.40), channel_id=1, source_target_pairs={{0,6},{1,7},{2,4},{3,5},{4,2},{5,3},{6,0},{7,1},{8,14},{9,15},{10,... | collective-permute-start | bytes 589832 | tf_op jit(solution)/shard_map/ppermute | solution.py:326
  19.2 5.7 %collective-permute-start.8 = (bf16[128,1152]{1,0:T(8,128)(2,1)S(1)}, bf16[128,1152]{1,0:T(8,128)(2,1)S(1)}, u32[]{:S(2)}, u32[]{:S(2)}) collective-permute-start(bf16[128,1152]{1,0:T(8,128)(2,1)S(1)} %get-tuple-element.37.refs_0_), channel_id=1, source_target_pairs={{0,1},{1,0},{2,3},{3,2},{4,5},{5,4},{6,7},{7,6},{8,9},{9,8},{10,11... | collective-permute-start | bytes 884744 | tf_op jit(solution)/shard_map/ppermute | solution.py:326
  22.4 2.6 %collective-permute-start.9 = (bf16[128,1152]{1,0:T(8,128)(2,1)S(1)}, bf16[128,1152]{1,0:T(8,128)(2,1)S(1)}, u32[]{:S(2)}, u32[]{:S(2)}) collective-permute-start(bf16[128,1152]{1,0:T(8,128)(2,1)S(1)} %collective-permute-done.4.refs_1_), channel_id=1, source_target_pairs={{0,1},{1,0},{2,3},{3,2},{4,5},{5,4},{6,7},{7,6},{8,9},{9,8},{10,11... | collective-permute-start | bytes 884744 | tf_op jit(solution)/shard_map/ppermute | solution.py:326
  22.4 1.7 %collective-permute-start.7 = (bf16[32,1024]{1,0:T(8,128)(2,1)S(1)}, bf16[32,1024]{1,0:T(8,128)(2,1)S(1)}, u32[]{:S(2)}, u32[]{:S(2)}) collective-permute-start(bf16[32,1024]{1,0:T(8,128)(2,1)S(1)} %collective-permute-done.2.refs_3_.refs_5_), channel_id=1, source_target_pairs={{0,1},{1,0},{2,3},{3,2},{4,5},{5,4},{6,7},{7,6},{8,9},{9,8},{10,11... | collective-permute-start | bytes 196616 | tf_op jit(solution)/shard_map/ppermute | solution.py:326
  23.3 3.1 %collective-permute-start.10 = (bf16[128,1024]{1,0:T(8,128)(2,1)S(1)}, bf16[128,1024]{1,0:T(8,128)(2,1)S(1)}, u32[]{:S(2)}, u32[]{:S(2)}) collective-permute-start(bf16[128,1024]{1,0:T(8,128)(2,1)S(1)} %shard_map.89.refs_2_.refs_4_), channel_id=1, source_target_pairs={{0,1},{1,0},{2,3},{3,2},{4,5},{5,4},{6,7},{7,6},{8,9},{9,8},{10,11... | collective-permute-start | bytes 786440 | tf_op jit(solution)/shard_map/ppermute | solution.py:326
  24.9 1.4 %collective-permute-start.11 = (bf16[96,1024]{1,0:T(8,128)(2,1)S(1)}, bf16[96,1024]{1,0:T(8,128)(2,1)S(1)}, u32[]{:S(2)}, u32[]{:S(2)}) collective-permute-start(bf16[96,1024]{1,0:T(8,128)(2,1)S(1)} %shard_map.90.refs_4_.refs_6_), channel_id=1, source_target_pairs={{0,1},{1,0},{2,3},{3,2},{4,5},{5,4},{6,7},{7,6},{8,9},{9,8},{10,11... | collective-permute-start | bytes 589832 | tf_op jit(solution)/shard_map/ppermute | solution.py:326
  27.3 14.2 %collective-permute-start.13 = (bf16[2048,512]{1,0:T(8,128)(2,1)S(1)}, bf16[2048,512]{1,0:T(8,128)(2,1)S(1)}, u32[]{:S(2)}, u32[]{:S(2)}) collective-permute-start(bf16[2048,512]{1,0:T(8,128)(2,1)S(1)} %shard_map.93), channel_id=1, source_target_pairs={{0,1},{1,0},{2,3},{3,2},{4,5},{5,4},{6,7},{7,6},{8,9},{9,8},{10,11... | collective-permute-start | bytes 6291464 | tf_op jit(solution)/shard_map/ppermute | solution.py:326
  27.5 14.0 %collective-permute-start.12 = (f32[256,512]{1,0:T(8,128)S(1)}, f32[256,512]{1,0:T(8,128)S(1)}, u32[]{:S(2)}, u32[]{:S(2)}) collective-permute-start(f32[256,512]{1,0:T(8,128)S(1)} %get-tuple-element.41.mine), channel_id=1, source_target_pairs={{0,1},{1,0},{2,3},{3,2},{4,5},{5,4},{6,7},{7,6},{8,9},{9,8},{10,11... | collective-permute-start | bytes 1572872 | tf_op jit(solution)/shard_map/ppermute | solution.py:326
  43.3 7.4 %collective-permute-start.18 = (bf16[64,1024]{1,0:T(8,128)(2,1)S(1)}, bf16[64,1024]{1,0:T(8,128)(2,1)S(1)}, u32[]{:S(2)}, u32[]{:S(2)}) collective-permute-start(bf16[64,1024]{1,0:T(8,128)(2,1)S(1)} %get-tuple-element.57), channel_id=1, source_target_pairs={{0,6},{1,7},{2,4},{3,5},{4,2},{5,3},{6,0},{7,1},{8,14},{9,15},{10,... | collective-permute-start | bytes 393224 | tf_op jit(solution)/shard_map/ppermute | solution.py:326
  44.0 9.5 %collective-permute-start.19 = (bf16[64,1024]{1,0:T(8,128)(2,1)S(1)}, bf16[64,1024]{1,0:T(8,128)(2,1)S(1)}, u32[]{:S(2)}, u32[]{:S(2)}) collective-permute-start(bf16[64,1024]{1,0:T(8,128)(2,1)S(1)} %get-tuple-element.58), channel_id=1, source_target_pairs={{0,4},{1,5},{2,6},{3,7},{4,0},{5,1},{6,2},{7,3},{8,12},{9,13},{10,... | collective-permute-start | bytes 393224 | tf_op jit(solution)/shard_map/ppermute | solution.py:326
  45.3 8.3 %collective-permute-start.20 = (bf16[64,1024]{1,0:T(8,128)(2,1)S(1)}, bf16[64,1024]{1,0:T(8,128)(2,1)S(1)}, u32[]{:S(2)}, u32[]{:S(2)}) collective-permute-start(bf16[64,1024]{1,0:T(8,128)(2,1)S(1)} %get-tuple-element.59), channel_id=1, source_target_pairs={{0,2},{1,3},{2,0},{3,1},{4,6},{5,7},{6,4},{7,5},{8,10},{9,11},{10,... | collective-permute-start | bytes 393224 | tf_op jit(solution)/shard_map/ppermute | solution.py:326
  46.8 9.8 %collective-permute-start.14 = (bf16[64,1024]{1,0:T(8,128)(2,1)S(1)}, bf16[64,1024]{1,0:T(8,128)(2,1)S(1)}, u32[]{:S(2)}, u32[]{:S(2)}) collective-permute-start(bf16[64,1024]{1,0:T(8,128)(2,1)S(1)} %get-tuple-element.47), channel_id=1, source_target_pairs={{0,6},{1,7},{2,4},{3,5},{4,2},{5,3},{6,0},{7,1},{8,14},{9,15},{10,... | collective-permute-start | bytes 393224 | tf_op jit(solution)/shard_map/ppermute | solution.py:326
  47.5 10.1 %collective-permute-start.15 = (bf16[64,1024]{1,0:T(8,128)(2,1)S(1)}, bf16[64,1024]{1,0:T(8,128)(2,1)S(1)}, u32[]{:S(2)}, u32[]{:S(2)}) collective-permute-start(bf16[64,1024]{1,0:T(8,128)(2,1)S(1)} %get-tuple-element.48), channel_id=1, source_target_pairs={{0,4},{1,5},{2,6},{3,7},{4,0},{5,1},{6,2},{7,3},{8,12},{9,13},{10,... | collective-permute-start | bytes 393224 | tf_op jit(solution)/shard_map/ppermute | solution.py:326
  50.6 6.9 %collective-permute-start.16 = (bf16[64,1024]{1,0:T(8,128)(2,1)S(1)}, bf16[64,1024]{1,0:T(8,128)(2,1)S(1)}, u32[]{:S(2)}, u32[]{:S(2)}) collective-permute-start(bf16[64,1024]{1,0:T(8,128)(2,1)S(1)} %get-tuple-element.49), channel_id=1, source_target_pairs={{0,2},{1,3},{2,0},{3,1},{4,6},{5,7},{6,4},{7,5},{8,10},{9,11},{10,... | collective-permute-start | bytes 393224 | tf_op jit(solution)/shard_map/ppermute | solution.py:326
  53.6 6.5 %collective-permute-start.21 = (bf16[32,1024]{1,0:T(8,128)(2,1)S(1)}, bf16[32,1024]{1,0:T(8,128)(2,1)S(1)}, u32[]{:S(2)}, u32[]{:S(2)}) collective-permute-start(bf16[32,1024]{1,0:T(8,128)(2,1)S(1)} %get-tuple-element.60), channel_id=1, source_target_pairs={{0,16},{1,17},{2,18},{3,19},{4,20},{5,21},{6,22},{7,23},{8,24},{9,... | collective-permute-start | bytes 196616 | tf_op jit(solution)/shard_map/ppermute | solution.py:326
  54.3 6.5 %collective-permute-start.22 = (bf16[32,1024]{1,0:T(8,128)(2,1)S(1)}, bf16[32,1024]{1,0:T(8,128)(2,1)S(1)}, u32[]{:S(2)}, u32[]{:S(2)}) collective-permute-start(bf16[32,1024]{1,0:T(8,128)(2,1)S(1)} %get-tuple-element.61), channel_id=1, source_target_pairs={{0,24},{1,25},{2,26},{3,27},{4,28},{5,29},{6,30},{7,31},{8,16},{9,... | collective-permute-start | bytes 196616 | tf_op jit(solution)/shard_map/ppermute | solution.py:326
  57.7 4.3 %collective-permute-start.17 = (bf16[32,1024]{1,0:T(8,128)(2,1)S(1)}, bf16[32,1024]{1,0:T(8,128)(2,1)S(1)}, u32[]{:S(2)}, u32[]{:S(2)}) collective-permute-start(bf16[32,1024]{1,0:T(8,128)(2,1)S(1)} %get-tuple-element.55), channel_id=1, source_target_pairs={{0,8},{1,9},{2,10},{3,11},{4,12},{5,13},{6,14},{7,15},{8,0},{9,1},... | collective-permute-start | bytes 196616 | tf_op jit(solution)/shard_map/ppermute | solution.py:326
